TPU v7x, 32 devices: a whole 2x2x4 slice. The times are simulated.
32 devices in a mesh: groups: 2 (over y), shard: 4 (over z), cache: 2 (over x), pair: 2 (over core).
Axes of the slice: x: 2, y: 2, z: 4, core: 2. Of those that a mesh axis runs over, the one named last changes fastest.
Arguments:
- cand_items: int32 [4096], P(('groups', 'shard', 'cache', 'pair')), parts along dimension 0, may hold values from 0 to 1023, as said below
- reader_users: int32 [256], P(('groups', 'shard', 'cache', 'pair')), parts along dimension 0, may hold values from 0 to 511, as said below
- item_table: bfloat16 [1024, 3072], P(('shard', 'cache')), may hold values from -6 to 6
- user_states: bfloat16 [1024, 3072], P(('groups', 'shard')), parts along dimension 0, may hold values from -0.109375 to 0.109375
- pair_mats: bfloat16 [512, 64, 64], P('pair'), may hold values from -0.00390625 to 0.00390625
- pair_fields: int32 [512, 2], P('pair'), may hold values from 0 to 47, as said below
Outputs:
- score: float32 [4096], P(('groups', 'shard', 'cache', 'pair')), parts along dimension 0
There are 2 independent parts, one for each index of `groups`. A program takes and returns all parts, laid end to end along the dimension named above; an argument that names none is the same for every part. Nothing has to cross between parts.
Inputs may be any that keep to these rules, and one draw needn't show every extreme that they name: `cand_items`: item ids; owner o holds ids o * 128 to (o + 1) * 128 - 1. The 128 candidates of one device name items of one owner at most 32 times, and one owner, the same for every device of the draw, exactly 32 times. `reader_users`: user ids; index s of shard holds ids s * 128 to (s + 1) * 128 - 1. The 8 users of one device lie in one such block at most 4 times, and one block, the same for every device of the draw, exactly 4 times. `pair_fields`: each row holds two field numbers a < b; no pair repeats.
All inputs are finite; a program needn't handle non-finite values.
Results may differ from a plain program's by a relative error of at most 0.0003.
Values may be sent and summed in bfloat16 or wider, within the bound.
No kernel may reach another device: no remote copies, remote signals or barrier semaphores. Data moves between devices by JAX's collectives and lax.ppermute only.
A program may use at most 64 MiB of HBM per device.

v0:
```python
import math

import jax
import jax.numpy as jnp
from jax import lax
from jax.sharding import PartitionSpec as P

K = 64
FI = 48


def owner_slots(owner, count):
    owner_marks = (owner[:, None] == jnp.arange(count, dtype=jnp.int32)[None, :]).astype(jnp.int32)
    earlier = jnp.cumsum(owner_marks, axis=0) - owner_marks
    return jnp.sum(earlier * owner_marks, axis=1)


def pack_requests(within, owner, count, capacity):
    position = owner * capacity + owner_slots(owner, count)
    buffer = jnp.full((count * capacity,), -1, jnp.int32).at[position].set(within)
    return (buffer.reshape(count, capacity), position)


def look_rows(lookup, wanted):
    present = wanted >= 0
    picked = jnp.take(lookup, jnp.maximum(wanted, 0), axis=0)
    return jnp.where(present[..., None], picked, jnp.zeros_like(picked))


def pair_terms(fetched, matrices, fields):
    row_count = fetched.shape[0]
    fields_view = fetched.reshape(row_count, FI, K)
    pair_count = matrices.shape[0]
    block_size = math.gcd(pair_count, 16)
    mats_blocked = matrices.reshape(pair_count // block_size, block_size, K, K)
    fields_blocked = fields.reshape(pair_count // block_size, block_size, 2)

    def accumulate(running, inputs):
        mats_now, fields_now = inputs
        left_side = jnp.take(fields_view, fields_now[:, 0], axis=1)
        right_side = jnp.take(fields_view, fields_now[:, 1], axis=1)
        product = jnp.einsum(
            "rpk,pkl->rpl", left_side, mats_now, preferred_element_type=jnp.float32
        )
        return (running + jnp.sum(product * right_side.astype(jnp.float32), axis=(1, 2)), None)

    result, leftover = lax.scan(
        accumulate, jnp.zeros((row_count,), jnp.float32), (mats_blocked, fields_blocked)
    )
    return result


def body(cand_items, reader_users, item_table, user_states, pair_mats, pair_fields):
    half = cand_items.shape[0]
    width = item_table.shape[1]
    owners = lax.axis_size(("shard", "cache"))
    item_rows = item_table.shape[0]
    item_cap = 2 * ((half + owners - 1) // owners)
    item_owner = cand_items // item_rows
    requests, item_place = pack_requests(cand_items % item_rows, item_owner, owners, item_cap)
    arrived = lax.all_to_all(requests, ("shard", "cache"), split_axis=0, concat_axis=0, tiled=True)
    rows_back = lax.all_to_all(
        look_rows(item_table, arrived), ("shard", "cache"), split_axis=0, concat_axis=0, tiled=True
    )
    returned = rows_back
    scores_back = jnp.zeros(arrived.shape, jnp.float32)
    returned = returned.reshape(owners * item_cap, width)
    scores_back = scores_back.reshape(owners * item_cap)
    fetched = jnp.take(returned, item_place, axis=0)
    readers = reader_users.shape[0]
    shard_total = lax.axis_size("shard")
    user_rows = user_states.shape[0]
    user_cap = 2 * ((readers + shard_total - 1) // shard_total)
    user_asks, user_place = pack_requests(
        reader_users % user_rows, reader_users // user_rows, shard_total, user_cap
    )
    states_back = lax.all_to_all(
        look_rows(
            user_states, lax.all_to_all(user_asks, "shard", split_axis=0, concat_axis=0, tiled=True)
        ),
        "shard",
        split_axis=0,
        concat_axis=0,
        tiled=True,
    )
    reader_state = jnp.take(states_back.reshape(shard_total * user_cap, width), user_place, axis=0)
    linear = jnp.einsum(
        "ulw,uw->ul",
        fetched.reshape(readers, half // readers, width),
        reader_state,
        preferred_element_type=jnp.float32,
    ).reshape(half)
    paired_terms = pair_terms(
        lax.all_gather(fetched, "pair", axis=0, tiled=True), pair_mats, pair_fields
    )
    pairwise = lax.psum_scatter(paired_terms, "pair", scatter_dimension=0, tiled=True)
    return linear + pairwise


def solution(mesh):
    return jax.shard_map(
        body,
        mesh=mesh,
        in_specs=(
            P(("groups", "shard", "cache", "pair")),
            P(("groups", "shard", "cache", "pair")),
            P(("shard", "cache"), None),
            P(("groups", "shard"), None),
            P("pair", None, None),
            P("pair", None),
        ),
        out_specs=P(("groups", "shard", "cache", "pair")),
        check_vma=False,
    )
```

profile of v0, /device:TPU:0, one launch (start us, length us, event | category | flops | bytes accessed | tf_op | source)
XLA Modules:
  0.0 141.2 jit_solution(10224537426224392198)
XLA Ops:
  6.5 0.7 and_select_fusion.2
  7.7 1.0 scatter_custom_fusion
  8.7 0.7 all_to_all.18
  9.4 7.3 %all-to-all-start = ((s32[8,1,32]{2,1,0:T(1,128)}), s32[8,1,32]{2,1,0:T(1,128)S(1)}, u32[]{:S(2)}, u32[]{:S(2)}) async-start(s32[8,1,32]{2,1,0:T(1,128)} %all_to_all.18), calls=%async_computation | async-start | bytes 8192 | tf_op jit(solution)/shard_map/all_to_all | solution.py:61
  16.6 0.7 and_select_fusion
  17.5 0.6 scatter_custom_fusion.1
  18.1 0.7 all_to_all.21
  18.8 4.3 %all-to-all-done = s32[8,1,32]{2,1,0:T(1,128)S(1)} async-done(((s32[8,1,32]{2,1,0:T(1,128)}), s32[8,1,32]{2,1,0:T(1,128)S(1)}, u32[]{:S(2)}, u32[]{:S(2)}) %all-to-all-start) | async-done | bytes 1056 | tf_op jit(solution)/shard_map/all_to_all | solution.py:61
  23.1 3.2 %all-to-all-start.2 = ((s32[4,1,4]{2,1,0:T(1,128)}), s32[4,1,4]{2,1,0:T(1,128)S(1)}, u32[]{:S(2)}, u32[]{:S(2)}) async-start(s32[4,1,4]{2,1,0:T(1,128)} %bitcast.7), calls=%async_computation.2 | async-start | bytes 4096 | tf_op jit(solution)/shard_map/all_to_all | solution.py:79
  26.5 1.6 %gather_fusion.2 = bf16[256,3072]{1,0:T(8,128)(2,1)S(1)} fusion(bf16[128,3072]{1,0:T(8,128)(2,1)S(1)} %copy-done, s32[1024]{0:T(1024)S(1)} %pad_clamp_fusion.5), kind=kCustom, calls=%fused_computation.2 | custom fusion | bytes 3146752 | tf_op jit(solution)/shard_map/jit(_take)/gather | solution.py:26
  28.0 1.4 %select_select_fusion = bf16[8,32,3072]{2,1,0:T(8,128)(2,1)} fusion(bf16[8,32,3072]{2,1,0:T(8,128)(2,1)S(1)} %bitcast.60, pred[8,32]{1,0:T(8,128)(4,1)S(1)} %get-tuple-element.95, pred[8,32]{1,0:T(8,128)(4,1)S(1)} %get-tuple-element.94), kind=kLoop, calls=%fused_computation.27 | loop fusion | flops 1572864 | bytes 3146240 | tf_op jit(solution)/shard_map/jit(_where)/select_n | solution.py:27
  29.5 2.2 %all-to-all-done.2 = s32[4,1,4]{2,1,0:T(1,128)S(1)} async-done(((s32[4,1,4]{2,1,0:T(1,128)}), s32[4,1,4]{2,1,0:T(1,128)S(1)}, u32[]{:S(2)}, u32[]{:S(2)}) %all-to-all-start.2) | async-done | bytes 96 | tf_op jit(solution)/shard_map/all_to_all | solution.py:79
  31.7 3.6 %all-to-all-start.1 = ((bf16[8,32,3072]{2,1,0:T(8,128)(2,1)}), bf16[8,32,3072]{2,1,0:T(8,128)(2,1)S(1)}, u32[]{:S(2)}, u32[]{:S(2)}) async-start(bf16[8,32,3072]{2,1,0:T(8,128)(2,1)} %select_select_fusion), calls=%async_computation.1 | async-start | bytes 3145728 | tf_op jit(solution)/shard_map/all_to_all | solution.py:62
  35.5 0.6 gather_fusion.4
  36.2 34.1 %all-to-all-done.1 = bf16[8,32,3072]{2,1,0:T(8,128)(2,1)S(1)} async-done(((bf16[8,32,3072]{2,1,0:T(8,128)(2,1)}), bf16[8,32,3072]{2,1,0:T(8,128)(2,1)S(1)}, u32[]{:S(2)}, u32[]{:S(2)}) %all-to-all-start.1) | async-done | bytes 1572896 | tf_op jit(solution)/shard_map/all_to_all | solution.py:62
  70.3 1.0 gather_fusion.3
  71.3 1.0 broadcast_select_fusion
  72.4 0.8 select_select_fusion.1
  73.1 3.3 %all-to-all-start.3 = ((bf16[4,4,3072]{2,1,0:T(4,128)(2,1)}), bf16[4,4,3072]{2,1,0:T(4,128)(2,1)S(1)}, u32[]{:S(2)}, u32[]{:S(2)}) async-start(bf16[4,4,3072]{2,1,0:T(4,128)(2,1)} %select_select_fusion.1), calls=%async_computation.3 | async-start | bytes 196608 | tf_op jit(solution)/shard_map/all_to_all | solution.py:77
  76.5 8.9 %copy.25 = bf16[256,64,64]{1,2,0:T(8,128)(2,1)} copy(bf16[256,64,64]{0,2,1:T(8,128)(2,1)} %param.14) | data formatting | bytes 4194304 | tf_op args[4]
  85.5 0.7 dynamic-slice
  86.9 0.6 gather_fusion.5
  88.1 1.7 %copy.26 = bf16[256,3072]{0,1:T(8,128)(2,1)S(1)} copy(bf16[256,3072]{1,0:T(8,128)(2,1)} %all-gather.2.cloned.1.call-done) | data formatting | bytes 3145728 | tf_op jit(solution)/shard_map/all_gather | solution.py:94
  89.9 41.4 %while.11 = (s32[]{:T(128)}, f32[256]{0:T(256)S(1)}, bf16[16,16,64,64]{2,3,1,0:T(8,128)(2,1)}, s32[16,16,2]{1,0,2:T(8,128)S(1)}, bf16[256,48,64]{0,2,1:T(8,128)(2,1)S(1)}, /*index=5*/s32[]{:T(128)}, s32[]{:T(128)}) while((s32[]{:T(128)}, f32[256]{0:T(256)S(1)}, bf16[16,16,64,64]{2,3,1,0:T(8,128)(2,1)}, ...), condition=%wide.region_8.10_spmd.clone, body=%wide.region_6.9_spmd.clone.sunk | while | flops 34867648 | bytes 3421595 | solution.py:47
  90.5 0.6 gather_fusion.1
  91.1 1.3 fusion.27
  93.7 1.3 fusion.27
  96.3 1.3 fusion.27
  98.9 1.3 fusion.27
  101.5 1.3 fusion.27
  104.0 1.3 fusion.27
  105.5 0.6 gather_fusion
  106.6 1.3 fusion.27
  108.1 0.6 gather_fusion
  108.6 0.6 gather_fusion.1
  109.2 1.3 fusion.27
  111.8 1.3 fusion.27
  113.2 0.6 gather_fusion
  113.8 0.6 gather_fusion.1
  114.4 1.3 fusion.27
  117.0 1.3 fusion.27
  119.6 1.3 fusion.27
  122.2 1.3 fusion.27
  124.8 1.3 fusion.27
  127.4 1.3 fusion.27
  129.9 1.3 fusion.27
  131.3 2.5 %all-reduce = f32[256]{0:T(256)S(1)} all-reduce(f32[256]{0:T(256)S(1)} %get-tuple-element.33), channel_id=2, replica_groups=mesh['groups'=2,'shard'=4,'cache'=2,'pair'=2] {'pair'}, use_global_device_ids=true, to_apply=%region_9.11.clone | all-reduce | flops 256 | bytes 2048
  133.8 0.6 dynamic-slice_add_fusion
  (129 shorter events, 17.5 us)
Async XLA Ops:
  6.5 19.9 %copy-start = (bf16[128,3072]{1,0:T(8,128)(2,1)S(1)}, bf16[128,3072]{1,0:T(8,128)(2,1)}, u32[]{:S(2)}) copy-start(bf16[128,3072]{1,0:T(8,128)(2,1)} %param.12) | copy-start | bytes 2359300
  9.4 13.7 %all-to-all-start = ((s32[8,1,32]{2,1,0:T(1,128)}), s32[8,1,32]{2,1,0:T(1,128)S(1)}, u32[]{:S(2)}, u32[]{:S(2)}) async-start(s32[8,1,32]{2,1,0:T(1,128)} %all_to_all.18), calls=%async_computation | async-start | bytes 8192 | tf_op jit(solution)/shard_map/all_to_all | solution.py:61
  23.1 8.6 %all-to-all-start.2 = ((s32[4,1,4]{2,1,0:T(1,128)}), s32[4,1,4]{2,1,0:T(1,128)S(1)}, u32[]{:S(2)}, u32[]{:S(2)}) async-start(s32[4,1,4]{2,1,0:T(1,128)} %bitcast.7), calls=%async_computation.2 | async-start | bytes 4096 | tf_op jit(solution)/shard_map/all_to_all | solution.py:79
  29.5 6.0 %copy-start.1 = (bf16[128,3072]{1,0:T(8,128)(2,1)S(1)}, bf16[128,3072]{1,0:T(8,128)(2,1)}, u32[]{:S(2)}) copy-start(bf16[128,3072]{1,0:T(8,128)(2,1)} %param.13) | copy-start | bytes 2359300
  31.7 38.6 %all-to-all-start.1 = ((bf16[8,32,3072]{2,1,0:T(8,128)(2,1)}), bf16[8,32,3072]{2,1,0:T(8,128)(2,1)S(1)}, u32[]{:S(2)}, u32[]{:S(2)}) async-start(bf16[8,32,3072]{2,1,0:T(8,128)(2,1)} %select_select_fusion), calls=%async_computation.1 | async-start | bytes 3145728 | tf_op jit(solution)/shard_map/all_to_all | solution.py:62
  35.3 52.8 %all-gather.2.cloned.1.call-start = ((), (), s32[]{:S(2)}) async-start(), calls=%async_computation.4 | async-start | bytes 2359296 | tf_op jit(solution)/shard_map/all_gather | solution.py:94
  73.1 13.8 %all-to-all-start.3 = ((bf16[4,4,3072]{2,1,0:T(4,128)(2,1)}), bf16[4,4,3072]{2,1,0:T(4,128)(2,1)S(1)}, u32[]{:S(2)}, u32[]{:S(2)}) async-start(bf16[4,4,3072]{2,1,0:T(4,128)(2,1)} %select_select_fusion.1), calls=%async_computation.3 | async-start | bytes 196608 | tf_op jit(solution)/shard_map/all_to_all | solution.py:77
  76.5 8.9 %copy-start.2 = (s32[256,2]{0,1:T(2,128)S(1)}, s32[256,2]{0,1:T(2,128)}, u32[]{:S(2)}) copy-start(s32[256,2]{0,1:T(2,128)} %param.15) | copy-start | bytes 6148
  76.5 9.0 %copy-start.3 = (u32[32]{0:T(128)S(1)}, u32[32]{0:T(128)}, u32[]{:S(2)}) copy-start(u32[32]{0:T(128)} %constant.152) | copy-start | bytes 388
Sparse Core Ops, SparseCore 0:
  72.5 8.6 all-gather.1
where the time goes:
time: 142 us; the launch traced here: 141 us
  waiting for transfers between devices  40.7 us (29%)
  local copies, waits for them, and re-layouts  37.2 us (26%)
  matrix products  21.7 us (15%)
  starting transfers between devices  17.4 us (12%)
  between operations  14.3 us (10%)
  other arithmetic  6.49 us (5%)
  blocking collectives  2.47 us (2%)
    all_to_all x1, waiting for transfers between devices, body(): lax.all_to_all(look_rows(item_table, arrived), ('shard', 'cache'), split_...  34.1 us
    dot_general x16, matrix products, accumulate(): jnp.einsum('rpk,pkl->rpl', left_side, mats_now, preferred_element_type=jn...  21.2 us
    unnamed x11, local copies, waits for them, and re-layouts  9.61 us
    gather x16, local copies, waits for them, and re-layouts, accumulate(): left_side = jnp.take(fields_view, fields_now[:, 0], axis=1)  9.29 us
    gather x16, local copies, waits for them, and re-layouts, accumulate(): right_side = jnp.take(fields_view, fields_now[:, 1], axis=1)  9.29 us
    all_to_all x1, starting transfers between devices, body(): lax.all_to_all(requests, ('shard', 'cache'), split_axis=0, concat_axis=0,...  7.25 us
    all_to_all x1, waiting for transfers between devices, body(): lax.all_to_all(requests, ('shard', 'cache'), split_axis=0, concat_axis=0,...  4.3 us
    all_to_all x1, starting transfers between devices, body(): lax.all_to_all(look_rows(item_table, arrived), ('shard', 'cache'), split_...  3.58 us
  transfers between devices with their start and end apart: 5, of which 3 were waited for; matrix products, arithmetic and copies ran while one was open for 12% of the time, Pallas kernels for 0%

commit v1 on v0

v1 whole, which is shorter than its diff:
```python
import functools

import jax
import jax.numpy as jnp
from jax import lax
from jax.experimental import pallas as pl
from jax.experimental.pallas import tpu as pltpu
from jax.sharding import PartitionSpec as P

K = 64
FI = 48
LANES = 128
VMEM_LIMIT = 48 * 1024 * 1024
NT = (((1,), (1,)), ((), ()))
TN = (((0,), (0,)), ((), ()))
NN = (((1,), (0,)), ((), ()))


def dot(a, b, dims, **kw):
    return lax.dot_general(a, b, dims, preferred_element_type=jnp.float32, **kw)


def iota(shape, dim):
    return lax.broadcasted_iota(jnp.int32, shape, dim)


def pair_kernel(fields, items, mats, out, mats_own, rows32, rows16, stacked, sem):
    count = mats_own.shape[2]
    first = pl.multiple_of(lax.axis_index("groups") * count, count)
    copy = pltpu.make_async_copy(mats.at[:, :, pl.ds(first, count)], mats_own, sem)
    copy.start()
    rows = items.shape[0]
    eye = (iota((LANES, LANES), 0) == iota((LANES, LANES), 1)).astype(jnp.bfloat16)
    for t in range(items.shape[1] // LANES):
        turned = dot(eye, items[:, t * LANES:(t + 1) * LANES], NT)
        rows32[t * LANES:(t + 1) * LANES, :] = turned
        rows16[t * LANES:(t + 1) * LANES, :] = turned.astype(jnp.bfloat16)
    copy.wait()
    eye_pairs = (iota((count, count), 0) == iota((count, count), 1)).astype(jnp.bfloat16)
    for k in range(K):
        both = jnp.concatenate([mats_own[k], mats_own[k]], axis=0)
        stacked[pl.ds(k, count, stride=K), :] = dot(eye_pairs, both, NT)

    def one(p, total):
        a = pl.multiple_of(fields[0, first + p] * K, K)
        b = pl.multiple_of(fields[1, first + p] * K, K)
        matrix = stacked[pl.ds(pl.multiple_of(p * K, K), K), :][:, :K].astype(jnp.bfloat16)
        moved = dot(matrix, rows16[pl.ds(b, K), :], NN)
        return total + moved * rows32[pl.ds(a, K), :]

    total = lax.fori_loop(0, count, one, jnp.zeros((K, rows), jnp.float32), unroll=8)
    line = jnp.sum(total, axis=0, keepdims=True)
    mine = iota(out.shape, 0) == lax.axis_index("cache")
    out[...] = jnp.where(mine, jnp.broadcast_to(line, out.shape), 0.0)


def pick_kernel(total, cap, *refs):
    users, (states, out) = refs[:total], refs[total:]
    own_rows = states.shape[0]
    me = lax.axis_index("shard")
    slots = out.shape[0]
    slot_index = iota((slots, own_rows), 0)
    row_index = iota((slots, own_rows), 1)
    chosen = jnp.zeros((slots, own_rows), jnp.float32)
    for j in range(total):
        taken = jnp.int32(0)
        source = lax.rem(me - j + total, total)
        for r in range(users[j].shape[0]):
            user = users[j][r]
            mine = user // own_rows == me
            slot = jnp.where(mine, source * cap + taken, -1)
            taken = taken + mine.astype(jnp.int32)
            chosen = jnp.where((slot_index == slot) & (row_index == user % own_rows), 1.0, chosen)
    out[...] = dot(chosen.astype(jnp.bfloat16), states[...], NN).astype(jnp.bfloat16)


def score_kernel(total, planes, parts, cap, *refs):
    users, refs = refs[:total], refs[total:]
    states, refs = refs[:total], refs[total:]
    cands, refs = refs[:total], refs[total:]
    items, refs = refs[:1 + (planes - 1) * parts], refs[1 + (planes - 1) * parts:]
    pairs, outs = refs[0], refs[1:]
    me = lax.axis_index("shard")
    plane = lax.axis_index("cache")
    core = lax.axis_index("pair")
    slots = states[0].shape[0]
    own_rows = items[0].shape[0]
    user_rows = slots_rows(users, total, cap, me)
    wanted = jnp.concatenate([ref[...] for ref in states], axis=0)
    blocks = []
    for q in range(planes):
        at = lax.rem(plane - q + planes, planes)
        base = (me * planes + at) * own_rows
        pair_row = pairs[pl.ds(at, 1), :]
        if q == 0:
            blocks.append((items[0], base, 0, pair_row))
        else:
            for h in range(parts):
                piece = own_rows // parts
                start = lax.rem(core - h + parts, parts) * piece
                blocks.append((items[1 + (q - 1) * parts + h], base + start, start, pair_row))
    linear = []
    for rows, base, start, pair_row in blocks:
        count = rows.shape[0]
        pick = iota((count, own_rows), 0) + start == iota((count, own_rows), 1)
        pair_column = jnp.sum(jnp.where(pick, pair_row, 0.0), axis=1, keepdims=True)
        linear.append((dot(rows[...], wanted, NT), base, pair_column))
    for j in range(total):
        width = cands[j].shape[1]
        readers = users[j].shape[0]
        lane = iota((1, width), 1) // (width // readers)
        slot_row = jnp.zeros((1, width), jnp.int32)
        for r in range(readers):
            slot_row = jnp.where(lane == r, user_rows[j][r], slot_row)
        spread = (iota((total * slots, width), 0) == slot_row).astype(jnp.float32)
        result = jnp.zeros((1, width), jnp.float32)
        for block, base, pair_column in linear:
            scores = dot(block, spread, NN, precision=lax.Precision.HIGHEST) + pair_column
            hit = iota(scores.shape, 0) + base == cands[j][...]
            result = result + jnp.sum(jnp.where(hit, scores, 0.0), axis=0, keepdims=True)
        outs[j][...] = result


def slots_rows(users, total, cap, me):
    result = []
    for j in range(total):
        source = lax.rem(me - j + total, total)
        holders = [users[j][r] // USER_ROWS[0] for r in range(users[j].shape[0])]
        line = []
        for r, holder in enumerate(holders):
            rank = jnp.int32(0)
            for earlier in holders[:r]:
                rank = rank + (earlier == holder).astype(jnp.int32)
            arrival = lax.rem(me - holder + total, total)
            line.append(arrival * (total * cap) + source * cap + rank)
        result.append(line)
    return result


USER_ROWS = [128]


def shift(x, axis, step):
    size = lax.axis_size(axis)
    return lax.ppermute(x, axis, [(s, (s + step) % size) for s in range(size)])


def body(cand_items, reader_users, item_table, user_states, pair_mats, pair_fields):
    total = lax.axis_size("shard")
    planes = lax.axis_size("cache")
    parts = lax.axis_size("pair")
    groups = lax.axis_size("groups")
    half = cand_items.shape[0]
    rows, width = item_table.shape
    readers = reader_users.shape[0]
    cap = 2 * ((readers + total - 1) // total)
    USER_ROWS[0] = user_states.shape[0]
    vmem = pl.BlockSpec(memory_space=pltpu.VMEM)
    smem = pl.BlockSpec(memory_space=pltpu.SMEM)
    anywhere = pl.BlockSpec(memory_space=pl.ANY)
    params = pltpu.CompilerParams(vmem_limit_bytes=VMEM_LIMIT)

    with jax.named_scope("ids"):
        users = [reader_users] + [shift(reader_users, "shard", j) for j in range(1, total)]
        cands = [cand_items] + [shift(cand_items, "shard", j) for j in range(1, total)]

    with jax.named_scope("item_rows"):
        piece = rows // parts
        mine = lax.dynamic_slice_in_dim(item_table, lax.axis_index("pair") * piece, piece, 0)
        items = [item_table]
        for q in range(1, planes):
            crossed = shift(mine, "cache", q)
            items.append(crossed)
            items.extend(shift(crossed, "pair", h) for h in range(1, parts))

    with jax.named_scope("pairs"):
        count = pair_mats.shape[0] // groups
        pair_scores = pl.pallas_call(
            pair_kernel,
            out_shape=jax.ShapeDtypeStruct((planes, rows), jnp.float32),
            in_specs=[smem, vmem, anywhere],
            out_specs=vmem,
            scratch_shapes=[
                pltpu.VMEM((K, K, count), jnp.bfloat16),
                pltpu.VMEM((width, rows), jnp.float32),
                pltpu.VMEM((width, rows), jnp.bfloat16),
                pltpu.VMEM((count * K, LANES), jnp.float32),
                pltpu.SemaphoreType.DMA,
            ],
            compiler_params=params,
            cost_estimate=pl.CostEstimate(flops=2 * count * K * K * rows * 16, bytes_accessed=2 * 1024 * 1024, transcendentals=0),
        )(pair_fields.T, item_table, jnp.transpose(pair_mats, (1, 2, 0)))
        pair_scores = lax.psum(pair_scores, ("groups", "cache", "pair"))

    with jax.named_scope("states"):
        picked = pl.pallas_call(
            functools.partial(pick_kernel, total, cap),
            out_shape=jax.ShapeDtypeStruct((total * cap, width), jnp.bfloat16),
            in_specs=[smem] * total + [vmem],
            out_specs=vmem,
            compiler_params=params,
            cost_estimate=pl.CostEstimate(flops=2 * total * cap * rows * width, bytes_accessed=1024 * 1024, transcendentals=0),
        )(*users, user_states)
        states = [picked] + [shift(picked, "shard", j) for j in range(1, total)]

    with jax.named_scope("scores"):
        outs = pl.pallas_call(
            functools.partial(score_kernel, total, planes, parts, cap),
            out_shape=[jax.ShapeDtypeStruct((1, half), jnp.float32)] * total,
            in_specs=[smem] * total + [vmem] * total + [vmem] * total + [vmem] * len(items) + [vmem],
            out_specs=[vmem] * total,
            compiler_params=params,
            cost_estimate=pl.CostEstimate(flops=2 * 64 * 256 * width, bytes_accessed=2 * 1024 * 1024, transcendentals=0),
        )(*users, *states, *[c.reshape(1, half) for c in cands], *items, pair_scores)

    with jax.named_scope("back"):
        result = outs[0]
        for j in range(1, total):
            result = result + shift(outs[j], "shard", -j)
    return result.reshape(half)


def solution(mesh):
    return jax.shard_map(
        body,
        mesh=mesh,
        in_specs=(
            P(("groups", "shard", "cache", "pair")),
            P(("groups", "shard", "cache", "pair")),
            P(("shard", "cache"), None),
            P(("groups", "shard"), None),
            P("pair", None, None),
            P("pair", None),
        ),
        out_specs=P(("groups", "shard", "cache", "pair")),
        check_vma=False,
    )
```

time: 142 us -> 63.3 us (0.45)
  local copies, waits for them, and re-layouts: 37.2 us -> 6.22 us
  waiting for transfers between devices: 40.7 us -> 14.8 us
  matrix products: 21.7 us -> 0 us
  between operations: 14.3 us -> 0.09 us
  Pallas kernels: 0 us -> 10.3 us
  blocking collectives: 2.47 us -> 11.8 us
  other arithmetic: 6.49 us -> 0.52 us
  starting transfers between devices: 17.4 us -> 19.1 us
    all_to_all x4 -> x0, waiting for transfers between devices: 40.6 us -> none  [the longest x1 34.1 us: body(): lax.all_to_all(look_rows(item_table, arrived), ('shard', 'cache'), split_...]
    gather x37 -> x0, local copies, waits for them, and re-layouts: 22.4 us -> none  [the longest x16 9.29 us: accumulate(): left_side = jnp.take(fields_view, fields_now[:, 0], axis=1)]
    dot_general x17 -> x0, matrix products: 21.7 us -> none  [the longest x16 21.2 us: accumulate(): jnp.einsum('rpk,pkl->rpl', left_side, mats_now, preferred_element_type=jn...]
    ppermute x0 -> x14, starting transfers between devices: none -> 19.1 us  [shift(): return lax.ppermute(x, axis, [(s, (s + step) % size) for s in range(size)])]
    all_to_all x4 -> x0, starting transfers between devices: 17.4 us -> none  [the longest x1 7.25 us: body(): lax.all_to_all(requests, ('shard', 'cache'), split_axis=0, concat_axis=0,...]
    ppermute x0 -> x14, waiting for transfers between devices: none -> 14.8 us  [shift(): return lax.ppermute(x, axis, [(s, (s + step) % size) for s in range(size)])]
    psum x0 -> x1, blocking collectives: none -> 11.8 us  [body(): pair_scores = lax.psum(pair_scores, ('groups', 'cache', 'pair'))]
    pallas_call x0 -> x3, Pallas kernels: none -> 10.3 us  [the longest x1 7.63 us: body(): pl.pallas_call(pair_kernel, out_shape=jax.ShapeDtypeStruct((planes, rows)...]
  transfers between devices with their start and end apart: 5 -> 14, of which waited for: 3 -> 5; matrix products, arithmetic and copies ran while one was open for 12% -> 0% of each run, Pallas kernels for 0% -> 14%
where the time goes in v1:
time: 63.3 us; the launch traced here: 62.9 us
  starting transfers between devices  19.1 us (30%)
  waiting for transfers between devices  14.8 us (23%)
  blocking collectives  11.8 us (19%)
  Pallas kernels  10.3 us (16%)
  local copies, waits for them, and re-layouts  6.22 us (10%)
    ppermute x14, starting transfers between devices, shift(): return lax.ppermute(x, axis, [(s, (s + step) % size) for s in range(size)])  19.1 us
    ppermute x14, waiting for transfers between devices, shift(): return lax.ppermute(x, axis, [(s, (s + step) % size) for s in range(size)])  14.8 us
    psum x1, blocking collectives, body(): pair_scores = lax.psum(pair_scores, ('groups', 'cache', 'pair'))  11.8 us
    pallas_call x1, Pallas kernels, body(): pl.pallas_call(pair_kernel, out_shape=jax.ShapeDtypeStruct((planes, rows)...  7.63 us
    unnamed x16, local copies, waits for them, and re-layouts  5.2 us
    pallas_call x1, Pallas kernels, body(): pl.pallas_call(functools.partial(score_kernel, total, planes, parts, cap)...  1.69 us
  transfers between devices with their start and end apart: 14, of which 5 were waited for; matrix products, arithmetic and copies ran while one was open for 0% of the time, Pallas kernels for 14%

profile of v1, /device:TPU:0, one launch (start us, length us, event | category | flops | bytes accessed | tf_op | source)
XLA Modules:
  0.0 62.9 jit_solution(14792298619746546397)
XLA Ops:
  0.0 1.0 %constant_dynamic-slice_fusion = bf16[64,3072]{1,0:T(8,128)(2,1)S(1)} fusion(bf16[128,3072]{1,0:T(8,128)(2,1)} %refs_12_.1, s32[]{:T(128)S(6)} %select_n.3), kind=kLoop, calls=%fused_computation.1 | loop fusion | bytes 786436 | tf_op jit(solution)/shard_map/item_rows/dynamic_slice | solution.py:169
  1.0 3.0 %collective-permute-start.9 = (bf16[64,3072]{1,0:T(8,128)(2,1)S(1)}, bf16[64,3072]{1,0:T(8,128)(2,1)S(1)}, u32[]{:S(2)}, u32[]{:S(2)}) collective-permute-start(bf16[64,3072]{1,0:T(8,128)(2,1)S(1)} %constant_dynamic-slice_fusion), channel_id=1, source_target_pairs={{0,2},{2,0},{1,3},{3,1},{4,6},{6,4},{5,7},{7,5},{8,10},{10,8},{9,1... | collective-permute-start | bytes 1179656 | tf_op jit(solution)/shard_map/item_rows/ppermute | solution.py:145
  4.0 9.1 %collective-permute-done.9.refs_13_ = bf16[64,3072]{1,0:T(8,128)(2,1)S(1)} collective-permute-done((bf16[64,3072]{1,0:T(8,128)(2,1)S(1)}, bf16[64,3072]{1,0:T(8,128)(2,1)S(1)}, u32[]{:S(2)}, u32[]{:S(2)}) %collective-permute-start.9) | collective-permute-done | bytes 393248 | tf_op jit(solution)/shard_map/item_rows/ppermute | solution.py:145
  13.1 0.0 collective-permute-start.10
  13.1 1.8 %collective-permute-start = (s32[8]{0:T(128)}, s32[8]{0:T(128)S(1)}, u32[]{:S(2)}, u32[]{:S(2)}) collective-permute-start(s32[8]{0:T(128)} %refs_0_.3), channel_id=1, source_target_pairs={{0,4},{4,8},{8,12},{12,0},{1,5},{5,9},{9,13},{13,1},{2,6},{6,10},{... | collective-permute-start | bytes 104 | tf_op jit(solution)/shard_map/ids/ppermute | solution.py:145
  15.0 2.6 %collective-permute-start.1 = (s32[8]{0:T(128)}, s32[8]{0:T(128)S(1)}, u32[]{:S(2)}, u32[]{:S(2)}) collective-permute-start(s32[8]{0:T(128)} %refs_0_.3), channel_id=1, source_target_pairs={{0,8},{4,12},{8,0},{12,4},{1,9},{5,13},{9,1},{13,5},{2,10},{6,14},... | collective-permute-start | bytes 104 | tf_op jit(solution)/shard_map/ids/ppermute | solution.py:145
  17.6 1.3 %collective-permute-start.2 = (s32[8]{0:T(128)}, s32[8]{0:T(128)S(1)}, u32[]{:S(2)}, u32[]{:S(2)}) collective-permute-start(s32[8]{0:T(128)} %refs_0_.3), channel_id=1, source_target_pairs={{0,12},{4,0},{8,4},{12,8},{1,13},{5,1},{9,5},{13,9},{2,14},{6,2},{... | collective-permute-start | bytes 104 | tf_op jit(solution)/shard_map/ids/ppermute | solution.py:145
  18.9 0.7 %collective-permute-start.6 = (s32[128]{0:T(128)}, s32[128]{0:T(128)S(1)}, u32[]{:S(2)}, u32[]{:S(2)}) collective-permute-start(s32[128]{0:T(128)} %param.6), channel_id=1, source_target_pairs={{0,4},{4,8},{8,12},{12,0},{1,5},{5,9},{9,13},{13,1},{2,6},{6,10},{... | collective-permute-start | bytes 1544 | tf_op jit(solution)/shard_map/ids/ppermute | solution.py:145
  19.6 0.0 collective-permute-done.refs_1_
  19.6 0.3 collective-permute-start.7
  19.9 0.0 collective-permute-done.1.refs_2_
  19.9 1.3 %collective-permute-done.2.refs_3_ = s32[8]{0:T(128)S(1)} collective-permute-done((s32[8]{0:T(128)}, s32[8]{0:T(128)S(1)}, u32[]{:S(2)}, u32[]{:S(2)}) %collective-permute-start.2) | collective-permute-done | bytes 64 | tf_op jit(solution)/shard_map/ids/ppermute | solution.py:145
  21.2 0.0 copy-start.2
  21.2 1.1 %copy-done.2 = bf16[128,3072]{1,0:T(8,128)(2,1)S(1)} copy-done((bf16[128,3072]{1,0:T(8,128)(2,1)S(1)}, bf16[128,3072]{1,0:T(8,128)(2,1)}, u32[]{:S(2)}) %copy-start.2) | copy-done | bytes 786456
  22.4 0.0 copy-start.3
  22.4 0.7 %copy-done.3 = s32[8]{0:T(128)S(1)} copy-done((s32[8]{0:T(128)S(1)}, s32[8]{0:T(128)}, u32[]{:S(2)}) %copy-start.3) | copy-done | bytes 56
  23.0 1.0 %states.1.refs_4_ = bf16[16,3072]{1,0:T(8,128)(2,1)S(1)} custom-call(s32[8]{0:T(128)S(1)} %copy-done.3, s32[8]{0:T(128)S(1)} %collective-permute-done.refs_1_, s32[8]{0:T(128)S(1)} %collective-permute-done.1.refs_2_, s32[8]{0:T(128)S(1)} %collective-permute-done.2.refs_3_, bf16[128,3072]{1,0:T(8,128)(2,1)S(1)} %copy-done.2), custom_call_target="tpu_custom_call" | custom-call | flops 12582912 | bytes 1048576 | tf_op jit(solution)/shard_map/states/pallas_call | solution.py:196
  24.0 2.1 %collective-permute-start.3 = (bf16[16,3072]{1,0:T(8,128)(2,1)S(1)}, bf16[16,3072]{1,0:T(8,128)(2,1)S(1)}, u32[]{:S(2)}, u32[]{:S(2)}) collective-permute-start(bf16[16,3072]{1,0:T(8,128)(2,1)S(1)} %states.1.refs_4_), channel_id=1, source_target_pairs={{0,4},{4,8},{8,12},{12,0},{1,5},{5,9},{9,13},{13,1},{2,6},{6,10},{... | collective-permute-start | bytes 294920 | tf_op jit(solution)/shard_map/states/ppermute | solution.py:145
  26.1 1.6 %collective-permute-start.4 = (bf16[16,3072]{1,0:T(8,128)(2,1)S(1)}, bf16[16,3072]{1,0:T(8,128)(2,1)S(1)}, u32[]{:S(2)}, u32[]{:S(2)}) collective-permute-start(bf16[16,3072]{1,0:T(8,128)(2,1)S(1)} %states.1.refs_4_), channel_id=1, source_target_pairs={{0,8},{4,12},{8,0},{12,4},{1,9},{5,13},{9,1},{13,5},{2,10},{6,14},... | collective-permute-start | bytes 294920 | tf_op jit(solution)/shard_map/states/ppermute | solution.py:145
  27.8 0.0 collective-permute-done.6
  27.8 0.8 %collective-permute-start.5 = (bf16[16,3072]{1,0:T(8,128)(2,1)S(1)}, bf16[16,3072]{1,0:T(8,128)(2,1)S(1)}, u32[]{:S(2)}, u32[]{:S(2)}) collective-permute-start(bf16[16,3072]{1,0:T(8,128)(2,1)S(1)} %states.1.refs_4_), channel_id=1, source_target_pairs={{0,12},{4,0},{8,4},{12,8},{1,13},{5,1},{9,5},{13,9},{2,14},{6,2},{... | collective-permute-start | bytes 294920 | tf_op jit(solution)/shard_map/states/ppermute | solution.py:145
  28.6 0.0 copy-start
  28.6 1.1 %copy-done = bf16[128,3072]{1,0:T(8,128)(2,1)S(1)} copy-done((bf16[128,3072]{1,0:T(8,128)(2,1)S(1)}, bf16[128,3072]{1,0:T(8,128)(2,1)}, u32[]{:S(2)}) %copy-start) | copy-done | bytes 786456
  29.7 0.0 copy-start.6
  29.7 1.6 %copy-done.6 = bf16[256,64,64]{0,2,1:T(8,128)(2,1)S(1)} copy-done((bf16[256,64,64]{0,2,1:T(8,128)(2,1)S(1)}, bf16[256,64,64]{0,2,1:T(8,128)(2,1)}, u32[]{:S(2)}) %copy-start.6) | copy-done | bytes 2097176
  31.3 0.0 copy-start.7
  31.3 0.7 %copy-done.7 = s32[256,2]{0,1:T(2,128)S(1)} copy-done((s32[256,2]{0,1:T(2,128)S(1)}, s32[256,2]{0,1:T(2,128)}, u32[]{:S(2)}) %copy-start.7) | copy-done | bytes 2072
  32.0 0.0 copy-start.5
  32.0 7.6 %pairs.1 = f32[2,128]{1,0:T(2,128)S(1)} custom-call(s32[2,256]{1,0:T(2,128)S(1)} %bitcast.13, bf16[128,3072]{1,0:T(8,128)(2,1)S(1)} %copy-done, bf16[64,64,256]{2,1,0:T(8,128)(2,1)S(1)} %bitcast.12), custom_call_target="tpu_custom_call" | custom-call | flops 2147483648 | bytes 2097152 | tf_op jit(solution)/shard_map/pairs/pallas_call | solution.py:178
  39.6 0.0 collective-permute-done.7
  39.6 0.0 copy-done.5
  39.7 2.0 %collective-permute-start.8 = (s32[128]{0:T(128)S(1)}, s32[128]{0:T(128)S(1)}, u32[]{:S(2)}, u32[]{:S(2)}) collective-permute-start(s32[128]{0:T(128)S(1)} %copy-done.5), channel_id=1, source_target_pairs={{0,12},{4,0},{8,4},{12,8},{1,13},{5,1},{9,5},{13,9},{2,14},{6,2},{... | collective-permute-start | bytes 1544 | tf_op jit(solution)/shard_map/ids/ppermute | solution.py:145
  41.7 11.8 %psum.7.refs_15_ = f32[2,128]{1,0:T(2,128)S(1)} all-reduce(f32[2,128]{1,0:T(2,128)S(1)} %pairs.1), channel_id=1, replica_groups=mesh['groups'=2,'shard'=4,'cache'=2,'pair'=2] {'groups','cache','pair'}, use_global_device_ids=true, to_apply=%region_0.0 | all-reduce | flops 256 | bytes 2048 | tf_op jit(solution)/shard_map/pairs/psum | solution.py:193
  53.5 0.0 collective-permute-done.8
  53.5 0.0 collective-permute-done.3.refs_5_
  53.5 0.0 collective-permute-done.4.refs_6_
  53.5 0.0 collective-permute-done.5.refs_7_
  53.5 0.0 collective-permute-done.10.refs_14_
  53.5 0.0 copy-done.1
  53.5 0.0 copy-done.4
  53.6 1.7 %scores.1 = (f32[1,128]{1,0:T(1,128)S(1)}, f32[1,128]{1,0:T(1,128)S(1)}, f32[1,128]{1,0:T(1,128)S(1)}, f32[1,128]{1,0:T(1,128)S(1)}) custom-call(s32[8]{0:T(128)S(1)} %copy-done.4, s32[8]{0:T(128)S(1)} %collective-permute-done.refs_1_, s32[8]{0:T(128)S(1)} %collective-permute-done.1.refs_2_, s32[8]{0:T(128)S(1)} %collective-permute-done.2.refs_3_, ...), custom_call_target="tpu_custom_call" | custom-call | flops 100663296 | bytes 2097152 | tf_op jit(solution)/shard_map/scores/pallas_call | solution.py:207
  55.2 0.9 %collective-permute-start.11 = (f32[1,128]{1,0:T(1,128)S(1)}, f32[1,128]{1,0:T(1,128)S(1)}, u32[]{:S(2)}, u32[]{:S(2)}) collective-permute-start(f32[1,128]{1,0:T(1,128)S(1)} %get-tuple-element.10), channel_id=1, source_target_pairs={{0,12},{4,0},{8,4},{12,8},{1,13},{5,1},{9,5},{13,9},{2,14},{6,2},{... | collective-permute-start | bytes 1544 | tf_op jit(solution)/shard_map/back/ppermute | solution.py:145
  56.1 1.0 %collective-permute-start.12 = (f32[1,128]{1,0:T(1,128)S(1)}, f32[1,128]{1,0:T(1,128)S(1)}, u32[]{:S(2)}, u32[]{:S(2)}) collective-permute-start(f32[1,128]{1,0:T(1,128)S(1)} %get-tuple-element.11), channel_id=1, source_target_pairs={{0,8},{4,12},{8,0},{12,4},{1,9},{5,13},{9,1},{13,5},{2,10},{6,14},... | collective-permute-start | bytes 1544 | tf_op jit(solution)/shard_map/back/ppermute | solution.py:145
  57.1 0.9 %collective-permute-start.13 = (f32[1,128]{1,0:T(1,128)S(1)}, f32[1,128]{1,0:T(1,128)S(1)}, u32[]{:S(2)}, u32[]{:S(2)}) collective-permute-start(f32[1,128]{1,0:T(1,128)S(1)} %get-tuple-element.12), channel_id=1, source_target_pairs={{0,4},{4,8},{8,12},{12,0},{1,5},{5,9},{9,13},{13,1},{2,6},{6,10},{... | collective-permute-start | bytes 1544 | tf_op jit(solution)/shard_map/back/ppermute | solution.py:145
  58.0 0.8 %collective-permute-done.11 = f32[1,128]{1,0:T(1,128)S(1)} collective-permute-done((f32[1,128]{1,0:T(1,128)S(1)}, f32[1,128]{1,0:T(1,128)S(1)}, u32[]{:S(2)}, u32[]{:S(2)}) %collective-permute-start.11) | collective-permute-done | bytes 544 | tf_op jit(solution)/shard_map/back/ppermute | solution.py:145
  58.8 1.7 %collective-permute-done.12 = f32[1,128]{1,0:T(1,128)S(1)} collective-permute-done((f32[1,128]{1,0:T(1,128)S(1)}, f32[1,128]{1,0:T(1,128)S(1)}, u32[]{:S(2)}, u32[]{:S(2)}) %collective-permute-start.12) | collective-permute-done | bytes 544 | tf_op jit(solution)/shard_map/back/ppermute | solution.py:145
  60.5 1.9 %collective-permute-done.13 = f32[1,128]{1,0:T(1,128)S(1)} collective-permute-done((f32[1,128]{1,0:T(1,128)S(1)}, f32[1,128]{1,0:T(1,128)S(1)}, u32[]{:S(2)}, u32[]{:S(2)}) %collective-permute-start.13) | collective-permute-done | bytes 544 | tf_op jit(solution)/shard_map/back/ppermute | solution.py:145
  62.4 0.5 add_bitcast_fusion
  (2 shorter events, 0.0 us)
Async XLA Ops:
  1.0 12.1 %collective-permute-start.9 = (bf16[64,3072]{1,0:T(8,128)(2,1)S(1)}, bf16[64,3072]{1,0:T(8,128)(2,1)S(1)}, u32[]{:S(2)}, u32[]{:S(2)}) collective-permute-start(bf16[64,3072]{1,0:T(8,128)(2,1)S(1)} %constant_dynamic-slice_fusion), channel_id=1, source_target_pairs={{0,2},{2,0},{1,3},{3,1},{4,6},{6,4},{5,7},{7,5},{8,10},{10,8},{9,1... | collective-permute-start | bytes 1179656 | tf_op jit(solution)/shard_map/item_rows/ppermute | solution.py:145
  13.1 40.4 %collective-permute-start.10 = (bf16[64,3072]{1,0:T(8,128)(2,1)S(1)}, bf16[64,3072]{1,0:T(8,128)(2,1)S(1)}, u32[]{:S(2)}, u32[]{:S(2)}) collective-permute-start(bf16[64,3072]{1,0:T(8,128)(2,1)S(1)} %collective-permute-done.9.refs_13_), channel_id=1, source_target_pairs={{0,1},{1,0},{2,3},{3,2},{4,5},{5,4},{6,7},{7,6},{8,9},{9,8},{10,11... | collective-permute-start | bytes 1179656 | tf_op jit(solution)/shard_map/item_rows/ppermute | solution.py:145
  13.1 6.4 %collective-permute-start = (s32[8]{0:T(128)}, s32[8]{0:T(128)S(1)}, u32[]{:S(2)}, u32[]{:S(2)}) collective-permute-start(s32[8]{0:T(128)} %refs_0_.3), channel_id=1, source_target_pairs={{0,4},{4,8},{8,12},{12,0},{1,5},{5,9},{9,13},{13,1},{2,6},{6,10},{... | collective-permute-start | bytes 104 | tf_op jit(solution)/shard_map/ids/ppermute | solution.py:145
  15.0 5.0 %collective-permute-start.1 = (s32[8]{0:T(128)}, s32[8]{0:T(128)S(1)}, u32[]{:S(2)}, u32[]{:S(2)}) collective-permute-start(s32[8]{0:T(128)} %refs_0_.3), channel_id=1, source_target_pairs={{0,8},{4,12},{8,0},{12,4},{1,9},{5,13},{9,1},{13,5},{2,10},{6,14},... | collective-permute-start | bytes 104 | tf_op jit(solution)/shard_map/ids/ppermute | solution.py:145
  17.6 3.7 %collective-permute-start.2 = (s32[8]{0:T(128)}, s32[8]{0:T(128)S(1)}, u32[]{:S(2)}, u32[]{:S(2)}) collective-permute-start(s32[8]{0:T(128)} %refs_0_.3), channel_id=1, source_target_pairs={{0,12},{4,0},{8,4},{12,8},{1,13},{5,1},{9,5},{13,9},{2,14},{6,2},{... | collective-permute-start | bytes 104 | tf_op jit(solution)/shard_map/ids/ppermute | solution.py:145
  18.9 8.9 %collective-permute-start.6 = (s32[128]{0:T(128)}, s32[128]{0:T(128)S(1)}, u32[]{:S(2)}, u32[]{:S(2)}) collective-permute-start(s32[128]{0:T(128)} %param.6), channel_id=1, source_target_pairs={{0,4},{4,8},{8,12},{12,0},{1,5},{5,9},{9,13},{13,1},{2,6},{6,10},{... | collective-permute-start | bytes 1544 | tf_op jit(solution)/shard_map/ids/ppermute | solution.py:145
  19.6 20.0 %collective-permute-start.7 = (s32[128]{0:T(128)}, s32[128]{0:T(128)S(1)}, u32[]{:S(2)}, u32[]{:S(2)}) collective-permute-start(s32[128]{0:T(128)} %param.6), channel_id=1, source_target_pairs={{0,8},{4,12},{8,0},{12,4},{1,9},{5,13},{9,1},{13,5},{2,10},{6,14},... | collective-permute-start | bytes 1544 | tf_op jit(solution)/shard_map/ids/ppermute | solution.py:145
  21.2 1.1 %copy-start.2 = (bf16[128,3072]{1,0:T(8,128)(2,1)S(1)}, bf16[128,3072]{1,0:T(8,128)(2,1)}, u32[]{:S(2)}) copy-start(bf16[128,3072]{1,0:T(8,128)(2,1)} %refs_4_.1) | copy-start | bytes 2359300
  22.4 0.7 %copy-start.3 = (s32[8]{0:T(128)S(1)}, s32[8]{0:T(128)}, u32[]{:S(2)}) copy-start(s32[8]{0:T(128)} %refs_0_.3) | copy-start | bytes 100
  24.0 29.5 %collective-permute-start.3 = (bf16[16,3072]{1,0:T(8,128)(2,1)S(1)}, bf16[16,3072]{1,0:T(8,128)(2,1)S(1)}, u32[]{:S(2)}, u32[]{:S(2)}) collective-permute-start(bf16[16,3072]{1,0:T(8,128)(2,1)S(1)} %states.1.refs_4_), channel_id=1, source_target_pairs={{0,4},{4,8},{8,12},{12,0},{1,5},{5,9},{9,13},{13,1},{2,6},{6,10},{... | collective-permute-start | bytes 294920 | tf_op jit(solution)/shard_map/states/ppermute | solution.py:145
  26.1 27.4 %collective-permute-start.4 = (bf16[16,3072]{1,0:T(8,128)(2,1)S(1)}, bf16[16,3072]{1,0:T(8,128)(2,1)S(1)}, u32[]{:S(2)}, u32[]{:S(2)}) collective-permute-start(bf16[16,3072]{1,0:T(8,128)(2,1)S(1)} %states.1.refs_4_), channel_id=1, source_target_pairs={{0,8},{4,12},{8,0},{12,4},{1,9},{5,13},{9,1},{13,5},{2,10},{6,14},... | collective-permute-start | bytes 294920 | tf_op jit(solution)/shard_map/states/ppermute | solution.py:145
  27.8 25.7 %collective-permute-start.5 = (bf16[16,3072]{1,0:T(8,128)(2,1)S(1)}, bf16[16,3072]{1,0:T(8,128)(2,1)S(1)}, u32[]{:S(2)}, u32[]{:S(2)}) collective-permute-start(bf16[16,3072]{1,0:T(8,128)(2,1)S(1)} %states.1.refs_4_), channel_id=1, source_target_pairs={{0,12},{4,0},{8,4},{12,8},{1,13},{5,1},{9,5},{13,9},{2,14},{6,2},{... | collective-permute-start | bytes 294920 | tf_op jit(solution)/shard_map/states/ppermute | solution.py:145
  28.6 1.1 %copy-start = (bf16[128,3072]{1,0:T(8,128)(2,1)S(1)}, bf16[128,3072]{1,0:T(8,128)(2,1)}, u32[]{:S(2)}) copy-start(bf16[128,3072]{1,0:T(8,128)(2,1)} %refs_12_.1) | copy-start | bytes 2359300
  29.7 1.6 %copy-start.6 = (bf16[256,64,64]{0,2,1:T(8,128)(2,1)S(1)}, bf16[256,64,64]{0,2,1:T(8,128)(2,1)}, u32[]{:S(2)}) copy-start(bf16[256,64,64]{0,2,1:T(8,128)(2,1)} %param.10) | copy-start | bytes 6291460
  31.3 0.7 %copy-start.7 = (s32[256,2]{0,1:T(2,128)S(1)}, s32[256,2]{0,1:T(2,128)}, u32[]{:S(2)}) copy-start(s32[256,2]{0,1:T(2,128)} %param.11) | copy-start | bytes 6148
  32.0 7.7 %copy-start.5 = (s32[128]{0:T(128)S(1)}, s32[128]{0:T(128)}, u32[]{:S(2)}) copy-start(s32[128]{0:T(128)} %param.6) | copy-start | bytes 1540
  32.0 21.5 %copy-start.1 = (bf16[128,3072]{1,0:T(8,128)(2,1)S(1)}, bf16[128,3072]{1,0:T(8,128)(2,1)}, u32[]{:S(2)}) copy-start(bf16[128,3072]{1,0:T(8,128)(2,1)} %refs_12_.1) | copy-start | bytes 2359300
  32.0 21.6 %copy-start.4 = (s32[8]{0:T(128)S(1)}, s32[8]{0:T(128)}, u32[]{:S(2)}) copy-start(s32[8]{0:T(128)} %refs_0_.3) | copy-start | bytes 100
  39.7 13.8 %collective-permute-start.8 = (s32[128]{0:T(128)S(1)}, s32[128]{0:T(128)S(1)}, u32[]{:S(2)}, u32[]{:S(2)}) collective-permute-start(s32[128]{0:T(128)S(1)} %copy-done.5), channel_id=1, source_target_pairs={{0,12},{4,0},{8,4},{12,8},{1,13},{5,1},{9,5},{13,9},{2,14},{6,2},{... | collective-permute-start | bytes 1544 | tf_op jit(solution)/shard_map/ids/ppermute | solution.py:145
  55.2 3.6 %collective-permute-start.11 = (f32[1,128]{1,0:T(1,128)S(1)}, f32[1,128]{1,0:T(1,128)S(1)}, u32[]{:S(2)}, u32[]{:S(2)}) collective-permute-start(f32[1,128]{1,0:T(1,128)S(1)} %get-tuple-element.10), channel_id=1, source_target_pairs={{0,12},{4,0},{8,4},{12,8},{1,13},{5,1},{9,5},{13,9},{2,14},{6,2},{... | collective-permute-start | bytes 1544 | tf_op jit(solution)/shard_map/back/ppermute | solution.py:145
  56.1 4.4 %collective-permute-start.12 = (f32[1,128]{1,0:T(1,128)S(1)}, f32[1,128]{1,0:T(1,128)S(1)}, u32[]{:S(2)}, u32[]{:S(2)}) collective-permute-start(f32[1,128]{1,0:T(1,128)S(1)} %get-tuple-element.11), channel_id=1, source_target_pairs={{0,8},{4,12},{8,0},{12,4},{1,9},{5,13},{9,1},{13,5},{2,10},{6,14},... | collective-permute-start | bytes 1544 | tf_op jit(solution)/shard_map/back/ppermute | solution.py:145
  57.1 5.3 %collective-permute-start.13 = (f32[1,128]{1,0:T(1,128)S(1)}, f32[1,128]{1,0:T(1,128)S(1)}, u32[]{:S(2)}, u32[]{:S(2)}) collective-permute-start(f32[1,128]{1,0:T(1,128)S(1)} %get-tuple-element.12), channel_id=1, source_target_pairs={{0,4},{4,8},{8,12},{12,0},{1,5},{5,9},{9,13},{13,1},{2,6},{6,10},{... | collective-permute-start | bytes 1544 | tf_op jit(solution)/shard_map/back/ppermute | solution.py:145

commit v2 on v1

v2 whole, which is shorter than its diff:
```python
import functools

import jax
import jax.numpy as jnp
from jax import lax
from jax.experimental import pallas as pl
from jax.experimental.pallas import tpu as pltpu
from jax.sharding import PartitionSpec as P

K = 64
FI = 48
LANES = 128
VMEM_LIMIT = 48 * 1024 * 1024
NT = (((1,), (1,)), ((), ()))
TN = (((0,), (0,)), ((), ()))
NN = (((1,), (0,)), ((), ()))


def dot(a, b, dims, **kw):
    return lax.dot_general(a, b, dims, preferred_element_type=jnp.float32, **kw)


def iota(shape, dim):
    return lax.broadcasted_iota(jnp.int32, shape, dim)


def pair_kernel(fields, items, mats, out, mats_own, rows32, rows16, stacked, sem):
    count = mats_own.shape[2]
    first = pl.multiple_of(lax.axis_index("groups") * count, count)
    copy = pltpu.make_async_copy(mats.at[:, :, pl.ds(first, count)], mats_own, sem)
    copy.start()
    rows = items.shape[0]
    eye = (iota((LANES, LANES), 0) == iota((LANES, LANES), 1)).astype(jnp.bfloat16)
    for t in range(items.shape[1] // LANES):
        turned = dot(eye, items[:, t * LANES:(t + 1) * LANES], NT)
        rows32[t * LANES:(t + 1) * LANES, :] = turned
        rows16[t * LANES:(t + 1) * LANES, :] = turned.astype(jnp.bfloat16)
    copy.wait()
    eye_pairs = (iota((count, count), 0) == iota((count, count), 1)).astype(jnp.bfloat16)
    for k in range(K):
        both = jnp.concatenate([mats_own[k], mats_own[k]], axis=0)
        stacked[pl.ds(k, count, stride=K), :] = dot(eye_pairs, both, NT)

    def one(p, total):
        a = pl.multiple_of(fields[0, first + p] * K, K)
        b = pl.multiple_of(fields[1, first + p] * K, K)
        matrix = stacked[pl.ds(pl.multiple_of(p * K, K), K), :][:, :K].astype(jnp.bfloat16)
        moved = dot(matrix, rows16[pl.ds(b, K), :], NN)
        return total + moved * rows32[pl.ds(a, K), :]

    total = lax.fori_loop(0, count, one, jnp.zeros((K, rows), jnp.float32), unroll=8)
    line = jnp.sum(total, axis=0, keepdims=True)
    mine = iota(out.shape, 0) == lax.axis_index("cache")
    out[...] = jnp.where(mine, jnp.broadcast_to(line, out.shape), 0.0)


def pick_kernel(cap, users, states, out):
    total, readers = users.shape
    own_rows = states.shape[0]
    me = lax.axis_index("shard")
    slots = out.shape[0]
    slot_index = iota((slots, own_rows), 0)
    row_index = iota((slots, own_rows), 1)

    def one(source, chosen):
        taken = jnp.int32(0)
        for r in range(readers):
            user = users[source, r]
            mine = user // own_rows == me
            slot = jnp.where(mine, source * cap + taken, -1)
            taken = taken + mine.astype(jnp.int32)
            chosen = jnp.where((slot_index == slot) & (row_index == user % own_rows), 1.0, chosen)
        return chosen

    chosen = lax.fori_loop(0, total, one, jnp.zeros((slots, own_rows), jnp.float32), unroll=total <= 8)
    out[...] = dot(chosen.astype(jnp.bfloat16), states[...], NN).astype(jnp.bfloat16)


def score_kernel(planes, parts, cap, user_rows, users, cands, states, pairs, *refs):
    items, out, linear = refs[:-2], refs[-2], refs[-1]
    total, readers = users.shape
    width = cands.shape[1]
    me = lax.axis_index("shard")
    plane = lax.axis_index("cache")
    core = lax.axis_index("pair")
    own_rows = items[0].shape[0]
    piece = own_rows // parts
    pair_sums = jnp.sum(pairs[...], axis=0)
    starts, pair_columns = [], []
    placed = 0
    for q in range(planes):
        at = lax.rem(plane - q + planes, planes)
        pair_row = jnp.sum(jnp.where(iota(pair_sums.shape, 0) == at, pair_sums, 0.0), axis=0, keepdims=True)
        for h in range(1 if q == 0 else parts):
            start = 0 if q == 0 else lax.rem(core - h + parts, parts) * piece
            rows = items[0 if q == 0 else 1 + (q - 1) * parts + h]
            count = rows.shape[0]
            linear[placed:placed + count, :] = dot(rows[...], states[...], NT)
            pick = iota((count, own_rows), 0) + start == iota((count, own_rows), 1)
            pair_columns.append(jnp.sum(jnp.where(pick, pair_row, 0.0), axis=1, keepdims=True))
            starts.append(iota((count, 1), 0) + (me * planes + at) * own_rows + start)
            placed += count
    pair_column = jnp.concatenate(pair_columns, axis=0)
    item_ids = jnp.concatenate(starts, axis=0)
    lane = iota((1, width), 1) // (width // readers)

    def one(source, carry):
        slot_row = jnp.zeros((1, width), jnp.int32)
        holders = [users[source, r] // user_rows for r in range(readers)]
        for r, holder in enumerate(holders):
            rank = jnp.int32(0)
            for earlier in holders[:r]:
                rank = rank + (earlier == holder).astype(jnp.int32)
            slot_row = jnp.where(lane == r, (holder * total + source) * cap + rank, slot_row)
        spread = (iota((states.shape[0], width), 0) == slot_row).astype(jnp.float32)
        scores = dot(linear[...], spread, NN, precision=lax.Precision.HIGHEST) + pair_column
        hit = item_ids == cands[pl.ds(source, 1), :]
        out[pl.ds(source, 1), :] = jnp.sum(jnp.where(hit, scores, 0.0), axis=0, keepdims=True)
        return carry

    lax.fori_loop(0, total, one, 0, unroll=total <= 8)


def shift(x, axis, step):
    size = lax.axis_size(axis)
    return lax.ppermute(x, axis, [(s, (s + step) % size) for s in range(size)])


def body(cand_items, reader_users, item_table, user_states, pair_mats, pair_fields):
    total = lax.axis_size("shard")
    planes = lax.axis_size("cache")
    parts = lax.axis_size("pair")
    groups = lax.axis_size("groups")
    half = cand_items.shape[0]
    rows, width = item_table.shape
    readers = reader_users.shape[0]
    cap = 2 * ((readers + total - 1) // total)
    vmem = pl.BlockSpec(memory_space=pltpu.VMEM)
    smem = pl.BlockSpec(memory_space=pltpu.SMEM)
    anywhere = pl.BlockSpec(memory_space=pl.ANY)
    params = pltpu.CompilerParams(vmem_limit_bytes=VMEM_LIMIT)

    with jax.named_scope("ids"):
        users = lax.all_gather(reader_users, "shard", axis=0)
        cands = lax.all_gather(cand_items, "shard", axis=0)

    with jax.named_scope("item_rows"):
        piece = rows // parts
        mine = lax.dynamic_slice_in_dim(item_table, lax.axis_index("pair") * piece, piece, 0)
        items = [item_table]
        for q in range(1, planes):
            crossed = shift(mine, "cache", q)
            items.append(crossed)
            items.extend(shift(crossed, "pair", h) for h in range(1, parts))

    with jax.named_scope("pairs"):
        count = pair_mats.shape[0] // groups
        pair_scores = pl.pallas_call(
            pair_kernel,
            out_shape=jax.ShapeDtypeStruct((planes, rows), jnp.float32),
            in_specs=[smem, vmem, anywhere],
            out_specs=vmem,
            scratch_shapes=[
                pltpu.VMEM((K, K, count), jnp.bfloat16),
                pltpu.VMEM((width, rows), jnp.float32),
                pltpu.VMEM((width, rows), jnp.bfloat16),
                pltpu.VMEM((count * K, LANES), jnp.float32),
                pltpu.SemaphoreType.DMA,
            ],
            compiler_params=params,
            cost_estimate=pl.CostEstimate(flops=2 * count * K * K * rows * 16, bytes_accessed=2 * 1024 * 1024, transcendentals=0),
        )(pair_fields.T, item_table, jnp.transpose(pair_mats, (1, 2, 0)))
        pair_scores = lax.all_gather(pair_scores, ("groups", "cache", "pair"), axis=0)

    with jax.named_scope("states"):
        picked = pl.pallas_call(
            functools.partial(pick_kernel, cap),
            out_shape=jax.ShapeDtypeStruct((total * cap, width), jnp.bfloat16),
            in_specs=[smem, vmem],
            out_specs=vmem,
            compiler_params=params,
            cost_estimate=pl.CostEstimate(flops=2 * total * cap * rows * width, bytes_accessed=1024 * 1024, transcendentals=0),
        )(users, user_states)
        states = lax.all_gather(picked, "shard", axis=0, tiled=True)

    with jax.named_scope("scores"):
        parted = pl.pallas_call(
            functools.partial(score_kernel, planes, parts, cap, user_states.shape[0]),
            out_shape=jax.ShapeDtypeStruct((total, half), jnp.float32),
            in_specs=[smem] + [vmem] * (3 + len(items)),
            out_specs=vmem,
            scratch_shapes=[pltpu.VMEM((planes * rows, total * total * cap), jnp.float32)],
            compiler_params=params,
            cost_estimate=pl.CostEstimate(flops=2 * 64 * 256 * width, bytes_accessed=2 * 1024 * 1024, transcendentals=0),
        )(users, cands, states, pair_scores, *items)

    with jax.named_scope("back"):
        result = lax.all_to_all(parted, "shard", split_axis=0, concat_axis=0, tiled=True)
        return jnp.sum(result, axis=0)


def solution(mesh):
    return jax.shard_map(
        body,
        mesh=mesh,
        in_specs=(
            P(("groups", "shard", "cache", "pair")),
            P(("groups", "shard", "cache", "pair")),
            P(("shard", "cache"), None),
            P(("groups", "shard"), None),
            P("pair", None, None),
            P("pair", None),
        ),
        out_specs=P(("groups", "shard", "cache", "pair")),
        check_vma=False,
    )
```

time: 63.3 us -> 81.9 us (1.29)
  blocking collectives: 11.8 us -> 50 us
  starting transfers between devices: 19.1 us -> 3.01 us
  waiting for transfers between devices: 14.8 us -> 9.12 us
  local copies, waits for them, and re-layouts: 6.22 us -> 7.76 us
    all_gather x0 -> x3, blocking collectives: none -> 33.5 us  [the longest x1 15.3 us: body(): states = lax.all_gather(picked, 'shard', axis=0, tiled=True)]
    ppermute x14 -> x2, starting transfers between devices: 19.1 us -> 3.01 us  [shift(): return lax.ppermute(x, axis, [(s, (s + step) % size) for s in range(size)])]
    psum x1 -> x0, blocking collectives: 11.8 us -> none  [body(): pair_scores = lax.psum(pair_scores, ('groups', 'cache', 'pair'))]
    unnamed x0 -> x1, blocking collectives: none -> 8.69 us
    all_to_all x0 -> x1, blocking collectives: none -> 7.89 us  [body(): lax.all_to_all(parted, 'shard', split_axis=0, concat_axis=0, tiled=True)]
    ppermute x14 -> x2, waiting for transfers between devices: 14.8 us -> 9.12 us  [shift(): return lax.ppermute(x, axis, [(s, (s + step) % size) for s in range(size)])]
    unnamed x16 -> x11, local copies, waits for them, and re-layouts: 5.2 us -> 6.65 us
  transfers between devices with their start and end apart: 14 -> 2, of which waited for: 5 -> 1; matrix products, arithmetic and copies ran while one was open for 0% -> 3% of each run, Pallas kernels for 14% -> 11%
where the time goes in v2:
time: 81.9 us; the launch traced here: 81.5 us
  blocking collectives  50 us (61%)
  Pallas kernels  10.3 us (13%)
  waiting for transfers between devices  9.12 us (11%)
  local copies, waits for them, and re-layouts  7.76 us (9%)
  starting transfers between devices  3.01 us (4%)
    all_gather x1, blocking collectives, body(): states = lax.all_gather(picked, 'shard', axis=0, tiled=True)  15.3 us
    all_gather x1, blocking collectives, body(): cands = lax.all_gather(cand_items, 'shard', axis=0)  9.24 us
    ppermute x2, waiting for transfers between devices, shift(): return lax.ppermute(x, axis, [(s, (s + step) % size) for s in range(size)])  9.12 us
    all_gather x1, blocking collectives, body(): lax.all_gather(pair_scores, ('groups', 'cache', 'pair'), axis=0)  8.9 us
    unnamed x1, blocking collectives  8.69 us
    all_to_all x1, blocking collectives, body(): lax.all_to_all(parted, 'shard', split_axis=0, concat_axis=0, tiled=True)  7.89 us
    pallas_call x1, Pallas kernels, body(): pl.pallas_call(pair_kernel, out_shape=jax.ShapeDtypeStruct((planes, rows)...  7.63 us
    unnamed x11, local copies, waits for them, and re-layouts  6.65 us
  transfers between devices with their start and end apart: 2, of which 1 were waited for; matrix products, arithmetic and copies ran while one was open for 3% of the time, Pallas kernels for 11%

profile of v2, /device:TPU:0, one launch (start us, length us, event | category | flops | bytes accessed | tf_op | source)
XLA Modules:
  0.0 81.5 jit_solution(16254171516992189823)
XLA Ops:
  0.0 1.0 %constant_dynamic-slice_fusion = bf16[64,3072]{1,0:T(8,128)(2,1)S(1)} fusion(bf16[128,3072]{1,0:T(8,128)(2,1)} %refs_0_.1, s32[]{:T(128)S(6)} %select_n.3), kind=kLoop, calls=%fused_computation | loop fusion | bytes 786436 | tf_op jit(solution)/shard_map/item_rows/dynamic_slice | solution.py:149
  1.0 3.0 %collective-permute-start = (bf16[64,3072]{1,0:T(8,128)(2,1)S(1)}, bf16[64,3072]{1,0:T(8,128)(2,1)S(1)}, u32[]{:S(2)}, u32[]{:S(2)}) collective-permute-start(bf16[64,3072]{1,0:T(8,128)(2,1)S(1)} %constant_dynamic-slice_fusion), channel_id=1, source_target_pairs={{0,2},{2,0},{1,3},{3,1},{4,6},{6,4},{5,7},{7,5},{8,10},{10,8},{9,1... | collective-permute-start | bytes 1179656 | tf_op jit(solution)/shard_map/item_rows/ppermute | solution.py:126
  4.0 9.1 %collective-permute-done.refs_1_ = bf16[64,3072]{1,0:T(8,128)(2,1)S(1)} collective-permute-done((bf16[64,3072]{1,0:T(8,128)(2,1)S(1)}, bf16[64,3072]{1,0:T(8,128)(2,1)S(1)}, u32[]{:S(2)}, u32[]{:S(2)}) %collective-permute-start) | collective-permute-done | bytes 393248 | tf_op jit(solution)/shard_map/item_rows/ppermute | solution.py:126
  13.1 0.0 collective-permute-start.1
  13.1 1.2 %dynamic-slice = u32[1]{0:T(128)} dynamic-slice(u32[32]{0:T(128)} %constant.15, u32[]{:T(128)S(6)} %add.4), dynamic_slice_sizes={1} | dynamic-slice | bytes 12
  15.0 0.9 %dynamic-update-slice = s32[32]{0:T(128)S(1)} dynamic-update-slice(s32[32]{0:T(128)S(1)} %broadcast, s32[8]{0:T(128)} %param.7, u32[]{:T(128)} %bitcast) | dynamic-update-slice | bytes 68
  15.9 8.7 %all-reduce = s32[32]{0:T(128)S(1)} all-reduce(s32[32]{0:T(128)S(1)} %dynamic-update-slice), channel_id=2, replica_groups=mesh['groups'=2,'shard'=4,'cache'=2,'pair'=2] {'shard'}, use_global_device_ids=true, to_apply=%add | all-reduce | flops 32 | bytes 256
  24.6 0.1 reshape.2.users
  24.7 9.2 %all-gather.3 = s32[4,1,128]{2,1,0:T(1,128)S(1)} all-gather(s32[1,1,128]{2,1,0:T(1,128)} %bitcast.14), channel_id=3, replica_groups=mesh['groups'=2,'shard'=4,'cache'=2,'pair'=2] {'shard'}, dimensions={0}, use_global_device_ids=true | all-gather | bytes 2560 | tf_op jit(solution)/shard_map/ids/all_gather | solution.py:145
  33.9 0.0 copy-start.1
  33.9 1.1 %copy-done.1 = bf16[128,3072]{1,0:T(8,128)(2,1)S(1)} copy-done((bf16[128,3072]{1,0:T(8,128)(2,1)S(1)}, bf16[128,3072]{1,0:T(8,128)(2,1)}, u32[]{:S(2)}) %copy-start.1) | copy-done | bytes 786456
  35.1 1.0 %states.2 = bf16[16,3072]{1,0:T(8,128)(2,1)S(1)} custom-call(s32[4,8]{1,0:T(4,128)S(1)} %reshape.2.users, bf16[128,3072]{1,0:T(8,128)(2,1)S(1)} %copy-done.1), custom_call_target="tpu_custom_call" | custom-call | flops 12582912 | bytes 1048576 | tf_op jit(solution)/shard_map/states/pallas_call | solution.py:176
  36.0 0.0 copy-start
  36.0 1.1 %copy-done = bf16[128,3072]{1,0:T(8,128)(2,1)S(1)} copy-done((bf16[128,3072]{1,0:T(8,128)(2,1)S(1)}, bf16[128,3072]{1,0:T(8,128)(2,1)}, u32[]{:S(2)}) %copy-start) | copy-done | bytes 786456
  37.2 0.0 copy-start.2
  37.2 1.6 %copy-done.2 = bf16[256,64,64]{0,2,1:T(8,128)(2,1)S(1)} copy-done((bf16[256,64,64]{0,2,1:T(8,128)(2,1)S(1)}, bf16[256,64,64]{0,2,1:T(8,128)(2,1)}, u32[]{:S(2)}) %copy-start.2) | copy-done | bytes 2097176
  38.8 0.0 copy-start.3
  38.8 0.7 copy-done.3
  39.5 7.6 %pairs.1 = f32[2,128]{1,0:T(2,128)S(1)} custom-call(s32[2,256]{1,0:T(2,128)S(1)} %bitcast.13, bf16[128,3072]{1,0:T(8,128)(2,1)S(1)} %copy-done, bf16[64,64,256]{2,1,0:T(8,128)(2,1)S(1)} %bitcast.12), custom_call_target="tpu_custom_call" | custom-call | flops 2147483648 | bytes 2097152 | tf_op jit(solution)/shard_map/pairs/pallas_call | solution.py:158
  47.1 8.9 %all-gather.4.pairs = f32[8,2,128]{2,1,0:T(2,128)S(1)} all-gather(f32[1,2,128]{2,1,0:T(2,128)S(1)} %bitcast.11), channel_id=4, replica_groups=mesh['groups'=2,'shard'=4,'cache'=2,'pair'=2] {'groups','cache','pair'}, dimensions={0}, use_global_device_ids=true | all-gather | bytes 9216 | tf_op jit(solution)/shard_map/pairs/all_gather | solution.py:173
  56.0 15.3 %all_gather.25.states = bf16[64,3072]{1,0:T(8,128)(2,1)S(1)} all-gather(bf16[16,3072]{1,0:T(8,128)(2,1)S(1)} %states.2), channel_id=1, replica_groups=mesh['groups'=2,'shard'=4,'cache'=2,'pair'=2] {'shard'}, dimensions={0}, use_global_device_ids=true | all-gather | bytes 491520 | tf_op jit(solution)/shard_map/states/all_gather | solution.py:184
  71.3 0.0 collective-permute-done.1.refs_2_
  71.3 1.7 %scores.1 = f32[4,128]{1,0:T(4,128)S(1)} custom-call(s32[4,8]{1,0:T(4,128)S(1)} %reshape.2.users, s32[4,128]{1,0:T(4,128)S(1)} %bitcast.9, bf16[64,3072]{1,0:T(8,128)(2,1)S(1)} %all_gather.25.states, f32[8,2,128]{2,1,0:T(2,128)S(1)} %all-gather.4.pairs, bf16[128,3072]{1,0:T(8,128)(2,1)S(1)} %copy-done, bf16[64,3072]{1,0:T(8,128)(2,1)S(1)} %collective-permute-done.refs_1_, ...), custom_call_target="tpu_custom_call" | custom-call | flops 100663296 | bytes 2097152 | tf_op jit(solution)/shard_map/scores/pallas_call | solution.py:187
  73.1 7.9 %all_to_all.9 = f32[4,1,128]{2,1,0:T(1,128)S(1)} all-to-all(f32[4,1,128]{2,1,0:T(1,128)S(1)} %bitcast.10), channel_id=1, replica_groups=mesh['groups'=2,'shard'=4,'cache'=2,'pair'=2] {'shard'}, dimensions={0} | all-to-all | bytes 4096 | tf_op jit(solution)/shard_map/back/all_to_all | solution.py:198
  80.9 0.5 reduce_sum.9
  (1 shorter events, 0.0 us)
Async XLA Ops:
  1.0 12.1 %collective-permute-start = (bf16[64,3072]{1,0:T(8,128)(2,1)S(1)}, bf16[64,3072]{1,0:T(8,128)(2,1)S(1)}, u32[]{:S(2)}, u32[]{:S(2)}) collective-permute-start(bf16[64,3072]{1,0:T(8,128)(2,1)S(1)} %constant_dynamic-slice_fusion), channel_id=1, source_target_pairs={{0,2},{2,0},{1,3},{3,1},{4,6},{6,4},{5,7},{7,5},{8,10},{10,8},{9,1... | collective-permute-start | bytes 1179656 | tf_op jit(solution)/shard_map/item_rows/ppermute | solution.py:126
  13.1 58.2 %collective-permute-start.1 = (bf16[64,3072]{1,0:T(8,128)(2,1)S(1)}, bf16[64,3072]{1,0:T(8,128)(2,1)S(1)}, u32[]{:S(2)}, u32[]{:S(2)}) collective-permute-start(bf16[64,3072]{1,0:T(8,128)(2,1)S(1)} %collective-permute-done.refs_1_), channel_id=1, source_target_pairs={{0,1},{1,0},{2,3},{3,2},{4,5},{5,4},{6,7},{7,6},{8,9},{9,8},{10,11... | collective-permute-start | bytes 1179656 | tf_op jit(solution)/shard_map/item_rows/ppermute | solution.py:126
  33.9 1.1 %copy-start.1 = (bf16[128,3072]{1,0:T(8,128)(2,1)S(1)}, bf16[128,3072]{1,0:T(8,128)(2,1)}, u32[]{:S(2)}) copy-start(bf16[128,3072]{1,0:T(8,128)(2,1)} %states.3) | copy-start | bytes 2359300
  36.0 1.2 %copy-start = (bf16[128,3072]{1,0:T(8,128)(2,1)S(1)}, bf16[128,3072]{1,0:T(8,128)(2,1)}, u32[]{:S(2)}) copy-start(bf16[128,3072]{1,0:T(8,128)(2,1)} %refs_0_.1) | copy-start | bytes 2359300
  37.2 1.6 %copy-start.2 = (bf16[256,64,64]{0,2,1:T(8,128)(2,1)S(1)}, bf16[256,64,64]{0,2,1:T(8,128)(2,1)}, u32[]{:S(2)}) copy-start(bf16[256,64,64]{0,2,1:T(8,128)(2,1)} %param.10) | copy-start | bytes 6291460
  38.8 0.7 copy-start.3

commit v3 on v2

v3 whole, which is shorter than its diff:
```python
import functools

import jax
import jax.numpy as jnp
from jax import lax
from jax.experimental import pallas as pl
from jax.experimental.pallas import tpu as pltpu
from jax.sharding import PartitionSpec as P

K = 64
LANES = 128
PITCH = 72
CODE = 128
VMEM_LIMIT = 40 * 1024 * 1024
NT = (((1,), (1,)), ((), ()))
NN = (((1,), (0,)), ((), ()))


def dot(a, b, dims, **kw):
    return lax.dot_general(a, b, dims, preferred_element_type=jnp.float32, **kw)


def iota(shape, dim):
    return lax.broadcasted_iota(jnp.int32, shape, dim)


def ring(index, size):
    return lax.rem(index + size, size)


def pick_kernel(total, cap, *refs):
    users, (own_users, cands, states_hbm, out, held, own, sems) = refs[:total - 1], refs[total - 1:]
    copies = [
        pltpu.make_async_copy(own_users, own, sems.at[0]),
        pltpu.make_async_copy(states_hbm, held, sems.at[1]),
    ]
    for copy in copies:
        copy.start()
    width = held.shape[1]
    code = cands[...]
    digits = jnp.where(iota((out.shape[0], code.shape[1]), 0) == 0, code // CODE, code % CODE)
    out[:, width:] = jnp.where(iota(digits.shape, 0) < 2, digits, 0).astype(jnp.float32).astype(jnp.bfloat16)
    copies[0].wait()
    own_rows = held.shape[0]
    me = lax.axis_index("shard")
    slots = out.shape[0]
    slot_index = iota((slots, own_rows), 0)
    row_index = iota((slots, own_rows), 1)
    chosen = jnp.zeros((slots, own_rows), jnp.float32)
    for j, line in enumerate((own,) + tuple(users)):
        source = ring(me - j, total)
        taken = jnp.int32(0)
        for r in range(line.shape[0]):
            user = line[r]
            mine = user // own_rows == me
            slot = jnp.where(mine, source * cap + taken, -1)
            taken = taken + mine.astype(jnp.int32)
            chosen = jnp.where((slot_index == slot) & (row_index == user % own_rows), 1.0, chosen)
    chosen = chosen.astype(jnp.bfloat16)
    copies[1].wait()
    out[:, :width] = dot(chosen, held[...], NN).astype(jnp.bfloat16)


def pair_kernel(fields_hbm, items_hbm, mats_hbm, picked, crossed, out, passed, fields, items, mats, rows32, rows16, stacked, sems):
    del picked, crossed, passed
    copies = [
        pltpu.make_async_copy(items_hbm, items, sems.at[0]),
        pltpu.make_async_copy(mats_hbm, mats, sems.at[1]),
        pltpu.make_async_copy(fields_hbm, fields, sems.at[2]),
    ]
    for copy in copies:
        copy.start()
    count = mats.shape[2]
    eye = (iota((LANES, LANES), 0) == iota((LANES, LANES), 1)).astype(jnp.bfloat16)
    copies[0].wait()
    for t in range(items.shape[1] // LANES):
        turned = dot(eye, items[:, t * LANES:(t + 1) * LANES], NT)
        rows32[t * LANES:(t + 1) * LANES, :] = turned
        rows16[t * LANES:(t + 1) * LANES, :] = turned.astype(jnp.bfloat16)
    eye_pairs = (iota((count, count), 0) == iota((count, count), 1)).astype(jnp.bfloat16)
    side = (iota((count, LANES), 0) % 2 == 0) == (iota((count, LANES), 1) < K)
    copies[1].wait()
    for k in range(K):
        both = jnp.concatenate([mats[k], mats[k]], axis=0)
        stacked[pl.ds(k, count, stride=PITCH), :] = jnp.where(side, dot(eye_pairs, both, NT), 0.0)
    copies[2].wait()

    def two(step, total):
        first = step * 2
        lefts, rights, mults = [], [], []
        for p in (first, first + 1):
            a = pl.multiple_of(fields[0, p] * K, K)
            b = pl.multiple_of(fields[1, p] * K, K)
            lefts.append(stacked[pl.ds(pl.multiple_of(p * PITCH, 8), K), :].astype(jnp.bfloat16))
            rights.append(rows16[pl.ds(b, K), :])
            mults.append(rows32[pl.ds(a, K), :])
        moved = dot(jnp.concatenate(lefts, axis=0), jnp.concatenate(rights, axis=0), NN)
        return total + moved * jnp.concatenate(mults, axis=0)

    total = lax.fori_loop(0, count // 2, two, jnp.zeros((2 * K, items.shape[0]), jnp.float32), unroll=16)
    out[...] = jnp.sum(total, axis=0, keepdims=True)


def score_kernel(total, planes, parts, cap, user_rows, *refs):
    users, refs = refs[:total], refs[total:]
    states, refs = refs[:total], refs[total:]
    pairs, refs = refs[:planes * parts], refs[planes * parts:]
    items, refs = refs[:1 + (planes - 1) * parts], refs[1 + (planes - 1) * parts:]
    outs, (asked, wanted, cands, linear, rows_out) = refs[:total], refs[total:]
    readers = users[0].shape[0]
    slots = states[0].shape[0]
    width = items[0].shape[1]
    half = outs[0].shape[1]
    me = lax.axis_index("shard")
    plane = lax.axis_index("cache")
    core = lax.axis_index("pair")
    for j in range(total):
        for r in range(readers):
            asked[j, r] = users[j][r]
        wanted[j * slots:(j + 1) * slots, :] = states[j][:, :width]
        digits = states[j][:, width:].astype(jnp.float32)
        place = iota(digits.shape, 0)
        weight = jnp.where(place == 0, float(CODE), jnp.where(place == 1, 1.0, 0.0))
        cands[j:j + 1, :] = jnp.sum(digits * weight, axis=0, keepdims=True).astype(jnp.int32)
    own_rows = items[0].shape[0]
    piece = own_rows // parts
    starts, pair_columns = [], []
    placed = 0
    for q in range(planes):
        at = ring(plane - q, planes)
        pair_row = sum(pairs[q * parts + h][...] for h in range(parts))
        for h in range(1 if q == 0 else parts):
            start = 0 if q == 0 else ring(core - h, parts) * piece
            rows = items[0 if q == 0 else 1 + (q - 1) * parts + h]
            count = rows.shape[0]
            linear[placed:placed + count, :] = dot(rows[...], wanted[...], NT)
            pick = iota((count, own_rows), 0) + start == iota((count, own_rows), 1)
            pair_columns.append(jnp.sum(jnp.where(pick, pair_row, 0.0), axis=1, keepdims=True))
            starts.append(iota((count, 1), 0) + (me * planes + at) * own_rows + start)
            placed += count
    pair_column = jnp.concatenate(pair_columns, axis=0)
    item_ids = jnp.concatenate(starts, axis=0)
    lane = iota((1, half), 1) // (half // readers)

    def one(j, carry):
        source = ring(me - j, total)
        slot_row = jnp.zeros((1, half), jnp.int32)
        holders = [asked[j, r] // user_rows for r in range(readers)]
        for r, holder in enumerate(holders):
            rank = jnp.int32(0)
            for earlier in holders[:r]:
                rank = rank + (earlier == holder).astype(jnp.int32)
            slot_row = jnp.where(lane == r, ring(me - holder, total) * slots + source * cap + rank, slot_row)
        spread = (iota((wanted.shape[0], half), 0) == slot_row).astype(jnp.float32)
        scores = dot(linear[...], spread, NN, precision=lax.Precision.HIGHEST) + pair_column
        hit = item_ids == cands[pl.ds(j, 1), :]
        rows_out[pl.ds(j, 1), :] = jnp.sum(jnp.where(hit, scores, 0.0), axis=0, keepdims=True)
        return carry

    lax.fori_loop(0, total, one, 0, unroll=total <= 8)
    for j in range(total):
        outs[j][...] = rows_out[j:j + 1, :]


def shift(x, axis, step):
    size = lax.axis_size(axis)
    return lax.ppermute(x, axis, [(s, (s + step) % size) for s in range(size)])


def body(cand_items, reader_users, item_table, user_states, pair_mats, pair_fields):
    total = lax.axis_size("shard")
    planes = lax.axis_size("cache")
    parts = lax.axis_size("pair")
    half = cand_items.shape[0]
    rows, width = item_table.shape
    readers = reader_users.shape[0]
    cap = 2 * ((readers + total - 1) // total)
    slots = -(-total * cap // 16) * 16
    count = pair_mats.shape[0]
    vmem = pl.BlockSpec(memory_space=pltpu.VMEM)
    smem = pl.BlockSpec(memory_space=pltpu.SMEM)
    hbm = pl.BlockSpec(memory_space=pltpu.HBM)
    anywhere = pl.BlockSpec(memory_space=pl.ANY)
    params = pltpu.CompilerParams(vmem_limit_bytes=VMEM_LIMIT)

    with jax.named_scope("ids"):
        others = [shift(reader_users, "shard", j) for j in range(1, total)]
        users = [reader_users] + others

    with jax.named_scope("item_rows"):
        piece = rows // parts
        mine = lax.dynamic_slice_in_dim(item_table, lax.axis_index("pair") * piece, piece, 0)
        crossed = [shift(mine, "cache", q) for q in range(1, planes)]

    with jax.named_scope("states"):
        picked = pl.pallas_call(
            functools.partial(pick_kernel, total, cap),
            out_shape=jax.ShapeDtypeStruct((slots, width + half), jnp.bfloat16),
            in_specs=[smem] * (total - 1) + [hbm, vmem, hbm],
            out_specs=vmem,
            scratch_shapes=[
                pltpu.VMEM(user_states.shape, jnp.bfloat16),
                pltpu.SMEM((readers,), jnp.int32),
                pltpu.SemaphoreType.DMA((2,)),
            ],
            compiler_params=params,
            cost_estimate=pl.CostEstimate(flops=2 * slots * rows * width, bytes_accessed=1024 * 1024, transcendentals=0),
        )(*others, reader_users, cand_items.reshape(1, half), user_states)
        states = [picked] + [shift(picked, "shard", j) for j in range(1, total)]

    with jax.named_scope("pairs"):
        pair_scores, passed = pl.pallas_call(
            pair_kernel,
            out_shape=(
                jax.ShapeDtypeStruct((1, rows), jnp.float32),
                jax.ShapeDtypeStruct(crossed[0].shape, crossed[0].dtype),
            ),
            in_specs=[hbm, hbm, hbm, anywhere, anywhere],
            out_specs=(vmem, anywhere),
            input_output_aliases={4: 1},
            scratch_shapes=[
                pltpu.SMEM((2, count), jnp.int32),
                pltpu.VMEM((rows, width), jnp.bfloat16),
                pltpu.VMEM((K, K, count), jnp.bfloat16),
                pltpu.VMEM((width, rows), jnp.float32),
                pltpu.VMEM((width, rows), jnp.bfloat16),
                pltpu.VMEM((count * PITCH, LANES), jnp.float32),
                pltpu.SemaphoreType.DMA((3,)),
            ],
            compiler_params=params,
            cost_estimate=pl.CostEstimate(flops=2 * count * K * K * rows * 16, bytes_accessed=4 * 1024 * 1024, transcendentals=0),
        )(pair_fields.T, item_table, jnp.transpose(pair_mats, (1, 2, 0)), picked, crossed[0])
        crossed[0] = passed
        items = [item_table]
        pairs = []
        for q in range(planes):
            moved = pair_scores if q == 0 else shift(pair_scores, "cache", q)
            pairs.append(moved)
            if q:
                items.append(crossed[q - 1])
            for h in range(1, parts):
                steps = [((c, d), ((c + q) % planes, (d + h) % parts)) for c in range(planes) for d in range(parts)]
                perm = [(c * parts + d, e * parts + f) for (c, d), (e, f) in steps]
                pairs.append(lax.ppermute(pair_scores, ("cache", "pair"), perm))
                if q:
                    items.append(shift(crossed[q - 1], "pair", h))

    with jax.named_scope("scores"):
        outs = pl.pallas_call(
            functools.partial(score_kernel, total, planes, parts, cap, user_states.shape[0]),
            out_shape=[jax.ShapeDtypeStruct((1, half), jnp.float32)] * total,
            in_specs=[smem] * total + [vmem] * (total + len(pairs) + len(items)),
            out_specs=[vmem] * total,
            scratch_shapes=[
                pltpu.SMEM((total, readers), jnp.int32),
                pltpu.VMEM((total * slots, width), jnp.bfloat16),
                pltpu.VMEM((-(-total // 8) * 8, half), jnp.int32),
                pltpu.VMEM((planes * rows, total * slots), jnp.float32),
                pltpu.VMEM((-(-total // 8) * 8, half), jnp.float32),
            ],
            compiler_params=params,
            cost_estimate=pl.CostEstimate(flops=2 * 64 * 256 * width, bytes_accessed=2 * 1024 * 1024, transcendentals=0),
        )(*users, *states, *pairs, *items)

    with jax.named_scope("back"):
        result = outs[0]
        for j in range(1, total):
            result = result + shift(outs[j], "shard", -j)
    return result.reshape(half)


def solution(mesh):
    return jax.shard_map(
        body,
        mesh=mesh,
        in_specs=(
            P(("groups", "shard", "cache", "pair")),
            P(("groups", "shard", "cache", "pair")),
            P(("shard", "cache"), None),
            P(("groups", "shard"), None),
            P("pair", None, None),
            P("pair", None),
        ),
        out_specs=P(("groups", "shard", "cache", "pair")),
        check_vma=False,
    )
```

time: 81.9 us -> 47.8 us (0.58)
  blocking collectives: 50 us -> 0 us
  starting transfers between devices: 3.01 us -> 14.5 us
  waiting for transfers between devices: 9.12 us -> 16.5 us
  Pallas kernels: 10.3 us -> 8.98 us
  local copies, waits for them, and re-layouts: 7.76 us -> 6.87 us
    all_gather x3 -> x0, blocking collectives: 33.5 us -> none  [the longest x1 15.3 us: body(): states = lax.all_gather(picked, 'shard', axis=0, tiled=True)]
    ppermute x2 -> x12, starting transfers between devices: 3.01 us -> 14.5 us  [shift(): return lax.ppermute(x, axis, [(s, (s + step) % size) for s in range(size)])]
    unnamed x1 -> x0, blocking collectives: 8.69 us -> none
    all_to_all x1 -> x0, blocking collectives: 7.89 us -> none  [body(): lax.all_to_all(parted, 'shard', split_axis=0, concat_axis=0, tiled=True)]
    ppermute x2 -> x12, waiting for transfers between devices: 9.12 us -> 15.4 us  [shift(): return lax.ppermute(x, axis, [(s, (s + step) % size) for s in range(size)])]
    pallas_call x3, Pallas kernels: 10.3 us -> 8.98 us  [the longest x1 5.64 us: body(): pl.pallas_call(pair_kernel, out_shape=(jax.ShapeDtypeStruct((1, rows), jn...]
    ppermute x0 -> x2, waiting for transfers between devices: none -> 1.1 us  [body(): pairs.append(lax.ppermute(pair_scores, ('cache', 'pair'), perm))]
    unnamed x11 -> x14, local copies, waits for them, and re-layouts: 6.65 us -> 5.85 us
  transfers between devices with their start and end apart: 2 -> 14, of which waited for: 1 -> 9; matrix products, arithmetic and copies ran while one was open for 3% -> 0% of each run, Pallas kernels for 11% -> 3%
where the time goes in v3:
time: 47.8 us; the launch traced here: 47.4 us
  waiting for transfers between devices  16.5 us (35%)
  starting transfers between devices  14.5 us (30%)
  Pallas kernels  8.98 us (19%)
  local copies, waits for them, and re-layouts  6.87 us (14%)
  other arithmetic  0.52 us (1%)
    ppermute x12, waiting for transfers between devices, shift(): return lax.ppermute(x, axis, [(s, (s + step) % size) for s in range(size)])  15.4 us
    ppermute x12, starting transfers between devices, shift(): return lax.ppermute(x, axis, [(s, (s + step) % size) for s in range(size)])  14.5 us
    unnamed x14, local copies, waits for them, and re-layouts  5.85 us
    pallas_call x1, Pallas kernels, body(): pl.pallas_call(pair_kernel, out_shape=(jax.ShapeDtypeStruct((1, rows), jn...  5.64 us
    pallas_call x1, Pallas kernels, body(): pl.pallas_call(functools.partial(score_kernel, total, planes, parts, cap,...  1.77 us
    pallas_call x1, Pallas kernels, body(): pl.pallas_call(functools.partial(pick_kernel, total, cap), out_shape=jax....  1.57 us
    ppermute x2, waiting for transfers between devices, body(): pairs.append(lax.ppermute(pair_scores, ('cache', 'pair'), perm))  1.1 us
    dynamic_slice x1, local copies, waits for them, and re-layouts, body(): lax.dynamic_slice_in_dim(item_table, lax.axis_index('pair') * piece, piec...  1.02 us
  transfers between devices with their start and end apart: 14, of which 9 were waited for; matrix products, arithmetic and copies ran while one was open for 0% of the time, Pallas kernels for 3%

profile of v3, /device:TPU:0, one launch (start us, length us, event | category | flops | bytes accessed | tf_op | source)
XLA Modules:
  0.0 47.4 jit_solution(17839129895518157094)
XLA Ops:
  0.0 1.0 %constant_dynamic-slice_fusion = bf16[64,3072]{1,0:T(8,128)(2,1)S(1)} fusion(bf16[128,3072]{1,0:T(8,128)(2,1)} %refs_12_.1, s32[]{:T(128)S(6)} %select_n.3), kind=kLoop, calls=%fused_computation.1 | loop fusion | bytes 786436 | tf_op jit(solution)/shard_map/item_rows/dynamic_slice | solution.py:192
  1.0 3.0 %collective-permute-start.6 = (bf16[64,3072]{1,0:T(8,128)(2,1)S(1)}, bf16[64,3072]{1,0:T(8,128)(2,1)S(1)}, u32[]{:S(2)}, u32[]{:S(2)}) collective-permute-start(bf16[64,3072]{1,0:T(8,128)(2,1)S(1)} %constant_dynamic-slice_fusion), channel_id=1, source_target_pairs={{0,2},{2,0},{1,3},{3,1},{4,6},{6,4},{5,7},{7,5},{8,10},{10,8},{9,1... | collective-permute-start | bytes 1179656 | tf_op jit(solution)/shard_map/item_rows/ppermute | solution.py:167
  4.0 3.6 %collective-permute-start.2 = (s32[8]{0:T(128)}, s32[8]{0:T(128)S(1)}, u32[]{:S(2)}, u32[]{:S(2)}) collective-permute-start(s32[8]{0:T(128)} %refs_0_.1), channel_id=1, source_target_pairs={{0,12},{4,0},{8,4},{12,8},{1,13},{5,1},{9,5},{13,9},{2,14},{6,2},{... | collective-permute-start | bytes 104 | tf_op jit(solution)/shard_map/ids/ppermute | solution.py:167
  7.6 0.0 collective-permute-start.1
  7.6 1.0 %collective-permute-start = (s32[8]{0:T(128)}, s32[8]{0:T(128)S(1)}, u32[]{:S(2)}, u32[]{:S(2)}) collective-permute-start(s32[8]{0:T(128)} %refs_0_.1), channel_id=1, source_target_pairs={{0,4},{4,8},{8,12},{12,0},{1,5},{5,9},{9,13},{13,1},{2,6},{6,10},{... | collective-permute-start | bytes 104 | tf_op jit(solution)/shard_map/ids/ppermute | solution.py:167
  8.6 0.4 collective-permute-done.2.refs_2_.refs_3_
  9.1 3.1 %collective-permute-done.1.refs_1_.refs_2_ = s32[8]{0:T(128)S(1)} collective-permute-done((s32[8]{0:T(128)}, s32[8]{0:T(128)S(1)}, u32[]{:S(2)}, u32[]{:S(2)}) %collective-permute-start.1) | collective-permute-done | bytes 64 | tf_op jit(solution)/shard_map/ids/ppermute | solution.py:167
  12.2 0.9 %collective-permute-done.refs_0_.refs_1_ = s32[8]{0:T(128)S(1)} collective-permute-done((s32[8]{0:T(128)}, s32[8]{0:T(128)S(1)}, u32[]{:S(2)}, u32[]{:S(2)}) %collective-permute-start) | collective-permute-done | bytes 64 | tf_op jit(solution)/shard_map/ids/ppermute | solution.py:167
  13.1 0.0 copy-start.2
  13.1 1.1 %copy-done.2 = bf16[128,3072]{1,0:T(8,128)(2,1)S(1)} copy-done((bf16[128,3072]{1,0:T(8,128)(2,1)S(1)}, bf16[128,3072]{1,0:T(8,128)(2,1)}, u32[]{:S(2)}) %copy-start.2) | copy-done | bytes 786456
  14.2 0.0 copy-start.3
  14.2 0.7 %copy-done.3 = s32[8]{0:T(128)S(1)} copy-done((s32[8]{0:T(128)S(1)}, s32[8]{0:T(128)}, u32[]{:S(2)}) %copy-start.3) | copy-done | bytes 56
  14.9 0.0 copy-start.4
  14.9 0.7 %copy-done.4 = s32[128]{0:T(128)S(1)} copy-done((s32[128]{0:T(128)S(1)}, s32[128]{0:T(128)}, u32[]{:S(2)}) %copy-start.4) | copy-done | bytes 536
  15.6 1.6 %states.1.picked.refs_4_ = bf16[16,3200]{1,0:T(8,128)(2,1)S(1)} custom-call(s32[8]{0:T(128)S(1)} %collective-permute-done.refs_0_.refs_1_, s32[8]{0:T(128)S(1)} %collective-permute-done.1.refs_1_.refs_2_, s32[8]{0:T(128)S(1)} %collective-permute-done.2.refs_2_.refs_3_, s32[8]{0:T(128)S(1)} %copy-done.3, s32[1,128]{1,0:T(1,128)S(1)} %bitcast.5, ...), custom_call_target="tpu_custom_call" | custom-call | flops 12582912 | bytes 1048576 | tf_op jit(solution)/shard_map/states/pallas_call | solution.py:196
  17.1 0.0 collective-permute-done.6.crossed
  17.1 0.0 copy-start
  17.2 1.1 %copy-done = bf16[128,3072]{1,0:T(8,128)(2,1)S(1)} copy-done((bf16[128,3072]{1,0:T(8,128)(2,1)S(1)}, bf16[128,3072]{1,0:T(8,128)(2,1)}, u32[]{:S(2)}) %copy-start) | copy-done | bytes 786456
  18.3 0.0 copy-start.5
  18.3 1.6 %copy-done.5 = bf16[256,64,64]{0,2,1:T(8,128)(2,1)S(1)} copy-done((bf16[256,64,64]{0,2,1:T(8,128)(2,1)S(1)}, bf16[256,64,64]{0,2,1:T(8,128)(2,1)}, u32[]{:S(2)}) %copy-start.5) | copy-done | bytes 2097176
  19.9 0.0 copy-start.6
  19.9 0.7 %copy-done.6 = s32[256,2]{0,1:T(2,128)S(1)} copy-done((s32[256,2]{0,1:T(2,128)S(1)}, s32[256,2]{0,1:T(2,128)}, u32[]{:S(2)}) %copy-start.6) | copy-done | bytes 2072
  20.6 0.0 copy-start.1
  20.6 5.6 %pairs.1 = (f32[1,128]{1,0:T(1,128)S(1)}, bf16[64,3072]{1,0:T(8,128)(2,1)S(1)}) custom-call(s32[2,256]{1,0:T(2,128)S(1)} %bitcast.7, bf16[128,3072]{1,0:T(8,128)(2,1)S(1)} %copy-done, bf16[64,64,256]{2,1,0:T(8,128)(2,1)S(1)} %bitcast.6, bf16[16,3200]{1,0:T(8,128)(2,1)S(1)} %states.1.picked.refs_4_, ...), custom_call_target="tpu_custom_call", output_to_operand_aliasing={{1}: (4, {})} | custom-call | flops 4294967296 | bytes 4194304 | tf_op jit(solution)/shard_map/pairs/pallas_call | solution.py:212
  26.2 0.1 collective-permute-start.10
  26.3 0.6 %collective-permute-start.5 = (bf16[16,3200]{1,0:T(8,128)(2,1)S(1)}, bf16[16,3200]{1,0:T(8,128)(2,1)S(1)}, u32[]{:S(2)}, u32[]{:S(2)}) collective-permute-start(bf16[16,3200]{1,0:T(8,128)(2,1)S(1)} %states.1.picked.refs_4_), channel_id=1, source_target_pairs={{0,12},{4,0},{8,4},{12,8},{1,13},{5,1},{9,5},{13,9},{2,14},{6,2},{... | collective-permute-start | bytes 307208 | tf_op jit(solution)/shard_map/states/ppermute | solution.py:167
  26.9 0.6 %collective-permute-start.4 = (bf16[16,3200]{1,0:T(8,128)(2,1)S(1)}, bf16[16,3200]{1,0:T(8,128)(2,1)S(1)}, u32[]{:S(2)}, u32[]{:S(2)}) collective-permute-start(bf16[16,3200]{1,0:T(8,128)(2,1)S(1)} %states.1.picked.refs_4_), channel_id=1, source_target_pairs={{0,8},{4,12},{8,0},{12,4},{1,9},{5,13},{9,1},{13,5},{2,10},{6,14},... | collective-permute-start | bytes 307208 | tf_op jit(solution)/shard_map/states/ppermute | solution.py:167
  27.6 1.9 %collective-permute-start.3 = (bf16[16,3200]{1,0:T(8,128)(2,1)S(1)}, bf16[16,3200]{1,0:T(8,128)(2,1)S(1)}, u32[]{:S(2)}, u32[]{:S(2)}) collective-permute-start(bf16[16,3200]{1,0:T(8,128)(2,1)S(1)} %states.1.picked.refs_4_), channel_id=1, source_target_pairs={{0,4},{4,8},{8,12},{12,0},{1,5},{5,9},{9,13},{13,1},{2,6},{6,10},{... | collective-permute-start | bytes 307208 | tf_op jit(solution)/shard_map/states/ppermute | solution.py:167
  29.5 0.0 collective-permute-start.9
  29.5 3.3 %collective-permute-done.5.refs_7_ = bf16[16,3200]{1,0:T(8,128)(2,1)S(1)} collective-permute-done((bf16[16,3200]{1,0:T(8,128)(2,1)S(1)}, bf16[16,3200]{1,0:T(8,128)(2,1)S(1)}, u32[]{:S(2)}, u32[]{:S(2)}) %collective-permute-start.5) | collective-permute-done | bytes 102432 | tf_op jit(solution)/shard_map/states/ppermute | solution.py:167
  32.8 0.5 %collective-permute-start.8 = (f32[1,128]{1,0:T(1,128)S(1)}, f32[1,128]{1,0:T(1,128)S(1)}, u32[]{:S(2)}, u32[]{:S(2)}) collective-permute-start(f32[1,128]{1,0:T(1,128)S(1)} %get-tuple-element.11.refs_8_), channel_id=1, source_target_pairs={{0,2},{2,0},{1,3},{3,1},{4,6},{6,4},{5,7},{7,5},{8,10},{10,8},{9,1... | collective-permute-start | bytes 1544 | tf_op jit(solution)/shard_map/pairs/ppermute | solution.py:167
  33.4 4.2 %collective-permute-done.4.refs_6_ = bf16[16,3200]{1,0:T(8,128)(2,1)S(1)} collective-permute-done((bf16[16,3200]{1,0:T(8,128)(2,1)S(1)}, bf16[16,3200]{1,0:T(8,128)(2,1)S(1)}, u32[]{:S(2)}, u32[]{:S(2)}) %collective-permute-start.4) | collective-permute-done | bytes 102432 | tf_op jit(solution)/shard_map/states/ppermute | solution.py:167
  37.5 0.0 collective-permute-start.7
  37.5 0.0 collective-permute-done.3.refs_5_
  37.5 0.0 collective-permute-done.9.refs_11_
  37.6 0.0 collective-permute-done.8.refs_10_
  37.6 1.1 %collective-permute-done.7.refs_9_ = f32[1,128]{1,0:T(1,128)S(1)} collective-permute-done((f32[1,128]{1,0:T(1,128)S(1)}, f32[1,128]{1,0:T(1,128)S(1)}, u32[]{:S(2)}, u32[]{:S(2)}) %collective-permute-start.7) | collective-permute-done | bytes 544 | tf_op jit(solution)/shard_map/pairs/ppermute | solution.py:244
  38.7 0.0 collective-permute-done.10.refs_14_
  38.7 0.0 copy-done.1
  38.7 1.8 %scores.1 = (f32[1,128]{1,0:T(1,128)S(1)}, f32[1,128]{1,0:T(1,128)S(1)}, f32[1,128]{1,0:T(1,128)S(1)}, f32[1,128]{1,0:T(1,128)S(1)}) custom-call(s32[8]{0:T(128)S(1)} %copy-done.3, s32[8]{0:T(128)S(1)} %collective-permute-done.refs_0_.refs_1_, s32[8]{0:T(128)S(1)} %collective-permute-done.1.refs_1_.refs_2_, s32[8]{0:T(128)S(1)} %collective-permute-done.2.refs_2_.refs_3_, ...), custom_call_target="tpu_custom_call" | custom-call | flops 100663296 | bytes 2097152 | tf_op jit(solution)/shard_map/scores/pallas_call | solution.py:249
  40.4 0.9 %collective-permute-start.11 = (f32[1,128]{1,0:T(1,128)S(1)}, f32[1,128]{1,0:T(1,128)S(1)}, u32[]{:S(2)}, u32[]{:S(2)}) collective-permute-start(f32[1,128]{1,0:T(1,128)S(1)} %get-tuple-element.14), channel_id=1, source_target_pairs={{0,12},{4,0},{8,4},{12,8},{1,13},{5,1},{9,5},{13,9},{2,14},{6,2},{... | collective-permute-start | bytes 1544 | tf_op jit(solution)/shard_map/back/ppermute | solution.py:167
  41.4 0.2 collective-permute-start.12
  41.6 1.9 %collective-permute-start.13 = (f32[1,128]{1,0:T(1,128)S(1)}, f32[1,128]{1,0:T(1,128)S(1)}, u32[]{:S(2)}, u32[]{:S(2)}) collective-permute-start(f32[1,128]{1,0:T(1,128)S(1)} %get-tuple-element.16), channel_id=1, source_target_pairs={{0,4},{4,8},{8,12},{12,0},{1,5},{5,9},{9,13},{13,1},{2,6},{6,10},{... | collective-permute-start | bytes 1544 | tf_op jit(solution)/shard_map/back/ppermute | solution.py:167
  43.5 0.5 %collective-permute-done.11 = f32[1,128]{1,0:T(1,128)S(1)} collective-permute-done((f32[1,128]{1,0:T(1,128)S(1)}, f32[1,128]{1,0:T(1,128)S(1)}, u32[]{:S(2)}, u32[]{:S(2)}) %collective-permute-start.11) | collective-permute-done | bytes 544 | tf_op jit(solution)/shard_map/back/ppermute | solution.py:167
  44.0 1.8 %collective-permute-done.12 = f32[1,128]{1,0:T(1,128)S(1)} collective-permute-done((f32[1,128]{1,0:T(1,128)S(1)}, f32[1,128]{1,0:T(1,128)S(1)}, u32[]{:S(2)}, u32[]{:S(2)}) %collective-permute-start.12) | collective-permute-done | bytes 544 | tf_op jit(solution)/shard_map/back/ppermute | solution.py:167
  45.8 1.1 %collective-permute-done.13 = f32[1,128]{1,0:T(1,128)S(1)} collective-permute-done((f32[1,128]{1,0:T(1,128)S(1)}, f32[1,128]{1,0:T(1,128)S(1)}, u32[]{:S(2)}, u32[]{:S(2)}) %collective-permute-start.13) | collective-permute-done | bytes 544 | tf_op jit(solution)/shard_map/back/ppermute | solution.py:167
  46.9 0.5 %add_bitcast_fusion = f32[128]{0:T(128)} fusion(f32[1,128]{1,0:T(1,128)S(1)} %collective-permute-done.13, f32[1,128]{1,0:T(1,128)S(1)} %collective-permute-done.12, f32[1,128]{1,0:T(1,128)S(1)} %get-tuple-element.13, f32[1,128]{1,0:T(1,128)S(1)} %collective-permute-done.11), kind=kLoop, calls=%fused_computation | loop fusion | flops 384 | bytes 2560 | tf_op jit(solution)/shard_map/reshape | solution.py:269
Async XLA Ops:
  1.0 16.1 %collective-permute-start.6 = (bf16[64,3072]{1,0:T(8,128)(2,1)S(1)}, bf16[64,3072]{1,0:T(8,128)(2,1)S(1)}, u32[]{:S(2)}, u32[]{:S(2)}) collective-permute-start(bf16[64,3072]{1,0:T(8,128)(2,1)S(1)} %constant_dynamic-slice_fusion), channel_id=1, source_target_pairs={{0,2},{2,0},{1,3},{3,1},{4,6},{6,4},{5,7},{7,5},{8,10},{10,8},{9,1... | collective-permute-start | bytes 1179656 | tf_op jit(solution)/shard_map/item_rows/ppermute | solution.py:167
  4.0 5.0 %collective-permute-start.2 = (s32[8]{0:T(128)}, s32[8]{0:T(128)S(1)}, u32[]{:S(2)}, u32[]{:S(2)}) collective-permute-start(s32[8]{0:T(128)} %refs_0_.1), channel_id=1, source_target_pairs={{0,12},{4,0},{8,4},{12,8},{1,13},{5,1},{9,5},{13,9},{2,14},{6,2},{... | collective-permute-start | bytes 104 | tf_op jit(solution)/shard_map/ids/ppermute | solution.py:167
  7.6 4.6 %collective-permute-start.1 = (s32[8]{0:T(128)}, s32[8]{0:T(128)S(1)}, u32[]{:S(2)}, u32[]{:S(2)}) collective-permute-start(s32[8]{0:T(128)} %refs_0_.1), channel_id=1, source_target_pairs={{0,8},{4,12},{8,0},{12,4},{1,9},{5,13},{9,1},{13,5},{2,10},{6,14},... | collective-permute-start | bytes 104 | tf_op jit(solution)/shard_map/ids/ppermute | solution.py:167
  7.6 5.5 %collective-permute-start = (s32[8]{0:T(128)}, s32[8]{0:T(128)S(1)}, u32[]{:S(2)}, u32[]{:S(2)}) collective-permute-start(s32[8]{0:T(128)} %refs_0_.1), channel_id=1, source_target_pairs={{0,4},{4,8},{8,12},{12,0},{1,5},{5,9},{9,13},{13,1},{2,6},{6,10},{... | collective-permute-start | bytes 104 | tf_op jit(solution)/shard_map/ids/ppermute | solution.py:167
  13.1 1.1 %copy-start.2 = (bf16[128,3072]{1,0:T(8,128)(2,1)S(1)}, bf16[128,3072]{1,0:T(8,128)(2,1)}, u32[]{:S(2)}) copy-start(bf16[128,3072]{1,0:T(8,128)(2,1)} %refs_5_.1) | copy-start | bytes 2359300
  14.2 0.7 %copy-start.3 = (s32[8]{0:T(128)S(1)}, s32[8]{0:T(128)}, u32[]{:S(2)}) copy-start(s32[8]{0:T(128)} %refs_0_.1) | copy-start | bytes 100
  14.9 0.7 %copy-start.4 = (s32[128]{0:T(128)S(1)}, s32[128]{0:T(128)}, u32[]{:S(2)}) copy-start(s32[128]{0:T(128)} %param.6) | copy-start | bytes 1540
  17.1 1.1 %copy-start = (bf16[128,3072]{1,0:T(8,128)(2,1)S(1)}, bf16[128,3072]{1,0:T(8,128)(2,1)}, u32[]{:S(2)}) copy-start(bf16[128,3072]{1,0:T(8,128)(2,1)} %refs_12_.1) | copy-start | bytes 2359300
  18.3 1.6 %copy-start.5 = (bf16[256,64,64]{0,2,1:T(8,128)(2,1)S(1)}, bf16[256,64,64]{0,2,1:T(8,128)(2,1)}, u32[]{:S(2)}) copy-start(bf16[256,64,64]{0,2,1:T(8,128)(2,1)} %param.10) | copy-start | bytes 6291460
  19.9 0.7 %copy-start.6 = (s32[256,2]{0,1:T(2,128)S(1)}, s32[256,2]{0,1:T(2,128)}, u32[]{:S(2)}) copy-start(s32[256,2]{0,1:T(2,128)} %param.11) | copy-start | bytes 6148
  20.6 18.1 %copy-start.1 = (bf16[128,3072]{1,0:T(8,128)(2,1)S(1)}, bf16[128,3072]{1,0:T(8,128)(2,1)}, u32[]{:S(2)}) copy-start(bf16[128,3072]{1,0:T(8,128)(2,1)} %refs_12_.1) | copy-start | bytes 2359300
  26.2 12.5 %collective-permute-start.10 = (bf16[64,3072]{1,0:T(8,128)(2,1)S(1)}, bf16[64,3072]{1,0:T(8,128)(2,1)S(1)}, u32[]{:S(2)}, u32[]{:S(2)}) collective-permute-start(bf16[64,3072]{1,0:T(8,128)(2,1)S(1)} %get-tuple-element.12.refs_13_), channel_id=1, source_target_pairs={{0,1},{1,0},{2,3},{3,2},{4,5},{5,4},{6,7},{7,6},{8,9},{9,8},{10,11... | collective-permute-start | bytes 1179656 | tf_op jit(solution)/shard_map/pairs/ppermute | solution.py:167
  26.3 6.6 %collective-permute-start.5 = (bf16[16,3200]{1,0:T(8,128)(2,1)S(1)}, bf16[16,3200]{1,0:T(8,128)(2,1)S(1)}, u32[]{:S(2)}, u32[]{:S(2)}) collective-permute-start(bf16[16,3200]{1,0:T(8,128)(2,1)S(1)} %states.1.picked.refs_4_), channel_id=1, source_target_pairs={{0,12},{4,0},{8,4},{12,8},{1,13},{5,1},{9,5},{13,9},{2,14},{6,2},{... | collective-permute-start | bytes 307208 | tf_op jit(solution)/shard_map/states/ppermute | solution.py:167
  26.9 10.6 %collective-permute-start.4 = (bf16[16,3200]{1,0:T(8,128)(2,1)S(1)}, bf16[16,3200]{1,0:T(8,128)(2,1)S(1)}, u32[]{:S(2)}, u32[]{:S(2)}) collective-permute-start(bf16[16,3200]{1,0:T(8,128)(2,1)S(1)} %states.1.picked.refs_4_), channel_id=1, source_target_pairs={{0,8},{4,12},{8,0},{12,4},{1,9},{5,13},{9,1},{13,5},{2,10},{6,14},... | collective-permute-start | bytes 307208 | tf_op jit(solution)/shard_map/states/ppermute | solution.py:167
  27.6 10.0 %collective-permute-start.3 = (bf16[16,3200]{1,0:T(8,128)(2,1)S(1)}, bf16[16,3200]{1,0:T(8,128)(2,1)S(1)}, u32[]{:S(2)}, u32[]{:S(2)}) collective-permute-start(bf16[16,3200]{1,0:T(8,128)(2,1)S(1)} %states.1.picked.refs_4_), channel_id=1, source_target_pairs={{0,4},{4,8},{8,12},{12,0},{1,5},{5,9},{9,13},{13,1},{2,6},{6,10},{... | collective-permute-start | bytes 307208 | tf_op jit(solution)/shard_map/states/ppermute | solution.py:167
  29.5 8.1 %collective-permute-start.9 = (f32[1,128]{1,0:T(1,128)S(1)}, f32[1,128]{1,0:T(1,128)S(1)}, u32[]{:S(2)}, u32[]{:S(2)}) collective-permute-start(f32[1,128]{1,0:T(1,128)S(1)} %get-tuple-element.11.refs_8_), channel_id=1, source_target_pairs={{0,3},{1,2},{2,1},{3,0},{4,7},{5,6},{6,5},{7,4},{8,11},{9,10},{10,... | collective-permute-start | bytes 1544 | tf_op jit(solution)/shard_map/pairs/ppermute | solution.py:244
  32.8 4.7 %collective-permute-start.8 = (f32[1,128]{1,0:T(1,128)S(1)}, f32[1,128]{1,0:T(1,128)S(1)}, u32[]{:S(2)}, u32[]{:S(2)}) collective-permute-start(f32[1,128]{1,0:T(1,128)S(1)} %get-tuple-element.11.refs_8_), channel_id=1, source_target_pairs={{0,2},{2,0},{1,3},{3,1},{4,6},{6,4},{5,7},{7,5},{8,10},{10,8},{9,1... | collective-permute-start | bytes 1544 | tf_op jit(solution)/shard_map/pairs/ppermute | solution.py:167
  37.5 1.1 %collective-permute-start.7 = (f32[1,128]{1,0:T(1,128)S(1)}, f32[1,128]{1,0:T(1,128)S(1)}, u32[]{:S(2)}, u32[]{:S(2)}) collective-permute-start(f32[1,128]{1,0:T(1,128)S(1)} %get-tuple-element.11.refs_8_), channel_id=1, source_target_pairs={{0,1},{1,0},{2,3},{3,2},{4,5},{5,4},{6,7},{7,6},{8,9},{9,8},{10,11... | collective-permute-start | bytes 1544 | tf_op jit(solution)/shard_map/pairs/ppermute | solution.py:244
  40.4 3.6 %collective-permute-start.11 = (f32[1,128]{1,0:T(1,128)S(1)}, f32[1,128]{1,0:T(1,128)S(1)}, u32[]{:S(2)}, u32[]{:S(2)}) collective-permute-start(f32[1,128]{1,0:T(1,128)S(1)} %get-tuple-element.14), channel_id=1, source_target_pairs={{0,12},{4,0},{8,4},{12,8},{1,13},{5,1},{9,5},{13,9},{2,14},{6,2},{... | collective-permute-start | bytes 1544 | tf_op jit(solution)/shard_map/back/ppermute | solution.py:167
  41.4 4.4 %collective-permute-start.12 = (f32[1,128]{1,0:T(1,128)S(1)}, f32[1,128]{1,0:T(1,128)S(1)}, u32[]{:S(2)}, u32[]{:S(2)}) collective-permute-start(f32[1,128]{1,0:T(1,128)S(1)} %get-tuple-element.15), channel_id=1, source_target_pairs={{0,8},{4,12},{8,0},{12,4},{1,9},{5,13},{9,1},{13,5},{2,10},{6,14},... | collective-permute-start | bytes 1544 | tf_op jit(solution)/shard_map/back/ppermute | solution.py:167
  41.6 5.3 %collective-permute-start.13 = (f32[1,128]{1,0:T(1,128)S(1)}, f32[1,128]{1,0:T(1,128)S(1)}, u32[]{:S(2)}, u32[]{:S(2)}) collective-permute-start(f32[1,128]{1,0:T(1,128)S(1)} %get-tuple-element.16), channel_id=1, source_target_pairs={{0,4},{4,8},{8,12},{12,0},{1,5},{5,9},{9,13},{13,1},{2,6},{6,10},{... | collective-permute-start | bytes 1544 | tf_op jit(solution)/shard_map/back/ppermute | solution.py:167

commit v4 on v3

--- a/solution.py
+++ b/solution.py
@@ -29,17 +29,15 @@
 
 
 def pick_kernel(total, cap, *refs):
-    users, (own_users, cands, states_hbm, out, held, own, sems) = refs[:total - 1], refs[total - 1:]
+    users, (own_users, own_cands, states_hbm, out, held, own, cands, sems) = refs[:total - 1], refs[total - 1:]
     copies = [
         pltpu.make_async_copy(own_users, own, sems.at[0]),
         pltpu.make_async_copy(states_hbm, held, sems.at[1]),
+        pltpu.make_async_copy(own_cands, cands, sems.at[2]),
     ]
     for copy in copies:
         copy.start()
     width = held.shape[1]
-    code = cands[...]
-    digits = jnp.where(iota((out.shape[0], code.shape[1]), 0) == 0, code // CODE, code % CODE)
-    out[:, width:] = jnp.where(iota(digits.shape, 0) < 2, digits, 0).astype(jnp.float32).astype(jnp.bfloat16)
     copies[0].wait()
     own_rows = held.shape[0]
     me = lax.axis_index("shard")
@@ -57,6 +55,10 @@
             taken = taken + mine.astype(jnp.int32)
             chosen = jnp.where((slot_index == slot) & (row_index == user % own_rows), 1.0, chosen)
     chosen = chosen.astype(jnp.bfloat16)
+    copies[2].wait()
+    code = cands[...]
+    digits = jnp.where(iota((slots, code.shape[1]), 0) == 0, code // CODE, code % CODE)
+    out[:, width:] = jnp.where(iota(digits.shape, 0) < 2, digits, 0).astype(jnp.float32).astype(jnp.bfloat16)
     copies[1].wait()
     out[:, :width] = dot(chosen, held[...], NN).astype(jnp.bfloat16)
 
@@ -98,13 +100,14 @@
         return total + moved * jnp.concatenate(mults, axis=0)
 
     total = lax.fori_loop(0, count // 2, two, jnp.zeros((2 * K, items.shape[0]), jnp.float32), unroll=16)
-    out[...] = jnp.sum(total, axis=0, keepdims=True)
+    mine = iota(out.shape, 0) == lax.axis_index("cache")
+    out[...] = jnp.where(mine, jnp.sum(total, axis=0, keepdims=True), 0.0)
 
 
 def score_kernel(total, planes, parts, cap, user_rows, *refs):
     users, refs = refs[:total], refs[total:]
     states, refs = refs[:total], refs[total:]
-    pairs, refs = refs[:planes * parts], refs[planes * parts:]
+    pairs, refs = refs[0], refs[1:]
     items, refs = refs[:1 + (planes - 1) * parts], refs[1 + (planes - 1) * parts:]
     outs, (asked, wanted, cands, linear, rows_out) = refs[:total], refs[total:]
     readers = users[0].shape[0]
@@ -128,7 +131,7 @@
     placed = 0
     for q in range(planes):
         at = ring(plane - q, planes)
-        pair_row = sum(pairs[q * parts + h][...] for h in range(parts))
+        pair_row = pairs[pl.ds(at, 1), :]
         for h in range(1 if q == 0 else parts):
             start = 0 if q == 0 else ring(core - h, parts) * piece
             rows = items[0 if q == 0 else 1 + (q - 1) * parts + h]
@@ -183,6 +186,9 @@
     anywhere = pl.BlockSpec(memory_space=pl.ANY)
     params = pltpu.CompilerParams(vmem_limit_bytes=VMEM_LIMIT)
 
+    def in_hbm(x):
+        return pltpu.with_memory_space_constraint(x, pltpu.HBM)
+
     with jax.named_scope("ids"):
         others = [shift(reader_users, "shard", j) for j in range(1, total)]
         users = [reader_users] + others
@@ -196,23 +202,24 @@
         picked = pl.pallas_call(
             functools.partial(pick_kernel, total, cap),
             out_shape=jax.ShapeDtypeStruct((slots, width + half), jnp.bfloat16),
-            in_specs=[smem] * (total - 1) + [hbm, vmem, hbm],
+            in_specs=[smem] * (total - 1) + [hbm, hbm, hbm],
             out_specs=vmem,
             scratch_shapes=[
                 pltpu.VMEM(user_states.shape, jnp.bfloat16),
                 pltpu.SMEM((readers,), jnp.int32),
-                pltpu.SemaphoreType.DMA((2,)),
+                pltpu.VMEM((1, half), jnp.int32),
+                pltpu.SemaphoreType.DMA((3,)),
             ],
             compiler_params=params,
             cost_estimate=pl.CostEstimate(flops=2 * slots * rows * width, bytes_accessed=1024 * 1024, transcendentals=0),
-        )(*others, reader_users, cand_items.reshape(1, half), user_states)
+        )(*others, in_hbm(reader_users), in_hbm(cand_items.reshape(1, half)), in_hbm(user_states))
         states = [picked] + [shift(picked, "shard", j) for j in range(1, total)]
 
     with jax.named_scope("pairs"):
         pair_scores, passed = pl.pallas_call(
             pair_kernel,
             out_shape=(
-                jax.ShapeDtypeStruct((1, rows), jnp.float32),
+                jax.ShapeDtypeStruct((planes, rows), jnp.float32),
                 jax.ShapeDtypeStruct(crossed[0].shape, crossed[0].dtype),
             ),
             in_specs=[hbm, hbm, hbm, anywhere, anywhere],
@@ -229,27 +236,18 @@
             ],
             compiler_params=params,
             cost_estimate=pl.CostEstimate(flops=2 * count * K * K * rows * 16, bytes_accessed=4 * 1024 * 1024, transcendentals=0),
-        )(pair_fields.T, item_table, jnp.transpose(pair_mats, (1, 2, 0)), picked, crossed[0])
+        )(in_hbm(pair_fields.T), in_hbm(item_table), in_hbm(jnp.transpose(pair_mats, (1, 2, 0))), picked, crossed[0])
         crossed[0] = passed
+        pair_scores = lax.psum(pair_scores, ("cache", "pair"))
         items = [item_table]
-        pairs = []
-        for q in range(planes):
-            moved = pair_scores if q == 0 else shift(pair_scores, "cache", q)
-            pairs.append(moved)
-            if q:
-                items.append(crossed[q - 1])
-            for h in range(1, parts):
-                steps = [((c, d), ((c + q) % planes, (d + h) % parts)) for c in range(planes) for d in range(parts)]
-                perm = [(c * parts + d, e * parts + f) for (c, d), (e, f) in steps]
-                pairs.append(lax.ppermute(pair_scores, ("cache", "pair"), perm))
-                if q:
-                    items.append(shift(crossed[q - 1], "pair", h))
+        for piece_in in crossed:
+            items += [piece_in] + [shift(piece_in, "pair", h) for h in range(1, parts)]
 
     with jax.named_scope("scores"):
         outs = pl.pallas_call(
             functools.partial(score_kernel, total, planes, parts, cap, user_states.shape[0]),
             out_shape=[jax.ShapeDtypeStruct((1, half), jnp.float32)] * total,
-            in_specs=[smem] * total + [vmem] * (total + len(pairs) + len(items)),
+            in_specs=[smem] * total + [vmem] * (total + 1 + len(items)),
             out_specs=[vmem] * total,
             scratch_shapes=[
                 pltpu.SMEM((total, readers), jnp.int32),
@@ -260,7 +258,7 @@
             ],
             compiler_params=params,
             cost_estimate=pl.CostEstimate(flops=2 * 64 * 256 * width, bytes_accessed=2 * 1024 * 1024, transcendentals=0),
-        )(*users, *states, *pairs, *items)
+        )(*users, *states, pair_scores, *items)
 
     with jax.named_scope("back"):
         result = outs[0]

time: 47.8 us -> 44.1 us (0.923)
  blocking collectives: 0 us -> 6.1 us
  waiting for transfers between devices: 16.5 us -> 10.6 us
  local copies, waits for them, and re-layouts: 6.87 us -> 1.03 us
  Pallas kernels: 8.98 us -> 10.5 us
  starting transfers between devices: 14.5 us -> 15 us
    psum x0 -> x1, blocking collectives: none -> 6.1 us  [body(): pair_scores = lax.psum(pair_scores, ('cache', 'pair'))]
    unnamed x14 -> x4, local copies, waits for them, and re-layouts: 5.85 us -> 0.01 us
    ppermute x12 -> x11, waiting for transfers between devices: 15.4 us -> 10.6 us  [shift(): return lax.ppermute(x, axis, [(s, (s + step) % size) for s in range(size)])]
    pallas_call x1, Pallas kernels: 5.64 us -> 6.77 us  [body(): pl.pallas_call(pair_kernel, out_shape=(jax.ShapeDtypeStruct((planes, rows...]
    ppermute x2 -> x0, waiting for transfers between devices: 1.1 us -> none  [body(): pairs.append(lax.ppermute(pair_scores, ('cache', 'pair'), perm))]
    ppermute x12 -> x11, starting transfers between devices: 14.5 us -> 15 us  [shift(): return lax.ppermute(x, axis, [(s, (s + step) % size) for s in range(size)])]
  transfers between devices with their start and end apart: 14 -> 11, of which waited for: 9 -> 6; matrix products, arithmetic and copies ran while one was open for 0% -> 0% of each run, Pallas kernels for 3% -> 4%
where the time goes in v4:
time: 44.1 us; the launch traced here: 43.9 us
  starting transfers between devices  15 us (34%)
  waiting for transfers between devices  10.6 us (24%)
  Pallas kernels  10.5 us (24%)
  blocking collectives  6.1 us (14%)
  local copies, waits for them, and re-layouts  1.03 us (2%)
  other arithmetic  0.52 us (1%)
    ppermute x11, starting transfers between devices, shift(): return lax.ppermute(x, axis, [(s, (s + step) % size) for s in range(size)])  15 us
    ppermute x11, waiting for transfers between devices, shift(): return lax.ppermute(x, axis, [(s, (s + step) % size) for s in range(size)])  10.6 us
    pallas_call x1, Pallas kernels, body(): pl.pallas_call(pair_kernel, out_shape=(jax.ShapeDtypeStruct((planes, rows...  6.77 us
    psum x1, blocking collectives, body(): pair_scores = lax.psum(pair_scores, ('cache', 'pair'))  6.1 us
    pallas_call x1, Pallas kernels, body(): pl.pallas_call(functools.partial(pick_kernel, total, cap), out_shape=jax....  1.93 us
    pallas_call x1, Pallas kernels, body(): pl.pallas_call(functools.partial(score_kernel, total, planes, parts, cap,...  1.79 us
    dynamic_slice x1, local copies, waits for them, and re-layouts, body(): lax.dynamic_slice_in_dim(item_table, lax.axis_index('pair') * piece, piec...  1.02 us
  transfers between devices with their start and end apart: 11, of which 6 were waited for; matrix products, arithmetic and copies ran while one was open for 0% of the time, Pallas kernels for 4%

profile of v4, /device:TPU:0, one launch (start us, length us, event | category | flops | bytes accessed | tf_op | source)
XLA Modules:
  0.0 43.9 jit_solution(5259851319947335944)
XLA Ops:
  0.0 1.0 %constant_dynamic-slice_fusion = bf16[64,3072]{1,0:T(8,128)(2,1)S(1)} fusion(bf16[128,3072]{1,0:T(8,128)(2,1)} %refs_9_.1, s32[]{:T(128)S(6)} %select_n.3), kind=kLoop, calls=%fused_computation.1 | loop fusion | bytes 786436 | tf_op jit(solution)/shard_map/item_rows/dynamic_slice | solution.py:198
  1.0 3.0 %collective-permute-start.6 = (bf16[64,3072]{1,0:T(8,128)(2,1)S(1)}, bf16[64,3072]{1,0:T(8,128)(2,1)S(1)}, u32[]{:S(2)}, u32[]{:S(2)}) collective-permute-start(bf16[64,3072]{1,0:T(8,128)(2,1)S(1)} %constant_dynamic-slice_fusion), channel_id=1, source_target_pairs={{0,2},{2,0},{1,3},{3,1},{4,6},{6,4},{5,7},{7,5},{8,10},{10,8},{9,1... | collective-permute-start | bytes 1179656 | tf_op jit(solution)/shard_map/item_rows/ppermute | solution.py:170
  4.0 3.6 %collective-permute-start.2 = (s32[8]{0:T(128)}, s32[8]{0:T(128)S(1)}, u32[]{:S(2)}, u32[]{:S(2)}) collective-permute-start(s32[8]{0:T(128)} %refs_0_.1), channel_id=1, source_target_pairs={{0,12},{4,0},{8,4},{12,8},{1,13},{5,1},{9,5},{13,9},{2,14},{6,2},{... | collective-permute-start | bytes 104 | tf_op jit(solution)/shard_map/ids/ppermute | solution.py:170
  7.6 0.0 collective-permute-start.1
  7.6 1.0 %collective-permute-start = (s32[8]{0:T(128)}, s32[8]{0:T(128)S(1)}, u32[]{:S(2)}, u32[]{:S(2)}) collective-permute-start(s32[8]{0:T(128)} %refs_0_.1), channel_id=1, source_target_pairs={{0,4},{4,8},{8,12},{12,0},{1,5},{5,9},{9,13},{13,1},{2,6},{6,10},{... | collective-permute-start | bytes 104 | tf_op jit(solution)/shard_map/ids/ppermute | solution.py:170
  8.6 0.4 collective-permute-done.2.refs_2_.refs_3_
  9.1 3.1 %collective-permute-done.1.refs_1_.refs_2_ = s32[8]{0:T(128)S(1)} collective-permute-done((s32[8]{0:T(128)}, s32[8]{0:T(128)S(1)}, u32[]{:S(2)}, u32[]{:S(2)}) %collective-permute-start.1) | collective-permute-done | bytes 64 | tf_op jit(solution)/shard_map/ids/ppermute | solution.py:170
  12.2 0.9 %collective-permute-done.refs_0_.refs_1_ = s32[8]{0:T(128)S(1)} collective-permute-done((s32[8]{0:T(128)}, s32[8]{0:T(128)S(1)}, u32[]{:S(2)}, u32[]{:S(2)}) %collective-permute-start) | collective-permute-done | bytes 64 | tf_op jit(solution)/shard_map/ids/ppermute | solution.py:170
  13.1 1.9 %states.1.picked.refs_4_ = bf16[16,3200]{1,0:T(8,128)(2,1)S(1)} custom-call(s32[8]{0:T(128)S(1)} %collective-permute-done.refs_0_.refs_1_, s32[8]{0:T(128)S(1)} %collective-permute-done.1.refs_1_.refs_2_, s32[8]{0:T(128)S(1)} %collective-permute-done.2.refs_2_.refs_3_, s32[8]{0:T(128)} %refs_0_.1, s32[1,128]{1,0:T(1,128)} %bitcast.5, bf16[128,3072]{1,0:T(8,128)(2,1)} %refs_5_.1), custom_call_target="tpu_custom_call" | custom-call | flops 12582912 | bytes 1048576 | tf_op jit(solution)/shard_map/states/pallas_call | solution.py:202
  15.0 0.0 collective-permute-done.6.crossed
  15.1 0.0 copy-start
  15.1 0.0 copy-start.1
  15.1 6.8 %pairs.1 = (f32[2,128]{1,0:T(2,128)S(1)}, bf16[64,3072]{1,0:T(8,128)(2,1)S(1)}) custom-call(s32[2,256]{1,0:T(2,128)} %bitcast.7, bf16[128,3072]{1,0:T(8,128)(2,1)} %refs_9_.1, bf16[64,64,256]{2,1,0:T(8,128)(2,1)} %bitcast.6, bf16[16,3200]{1,0:T(8,128)(2,1)S(1)} %states.1.picked.refs_4_, ...), custom_call_target="tpu_custom_call", output_to_operand_aliasing={{1}: (4, {})} | custom-call | flops 4294967296 | bytes 4194304 | tf_op jit(solution)/shard_map/pairs/pallas_call | solution.py:219
  21.9 0.1 collective-permute-start.7
  21.9 2.0 %collective-permute-start.5 = (bf16[16,3200]{1,0:T(8,128)(2,1)S(1)}, bf16[16,3200]{1,0:T(8,128)(2,1)S(1)}, u32[]{:S(2)}, u32[]{:S(2)}) collective-permute-start(bf16[16,3200]{1,0:T(8,128)(2,1)S(1)} %states.1.picked.refs_4_), channel_id=1, source_target_pairs={{0,12},{4,0},{8,4},{12,8},{1,13},{5,1},{9,5},{13,9},{2,14},{6,2},{... | collective-permute-start | bytes 307208 | tf_op jit(solution)/shard_map/states/ppermute | solution.py:170
  23.9 0.0 collective-permute-start.4
  23.9 1.2 %collective-permute-start.3 = (bf16[16,3200]{1,0:T(8,128)(2,1)S(1)}, bf16[16,3200]{1,0:T(8,128)(2,1)S(1)}, u32[]{:S(2)}, u32[]{:S(2)}) collective-permute-start(bf16[16,3200]{1,0:T(8,128)(2,1)S(1)} %states.1.picked.refs_4_), channel_id=1, source_target_pairs={{0,4},{4,8},{8,12},{12,0},{1,5},{5,9},{9,13},{13,1},{2,6},{6,10},{... | collective-permute-start | bytes 307208 | tf_op jit(solution)/shard_map/states/ppermute | solution.py:170
  25.1 6.1 %psum.7.refs_8_ = f32[2,128]{1,0:T(2,128)S(1)} all-reduce(f32[2,128]{1,0:T(2,128)S(1)} %get-tuple-element.11), channel_id=1, replica_groups=mesh['groups'=2,'shard'=4,'cache'=2,'pair'=2] {'cache','pair'}, use_global_device_ids=true, to_apply=%region_0.0 | all-reduce | flops 256 | bytes 2048 | tf_op jit(solution)/shard_map/pairs/psum | solution.py:241
  31.2 0.0 collective-permute-done.5.refs_7_
  31.2 2.8 %collective-permute-done.4.refs_6_ = bf16[16,3200]{1,0:T(8,128)(2,1)S(1)} collective-permute-done((bf16[16,3200]{1,0:T(8,128)(2,1)S(1)}, bf16[16,3200]{1,0:T(8,128)(2,1)S(1)}, u32[]{:S(2)}, u32[]{:S(2)}) %collective-permute-start.4) | collective-permute-done | bytes 102432 | tf_op jit(solution)/shard_map/states/ppermute | solution.py:170
  34.0 0.0 collective-permute-done.3.refs_5_
  34.0 0.0 collective-permute-done.7.refs_11_
  34.0 0.0 copy-done
  34.0 0.0 copy-done.1
  34.0 1.8 %scores.1 = (f32[1,128]{1,0:T(1,128)S(1)}, f32[1,128]{1,0:T(1,128)S(1)}, f32[1,128]{1,0:T(1,128)S(1)}, f32[1,128]{1,0:T(1,128)S(1)}) custom-call(s32[8]{0:T(128)S(1)} %copy-done.1, s32[8]{0:T(128)S(1)} %collective-permute-done.refs_0_.refs_1_, s32[8]{0:T(128)S(1)} %collective-permute-done.1.refs_1_.refs_2_, s32[8]{0:T(128)S(1)} %collective-permute-done.2.refs_2_.refs_3_, ...), custom_call_target="tpu_custom_call" | custom-call | flops 100663296 | bytes 2097152 | tf_op jit(solution)/shard_map/scores/pallas_call | solution.py:247
  35.8 1.4 %collective-permute-start.8 = (f32[1,128]{1,0:T(1,128)S(1)}, f32[1,128]{1,0:T(1,128)S(1)}, u32[]{:S(2)}, u32[]{:S(2)}) collective-permute-start(f32[1,128]{1,0:T(1,128)S(1)} %get-tuple-element.14), channel_id=1, source_target_pairs={{0,12},{4,0},{8,4},{12,8},{1,13},{5,1},{9,5},{13,9},{2,14},{6,2},{... | collective-permute-start | bytes 1544 | tf_op jit(solution)/shard_map/back/ppermute | solution.py:170
  37.3 0.8 %collective-permute-start.9 = (f32[1,128]{1,0:T(1,128)S(1)}, f32[1,128]{1,0:T(1,128)S(1)}, u32[]{:S(2)}, u32[]{:S(2)}) collective-permute-start(f32[1,128]{1,0:T(1,128)S(1)} %get-tuple-element.15), channel_id=1, source_target_pairs={{0,8},{4,12},{8,0},{12,4},{1,9},{5,13},{9,1},{13,5},{2,10},{6,14},... | collective-permute-start | bytes 1544 | tf_op jit(solution)/shard_map/back/ppermute | solution.py:170
  38.0 1.9 %collective-permute-start.10 = (f32[1,128]{1,0:T(1,128)S(1)}, f32[1,128]{1,0:T(1,128)S(1)}, u32[]{:S(2)}, u32[]{:S(2)}) collective-permute-start(f32[1,128]{1,0:T(1,128)S(1)} %get-tuple-element.16), channel_id=1, source_target_pairs={{0,4},{4,8},{8,12},{12,0},{1,5},{5,9},{9,13},{13,1},{2,6},{6,10},{... | collective-permute-start | bytes 1544 | tf_op jit(solution)/shard_map/back/ppermute | solution.py:170
  40.0 0.0 collective-permute-done.8
  40.0 1.7 %collective-permute-done.9 = f32[1,128]{1,0:T(1,128)S(1)} collective-permute-done((f32[1,128]{1,0:T(1,128)S(1)}, f32[1,128]{1,0:T(1,128)S(1)}, u32[]{:S(2)}, u32[]{:S(2)}) %collective-permute-start.9) | collective-permute-done | bytes 544 | tf_op jit(solution)/shard_map/back/ppermute | solution.py:170
  41.7 1.7 %collective-permute-done.10 = f32[1,128]{1,0:T(1,128)S(1)} collective-permute-done((f32[1,128]{1,0:T(1,128)S(1)}, f32[1,128]{1,0:T(1,128)S(1)}, u32[]{:S(2)}, u32[]{:S(2)}) %collective-permute-start.10) | collective-permute-done | bytes 544 | tf_op jit(solution)/shard_map/back/ppermute | solution.py:170
  43.4 0.5 %add_bitcast_fusion = f32[128]{0:T(128)} fusion(f32[1,128]{1,0:T(1,128)S(1)} %collective-permute-done.10, f32[1,128]{1,0:T(1,128)S(1)} %collective-permute-done.9, f32[1,128]{1,0:T(1,128)S(1)} %get-tuple-element.13, f32[1,128]{1,0:T(1,128)S(1)} %collective-permute-done.8), kind=kLoop, calls=%fused_computation | loop fusion | flops 384 | bytes 2560 | tf_op jit(solution)/shard_map/reshape | solution.py:267
Async XLA Ops:
  1.0 14.0 %collective-permute-start.6 = (bf16[64,3072]{1,0:T(8,128)(2,1)S(1)}, bf16[64,3072]{1,0:T(8,128)(2,1)S(1)}, u32[]{:S(2)}, u32[]{:S(2)}) collective-permute-start(bf16[64,3072]{1,0:T(8,128)(2,1)S(1)} %constant_dynamic-slice_fusion), channel_id=1, source_target_pairs={{0,2},{2,0},{1,3},{3,1},{4,6},{6,4},{5,7},{7,5},{8,10},{10,8},{9,1... | collective-permute-start | bytes 1179656 | tf_op jit(solution)/shard_map/item_rows/ppermute | solution.py:170
  4.0 5.0 %collective-permute-start.2 = (s32[8]{0:T(128)}, s32[8]{0:T(128)S(1)}, u32[]{:S(2)}, u32[]{:S(2)}) collective-permute-start(s32[8]{0:T(128)} %refs_0_.1), channel_id=1, source_target_pairs={{0,12},{4,0},{8,4},{12,8},{1,13},{5,1},{9,5},{13,9},{2,14},{6,2},{... | collective-permute-start | bytes 104 | tf_op jit(solution)/shard_map/ids/ppermute | solution.py:170
  7.6 4.6 %collective-permute-start.1 = (s32[8]{0:T(128)}, s32[8]{0:T(128)S(1)}, u32[]{:S(2)}, u32[]{:S(2)}) collective-permute-start(s32[8]{0:T(128)} %refs_0_.1), channel_id=1, source_target_pairs={{0,8},{4,12},{8,0},{12,4},{1,9},{5,13},{9,1},{13,5},{2,10},{6,14},... | collective-permute-start | bytes 104 | tf_op jit(solution)/shard_map/ids/ppermute | solution.py:170
  7.6 5.5 %collective-permute-start = (s32[8]{0:T(128)}, s32[8]{0:T(128)S(1)}, u32[]{:S(2)}, u32[]{:S(2)}) collective-permute-start(s32[8]{0:T(128)} %refs_0_.1), channel_id=1, source_target_pairs={{0,4},{4,8},{8,12},{12,0},{1,5},{5,9},{9,13},{13,1},{2,6},{6,10},{... | collective-permute-start | bytes 104 | tf_op jit(solution)/shard_map/ids/ppermute | solution.py:170
  15.1 19.0 %copy-start = (bf16[128,3072]{1,0:T(8,128)(2,1)S(1)}, bf16[128,3072]{1,0:T(8,128)(2,1)}, u32[]{:S(2)}) copy-start(bf16[128,3072]{1,0:T(8,128)(2,1)} %refs_9_.1) | copy-start | bytes 2359300
  15.1 19.0 %copy-start.1 = (s32[8]{0:T(128)S(1)}, s32[8]{0:T(128)}, u32[]{:S(2)}) copy-start(s32[8]{0:T(128)} %refs_0_.1) | copy-start | bytes 100
  21.9 12.2 %collective-permute-start.7 = (bf16[64,3072]{1,0:T(8,128)(2,1)S(1)}, bf16[64,3072]{1,0:T(8,128)(2,1)S(1)}, u32[]{:S(2)}, u32[]{:S(2)}) collective-permute-start(bf16[64,3072]{1,0:T(8,128)(2,1)S(1)} %get-tuple-element.12.refs_10_), channel_id=1, source_target_pairs={{0,1},{1,0},{2,3},{3,2},{4,5},{5,4},{6,7},{7,6},{8,9},{9,8},{10,11... | collective-permute-start | bytes 1179656 | tf_op jit(solution)/shard_map/pairs/ppermute | solution.py:170
  21.9 9.3 %collective-permute-start.5 = (bf16[16,3200]{1,0:T(8,128)(2,1)S(1)}, bf16[16,3200]{1,0:T(8,128)(2,1)S(1)}, u32[]{:S(2)}, u32[]{:S(2)}) collective-permute-start(bf16[16,3200]{1,0:T(8,128)(2,1)S(1)} %states.1.picked.refs_4_), channel_id=1, source_target_pairs={{0,12},{4,0},{8,4},{12,8},{1,13},{5,1},{9,5},{13,9},{2,14},{6,2},{... | collective-permute-start | bytes 307208 | tf_op jit(solution)/shard_map/states/ppermute | solution.py:170
  23.9 10.1 %collective-permute-start.4 = (bf16[16,3200]{1,0:T(8,128)(2,1)S(1)}, bf16[16,3200]{1,0:T(8,128)(2,1)S(1)}, u32[]{:S(2)}, u32[]{:S(2)}) collective-permute-start(bf16[16,3200]{1,0:T(8,128)(2,1)S(1)} %states.1.picked.refs_4_), channel_id=1, source_target_pairs={{0,8},{4,12},{8,0},{12,4},{1,9},{5,13},{9,1},{13,5},{2,10},{6,14},... | collective-permute-start | bytes 307208 | tf_op jit(solution)/shard_map/states/ppermute | solution.py:170
  23.9 10.1 %collective-permute-start.3 = (bf16[16,3200]{1,0:T(8,128)(2,1)S(1)}, bf16[16,3200]{1,0:T(8,128)(2,1)S(1)}, u32[]{:S(2)}, u32[]{:S(2)}) collective-permute-start(bf16[16,3200]{1,0:T(8,128)(2,1)S(1)} %states.1.picked.refs_4_), channel_id=1, source_target_pairs={{0,4},{4,8},{8,12},{12,0},{1,5},{5,9},{9,13},{13,1},{2,6},{6,10},{... | collective-permute-start | bytes 307208 | tf_op jit(solution)/shard_map/states/ppermute | solution.py:170
  35.8 4.2 %collective-permute-start.8 = (f32[1,128]{1,0:T(1,128)S(1)}, f32[1,128]{1,0:T(1,128)S(1)}, u32[]{:S(2)}, u32[]{:S(2)}) collective-permute-start(f32[1,128]{1,0:T(1,128)S(1)} %get-tuple-element.14), channel_id=1, source_target_pairs={{0,12},{4,0},{8,4},{12,8},{1,13},{5,1},{9,5},{13,9},{2,14},{6,2},{... | collective-permute-start | bytes 1544 | tf_op jit(solution)/shard_map/back/ppermute | solution.py:170
  37.3 4.4 %collective-permute-start.9 = (f32[1,128]{1,0:T(1,128)S(1)}, f32[1,128]{1,0:T(1,128)S(1)}, u32[]{:S(2)}, u32[]{:S(2)}) collective-permute-start(f32[1,128]{1,0:T(1,128)S(1)} %get-tuple-element.15), channel_id=1, source_target_pairs={{0,8},{4,12},{8,0},{12,4},{1,9},{5,13},{9,1},{13,5},{2,10},{6,14},... | collective-permute-start | bytes 1544 | tf_op jit(solution)/shard_map/back/ppermute | solution.py:170
  38.0 5.3 %collective-permute-start.10 = (f32[1,128]{1,0:T(1,128)S(1)}, f32[1,128]{1,0:T(1,128)S(1)}, u32[]{:S(2)}, u32[]{:S(2)}) collective-permute-start(f32[1,128]{1,0:T(1,128)S(1)} %get-tuple-element.16), channel_id=1, source_target_pairs={{0,4},{4,8},{8,12},{12,0},{1,5},{5,9},{9,13},{13,1},{2,6},{6,10},{... | collective-permute-start | bytes 1544 | tf_op jit(solution)/shard_map/back/ppermute | solution.py:170

commit v5 on v4

v5 whole, which is shorter than its diff:
```python
import functools

import jax
import jax.numpy as jnp
from jax import lax
from jax.experimental import pallas as pl
from jax.experimental.pallas import tpu as pltpu
from jax.sharding import PartitionSpec as P

K = 64
LANES = 128
PITCH = 72
CODE = 128
VMEM_LIMIT = 40 * 1024 * 1024
NT = (((1,), (1,)), ((), ()))
NN = (((1,), (0,)), ((), ()))


def dot(a, b, dims, **kw):
    return lax.dot_general(a, b, dims, preferred_element_type=jnp.float32, **kw)


def iota(shape, dim):
    return lax.broadcasted_iota(jnp.int32, shape, dim)


def ring(index, size):
    return lax.rem(index + size, size)


def pick_kernel(total, cap, *refs):
    users, (cands, states, later, out) = refs[:total], refs[total:]
    del later
    width = states.shape[1]
    own_rows = states.shape[0]
    me = lax.axis_index("shard")
    slots = out.shape[0]
    slot_index = iota((slots, own_rows), 0)
    row_index = iota((slots, own_rows), 1)
    chosen = jnp.zeros((slots, own_rows), jnp.float32)
    for j, line in enumerate(users):
        source = ring(me - j, total)
        taken = jnp.int32(0)
        for r in range(line.shape[0]):
            user = line[r]
            mine = user // own_rows == me
            slot = jnp.where(mine, source * cap + taken, -1)
            taken = taken + mine.astype(jnp.int32)
            chosen = jnp.where((slot_index == slot) & (row_index == user % own_rows), 1.0, chosen)
    code = cands[...]
    digits = jnp.where(iota((slots, code.shape[1]), 0) == 0, code // CODE, code % CODE)
    out[:, width:] = jnp.where(iota(digits.shape, 0) < 2, digits, 0).astype(jnp.float32).astype(jnp.bfloat16)
    out[:, :width] = dot(chosen.astype(jnp.bfloat16), states[...], NN).astype(jnp.bfloat16)


def pair_kernel(fields_hbm, items_hbm, mats_hbm, out, fields, items, mats, rows32, rows16, stacked, sems):
    copies = [
        pltpu.make_async_copy(items_hbm, items, sems.at[0]),
        pltpu.make_async_copy(mats_hbm, mats, sems.at[1]),
        pltpu.make_async_copy(fields_hbm, fields, sems.at[2]),
    ]
    for copy in copies:
        copy.start()
    count = mats.shape[2]
    eye = (iota((LANES, LANES), 0) == iota((LANES, LANES), 1)).astype(jnp.bfloat16)
    copies[0].wait()
    for t in range(items.shape[1] // LANES):
        turned = dot(eye, items[:, t * LANES:(t + 1) * LANES], NT)
        rows32[t * LANES:(t + 1) * LANES, :] = turned
        rows16[t * LANES:(t + 1) * LANES, :] = turned.astype(jnp.bfloat16)
    eye_pairs = (iota((count, count), 0) == iota((count, count), 1)).astype(jnp.bfloat16)
    side = (iota((count, LANES), 0) % 2 == 0) == (iota((count, LANES), 1) < K)
    copies[1].wait()
    for k in range(K):
        both = jnp.concatenate([mats[k], mats[k]], axis=0)
        stacked[pl.ds(k, count, stride=PITCH), :] = jnp.where(side, dot(eye_pairs, both, NT), 0.0)
    copies[2].wait()

    def two(step, total):
        first = step * 2
        lefts, rights, mults = [], [], []
        for p in (first, first + 1):
            a = pl.multiple_of(fields[0, p] * K, K)
            b = pl.multiple_of(fields[1, p] * K, K)
            lefts.append(stacked[pl.ds(pl.multiple_of(p * PITCH, 8), K), :].astype(jnp.bfloat16))
            rights.append(rows16[pl.ds(b, K), :])
            mults.append(rows32[pl.ds(a, K), :])
        moved = dot(jnp.concatenate(lefts, axis=0), jnp.concatenate(rights, axis=0), NN)
        return total + moved * jnp.concatenate(mults, axis=0)

    total = lax.fori_loop(0, count // 2, two, jnp.zeros((2 * K, items.shape[0]), jnp.float32), unroll=16)
    mine = iota(out.shape, 0) == lax.axis_index("cache")
    out[...] = jnp.where(mine, jnp.sum(total, axis=0, keepdims=True), 0.0)


def score_kernel(total, cap, user_rows, *refs):
    users, refs = refs[:total], refs[total:]
    states, refs = refs[:total], refs[total:]
    pairs, items, out, asked, wanted, cands, linear = refs
    readers = users[0].shape[0]
    slots = states[0].shape[0]
    count, width = items.shape
    half = out.shape[1]
    me = lax.axis_index("shard")
    for j in range(total):
        for r in range(readers):
            asked[j, r] = users[j][r]
        wanted[j * slots:(j + 1) * slots, :] = states[j][:, :width]
        digits = states[j][:, width:].astype(jnp.float32)
        place = iota(digits.shape, 0)
        weight = jnp.where(place == 0, float(CODE), jnp.where(place == 1, 1.0, 0.0))
        cands[j:j + 1, :] = jnp.sum(digits * weight, axis=0, keepdims=True).astype(jnp.int32)
    linear[...] = dot(items[...], wanted[...], NT)
    planes, own_rows = pairs.shape
    eye = iota((own_rows, own_rows), 0) == iota((own_rows, own_rows), 1)
    columns = [jnp.sum(jnp.where(eye, pairs[q:q + 1, :], 0.0), axis=1, keepdims=True) for q in range(planes)]
    pair_column = jnp.concatenate(columns, axis=0)
    item_ids = iota((count, 1), 0) + me * count
    lane = iota((1, half), 1) // (half // readers)

    def one(j, carry):
        source = ring(me - j, total)
        slot_row = jnp.zeros((1, half), jnp.int32)
        holders = [asked[j, r] // user_rows for r in range(readers)]
        for r, holder in enumerate(holders):
            rank = jnp.int32(0)
            for earlier in holders[:r]:
                rank = rank + (earlier == holder).astype(jnp.int32)
            slot_row = jnp.where(lane == r, ring(me - holder, total) * slots + source * cap + rank, slot_row)
        spread = (iota((wanted.shape[0], half), 0) == slot_row).astype(jnp.float32)
        scores = dot(linear[...], spread, NN, precision=lax.Precision.HIGHEST) + pair_column
        hit = item_ids == cands[pl.ds(j, 1), :]
        out[pl.ds(source, 1), :] = jnp.sum(jnp.where(hit, scores, 0.0), axis=0, keepdims=True)
        return carry

    lax.fori_loop(0, total, one, 0, unroll=total <= 8)


def shift(x, axis, step):
    size = lax.axis_size(axis)
    return lax.ppermute(x, axis, [(s, (s + step) % size) for s in range(size)])


def body(cand_items, reader_users, item_table, user_states, pair_mats, pair_fields):
    total = lax.axis_size("shard")
    planes = lax.axis_size("cache")
    half = cand_items.shape[0]
    rows, width = item_table.shape
    readers = reader_users.shape[0]
    cap = 2 * ((readers + total - 1) // total)
    slots = -(-total * cap // 16) * 16
    count = pair_mats.shape[0]
    vmem = pl.BlockSpec(memory_space=pltpu.VMEM)
    smem = pl.BlockSpec(memory_space=pltpu.SMEM)
    hbm = pl.BlockSpec(memory_space=pltpu.HBM)
    anywhere = pl.BlockSpec(memory_space=pl.ANY)
    params = pltpu.CompilerParams(vmem_limit_bytes=VMEM_LIMIT)

    def in_hbm(x):
        return pltpu.with_memory_space_constraint(x, pltpu.HBM)

    with jax.named_scope("ids"):
        others = [shift(reader_users, "shard", j) for j in range(1, total)]
        users = [reader_users] + others

    with jax.named_scope("item_rows"):
        items = lax.all_gather(item_table, "cache", axis=0, tiled=True)

    with jax.named_scope("pairs"):
        pair_parts = pl.pallas_call(
            pair_kernel,
            out_shape=jax.ShapeDtypeStruct((planes, rows), jnp.float32),
            in_specs=[hbm, hbm, hbm],
            out_specs=vmem,
            scratch_shapes=[
                pltpu.SMEM((2, count), jnp.int32),
                pltpu.VMEM((rows, width), jnp.bfloat16),
                pltpu.VMEM((K, K, count), jnp.bfloat16),
                pltpu.VMEM((width, rows), jnp.float32),
                pltpu.VMEM((width, rows), jnp.bfloat16),
                pltpu.VMEM((count * PITCH, LANES), jnp.float32),
                pltpu.SemaphoreType.DMA((3,)),
            ],
            compiler_params=params,
            cost_estimate=pl.CostEstimate(flops=2 * count * K * K * rows * 16, bytes_accessed=4 * 1024 * 1024, transcendentals=0),
        )(in_hbm(pair_fields.T), in_hbm(item_table), in_hbm(jnp.transpose(pair_mats, (1, 2, 0))))
        pair_scores = lax.psum(pair_parts, ("cache", "pair"))

    with jax.named_scope("states"):
        picked = pl.pallas_call(
            functools.partial(pick_kernel, total, cap),
            out_shape=jax.ShapeDtypeStruct((slots, width + half), jnp.bfloat16),
            in_specs=[smem] * total + [vmem, vmem, anywhere],
            out_specs=vmem,
            compiler_params=params,
            cost_estimate=pl.CostEstimate(flops=2 * slots * rows * width, bytes_accessed=1024 * 1024, transcendentals=0),
        )(*users, cand_items.reshape(1, half), user_states, pair_parts)
        states = [picked] + [shift(picked, "shard", j) for j in range(1, total)]

    with jax.named_scope("scores"):
        parted = pl.pallas_call(
            functools.partial(score_kernel, total, cap, user_states.shape[0]),
            out_shape=jax.ShapeDtypeStruct((total, half), jnp.float32),
            in_specs=[smem] * total + [vmem] * (total + 2),
            out_specs=vmem,
            scratch_shapes=[
                pltpu.SMEM((total, readers), jnp.int32),
                pltpu.VMEM((total * slots, width), jnp.bfloat16),
                pltpu.VMEM((-(-total // 8) * 8, half), jnp.int32),
                pltpu.VMEM((planes * rows, total * slots), jnp.float32),
            ],
            compiler_params=params,
            cost_estimate=pl.CostEstimate(flops=2 * 64 * 256 * width, bytes_accessed=2 * 1024 * 1024, transcendentals=0),
        )(*users, *states, pair_scores, items)

    with jax.named_scope("back"):
        return lax.psum_scatter(parted, "shard", scatter_dimension=0, tiled=True).reshape(half)


def solution(mesh):
    return jax.shard_map(
        body,
        mesh=mesh,
        in_specs=(
            P(("groups", "shard", "cache", "pair")),
            P(("groups", "shard", "cache", "pair")),
            P(("shard", "cache"), None),
            P(("groups", "shard"), None),
            P("pair", None, None),
            P("pair", None),
        ),
        out_specs=P(("groups", "shard", "cache", "pair")),
        check_vma=False,
    )
```

time: 44.1 us -> 62.8 us (1.42)
  between operations: 0.07 us -> 13.5 us
  blocking collectives: 6.1 us -> 17.8 us
  starting transfers between devices: 15 us -> 10.9 us
  waiting for transfers between devices: 10.6 us -> 7.01 us
  local copies, waits for them, and re-layouts: 1.03 us -> 3.26 us
    unnamed x0 -> x1, blocking collectives: none -> 11.7 us
    ppermute x11 -> x6, waiting for transfers between devices: 10.6 us -> 0.02 us  [shift(): return lax.ppermute(x, axis, [(s, (s + step) % size) for s in range(size)])]
    all_gather x0 -> x1, waiting for transfers between devices: none -> 6.29 us  [body(): items = lax.all_gather(item_table, 'cache', axis=0, tiled=True)]
    ppermute x11 -> x6, starting transfers between devices: 15 us -> 10.9 us  [shift(): return lax.ppermute(x, axis, [(s, (s + step) % size) for s in range(size)])]
    unnamed x4 -> x11, local copies, waits for them, and re-layouts: 0.01 us -> 2.07 us
    reshape x0 -> x1, local copies, waits for them, and re-layouts: none -> 1.19 us  [body(): lax.psum_scatter(parted, 'shard', scatter_dimension=0, tiled=True)]
    dynamic_slice x1 -> x0, local copies, waits for them, and re-layouts: 1.02 us -> none  [body(): lax.dynamic_slice_in_dim(item_table, lax.axis_index('pair') * piece, piec...]
    pallas_call x1, Pallas kernels: 1.93 us -> 0.99 us  [body(): pl.pallas_call(functools.partial(pick_kernel, total, cap), out_shape=jax....]
  transfers between devices with their start and end apart: 11 -> 7, of which waited for: 6 -> 1; matrix products, arithmetic and copies ran while one was open for 0% -> 1% of each run, Pallas kernels for 4% -> 12%
where the time goes in v5:
time: 62.8 us; the launch traced here: 62.6 us
  blocking collectives  17.8 us (28%)
  between operations  13.5 us (21%)
  starting transfers between devices  10.9 us (17%)
  Pallas kernels  10.1 us (16%)
  waiting for transfers between devices  7.01 us (11%)
  local copies, waits for them, and re-layouts  3.26 us (5%)
    unnamed x1, blocking collectives  11.7 us
    ppermute x6, starting transfers between devices, shift(): return lax.ppermute(x, axis, [(s, (s + step) % size) for s in range(size)])  10.9 us
    pallas_call x1, Pallas kernels, body(): pl.pallas_call(pair_kernel, out_shape=jax.ShapeDtypeStruct((planes, rows)...  6.67 us
    all_gather x1, waiting for transfers between devices, body(): items = lax.all_gather(item_table, 'cache', axis=0, tiled=True)  6.29 us
    psum x1, blocking collectives, body(): pair_scores = lax.psum(pair_parts, ('cache', 'pair'))  6.14 us
    pallas_call x1, Pallas kernels, body(): pl.pallas_call(functools.partial(score_kernel, total, cap, user_states.sh...  2.47 us
    unnamed x11, local copies, waits for them, and re-layouts  2.07 us
  transfers between devices with their start and end apart: 7, of which 1 were waited for; matrix products, arithmetic and copies ran while one was open for 1% of the time, Pallas kernels for 12%

profile of v5, /device:TPU:0, one launch (start us, length us, event | category | flops | bytes accessed | tf_op | source)
XLA Modules:
  0.0 62.6 jit_solution(18065162989539054262)
XLA Ops:
  6.5 0.0 all-gather.2.cloned.1.call-start
  6.5 0.7 %all-gather.2.cloned.1.call-update = ((bf16[128,3072]{1,0:T(8,128)(2,1)}), bf16[256,3072]{1,0:T(8,128)(2,1)}) async-update(((), (), s32[]{:S(2)}) %all-gather.2.cloned.1.call-start, bf16[128,3072]{1,0:T(8,128)(2,1)} %items_hbm.1) | async-update | bytes 3145752
  7.3 3.1 %collective-permute-start = (s32[8]{0:T(128)}, s32[8]{0:T(128)S(1)}, u32[]{:S(2)}, u32[]{:S(2)}) collective-permute-start(s32[8]{0:T(128)} %refs_0_.3), channel_id=1, source_target_pairs={{0,4},{4,8},{8,12},{12,0},{1,5},{5,9},{9,13},{13,1},{2,6},{6,10},{... | collective-permute-start | bytes 104 | tf_op jit(solution)/shard_map/ids/ppermute | solution.py:141
  10.3 2.6 %collective-permute-start.1 = (s32[8]{0:T(128)}, s32[8]{0:T(128)S(1)}, u32[]{:S(2)}, u32[]{:S(2)}) collective-permute-start(s32[8]{0:T(128)} %refs_0_.3), channel_id=1, source_target_pairs={{0,8},{4,12},{8,0},{12,4},{1,9},{5,13},{9,1},{13,5},{2,10},{6,14},... | collective-permute-start | bytes 104 | tf_op jit(solution)/shard_map/ids/ppermute | solution.py:141
  12.9 1.3 %collective-permute-start.2 = (s32[8]{0:T(128)}, s32[8]{0:T(128)S(1)}, u32[]{:S(2)}, u32[]{:S(2)}) collective-permute-start(s32[8]{0:T(128)} %refs_0_.3), channel_id=1, source_target_pairs={{0,12},{4,0},{8,4},{12,8},{1,13},{5,1},{9,5},{13,9},{2,14},{6,2},{... | collective-permute-start | bytes 104 | tf_op jit(solution)/shard_map/ids/ppermute | solution.py:141
  14.3 0.0 copy-start.1
  14.3 0.0 copy-start.2
  14.3 0.0 copy-start.3
  14.3 0.0 copy-start.4
  14.3 6.7 %pairs.1.refs_6_ = f32[2,128]{1,0:T(2,128)S(1)} custom-call(s32[2,256]{1,0:T(2,128)} %bitcast.8, bf16[128,3072]{1,0:T(8,128)(2,1)} %items_hbm.1, bf16[64,64,256]{2,1,0:T(8,128)(2,1)} %bitcast.7), custom_call_target="tpu_custom_call" | custom-call | flops 4294967296 | bytes 4194304 | tf_op jit(solution)/shard_map/pairs/pallas_call | solution.py:170
  21.0 0.0 collective-permute-done.refs_1_
  21.0 0.0 collective-permute-done.1.refs_2_
  21.0 0.0 collective-permute-done.2.refs_3_
  21.0 0.0 copy-done.1
  21.0 0.0 copy-done.2
  21.0 0.0 copy-done.3
  21.0 1.0 %states.1.refs_4_ = bf16[16,3200]{1,0:T(8,128)(2,1)S(1)} custom-call(s32[8]{0:T(128)S(1)} %copy-done.2, s32[8]{0:T(128)S(1)} %collective-permute-done.refs_1_, s32[8]{0:T(128)S(1)} %collective-permute-done.1.refs_2_, s32[8]{0:T(128)S(1)} %collective-permute-done.2.refs_3_, s32[1,128]{1,0:T(1,128)S(1)} %bitcast.6, bf16[128,3072]{1,0:T(8,128)(2,1)S(1)} %copy-done.1, ...), custom_call_target="tpu_custom_call" | custom-call | flops 12582912 | bytes 1048576 | tf_op jit(solution)/shard_map/states/pallas_call | solution.py:190
  22.0 0.7 %collective-permute-start.3 = (bf16[16,3200]{1,0:T(8,128)(2,1)S(1)}, bf16[16,3200]{1,0:T(8,128)(2,1)S(1)}, u32[]{:S(2)}, u32[]{:S(2)}) collective-permute-start(bf16[16,3200]{1,0:T(8,128)(2,1)S(1)} %states.1.refs_4_), channel_id=1, source_target_pairs={{0,4},{4,8},{8,12},{12,0},{1,5},{5,9},{9,13},{13,1},{2,6},{6,10},{... | collective-permute-start | bytes 307208 | tf_op jit(solution)/shard_map/states/ppermute | solution.py:141
  22.7 0.3 collective-permute-start.4
  23.1 2.8 %collective-permute-start.5 = (bf16[16,3200]{1,0:T(8,128)(2,1)S(1)}, bf16[16,3200]{1,0:T(8,128)(2,1)S(1)}, u32[]{:S(2)}, u32[]{:S(2)}) collective-permute-start(bf16[16,3200]{1,0:T(8,128)(2,1)S(1)} %states.1.refs_4_), channel_id=1, source_target_pairs={{0,12},{4,0},{8,4},{12,8},{1,13},{5,1},{9,5},{13,9},{2,14},{6,2},{... | collective-permute-start | bytes 307208 | tf_op jit(solution)/shard_map/states/ppermute | solution.py:141
  25.9 0.0 copy-done.4
  25.9 0.6 %dynamic-slice = u32[1]{0:T(128)} dynamic-slice(u32[32]{0:T(128)S(1)} %copy-done.4, u32[]{:T(128)S(6)} %add.5), dynamic_slice_sizes={1} | dynamic-slice | bytes 12
  26.5 6.1 %psum.7.refs_8_ = f32[2,128]{1,0:T(2,128)S(1)} all-reduce(f32[2,128]{1,0:T(2,128)S(1)} %pairs.1.refs_6_), channel_id=1, replica_groups=mesh['groups'=2,'shard'=4,'cache'=2,'pair'=2] {'cache','pair'}, use_global_device_ids=true, to_apply=%region_0.0 | all-reduce | flops 256 | bytes 2048 | tf_op jit(solution)/shard_map/pairs/psum | solution.py:187
  32.7 0.0 collective-permute-done.3.refs_5_
  32.7 0.0 collective-permute-done.4.refs_6_
  32.7 0.0 collective-permute-done.5.refs_7_
  32.7 6.3 %all-gather.2.cloned.1.call-done.refs_9_ = bf16[256,3072]{1,0:T(8,128)(2,1)} async-done(((bf16[128,3072]{1,0:T(8,128)(2,1)}), bf16[256,3072]{1,0:T(8,128)(2,1)}) %all-gather.2.cloned.1.call-update) | async-done | bytes 1572880 | tf_op jit(solution)/shard_map/item_rows/all_gather | solution.py:167
  39.0 0.0 copy-start
  39.0 1.4 %copy-done = bf16[256,3072]{1,0:T(8,128)(2,1)S(1)} copy-done((bf16[256,3072]{1,0:T(8,128)(2,1)S(1)}, bf16[256,3072]{1,0:T(8,128)(2,1)}, u32[]{:S(2)}) %copy-start) | copy-done | bytes 1572888
  40.4 2.5 %scores.1 = f32[4,128]{1,0:T(4,128)S(1)} custom-call(s32[8]{0:T(128)S(1)} %copy-done.2, s32[8]{0:T(128)S(1)} %collective-permute-done.refs_1_, s32[8]{0:T(128)S(1)} %collective-permute-done.1.refs_2_, s32[8]{0:T(128)S(1)} %collective-permute-done.2.refs_3_, bf16[16,3200]{1,0:T(8,128)(2,1)S(1)} %states.1.refs_4_, ...), custom_call_target="tpu_custom_call" | custom-call | flops 100663296 | bytes 2097152 | tf_op jit(solution)/shard_map/scores/pallas_call | solution.py:201
  42.9 11.7 %all-reduce = f32[4,128]{1,0:T(4,128)S(1)} all-reduce(f32[4,128]{1,0:T(4,128)S(1)} %scores.1), channel_id=2, replica_groups=mesh['groups'=2,'shard'=4,'cache'=2,'pair'=2] {'shard'}, use_global_device_ids=true, to_apply=%region_1.0.clone | all-reduce | flops 512 | bytes 4096
  54.6 1.2 %dynamic-slice_bitcast_fusion = f32[128]{0:T(128)} fusion(f32[4,128]{1,0:T(4,128)S(1)} %all-reduce, u32[]{:T(128)} %bitcast.3), kind=kLoop, calls=%fused_computation | loop fusion | bytes 1028 | tf_op jit(solution)/shard_map/back/reshape | solution.py:217
Async XLA Ops:
  6.5 32.4 %all-gather.2.cloned.1.call-start = ((), (), s32[]{:S(2)}) async-start(), calls=%async_computation | async-start | bytes 2359296 | tf_op jit(solution)/shard_map/item_rows/all_gather | solution.py:167
  7.3 13.7 %collective-permute-start = (s32[8]{0:T(128)}, s32[8]{0:T(128)S(1)}, u32[]{:S(2)}, u32[]{:S(2)}) collective-permute-start(s32[8]{0:T(128)} %refs_0_.3), channel_id=1, source_target_pairs={{0,4},{4,8},{8,12},{12,0},{1,5},{5,9},{9,13},{13,1},{2,6},{6,10},{... | collective-permute-start | bytes 104 | tf_op jit(solution)/shard_map/ids/ppermute | solution.py:141
  10.3 10.6 %collective-permute-start.1 = (s32[8]{0:T(128)}, s32[8]{0:T(128)S(1)}, u32[]{:S(2)}, u32[]{:S(2)}) collective-permute-start(s32[8]{0:T(128)} %refs_0_.3), channel_id=1, source_target_pairs={{0,8},{4,12},{8,0},{12,4},{1,9},{5,13},{9,1},{13,5},{2,10},{6,14},... | collective-permute-start | bytes 104 | tf_op jit(solution)/shard_map/ids/ppermute | solution.py:141
  12.9 8.1 %collective-permute-start.2 = (s32[8]{0:T(128)}, s32[8]{0:T(128)S(1)}, u32[]{:S(2)}, u32[]{:S(2)}) collective-permute-start(s32[8]{0:T(128)} %refs_0_.3), channel_id=1, source_target_pairs={{0,12},{4,0},{8,4},{12,8},{1,13},{5,1},{9,5},{13,9},{2,14},{6,2},{... | collective-permute-start | bytes 104 | tf_op jit(solution)/shard_map/ids/ppermute | solution.py:141
  14.3 6.7 %copy-start.1 = (bf16[128,3072]{1,0:T(8,128)(2,1)S(1)}, bf16[128,3072]{1,0:T(8,128)(2,1)}, u32[]{:S(2)}) copy-start(bf16[128,3072]{1,0:T(8,128)(2,1)} %refs_5_.1) | copy-start | bytes 2359300
  14.3 6.7 %copy-start.2 = (s32[8]{0:T(128)S(1)}, s32[8]{0:T(128)}, u32[]{:S(2)}) copy-start(s32[8]{0:T(128)} %refs_0_.3) | copy-start | bytes 100
  14.3 6.7 %copy-start.3 = (s32[128]{0:T(128)S(1)}, s32[128]{0:T(128)}, u32[]{:S(2)}) copy-start(s32[128]{0:T(128)} %param.6) | copy-start | bytes 1540
  14.3 11.6 %copy-start.4 = (u32[32]{0:T(128)S(1)}, u32[32]{0:T(128)}, u32[]{:S(2)}) copy-start(u32[32]{0:T(128)} %constant.3) | copy-start | bytes 388
  22.0 10.7 %collective-permute-start.3 = (bf16[16,3200]{1,0:T(8,128)(2,1)S(1)}, bf16[16,3200]{1,0:T(8,128)(2,1)S(1)}, u32[]{:S(2)}, u32[]{:S(2)}) collective-permute-start(bf16[16,3200]{1,0:T(8,128)(2,1)S(1)} %states.1.refs_4_), channel_id=1, source_target_pairs={{0,4},{4,8},{8,12},{12,0},{1,5},{5,9},{9,13},{13,1},{2,6},{6,10},{... | collective-permute-start | bytes 307208 | tf_op jit(solution)/shard_map/states/ppermute | solution.py:141
  22.7 10.0 %collective-permute-start.4 = (bf16[16,3200]{1,0:T(8,128)(2,1)S(1)}, bf16[16,3200]{1,0:T(8,128)(2,1)S(1)}, u32[]{:S(2)}, u32[]{:S(2)}) collective-permute-start(bf16[16,3200]{1,0:T(8,128)(2,1)S(1)} %states.1.refs_4_), channel_id=1, source_target_pairs={{0,8},{4,12},{8,0},{12,4},{1,9},{5,13},{9,1},{13,5},{2,10},{6,14},... | collective-permute-start | bytes 307208 | tf_op jit(solution)/shard_map/states/ppermute | solution.py:141
  23.1 9.6 %collective-permute-start.5 = (bf16[16,3200]{1,0:T(8,128)(2,1)S(1)}, bf16[16,3200]{1,0:T(8,128)(2,1)S(1)}, u32[]{:S(2)}, u32[]{:S(2)}) collective-permute-start(bf16[16,3200]{1,0:T(8,128)(2,1)S(1)} %states.1.refs_4_), channel_id=1, source_target_pairs={{0,12},{4,0},{8,4},{12,8},{1,13},{5,1},{9,5},{13,9},{2,14},{6,2},{... | collective-permute-start | bytes 307208 | tf_op jit(solution)/shard_map/states/ppermute | solution.py:141
  39.0 1.4 %copy-start = (bf16[256,3072]{1,0:T(8,128)(2,1)S(1)}, bf16[256,3072]{1,0:T(8,128)(2,1)}, u32[]{:S(2)}) copy-start(bf16[256,3072]{1,0:T(8,128)(2,1)} %all-gather.2.cloned.1.call-done.refs_9_) | copy-start | bytes 4718596
Sparse Core Ops, SparseCore 0:
  8.9 30.0 all-gather.1

commit v6 on v4

v6 whole, which is shorter than its diff:
```python
import functools

import jax
import jax.numpy as jnp
from jax import lax
from jax.experimental import pallas as pl
from jax.experimental.pallas import tpu as pltpu
from jax.sharding import PartitionSpec as P

K = 64
LANES = 128
PITCH = 72
CODE = 128
VMEM_LIMIT = 40 * 1024 * 1024
NT = (((1,), (1,)), ((), ()))
NN = (((1,), (0,)), ((), ()))


def dot(a, b, dims, **kw):
    return lax.dot_general(a, b, dims, preferred_element_type=jnp.float32, **kw)


def iota(shape, dim):
    return lax.broadcasted_iota(jnp.int32, shape, dim)


def ring(index, size):
    return lax.rem(index + size, size)


def pick_kernel(total, cap, *refs):
    users, (own_cands, states_hbm, out, held, asked, cands, sems) = refs[:total], refs[total:]
    fetch = pltpu.make_async_copy(states_hbm, held, sems.at[total])
    digit_fetch = pltpu.make_async_copy(own_cands, cands, sems.at[total + 1])
    id_fetches = [pltpu.make_async_copy(users[j], asked.at[j], sems.at[j]) for j in range(total)]
    for copy in id_fetches + [fetch, digit_fetch]:
        copy.start()
    own_rows, width = held.shape
    me = lax.axis_index("shard")
    slots = out.shape[0]
    slot_index = iota((slots, own_rows), 0)
    row_index = iota((slots, own_rows), 1)
    chosen = jnp.zeros((slots, own_rows), jnp.float32)
    for copy in id_fetches:
        copy.wait()
    for j in range(total):
        source = ring(me - j, total)
        taken = jnp.int32(0)
        for r in range(asked.shape[1]):
            user = asked[j, r]
            mine = user // own_rows == me
            slot = jnp.where(mine, source * cap + taken, -1)
            taken = taken + mine.astype(jnp.int32)
            chosen = jnp.where((slot_index == slot) & (row_index == user % own_rows), 1.0, chosen)
    chosen = chosen.astype(jnp.bfloat16)
    digit_fetch.wait()
    code = cands[...]
    digits = jnp.where(iota((slots, code.shape[1]), 0) == 0, code // CODE, code % CODE)
    out[:, width:] = jnp.where(iota(digits.shape, 0) < 2, digits, 0).astype(jnp.float32).astype(jnp.bfloat16)
    fetch.wait()
    out[:, :width] = dot(chosen, held[...], NN).astype(jnp.bfloat16)


def slot_rows(asked, cap, slots, user_rows, half):
    total, readers = asked.shape
    me = lax.axis_index("shard")
    lane = iota((1, half), 1) // (half // readers)
    rows = []
    for j in range(total):
        source = ring(me - j, total)
        holders = [asked[j, r] // user_rows for r in range(readers)]
        row = jnp.zeros((1, half), jnp.int32)
        for r, holder in enumerate(holders):
            rank = jnp.int32(0)
            for earlier in holders[:r]:
                rank = rank + (earlier == holder).astype(jnp.int32)
            row = jnp.where(lane == r, ring(me - holder, total) * slots + source * cap + rank, row)
        rows.append(row)
    return rows


def pair_kernel(total, cap, slots, user_rows, *refs):
    users, refs = refs[:total], refs[total:]
    fields_hbm, items_hbm, mats_hbm, picked, out, places, asked, fields, items, mats, rows32, rows16, stacked, sems = refs
    del picked
    chunks = 4
    wide = items.shape[1] // chunks
    item_fetches = [
        pltpu.make_async_copy(items_hbm.at[:, pl.ds(t * wide, wide)], items.at[:, pl.ds(t * wide, wide)], sems.at[t])
        for t in range(chunks)
    ]
    mats_fetch = pltpu.make_async_copy(mats_hbm, mats, sems.at[chunks])
    fields_fetch = pltpu.make_async_copy(fields_hbm, fields, sems.at[chunks + 1])
    id_fetches = [pltpu.make_async_copy(users[j], asked.at[j], sems.at[chunks + 2 + j]) for j in range(total)]
    for copy in item_fetches + [mats_fetch, fields_fetch] + id_fetches:
        copy.start()
    count = mats.shape[2]
    eye = (iota((LANES, LANES), 0) == iota((LANES, LANES), 1)).astype(jnp.bfloat16)
    for t in range(items.shape[1] // LANES):
        if t * LANES % wide == 0:
            item_fetches[t * LANES // wide].wait()
        turned = dot(eye, items[:, t * LANES:(t + 1) * LANES], NT)
        rows32[t * LANES:(t + 1) * LANES, :] = turned
        rows16[t * LANES:(t + 1) * LANES, :] = turned.astype(jnp.bfloat16)
    eye_pairs = (iota((count, count), 0) == iota((count, count), 1)).astype(jnp.bfloat16)
    side = (iota((count, LANES), 0) % 2 == 0) == (iota((count, LANES), 1) < K)
    mats_fetch.wait()
    for k in range(K):
        both = jnp.concatenate([mats[k], mats[k]], axis=0)
        stacked[pl.ds(k, count, stride=PITCH), :] = jnp.where(side, dot(eye_pairs, both, NT), 0.0)
    fields_fetch.wait()

    def two(step, total):
        first = step * 2
        lefts, rights, mults = [], [], []
        for p in (first, first + 1):
            a = pl.multiple_of(fields[0, p] * K, K)
            b = pl.multiple_of(fields[1, p] * K, K)
            lefts.append(stacked[pl.ds(pl.multiple_of(p * PITCH, 8), K), :].astype(jnp.bfloat16))
            rights.append(rows16[pl.ds(b, K), :])
            mults.append(rows32[pl.ds(a, K), :])
        moved = dot(jnp.concatenate(lefts, axis=0), jnp.concatenate(rights, axis=0), NN)
        return total + moved * jnp.concatenate(mults, axis=0)

    sums = lax.fori_loop(0, count // 2, two, jnp.zeros((2 * K, items.shape[0]), jnp.float32), unroll=16)
    mine = iota(out.shape, 0) == lax.axis_index("cache")
    out[...] = jnp.where(mine, jnp.sum(sums, axis=0, keepdims=True), 0.0)
    for copy in id_fetches:
        copy.wait()
    for j, row in enumerate(slot_rows(asked, cap, slots, user_rows, places.shape[1])):
        places[j:j + 1, :] = row


def thirds(x):
    high = x.astype(jnp.bfloat16)
    rest = x - high.astype(jnp.float32)
    middle = rest.astype(jnp.bfloat16)
    return high, middle, (rest - middle.astype(jnp.float32)).astype(jnp.bfloat16)


def score_kernel(total, planes, *refs):
    states, refs = refs[:total], refs[total:]
    items, refs = refs[:planes], refs[planes:]
    places, pairs = refs[:2]
    outs, (wanted, cands, linear) = refs[2:2 + total], refs[2 + total:]
    slots = states[0].shape[0]
    own_rows, width = items[0].shape
    me = lax.axis_index("shard")
    plane = lax.axis_index("cache")
    count = total * slots
    for j in range(total):
        wanted[j * slots:(j + 1) * slots, :] = states[j][:, :width]
        digits = states[j][:, width:].astype(jnp.float32)
        place = iota(digits.shape, 0)
        weight = jnp.where(place == 0, float(CODE), jnp.where(place == 1, 1.0, 0.0))
        cands[j:j + 1, :] = jnp.sum(digits * weight, axis=0, keepdims=True).astype(jnp.int32)
    eye = iota((own_rows, own_rows), 0) == iota((own_rows, own_rows), 1)
    ids, columns = [], []
    for q in range(planes):
        at = ring(plane - q, planes)
        scores = dot(items[q][...], wanted[...], NT)
        for t, part in enumerate(thirds(scores)):
            linear[q * own_rows:(q + 1) * own_rows, t * count:(t + 1) * count] = part
        columns.append(jnp.sum(jnp.where(eye, pairs[pl.ds(at, 1), :], 0.0), axis=1, keepdims=True))
        ids.append(iota((own_rows, 1), 0) + (me * planes + at) * own_rows)
    pair_column = jnp.concatenate(columns, axis=0)
    item_ids = jnp.concatenate(ids, axis=0)
    for j in range(total):
        half = outs[j].shape[1]
        spread = (iota((count, half), 0) == places[j:j + 1, :]).astype(jnp.float32).astype(jnp.bfloat16)
        scores = dot(linear[...], jnp.concatenate([spread] * 3, axis=0), NN) + pair_column
        hit = item_ids == cands[j:j + 1, :]
        outs[j][...] = jnp.sum(jnp.where(hit, scores, 0.0), axis=0, keepdims=True)


def shift(x, axis, step):
    size = lax.axis_size(axis)
    return lax.ppermute(x, axis, [(s, (s + step) % size) for s in range(size)])


def body(cand_items, reader_users, item_table, user_states, pair_mats, pair_fields):
    total = lax.axis_size("shard")
    planes = lax.axis_size("cache")
    half = cand_items.shape[0]
    rows, width = item_table.shape
    readers = reader_users.shape[0]
    cap = 2 * ((readers + total - 1) // total)
    slots = -(-total * cap // 16) * 16
    count = pair_mats.shape[0]
    vmem = pl.BlockSpec(memory_space=pltpu.VMEM)
    hbm = pl.BlockSpec(memory_space=pltpu.HBM)
    anywhere = pl.BlockSpec(memory_space=pl.ANY)
    params = pltpu.CompilerParams(vmem_limit_bytes=VMEM_LIMIT)

    def in_hbm(x):
        return pltpu.with_memory_space_constraint(x, pltpu.HBM)

    with jax.named_scope("item_rows"):
        items = [item_table] + [shift(item_table, "cache", q) for q in range(1, planes)]

    with jax.named_scope("ids"):
        users = [in_hbm(reader_users)] + [shift(reader_users, "shard", j) for j in range(1, total)]

    with jax.named_scope("states"):
        picked = pl.pallas_call(
            functools.partial(pick_kernel, total, cap),
            out_shape=jax.ShapeDtypeStruct((slots, width + half), jnp.bfloat16),
            in_specs=[anywhere] * total + [hbm, hbm],
            out_specs=vmem,
            scratch_shapes=[
                pltpu.VMEM(user_states.shape, jnp.bfloat16),
                pltpu.SMEM((total, readers), jnp.int32),
                pltpu.VMEM((1, half), jnp.int32),
                pltpu.SemaphoreType.DMA((total + 2,)),
            ],
            compiler_params=params,
            cost_estimate=pl.CostEstimate(flops=2 * slots * rows * width, bytes_accessed=1024 * 1024, transcendentals=0),
        )(*users, in_hbm(cand_items.reshape(1, half)), in_hbm(user_states))
        states = [picked] + [shift(picked, "shard", j) for j in range(1, total)]

    with jax.named_scope("pairs"):
        pair_parts, places = pl.pallas_call(
            functools.partial(pair_kernel, total, cap, slots, user_states.shape[0]),
            out_shape=(
                jax.ShapeDtypeStruct((planes, rows), jnp.float32),
                jax.ShapeDtypeStruct((total, half), jnp.int32),
            ),
            in_specs=[anywhere] * total + [hbm, hbm, hbm, anywhere],
            out_specs=(vmem, vmem),
            scratch_shapes=[
                pltpu.SMEM((total, readers), jnp.int32),
                pltpu.SMEM((2, count), jnp.int32),
                pltpu.VMEM((rows, width), jnp.bfloat16),
                pltpu.VMEM((K, K, count), jnp.bfloat16),
                pltpu.VMEM((width, rows), jnp.float32),
                pltpu.VMEM((width, rows), jnp.bfloat16),
                pltpu.VMEM((count * PITCH, LANES), jnp.float32),
                pltpu.SemaphoreType.DMA((6 + total,)),
            ],
            compiler_params=params,
            cost_estimate=pl.CostEstimate(flops=2 * count * K * K * rows * 16, bytes_accessed=4 * 1024 * 1024, transcendentals=0),
        )(*users, in_hbm(pair_fields.T), in_hbm(item_table), in_hbm(jnp.transpose(pair_mats, (1, 2, 0))), picked)
        pair_scores = lax.psum(pair_parts, ("cache", "pair"))

    with jax.named_scope("scores"):
        outs = pl.pallas_call(
            functools.partial(score_kernel, total, planes),
            out_shape=[jax.ShapeDtypeStruct((1, half), jnp.float32)] * total,
            in_specs=[vmem] * (total + planes + 2),
            out_specs=[vmem] * total,
            scratch_shapes=[
                pltpu.VMEM((total * slots, width), jnp.bfloat16),
                pltpu.VMEM((-(-total // 8) * 8, half), jnp.int32),
                pltpu.VMEM((planes * rows, 3 * total * slots), jnp.bfloat16),
            ],
            compiler_params=params,
            cost_estimate=pl.CostEstimate(flops=2 * 64 * 256 * width, bytes_accessed=2 * 1024 * 1024, transcendentals=0),
        )(*states, *items, places, pair_scores)

    with jax.named_scope("back"):
        result = outs[0]
        for j in range(1, total):
            result = result + shift(outs[j], "shard", -j)
    return result.reshape(half)


def solution(mesh):
    return jax.shard_map(
        body,
        mesh=mesh,
        in_specs=(
            P(("groups", "shard", "cache", "pair")),
            P(("groups", "shard", "cache", "pair")),
            P(("shard", "cache"), None),
            P(("groups", "shard"), None),
            P("pair", None, None),
            P("pair", None),
        ),
        out_specs=P(("groups", "shard", "cache", "pair")),
        check_vma=False,
    )
```

time: 44.1 us -> 37.3 us (0.85)
  waiting for transfers between devices: 10.6 us -> 3.74 us
  starting transfers between devices: 15 us -> 17.3 us
  local copies, waits for them, and re-layouts: 1.03 us -> 0.01 us
  Pallas kernels: 10.5 us -> 9.55 us
    ppermute x11 -> x10, waiting for transfers between devices: 10.6 us -> 3.74 us  [shift(): return lax.ppermute(x, axis, [(s, (s + step) % size) for s in range(size)])]
    ppermute x11 -> x10, starting transfers between devices: 15 us -> 17.3 us  [shift(): return lax.ppermute(x, axis, [(s, (s + step) % size) for s in range(size)])]
    dynamic_slice x1 -> x0, local copies, waits for them, and re-layouts: 1.02 us -> none  [body(): lax.dynamic_slice_in_dim(item_table, lax.axis_index('pair') * piece, piec...]
    pallas_call x1, Pallas kernels: 1.93 us -> 1.41 us  [body(): pl.pallas_call(functools.partial(pick_kernel, total, cap), out_shape=jax....]
  transfers between devices with their start and end apart: 11 -> 10, of which waited for: 6 -> 4; matrix products, arithmetic and copies ran while one was open for 0% -> 0% of each run, Pallas kernels for 4% -> 23%
where the time goes in v6:
time: 37.3 us; the launch traced here: 37.1 us
  starting transfers between devices  17.3 us (46%)
  Pallas kernels  9.55 us (26%)
  blocking collectives  5.91 us (16%)
  waiting for transfers between devices  3.74 us (10%)
  other arithmetic  0.52 us (1%)
    ppermute x10, starting transfers between devices, shift(): return lax.ppermute(x, axis, [(s, (s + step) % size) for s in range(size)])  17.3 us
    pallas_call x1, Pallas kernels, body(): pl.pallas_call(functools.partial(pair_kernel, total, cap, slots, user_sta...  7.25 us
    psum x1, blocking collectives, body(): pair_scores = lax.psum(pair_parts, ('cache', 'pair'))  5.91 us
    ppermute x10, waiting for transfers between devices, shift(): return lax.ppermute(x, axis, [(s, (s + step) % size) for s in range(size)])  3.74 us
    pallas_call x1, Pallas kernels, body(): pl.pallas_call(functools.partial(pick_kernel, total, cap), out_shape=jax....  1.41 us
    pallas_call x1, Pallas kernels, body(): pl.pallas_call(functools.partial(score_kernel, total, planes), out_shape=...  0.89 us
  transfers between devices with their start and end apart: 10, of which 4 were waited for; matrix products, arithmetic and copies ran while one was open for 0% of the time, Pallas kernels for 23%

profile of v6, /device:TPU:0, one launch (start us, length us, event | category | flops | bytes accessed | tf_op | source)
XLA Modules:
  0.0 37.1 jit_solution(15662972424779749488)
XLA Ops:
  0.0 2.9 %collective-permute-start.6 = (bf16[128,3072]{1,0:T(8,128)(2,1)}, bf16[128,3072]{1,0:T(8,128)(2,1)S(1)}, u32[]{:S(2)}, u32[]{:S(2)}) collective-permute-start(bf16[128,3072]{1,0:T(8,128)(2,1)} %refs_4_.1), channel_id=1, source_target_pairs={{0,2},{2,0},{1,3},{3,1},{4,6},{6,4},{5,7},{7,5},{8,10},{10,8},{9,1... | collective-permute-start | bytes 2359304 | tf_op jit(solution)/shard_map/item_rows/ppermute | solution.py:178
  2.9 1.6 %collective-permute-start = (s32[8]{0:T(128)}, s32[8]{0:T(128)S(1)}, u32[]{:S(2)}, u32[]{:S(2)}) collective-permute-start(s32[8]{0:T(128)} %refs_0_.3), channel_id=1, source_target_pairs={{0,4},{4,8},{8,12},{12,0},{1,5},{5,9},{9,13},{13,1},{2,6},{6,10},{... | collective-permute-start | bytes 104 | tf_op jit(solution)/shard_map/ids/ppermute | solution.py:178
  4.5 2.6 %collective-permute-start.1 = (s32[8]{0:T(128)}, s32[8]{0:T(128)S(1)}, u32[]{:S(2)}, u32[]{:S(2)}) collective-permute-start(s32[8]{0:T(128)} %refs_0_.3), channel_id=1, source_target_pairs={{0,8},{4,12},{8,0},{12,4},{1,9},{5,13},{9,1},{13,5},{2,10},{6,14},... | collective-permute-start | bytes 104 | tf_op jit(solution)/shard_map/ids/ppermute | solution.py:178
  7.1 1.3 %collective-permute-start.2 = (s32[8]{0:T(128)}, s32[8]{0:T(128)S(1)}, u32[]{:S(2)}, u32[]{:S(2)}) collective-permute-start(s32[8]{0:T(128)} %refs_0_.3), channel_id=1, source_target_pairs={{0,12},{4,0},{8,4},{12,8},{1,13},{5,1},{9,5},{13,9},{2,14},{6,2},{... | collective-permute-start | bytes 104 | tf_op jit(solution)/shard_map/ids/ppermute | solution.py:178
  8.5 0.0 collective-permute-done.refs_1_
  8.5 0.6 %collective-permute-done.1.refs_2_ = s32[8]{0:T(128)S(1)} collective-permute-done((s32[8]{0:T(128)}, s32[8]{0:T(128)S(1)}, u32[]{:S(2)}, u32[]{:S(2)}) %collective-permute-start.1) | collective-permute-done | bytes 64 | tf_op jit(solution)/shard_map/ids/ppermute | solution.py:178
  9.1 1.7 %collective-permute-done.2.refs_3_ = s32[8]{0:T(128)S(1)} collective-permute-done((s32[8]{0:T(128)}, s32[8]{0:T(128)S(1)}, u32[]{:S(2)}, u32[]{:S(2)}) %collective-permute-start.2) | collective-permute-done | bytes 64 | tf_op jit(solution)/shard_map/ids/ppermute | solution.py:178
  10.8 1.4 %states.1.refs_7_.refs_0_ = bf16[16,3200]{1,0:T(8,128)(2,1)S(1)} custom-call(s32[8]{0:T(128)} %refs_0_.3, s32[8]{0:T(128)S(1)} %collective-permute-done.refs_1_, s32[8]{0:T(128)S(1)} %collective-permute-done.1.refs_2_, s32[8]{0:T(128)S(1)} %collective-permute-done.2.refs_3_, s32[1,128]{1,0:T(1,128)} %bitcast.5, bf16[128,3072]{1,0:T(8,128)(2,1)} %refs_5_.2), custom_call_target="tpu_custom_call" | custom-call | flops 12582912 | bytes 1048576 | tf_op jit(solution)/shard_map/states/pallas_call | solution.py:205
  12.2 0.3 collective-permute-start.3
  12.5 3.5 %collective-permute-start.4 = (bf16[16,3200]{1,0:T(8,128)(2,1)S(1)}, bf16[16,3200]{1,0:T(8,128)(2,1)S(1)}, u32[]{:S(2)}, u32[]{:S(2)}) collective-permute-start(bf16[16,3200]{1,0:T(8,128)(2,1)S(1)} %states.1.refs_7_.refs_0_), channel_id=1, source_target_pairs={{0,8},{4,12},{8,0},{12,4},{1,9},{5,13},{9,1},{13,5},{2,10},{6,14},... | collective-permute-start | bytes 307208 | tf_op jit(solution)/shard_map/states/ppermute | solution.py:178
  16.0 0.1 collective-permute-start.5
  16.1 0.0 copy-start
  16.1 7.3 %pairs.1 = (f32[2,128]{1,0:T(2,128)S(1)}, s32[4,128]{1,0:T(4,128)S(1)}) custom-call(s32[8]{0:T(128)} %refs_0_.3, s32[8]{0:T(128)S(1)} %collective-permute-done.refs_1_, s32[8]{0:T(128)S(1)} %collective-permute-done.1.refs_2_, s32[8]{0:T(128)S(1)} %collective-permute-done.2.refs_3_, s32[2,256]{1,0:T(2,128)} %bitcast.7, bf16[128,3072]{1,0:T(8,128)(2,1)} %refs_4_.1, ...), custom_call_target="tpu_custom_call" | custom-call | flops 4294967296 | bytes 4194304 | tf_op jit(solution)/shard_map/pairs/pallas_call | solution.py:222
  23.3 5.9 %psum.7.refs_7_ = f32[2,128]{1,0:T(2,128)S(1)} all-reduce(f32[2,128]{1,0:T(2,128)S(1)} %get-tuple-element.12), channel_id=1, replica_groups=mesh['groups'=2,'shard'=4,'cache'=2,'pair'=2] {'cache','pair'}, use_global_device_ids=true, to_apply=%region_0.0 | all-reduce | flops 256 | bytes 2048 | tf_op jit(solution)/shard_map/pairs/psum | solution.py:243
  29.3 0.0 collective-permute-done.3.refs_1_
  29.3 0.0 collective-permute-done.4.refs_2_
  29.3 0.0 collective-permute-done.5.refs_3_
  29.3 0.0 collective-permute-done.6.refs_5_
  29.3 0.0 copy-done
  29.3 0.9 %scores.1 = (f32[1,128]{1,0:T(1,128)S(1)}, f32[1,128]{1,0:T(1,128)S(1)}, f32[1,128]{1,0:T(1,128)S(1)}, f32[1,128]{1,0:T(1,128)S(1)}) custom-call(bf16[16,3200]{1,0:T(8,128)(2,1)S(1)} %states.1.refs_7_.refs_0_, bf16[16,3200]{1,0:T(8,128)(2,1)S(1)} %collective-permute-done.3.refs_1_, bf16[16,3200]{1,0:T(8,128)(2,1)S(1)} %collective-permute-done.4.refs_2_, ...), custom_call_target="tpu_custom_call" | custom-call | flops 100663296 | bytes 2097152 | tf_op jit(solution)/shard_map/scores/pallas_call | solution.py:246
  30.2 2.0 %collective-permute-start.9 = (f32[1,128]{1,0:T(1,128)S(1)}, f32[1,128]{1,0:T(1,128)S(1)}, u32[]{:S(2)}, u32[]{:S(2)}) collective-permute-start(f32[1,128]{1,0:T(1,128)S(1)} %get-tuple-element.16), channel_id=1, source_target_pairs={{0,4},{4,8},{8,12},{12,0},{1,5},{5,9},{9,13},{13,1},{2,6},{6,10},{... | collective-permute-start | bytes 1544 | tf_op jit(solution)/shard_map/back/ppermute | solution.py:178
  32.1 0.2 collective-permute-start.8
  32.3 2.8 %collective-permute-start.7 = (f32[1,128]{1,0:T(1,128)S(1)}, f32[1,128]{1,0:T(1,128)S(1)}, u32[]{:S(2)}, u32[]{:S(2)}) collective-permute-start(f32[1,128]{1,0:T(1,128)S(1)} %get-tuple-element.14), channel_id=1, source_target_pairs={{0,12},{4,0},{8,4},{12,8},{1,13},{5,1},{9,5},{13,9},{2,14},{6,2},{... | collective-permute-start | bytes 1544 | tf_op jit(solution)/shard_map/back/ppermute | solution.py:178
  35.2 0.4 %collective-permute-done.9 = f32[1,128]{1,0:T(1,128)S(1)} collective-permute-done((f32[1,128]{1,0:T(1,128)S(1)}, f32[1,128]{1,0:T(1,128)S(1)}, u32[]{:S(2)}, u32[]{:S(2)}) %collective-permute-start.9) | collective-permute-done | bytes 544 | tf_op jit(solution)/shard_map/back/ppermute | solution.py:178
  35.6 1.0 %collective-permute-done.8 = f32[1,128]{1,0:T(1,128)S(1)} collective-permute-done((f32[1,128]{1,0:T(1,128)S(1)}, f32[1,128]{1,0:T(1,128)S(1)}, u32[]{:S(2)}, u32[]{:S(2)}) %collective-permute-start.8) | collective-permute-done | bytes 544 | tf_op jit(solution)/shard_map/back/ppermute | solution.py:178
  36.6 0.0 collective-permute-done.7
  36.6 0.5 %add_bitcast_fusion = f32[128]{0:T(128)} fusion(f32[1,128]{1,0:T(1,128)S(1)} %collective-permute-done.9, f32[1,128]{1,0:T(1,128)S(1)} %collective-permute-done.8, f32[1,128]{1,0:T(1,128)S(1)} %get-tuple-element.13, f32[1,128]{1,0:T(1,128)S(1)} %collective-permute-done.7), kind=kLoop, calls=%fused_computation | loop fusion | flops 384 | bytes 2560 | tf_op jit(solution)/shard_map/reshape | solution.py:264
Async XLA Ops:
  0.0 29.3 %collective-permute-start.6 = (bf16[128,3072]{1,0:T(8,128)(2,1)}, bf16[128,3072]{1,0:T(8,128)(2,1)S(1)}, u32[]{:S(2)}, u32[]{:S(2)}) collective-permute-start(bf16[128,3072]{1,0:T(8,128)(2,1)} %refs_4_.1), channel_id=1, source_target_pairs={{0,2},{2,0},{1,3},{3,1},{4,6},{6,4},{5,7},{7,5},{8,10},{10,8},{9,1... | collective-permute-start | bytes 2359304 | tf_op jit(solution)/shard_map/item_rows/ppermute | solution.py:178
  2.9 5.5 %collective-permute-start = (s32[8]{0:T(128)}, s32[8]{0:T(128)S(1)}, u32[]{:S(2)}, u32[]{:S(2)}) collective-permute-start(s32[8]{0:T(128)} %refs_0_.3), channel_id=1, source_target_pairs={{0,4},{4,8},{8,12},{12,0},{1,5},{5,9},{9,13},{13,1},{2,6},{6,10},{... | collective-permute-start | bytes 104 | tf_op jit(solution)/shard_map/ids/ppermute | solution.py:178
  4.5 4.6 %collective-permute-start.1 = (s32[8]{0:T(128)}, s32[8]{0:T(128)S(1)}, u32[]{:S(2)}, u32[]{:S(2)}) collective-permute-start(s32[8]{0:T(128)} %refs_0_.3), channel_id=1, source_target_pairs={{0,8},{4,12},{8,0},{12,4},{1,9},{5,13},{9,1},{13,5},{2,10},{6,14},... | collective-permute-start | bytes 104 | tf_op jit(solution)/shard_map/ids/ppermute | solution.py:178
  7.1 3.7 %collective-permute-start.2 = (s32[8]{0:T(128)}, s32[8]{0:T(128)S(1)}, u32[]{:S(2)}, u32[]{:S(2)}) collective-permute-start(s32[8]{0:T(128)} %refs_0_.3), channel_id=1, source_target_pairs={{0,12},{4,0},{8,4},{12,8},{1,13},{5,1},{9,5},{13,9},{2,14},{6,2},{... | collective-permute-start | bytes 104 | tf_op jit(solution)/shard_map/ids/ppermute | solution.py:178
  12.2 17.1 %collective-permute-start.3 = (bf16[16,3200]{1,0:T(8,128)(2,1)S(1)}, bf16[16,3200]{1,0:T(8,128)(2,1)S(1)}, u32[]{:S(2)}, u32[]{:S(2)}) collective-permute-start(bf16[16,3200]{1,0:T(8,128)(2,1)S(1)} %states.1.refs_7_.refs_0_), channel_id=1, source_target_pairs={{0,4},{4,8},{8,12},{12,0},{1,5},{5,9},{9,13},{13,1},{2,6},{6,10},{... | collective-permute-start | bytes 307208 | tf_op jit(solution)/shard_map/states/ppermute | solution.py:178
  12.5 16.8 %collective-permute-start.4 = (bf16[16,3200]{1,0:T(8,128)(2,1)S(1)}, bf16[16,3200]{1,0:T(8,128)(2,1)S(1)}, u32[]{:S(2)}, u32[]{:S(2)}) collective-permute-start(bf16[16,3200]{1,0:T(8,128)(2,1)S(1)} %states.1.refs_7_.refs_0_), channel_id=1, source_target_pairs={{0,8},{4,12},{8,0},{12,4},{1,9},{5,13},{9,1},{13,5},{2,10},{6,14},... | collective-permute-start | bytes 307208 | tf_op jit(solution)/shard_map/states/ppermute | solution.py:178
  16.0 13.3 %collective-permute-start.5 = (bf16[16,3200]{1,0:T(8,128)(2,1)S(1)}, bf16[16,3200]{1,0:T(8,128)(2,1)S(1)}, u32[]{:S(2)}, u32[]{:S(2)}) collective-permute-start(bf16[16,3200]{1,0:T(8,128)(2,1)S(1)} %states.1.refs_7_.refs_0_), channel_id=1, source_target_pairs={{0,12},{4,0},{8,4},{12,8},{1,13},{5,1},{9,5},{13,9},{2,14},{6,2},{... | collective-permute-start | bytes 307208 | tf_op jit(solution)/shard_map/states/ppermute | solution.py:178
  16.1 13.2 %copy-start = (bf16[128,3072]{1,0:T(8,128)(2,1)S(1)}, bf16[128,3072]{1,0:T(8,128)(2,1)}, u32[]{:S(2)}) copy-start(bf16[128,3072]{1,0:T(8,128)(2,1)} %refs_4_.1) | copy-start | bytes 2359300
  30.2 5.4 %collective-permute-start.9 = (f32[1,128]{1,0:T(1,128)S(1)}, f32[1,128]{1,0:T(1,128)S(1)}, u32[]{:S(2)}, u32[]{:S(2)}) collective-permute-start(f32[1,128]{1,0:T(1,128)S(1)} %get-tuple-element.16), channel_id=1, source_target_pairs={{0,4},{4,8},{8,12},{12,0},{1,5},{5,9},{9,13},{13,1},{2,6},{6,10},{... | collective-permute-start | bytes 1544 | tf_op jit(solution)/shard_map/back/ppermute | solution.py:178
  32.1 4.4 %collective-permute-start.8 = (f32[1,128]{1,0:T(1,128)S(1)}, f32[1,128]{1,0:T(1,128)S(1)}, u32[]{:S(2)}, u32[]{:S(2)}) collective-permute-start(f32[1,128]{1,0:T(1,128)S(1)} %get-tuple-element.15), channel_id=1, source_target_pairs={{0,8},{4,12},{8,0},{12,4},{1,9},{5,13},{9,1},{13,5},{2,10},{6,14},... | collective-permute-start | bytes 1544 | tf_op jit(solution)/shard_map/back/ppermute | solution.py:178
  32.3 4.3 %collective-permute-start.7 = (f32[1,128]{1,0:T(1,128)S(1)}, f32[1,128]{1,0:T(1,128)S(1)}, u32[]{:S(2)}, u32[]{:S(2)}) collective-permute-start(f32[1,128]{1,0:T(1,128)S(1)} %get-tuple-element.14), channel_id=1, source_target_pairs={{0,12},{4,0},{8,4},{12,8},{1,13},{5,1},{9,5},{13,9},{2,14},{6,2},{... | collective-permute-start | bytes 1544 | tf_op jit(solution)/shard_map/back/ppermute | solution.py:178

commit v7 on v6

--- a/solution.py
+++ b/solution.py
@@ -44,7 +44,7 @@
     for copy in id_fetches:
         copy.wait()
     for j in range(total):
-        source = ring(me - j, total)
+        source = me ^ j
         taken = jnp.int32(0)
         for r in range(asked.shape[1]):
             user = asked[j, r]
@@ -67,14 +67,14 @@
     lane = iota((1, half), 1) // (half // readers)
     rows = []
     for j in range(total):
-        source = ring(me - j, total)
+        source = me ^ j
         holders = [asked[j, r] // user_rows for r in range(readers)]
         row = jnp.zeros((1, half), jnp.int32)
         for r, holder in enumerate(holders):
             rank = jnp.int32(0)
             for earlier in holders[:r]:
                 rank = rank + (earlier == holder).astype(jnp.int32)
-            row = jnp.where(lane == r, ring(me - holder, total) * slots + source * cap + rank, row)
+            row = jnp.where(lane == r, (me ^ holder) * slots + source * cap + rank, row)
         rows.append(row)
     return rows
 
@@ -178,6 +178,10 @@
     return lax.ppermute(x, axis, [(s, (s + step) % size) for s in range(size)])
 
 
+def swap(x, axis, mask):
+    return lax.ppermute(x, axis, [(s, s ^ mask) for s in range(lax.axis_size(axis))])
+
+
 def body(cand_items, reader_users, item_table, user_states, pair_mats, pair_fields):
     total = lax.axis_size("shard")
     planes = lax.axis_size("cache")
@@ -199,7 +203,7 @@
         items = [item_table] + [shift(item_table, "cache", q) for q in range(1, planes)]
 
     with jax.named_scope("ids"):
-        users = [in_hbm(reader_users)] + [shift(reader_users, "shard", j) for j in range(1, total)]
+        users = [in_hbm(reader_users)] + [swap(reader_users, "shard", j) for j in range(1, total)]
 
     with jax.named_scope("states"):
         picked = pl.pallas_call(
@@ -216,7 +220,7 @@
             compiler_params=params,
             cost_estimate=pl.CostEstimate(flops=2 * slots * rows * width, bytes_accessed=1024 * 1024, transcendentals=0),
         )(*users, in_hbm(cand_items.reshape(1, half)), in_hbm(user_states))
-        states = [picked] + [shift(picked, "shard", j) for j in range(1, total)]
+        states = [picked] + [swap(picked, "shard", j) for j in range(1, total)]
 
     with jax.named_scope("pairs"):
         pair_parts, places = pl.pallas_call(
@@ -260,7 +264,7 @@
     with jax.named_scope("back"):
         result = outs[0]
         for j in range(1, total):
-            result = result + shift(outs[j], "shard", -j)
+            result = result + swap(outs[j], "shard", j)
     return result.reshape(half)
 
 

time: 37.3 us -> 39.1 us (1.048)
  waiting for transfers between devices: 3.74 us -> 6.78 us
  starting transfers between devices: 17.3 us -> 16.2 us
    ppermute x10 -> x1, starting transfers between devices: 17.3 us -> 2.94 us  [shift(): return lax.ppermute(x, axis, [(s, (s + step) % size) for s in range(size)])]
    ppermute x0 -> x9, starting transfers between devices: none -> 13.3 us  [swap(): lax.ppermute(x, axis, [(s, s ^ mask) for s in range(lax.axis_size(axis))])]
    ppermute x0 -> x9, waiting for transfers between devices: none -> 6.77 us  [swap(): lax.ppermute(x, axis, [(s, s ^ mask) for s in range(lax.axis_size(axis))])]
    ppermute x10 -> x1, waiting for transfers between devices: 3.74 us -> 0.01 us  [shift(): return lax.ppermute(x, axis, [(s, (s + step) % size) for s in range(size)])]
  transfers between devices with their start and end apart: 10 -> 10, of which waited for: 4 -> 4; matrix products, arithmetic and copies ran while one was open for 0% -> 0% of each run, Pallas kernels for 23% -> 22%
where the time goes in v7:
time: 39.1 us; the launch traced here: 39 us
  starting transfers between devices  16.2 us (41%)
  Pallas kernels  9.49 us (24%)
  waiting for transfers between devices  6.78 us (17%)
  blocking collectives  5.91 us (15%)
  other arithmetic  0.52 us (1%)
    ppermute x9, starting transfers between devices, swap(): lax.ppermute(x, axis, [(s, s ^ mask) for s in range(lax.axis_size(axis))])  13.3 us
    pallas_call x1, Pallas kernels, body(): pl.pallas_call(functools.partial(pair_kernel, total, cap, slots, user_sta...  7.19 us
    ppermute x9, waiting for transfers between devices, swap(): lax.ppermute(x, axis, [(s, s ^ mask) for s in range(lax.axis_size(axis))])  6.77 us
    psum x1, blocking collectives, body(): pair_scores = lax.psum(pair_parts, ('cache', 'pair'))  5.91 us
    ppermute x1, starting transfers between devices, shift(): return lax.ppermute(x, axis, [(s, (s + step) % size) for s in range(size)])  2.94 us
    pallas_call x1, Pallas kernels, body(): pl.pallas_call(functools.partial(pick_kernel, total, cap), out_shape=jax....  1.41 us
    pallas_call x1, Pallas kernels, body(): pl.pallas_call(functools.partial(score_kernel, total, planes), out_shape=...  0.89 us
  transfers between devices with their start and end apart: 10, of which 4 were waited for; matrix products, arithmetic and copies ran while one was open for 0% of the time, Pallas kernels for 22%

profile of v7, /device:TPU:0, one launch (start us, length us, event | category | flops | bytes accessed | tf_op | source)
XLA Modules:
  0.0 39.0 jit_solution(12476946394503135832)
XLA Ops:
  0.0 2.9 %collective-permute-start.6 = (bf16[128,3072]{1,0:T(8,128)(2,1)}, bf16[128,3072]{1,0:T(8,128)(2,1)S(1)}, u32[]{:S(2)}, u32[]{:S(2)}) collective-permute-start(bf16[128,3072]{1,0:T(8,128)(2,1)} %refs_4_.1), channel_id=1, source_target_pairs={{0,2},{2,0},{1,3},{3,1},{4,6},{6,4},{5,7},{7,5},{8,10},{10,8},{9,1... | collective-permute-start | bytes 2359304 | tf_op jit(solution)/shard_map/item_rows/ppermute | solution.py:178
  2.9 1.6 %collective-permute-start = (s32[8]{0:T(128)}, s32[8]{0:T(128)S(1)}, u32[]{:S(2)}, u32[]{:S(2)}) collective-permute-start(s32[8]{0:T(128)} %refs_0_.3), channel_id=1, source_target_pairs={{0,4},{4,0},{8,12},{12,8},{1,5},{5,1},{9,13},{13,9},{2,6},{6,2},{1... | collective-permute-start | bytes 104 | tf_op jit(solution)/shard_map/ids/ppermute | solution.py:182
  4.5 2.6 %collective-permute-start.1 = (s32[8]{0:T(128)}, s32[8]{0:T(128)S(1)}, u32[]{:S(2)}, u32[]{:S(2)}) collective-permute-start(s32[8]{0:T(128)} %refs_0_.3), channel_id=1, source_target_pairs={{0,8},{4,12},{8,0},{12,4},{1,9},{5,13},{9,1},{13,5},{2,10},{6,14},... | collective-permute-start | bytes 104 | tf_op jit(solution)/shard_map/ids/ppermute | solution.py:182
  7.1 0.2 collective-permute-start.2
  7.3 0.0 collective-permute-done.refs_1_
  7.3 1.8 %collective-permute-done.1.refs_2_ = s32[8]{0:T(128)S(1)} collective-permute-done((s32[8]{0:T(128)}, s32[8]{0:T(128)S(1)}, u32[]{:S(2)}, u32[]{:S(2)}) %collective-permute-start.1) | collective-permute-done | bytes 64 | tf_op jit(solution)/shard_map/ids/ppermute | solution.py:182
  9.1 3.5 %collective-permute-done.2.refs_3_ = s32[8]{0:T(128)S(1)} collective-permute-done((s32[8]{0:T(128)}, s32[8]{0:T(128)S(1)}, u32[]{:S(2)}, u32[]{:S(2)}) %collective-permute-start.2) | collective-permute-done | bytes 64 | tf_op jit(solution)/shard_map/ids/ppermute | solution.py:182
  12.6 1.4 %states.1.refs_7_.refs_0_ = bf16[16,3200]{1,0:T(8,128)(2,1)S(1)} custom-call(s32[8]{0:T(128)} %refs_0_.3, s32[8]{0:T(128)S(1)} %collective-permute-done.refs_1_, s32[8]{0:T(128)S(1)} %collective-permute-done.1.refs_2_, s32[8]{0:T(128)S(1)} %collective-permute-done.2.refs_3_, s32[1,128]{1,0:T(1,128)} %bitcast.5, bf16[128,3072]{1,0:T(8,128)(2,1)} %refs_5_.2), custom_call_target="tpu_custom_call" | custom-call | flops 12582912 | bytes 1048576 | tf_op jit(solution)/shard_map/states/pallas_call | solution.py:209
  14.0 0.1 collective-permute-start.3
  14.1 0.8 %collective-permute-start.4 = (bf16[16,3200]{1,0:T(8,128)(2,1)S(1)}, bf16[16,3200]{1,0:T(8,128)(2,1)S(1)}, u32[]{:S(2)}, u32[]{:S(2)}) collective-permute-start(bf16[16,3200]{1,0:T(8,128)(2,1)S(1)} %states.1.refs_7_.refs_0_), channel_id=1, source_target_pairs={{0,8},{4,12},{8,0},{12,4},{1,9},{5,13},{9,1},{13,5},{2,10},{6,14},... | collective-permute-start | bytes 307208 | tf_op jit(solution)/shard_map/states/ppermute | solution.py:182
  14.8 3.6 %collective-permute-start.5 = (bf16[16,3200]{1,0:T(8,128)(2,1)S(1)}, bf16[16,3200]{1,0:T(8,128)(2,1)S(1)}, u32[]{:S(2)}, u32[]{:S(2)}) collective-permute-start(bf16[16,3200]{1,0:T(8,128)(2,1)S(1)} %states.1.refs_7_.refs_0_), channel_id=1, source_target_pairs={{0,12},{4,8},{8,4},{12,0},{1,13},{5,9},{9,5},{13,1},{2,14},{6,10},... | collective-permute-start | bytes 307208 | tf_op jit(solution)/shard_map/states/ppermute | solution.py:182
  18.4 0.0 copy-start
  18.5 7.2 %pairs.1 = (f32[2,128]{1,0:T(2,128)S(1)}, s32[4,128]{1,0:T(4,128)S(1)}) custom-call(s32[8]{0:T(128)} %refs_0_.3, s32[8]{0:T(128)S(1)} %collective-permute-done.refs_1_, s32[8]{0:T(128)S(1)} %collective-permute-done.1.refs_2_, s32[8]{0:T(128)S(1)} %collective-permute-done.2.refs_3_, s32[2,256]{1,0:T(2,128)} %bitcast.7, bf16[128,3072]{1,0:T(8,128)(2,1)} %refs_4_.1, ...), custom_call_target="tpu_custom_call" | custom-call | flops 4294967296 | bytes 4194304 | tf_op jit(solution)/shard_map/pairs/pallas_call | solution.py:226
  25.6 5.9 %psum.7.refs_7_ = f32[2,128]{1,0:T(2,128)S(1)} all-reduce(f32[2,128]{1,0:T(2,128)S(1)} %get-tuple-element.12), channel_id=1, replica_groups=mesh['groups'=2,'shard'=4,'cache'=2,'pair'=2] {'cache','pair'}, use_global_device_ids=true, to_apply=%region_0.0 | all-reduce | flops 256 | bytes 2048 | tf_op jit(solution)/shard_map/pairs/psum | solution.py:247
  31.6 0.0 collective-permute-done.3.refs_1_
  31.6 0.0 collective-permute-done.4.refs_2_
  31.6 0.0 collective-permute-done.5.refs_3_
  31.6 0.0 collective-permute-done.6.refs_5_
  31.6 0.0 copy-done
  31.6 0.9 %scores.1 = (f32[1,128]{1,0:T(1,128)S(1)}, f32[1,128]{1,0:T(1,128)S(1)}, f32[1,128]{1,0:T(1,128)S(1)}, f32[1,128]{1,0:T(1,128)S(1)}) custom-call(bf16[16,3200]{1,0:T(8,128)(2,1)S(1)} %states.1.refs_7_.refs_0_, bf16[16,3200]{1,0:T(8,128)(2,1)S(1)} %collective-permute-done.3.refs_1_, bf16[16,3200]{1,0:T(8,128)(2,1)S(1)} %collective-permute-done.4.refs_2_, ...), custom_call_target="tpu_custom_call" | custom-call | flops 100663296 | bytes 2097152 | tf_op jit(solution)/shard_map/scores/pallas_call | solution.py:250
  32.5 0.1 collective-permute-start.9
  32.6 0.6 %collective-permute-start.8 = (f32[1,128]{1,0:T(1,128)S(1)}, f32[1,128]{1,0:T(1,128)S(1)}, u32[]{:S(2)}, u32[]{:S(2)}) collective-permute-start(f32[1,128]{1,0:T(1,128)S(1)} %get-tuple-element.15), channel_id=1, source_target_pairs={{0,8},{4,12},{8,0},{12,4},{1,9},{5,13},{9,1},{13,5},{2,10},{6,14},... | collective-permute-start | bytes 1544 | tf_op jit(solution)/shard_map/back/ppermute | solution.py:182
  33.2 3.7 %collective-permute-start.7 = (f32[1,128]{1,0:T(1,128)S(1)}, f32[1,128]{1,0:T(1,128)S(1)}, u32[]{:S(2)}, u32[]{:S(2)}) collective-permute-start(f32[1,128]{1,0:T(1,128)S(1)} %get-tuple-element.14), channel_id=1, source_target_pairs={{0,4},{4,0},{8,12},{12,8},{1,5},{5,1},{9,13},{13,9},{2,6},{6,2},{1... | collective-permute-start | bytes 1544 | tf_op jit(solution)/shard_map/back/ppermute | solution.py:182
  36.9 0.9 %collective-permute-done.9 = f32[1,128]{1,0:T(1,128)S(1)} collective-permute-done((f32[1,128]{1,0:T(1,128)S(1)}, f32[1,128]{1,0:T(1,128)S(1)}, u32[]{:S(2)}, u32[]{:S(2)}) %collective-permute-start.9) | collective-permute-done | bytes 544 | tf_op jit(solution)/shard_map/back/ppermute | solution.py:182
  37.9 0.0 collective-permute-done.8
  37.9 0.6 %collective-permute-done.7 = f32[1,128]{1,0:T(1,128)S(1)} collective-permute-done((f32[1,128]{1,0:T(1,128)S(1)}, f32[1,128]{1,0:T(1,128)S(1)}, u32[]{:S(2)}, u32[]{:S(2)}) %collective-permute-start.7) | collective-permute-done | bytes 544 | tf_op jit(solution)/shard_map/back/ppermute | solution.py:182
  38.5 0.5 %add_bitcast_fusion = f32[128]{0:T(128)} fusion(f32[1,128]{1,0:T(1,128)S(1)} %collective-permute-done.9, f32[1,128]{1,0:T(1,128)S(1)} %collective-permute-done.8, f32[1,128]{1,0:T(1,128)S(1)} %get-tuple-element.13, f32[1,128]{1,0:T(1,128)S(1)} %collective-permute-done.7), kind=kLoop, calls=%fused_computation | loop fusion | flops 384 | bytes 2560 | tf_op jit(solution)/shard_map/reshape | solution.py:268
Async XLA Ops:
  0.0 31.6 %collective-permute-start.6 = (bf16[128,3072]{1,0:T(8,128)(2,1)}, bf16[128,3072]{1,0:T(8,128)(2,1)S(1)}, u32[]{:S(2)}, u32[]{:S(2)}) collective-permute-start(bf16[128,3072]{1,0:T(8,128)(2,1)} %refs_4_.1), channel_id=1, source_target_pairs={{0,2},{2,0},{1,3},{3,1},{4,6},{6,4},{5,7},{7,5},{8,10},{10,8},{9,1... | collective-permute-start | bytes 2359304 | tf_op jit(solution)/shard_map/item_rows/ppermute | solution.py:178
  2.9 4.4 %collective-permute-start = (s32[8]{0:T(128)}, s32[8]{0:T(128)S(1)}, u32[]{:S(2)}, u32[]{:S(2)}) collective-permute-start(s32[8]{0:T(128)} %refs_0_.3), channel_id=1, source_target_pairs={{0,4},{4,0},{8,12},{12,8},{1,5},{5,1},{9,13},{13,9},{2,6},{6,2},{1... | collective-permute-start | bytes 104 | tf_op jit(solution)/shard_map/ids/ppermute | solution.py:182
  4.5 4.6 %collective-permute-start.1 = (s32[8]{0:T(128)}, s32[8]{0:T(128)S(1)}, u32[]{:S(2)}, u32[]{:S(2)}) collective-permute-start(s32[8]{0:T(128)} %refs_0_.3), channel_id=1, source_target_pairs={{0,8},{4,12},{8,0},{12,4},{1,9},{5,13},{9,1},{13,5},{2,10},{6,14},... | collective-permute-start | bytes 104 | tf_op jit(solution)/shard_map/ids/ppermute | solution.py:182
  7.1 5.5 %collective-permute-start.2 = (s32[8]{0:T(128)}, s32[8]{0:T(128)S(1)}, u32[]{:S(2)}, u32[]{:S(2)}) collective-permute-start(s32[8]{0:T(128)} %refs_0_.3), channel_id=1, source_target_pairs={{0,12},{4,8},{8,4},{12,0},{1,13},{5,9},{9,5},{13,1},{2,14},{6,10},... | collective-permute-start | bytes 104 | tf_op jit(solution)/shard_map/ids/ppermute | solution.py:182
  14.0 17.6 %collective-permute-start.3 = (bf16[16,3200]{1,0:T(8,128)(2,1)S(1)}, bf16[16,3200]{1,0:T(8,128)(2,1)S(1)}, u32[]{:S(2)}, u32[]{:S(2)}) collective-permute-start(bf16[16,3200]{1,0:T(8,128)(2,1)S(1)} %states.1.refs_7_.refs_0_), channel_id=1, source_target_pairs={{0,4},{4,0},{8,12},{12,8},{1,5},{5,1},{9,13},{13,9},{2,6},{6,2},{1... | collective-permute-start | bytes 307208 | tf_op jit(solution)/shard_map/states/ppermute | solution.py:182
  14.1 17.5 %collective-permute-start.4 = (bf16[16,3200]{1,0:T(8,128)(2,1)S(1)}, bf16[16,3200]{1,0:T(8,128)(2,1)S(1)}, u32[]{:S(2)}, u32[]{:S(2)}) collective-permute-start(bf16[16,3200]{1,0:T(8,128)(2,1)S(1)} %states.1.refs_7_.refs_0_), channel_id=1, source_target_pairs={{0,8},{4,12},{8,0},{12,4},{1,9},{5,13},{9,1},{13,5},{2,10},{6,14},... | collective-permute-start | bytes 307208 | tf_op jit(solution)/shard_map/states/ppermute | solution.py:182
  14.8 16.7 %collective-permute-start.5 = (bf16[16,3200]{1,0:T(8,128)(2,1)S(1)}, bf16[16,3200]{1,0:T(8,128)(2,1)S(1)}, u32[]{:S(2)}, u32[]{:S(2)}) collective-permute-start(bf16[16,3200]{1,0:T(8,128)(2,1)S(1)} %states.1.refs_7_.refs_0_), channel_id=1, source_target_pairs={{0,12},{4,8},{8,4},{12,0},{1,13},{5,9},{9,5},{13,1},{2,14},{6,10},... | collective-permute-start | bytes 307208 | tf_op jit(solution)/shard_map/states/ppermute | solution.py:182
  18.4 13.1 %copy-start = (bf16[128,3072]{1,0:T(8,128)(2,1)S(1)}, bf16[128,3072]{1,0:T(8,128)(2,1)}, u32[]{:S(2)}) copy-start(bf16[128,3072]{1,0:T(8,128)(2,1)} %refs_4_.1) | copy-start | bytes 2359300
  32.5 5.4 %collective-permute-start.9 = (f32[1,128]{1,0:T(1,128)S(1)}, f32[1,128]{1,0:T(1,128)S(1)}, u32[]{:S(2)}, u32[]{:S(2)}) collective-permute-start(f32[1,128]{1,0:T(1,128)S(1)} %get-tuple-element.16), channel_id=1, source_target_pairs={{0,12},{4,8},{8,4},{12,0},{1,13},{5,9},{9,5},{13,1},{2,14},{6,10},... | collective-permute-start | bytes 1544 | tf_op jit(solution)/shard_map/back/ppermute | solution.py:182
  32.6 5.3 %collective-permute-start.8 = (f32[1,128]{1,0:T(1,128)S(1)}, f32[1,128]{1,0:T(1,128)S(1)}, u32[]{:S(2)}, u32[]{:S(2)}) collective-permute-start(f32[1,128]{1,0:T(1,128)S(1)} %get-tuple-element.15), channel_id=1, source_target_pairs={{0,8},{4,12},{8,0},{12,4},{1,9},{5,13},{9,1},{13,5},{2,10},{6,14},... | collective-permute-start | bytes 1544 | tf_op jit(solution)/shard_map/back/ppermute | solution.py:182
  33.2 5.3 %collective-permute-start.7 = (f32[1,128]{1,0:T(1,128)S(1)}, f32[1,128]{1,0:T(1,128)S(1)}, u32[]{:S(2)}, u32[]{:S(2)}) collective-permute-start(f32[1,128]{1,0:T(1,128)S(1)} %get-tuple-element.14), channel_id=1, source_target_pairs={{0,4},{4,0},{8,12},{12,8},{1,5},{5,1},{9,13},{13,9},{2,6},{6,2},{1... | collective-permute-start | bytes 1544 | tf_op jit(solution)/shard_map/back/ppermute | solution.py:182

commit v8 on v6

--- a/solution.py
+++ b/solution.py
@@ -29,7 +29,8 @@
 
 
 def pick_kernel(total, cap, *refs):
-    users, (own_cands, states_hbm, out, held, asked, cands, sems) = refs[:total], refs[total:]
+    users, (own_cands, states_hbm, later, out, held, asked, cands, sems) = refs[:total], refs[total:]
+    del later
     fetch = pltpu.make_async_copy(states_hbm, held, sems.at[total])
     digit_fetch = pltpu.make_async_copy(own_cands, cands, sems.at[total + 1])
     id_fetches = [pltpu.make_async_copy(users[j], asked.at[j], sems.at[j]) for j in range(total)]
@@ -79,22 +80,16 @@
     return rows
 
 
-def pair_kernel(total, cap, slots, user_rows, *refs):
-    users, refs = refs[:total], refs[total:]
-    fields_hbm, items_hbm, mats_hbm, picked, out, places, asked, fields, items, mats, rows32, rows16, stacked, sems = refs
-    del picked
-    chunks = 4
+def turn_kernel(items_hbm, mats_hbm, rows32, rows16, mats, items, sems):
+    chunks = sems.shape[0] - 1
     wide = items.shape[1] // chunks
     item_fetches = [
         pltpu.make_async_copy(items_hbm.at[:, pl.ds(t * wide, wide)], items.at[:, pl.ds(t * wide, wide)], sems.at[t])
         for t in range(chunks)
     ]
     mats_fetch = pltpu.make_async_copy(mats_hbm, mats, sems.at[chunks])
-    fields_fetch = pltpu.make_async_copy(fields_hbm, fields, sems.at[chunks + 1])
-    id_fetches = [pltpu.make_async_copy(users[j], asked.at[j], sems.at[chunks + 2 + j]) for j in range(total)]
-    for copy in item_fetches + [mats_fetch, fields_fetch] + id_fetches:
+    for copy in item_fetches + [mats_fetch]:
         copy.start()
-    count = mats.shape[2]
     eye = (iota((LANES, LANES), 0) == iota((LANES, LANES), 1)).astype(jnp.bfloat16)
     for t in range(items.shape[1] // LANES):
         if t * LANES % wide == 0:
@@ -102,12 +97,25 @@
         turned = dot(eye, items[:, t * LANES:(t + 1) * LANES], NT)
         rows32[t * LANES:(t + 1) * LANES, :] = turned
         rows16[t * LANES:(t + 1) * LANES, :] = turned.astype(jnp.bfloat16)
+    mats_fetch.wait()
+
+
+def pair_kernel(total, cap, slots, user_rows, *refs):
+    users, refs = refs[:total], refs[total:]
+    fields_hbm, rows32, rows16, mats, picked, out, places, asked, fields, stacked, sems = refs
+    del picked
+    fields_fetch = pltpu.make_async_copy(fields_hbm, fields, sems.at[total])
+    id_fetches = [pltpu.make_async_copy(users[j], asked.at[j], sems.at[j]) for j in range(total)]
+    for copy in [fields_fetch] + id_fetches:
+        copy.start()
+    count = mats.shape[2]
     eye_pairs = (iota((count, count), 0) == iota((count, count), 1)).astype(jnp.bfloat16)
     side = (iota((count, LANES), 0) % 2 == 0) == (iota((count, LANES), 1) < K)
-    mats_fetch.wait()
-    for k in range(K):
-        both = jnp.concatenate([mats[k], mats[k]], axis=0)
-        stacked[pl.ds(k, count, stride=PITCH), :] = jnp.where(side, dot(eye_pairs, both, NT), 0.0)
+    for k in range(0, K, 2):
+        twice = jnp.concatenate([mats[k], mats[k], mats[k + 1], mats[k + 1]], axis=0)
+        turned = dot(eye_pairs, twice, NT)
+        stacked[pl.ds(k, count, stride=PITCH), :] = jnp.where(side, turned[:, :LANES], 0.0)
+        stacked[pl.ds(k + 1, count, stride=PITCH), :] = jnp.where(side, turned[:, LANES:], 0.0)
     fields_fetch.wait()
 
     def two(step, total):
@@ -122,7 +130,7 @@
         moved = dot(jnp.concatenate(lefts, axis=0), jnp.concatenate(rights, axis=0), NN)
         return total + moved * jnp.concatenate(mults, axis=0)
 
-    sums = lax.fori_loop(0, count // 2, two, jnp.zeros((2 * K, items.shape[0]), jnp.float32), unroll=16)
+    sums = lax.fori_loop(0, count // 2, two, jnp.zeros((2 * K, rows32.shape[1]), jnp.float32), unroll=16)
     mine = iota(out.shape, 0) == lax.axis_index("cache")
     out[...] = jnp.where(mine, jnp.sum(sums, axis=0, keepdims=True), 0.0)
     for copy in id_fetches:
@@ -201,11 +209,26 @@
     with jax.named_scope("ids"):
         users = [in_hbm(reader_users)] + [shift(reader_users, "shard", j) for j in range(1, total)]
 
+    with jax.named_scope("turn"):
+        turned = pl.pallas_call(
+            turn_kernel,
+            out_shape=(
+                jax.ShapeDtypeStruct((width, rows), jnp.float32),
+                jax.ShapeDtypeStruct((width, rows), jnp.bfloat16),
+                jax.ShapeDtypeStruct((K, K, count), jnp.bfloat16),
+            ),
+            in_specs=[hbm, hbm],
+            out_specs=(vmem, vmem, vmem),
+            scratch_shapes=[pltpu.VMEM((rows, width), jnp.bfloat16), pltpu.SemaphoreType.DMA((5,))],
+            compiler_params=params,
+            cost_estimate=pl.CostEstimate(flops=2 * rows * rows * width * 16, bytes_accessed=8 * 1024 * 1024, transcendentals=0),
+        )(in_hbm(item_table), in_hbm(jnp.transpose(pair_mats, (1, 2, 0))))
+
     with jax.named_scope("states"):
         picked = pl.pallas_call(
             functools.partial(pick_kernel, total, cap),
             out_shape=jax.ShapeDtypeStruct((slots, width + half), jnp.bfloat16),
-            in_specs=[anywhere] * total + [hbm, hbm],
+            in_specs=[anywhere] * total + [hbm, hbm, anywhere],
             out_specs=vmem,
             scratch_shapes=[
                 pltpu.VMEM(user_states.shape, jnp.bfloat16),
@@ -215,7 +238,7 @@
             ],
             compiler_params=params,
             cost_estimate=pl.CostEstimate(flops=2 * slots * rows * width, bytes_accessed=1024 * 1024, transcendentals=0),
-        )(*users, in_hbm(cand_items.reshape(1, half)), in_hbm(user_states))
+        )(*users, in_hbm(cand_items.reshape(1, half)), in_hbm(user_states), turned[1])
         states = [picked] + [shift(picked, "shard", j) for j in range(1, total)]
 
     with jax.named_scope("pairs"):
@@ -225,21 +248,17 @@
                 jax.ShapeDtypeStruct((planes, rows), jnp.float32),
                 jax.ShapeDtypeStruct((total, half), jnp.int32),
             ),
-            in_specs=[anywhere] * total + [hbm, hbm, hbm, anywhere],
+            in_specs=[anywhere] * total + [hbm, vmem, vmem, vmem, anywhere],
             out_specs=(vmem, vmem),
             scratch_shapes=[
                 pltpu.SMEM((total, readers), jnp.int32),
                 pltpu.SMEM((2, count), jnp.int32),
-                pltpu.VMEM((rows, width), jnp.bfloat16),
-                pltpu.VMEM((K, K, count), jnp.bfloat16),
-                pltpu.VMEM((width, rows), jnp.float32),
-                pltpu.VMEM((width, rows), jnp.bfloat16),
                 pltpu.VMEM((count * PITCH, LANES), jnp.float32),
-                pltpu.SemaphoreType.DMA((6 + total,)),
+                pltpu.SemaphoreType.DMA((1 + total,)),
             ],
             compiler_params=params,
             cost_estimate=pl.CostEstimate(flops=2 * count * K * K * rows * 16, bytes_accessed=4 * 1024 * 1024, transcendentals=0),
-        )(*users, in_hbm(pair_fields.T), in_hbm(item_table), in_hbm(jnp.transpose(pair_mats, (1, 2, 0))), picked)
+        )(*users, in_hbm(pair_fields.T), *turned, picked)
         pair_scores = lax.psum(pair_parts, ("cache", "pair"))
 
     with jax.named_scope("scores"):

time: 37.3 us -> 37.7 us (1.011)
  waiting for transfers between devices: 3.74 us -> 4.98 us
  starting transfers between devices: 17.3 us -> 16.4 us
    pallas_call x0 -> x1, Pallas kernels: none -> 2.01 us  [body(): pl.pallas_call(turn_kernel, out_shape=(jax.ShapeDtypeStruct((width, rows)...]
    pallas_call x1, Pallas kernels: 7.25 us -> 5.26 us  [body(): pl.pallas_call(functools.partial(pair_kernel, total, cap, slots, user_sta...]
    ppermute x10, waiting for transfers between devices: 3.74 us -> 4.98 us  [shift(): return lax.ppermute(x, axis, [(s, (s + step) % size) for s in range(size)])]
    ppermute x10, starting transfers between devices: 17.3 us -> 16.4 us  [shift(): return lax.ppermute(x, axis, [(s, (s + step) % size) for s in range(size)])]
  transfers between devices with their start and end apart: 10 -> 10, of which waited for: 4 -> 3; matrix products, arithmetic and copies ran while one was open for 0% -> 0% of each run, Pallas kernels for 23% -> 23%
where the time goes in v8:
time: 37.7 us; the launch traced here: 37.5 us
  starting transfers between devices  16.4 us (44%)
  Pallas kernels  9.57 us (25%)
  blocking collectives  5.91 us (16%)
  waiting for transfers between devices  4.98 us (13%)
  other arithmetic  0.52 us (1%)
    ppermute x10, starting transfers between devices, shift(): return lax.ppermute(x, axis, [(s, (s + step) % size) for s in range(size)])  16.4 us
    psum x1, blocking collectives, body(): pair_scores = lax.psum(pair_parts, ('cache', 'pair'))  5.91 us
    pallas_call x1, Pallas kernels, body(): pl.pallas_call(functools.partial(pair_kernel, total, cap, slots, user_sta...  5.26 us
    ppermute x10, waiting for transfers between devices, shift(): return lax.ppermute(x, axis, [(s, (s + step) % size) for s in range(size)])  4.98 us
    pallas_call x1, Pallas kernels, body(): pl.pallas_call(turn_kernel, out_shape=(jax.ShapeDtypeStruct((width, rows)...  2.01 us
    pallas_call x1, Pallas kernels, body(): pl.pallas_call(functools.partial(pick_kernel, total, cap), out_shape=jax....  1.41 us
    pallas_call x1, Pallas kernels, body(): pl.pallas_call(functools.partial(score_kernel, total, planes), out_shape=...  0.89 us
  transfers between devices with their start and end apart: 10, of which 3 were waited for; matrix products, arithmetic and copies ran while one was open for 0% of the time, Pallas kernels for 23%

profile of v8, /device:TPU:0, one launch (start us, length us, event | category | flops | bytes accessed | tf_op | source)
XLA Modules:
  0.0 37.5 jit_solution(14503774690806614657)
XLA Ops:
  0.0 2.9 %collective-permute-start.6 = (bf16[128,3072]{1,0:T(8,128)(2,1)}, bf16[128,3072]{1,0:T(8,128)(2,1)S(1)}, u32[]{:S(2)}, u32[]{:S(2)}) collective-permute-start(bf16[128,3072]{1,0:T(8,128)(2,1)} %refs_4_.1), channel_id=1, source_target_pairs={{0,2},{2,0},{1,3},{3,1},{4,6},{6,4},{5,7},{7,5},{8,10},{10,8},{9,1... | collective-permute-start | bytes 2359304 | tf_op jit(solution)/shard_map/item_rows/ppermute | solution.py:186
  2.9 1.6 %collective-permute-start = (s32[8]{0:T(128)}, s32[8]{0:T(128)S(1)}, u32[]{:S(2)}, u32[]{:S(2)}) collective-permute-start(s32[8]{0:T(128)} %refs_0_.3), channel_id=1, source_target_pairs={{0,4},{4,8},{8,12},{12,0},{1,5},{5,9},{9,13},{13,1},{2,6},{6,10},{... | collective-permute-start | bytes 104 | tf_op jit(solution)/shard_map/ids/ppermute | solution.py:186
  4.5 2.6 %collective-permute-start.1 = (s32[8]{0:T(128)}, s32[8]{0:T(128)S(1)}, u32[]{:S(2)}, u32[]{:S(2)}) collective-permute-start(s32[8]{0:T(128)} %refs_0_.3), channel_id=1, source_target_pairs={{0,8},{4,12},{8,0},{12,4},{1,9},{5,13},{9,1},{13,5},{2,10},{6,14},... | collective-permute-start | bytes 104 | tf_op jit(solution)/shard_map/ids/ppermute | solution.py:186
  7.1 1.3 %collective-permute-start.2 = (s32[8]{0:T(128)}, s32[8]{0:T(128)S(1)}, u32[]{:S(2)}, u32[]{:S(2)}) collective-permute-start(s32[8]{0:T(128)} %refs_0_.3), channel_id=1, source_target_pairs={{0,12},{4,0},{8,4},{12,8},{1,13},{5,1},{9,5},{13,9},{2,14},{6,2},{... | collective-permute-start | bytes 104 | tf_op jit(solution)/shard_map/ids/ppermute | solution.py:186
  8.5 2.0 %turn.1 = (f32[3072,128]{1,0:T(8,128)S(1)}, bf16[3072,128]{1,0:T(8,128)(2,1)S(1)}, bf16[64,64,256]{2,1,0:T(8,128)(2,1)S(1)}) custom-call(bf16[128,3072]{1,0:T(8,128)(2,1)} %refs_4_.1, bf16[64,64,256]{2,1,0:T(8,128)(2,1)} %bitcast.6), custom_call_target="tpu_custom_call" | custom-call | flops 1610612736 | bytes 8388608 | tf_op jit(solution)/shard_map/turn/pallas_call | solution.py:213
  10.5 0.0 collective-permute-done.refs_1_
  10.5 0.0 collective-permute-done.1.refs_2_
  10.5 0.3 collective-permute-done.2.refs_3_
  10.8 1.4 %states.1.refs_8_.refs_0_ = bf16[16,3200]{1,0:T(8,128)(2,1)S(1)} custom-call(s32[8]{0:T(128)} %refs_0_.3, s32[8]{0:T(128)S(1)} %collective-permute-done.refs_1_, s32[8]{0:T(128)S(1)} %collective-permute-done.1.refs_2_, s32[8]{0:T(128)S(1)} %collective-permute-done.2.refs_3_, s32[1,128]{1,0:T(1,128)} %bitcast.5, bf16[128,3072]{1,0:T(8,128)(2,1)} %refs_5_.1, ...), custom_call_target="tpu_custom_call" | custom-call | flops 12582912 | bytes 1048576 | tf_op jit(solution)/shard_map/states/pallas_call | solution.py:228
  12.2 0.5 %collective-permute-start.3 = (bf16[16,3200]{1,0:T(8,128)(2,1)S(1)}, bf16[16,3200]{1,0:T(8,128)(2,1)S(1)}, u32[]{:S(2)}, u32[]{:S(2)}) collective-permute-start(bf16[16,3200]{1,0:T(8,128)(2,1)S(1)} %states.1.refs_8_.refs_0_), channel_id=1, source_target_pairs={{0,4},{4,8},{8,12},{12,0},{1,5},{5,9},{9,13},{13,1},{2,6},{6,10},{... | collective-permute-start | bytes 307208 | tf_op jit(solution)/shard_map/states/ppermute | solution.py:186
  12.7 3.3 %collective-permute-start.4 = (bf16[16,3200]{1,0:T(8,128)(2,1)S(1)}, bf16[16,3200]{1,0:T(8,128)(2,1)S(1)}, u32[]{:S(2)}, u32[]{:S(2)}) collective-permute-start(bf16[16,3200]{1,0:T(8,128)(2,1)S(1)} %states.1.refs_8_.refs_0_), channel_id=1, source_target_pairs={{0,8},{4,12},{8,0},{12,4},{1,9},{5,13},{9,1},{13,5},{2,10},{6,14},... | collective-permute-start | bytes 307208 | tf_op jit(solution)/shard_map/states/ppermute | solution.py:186
  16.0 0.1 collective-permute-start.5
  16.1 0.0 copy-start
  16.1 5.3 %pairs.1 = (f32[2,128]{1,0:T(2,128)S(1)}, s32[4,128]{1,0:T(4,128)S(1)}) custom-call(s32[8]{0:T(128)} %refs_0_.3, s32[8]{0:T(128)S(1)} %collective-permute-done.refs_1_, s32[8]{0:T(128)S(1)} %collective-permute-done.1.refs_2_, s32[8]{0:T(128)S(1)} %collective-permute-done.2.refs_3_, s32[2,256]{1,0:T(2,128)} %bitcast.7, ...), custom_call_target="tpu_custom_call" | custom-call | flops 4294967296 | bytes 4194304 | tf_op jit(solution)/shard_map/pairs/pallas_call | solution.py:245
  21.3 5.9 %psum.7.refs_7_ = f32[2,128]{1,0:T(2,128)S(1)} all-reduce(f32[2,128]{1,0:T(2,128)S(1)} %get-tuple-element.18), channel_id=1, replica_groups=mesh['groups'=2,'shard'=4,'cache'=2,'pair'=2] {'cache','pair'}, use_global_device_ids=true, to_apply=%region_0.0 | all-reduce | flops 256 | bytes 2048 | tf_op jit(solution)/shard_map/pairs/psum | solution.py:262
  27.3 0.0 collective-permute-done.3.refs_1_
  27.3 0.0 collective-permute-done.4.refs_2_
  27.3 0.0 collective-permute-done.5.refs_3_
  27.3 0.0 collective-permute-done.6.refs_5_
  27.3 0.0 copy-done
  27.3 0.9 %scores.1 = (f32[1,128]{1,0:T(1,128)S(1)}, f32[1,128]{1,0:T(1,128)S(1)}, f32[1,128]{1,0:T(1,128)S(1)}, f32[1,128]{1,0:T(1,128)S(1)}) custom-call(bf16[16,3200]{1,0:T(8,128)(2,1)S(1)} %states.1.refs_8_.refs_0_, bf16[16,3200]{1,0:T(8,128)(2,1)S(1)} %collective-permute-done.3.refs_1_, bf16[16,3200]{1,0:T(8,128)(2,1)S(1)} %collective-permute-done.4.refs_2_, ...), custom_call_target="tpu_custom_call" | custom-call | flops 100663296 | bytes 2097152 | tf_op jit(solution)/shard_map/scores/pallas_call | solution.py:265
  28.2 1.4 %collective-permute-start.7 = (f32[1,128]{1,0:T(1,128)S(1)}, f32[1,128]{1,0:T(1,128)S(1)}, u32[]{:S(2)}, u32[]{:S(2)}) collective-permute-start(f32[1,128]{1,0:T(1,128)S(1)} %get-tuple-element.20), channel_id=1, source_target_pairs={{0,12},{4,0},{8,4},{12,8},{1,13},{5,1},{9,5},{13,9},{2,14},{6,2},{... | collective-permute-start | bytes 1544 | tf_op jit(solution)/shard_map/back/ppermute | solution.py:186
  29.6 2.0 %collective-permute-start.8 = (f32[1,128]{1,0:T(1,128)S(1)}, f32[1,128]{1,0:T(1,128)S(1)}, u32[]{:S(2)}, u32[]{:S(2)}) collective-permute-start(f32[1,128]{1,0:T(1,128)S(1)} %get-tuple-element.21), channel_id=1, source_target_pairs={{0,8},{4,12},{8,0},{12,4},{1,9},{5,13},{9,1},{13,5},{2,10},{6,14},... | collective-permute-start | bytes 1544 | tf_op jit(solution)/shard_map/back/ppermute | solution.py:186
  31.6 0.7 %collective-permute-start.9 = (f32[1,128]{1,0:T(1,128)S(1)}, f32[1,128]{1,0:T(1,128)S(1)}, u32[]{:S(2)}, u32[]{:S(2)}) collective-permute-start(f32[1,128]{1,0:T(1,128)S(1)} %get-tuple-element.22), channel_id=1, source_target_pairs={{0,4},{4,8},{8,12},{12,0},{1,5},{5,9},{9,13},{13,1},{2,6},{6,10},{... | collective-permute-start | bytes 1544 | tf_op jit(solution)/shard_map/back/ppermute | solution.py:186
  32.3 0.0 collective-permute-done.7
  32.3 1.7 %collective-permute-done.8 = f32[1,128]{1,0:T(1,128)S(1)} collective-permute-done((f32[1,128]{1,0:T(1,128)S(1)}, f32[1,128]{1,0:T(1,128)S(1)}, u32[]{:S(2)}, u32[]{:S(2)}) %collective-permute-start.8) | collective-permute-done | bytes 544 | tf_op jit(solution)/shard_map/back/ppermute | solution.py:186
  34.0 2.9 %collective-permute-done.9 = f32[1,128]{1,0:T(1,128)S(1)} collective-permute-done((f32[1,128]{1,0:T(1,128)S(1)}, f32[1,128]{1,0:T(1,128)S(1)}, u32[]{:S(2)}, u32[]{:S(2)}) %collective-permute-start.9) | collective-permute-done | bytes 544 | tf_op jit(solution)/shard_map/back/ppermute | solution.py:186
  37.0 0.5 %add_bitcast_fusion = f32[128]{0:T(128)} fusion(f32[1,128]{1,0:T(1,128)S(1)} %collective-permute-done.9, f32[1,128]{1,0:T(1,128)S(1)} %collective-permute-done.8, f32[1,128]{1,0:T(1,128)S(1)} %get-tuple-element.19, f32[1,128]{1,0:T(1,128)S(1)} %collective-permute-done.7), kind=kLoop, calls=%fused_computation | loop fusion | flops 384 | bytes 2560 | tf_op jit(solution)/shard_map/reshape | solution.py:283
Async XLA Ops:
  0.0 27.3 %collective-permute-start.6 = (bf16[128,3072]{1,0:T(8,128)(2,1)}, bf16[128,3072]{1,0:T(8,128)(2,1)S(1)}, u32[]{:S(2)}, u32[]{:S(2)}) collective-permute-start(bf16[128,3072]{1,0:T(8,128)(2,1)} %refs_4_.1), channel_id=1, source_target_pairs={{0,2},{2,0},{1,3},{3,1},{4,6},{6,4},{5,7},{7,5},{8,10},{10,8},{9,1... | collective-permute-start | bytes 2359304 | tf_op jit(solution)/shard_map/item_rows/ppermute | solution.py:186
  2.9 7.5 %collective-permute-start = (s32[8]{0:T(128)}, s32[8]{0:T(128)S(1)}, u32[]{:S(2)}, u32[]{:S(2)}) collective-permute-start(s32[8]{0:T(128)} %refs_0_.3), channel_id=1, source_target_pairs={{0,4},{4,8},{8,12},{12,0},{1,5},{5,9},{9,13},{13,1},{2,6},{6,10},{... | collective-permute-start | bytes 104 | tf_op jit(solution)/shard_map/ids/ppermute | solution.py:186
  4.5 6.0 %collective-permute-start.1 = (s32[8]{0:T(128)}, s32[8]{0:T(128)S(1)}, u32[]{:S(2)}, u32[]{:S(2)}) collective-permute-start(s32[8]{0:T(128)} %refs_0_.3), channel_id=1, source_target_pairs={{0,8},{4,12},{8,0},{12,4},{1,9},{5,13},{9,1},{13,5},{2,10},{6,14},... | collective-permute-start | bytes 104 | tf_op jit(solution)/shard_map/ids/ppermute | solution.py:186
  7.1 3.7 %collective-permute-start.2 = (s32[8]{0:T(128)}, s32[8]{0:T(128)S(1)}, u32[]{:S(2)}, u32[]{:S(2)}) collective-permute-start(s32[8]{0:T(128)} %refs_0_.3), channel_id=1, source_target_pairs={{0,12},{4,0},{8,4},{12,8},{1,13},{5,1},{9,5},{13,9},{2,14},{6,2},{... | collective-permute-start | bytes 104 | tf_op jit(solution)/shard_map/ids/ppermute | solution.py:186
  12.2 15.1 %collective-permute-start.3 = (bf16[16,3200]{1,0:T(8,128)(2,1)S(1)}, bf16[16,3200]{1,0:T(8,128)(2,1)S(1)}, u32[]{:S(2)}, u32[]{:S(2)}) collective-permute-start(bf16[16,3200]{1,0:T(8,128)(2,1)S(1)} %states.1.refs_8_.refs_0_), channel_id=1, source_target_pairs={{0,4},{4,8},{8,12},{12,0},{1,5},{5,9},{9,13},{13,1},{2,6},{6,10},{... | collective-permute-start | bytes 307208 | tf_op jit(solution)/shard_map/states/ppermute | solution.py:186
  12.7 14.6 %collective-permute-start.4 = (bf16[16,3200]{1,0:T(8,128)(2,1)S(1)}, bf16[16,3200]{1,0:T(8,128)(2,1)S(1)}, u32[]{:S(2)}, u32[]{:S(2)}) collective-permute-start(bf16[16,3200]{1,0:T(8,128)(2,1)S(1)} %states.1.refs_8_.refs_0_), channel_id=1, source_target_pairs={{0,8},{4,12},{8,0},{12,4},{1,9},{5,13},{9,1},{13,5},{2,10},{6,14},... | collective-permute-start | bytes 307208 | tf_op jit(solution)/shard_map/states/ppermute | solution.py:186
  16.0 11.3 %collective-permute-start.5 = (bf16[16,3200]{1,0:T(8,128)(2,1)S(1)}, bf16[16,3200]{1,0:T(8,128)(2,1)S(1)}, u32[]{:S(2)}, u32[]{:S(2)}) collective-permute-start(bf16[16,3200]{1,0:T(8,128)(2,1)S(1)} %states.1.refs_8_.refs_0_), channel_id=1, source_target_pairs={{0,12},{4,0},{8,4},{12,8},{1,13},{5,1},{9,5},{13,9},{2,14},{6,2},{... | collective-permute-start | bytes 307208 | tf_op jit(solution)/shard_map/states/ppermute | solution.py:186
  16.1 11.2 %copy-start = (bf16[128,3072]{1,0:T(8,128)(2,1)S(1)}, bf16[128,3072]{1,0:T(8,128)(2,1)}, u32[]{:S(2)}) copy-start(bf16[128,3072]{1,0:T(8,128)(2,1)} %refs_4_.1) | copy-start | bytes 2359300
  28.2 4.1 %collective-permute-start.7 = (f32[1,128]{1,0:T(1,128)S(1)}, f32[1,128]{1,0:T(1,128)S(1)}, u32[]{:S(2)}, u32[]{:S(2)}) collective-permute-start(f32[1,128]{1,0:T(1,128)S(1)} %get-tuple-element.20), channel_id=1, source_target_pairs={{0,12},{4,0},{8,4},{12,8},{1,13},{5,1},{9,5},{13,9},{2,14},{6,2},{... | collective-permute-start | bytes 1544 | tf_op jit(solution)/shard_map/back/ppermute | solution.py:186
  29.6 4.4 %collective-permute-start.8 = (f32[1,128]{1,0:T(1,128)S(1)}, f32[1,128]{1,0:T(1,128)S(1)}, u32[]{:S(2)}, u32[]{:S(2)}) collective-permute-start(f32[1,128]{1,0:T(1,128)S(1)} %get-tuple-element.21), channel_id=1, source_target_pairs={{0,8},{4,12},{8,0},{12,4},{1,9},{5,13},{9,1},{13,5},{2,10},{6,14},... | collective-permute-start | bytes 1544 | tf_op jit(solution)/shard_map/back/ppermute | solution.py:186
  31.6 5.3 %collective-permute-start.9 = (f32[1,128]{1,0:T(1,128)S(1)}, f32[1,128]{1,0:T(1,128)S(1)}, u32[]{:S(2)}, u32[]{:S(2)}) collective-permute-start(f32[1,128]{1,0:T(1,128)S(1)} %get-tuple-element.22), channel_id=1, source_target_pairs={{0,4},{4,8},{8,12},{12,0},{1,5},{5,9},{9,13},{13,1},{2,6},{6,10},{... | collective-permute-start | bytes 1544 | tf_op jit(solution)/shard_map/back/ppermute | solution.py:186

commit v9 on v8

--- a/solution.py
+++ b/solution.py
@@ -29,12 +29,10 @@
 
 
 def pick_kernel(total, cap, *refs):
-    users, (own_cands, states_hbm, later, out, held, asked, cands, sems) = refs[:total], refs[total:]
-    del later
-    fetch = pltpu.make_async_copy(states_hbm, held, sems.at[total])
-    digit_fetch = pltpu.make_async_copy(own_cands, cands, sems.at[total + 1])
+    users, (own_cands, held, out, asked, cands, sems) = refs[:total], refs[total:]
+    digit_fetch = pltpu.make_async_copy(own_cands, cands, sems.at[total])
     id_fetches = [pltpu.make_async_copy(users[j], asked.at[j], sems.at[j]) for j in range(total)]
-    for copy in id_fetches + [fetch, digit_fetch]:
+    for copy in id_fetches + [digit_fetch]:
         copy.start()
     own_rows, width = held.shape
     me = lax.axis_index("shard")
@@ -58,7 +56,6 @@
     code = cands[...]
     digits = jnp.where(iota((slots, code.shape[1]), 0) == 0, code // CODE, code % CODE)
     out[:, width:] = jnp.where(iota(digits.shape, 0) < 2, digits, 0).astype(jnp.float32).astype(jnp.bfloat16)
-    fetch.wait()
     out[:, :width] = dot(chosen, held[...], NN).astype(jnp.bfloat16)
 
 
@@ -80,15 +77,16 @@
     return rows
 
 
-def turn_kernel(items_hbm, mats_hbm, rows32, rows16, mats, items, sems):
-    chunks = sems.shape[0] - 1
+def turn_kernel(items_hbm, mats_hbm, states_hbm, rows32, rows16, mats, states, items, sems):
+    chunks = sems.shape[0] - 2
     wide = items.shape[1] // chunks
     item_fetches = [
         pltpu.make_async_copy(items_hbm.at[:, pl.ds(t * wide, wide)], items.at[:, pl.ds(t * wide, wide)], sems.at[t])
         for t in range(chunks)
     ]
     mats_fetch = pltpu.make_async_copy(mats_hbm, mats, sems.at[chunks])
-    for copy in item_fetches + [mats_fetch]:
+    states_fetch = pltpu.make_async_copy(states_hbm, states, sems.at[chunks + 1])
+    for copy in item_fetches + [mats_fetch, states_fetch]:
         copy.start()
     eye = (iota((LANES, LANES), 0) == iota((LANES, LANES), 1)).astype(jnp.bfloat16)
     for t in range(items.shape[1] // LANES):
@@ -98,6 +96,7 @@
         rows32[t * LANES:(t + 1) * LANES, :] = turned
         rows16[t * LANES:(t + 1) * LANES, :] = turned.astype(jnp.bfloat16)
     mats_fetch.wait()
+    states_fetch.wait()
 
 
 def pair_kernel(total, cap, slots, user_rows, *refs):
@@ -131,8 +130,7 @@
         return total + moved * jnp.concatenate(mults, axis=0)
 
     sums = lax.fori_loop(0, count // 2, two, jnp.zeros((2 * K, rows32.shape[1]), jnp.float32), unroll=16)
-    mine = iota(out.shape, 0) == lax.axis_index("cache")
-    out[...] = jnp.where(mine, jnp.sum(sums, axis=0, keepdims=True), 0.0)
+    out[...] = jnp.sum(sums, axis=0, keepdims=True)
     for copy in id_fetches:
         copy.wait()
     for j, row in enumerate(slot_rows(asked, cap, slots, user_rows, places.shape[1])):
@@ -146,11 +144,11 @@
     return high, middle, (rest - middle.astype(jnp.float32)).astype(jnp.bfloat16)
 
 
-def score_kernel(total, planes, *refs):
+def score_kernel(total, planes, parts, *refs):
     states, refs = refs[:total], refs[total:]
     items, refs = refs[:planes], refs[planes:]
-    places, pairs = refs[:2]
-    outs, (wanted, cands, linear) = refs[2:2 + total], refs[2 + total:]
+    places, pairs, refs = refs[0], refs[1:1 + planes * parts], refs[1 + planes * parts:]
+    outs, (wanted, cands, linear) = refs[:total], refs[total:]
     slots = states[0].shape[0]
     own_rows, width = items[0].shape
     me = lax.axis_index("shard")
@@ -169,7 +167,8 @@
         scores = dot(items[q][...], wanted[...], NT)
         for t, part in enumerate(thirds(scores)):
             linear[q * own_rows:(q + 1) * own_rows, t * count:(t + 1) * count] = part
-        columns.append(jnp.sum(jnp.where(eye, pairs[pl.ds(at, 1), :], 0.0), axis=1, keepdims=True))
+        row = sum(pairs[q * parts + h][...] for h in range(parts))
+        columns.append(jnp.sum(jnp.where(eye, row, 0.0), axis=1, keepdims=True))
         ids.append(iota((own_rows, 1), 0) + (me * planes + at) * own_rows)
     pair_column = jnp.concatenate(columns, axis=0)
     item_ids = jnp.concatenate(ids, axis=0)
@@ -189,6 +188,7 @@
 def body(cand_items, reader_users, item_table, user_states, pair_mats, pair_fields):
     total = lax.axis_size("shard")
     planes = lax.axis_size("cache")
+    parts = lax.axis_size("pair")
     half = cand_items.shape[0]
     rows, width = item_table.shape
     readers = reader_users.shape[0]
@@ -210,42 +210,42 @@
         users = [in_hbm(reader_users)] + [shift(reader_users, "shard", j) for j in range(1, total)]
 
     with jax.named_scope("turn"):
-        turned = pl.pallas_call(
+        *turned, states_near = pl.pallas_call(
             turn_kernel,
             out_shape=(
                 jax.ShapeDtypeStruct((width, rows), jnp.float32),
                 jax.ShapeDtypeStruct((width, rows), jnp.bfloat16),
                 jax.ShapeDtypeStruct((K, K, count), jnp.bfloat16),
+                jax.ShapeDtypeStruct(user_states.shape, jnp.bfloat16),
             ),
-            in_specs=[hbm, hbm],
-            out_specs=(vmem, vmem, vmem),
-            scratch_shapes=[pltpu.VMEM((rows, width), jnp.bfloat16), pltpu.SemaphoreType.DMA((5,))],
+            in_specs=[hbm, hbm, hbm],
+            out_specs=(vmem, vmem, vmem, vmem),
+            scratch_shapes=[pltpu.VMEM((rows, width), jnp.bfloat16), pltpu.SemaphoreType.DMA((6,))],
             compiler_params=params,
             cost_estimate=pl.CostEstimate(flops=2 * rows * rows * width * 16, bytes_accessed=8 * 1024 * 1024, transcendentals=0),
-        )(in_hbm(item_table), in_hbm(jnp.transpose(pair_mats, (1, 2, 0))))
+        )(in_hbm(item_table), in_hbm(jnp.transpose(pair_mats, (1, 2, 0))), in_hbm(user_states))
 
     with jax.named_scope("states"):
         picked = pl.pallas_call(
             functools.partial(pick_kernel, total, cap),
             out_shape=jax.ShapeDtypeStruct((slots, width + half), jnp.bfloat16),
-            in_specs=[anywhere] * total + [hbm, hbm, anywhere],
+            in_specs=[anywhere] * total + [hbm, vmem],
             out_specs=vmem,
             scratch_shapes=[
-                pltpu.VMEM(user_states.shape, jnp.bfloat16),
                 pltpu.SMEM((total, readers), jnp.int32),
                 pltpu.VMEM((1, half), jnp.int32),
-                pltpu.SemaphoreType.DMA((total + 2,)),
+                pltpu.SemaphoreType.DMA((total + 1,)),
             ],
             compiler_params=params,
             cost_estimate=pl.CostEstimate(flops=2 * slots * rows * width, bytes_accessed=1024 * 1024, transcendentals=0),
-        )(*users, in_hbm(cand_items.reshape(1, half)), in_hbm(user_states), turned[1])
+        )(*users, in_hbm(cand_items.reshape(1, half)), states_near)
         states = [picked] + [shift(picked, "shard", j) for j in range(1, total)]
 
     with jax.named_scope("pairs"):
         pair_parts, places = pl.pallas_call(
             functools.partial(pair_kernel, total, cap, slots, user_states.shape[0]),
             out_shape=(
-                jax.ShapeDtypeStruct((planes, rows), jnp.float32),
+                jax.ShapeDtypeStruct((1, rows), jnp.float32),
                 jax.ShapeDtypeStruct((total, half), jnp.int32),
             ),
             in_specs=[anywhere] * total + [hbm, vmem, vmem, vmem, anywhere],
@@ -259,13 +259,23 @@
             compiler_params=params,
             cost_estimate=pl.CostEstimate(flops=2 * count * K * K * rows * 16, bytes_accessed=4 * 1024 * 1024, transcendentals=0),
         )(*users, in_hbm(pair_fields.T), *turned, picked)
-        pair_scores = lax.psum(pair_parts, ("cache", "pair"))
+        pair_scores, moved = [], 0
+        for q in range(planes):
+            for h in range(parts):
+                perm = [
+                    (c * parts + d, (c + q) % planes * parts + (d + h) % parts) for c in range(planes) for d in range(parts)
+                ]
+                source = pair_parts
+                if 0 < moved < total:
+                    source, states[moved] = lax.optimization_barrier((pair_parts, states[moved]))
+                pair_scores.append(lax.ppermute(source, ("cache", "pair"), perm) if q or h else pair_parts)
+                moved += q + h > 0
 
     with jax.named_scope("scores"):
         outs = pl.pallas_call(
-            functools.partial(score_kernel, total, planes),
+            functools.partial(score_kernel, total, planes, parts),
             out_shape=[jax.ShapeDtypeStruct((1, half), jnp.float32)] * total,
-            in_specs=[vmem] * (total + planes + 2),
+            in_specs=[vmem] * (total + planes + 1 + planes * parts),
             out_specs=[vmem] * total,
             scratch_shapes=[
                 pltpu.VMEM((total * slots, width), jnp.bfloat16),
@@ -274,11 +284,11 @@
             ],
             compiler_params=params,
             cost_estimate=pl.CostEstimate(flops=2 * 64 * 256 * width, bytes_accessed=2 * 1024 * 1024, transcendentals=0),
-        )(*states, *items, places, pair_scores)
+        )(*states, *items, places, *pair_scores)
 
     with jax.named_scope("back"):
         result = outs[0]
-        for j in range(1, total):
+        for j in range(total - 1, 0, -1):
             result = result + shift(outs[j], "shard", -j)
     return result.reshape(half)
 

time: 37.7 us -> 33.8 us (0.90)
  blocking collectives: 5.91 us -> 0 us
  starting transfers between devices: 16.4 us -> 19.3 us
  waiting for transfers between devices: 4.98 us -> 4.25 us
    psum x1 -> x0, blocking collectives: 5.91 us -> none  [body(): pair_scores = lax.psum(pair_parts, ('cache', 'pair'))]
    ppermute x10, waiting for transfers between devices: 4.98 us -> 2.21 us  [shift(): return lax.ppermute(x, axis, [(s, (s + step) % size) for s in range(size)])]
    ppermute x0 -> x3, starting transfers between devices: none -> 2.21 us  [body(): lax.ppermute(source, ('cache', 'pair'), perm)]
    ppermute x0 -> x3, waiting for transfers between devices: none -> 2.04 us  [body(): lax.ppermute(source, ('cache', 'pair'), perm)]
    ppermute x10, starting transfers between devices: 16.4 us -> 17.1 us  [shift(): return lax.ppermute(x, axis, [(s, (s + step) % size) for s in range(size)])]
  transfers between devices with their start and end apart: 10 -> 13, of which waited for: 3 -> 6; matrix products, arithmetic and copies ran while one was open for 0% -> 0% of each run, Pallas kernels for 23% -> 26%
where the time goes in v9:
time: 33.8 us; the launch traced here: 33.6 us
  starting transfers between devices  19.3 us (57%)
  Pallas kernels  9.46 us (28%)
  waiting for transfers between devices  4.25 us (13%)
  other arithmetic  0.52 us (2%)
    ppermute x10, starting transfers between devices, shift(): return lax.ppermute(x, axis, [(s, (s + step) % size) for s in range(size)])  17.1 us
    pallas_call x1, Pallas kernels, body(): pl.pallas_call(functools.partial(pair_kernel, total, cap, slots, user_sta...  5.18 us
    ppermute x10, waiting for transfers between devices, shift(): return lax.ppermute(x, axis, [(s, (s + step) % size) for s in range(size)])  2.21 us
    ppermute x3, starting transfers between devices, body(): lax.ppermute(source, ('cache', 'pair'), perm)  2.21 us
    pallas_call x1, Pallas kernels, body(): pl.pallas_call(turn_kernel, out_shape=(jax.ShapeDtypeStruct((width, rows)...  2.18 us
    ppermute x3, waiting for transfers between devices, body(): lax.ppermute(source, ('cache', 'pair'), perm)  2.04 us
    pallas_call x1, Pallas kernels, body(): pl.pallas_call(functools.partial(pick_kernel, total, cap), out_shape=jax....  1.21 us
    pallas_call x1, Pallas kernels, body(): pl.pallas_call(functools.partial(score_kernel, total, planes, parts), out...  0.89 us
  transfers between devices with their start and end apart: 13, of which 6 were waited for; matrix products, arithmetic and copies ran while one was open for 0% of the time, Pallas kernels for 26%

profile of v9, /device:TPU:0, one launch (start us, length us, event | category | flops | bytes accessed | tf_op | source)
XLA Modules:
  0.0 33.6 jit_solution(15621387787318797023)
XLA Ops:
  0.0 2.9 %collective-permute-start.6 = (bf16[128,3072]{1,0:T(8,128)(2,1)}, bf16[128,3072]{1,0:T(8,128)(2,1)S(1)}, u32[]{:S(2)}, u32[]{:S(2)}) collective-permute-start(bf16[128,3072]{1,0:T(8,128)(2,1)} %refs_4_.1), channel_id=1, source_target_pairs={{0,2},{2,0},{1,3},{3,1},{4,6},{6,4},{5,7},{7,5},{8,10},{10,8},{9,1... | collective-permute-start | bytes 2359304 | tf_op jit(solution)/shard_map/item_rows/ppermute | solution.py:185
  2.9 1.6 %collective-permute-start = (s32[8]{0:T(128)}, s32[8]{0:T(128)S(1)}, u32[]{:S(2)}, u32[]{:S(2)}) collective-permute-start(s32[8]{0:T(128)} %refs_0_.3), channel_id=1, source_target_pairs={{0,4},{4,8},{8,12},{12,0},{1,5},{5,9},{9,13},{13,1},{2,6},{6,10},{... | collective-permute-start | bytes 104 | tf_op jit(solution)/shard_map/ids/ppermute | solution.py:185
  4.5 2.6 %collective-permute-start.1 = (s32[8]{0:T(128)}, s32[8]{0:T(128)S(1)}, u32[]{:S(2)}, u32[]{:S(2)}) collective-permute-start(s32[8]{0:T(128)} %refs_0_.3), channel_id=1, source_target_pairs={{0,8},{4,12},{8,0},{12,4},{1,9},{5,13},{9,1},{13,5},{2,10},{6,14},... | collective-permute-start | bytes 104 | tf_op jit(solution)/shard_map/ids/ppermute | solution.py:185
  7.1 1.3 %collective-permute-start.2 = (s32[8]{0:T(128)}, s32[8]{0:T(128)S(1)}, u32[]{:S(2)}, u32[]{:S(2)}) collective-permute-start(s32[8]{0:T(128)} %refs_0_.3), channel_id=1, source_target_pairs={{0,12},{4,0},{8,4},{12,8},{1,13},{5,1},{9,5},{13,9},{2,14},{6,2},{... | collective-permute-start | bytes 104 | tf_op jit(solution)/shard_map/ids/ppermute | solution.py:185
  8.5 2.2 %turn.1 = (f32[3072,128]{1,0:T(8,128)S(1)}, bf16[3072,128]{1,0:T(8,128)(2,1)S(1)}, bf16[64,64,256]{2,1,0:T(8,128)(2,1)S(1)}, bf16[128,3072]{1,0:T(8,128)(2,1)S(1)}) custom-call(bf16[128,3072]{1,0:T(8,128)(2,1)} %refs_4_.1, bf16[64,64,256]{2,1,0:T(8,128)(2,1)} %bitcast.6, bf16[128,3072]{1,0:T(8,128)(2,1)} %states_hbm.1), custom_call_target="tpu_custom_call" | custom-call | flops 1610612736 | bytes 8388608 | tf_op jit(solution)/shard_map/turn/pallas_call | solution.py:213
  10.6 0.0 collective-permute-done.refs_1_
  10.7 0.0 collective-permute-done.1.refs_2_
  10.7 0.1 collective-permute-done.2.refs_3_
  10.8 1.2 %states.1.refs_8_.refs_0_ = bf16[16,3200]{1,0:T(8,128)(2,1)S(1)} custom-call(s32[8]{0:T(128)} %refs_0_.3, s32[8]{0:T(128)S(1)} %collective-permute-done.refs_1_, s32[8]{0:T(128)S(1)} %collective-permute-done.1.refs_2_, s32[8]{0:T(128)S(1)} %collective-permute-done.2.refs_3_, s32[1,128]{1,0:T(1,128)} %bitcast.5, bf16[128,3072]{1,0:T(8,128)(2,1)S(1)} %get-tuple-element.19.refs_5_), custom_call_target="tpu_custom_call" | custom-call | flops 12582912 | bytes 1048576 | tf_op jit(solution)/shard_map/states/pallas_call | solution.py:229
  12.0 1.0 %collective-permute-start.4 = (bf16[16,3200]{1,0:T(8,128)(2,1)S(1)}, bf16[16,3200]{1,0:T(8,128)(2,1)S(1)}, u32[]{:S(2)}, u32[]{:S(2)}) collective-permute-start(bf16[16,3200]{1,0:T(8,128)(2,1)S(1)} %states.1.refs_8_.refs_0_), channel_id=1, source_target_pairs={{0,8},{4,12},{8,0},{12,4},{1,9},{5,13},{9,1},{13,5},{2,10},{6,14},... | collective-permute-start | bytes 307208 | tf_op jit(solution)/shard_map/states/ppermute | solution.py:185
  13.0 2.8 %collective-permute-start.3 = (bf16[16,3200]{1,0:T(8,128)(2,1)S(1)}, bf16[16,3200]{1,0:T(8,128)(2,1)S(1)}, u32[]{:S(2)}, u32[]{:S(2)}) collective-permute-start(bf16[16,3200]{1,0:T(8,128)(2,1)S(1)} %states.1.refs_8_.refs_0_), channel_id=1, source_target_pairs={{0,4},{4,8},{8,12},{12,0},{1,5},{5,9},{9,13},{13,1},{2,6},{6,10},{... | collective-permute-start | bytes 307208 | tf_op jit(solution)/shard_map/states/ppermute | solution.py:185
  15.8 1.0 %collective-permute-start.5 = (bf16[16,3200]{1,0:T(8,128)(2,1)S(1)}, bf16[16,3200]{1,0:T(8,128)(2,1)S(1)}, u32[]{:S(2)}, u32[]{:S(2)}) collective-permute-start(bf16[16,3200]{1,0:T(8,128)(2,1)S(1)} %states.1.refs_8_.refs_0_), channel_id=1, source_target_pairs={{0,12},{4,0},{8,4},{12,8},{1,13},{5,1},{9,5},{13,9},{2,14},{6,2},{... | collective-permute-start | bytes 307208 | tf_op jit(solution)/shard_map/states/ppermute | solution.py:185
  16.8 0.0 copy-start
  16.8 5.2 %pairs.1 = (f32[1,128]{1,0:T(1,128)S(1)}, s32[4,128]{1,0:T(4,128)S(1)}) custom-call(s32[8]{0:T(128)} %refs_0_.3, s32[8]{0:T(128)S(1)} %collective-permute-done.refs_1_, s32[8]{0:T(128)S(1)} %collective-permute-done.1.refs_2_, s32[8]{0:T(128)S(1)} %collective-permute-done.2.refs_3_, s32[2,256]{1,0:T(2,128)} %bitcast.7, ...), custom_call_target="tpu_custom_call" | custom-call | flops 4294967296 | bytes 4194304 | tf_op jit(solution)/shard_map/pairs/pallas_call | solution.py:245
  22.0 0.1 collective-permute-start.7
  22.1 0.0 collective-permute-done.4.refs_2_
  22.1 0.6 %collective-permute-start.9 = (f32[1,128]{1,0:T(1,128)S(1)}, f32[1,128]{1,0:T(1,128)S(1)}, u32[]{:S(2)}, u32[]{:S(2)}) collective-permute-start(f32[1,128]{1,0:T(1,128)S(1)} %get-tuple-element.28.refs_7_), channel_id=1, source_target_pairs={{0,3},{1,2},{2,1},{3,0},{4,7},{5,6},{6,5},{7,4},{8,11},{9,10},{10,... | collective-permute-start | bytes 1544 | tf_op jit(solution)/shard_map/pairs/ppermute | solution.py:271
  22.7 0.0 collective-permute-done.3.refs_1_
  22.7 1.5 %collective-permute-start.8 = (f32[1,128]{1,0:T(1,128)S(1)}, f32[1,128]{1,0:T(1,128)S(1)}, u32[]{:S(2)}, u32[]{:S(2)}) collective-permute-start(f32[1,128]{1,0:T(1,128)S(1)} %get-tuple-element.28.refs_7_), channel_id=1, source_target_pairs={{0,2},{1,3},{2,0},{3,1},{4,6},{5,7},{6,4},{7,5},{8,10},{9,11},{10,... | collective-permute-start | bytes 1544 | tf_op jit(solution)/shard_map/pairs/ppermute | solution.py:271
  24.2 0.0 collective-permute-done.7.refs_8_
  24.2 0.0 collective-permute-done.5.refs_3_
  24.2 0.9 %collective-permute-done.9.refs_10_ = f32[1,128]{1,0:T(1,128)S(1)} collective-permute-done((f32[1,128]{1,0:T(1,128)S(1)}, f32[1,128]{1,0:T(1,128)S(1)}, u32[]{:S(2)}, u32[]{:S(2)}) %collective-permute-start.9) | collective-permute-done | bytes 544 | tf_op jit(solution)/shard_map/pairs/ppermute | solution.py:271
  25.1 1.2 %collective-permute-done.8.refs_9_ = f32[1,128]{1,0:T(1,128)S(1)} collective-permute-done((f32[1,128]{1,0:T(1,128)S(1)}, f32[1,128]{1,0:T(1,128)S(1)}, u32[]{:S(2)}, u32[]{:S(2)}) %collective-permute-start.8) | collective-permute-done | bytes 544 | tf_op jit(solution)/shard_map/pairs/ppermute | solution.py:271
  26.3 0.0 collective-permute-done.6.refs_5_
  26.3 0.0 copy-done
  26.3 0.9 %scores.1 = (f32[1,128]{1,0:T(1,128)S(1)}, f32[1,128]{1,0:T(1,128)S(1)}, f32[1,128]{1,0:T(1,128)S(1)}, f32[1,128]{1,0:T(1,128)S(1)}) custom-call(bf16[16,3200]{1,0:T(8,128)(2,1)S(1)} %states.1.refs_8_.refs_0_, bf16[16,3200]{1,0:T(8,128)(2,1)S(1)} %collective-permute-done.3.refs_1_, bf16[16,3200]{1,0:T(8,128)(2,1)S(1)} %collective-permute-done.4.refs_2_, ...), custom_call_target="tpu_custom_call" | custom-call | flops 100663296 | bytes 2097152 | tf_op jit(solution)/shard_map/scores/pallas_call | solution.py:275
  27.2 1.1 %collective-permute-start.10 = (f32[1,128]{1,0:T(1,128)S(1)}, f32[1,128]{1,0:T(1,128)S(1)}, u32[]{:S(2)}, u32[]{:S(2)}) collective-permute-start(f32[1,128]{1,0:T(1,128)S(1)} %get-tuple-element.30), channel_id=1, source_target_pairs={{0,4},{4,8},{8,12},{12,0},{1,5},{5,9},{9,13},{13,1},{2,6},{6,10},{... | collective-permute-start | bytes 1544 | tf_op jit(solution)/shard_map/back/ppermute | solution.py:185
  28.2 0.1 collective-permute-start.11
  28.3 2.7 %collective-permute-start.12 = (f32[1,128]{1,0:T(1,128)S(1)}, f32[1,128]{1,0:T(1,128)S(1)}, u32[]{:S(2)}, u32[]{:S(2)}) collective-permute-start(f32[1,128]{1,0:T(1,128)S(1)} %get-tuple-element.32), channel_id=1, source_target_pairs={{0,12},{4,0},{8,4},{12,8},{1,13},{5,1},{9,5},{13,9},{2,14},{6,2},{... | collective-permute-start | bytes 1544 | tf_op jit(solution)/shard_map/back/ppermute | solution.py:185
  31.0 1.5 %collective-permute-done.10 = f32[1,128]{1,0:T(1,128)S(1)} collective-permute-done((f32[1,128]{1,0:T(1,128)S(1)}, f32[1,128]{1,0:T(1,128)S(1)}, u32[]{:S(2)}, u32[]{:S(2)}) %collective-permute-start.10) | collective-permute-done | bytes 544 | tf_op jit(solution)/shard_map/back/ppermute | solution.py:185
  32.6 0.1 collective-permute-done.11
  32.7 0.5 %collective-permute-done.12 = f32[1,128]{1,0:T(1,128)S(1)} collective-permute-done((f32[1,128]{1,0:T(1,128)S(1)}, f32[1,128]{1,0:T(1,128)S(1)}, u32[]{:S(2)}, u32[]{:S(2)}) %collective-permute-start.12) | collective-permute-done | bytes 544 | tf_op jit(solution)/shard_map/back/ppermute | solution.py:185
  33.1 0.5 %add_bitcast_fusion = f32[128]{0:T(128)} fusion(f32[1,128]{1,0:T(1,128)S(1)} %collective-permute-done.12, f32[1,128]{1,0:T(1,128)S(1)} %collective-permute-done.11, f32[1,128]{1,0:T(1,128)S(1)} %get-tuple-element.29, f32[1,128]{1,0:T(1,128)S(1)} %collective-permute-done.10), kind=kLoop, calls=%fused_computation | loop fusion | flops 384 | bytes 2560 | tf_op jit(solution)/shard_map/reshape | solution.py:293
Async XLA Ops:
  0.0 26.3 %collective-permute-start.6 = (bf16[128,3072]{1,0:T(8,128)(2,1)}, bf16[128,3072]{1,0:T(8,128)(2,1)S(1)}, u32[]{:S(2)}, u32[]{:S(2)}) collective-permute-start(bf16[128,3072]{1,0:T(8,128)(2,1)} %refs_4_.1), channel_id=1, source_target_pairs={{0,2},{2,0},{1,3},{3,1},{4,6},{6,4},{5,7},{7,5},{8,10},{10,8},{9,1... | collective-permute-start | bytes 2359304 | tf_op jit(solution)/shard_map/item_rows/ppermute | solution.py:185
  2.9 7.7 %collective-permute-start = (s32[8]{0:T(128)}, s32[8]{0:T(128)S(1)}, u32[]{:S(2)}, u32[]{:S(2)}) collective-permute-start(s32[8]{0:T(128)} %refs_0_.3), channel_id=1, source_target_pairs={{0,4},{4,8},{8,12},{12,0},{1,5},{5,9},{9,13},{13,1},{2,6},{6,10},{... | collective-permute-start | bytes 104 | tf_op jit(solution)/shard_map/ids/ppermute | solution.py:185
  4.5 6.1 %collective-permute-start.1 = (s32[8]{0:T(128)}, s32[8]{0:T(128)S(1)}, u32[]{:S(2)}, u32[]{:S(2)}) collective-permute-start(s32[8]{0:T(128)} %refs_0_.3), channel_id=1, source_target_pairs={{0,8},{4,12},{8,0},{12,4},{1,9},{5,13},{9,1},{13,5},{2,10},{6,14},... | collective-permute-start | bytes 104 | tf_op jit(solution)/shard_map/ids/ppermute | solution.py:185
  7.1 3.7 %collective-permute-start.2 = (s32[8]{0:T(128)}, s32[8]{0:T(128)S(1)}, u32[]{:S(2)}, u32[]{:S(2)}) collective-permute-start(s32[8]{0:T(128)} %refs_0_.3), channel_id=1, source_target_pairs={{0,12},{4,0},{8,4},{12,8},{1,13},{5,1},{9,5},{13,9},{2,14},{6,2},{... | collective-permute-start | bytes 104 | tf_op jit(solution)/shard_map/ids/ppermute | solution.py:185
  12.0 10.1 %collective-permute-start.4 = (bf16[16,3200]{1,0:T(8,128)(2,1)S(1)}, bf16[16,3200]{1,0:T(8,128)(2,1)S(1)}, u32[]{:S(2)}, u32[]{:S(2)}) collective-permute-start(bf16[16,3200]{1,0:T(8,128)(2,1)S(1)} %states.1.refs_8_.refs_0_), channel_id=1, source_target_pairs={{0,8},{4,12},{8,0},{12,4},{1,9},{5,13},{9,1},{13,5},{2,10},{6,14},... | collective-permute-start | bytes 307208 | tf_op jit(solution)/shard_map/states/ppermute | solution.py:185
  13.0 9.8 %collective-permute-start.3 = (bf16[16,3200]{1,0:T(8,128)(2,1)S(1)}, bf16[16,3200]{1,0:T(8,128)(2,1)S(1)}, u32[]{:S(2)}, u32[]{:S(2)}) collective-permute-start(bf16[16,3200]{1,0:T(8,128)(2,1)S(1)} %states.1.refs_8_.refs_0_), channel_id=1, source_target_pairs={{0,4},{4,8},{8,12},{12,0},{1,5},{5,9},{9,13},{13,1},{2,6},{6,10},{... | collective-permute-start | bytes 307208 | tf_op jit(solution)/shard_map/states/ppermute | solution.py:185
  15.8 8.4 %collective-permute-start.5 = (bf16[16,3200]{1,0:T(8,128)(2,1)S(1)}, bf16[16,3200]{1,0:T(8,128)(2,1)S(1)}, u32[]{:S(2)}, u32[]{:S(2)}) collective-permute-start(bf16[16,3200]{1,0:T(8,128)(2,1)S(1)} %states.1.refs_8_.refs_0_), channel_id=1, source_target_pairs={{0,12},{4,0},{8,4},{12,8},{1,13},{5,1},{9,5},{13,9},{2,14},{6,2},{... | collective-permute-start | bytes 307208 | tf_op jit(solution)/shard_map/states/ppermute | solution.py:185
  16.8 9.5 %copy-start = (bf16[128,3072]{1,0:T(8,128)(2,1)S(1)}, bf16[128,3072]{1,0:T(8,128)(2,1)}, u32[]{:S(2)}) copy-start(bf16[128,3072]{1,0:T(8,128)(2,1)} %refs_4_.1) | copy-start | bytes 2359300
  22.0 2.2 %collective-permute-start.7 = (f32[1,128]{1,0:T(1,128)S(1)}, f32[1,128]{1,0:T(1,128)S(1)}, u32[]{:S(2)}, u32[]{:S(2)}) collective-permute-start(f32[1,128]{1,0:T(1,128)S(1)} %get-tuple-element.28.refs_7_), channel_id=1, source_target_pairs={{0,1},{1,0},{2,3},{3,2},{4,5},{5,4},{6,7},{7,6},{8,9},{9,8},{10,11... | collective-permute-start | bytes 1544 | tf_op jit(solution)/shard_map/pairs/ppermute | solution.py:271
  22.1 3.0 %collective-permute-start.9 = (f32[1,128]{1,0:T(1,128)S(1)}, f32[1,128]{1,0:T(1,128)S(1)}, u32[]{:S(2)}, u32[]{:S(2)}) collective-permute-start(f32[1,128]{1,0:T(1,128)S(1)} %get-tuple-element.28.refs_7_), channel_id=1, source_target_pairs={{0,3},{1,2},{2,1},{3,0},{4,7},{5,6},{6,5},{7,4},{8,11},{9,10},{10,... | collective-permute-start | bytes 1544 | tf_op jit(solution)/shard_map/pairs/ppermute | solution.py:271
  22.7 3.5 %collective-permute-start.8 = (f32[1,128]{1,0:T(1,128)S(1)}, f32[1,128]{1,0:T(1,128)S(1)}, u32[]{:S(2)}, u32[]{:S(2)}) collective-permute-start(f32[1,128]{1,0:T(1,128)S(1)} %get-tuple-element.28.refs_7_), channel_id=1, source_target_pairs={{0,2},{1,3},{2,0},{3,1},{4,6},{5,7},{6,4},{7,5},{8,10},{9,11},{10,... | collective-permute-start | bytes 1544 | tf_op jit(solution)/shard_map/pairs/ppermute | solution.py:271
  27.2 5.4 %collective-permute-start.10 = (f32[1,128]{1,0:T(1,128)S(1)}, f32[1,128]{1,0:T(1,128)S(1)}, u32[]{:S(2)}, u32[]{:S(2)}) collective-permute-start(f32[1,128]{1,0:T(1,128)S(1)} %get-tuple-element.30), channel_id=1, source_target_pairs={{0,4},{4,8},{8,12},{12,0},{1,5},{5,9},{9,13},{13,1},{2,6},{6,10},{... | collective-permute-start | bytes 1544 | tf_op jit(solution)/shard_map/back/ppermute | solution.py:185
  28.2 4.4 %collective-permute-start.11 = (f32[1,128]{1,0:T(1,128)S(1)}, f32[1,128]{1,0:T(1,128)S(1)}, u32[]{:S(2)}, u32[]{:S(2)}) collective-permute-start(f32[1,128]{1,0:T(1,128)S(1)} %get-tuple-element.31), channel_id=1, source_target_pairs={{0,8},{4,12},{8,0},{12,4},{1,9},{5,13},{9,1},{13,5},{2,10},{6,14},... | collective-permute-start | bytes 1544 | tf_op jit(solution)/shard_map/back/ppermute | solution.py:185
  28.3 4.8 %collective-permute-start.12 = (f32[1,128]{1,0:T(1,128)S(1)}, f32[1,128]{1,0:T(1,128)S(1)}, u32[]{:S(2)}, u32[]{:S(2)}) collective-permute-start(f32[1,128]{1,0:T(1,128)S(1)} %get-tuple-element.32), channel_id=1, source_target_pairs={{0,12},{4,0},{8,4},{12,8},{1,13},{5,1},{9,5},{13,9},{2,14},{6,2},{... | collective-permute-start | bytes 1544 | tf_op jit(solution)/shard_map/back/ppermute | solution.py:185

commit v10 on v9

--- a/solution.py
+++ b/solution.py
@@ -26,6 +26,13 @@
 
 def ring(index, size):
     return lax.rem(index + size, size)
+
+
+def place_of(device, size):
+    down = device % 2 == 0
+    if isinstance(device, int):
+        return (size - device // 2) % size if down else (device + 1) // 2
+    return jnp.where(down, lax.rem(size - device // 2, size), (device + 1) // 2)
 
 
 def pick_kernel(total, cap, *refs):
@@ -36,6 +43,7 @@
         copy.start()
     own_rows, width = held.shape
     me = lax.axis_index("shard")
+    place = place_of(me, total)
     slots = out.shape[0]
     slot_index = iota((slots, own_rows), 0)
     row_index = iota((slots, own_rows), 1)
@@ -43,7 +51,7 @@
     for copy in id_fetches:
         copy.wait()
     for j in range(total):
-        source = ring(me - j, total)
+        source = ring(place - j, total)
         taken = jnp.int32(0)
         for r in range(asked.shape[1]):
             user = asked[j, r]
@@ -61,7 +69,7 @@
 
 def slot_rows(asked, cap, slots, user_rows, half):
     total, readers = asked.shape
-    me = lax.axis_index("shard")
+    me = place_of(lax.axis_index("shard"), total)
     lane = iota((1, half), 1) // (half // readers)
     rows = []
     for j in range(total):
@@ -72,7 +80,8 @@
             rank = jnp.int32(0)
             for earlier in holders[:r]:
                 rank = rank + (earlier == holder).astype(jnp.int32)
-            row = jnp.where(lane == r, ring(me - holder, total) * slots + source * cap + rank, row)
+            arrival = ring(me - place_of(holder, total), total)
+            row = jnp.where(lane == r, arrival * slots + source * cap + rank, row)
         rows.append(row)
     return rows
 
@@ -185,6 +194,12 @@
     return lax.ppermute(x, axis, [(s, (s + step) % size) for s in range(size)])
 
 
+def along(x, step):
+    total = lax.axis_size("shard")
+    device_at = {place_of(s, total): s for s in range(total)}
+    return lax.ppermute(x, "shard", [(device_at[p], device_at[(p + step) % total]) for p in range(total)])
+
+
 def body(cand_items, reader_users, item_table, user_states, pair_mats, pair_fields):
     total = lax.axis_size("shard")
     planes = lax.axis_size("cache")
@@ -207,7 +222,7 @@
         items = [item_table] + [shift(item_table, "cache", q) for q in range(1, planes)]
 
     with jax.named_scope("ids"):
-        users = [in_hbm(reader_users)] + [shift(reader_users, "shard", j) for j in range(1, total)]
+        users = [in_hbm(reader_users)] + [along(reader_users, j) for j in range(1, total)]
 
     with jax.named_scope("turn"):
         *turned, states_near = pl.pallas_call(
@@ -239,7 +254,7 @@
             compiler_params=params,
             cost_estimate=pl.CostEstimate(flops=2 * slots * rows * width, bytes_accessed=1024 * 1024, transcendentals=0),
         )(*users, in_hbm(cand_items.reshape(1, half)), states_near)
-        states = [picked] + [shift(picked, "shard", j) for j in range(1, total)]
+        states = [picked] + [along(picked, j) for j in range(1, total)]
 
     with jax.named_scope("pairs"):
         pair_parts, places = pl.pallas_call(
@@ -267,7 +282,7 @@
                 ]
                 source = pair_parts
                 if 0 < moved < total:
-                    source, states[moved] = lax.optimization_barrier((pair_parts, states[moved]))
+                    source, states[1] = lax.optimization_barrier((pair_parts, states[1]))
                 pair_scores.append(lax.ppermute(source, ("cache", "pair"), perm) if q or h else pair_parts)
                 moved += q + h > 0
 
@@ -289,7 +304,7 @@
     with jax.named_scope("back"):
         result = outs[0]
         for j in range(total - 1, 0, -1):
-            result = result + shift(outs[j], "shard", -j)
+            result = result + along(outs[j], -j)
     return result.reshape(half)
 
 

time: 33.8 us -> 35.2 us (1.041)
  waiting for transfers between devices: 4.25 us -> 6.68 us
  starting transfers between devices: 19.3 us -> 17.9 us
  Pallas kernels: 9.46 us -> 9.87 us
    ppermute x10 -> x1, starting transfers between devices: 17.1 us -> 2.94 us  [shift(): return lax.ppermute(x, axis, [(s, (s + step) % size) for s in range(size)])]
    ppermute x0 -> x9, starting transfers between devices: none -> 13.6 us  [along(): lax.ppermute(x, 'shard', [(device_at[p], device_at[(p + step) % total]) f...]
    ppermute x0 -> x9, waiting for transfers between devices: none -> 3.7 us  [along(): lax.ppermute(x, 'shard', [(device_at[p], device_at[(p + step) % total]) f...]
    ppermute x10 -> x1, waiting for transfers between devices: 2.21 us -> 0.01 us  [shift(): return lax.ppermute(x, axis, [(s, (s + step) % size) for s in range(size)])]
    ppermute x3, waiting for transfers between devices: 2.04 us -> 2.97 us  [body(): lax.ppermute(source, ('cache', 'pair'), perm)]
    ppermute x3, starting transfers between devices: 2.21 us -> 1.35 us  [body(): lax.ppermute(source, ('cache', 'pair'), perm)]
    pallas_call x1, Pallas kernels: 5.18 us -> 5.59 us  [body(): pl.pallas_call(functools.partial(pair_kernel, total, cap, slots, user_sta...]
where the time goes in v10:
time: 35.2 us; the launch traced here: 35 us
  starting transfers between devices  17.9 us (51%)
  Pallas kernels  9.87 us (28%)
  waiting for transfers between devices  6.68 us (19%)
  other arithmetic  0.52 us (1%)
    ppermute x9, starting transfers between devices, along(): lax.ppermute(x, 'shard', [(device_at[p], device_at[(p + step) % total]) f...  13.6 us
    pallas_call x1, Pallas kernels, body(): pl.pallas_call(functools.partial(pair_kernel, total, cap, slots, user_sta...  5.59 us
    ppermute x9, waiting for transfers between devices, along(): lax.ppermute(x, 'shard', [(device_at[p], device_at[(p + step) % total]) f...  3.7 us
    ppermute x3, waiting for transfers between devices, body(): lax.ppermute(source, ('cache', 'pair'), perm)  2.97 us
    ppermute x1, starting transfers between devices, shift(): return lax.ppermute(x, axis, [(s, (s + step) % size) for s in range(size)])  2.94 us
    pallas_call x1, Pallas kernels, body(): pl.pallas_call(turn_kernel, out_shape=(jax.ShapeDtypeStruct((width, rows)...  2.18 us
    ppermute x3, starting transfers between devices, body(): lax.ppermute(source, ('cache', 'pair'), perm)  1.35 us
    pallas_call x1, Pallas kernels, body(): pl.pallas_call(functools.partial(pick_kernel, total, cap), out_shape=jax....  1.21 us
  transfers between devices with their start and end apart: 13, of which 6 were waited for; matrix products, arithmetic and copies ran while one was open for 0% of the time, Pallas kernels for 26%

profile of v10, /device:TPU:0, one launch (start us, length us, event | category | flops | bytes accessed | tf_op | source)
XLA Modules:
  0.0 35.0 jit_solution(1990703943071703280)
XLA Ops:
  0.0 2.9 %collective-permute-start.6 = (bf16[128,3072]{1,0:T(8,128)(2,1)}, bf16[128,3072]{1,0:T(8,128)(2,1)S(1)}, u32[]{:S(2)}, u32[]{:S(2)}) collective-permute-start(bf16[128,3072]{1,0:T(8,128)(2,1)} %refs_4_.1), channel_id=1, source_target_pairs={{0,2},{2,0},{1,3},{3,1},{4,6},{6,4},{5,7},{7,5},{8,10},{10,8},{9,1... | collective-permute-start | bytes 2359304 | tf_op jit(solution)/shard_map/item_rows/ppermute | solution.py:194
  2.9 1.6 %collective-permute-start = (s32[8]{0:T(128)}, s32[8]{0:T(128)S(1)}, u32[]{:S(2)}, u32[]{:S(2)}) collective-permute-start(s32[8]{0:T(128)} %refs_0_.3), channel_id=1, source_target_pairs={{0,4},{4,12},{12,8},{8,0},{1,5},{5,13},{13,9},{9,1},{2,6},{6,14},{... | collective-permute-start | bytes 104 | tf_op jit(solution)/shard_map/ids/ppermute | solution.py:200
  4.5 2.5 %collective-permute-start.1 = (s32[8]{0:T(128)}, s32[8]{0:T(128)S(1)}, u32[]{:S(2)}, u32[]{:S(2)}) collective-permute-start(s32[8]{0:T(128)} %refs_0_.3), channel_id=1, source_target_pairs={{0,12},{4,8},{12,0},{8,4},{1,13},{5,9},{13,1},{9,5},{2,14},{6,10},... | collective-permute-start | bytes 104 | tf_op jit(solution)/shard_map/ids/ppermute | solution.py:200
  7.0 1.6 %collective-permute-start.2 = (s32[8]{0:T(128)}, s32[8]{0:T(128)S(1)}, u32[]{:S(2)}, u32[]{:S(2)}) collective-permute-start(s32[8]{0:T(128)} %refs_0_.3), channel_id=1, source_target_pairs={{0,8},{4,0},{12,4},{8,12},{1,9},{5,1},{13,5},{9,13},{2,10},{6,2},{... | collective-permute-start | bytes 104 | tf_op jit(solution)/shard_map/ids/ppermute | solution.py:200
  8.6 2.2 %turn.1 = (f32[3072,128]{1,0:T(8,128)S(1)}, bf16[3072,128]{1,0:T(8,128)(2,1)S(1)}, bf16[64,64,256]{2,1,0:T(8,128)(2,1)S(1)}, bf16[128,3072]{1,0:T(8,128)(2,1)S(1)}) custom-call(bf16[128,3072]{1,0:T(8,128)(2,1)} %refs_4_.1, bf16[64,64,256]{2,1,0:T(8,128)(2,1)} %bitcast.6, bf16[128,3072]{1,0:T(8,128)(2,1)} %states_hbm.1), custom_call_target="tpu_custom_call" | custom-call | flops 1610612736 | bytes 8388608 | tf_op jit(solution)/shard_map/turn/pallas_call | solution.py:228
  10.8 0.0 collective-permute-done.refs_1_
  10.8 0.0 collective-permute-done.1.refs_2_
  10.8 0.0 collective-permute-done.2.refs_3_
  10.8 1.2 %states.1.refs_8_.refs_0_ = bf16[16,3200]{1,0:T(8,128)(2,1)S(1)} custom-call(s32[8]{0:T(128)} %refs_0_.3, s32[8]{0:T(128)S(1)} %collective-permute-done.refs_1_, s32[8]{0:T(128)S(1)} %collective-permute-done.1.refs_2_, s32[8]{0:T(128)S(1)} %collective-permute-done.2.refs_3_, s32[1,128]{1,0:T(1,128)} %bitcast.5, bf16[128,3072]{1,0:T(8,128)(2,1)S(1)} %get-tuple-element.19.refs_5_), custom_call_target="tpu_custom_call" | custom-call | flops 12582912 | bytes 1048576 | tf_op jit(solution)/shard_map/states/pallas_call | solution.py:244
  12.0 0.9 %collective-permute-start.3 = (bf16[16,3200]{1,0:T(8,128)(2,1)S(1)}, bf16[16,3200]{1,0:T(8,128)(2,1)S(1)}, u32[]{:S(2)}, u32[]{:S(2)}) collective-permute-start(bf16[16,3200]{1,0:T(8,128)(2,1)S(1)} %states.1.refs_8_.refs_0_), channel_id=1, source_target_pairs={{0,4},{4,12},{12,8},{8,0},{1,5},{5,13},{13,9},{9,1},{2,6},{6,14},{... | collective-permute-start | bytes 307208 | tf_op jit(solution)/shard_map/states/ppermute | solution.py:200
  13.0 2.9 %collective-permute-start.4 = (bf16[16,3200]{1,0:T(8,128)(2,1)S(1)}, bf16[16,3200]{1,0:T(8,128)(2,1)S(1)}, u32[]{:S(2)}, u32[]{:S(2)}) collective-permute-start(bf16[16,3200]{1,0:T(8,128)(2,1)S(1)} %states.1.refs_8_.refs_0_), channel_id=1, source_target_pairs={{0,12},{4,8},{12,0},{8,4},{1,13},{5,9},{13,1},{9,5},{2,14},{6,10},... | collective-permute-start | bytes 307208 | tf_op jit(solution)/shard_map/states/ppermute | solution.py:200
  15.9 0.0 collective-permute-start.5
  15.9 0.0 copy-start
  15.9 5.6 %pairs.1 = (f32[1,128]{1,0:T(1,128)S(1)}, s32[4,128]{1,0:T(4,128)S(1)}) custom-call(s32[8]{0:T(128)} %refs_0_.3, s32[8]{0:T(128)S(1)} %collective-permute-done.refs_1_, s32[8]{0:T(128)S(1)} %collective-permute-done.1.refs_2_, s32[8]{0:T(128)S(1)} %collective-permute-done.2.refs_3_, s32[2,256]{1,0:T(2,128)} %bitcast.7, ...), custom_call_target="tpu_custom_call" | custom-call | flops 4294967296 | bytes 4194304 | tf_op jit(solution)/shard_map/pairs/pallas_call | solution.py:260
  21.5 0.1 collective-permute-start.7
  21.6 0.4 %collective-permute-done.3.refs_1_ = bf16[16,3200]{1,0:T(8,128)(2,1)S(1)} collective-permute-done((bf16[16,3200]{1,0:T(8,128)(2,1)S(1)}, bf16[16,3200]{1,0:T(8,128)(2,1)S(1)}, u32[]{:S(2)}, u32[]{:S(2)}) %collective-permute-start.3) | collective-permute-done | bytes 102432 | tf_op jit(solution)/shard_map/states/ppermute | solution.py:200
  21.9 0.3 collective-permute-start.9
  22.2 0.5 %collective-permute-done.7.refs_8_ = f32[1,128]{1,0:T(1,128)S(1)} collective-permute-done((f32[1,128]{1,0:T(1,128)S(1)}, f32[1,128]{1,0:T(1,128)S(1)}, u32[]{:S(2)}, u32[]{:S(2)}) %collective-permute-start.7) | collective-permute-done | bytes 544 | tf_op jit(solution)/shard_map/pairs/ppermute | solution.py:286
  22.7 1.0 %collective-permute-start.8 = (f32[1,128]{1,0:T(1,128)S(1)}, f32[1,128]{1,0:T(1,128)S(1)}, u32[]{:S(2)}, u32[]{:S(2)}) collective-permute-start(f32[1,128]{1,0:T(1,128)S(1)} %get-tuple-element.28.refs_7_), channel_id=1, source_target_pairs={{0,2},{1,3},{2,0},{3,1},{4,6},{5,7},{6,4},{7,5},{8,10},{9,11},{10,... | collective-permute-start | bytes 1544 | tf_op jit(solution)/shard_map/pairs/ppermute | solution.py:286
  23.7 0.0 collective-permute-done.4.refs_2_
  23.7 0.0 collective-permute-done.5.refs_3_
  23.7 1.2 %collective-permute-done.9.refs_10_ = f32[1,128]{1,0:T(1,128)S(1)} collective-permute-done((f32[1,128]{1,0:T(1,128)S(1)}, f32[1,128]{1,0:T(1,128)S(1)}, u32[]{:S(2)}, u32[]{:S(2)}) %collective-permute-start.9) | collective-permute-done | bytes 544 | tf_op jit(solution)/shard_map/pairs/ppermute | solution.py:286
  24.9 1.3 %collective-permute-done.8.refs_9_ = f32[1,128]{1,0:T(1,128)S(1)} collective-permute-done((f32[1,128]{1,0:T(1,128)S(1)}, f32[1,128]{1,0:T(1,128)S(1)}, u32[]{:S(2)}, u32[]{:S(2)}) %collective-permute-start.8) | collective-permute-done | bytes 544 | tf_op jit(solution)/shard_map/pairs/ppermute | solution.py:286
  26.2 0.0 collective-permute-done.6.refs_5_
  26.2 0.0 copy-done
  26.2 0.9 %scores.1 = (f32[1,128]{1,0:T(1,128)S(1)}, f32[1,128]{1,0:T(1,128)S(1)}, f32[1,128]{1,0:T(1,128)S(1)}, f32[1,128]{1,0:T(1,128)S(1)}) custom-call(bf16[16,3200]{1,0:T(8,128)(2,1)S(1)} %states.1.refs_8_.refs_0_, bf16[16,3200]{1,0:T(8,128)(2,1)S(1)} %collective-permute-done.3.refs_1_, bf16[16,3200]{1,0:T(8,128)(2,1)S(1)} %collective-permute-done.4.refs_2_, ...), custom_call_target="tpu_custom_call" | custom-call | flops 100663296 | bytes 2097152 | tf_op jit(solution)/shard_map/scores/pallas_call | solution.py:290
  27.1 2.1 %collective-permute-start.10 = (f32[1,128]{1,0:T(1,128)S(1)}, f32[1,128]{1,0:T(1,128)S(1)}, u32[]{:S(2)}, u32[]{:S(2)}) collective-permute-start(f32[1,128]{1,0:T(1,128)S(1)} %get-tuple-element.30), channel_id=1, source_target_pairs={{0,4},{4,12},{12,8},{8,0},{1,5},{5,13},{13,9},{9,1},{2,6},{6,14},{... | collective-permute-start | bytes 1544 | tf_op jit(solution)/shard_map/back/ppermute | solution.py:200
  29.2 0.9 %collective-permute-start.11 = (f32[1,128]{1,0:T(1,128)S(1)}, f32[1,128]{1,0:T(1,128)S(1)}, u32[]{:S(2)}, u32[]{:S(2)}) collective-permute-start(f32[1,128]{1,0:T(1,128)S(1)} %get-tuple-element.31), channel_id=1, source_target_pairs={{0,12},{4,8},{12,0},{8,4},{1,13},{5,9},{13,1},{9,5},{2,14},{6,10},... | collective-permute-start | bytes 1544 | tf_op jit(solution)/shard_map/back/ppermute | solution.py:200
  30.1 1.1 %collective-permute-start.12 = (f32[1,128]{1,0:T(1,128)S(1)}, f32[1,128]{1,0:T(1,128)S(1)}, u32[]{:S(2)}, u32[]{:S(2)}) collective-permute-start(f32[1,128]{1,0:T(1,128)S(1)} %get-tuple-element.32), channel_id=1, source_target_pairs={{0,8},{4,0},{12,4},{8,12},{1,9},{5,1},{13,5},{9,13},{2,10},{6,2},{... | collective-permute-start | bytes 1544 | tf_op jit(solution)/shard_map/back/ppermute | solution.py:200
  31.2 0.4 %collective-permute-done.10 = f32[1,128]{1,0:T(1,128)S(1)} collective-permute-done((f32[1,128]{1,0:T(1,128)S(1)}, f32[1,128]{1,0:T(1,128)S(1)}, u32[]{:S(2)}, u32[]{:S(2)}) %collective-permute-start.10) | collective-permute-done | bytes 544 | tf_op jit(solution)/shard_map/back/ppermute | solution.py:200
  31.6 2.9 %collective-permute-done.11 = f32[1,128]{1,0:T(1,128)S(1)} collective-permute-done((f32[1,128]{1,0:T(1,128)S(1)}, f32[1,128]{1,0:T(1,128)S(1)}, u32[]{:S(2)}, u32[]{:S(2)}) %collective-permute-start.11) | collective-permute-done | bytes 544 | tf_op jit(solution)/shard_map/back/ppermute | solution.py:200
  34.5 0.0 collective-permute-done.12
  34.5 0.5 %add_bitcast_fusion = f32[128]{0:T(128)} fusion(f32[1,128]{1,0:T(1,128)S(1)} %collective-permute-done.12, f32[1,128]{1,0:T(1,128)S(1)} %collective-permute-done.11, f32[1,128]{1,0:T(1,128)S(1)} %get-tuple-element.29, f32[1,128]{1,0:T(1,128)S(1)} %collective-permute-done.10), kind=kLoop, calls=%fused_computation | loop fusion | flops 384 | bytes 2560 | tf_op jit(solution)/shard_map/reshape | solution.py:308
Async XLA Ops:
  0.0 26.2 %collective-permute-start.6 = (bf16[128,3072]{1,0:T(8,128)(2,1)}, bf16[128,3072]{1,0:T(8,128)(2,1)S(1)}, u32[]{:S(2)}, u32[]{:S(2)}) collective-permute-start(bf16[128,3072]{1,0:T(8,128)(2,1)} %refs_4_.1), channel_id=1, source_target_pairs={{0,2},{2,0},{1,3},{3,1},{4,6},{6,4},{5,7},{7,5},{8,10},{10,8},{9,1... | collective-permute-start | bytes 2359304 | tf_op jit(solution)/shard_map/item_rows/ppermute | solution.py:194
  2.9 7.8 %collective-permute-start = (s32[8]{0:T(128)}, s32[8]{0:T(128)S(1)}, u32[]{:S(2)}, u32[]{:S(2)}) collective-permute-start(s32[8]{0:T(128)} %refs_0_.3), channel_id=1, source_target_pairs={{0,4},{4,12},{12,8},{8,0},{1,5},{5,13},{13,9},{9,1},{2,6},{6,14},{... | collective-permute-start | bytes 104 | tf_op jit(solution)/shard_map/ids/ppermute | solution.py:200
  4.5 6.3 %collective-permute-start.1 = (s32[8]{0:T(128)}, s32[8]{0:T(128)S(1)}, u32[]{:S(2)}, u32[]{:S(2)}) collective-permute-start(s32[8]{0:T(128)} %refs_0_.3), channel_id=1, source_target_pairs={{0,12},{4,8},{12,0},{8,4},{1,13},{5,9},{13,1},{9,5},{2,14},{6,10},... | collective-permute-start | bytes 104 | tf_op jit(solution)/shard_map/ids/ppermute | solution.py:200
  7.0 3.8 %collective-permute-start.2 = (s32[8]{0:T(128)}, s32[8]{0:T(128)S(1)}, u32[]{:S(2)}, u32[]{:S(2)}) collective-permute-start(s32[8]{0:T(128)} %refs_0_.3), channel_id=1, source_target_pairs={{0,8},{4,0},{12,4},{8,12},{1,9},{5,1},{13,5},{9,13},{2,10},{6,2},{... | collective-permute-start | bytes 104 | tf_op jit(solution)/shard_map/ids/ppermute | solution.py:200
  12.0 9.9 %collective-permute-start.3 = (bf16[16,3200]{1,0:T(8,128)(2,1)S(1)}, bf16[16,3200]{1,0:T(8,128)(2,1)S(1)}, u32[]{:S(2)}, u32[]{:S(2)}) collective-permute-start(bf16[16,3200]{1,0:T(8,128)(2,1)S(1)} %states.1.refs_8_.refs_0_), channel_id=1, source_target_pairs={{0,4},{4,12},{12,8},{8,0},{1,5},{5,13},{13,9},{9,1},{2,6},{6,14},{... | collective-permute-start | bytes 307208 | tf_op jit(solution)/shard_map/states/ppermute | solution.py:200
  13.0 10.7 %collective-permute-start.4 = (bf16[16,3200]{1,0:T(8,128)(2,1)S(1)}, bf16[16,3200]{1,0:T(8,128)(2,1)S(1)}, u32[]{:S(2)}, u32[]{:S(2)}) collective-permute-start(bf16[16,3200]{1,0:T(8,128)(2,1)S(1)} %states.1.refs_8_.refs_0_), channel_id=1, source_target_pairs={{0,12},{4,8},{12,0},{8,4},{1,13},{5,9},{13,1},{9,5},{2,14},{6,10},... | collective-permute-start | bytes 307208 | tf_op jit(solution)/shard_map/states/ppermute | solution.py:200
  15.9 7.8 %collective-permute-start.5 = (bf16[16,3200]{1,0:T(8,128)(2,1)S(1)}, bf16[16,3200]{1,0:T(8,128)(2,1)S(1)}, u32[]{:S(2)}, u32[]{:S(2)}) collective-permute-start(bf16[16,3200]{1,0:T(8,128)(2,1)S(1)} %states.1.refs_8_.refs_0_), channel_id=1, source_target_pairs={{0,8},{4,0},{12,4},{8,12},{1,9},{5,1},{13,5},{9,13},{2,10},{6,2},{... | collective-permute-start | bytes 307208 | tf_op jit(solution)/shard_map/states/ppermute | solution.py:200
  15.9 10.3 %copy-start = (bf16[128,3072]{1,0:T(8,128)(2,1)S(1)}, bf16[128,3072]{1,0:T(8,128)(2,1)}, u32[]{:S(2)}) copy-start(bf16[128,3072]{1,0:T(8,128)(2,1)} %refs_4_.1) | copy-start | bytes 2359300
  21.5 1.2 %collective-permute-start.7 = (f32[1,128]{1,0:T(1,128)S(1)}, f32[1,128]{1,0:T(1,128)S(1)}, u32[]{:S(2)}, u32[]{:S(2)}) collective-permute-start(f32[1,128]{1,0:T(1,128)S(1)} %get-tuple-element.28.refs_7_), channel_id=1, source_target_pairs={{0,1},{1,0},{2,3},{3,2},{4,5},{5,4},{6,7},{7,6},{8,9},{9,8},{10,11... | collective-permute-start | bytes 1544 | tf_op jit(solution)/shard_map/pairs/ppermute | solution.py:286
  21.9 3.0 %collective-permute-start.9 = (f32[1,128]{1,0:T(1,128)S(1)}, f32[1,128]{1,0:T(1,128)S(1)}, u32[]{:S(2)}, u32[]{:S(2)}) collective-permute-start(f32[1,128]{1,0:T(1,128)S(1)} %get-tuple-element.28.refs_7_), channel_id=1, source_target_pairs={{0,3},{1,2},{2,1},{3,0},{4,7},{5,6},{6,5},{7,4},{8,11},{9,10},{10,... | collective-permute-start | bytes 1544 | tf_op jit(solution)/shard_map/pairs/ppermute | solution.py:286
  22.7 3.5 %collective-permute-start.8 = (f32[1,128]{1,0:T(1,128)S(1)}, f32[1,128]{1,0:T(1,128)S(1)}, u32[]{:S(2)}, u32[]{:S(2)}) collective-permute-start(f32[1,128]{1,0:T(1,128)S(1)} %get-tuple-element.28.refs_7_), channel_id=1, source_target_pairs={{0,2},{1,3},{2,0},{3,1},{4,6},{5,7},{6,4},{7,5},{8,10},{9,11},{10,... | collective-permute-start | bytes 1544 | tf_op jit(solution)/shard_map/pairs/ppermute | solution.py:286
  27.1 4.5 %collective-permute-start.10 = (f32[1,128]{1,0:T(1,128)S(1)}, f32[1,128]{1,0:T(1,128)S(1)}, u32[]{:S(2)}, u32[]{:S(2)}) collective-permute-start(f32[1,128]{1,0:T(1,128)S(1)} %get-tuple-element.30), channel_id=1, source_target_pairs={{0,4},{4,12},{12,8},{8,0},{1,5},{5,13},{13,9},{9,1},{2,6},{6,14},{... | collective-permute-start | bytes 1544 | tf_op jit(solution)/shard_map/back/ppermute | solution.py:200
  29.2 5.3 %collective-permute-start.11 = (f32[1,128]{1,0:T(1,128)S(1)}, f32[1,128]{1,0:T(1,128)S(1)}, u32[]{:S(2)}, u32[]{:S(2)}) collective-permute-start(f32[1,128]{1,0:T(1,128)S(1)} %get-tuple-element.31), channel_id=1, source_target_pairs={{0,12},{4,8},{12,0},{8,4},{1,13},{5,9},{13,1},{9,5},{2,14},{6,10},... | collective-permute-start | bytes 1544 | tf_op jit(solution)/shard_map/back/ppermute | solution.py:200
  30.1 4.4 %collective-permute-start.12 = (f32[1,128]{1,0:T(1,128)S(1)}, f32[1,128]{1,0:T(1,128)S(1)}, u32[]{:S(2)}, u32[]{:S(2)}) collective-permute-start(f32[1,128]{1,0:T(1,128)S(1)} %get-tuple-element.32), channel_id=1, source_target_pairs={{0,8},{4,0},{12,4},{8,12},{1,9},{5,1},{13,5},{9,13},{2,10},{6,2},{... | collective-permute-start | bytes 1544 | tf_op jit(solution)/shard_map/back/ppermute | solution.py:200

commit v11 on v9

--- a/solution.py
+++ b/solution.py
@@ -10,7 +10,7 @@
 K = 64
 LANES = 128
 PITCH = 72
-CODE = 128
+CODE_BITS = 7
 VMEM_LIMIT = 40 * 1024 * 1024
 NT = (((1,), (1,)), ((), ()))
 NN = (((1,), (0,)), ((), ()))
@@ -29,34 +29,27 @@
 
 
 def pick_kernel(total, cap, *refs):
-    users, (own_cands, held, out, asked, cands, sems) = refs[:total], refs[total:]
-    digit_fetch = pltpu.make_async_copy(own_cands, cands, sems.at[total])
-    id_fetches = [pltpu.make_async_copy(users[j], asked.at[j], sems.at[j]) for j in range(total)]
-    for copy in id_fetches + [digit_fetch]:
-        copy.start()
-    own_rows, width = held.shape
+    users, (digits, states, out) = refs[:total], refs[total:]
+    own_rows, width = states.shape
+    slots = out.shape[0]
+    readers = users[0].shape[1]
     me = lax.axis_index("shard")
-    slots = out.shape[0]
-    slot_index = iota((slots, own_rows), 0)
-    row_index = iota((slots, own_rows), 1)
+    first = me * own_rows
+    across = iota((readers, readers), 1)
+    down = iota((readers, readers), 0)
     chosen = jnp.zeros((slots, own_rows), jnp.float32)
-    for copy in id_fetches:
-        copy.wait()
     for j in range(total):
-        source = ring(me - j, total)
-        taken = jnp.int32(0)
-        for r in range(asked.shape[1]):
-            user = asked[j, r]
-            mine = user // own_rows == me
-            slot = jnp.where(mine, source * cap + taken, -1)
-            taken = taken + mine.astype(jnp.int32)
-            chosen = jnp.where((slot_index == slot) & (row_index == user % own_rows), 1.0, chosen)
-    chosen = chosen.astype(jnp.bfloat16)
-    digit_fetch.wait()
-    code = cands[...]
-    digits = jnp.where(iota((slots, code.shape[1]), 0) == 0, code // CODE, code % CODE)
-    out[:, width:] = jnp.where(iota(digits.shape, 0) < 2, digits, 0).astype(jnp.float32).astype(jnp.bfloat16)
-    out[:, :width] = dot(chosen, held[...], NN).astype(jnp.bfloat16)
+        row = users[j][...]
+        column = jnp.sum(jnp.where(across == down, row, 0), axis=1, keepdims=True)
+        mine = (column >= first) & (column < first + own_rows)
+        rank = jnp.sum(jnp.where((down < across) & mine, 1, 0), axis=0, keepdims=True)
+        held = (row >= first) & (row < first + own_rows)
+        slot = jnp.where(held, ring(me - j, total) * cap + rank, -1)
+        to_slot = (iota((slots, readers), 0) == slot).astype(jnp.float32).astype(jnp.bfloat16)
+        from_row = (iota((readers, own_rows), 1) + first == column).astype(jnp.float32).astype(jnp.bfloat16)
+        chosen = chosen + dot(to_slot, from_row, NN)
+    out[:, width:] = digits[...]
+    out[:, :width] = dot(chosen.astype(jnp.bfloat16), states[...], NN).astype(jnp.bfloat16)
 
 
 def slot_rows(asked, cap, slots, user_rows, half):
@@ -77,8 +70,8 @@
     return rows
 
 
-def turn_kernel(items_hbm, mats_hbm, states_hbm, rows32, rows16, mats, states, items, sems):
-    chunks = sems.shape[0] - 2
+def turn_kernel(items_hbm, mats_hbm, states_hbm, ids_hbm, cands_hbm, rows32, rows16, mats, states, ids, digits, items, cands, sems):
+    chunks = sems.shape[0] - 4
     wide = items.shape[1] // chunks
     item_fetches = [
         pltpu.make_async_copy(items_hbm.at[:, pl.ds(t * wide, wide)], items.at[:, pl.ds(t * wide, wide)], sems.at[t])
@@ -86,7 +79,9 @@
     ]
     mats_fetch = pltpu.make_async_copy(mats_hbm, mats, sems.at[chunks])
     states_fetch = pltpu.make_async_copy(states_hbm, states, sems.at[chunks + 1])
-    for copy in item_fetches + [mats_fetch, states_fetch]:
+    ids_fetch = pltpu.make_async_copy(ids_hbm, ids, sems.at[chunks + 2])
+    cands_fetch = pltpu.make_async_copy(cands_hbm, cands, sems.at[chunks + 3])
+    for copy in item_fetches + [mats_fetch, states_fetch, ids_fetch, cands_fetch]:
         copy.start()
     eye = (iota((LANES, LANES), 0) == iota((LANES, LANES), 1)).astype(jnp.bfloat16)
     for t in range(items.shape[1] // LANES):
@@ -95,6 +90,12 @@
         turned = dot(eye, items[:, t * LANES:(t + 1) * LANES], NT)
         rows32[t * LANES:(t + 1) * LANES, :] = turned
         rows16[t * LANES:(t + 1) * LANES, :] = turned.astype(jnp.bfloat16)
+    cands_fetch.wait()
+    code = jnp.broadcast_to(cands[...], digits.shape)
+    place = iota(digits.shape, 0)
+    digit = jnp.where(place == 0, code >> CODE_BITS, jnp.where(place == 1, code & ((1 << CODE_BITS) - 1), 0))
+    digits[...] = digit.astype(jnp.float32).astype(jnp.bfloat16)
+    ids_fetch.wait()
     mats_fetch.wait()
     states_fetch.wait()
 
@@ -158,7 +159,7 @@
         wanted[j * slots:(j + 1) * slots, :] = states[j][:, :width]
         digits = states[j][:, width:].astype(jnp.float32)
         place = iota(digits.shape, 0)
-        weight = jnp.where(place == 0, float(CODE), jnp.where(place == 1, 1.0, 0.0))
+        weight = jnp.where(place == 0, float(1 << CODE_BITS), jnp.where(place == 1, 1.0, 0.0))
         cands[j:j + 1, :] = jnp.sum(digits * weight, axis=0, keepdims=True).astype(jnp.int32)
     eye = iota((own_rows, own_rows), 0) == iota((own_rows, own_rows), 1)
     ids, columns = [], []
@@ -210,35 +211,42 @@
         users = [in_hbm(reader_users)] + [shift(reader_users, "shard", j) for j in range(1, total)]
 
     with jax.named_scope("turn"):
-        *turned, states_near = pl.pallas_call(
+        *turned, states_near, own_ids, digits = pl.pallas_call(
             turn_kernel,
             out_shape=(
                 jax.ShapeDtypeStruct((width, rows), jnp.float32),
                 jax.ShapeDtypeStruct((width, rows), jnp.bfloat16),
                 jax.ShapeDtypeStruct((K, K, count), jnp.bfloat16),
                 jax.ShapeDtypeStruct(user_states.shape, jnp.bfloat16),
+                jax.ShapeDtypeStruct((1, readers), jnp.int32),
+                jax.ShapeDtypeStruct((slots, half), jnp.bfloat16),
             ),
-            in_specs=[hbm, hbm, hbm],
-            out_specs=(vmem, vmem, vmem, vmem),
-            scratch_shapes=[pltpu.VMEM((rows, width), jnp.bfloat16), pltpu.SemaphoreType.DMA((6,))],
+            in_specs=[hbm] * 5,
+            out_specs=(vmem,) * 6,
+            scratch_shapes=[
+                pltpu.VMEM((rows, width), jnp.bfloat16),
+                pltpu.VMEM((1, half), jnp.int32),
+                pltpu.SemaphoreType.DMA((8,)),
+            ],
             compiler_params=params,
             cost_estimate=pl.CostEstimate(flops=2 * rows * rows * width * 16, bytes_accessed=8 * 1024 * 1024, transcendentals=0),
-        )(in_hbm(item_table), in_hbm(jnp.transpose(pair_mats, (1, 2, 0))), in_hbm(user_states))
+        )(
+            in_hbm(item_table),
+            in_hbm(jnp.transpose(pair_mats, (1, 2, 0))),
+            in_hbm(user_states),
+            in_hbm(reader_users.reshape(1, readers)),
+            in_hbm(cand_items.reshape(1, half)),
+        )
 
     with jax.named_scope("states"):
         picked = pl.pallas_call(
             functools.partial(pick_kernel, total, cap),
             out_shape=jax.ShapeDtypeStruct((slots, width + half), jnp.bfloat16),
-            in_specs=[anywhere] * total + [hbm, vmem],
+            in_specs=[vmem] * (total + 2),
             out_specs=vmem,
-            scratch_shapes=[
-                pltpu.SMEM((total, readers), jnp.int32),
-                pltpu.VMEM((1, half), jnp.int32),
-                pltpu.SemaphoreType.DMA((total + 1,)),
-            ],
             compiler_params=params,
             cost_estimate=pl.CostEstimate(flops=2 * slots * rows * width, bytes_accessed=1024 * 1024, transcendentals=0),
-        )(*users, in_hbm(cand_items.reshape(1, half)), states_near)
+        )(own_ids, *[ids.reshape(1, readers) for ids in users[1:]], digits, states_near)
         states = [picked] + [shift(picked, "shard", j) for j in range(1, total)]
 
     with jax.named_scope("pairs"):
@@ -267,7 +275,7 @@
                 ]
                 source = pair_parts
                 if 0 < moved < total:
-                    source, states[moved] = lax.optimization_barrier((pair_parts, states[moved]))
+                    source, states[1] = lax.optimization_barrier((pair_parts, states[1]))
                 pair_scores.append(lax.ppermute(source, ("cache", "pair"), perm) if q or h else pair_parts)
                 moved += q + h > 0
 

time: 33.8 us -> 32.9 us (0.973)
  Pallas kernels: 9.46 us -> 8.67 us
    ppermute x3, waiting for transfers between devices: 2.04 us -> 2.94 us  [body(): lax.ppermute(source, ('cache', 'pair'), perm)]
    pallas_call x1, Pallas kernels: 1.21 us -> 0.4 us  [body(): pl.pallas_call(functools.partial(pick_kernel, total, cap), out_shape=jax....]
    ppermute x10, waiting for transfers between devices: 2.21 us -> 1.52 us  [shift(): return lax.ppermute(x, axis, [(s, (s + step) % size) for s in range(size)])]
    ppermute x3, starting transfers between devices: 2.21 us -> 1.76 us  [body(): lax.ppermute(source, ('cache', 'pair'), perm)]
  transfers between devices with their start and end apart: 13 -> 13, of which waited for: 6 -> 6; matrix products, arithmetic and copies ran while one was open for 0% -> 0% of each run, Pallas kernels for 26% -> 24%
where the time goes in v11:
time: 32.9 us; the launch traced here: 32.8 us
  starting transfers between devices  19.1 us (58%)
  Pallas kernels  8.67 us (26%)
  waiting for transfers between devices  4.46 us (14%)
  other arithmetic  0.52 us (2%)
    ppermute x10, starting transfers between devices, shift(): return lax.ppermute(x, axis, [(s, (s + step) % size) for s in range(size)])  17.3 us
    pallas_call x1, Pallas kernels, body(): pl.pallas_call(functools.partial(pair_kernel, total, cap, slots, user_sta...  5.18 us
    ppermute x3, waiting for transfers between devices, body(): lax.ppermute(source, ('cache', 'pair'), perm)  2.94 us
    pallas_call x1, Pallas kernels, body(): pl.pallas_call(turn_kernel, out_shape=(jax.ShapeDtypeStruct((width, rows)...  2.2 us
    ppermute x3, starting transfers between devices, body(): lax.ppermute(source, ('cache', 'pair'), perm)  1.76 us
    ppermute x10, waiting for transfers between devices, shift(): return lax.ppermute(x, axis, [(s, (s + step) % size) for s in range(size)])  1.52 us
    pallas_call x1, Pallas kernels, body(): pl.pallas_call(functools.partial(score_kernel, total, planes, parts), out...  0.88 us
  transfers between devices with their start and end apart: 13, of which 6 were waited for; matrix products, arithmetic and copies ran while one was open for 0% of the time, Pallas kernels for 24%

profile of v11, /device:TPU:0, one launch (start us, length us, event | category | flops | bytes accessed | tf_op | source)
XLA Modules:
  0.0 32.8 jit_solution(2203888863943195374)
XLA Ops:
  0.0 2.9 %collective-permute-start.6 = (bf16[128,3072]{1,0:T(8,128)(2,1)}, bf16[128,3072]{1,0:T(8,128)(2,1)S(1)}, u32[]{:S(2)}, u32[]{:S(2)}) collective-permute-start(bf16[128,3072]{1,0:T(8,128)(2,1)} %refs_4_.1), channel_id=1, source_target_pairs={{0,2},{2,0},{1,3},{3,1},{4,6},{6,4},{5,7},{7,5},{8,10},{10,8},{9,1... | collective-permute-start | bytes 2359304 | tf_op jit(solution)/shard_map/item_rows/ppermute | solution.py:186
  2.9 1.6 %collective-permute-start = (s32[8]{0:T(128)}, s32[8]{0:T(128)S(1)}, u32[]{:S(2)}, u32[]{:S(2)}) collective-permute-start(s32[8]{0:T(128)} %refs_0_.1), channel_id=1, source_target_pairs={{0,4},{4,8},{8,12},{12,0},{1,5},{5,9},{9,13},{13,1},{2,6},{6,10},{... | collective-permute-start | bytes 104 | tf_op jit(solution)/shard_map/ids/ppermute | solution.py:186
  4.5 2.6 %collective-permute-start.1 = (s32[8]{0:T(128)}, s32[8]{0:T(128)S(1)}, u32[]{:S(2)}, u32[]{:S(2)}) collective-permute-start(s32[8]{0:T(128)} %refs_0_.1), channel_id=1, source_target_pairs={{0,8},{4,12},{8,0},{12,4},{1,9},{5,13},{9,1},{13,5},{2,10},{6,14},... | collective-permute-start | bytes 104 | tf_op jit(solution)/shard_map/ids/ppermute | solution.py:186
  7.1 1.3 %collective-permute-start.2 = (s32[8]{0:T(128)}, s32[8]{0:T(128)S(1)}, u32[]{:S(2)}, u32[]{:S(2)}) collective-permute-start(s32[8]{0:T(128)} %refs_0_.1), channel_id=1, source_target_pairs={{0,12},{4,0},{8,4},{12,8},{1,13},{5,1},{9,5},{13,9},{2,14},{6,2},{... | collective-permute-start | bytes 104 | tf_op jit(solution)/shard_map/ids/ppermute | solution.py:186
  8.5 2.2 %turn.1 = (f32[3072,128]{1,0:T(8,128)S(1)}, bf16[3072,128]{1,0:T(8,128)(2,1)S(1)}, bf16[64,64,256]{2,1,0:T(8,128)(2,1)S(1)}, bf16[128,3072]{1,0:T(8,128)(2,1)S(1...) custom-call(bf16[128,3072]{1,0:T(8,128)(2,1)} %refs_4_.1, bf16[64,64,256]{2,1,0:T(8,128)(2,1)} %bitcast.12, ...), custom_call_target="tpu_custom_call" | custom-call | flops 1610612736 | bytes 8388608 | tf_op jit(solution)/shard_map/turn/pallas_call | solution.py:214
  10.7 0.0 collective-permute-done.refs_1_
  10.7 0.0 collective-permute-done.1.refs_2_
  10.7 0.1 collective-permute-done.2.refs_3_
  10.8 0.4 %states.1.refs_8_.refs_0_ = bf16[16,3200]{1,0:T(8,128)(2,1)S(1)} custom-call(s32[1,8]{1,0:T(1,128)S(1)} %get-tuple-element.21.refs_0_, s32[1,8]{1,0:T(1,128)S(1)} %bitcast.9, s32[1,8]{1,0:T(1,128)S(1)} %bitcast.10, s32[1,8]{1,0:T(1,128)S(1)} %bitcast.11, bf16[16,128]{1,0:T(8,128)(2,1)S(1)} %get-tuple-element.22.refs_4_, ...), custom_call_target="tpu_custom_call" | custom-call | flops 12582912 | bytes 1048576 | tf_op jit(solution)/shard_map/states/pallas_call | solution.py:242
  11.2 0.6 %collective-permute-start.3 = (bf16[16,3200]{1,0:T(8,128)(2,1)S(1)}, bf16[16,3200]{1,0:T(8,128)(2,1)S(1)}, u32[]{:S(2)}, u32[]{:S(2)}) collective-permute-start(bf16[16,3200]{1,0:T(8,128)(2,1)S(1)} %states.1.refs_8_.refs_0_), channel_id=1, source_target_pairs={{0,4},{4,8},{8,12},{12,0},{1,5},{5,9},{9,13},{13,1},{2,6},{6,10},{... | collective-permute-start | bytes 307208 | tf_op jit(solution)/shard_map/states/ppermute | solution.py:186
  11.8 3.1 %collective-permute-start.4 = (bf16[16,3200]{1,0:T(8,128)(2,1)S(1)}, bf16[16,3200]{1,0:T(8,128)(2,1)S(1)}, u32[]{:S(2)}, u32[]{:S(2)}) collective-permute-start(bf16[16,3200]{1,0:T(8,128)(2,1)S(1)} %states.1.refs_8_.refs_0_), channel_id=1, source_target_pairs={{0,8},{4,12},{8,0},{12,4},{1,9},{5,13},{9,1},{13,5},{2,10},{6,14},... | collective-permute-start | bytes 307208 | tf_op jit(solution)/shard_map/states/ppermute | solution.py:186
  14.9 0.1 collective-permute-start.5
  15.1 0.0 copy-start
  15.1 5.2 %pairs.1 = (f32[1,128]{1,0:T(1,128)S(1)}, s32[4,128]{1,0:T(4,128)S(1)}) custom-call(s32[8]{0:T(128)} %refs_0_.1, s32[8]{0:T(128)S(1)} %collective-permute-done.refs_1_, s32[8]{0:T(128)S(1)} %collective-permute-done.1.refs_2_, s32[8]{0:T(128)S(1)} %collective-permute-done.2.refs_3_, s32[2,256]{1,0:T(2,128)} %bitcast.13, ...), custom_call_target="tpu_custom_call" | custom-call | flops 4294967296 | bytes 4194304 | tf_op jit(solution)/shard_map/pairs/pallas_call | solution.py:253
  20.2 0.1 collective-permute-start.7
  20.3 0.0 collective-permute-done.3.refs_1_
  20.3 0.7 %collective-permute-start.9 = (f32[1,128]{1,0:T(1,128)S(1)}, f32[1,128]{1,0:T(1,128)S(1)}, u32[]{:S(2)}, u32[]{:S(2)}) collective-permute-start(f32[1,128]{1,0:T(1,128)S(1)} %get-tuple-element.32.refs_7_), channel_id=1, source_target_pairs={{0,3},{1,2},{2,1},{3,0},{4,7},{5,6},{6,5},{7,4},{8,11},{9,10},{10,... | collective-permute-start | bytes 1544 | tf_op jit(solution)/shard_map/pairs/ppermute | solution.py:279
  21.0 0.4 %collective-permute-done.7.refs_8_ = f32[1,128]{1,0:T(1,128)S(1)} collective-permute-done((f32[1,128]{1,0:T(1,128)S(1)}, f32[1,128]{1,0:T(1,128)S(1)}, u32[]{:S(2)}, u32[]{:S(2)}) %collective-permute-start.7) | collective-permute-done | bytes 544 | tf_op jit(solution)/shard_map/pairs/ppermute | solution.py:279
  21.4 1.0 %collective-permute-start.8 = (f32[1,128]{1,0:T(1,128)S(1)}, f32[1,128]{1,0:T(1,128)S(1)}, u32[]{:S(2)}, u32[]{:S(2)}) collective-permute-start(f32[1,128]{1,0:T(1,128)S(1)} %get-tuple-element.32.refs_7_), channel_id=1, source_target_pairs={{0,2},{1,3},{2,0},{3,1},{4,6},{5,7},{6,4},{7,5},{8,10},{9,11},{10,... | collective-permute-start | bytes 1544 | tf_op jit(solution)/shard_map/pairs/ppermute | solution.py:279
  22.5 0.0 collective-permute-done.4.refs_2_
  22.5 0.0 collective-permute-done.5.refs_3_
  22.5 0.9 %collective-permute-done.9.refs_10_ = f32[1,128]{1,0:T(1,128)S(1)} collective-permute-done((f32[1,128]{1,0:T(1,128)S(1)}, f32[1,128]{1,0:T(1,128)S(1)}, u32[]{:S(2)}, u32[]{:S(2)}) %collective-permute-start.9) | collective-permute-done | bytes 544 | tf_op jit(solution)/shard_map/pairs/ppermute | solution.py:279
  23.4 1.6 %collective-permute-done.8.refs_9_ = f32[1,128]{1,0:T(1,128)S(1)} collective-permute-done((f32[1,128]{1,0:T(1,128)S(1)}, f32[1,128]{1,0:T(1,128)S(1)}, u32[]{:S(2)}, u32[]{:S(2)}) %collective-permute-start.8) | collective-permute-done | bytes 544 | tf_op jit(solution)/shard_map/pairs/ppermute | solution.py:279
  25.0 0.0 collective-permute-done.6.refs_5_
  25.0 0.0 copy-done
  25.0 0.9 %scores.1 = (f32[1,128]{1,0:T(1,128)S(1)}, f32[1,128]{1,0:T(1,128)S(1)}, f32[1,128]{1,0:T(1,128)S(1)}, f32[1,128]{1,0:T(1,128)S(1)}) custom-call(bf16[16,3200]{1,0:T(8,128)(2,1)S(1)} %states.1.refs_8_.refs_0_, bf16[16,3200]{1,0:T(8,128)(2,1)S(1)} %collective-permute-done.3.refs_1_, bf16[16,3200]{1,0:T(8,128)(2,1)S(1)} %collective-permute-done.4.refs_2_, ...), custom_call_target="tpu_custom_call" | custom-call | flops 100663296 | bytes 2097152 | tf_op jit(solution)/shard_map/scores/pallas_call | solution.py:283
  25.9 2.0 %collective-permute-start.10 = (f32[1,128]{1,0:T(1,128)S(1)}, f32[1,128]{1,0:T(1,128)S(1)}, u32[]{:S(2)}, u32[]{:S(2)}) collective-permute-start(f32[1,128]{1,0:T(1,128)S(1)} %get-tuple-element.34), channel_id=1, source_target_pairs={{0,4},{4,8},{8,12},{12,0},{1,5},{5,9},{9,13},{13,1},{2,6},{6,10},{... | collective-permute-start | bytes 1544 | tf_op jit(solution)/shard_map/back/ppermute | solution.py:186
  27.8 0.2 collective-permute-start.11
  28.0 2.8 %collective-permute-start.12 = (f32[1,128]{1,0:T(1,128)S(1)}, f32[1,128]{1,0:T(1,128)S(1)}, u32[]{:S(2)}, u32[]{:S(2)}) collective-permute-start(f32[1,128]{1,0:T(1,128)S(1)} %get-tuple-element.36), channel_id=1, source_target_pairs={{0,12},{4,0},{8,4},{12,8},{1,13},{5,1},{9,5},{13,9},{2,14},{6,2},{... | collective-permute-start | bytes 1544 | tf_op jit(solution)/shard_map/back/ppermute | solution.py:186
  30.9 0.4 %collective-permute-done.10 = f32[1,128]{1,0:T(1,128)S(1)} collective-permute-done((f32[1,128]{1,0:T(1,128)S(1)}, f32[1,128]{1,0:T(1,128)S(1)}, u32[]{:S(2)}, u32[]{:S(2)}) %collective-permute-start.10) | collective-permute-done | bytes 544 | tf_op jit(solution)/shard_map/back/ppermute | solution.py:186
  31.3 1.0 %collective-permute-done.11 = f32[1,128]{1,0:T(1,128)S(1)} collective-permute-done((f32[1,128]{1,0:T(1,128)S(1)}, f32[1,128]{1,0:T(1,128)S(1)}, u32[]{:S(2)}, u32[]{:S(2)}) %collective-permute-start.11) | collective-permute-done | bytes 544 | tf_op jit(solution)/shard_map/back/ppermute | solution.py:186
  32.3 0.0 collective-permute-done.12
  32.3 0.5 %add_bitcast_fusion = f32[128]{0:T(128)} fusion(f32[1,128]{1,0:T(1,128)S(1)} %collective-permute-done.12, f32[1,128]{1,0:T(1,128)S(1)} %collective-permute-done.11, f32[1,128]{1,0:T(1,128)S(1)} %get-tuple-element.33, f32[1,128]{1,0:T(1,128)S(1)} %collective-permute-done.10), kind=kLoop, calls=%fused_computation | loop fusion | flops 384 | bytes 2560 | tf_op jit(solution)/shard_map/reshape | solution.py:301
Async XLA Ops:
  0.0 25.0 %collective-permute-start.6 = (bf16[128,3072]{1,0:T(8,128)(2,1)}, bf16[128,3072]{1,0:T(8,128)(2,1)S(1)}, u32[]{:S(2)}, u32[]{:S(2)}) collective-permute-start(bf16[128,3072]{1,0:T(8,128)(2,1)} %refs_4_.1), channel_id=1, source_target_pairs={{0,2},{2,0},{1,3},{3,1},{4,6},{6,4},{5,7},{7,5},{8,10},{10,8},{9,1... | collective-permute-start | bytes 2359304 | tf_op jit(solution)/shard_map/item_rows/ppermute | solution.py:186
  2.9 7.7 %collective-permute-start = (s32[8]{0:T(128)}, s32[8]{0:T(128)S(1)}, u32[]{:S(2)}, u32[]{:S(2)}) collective-permute-start(s32[8]{0:T(128)} %refs_0_.1), channel_id=1, source_target_pairs={{0,4},{4,8},{8,12},{12,0},{1,5},{5,9},{9,13},{13,1},{2,6},{6,10},{... | collective-permute-start | bytes 104 | tf_op jit(solution)/shard_map/ids/ppermute | solution.py:186
  4.5 6.2 %collective-permute-start.1 = (s32[8]{0:T(128)}, s32[8]{0:T(128)S(1)}, u32[]{:S(2)}, u32[]{:S(2)}) collective-permute-start(s32[8]{0:T(128)} %refs_0_.1), channel_id=1, source_target_pairs={{0,8},{4,12},{8,0},{12,4},{1,9},{5,13},{9,1},{13,5},{2,10},{6,14},... | collective-permute-start | bytes 104 | tf_op jit(solution)/shard_map/ids/ppermute | solution.py:186
  7.1 3.7 %collective-permute-start.2 = (s32[8]{0:T(128)}, s32[8]{0:T(128)S(1)}, u32[]{:S(2)}, u32[]{:S(2)}) collective-permute-start(s32[8]{0:T(128)} %refs_0_.1), channel_id=1, source_target_pairs={{0,12},{4,0},{8,4},{12,8},{1,13},{5,1},{9,5},{13,9},{2,14},{6,2},{... | collective-permute-start | bytes 104 | tf_op jit(solution)/shard_map/ids/ppermute | solution.py:186
  11.2 9.1 %collective-permute-start.3 = (bf16[16,3200]{1,0:T(8,128)(2,1)S(1)}, bf16[16,3200]{1,0:T(8,128)(2,1)S(1)}, u32[]{:S(2)}, u32[]{:S(2)}) collective-permute-start(bf16[16,3200]{1,0:T(8,128)(2,1)S(1)} %states.1.refs_8_.refs_0_), channel_id=1, source_target_pairs={{0,4},{4,8},{8,12},{12,0},{1,5},{5,9},{9,13},{13,1},{2,6},{6,10},{... | collective-permute-start | bytes 307208 | tf_op jit(solution)/shard_map/states/ppermute | solution.py:186
  11.8 10.7 %collective-permute-start.4 = (bf16[16,3200]{1,0:T(8,128)(2,1)S(1)}, bf16[16,3200]{1,0:T(8,128)(2,1)S(1)}, u32[]{:S(2)}, u32[]{:S(2)}) collective-permute-start(bf16[16,3200]{1,0:T(8,128)(2,1)S(1)} %states.1.refs_8_.refs_0_), channel_id=1, source_target_pairs={{0,8},{4,12},{8,0},{12,4},{1,9},{5,13},{9,1},{13,5},{2,10},{6,14},... | collective-permute-start | bytes 307208 | tf_op jit(solution)/shard_map/states/ppermute | solution.py:186
  14.9 7.5 %collective-permute-start.5 = (bf16[16,3200]{1,0:T(8,128)(2,1)S(1)}, bf16[16,3200]{1,0:T(8,128)(2,1)S(1)}, u32[]{:S(2)}, u32[]{:S(2)}) collective-permute-start(bf16[16,3200]{1,0:T(8,128)(2,1)S(1)} %states.1.refs_8_.refs_0_), channel_id=1, source_target_pairs={{0,12},{4,0},{8,4},{12,8},{1,13},{5,1},{9,5},{13,9},{2,14},{6,2},{... | collective-permute-start | bytes 307208 | tf_op jit(solution)/shard_map/states/ppermute | solution.py:186
  15.1 9.9 %copy-start = (bf16[128,3072]{1,0:T(8,128)(2,1)S(1)}, bf16[128,3072]{1,0:T(8,128)(2,1)}, u32[]{:S(2)}) copy-start(bf16[128,3072]{1,0:T(8,128)(2,1)} %refs_4_.1) | copy-start | bytes 2359300
  20.2 1.2 %collective-permute-start.7 = (f32[1,128]{1,0:T(1,128)S(1)}, f32[1,128]{1,0:T(1,128)S(1)}, u32[]{:S(2)}, u32[]{:S(2)}) collective-permute-start(f32[1,128]{1,0:T(1,128)S(1)} %get-tuple-element.32.refs_7_), channel_id=1, source_target_pairs={{0,1},{1,0},{2,3},{3,2},{4,5},{5,4},{6,7},{7,6},{8,9},{9,8},{10,11... | collective-permute-start | bytes 1544 | tf_op jit(solution)/shard_map/pairs/ppermute | solution.py:279
  20.3 3.0 %collective-permute-start.9 = (f32[1,128]{1,0:T(1,128)S(1)}, f32[1,128]{1,0:T(1,128)S(1)}, u32[]{:S(2)}, u32[]{:S(2)}) collective-permute-start(f32[1,128]{1,0:T(1,128)S(1)} %get-tuple-element.32.refs_7_), channel_id=1, source_target_pairs={{0,3},{1,2},{2,1},{3,0},{4,7},{5,6},{6,5},{7,4},{8,11},{9,10},{10,... | collective-permute-start | bytes 1544 | tf_op jit(solution)/shard_map/pairs/ppermute | solution.py:279
  21.4 3.5 %collective-permute-start.8 = (f32[1,128]{1,0:T(1,128)S(1)}, f32[1,128]{1,0:T(1,128)S(1)}, u32[]{:S(2)}, u32[]{:S(2)}) collective-permute-start(f32[1,128]{1,0:T(1,128)S(1)} %get-tuple-element.32.refs_7_), channel_id=1, source_target_pairs={{0,2},{1,3},{2,0},{3,1},{4,6},{5,7},{6,4},{7,5},{8,10},{9,11},{10,... | collective-permute-start | bytes 1544 | tf_op jit(solution)/shard_map/pairs/ppermute | solution.py:279
  25.9 5.4 %collective-permute-start.10 = (f32[1,128]{1,0:T(1,128)S(1)}, f32[1,128]{1,0:T(1,128)S(1)}, u32[]{:S(2)}, u32[]{:S(2)}) collective-permute-start(f32[1,128]{1,0:T(1,128)S(1)} %get-tuple-element.34), channel_id=1, source_target_pairs={{0,4},{4,8},{8,12},{12,0},{1,5},{5,9},{9,13},{13,1},{2,6},{6,10},{... | collective-permute-start | bytes 1544 | tf_op jit(solution)/shard_map/back/ppermute | solution.py:186
  27.8 4.4 %collective-permute-start.11 = (f32[1,128]{1,0:T(1,128)S(1)}, f32[1,128]{1,0:T(1,128)S(1)}, u32[]{:S(2)}, u32[]{:S(2)}) collective-permute-start(f32[1,128]{1,0:T(1,128)S(1)} %get-tuple-element.35), channel_id=1, source_target_pairs={{0,8},{4,12},{8,0},{12,4},{1,9},{5,13},{9,1},{13,5},{2,10},{6,14},... | collective-permute-start | bytes 1544 | tf_op jit(solution)/shard_map/back/ppermute | solution.py:186
  28.0 4.2 %collective-permute-start.12 = (f32[1,128]{1,0:T(1,128)S(1)}, f32[1,128]{1,0:T(1,128)S(1)}, u32[]{:S(2)}, u32[]{:S(2)}) collective-permute-start(f32[1,128]{1,0:T(1,128)S(1)} %get-tuple-element.36), channel_id=1, source_target_pairs={{0,12},{4,0},{8,4},{12,8},{1,13},{5,1},{9,5},{13,9},{2,14},{6,2},{... | collective-permute-start | bytes 1544 | tf_op jit(solution)/shard_map/back/ppermute | solution.py:186

commit v12 on v11

--- a/solution.py
+++ b/solution.py
@@ -267,17 +267,16 @@
             compiler_params=params,
             cost_estimate=pl.CostEstimate(flops=2 * count * K * K * rows * 16, bytes_accessed=4 * 1024 * 1024, transcendentals=0),
         )(*users, in_hbm(pair_fields.T), *turned, picked)
-        pair_scores, moved = [], 0
-        for q in range(planes):
-            for h in range(parts):
-                perm = [
-                    (c * parts + d, (c + q) % planes * parts + (d + h) % parts) for c in range(planes) for d in range(parts)
-                ]
-                source = pair_parts
-                if 0 < moved < total:
-                    source, states[1] = lax.optimization_barrier((pair_parts, states[1]))
-                pair_scores.append(lax.ppermute(source, ("cache", "pair"), perm) if q or h else pair_parts)
-                moved += q + h > 0
+        pair_scores = {(0, 0): pair_parts}
+        for q, h in [(q, h) for q in range(planes - 1, -1, -1) for h in range(parts) if q or h]:
+            perm = [
+                (c * parts + d, (c + q) % planes * parts + (d + h) % parts) for c in range(planes) for d in range(parts)
+            ]
+            source, after = pair_parts, {1: 3, 2: 2}.get(len(pair_scores) - 1, 0)
+            if after:
+                source, states[after] = lax.optimization_barrier((pair_parts, states[after]))
+            pair_scores[q, h] = lax.ppermute(source, ("cache", "pair"), perm)
+        pair_scores = [pair_scores[q, h] for q in range(planes) for h in range(parts)]
 
     with jax.named_scope("scores"):
         outs = pl.pallas_call(

time: 32.9 us -> 32.8 us (level)
  starting transfers between devices: 19.1 us -> 18.4 us
  waiting for transfers between devices: 4.46 us -> 4.92 us
    ppermute x10, waiting for transfers between devices: 1.52 us -> 3.52 us  [shift(): return lax.ppermute(x, axis, [(s, (s + step) % size) for s in range(size)])]
    ppermute x3, waiting for transfers between devices: 2.94 us -> 1.4 us  [body(): pair_scores[q, h] = lax.ppermute(source, ('cache', 'pair'), perm)]
    ppermute x3, starting transfers between devices: 1.76 us -> 0.81 us  [body(): pair_scores[q, h] = lax.ppermute(source, ('cache', 'pair'), perm)]
  transfers between devices with their start and end apart: 13 -> 13, of which waited for: 6 -> 5; matrix products, arithmetic and copies ran while one was open for 0% -> 0% of each run, Pallas kernels for 24% -> 24%
where the time goes in v12:
time: 32.8 us; the launch traced here: 32.6 us
  starting transfers between devices  18.4 us (56%)
  Pallas kernels  8.68 us (26%)
  waiting for transfers between devices  4.92 us (15%)
  other arithmetic  0.52 us (2%)
    ppermute x10, starting transfers between devices, shift(): return lax.ppermute(x, axis, [(s, (s + step) % size) for s in range(size)])  17.6 us
    pallas_call x1, Pallas kernels, body(): pl.pallas_call(functools.partial(pair_kernel, total, cap, slots, user_sta...  5.19 us
    ppermute x10, waiting for transfers between devices, shift(): return lax.ppermute(x, axis, [(s, (s + step) % size) for s in range(size)])  3.52 us
    pallas_call x1, Pallas kernels, body(): pl.pallas_call(turn_kernel, out_shape=(jax.ShapeDtypeStruct((width, rows)...  2.2 us
    ppermute x3, waiting for transfers between devices, body(): pair_scores[q, h] = lax.ppermute(source, ('cache', 'pair'), perm)  1.4 us
    pallas_call x1, Pallas kernels, body(): pl.pallas_call(functools.partial(score_kernel, total, planes, parts), out...  0.89 us
    ppermute x3, starting transfers between devices, body(): pair_scores[q, h] = lax.ppermute(source, ('cache', 'pair'), perm)  0.81 us
  transfers between devices with their start and end apart: 13, of which 5 were waited for; matrix products, arithmetic and copies ran while one was open for 0% of the time, Pallas kernels for 24%

profile of v12, /device:TPU:0, one launch (start us, length us, event | category | flops | bytes accessed | tf_op | source)
XLA Modules:
  0.0 32.6 jit_solution(5946592406786134915)
XLA Ops:
  0.0 2.9 %collective-permute-start.6 = (bf16[128,3072]{1,0:T(8,128)(2,1)}, bf16[128,3072]{1,0:T(8,128)(2,1)S(1)}, u32[]{:S(2)}, u32[]{:S(2)}) collective-permute-start(bf16[128,3072]{1,0:T(8,128)(2,1)} %refs_4_.1), channel_id=1, source_target_pairs={{0,2},{2,0},{1,3},{3,1},{4,6},{6,4},{5,7},{7,5},{8,10},{10,8},{9,1... | collective-permute-start | bytes 2359304 | tf_op jit(solution)/shard_map/item_rows/ppermute | solution.py:186
  2.9 1.6 %collective-permute-start = (s32[8]{0:T(128)}, s32[8]{0:T(128)S(1)}, u32[]{:S(2)}, u32[]{:S(2)}) collective-permute-start(s32[8]{0:T(128)} %refs_0_.1), channel_id=1, source_target_pairs={{0,4},{4,8},{8,12},{12,0},{1,5},{5,9},{9,13},{13,1},{2,6},{6,10},{... | collective-permute-start | bytes 104 | tf_op jit(solution)/shard_map/ids/ppermute | solution.py:186
  4.5 2.6 %collective-permute-start.1 = (s32[8]{0:T(128)}, s32[8]{0:T(128)S(1)}, u32[]{:S(2)}, u32[]{:S(2)}) collective-permute-start(s32[8]{0:T(128)} %refs_0_.1), channel_id=1, source_target_pairs={{0,8},{4,12},{8,0},{12,4},{1,9},{5,13},{9,1},{13,5},{2,10},{6,14},... | collective-permute-start | bytes 104 | tf_op jit(solution)/shard_map/ids/ppermute | solution.py:186
  7.1 1.3 %collective-permute-start.2 = (s32[8]{0:T(128)}, s32[8]{0:T(128)S(1)}, u32[]{:S(2)}, u32[]{:S(2)}) collective-permute-start(s32[8]{0:T(128)} %refs_0_.1), channel_id=1, source_target_pairs={{0,12},{4,0},{8,4},{12,8},{1,13},{5,1},{9,5},{13,9},{2,14},{6,2},{... | collective-permute-start | bytes 104 | tf_op jit(solution)/shard_map/ids/ppermute | solution.py:186
  8.5 2.2 %turn.1 = (f32[3072,128]{1,0:T(8,128)S(1)}, bf16[3072,128]{1,0:T(8,128)(2,1)S(1)}, bf16[64,64,256]{2,1,0:T(8,128)(2,1)S(1)}, bf16[128,3072]{1,0:T(8,128)(2,1)S(1...) custom-call(bf16[128,3072]{1,0:T(8,128)(2,1)} %refs_4_.1, bf16[64,64,256]{2,1,0:T(8,128)(2,1)} %bitcast.12, ...), custom_call_target="tpu_custom_call" | custom-call | flops 1610612736 | bytes 8388608 | tf_op jit(solution)/shard_map/turn/pallas_call | solution.py:214
  10.7 0.0 collective-permute-done.refs_1_
  10.7 0.0 collective-permute-done.1.refs_2_
  10.7 0.1 collective-permute-done.2.refs_3_
  10.8 0.4 %states.1.refs_8_.refs_0_ = bf16[16,3200]{1,0:T(8,128)(2,1)S(1)} custom-call(s32[1,8]{1,0:T(1,128)S(1)} %get-tuple-element.21.refs_0_, s32[1,8]{1,0:T(1,128)S(1)} %bitcast.9, s32[1,8]{1,0:T(1,128)S(1)} %bitcast.10, s32[1,8]{1,0:T(1,128)S(1)} %bitcast.11, bf16[16,128]{1,0:T(8,128)(2,1)S(1)} %get-tuple-element.22.refs_4_, ...), custom_call_target="tpu_custom_call" | custom-call | flops 12582912 | bytes 1048576 | tf_op jit(solution)/shard_map/states/pallas_call | solution.py:242
  11.2 3.2 %collective-permute-start.5 = (bf16[16,3200]{1,0:T(8,128)(2,1)S(1)}, bf16[16,3200]{1,0:T(8,128)(2,1)S(1)}, u32[]{:S(2)}, u32[]{:S(2)}) collective-permute-start(bf16[16,3200]{1,0:T(8,128)(2,1)S(1)} %states.1.refs_8_.refs_0_), channel_id=1, source_target_pairs={{0,12},{4,0},{8,4},{12,8},{1,13},{5,1},{9,5},{13,9},{2,14},{6,2},{... | collective-permute-start | bytes 307208 | tf_op jit(solution)/shard_map/states/ppermute | solution.py:186
  14.4 0.0 collective-permute-start.4
  14.4 0.6 %collective-permute-start.3 = (bf16[16,3200]{1,0:T(8,128)(2,1)S(1)}, bf16[16,3200]{1,0:T(8,128)(2,1)S(1)}, u32[]{:S(2)}, u32[]{:S(2)}) collective-permute-start(bf16[16,3200]{1,0:T(8,128)(2,1)S(1)} %states.1.refs_8_.refs_0_), channel_id=1, source_target_pairs={{0,4},{4,8},{8,12},{12,0},{1,5},{5,9},{9,13},{13,1},{2,6},{6,10},{... | collective-permute-start | bytes 307208 | tf_op jit(solution)/shard_map/states/ppermute | solution.py:186
  15.0 0.0 copy-start
  15.0 5.2 %pairs.1 = (f32[1,128]{1,0:T(1,128)S(1)}, s32[4,128]{1,0:T(4,128)S(1)}) custom-call(s32[8]{0:T(128)} %refs_0_.1, s32[8]{0:T(128)S(1)} %collective-permute-done.refs_1_, s32[8]{0:T(128)S(1)} %collective-permute-done.1.refs_2_, s32[8]{0:T(128)S(1)} %collective-permute-done.2.refs_3_, s32[2,256]{1,0:T(2,128)} %bitcast.13, ...), custom_call_target="tpu_custom_call" | custom-call | flops 4294967296 | bytes 4194304 | tf_op jit(solution)/shard_map/pairs/pallas_call | solution.py:253
  20.2 0.6 %collective-permute-start.8 = (f32[1,128]{1,0:T(1,128)S(1)}, f32[1,128]{1,0:T(1,128)S(1)}, u32[]{:S(2)}, u32[]{:S(2)}) collective-permute-start(f32[1,128]{1,0:T(1,128)S(1)} %get-tuple-element.32.refs_7_), channel_id=1, source_target_pairs={{0,2},{1,3},{2,0},{3,1},{4,6},{5,7},{6,4},{7,5},{8,10},{9,11},{10,... | collective-permute-start | bytes 1544 | tf_op jit(solution)/shard_map/pairs/ppermute | solution.py:278
  20.8 0.0 collective-permute-done.5.refs_3_
  20.8 0.0 collective-permute-start.9
  20.8 1.4 %collective-permute-done.4.refs_2_ = bf16[16,3200]{1,0:T(8,128)(2,1)S(1)} collective-permute-done((bf16[16,3200]{1,0:T(8,128)(2,1)S(1)}, bf16[16,3200]{1,0:T(8,128)(2,1)S(1)}, u32[]{:S(2)}, u32[]{:S(2)}) %collective-permute-start.4) | collective-permute-done | bytes 102432 | tf_op jit(solution)/shard_map/states/ppermute | solution.py:186
  22.2 0.2 collective-permute-start.7
  22.4 1.4 %collective-permute-done.8.refs_9_ = f32[1,128]{1,0:T(1,128)S(1)} collective-permute-done((f32[1,128]{1,0:T(1,128)S(1)}, f32[1,128]{1,0:T(1,128)S(1)}, u32[]{:S(2)}, u32[]{:S(2)}) %collective-permute-start.8) | collective-permute-done | bytes 544 | tf_op jit(solution)/shard_map/pairs/ppermute | solution.py:278
  23.8 0.0 collective-permute-done.3.refs_1_
  23.8 0.0 collective-permute-done.9.refs_10_
  23.8 0.0 collective-permute-done.7.refs_8_
  23.8 0.0 collective-permute-done.6.refs_5_
  23.8 0.0 copy-done
  23.9 0.9 %scores.1 = (f32[1,128]{1,0:T(1,128)S(1)}, f32[1,128]{1,0:T(1,128)S(1)}, f32[1,128]{1,0:T(1,128)S(1)}, f32[1,128]{1,0:T(1,128)S(1)}) custom-call(bf16[16,3200]{1,0:T(8,128)(2,1)S(1)} %states.1.refs_8_.refs_0_, bf16[16,3200]{1,0:T(8,128)(2,1)S(1)} %collective-permute-done.3.refs_1_, bf16[16,3200]{1,0:T(8,128)(2,1)S(1)} %collective-permute-done.4.refs_2_, ...), custom_call_target="tpu_custom_call" | custom-call | flops 100663296 | bytes 2097152 | tf_op jit(solution)/shard_map/scores/pallas_call | solution.py:282
  24.8 2.9 %collective-permute-start.10 = (f32[1,128]{1,0:T(1,128)S(1)}, f32[1,128]{1,0:T(1,128)S(1)}, u32[]{:S(2)}, u32[]{:S(2)}) collective-permute-start(f32[1,128]{1,0:T(1,128)S(1)} %get-tuple-element.34), channel_id=1, source_target_pairs={{0,4},{4,8},{8,12},{12,0},{1,5},{5,9},{9,13},{13,1},{2,6},{6,10},{... | collective-permute-start | bytes 1544 | tf_op jit(solution)/shard_map/back/ppermute | solution.py:186
  27.6 0.9 %collective-permute-start.11 = (f32[1,128]{1,0:T(1,128)S(1)}, f32[1,128]{1,0:T(1,128)S(1)}, u32[]{:S(2)}, u32[]{:S(2)}) collective-permute-start(f32[1,128]{1,0:T(1,128)S(1)} %get-tuple-element.35), channel_id=1, source_target_pairs={{0,8},{4,12},{8,0},{12,4},{1,9},{5,13},{9,1},{13,5},{2,10},{6,14},... | collective-permute-start | bytes 1544 | tf_op jit(solution)/shard_map/back/ppermute | solution.py:186
  28.5 1.5 %collective-permute-start.12 = (f32[1,128]{1,0:T(1,128)S(1)}, f32[1,128]{1,0:T(1,128)S(1)}, u32[]{:S(2)}, u32[]{:S(2)}) collective-permute-start(f32[1,128]{1,0:T(1,128)S(1)} %get-tuple-element.36), channel_id=1, source_target_pairs={{0,12},{4,0},{8,4},{12,8},{1,13},{5,1},{9,5},{13,9},{2,14},{6,2},{... | collective-permute-start | bytes 1544 | tf_op jit(solution)/shard_map/back/ppermute | solution.py:186
  30.1 0.1 collective-permute-done.10
  30.1 1.9 %collective-permute-done.11 = f32[1,128]{1,0:T(1,128)S(1)} collective-permute-done((f32[1,128]{1,0:T(1,128)S(1)}, f32[1,128]{1,0:T(1,128)S(1)}, u32[]{:S(2)}, u32[]{:S(2)}) %collective-permute-start.11) | collective-permute-done | bytes 544 | tf_op jit(solution)/shard_map/back/ppermute | solution.py:186
  32.1 0.0 collective-permute-done.12
  32.1 0.5 %add_bitcast_fusion = f32[128]{0:T(128)} fusion(f32[1,128]{1,0:T(1,128)S(1)} %collective-permute-done.12, f32[1,128]{1,0:T(1,128)S(1)} %collective-permute-done.11, f32[1,128]{1,0:T(1,128)S(1)} %get-tuple-element.33, f32[1,128]{1,0:T(1,128)S(1)} %collective-permute-done.10), kind=kLoop, calls=%fused_computation | loop fusion | flops 384 | bytes 2560 | tf_op jit(solution)/shard_map/reshape | solution.py:300
Async XLA Ops:
  0.0 23.8 %collective-permute-start.6 = (bf16[128,3072]{1,0:T(8,128)(2,1)}, bf16[128,3072]{1,0:T(8,128)(2,1)S(1)}, u32[]{:S(2)}, u32[]{:S(2)}) collective-permute-start(bf16[128,3072]{1,0:T(8,128)(2,1)} %refs_4_.1), channel_id=1, source_target_pairs={{0,2},{2,0},{1,3},{3,1},{4,6},{6,4},{5,7},{7,5},{8,10},{10,8},{9,1... | collective-permute-start | bytes 2359304 | tf_op jit(solution)/shard_map/item_rows/ppermute | solution.py:186
  2.9 7.7 %collective-permute-start = (s32[8]{0:T(128)}, s32[8]{0:T(128)S(1)}, u32[]{:S(2)}, u32[]{:S(2)}) collective-permute-start(s32[8]{0:T(128)} %refs_0_.1), channel_id=1, source_target_pairs={{0,4},{4,8},{8,12},{12,0},{1,5},{5,9},{9,13},{13,1},{2,6},{6,10},{... | collective-permute-start | bytes 104 | tf_op jit(solution)/shard_map/ids/ppermute | solution.py:186
  4.5 6.2 %collective-permute-start.1 = (s32[8]{0:T(128)}, s32[8]{0:T(128)S(1)}, u32[]{:S(2)}, u32[]{:S(2)}) collective-permute-start(s32[8]{0:T(128)} %refs_0_.1), channel_id=1, source_target_pairs={{0,8},{4,12},{8,0},{12,4},{1,9},{5,13},{9,1},{13,5},{2,10},{6,14},... | collective-permute-start | bytes 104 | tf_op jit(solution)/shard_map/ids/ppermute | solution.py:186
  7.1 3.7 %collective-permute-start.2 = (s32[8]{0:T(128)}, s32[8]{0:T(128)S(1)}, u32[]{:S(2)}, u32[]{:S(2)}) collective-permute-start(s32[8]{0:T(128)} %refs_0_.1), channel_id=1, source_target_pairs={{0,12},{4,0},{8,4},{12,8},{1,13},{5,1},{9,5},{13,9},{2,14},{6,2},{... | collective-permute-start | bytes 104 | tf_op jit(solution)/shard_map/ids/ppermute | solution.py:186
  11.2 9.6 %collective-permute-start.5 = (bf16[16,3200]{1,0:T(8,128)(2,1)S(1)}, bf16[16,3200]{1,0:T(8,128)(2,1)S(1)}, u32[]{:S(2)}, u32[]{:S(2)}) collective-permute-start(bf16[16,3200]{1,0:T(8,128)(2,1)S(1)} %states.1.refs_8_.refs_0_), channel_id=1, source_target_pairs={{0,12},{4,0},{8,4},{12,8},{1,13},{5,1},{9,5},{13,9},{2,14},{6,2},{... | collective-permute-start | bytes 307208 | tf_op jit(solution)/shard_map/states/ppermute | solution.py:186
  14.4 7.8 %collective-permute-start.4 = (bf16[16,3200]{1,0:T(8,128)(2,1)S(1)}, bf16[16,3200]{1,0:T(8,128)(2,1)S(1)}, u32[]{:S(2)}, u32[]{:S(2)}) collective-permute-start(bf16[16,3200]{1,0:T(8,128)(2,1)S(1)} %states.1.refs_8_.refs_0_), channel_id=1, source_target_pairs={{0,8},{4,12},{8,0},{12,4},{1,9},{5,13},{9,1},{13,5},{2,10},{6,14},... | collective-permute-start | bytes 307208 | tf_op jit(solution)/shard_map/states/ppermute | solution.py:186
  14.4 9.5 %collective-permute-start.3 = (bf16[16,3200]{1,0:T(8,128)(2,1)S(1)}, bf16[16,3200]{1,0:T(8,128)(2,1)S(1)}, u32[]{:S(2)}, u32[]{:S(2)}) collective-permute-start(bf16[16,3200]{1,0:T(8,128)(2,1)S(1)} %states.1.refs_8_.refs_0_), channel_id=1, source_target_pairs={{0,4},{4,8},{8,12},{12,0},{1,5},{5,9},{9,13},{13,1},{2,6},{6,10},{... | collective-permute-start | bytes 307208 | tf_op jit(solution)/shard_map/states/ppermute | solution.py:186
  15.0 8.8 %copy-start = (bf16[128,3072]{1,0:T(8,128)(2,1)S(1)}, bf16[128,3072]{1,0:T(8,128)(2,1)}, u32[]{:S(2)}) copy-start(bf16[128,3072]{1,0:T(8,128)(2,1)} %refs_4_.1) | copy-start | bytes 2359300
  20.2 3.6 %collective-permute-start.8 = (f32[1,128]{1,0:T(1,128)S(1)}, f32[1,128]{1,0:T(1,128)S(1)}, u32[]{:S(2)}, u32[]{:S(2)}) collective-permute-start(f32[1,128]{1,0:T(1,128)S(1)} %get-tuple-element.32.refs_7_), channel_id=1, source_target_pairs={{0,2},{1,3},{2,0},{3,1},{4,6},{5,7},{6,4},{7,5},{8,10},{9,11},{10,... | collective-permute-start | bytes 1544 | tf_op jit(solution)/shard_map/pairs/ppermute | solution.py:278
  20.8 3.0 %collective-permute-start.9 = (f32[1,128]{1,0:T(1,128)S(1)}, f32[1,128]{1,0:T(1,128)S(1)}, u32[]{:S(2)}, u32[]{:S(2)}) collective-permute-start(f32[1,128]{1,0:T(1,128)S(1)} %get-tuple-element.32.refs_7_), channel_id=1, source_target_pairs={{0,3},{1,2},{2,1},{3,0},{4,7},{5,6},{6,5},{7,4},{8,11},{9,10},{10,... | collective-permute-start | bytes 1544 | tf_op jit(solution)/shard_map/pairs/ppermute | solution.py:278
  22.2 1.6 %collective-permute-start.7 = (f32[1,128]{1,0:T(1,128)S(1)}, f32[1,128]{1,0:T(1,128)S(1)}, u32[]{:S(2)}, u32[]{:S(2)}) collective-permute-start(f32[1,128]{1,0:T(1,128)S(1)} %get-tuple-element.32.refs_7_), channel_id=1, source_target_pairs={{0,1},{1,0},{2,3},{3,2},{4,5},{5,4},{6,7},{7,6},{8,9},{9,8},{10,11... | collective-permute-start | bytes 1544 | tf_op jit(solution)/shard_map/pairs/ppermute | solution.py:278
  24.8 5.4 %collective-permute-start.10 = (f32[1,128]{1,0:T(1,128)S(1)}, f32[1,128]{1,0:T(1,128)S(1)}, u32[]{:S(2)}, u32[]{:S(2)}) collective-permute-start(f32[1,128]{1,0:T(1,128)S(1)} %get-tuple-element.34), channel_id=1, source_target_pairs={{0,4},{4,8},{8,12},{12,0},{1,5},{5,9},{9,13},{13,1},{2,6},{6,10},{... | collective-permute-start | bytes 1544 | tf_op jit(solution)/shard_map/back/ppermute | solution.py:186
  27.6 4.4 %collective-permute-start.11 = (f32[1,128]{1,0:T(1,128)S(1)}, f32[1,128]{1,0:T(1,128)S(1)}, u32[]{:S(2)}, u32[]{:S(2)}) collective-permute-start(f32[1,128]{1,0:T(1,128)S(1)} %get-tuple-element.35), channel_id=1, source_target_pairs={{0,8},{4,12},{8,0},{12,4},{1,9},{5,13},{9,1},{13,5},{2,10},{6,14},... | collective-permute-start | bytes 1544 | tf_op jit(solution)/shard_map/back/ppermute | solution.py:186
  28.5 3.5 %collective-permute-start.12 = (f32[1,128]{1,0:T(1,128)S(1)}, f32[1,128]{1,0:T(1,128)S(1)}, u32[]{:S(2)}, u32[]{:S(2)}) collective-permute-start(f32[1,128]{1,0:T(1,128)S(1)} %get-tuple-element.36), channel_id=1, source_target_pairs={{0,12},{4,0},{8,4},{12,8},{1,13},{5,1},{9,5},{13,9},{2,14},{6,2},{... | collective-permute-start | bytes 1544 | tf_op jit(solution)/shard_map/back/ppermute | solution.py:186

commit v13 on v12

--- a/solution.py
+++ b/solution.py
@@ -146,7 +146,7 @@
 
 
 def score_kernel(total, planes, parts, *refs):
-    states, refs = refs[:total], refs[total:]
+    states, refs = refs[:1] + refs[total - 1:0:-1], refs[total:]
     items, refs = refs[:planes], refs[planes:]
     places, pairs, refs = refs[0], refs[1:1 + planes * parts], refs[1 + planes * parts:]
     outs, (wanted, cands, linear) = refs[:total], refs[total:]
@@ -272,7 +272,7 @@
             perm = [
                 (c * parts + d, (c + q) % planes * parts + (d + h) % parts) for c in range(planes) for d in range(parts)
             ]
-            source, after = pair_parts, {1: 3, 2: 2}.get(len(pair_scores) - 1, 0)
+            source, after = pair_parts, {1: 1, 2: 2}.get(len(pair_scores) - 1, 0)
             if after:
                 source, states[after] = lax.optimization_barrier((pair_parts, states[after]))
             pair_scores[q, h] = lax.ppermute(source, ("cache", "pair"), perm)
@@ -291,7 +291,7 @@
             ],
             compiler_params=params,
             cost_estimate=pl.CostEstimate(flops=2 * 64 * 256 * width, bytes_accessed=2 * 1024 * 1024, transcendentals=0),
-        )(*states, *items, places, *pair_scores)
+        )(picked, *states[:0:-1], *items, places, *pair_scores)
 
     with jax.named_scope("back"):
         result = outs[0]

time: 32.8 us -> 31.9 us (0.973)
  waiting for transfers between devices: 4.92 us -> 3.04 us
  starting transfers between devices: 18.4 us -> 19.4 us
    ppermute x10, waiting for transfers between devices: 3.52 us -> 1.65 us  [shift(): return lax.ppermute(x, axis, [(s, (s + step) % size) for s in range(size)])]
    ppermute x3, starting transfers between devices: 0.81 us -> 2.08 us  [body(): pair_scores[q, h] = lax.ppermute(source, ('cache', 'pair'), perm)]
  transfers between devices with their start and end apart: 13 -> 13, of which waited for: 5 -> 5; matrix products, arithmetic and copies ran while one was open for 0% -> 0% of each run, Pallas kernels for 24% -> 25%
where the time goes in v13:
time: 31.9 us; the launch traced here: 31.7 us
  starting transfers between devices  19.4 us (61%)
  Pallas kernels  8.67 us (27%)
  waiting for transfers between devices  3.04 us (10%)
  other arithmetic  0.52 us (2%)
    ppermute x10, starting transfers between devices, shift(): return lax.ppermute(x, axis, [(s, (s + step) % size) for s in range(size)])  17.3 us
    pallas_call x1, Pallas kernels, body(): pl.pallas_call(functools.partial(pair_kernel, total, cap, slots, user_sta...  5.18 us
    pallas_call x1, Pallas kernels, body(): pl.pallas_call(turn_kernel, out_shape=(jax.ShapeDtypeStruct((width, rows)...  2.2 us
    ppermute x3, starting transfers between devices, body(): pair_scores[q, h] = lax.ppermute(source, ('cache', 'pair'), perm)  2.08 us
    ppermute x10, waiting for transfers between devices, shift(): return lax.ppermute(x, axis, [(s, (s + step) % size) for s in range(size)])  1.65 us
    ppermute x3, waiting for transfers between devices, body(): pair_scores[q, h] = lax.ppermute(source, ('cache', 'pair'), perm)  1.4 us
    pallas_call x1, Pallas kernels, body(): pl.pallas_call(functools.partial(score_kernel, total, planes, parts), out...  0.89 us
  transfers between devices with their start and end apart: 13, of which 5 were waited for; matrix products, arithmetic and copies ran while one was open for 0% of the time, Pallas kernels for 25%

profile of v13, /device:TPU:0, one launch (start us, length us, event | category | flops | bytes accessed | tf_op | source)
XLA Modules:
  0.0 31.7 jit_solution(3445273704492484769)
XLA Ops:
  0.0 2.9 %collective-permute-start.6 = (bf16[128,3072]{1,0:T(8,128)(2,1)}, bf16[128,3072]{1,0:T(8,128)(2,1)S(1)}, u32[]{:S(2)}, u32[]{:S(2)}) collective-permute-start(bf16[128,3072]{1,0:T(8,128)(2,1)} %refs_4_.1), channel_id=1, source_target_pairs={{0,2},{2,0},{1,3},{3,1},{4,6},{6,4},{5,7},{7,5},{8,10},{10,8},{9,1... | collective-permute-start | bytes 2359304 | tf_op jit(solution)/shard_map/item_rows/ppermute | solution.py:186
  2.9 1.6 %collective-permute-start = (s32[8]{0:T(128)}, s32[8]{0:T(128)S(1)}, u32[]{:S(2)}, u32[]{:S(2)}) collective-permute-start(s32[8]{0:T(128)} %refs_0_.1), channel_id=1, source_target_pairs={{0,4},{4,8},{8,12},{12,0},{1,5},{5,9},{9,13},{13,1},{2,6},{6,10},{... | collective-permute-start | bytes 104 | tf_op jit(solution)/shard_map/ids/ppermute | solution.py:186
  4.5 2.6 %collective-permute-start.1 = (s32[8]{0:T(128)}, s32[8]{0:T(128)S(1)}, u32[]{:S(2)}, u32[]{:S(2)}) collective-permute-start(s32[8]{0:T(128)} %refs_0_.1), channel_id=1, source_target_pairs={{0,8},{4,12},{8,0},{12,4},{1,9},{5,13},{9,1},{13,5},{2,10},{6,14},... | collective-permute-start | bytes 104 | tf_op jit(solution)/shard_map/ids/ppermute | solution.py:186
  7.1 1.3 %collective-permute-start.2 = (s32[8]{0:T(128)}, s32[8]{0:T(128)S(1)}, u32[]{:S(2)}, u32[]{:S(2)}) collective-permute-start(s32[8]{0:T(128)} %refs_0_.1), channel_id=1, source_target_pairs={{0,12},{4,0},{8,4},{12,8},{1,13},{5,1},{9,5},{13,9},{2,14},{6,2},{... | collective-permute-start | bytes 104 | tf_op jit(solution)/shard_map/ids/ppermute | solution.py:186
  8.5 2.2 %turn.1 = (f32[3072,128]{1,0:T(8,128)S(1)}, bf16[3072,128]{1,0:T(8,128)(2,1)S(1)}, bf16[64,64,256]{2,1,0:T(8,128)(2,1)S(1)}, bf16[128,3072]{1,0:T(8,128)(2,1)S(1...) custom-call(bf16[128,3072]{1,0:T(8,128)(2,1)} %refs_4_.1, bf16[64,64,256]{2,1,0:T(8,128)(2,1)} %bitcast.12, ...), custom_call_target="tpu_custom_call" | custom-call | flops 1610612736 | bytes 8388608 | tf_op jit(solution)/shard_map/turn/pallas_call | solution.py:214
  10.7 0.0 collective-permute-done.refs_1_
  10.7 0.0 collective-permute-done.1.refs_2_
  10.7 0.1 collective-permute-done.2.refs_3_
  10.8 0.4 %states.1.refs_8_.refs_0_ = bf16[16,3200]{1,0:T(8,128)(2,1)S(1)} custom-call(s32[1,8]{1,0:T(1,128)S(1)} %get-tuple-element.21.refs_0_, s32[1,8]{1,0:T(1,128)S(1)} %bitcast.9, s32[1,8]{1,0:T(1,128)S(1)} %bitcast.10, s32[1,8]{1,0:T(1,128)S(1)} %bitcast.11, bf16[16,128]{1,0:T(8,128)(2,1)S(1)} %get-tuple-element.22.refs_4_, ...), custom_call_target="tpu_custom_call" | custom-call | flops 12582912 | bytes 1048576 | tf_op jit(solution)/shard_map/states/pallas_call | solution.py:242
  11.2 0.6 %collective-permute-start.5 = (bf16[16,3200]{1,0:T(8,128)(2,1)S(1)}, bf16[16,3200]{1,0:T(8,128)(2,1)S(1)}, u32[]{:S(2)}, u32[]{:S(2)}) collective-permute-start(bf16[16,3200]{1,0:T(8,128)(2,1)S(1)} %states.1.refs_8_.refs_0_), channel_id=1, source_target_pairs={{0,4},{4,8},{8,12},{12,0},{1,5},{5,9},{9,13},{13,1},{2,6},{6,10},{... | collective-permute-start | bytes 307208 | tf_op jit(solution)/shard_map/states/ppermute | solution.py:186
  11.8 3.1 %collective-permute-start.4 = (bf16[16,3200]{1,0:T(8,128)(2,1)S(1)}, bf16[16,3200]{1,0:T(8,128)(2,1)S(1)}, u32[]{:S(2)}, u32[]{:S(2)}) collective-permute-start(bf16[16,3200]{1,0:T(8,128)(2,1)S(1)} %states.1.refs_8_.refs_0_), channel_id=1, source_target_pairs={{0,8},{4,12},{8,0},{12,4},{1,9},{5,13},{9,1},{13,5},{2,10},{6,14},... | collective-permute-start | bytes 307208 | tf_op jit(solution)/shard_map/states/ppermute | solution.py:186
  14.9 0.1 collective-permute-start.3
  15.1 0.0 copy-start
  15.1 5.2 %pairs.1 = (f32[1,128]{1,0:T(1,128)S(1)}, s32[4,128]{1,0:T(4,128)S(1)}) custom-call(s32[8]{0:T(128)} %refs_0_.1, s32[8]{0:T(128)S(1)} %collective-permute-done.refs_1_, s32[8]{0:T(128)S(1)} %collective-permute-done.1.refs_2_, s32[8]{0:T(128)S(1)} %collective-permute-done.2.refs_3_, s32[2,256]{1,0:T(2,128)} %bitcast.13, ...), custom_call_target="tpu_custom_call" | custom-call | flops 4294967296 | bytes 4194304 | tf_op jit(solution)/shard_map/pairs/pallas_call | solution.py:253
  20.2 0.6 %collective-permute-start.8 = (f32[1,128]{1,0:T(1,128)S(1)}, f32[1,128]{1,0:T(1,128)S(1)}, u32[]{:S(2)}, u32[]{:S(2)}) collective-permute-start(f32[1,128]{1,0:T(1,128)S(1)} %get-tuple-element.32.refs_7_), channel_id=1, source_target_pairs={{0,2},{1,3},{2,0},{3,1},{4,6},{5,7},{6,4},{7,5},{8,10},{9,11},{10,... | collective-permute-start | bytes 1544 | tf_op jit(solution)/shard_map/pairs/ppermute | solution.py:278
  20.9 0.0 collective-permute-done.5.refs_3_
  20.9 0.0 collective-permute-start.9
  20.9 0.1 collective-permute-done.4.refs_2_
  21.0 1.5 %collective-permute-start.7 = (f32[1,128]{1,0:T(1,128)S(1)}, f32[1,128]{1,0:T(1,128)S(1)}, u32[]{:S(2)}, u32[]{:S(2)}) collective-permute-start(f32[1,128]{1,0:T(1,128)S(1)} %get-tuple-element.32.refs_7_), channel_id=1, source_target_pairs={{0,1},{1,0},{2,3},{3,2},{4,5},{5,4},{6,7},{7,6},{8,9},{9,8},{10,11... | collective-permute-start | bytes 1544 | tf_op jit(solution)/shard_map/pairs/ppermute | solution.py:278
  22.5 1.4 %collective-permute-done.8.refs_9_ = f32[1,128]{1,0:T(1,128)S(1)} collective-permute-done((f32[1,128]{1,0:T(1,128)S(1)}, f32[1,128]{1,0:T(1,128)S(1)}, u32[]{:S(2)}, u32[]{:S(2)}) %collective-permute-start.8) | collective-permute-done | bytes 544 | tf_op jit(solution)/shard_map/pairs/ppermute | solution.py:278
  23.9 0.0 collective-permute-done.3.refs_1_
  23.9 0.0 collective-permute-done.9.refs_10_
  23.9 0.0 collective-permute-done.7.refs_8_
  23.9 0.0 collective-permute-done.6.refs_5_
  23.9 0.0 copy-done
  23.9 0.9 %scores.1 = (f32[1,128]{1,0:T(1,128)S(1)}, f32[1,128]{1,0:T(1,128)S(1)}, f32[1,128]{1,0:T(1,128)S(1)}, f32[1,128]{1,0:T(1,128)S(1)}) custom-call(bf16[16,3200]{1,0:T(8,128)(2,1)S(1)} %states.1.refs_8_.refs_0_, bf16[16,3200]{1,0:T(8,128)(2,1)S(1)} %collective-permute-done.3.refs_1_, bf16[16,3200]{1,0:T(8,128)(2,1)S(1)} %collective-permute-done.4.refs_2_, ...), custom_call_target="tpu_custom_call" | custom-call | flops 100663296 | bytes 2097152 | tf_op jit(solution)/shard_map/scores/pallas_call | solution.py:282
  24.8 2.0 %collective-permute-start.10 = (f32[1,128]{1,0:T(1,128)S(1)}, f32[1,128]{1,0:T(1,128)S(1)}, u32[]{:S(2)}, u32[]{:S(2)}) collective-permute-start(f32[1,128]{1,0:T(1,128)S(1)} %get-tuple-element.34), channel_id=1, source_target_pairs={{0,4},{4,8},{8,12},{12,0},{1,5},{5,9},{9,13},{13,1},{2,6},{6,10},{... | collective-permute-start | bytes 1544 | tf_op jit(solution)/shard_map/back/ppermute | solution.py:186
  26.7 0.2 collective-permute-start.11
  26.9 2.8 %collective-permute-start.12 = (f32[1,128]{1,0:T(1,128)S(1)}, f32[1,128]{1,0:T(1,128)S(1)}, u32[]{:S(2)}, u32[]{:S(2)}) collective-permute-start(f32[1,128]{1,0:T(1,128)S(1)} %get-tuple-element.36), channel_id=1, source_target_pairs={{0,12},{4,0},{8,4},{12,8},{1,13},{5,1},{9,5},{13,9},{2,14},{6,2},{... | collective-permute-start | bytes 1544 | tf_op jit(solution)/shard_map/back/ppermute | solution.py:186
  29.8 0.4 %collective-permute-done.10 = f32[1,128]{1,0:T(1,128)S(1)} collective-permute-done((f32[1,128]{1,0:T(1,128)S(1)}, f32[1,128]{1,0:T(1,128)S(1)}, u32[]{:S(2)}, u32[]{:S(2)}) %collective-permute-start.10) | collective-permute-done | bytes 544 | tf_op jit(solution)/shard_map/back/ppermute | solution.py:186
  30.2 1.0 %collective-permute-done.11 = f32[1,128]{1,0:T(1,128)S(1)} collective-permute-done((f32[1,128]{1,0:T(1,128)S(1)}, f32[1,128]{1,0:T(1,128)S(1)}, u32[]{:S(2)}, u32[]{:S(2)}) %collective-permute-start.11) | collective-permute-done | bytes 544 | tf_op jit(solution)/shard_map/back/ppermute | solution.py:186
  31.2 0.0 collective-permute-done.12
  31.2 0.5 %add_bitcast_fusion = f32[128]{0:T(128)} fusion(f32[1,128]{1,0:T(1,128)S(1)} %collective-permute-done.12, f32[1,128]{1,0:T(1,128)S(1)} %collective-permute-done.11, f32[1,128]{1,0:T(1,128)S(1)} %get-tuple-element.33, f32[1,128]{1,0:T(1,128)S(1)} %collective-permute-done.10), kind=kLoop, calls=%fused_computation | loop fusion | flops 384 | bytes 2560 | tf_op jit(solution)/shard_map/reshape | solution.py:300
Async XLA Ops:
  0.0 23.9 %collective-permute-start.6 = (bf16[128,3072]{1,0:T(8,128)(2,1)}, bf16[128,3072]{1,0:T(8,128)(2,1)S(1)}, u32[]{:S(2)}, u32[]{:S(2)}) collective-permute-start(bf16[128,3072]{1,0:T(8,128)(2,1)} %refs_4_.1), channel_id=1, source_target_pairs={{0,2},{2,0},{1,3},{3,1},{4,6},{6,4},{5,7},{7,5},{8,10},{10,8},{9,1... | collective-permute-start | bytes 2359304 | tf_op jit(solution)/shard_map/item_rows/ppermute | solution.py:186
  2.9 7.7 %collective-permute-start = (s32[8]{0:T(128)}, s32[8]{0:T(128)S(1)}, u32[]{:S(2)}, u32[]{:S(2)}) collective-permute-start(s32[8]{0:T(128)} %refs_0_.1), channel_id=1, source_target_pairs={{0,4},{4,8},{8,12},{12,0},{1,5},{5,9},{9,13},{13,1},{2,6},{6,10},{... | collective-permute-start | bytes 104 | tf_op jit(solution)/shard_map/ids/ppermute | solution.py:186
  4.5 6.2 %collective-permute-start.1 = (s32[8]{0:T(128)}, s32[8]{0:T(128)S(1)}, u32[]{:S(2)}, u32[]{:S(2)}) collective-permute-start(s32[8]{0:T(128)} %refs_0_.1), channel_id=1, source_target_pairs={{0,8},{4,12},{8,0},{12,4},{1,9},{5,13},{9,1},{13,5},{2,10},{6,14},... | collective-permute-start | bytes 104 | tf_op jit(solution)/shard_map/ids/ppermute | solution.py:186
  7.1 3.7 %collective-permute-start.2 = (s32[8]{0:T(128)}, s32[8]{0:T(128)S(1)}, u32[]{:S(2)}, u32[]{:S(2)}) collective-permute-start(s32[8]{0:T(128)} %refs_0_.1), channel_id=1, source_target_pairs={{0,12},{4,0},{8,4},{12,8},{1,13},{5,1},{9,5},{13,9},{2,14},{6,2},{... | collective-permute-start | bytes 104 | tf_op jit(solution)/shard_map/ids/ppermute | solution.py:186
  11.2 9.7 %collective-permute-start.5 = (bf16[16,3200]{1,0:T(8,128)(2,1)S(1)}, bf16[16,3200]{1,0:T(8,128)(2,1)S(1)}, u32[]{:S(2)}, u32[]{:S(2)}) collective-permute-start(bf16[16,3200]{1,0:T(8,128)(2,1)S(1)} %states.1.refs_8_.refs_0_), channel_id=1, source_target_pairs={{0,4},{4,8},{8,12},{12,0},{1,5},{5,9},{9,13},{13,1},{2,6},{6,10},{... | collective-permute-start | bytes 307208 | tf_op jit(solution)/shard_map/states/ppermute | solution.py:186
  11.8 9.2 %collective-permute-start.4 = (bf16[16,3200]{1,0:T(8,128)(2,1)S(1)}, bf16[16,3200]{1,0:T(8,128)(2,1)S(1)}, u32[]{:S(2)}, u32[]{:S(2)}) collective-permute-start(bf16[16,3200]{1,0:T(8,128)(2,1)S(1)} %states.1.refs_8_.refs_0_), channel_id=1, source_target_pairs={{0,8},{4,12},{8,0},{12,4},{1,9},{5,13},{9,1},{13,5},{2,10},{6,14},... | collective-permute-start | bytes 307208 | tf_op jit(solution)/shard_map/states/ppermute | solution.py:186
  14.9 8.9 %collective-permute-start.3 = (bf16[16,3200]{1,0:T(8,128)(2,1)S(1)}, bf16[16,3200]{1,0:T(8,128)(2,1)S(1)}, u32[]{:S(2)}, u32[]{:S(2)}) collective-permute-start(bf16[16,3200]{1,0:T(8,128)(2,1)S(1)} %states.1.refs_8_.refs_0_), channel_id=1, source_target_pairs={{0,12},{4,0},{8,4},{12,8},{1,13},{5,1},{9,5},{13,9},{2,14},{6,2},{... | collective-permute-start | bytes 307208 | tf_op jit(solution)/shard_map/states/ppermute | solution.py:186
  15.1 8.8 %copy-start = (bf16[128,3072]{1,0:T(8,128)(2,1)S(1)}, bf16[128,3072]{1,0:T(8,128)(2,1)}, u32[]{:S(2)}) copy-start(bf16[128,3072]{1,0:T(8,128)(2,1)} %refs_4_.1) | copy-start | bytes 2359300
  20.2 3.6 %collective-permute-start.8 = (f32[1,128]{1,0:T(1,128)S(1)}, f32[1,128]{1,0:T(1,128)S(1)}, u32[]{:S(2)}, u32[]{:S(2)}) collective-permute-start(f32[1,128]{1,0:T(1,128)S(1)} %get-tuple-element.32.refs_7_), channel_id=1, source_target_pairs={{0,2},{1,3},{2,0},{3,1},{4,6},{5,7},{6,4},{7,5},{8,10},{9,11},{10,... | collective-permute-start | bytes 1544 | tf_op jit(solution)/shard_map/pairs/ppermute | solution.py:278
  20.9 3.0 %collective-permute-start.9 = (f32[1,128]{1,0:T(1,128)S(1)}, f32[1,128]{1,0:T(1,128)S(1)}, u32[]{:S(2)}, u32[]{:S(2)}) collective-permute-start(f32[1,128]{1,0:T(1,128)S(1)} %get-tuple-element.32.refs_7_), channel_id=1, source_target_pairs={{0,3},{1,2},{2,1},{3,0},{4,7},{5,6},{6,5},{7,4},{8,11},{9,10},{10,... | collective-permute-start | bytes 1544 | tf_op jit(solution)/shard_map/pairs/ppermute | solution.py:278
  21.0 2.9 %collective-permute-start.7 = (f32[1,128]{1,0:T(1,128)S(1)}, f32[1,128]{1,0:T(1,128)S(1)}, u32[]{:S(2)}, u32[]{:S(2)}) collective-permute-start(f32[1,128]{1,0:T(1,128)S(1)} %get-tuple-element.32.refs_7_), channel_id=1, source_target_pairs={{0,1},{1,0},{2,3},{3,2},{4,5},{5,4},{6,7},{7,6},{8,9},{9,8},{10,11... | collective-permute-start | bytes 1544 | tf_op jit(solution)/shard_map/pairs/ppermute | solution.py:278
  24.8 5.4 %collective-permute-start.10 = (f32[1,128]{1,0:T(1,128)S(1)}, f32[1,128]{1,0:T(1,128)S(1)}, u32[]{:S(2)}, u32[]{:S(2)}) collective-permute-start(f32[1,128]{1,0:T(1,128)S(1)} %get-tuple-element.34), channel_id=1, source_target_pairs={{0,4},{4,8},{8,12},{12,0},{1,5},{5,9},{9,13},{13,1},{2,6},{6,10},{... | collective-permute-start | bytes 1544 | tf_op jit(solution)/shard_map/back/ppermute | solution.py:186
  26.7 4.4 %collective-permute-start.11 = (f32[1,128]{1,0:T(1,128)S(1)}, f32[1,128]{1,0:T(1,128)S(1)}, u32[]{:S(2)}, u32[]{:S(2)}) collective-permute-start(f32[1,128]{1,0:T(1,128)S(1)} %get-tuple-element.35), channel_id=1, source_target_pairs={{0,8},{4,12},{8,0},{12,4},{1,9},{5,13},{9,1},{13,5},{2,10},{6,14},... | collective-permute-start | bytes 1544 | tf_op jit(solution)/shard_map/back/ppermute | solution.py:186
  26.9 4.3 %collective-permute-start.12 = (f32[1,128]{1,0:T(1,128)S(1)}, f32[1,128]{1,0:T(1,128)S(1)}, u32[]{:S(2)}, u32[]{:S(2)}) collective-permute-start(f32[1,128]{1,0:T(1,128)S(1)} %get-tuple-element.36), channel_id=1, source_target_pairs={{0,12},{4,0},{8,4},{12,8},{1,13},{5,1},{9,5},{13,9},{2,14},{6,2},{... | collective-permute-start | bytes 1544 | tf_op jit(solution)/shard_map/back/ppermute | solution.py:186

commit v14 on v12

--- a/solution.py
+++ b/solution.py
@@ -145,40 +145,47 @@
     return high, middle, (rest - middle.astype(jnp.float32)).astype(jnp.bfloat16)
 
 
-def score_kernel(total, planes, parts, *refs):
+def linear_kernel(total, planes, *refs):
     states, refs = refs[:total], refs[total:]
-    items, refs = refs[:planes], refs[planes:]
-    places, pairs, refs = refs[0], refs[1:1 + planes * parts], refs[1 + planes * parts:]
-    outs, (wanted, cands, linear) = refs[:total], refs[total:]
+    items, (places, out, hits, wanted, linear) = refs[:planes], refs[planes:]
     slots = states[0].shape[0]
     own_rows, width = items[0].shape
+    half = out.shape[1]
     me = lax.axis_index("shard")
     plane = lax.axis_index("cache")
     count = total * slots
+    cands = []
     for j in range(total):
         wanted[j * slots:(j + 1) * slots, :] = states[j][:, :width]
         digits = states[j][:, width:].astype(jnp.float32)
         place = iota(digits.shape, 0)
         weight = jnp.where(place == 0, float(1 << CODE_BITS), jnp.where(place == 1, 1.0, 0.0))
-        cands[j:j + 1, :] = jnp.sum(digits * weight, axis=0, keepdims=True).astype(jnp.int32)
-    eye = iota((own_rows, own_rows), 0) == iota((own_rows, own_rows), 1)
-    ids, columns = [], []
-    for q in range(planes):
-        at = ring(plane - q, planes)
-        scores = dot(items[q][...], wanted[...], NT)
-        for t, part in enumerate(thirds(scores)):
+        cands.append(jnp.sum(digits * weight, axis=0, keepdims=True).astype(jnp.int32))
+
+    for q, rows in enumerate(items):
+        for t, part in enumerate(thirds(dot(rows[...], wanted[...], NT))):
             linear[q * own_rows:(q + 1) * own_rows, t * count:(t + 1) * count] = part
-        row = sum(pairs[q * parts + h][...] for h in range(parts))
-        columns.append(jnp.sum(jnp.where(eye, row, 0.0), axis=1, keepdims=True))
-        ids.append(iota((own_rows, 1), 0) + (me * planes + at) * own_rows)
-    pair_column = jnp.concatenate(columns, axis=0)
+    ids = [iota((own_rows, 1), 0) + (me * planes + ring(plane - q, planes)) * own_rows for q in range(planes)]
     item_ids = jnp.concatenate(ids, axis=0)
     for j in range(total):
-        half = outs[j].shape[1]
         spread = (iota((count, half), 0) == places[j:j + 1, :]).astype(jnp.float32).astype(jnp.bfloat16)
-        scores = dot(linear[...], jnp.concatenate([spread] * 3, axis=0), NN) + pair_column
-        hit = item_ids == cands[j:j + 1, :]
-        outs[j][...] = jnp.sum(jnp.where(hit, scores, 0.0), axis=0, keepdims=True)
+        scores = dot(linear[...], jnp.concatenate([spread] * 3, axis=0), NN)
+        hit = item_ids == cands[j]
+        out[j:j + 1, :] = jnp.sum(jnp.where(hit, scores, 0.0), axis=0, keepdims=True)
+        hits[:, j * half:(j + 1) * half] = hit.astype(jnp.float32).astype(jnp.bfloat16)
+
+
+def score_kernel(total, planes, parts, *refs):
+    pairs, (linear, hits), outs = refs[:planes * parts], refs[planes * parts:planes * parts + 2], refs[planes * parts + 2:]
+    half = linear.shape[1]
+    sums = [sum(pairs[q * parts + h][...] for h in range(parts)) for q in range(planes)]
+    row = jnp.concatenate(sums, axis=1)
+    pieces = jnp.zeros((16, row.shape[1]), jnp.float32)
+    for t, part in enumerate(thirds(row)):
+        pieces = jnp.where(iota(pieces.shape, 0) == t, part.astype(jnp.float32), pieces)
+    added = jnp.sum(dot(pieces.astype(jnp.bfloat16), hits[...], NN), axis=0, keepdims=True)
+    for j in range(total):
+        outs[j][...] = linear[j:j + 1, :] + added[:, j * half:(j + 1) * half]
 
 
 def shift(x, axis, step):
@@ -268,34 +275,45 @@
             cost_estimate=pl.CostEstimate(flops=2 * count * K * K * rows * 16, bytes_accessed=4 * 1024 * 1024, transcendentals=0),
         )(*users, in_hbm(pair_fields.T), *turned, picked)
         pair_scores = {(0, 0): pair_parts}
-        for q, h in [(q, h) for q in range(planes - 1, -1, -1) for h in range(parts) if q or h]:
+        steps = [(q, h) for q in range(planes - 1, -1, -1) for h in range(parts) if q or h]
+        for q, h in sorted(steps, key=lambda step: bool(step[0] and step[1])):
             perm = [
                 (c * parts + d, (c + q) % planes * parts + (d + h) % parts) for c in range(planes) for d in range(parts)
             ]
-            source, after = pair_parts, {1: 3, 2: 2}.get(len(pair_scores) - 1, 0)
+            source, after = pair_parts, {1: 2, 2: 1}.get(len(pair_scores) - 1, 0)
             if after:
                 source, states[after] = lax.optimization_barrier((pair_parts, states[after]))
             pair_scores[q, h] = lax.ppermute(source, ("cache", "pair"), perm)
         pair_scores = [pair_scores[q, h] for q in range(planes) for h in range(parts)]
 
     with jax.named_scope("scores"):
+        linear, hits = pl.pallas_call(
+            functools.partial(linear_kernel, total, planes),
+            out_shape=(
+                jax.ShapeDtypeStruct((total, half), jnp.float32),
+                jax.ShapeDtypeStruct((planes * rows, total * half), jnp.bfloat16),
+            ),
+            in_specs=[vmem] * (total + len(items) + 1),
+            out_specs=(vmem, vmem),
+            scratch_shapes=[
+                pltpu.VMEM((total * slots, width), jnp.bfloat16),
+                pltpu.VMEM((planes * rows, 3 * total * slots), jnp.bfloat16),
+            ],
+            compiler_params=params,
+            cost_estimate=pl.CostEstimate(flops=2 * 64 * 256 * width, bytes_accessed=2 * 1024 * 1024, transcendentals=0),
+        )(*states, *items, places)
         outs = pl.pallas_call(
             functools.partial(score_kernel, total, planes, parts),
             out_shape=[jax.ShapeDtypeStruct((1, half), jnp.float32)] * total,
-            in_specs=[vmem] * (total + planes + 1 + planes * parts),
+            in_specs=[vmem] * (planes * parts + 2),
             out_specs=[vmem] * total,
-            scratch_shapes=[
-                pltpu.VMEM((total * slots, width), jnp.bfloat16),
-                pltpu.VMEM((-(-total // 8) * 8, half), jnp.int32),
-                pltpu.VMEM((planes * rows, 3 * total * slots), jnp.bfloat16),
-            ],
-            compiler_params=params,
-            cost_estimate=pl.CostEstimate(flops=2 * 64 * 256 * width, bytes_accessed=2 * 1024 * 1024, transcendentals=0),
-        )(*states, *items, places, *pair_scores)
+            compiler_params=params,
+            cost_estimate=pl.CostEstimate(flops=2 * 16 * 256 * 512, bytes_accessed=512 * 1024, transcendentals=0),
+        )(*pair_scores, linear, hits)
 
     with jax.named_scope("back"):
         result = outs[0]
-        for j in range(total - 1, 0, -1):
+        for j in range(1, total):
             result = result + shift(outs[j], "shard", -j)
     return result.reshape(half)
 

time: 32.8 us -> 31.6 us (0.963)
  waiting for transfers between devices: 4.92 us -> 2.7 us
  starting transfers between devices: 18.4 us -> 19.3 us
    ppermute x3, starting transfers between devices: 0.81 us -> 2.2 us  [body(): pair_scores[q, h] = lax.ppermute(source, ('cache', 'pair'), perm)]
    ppermute x10, waiting for transfers between devices: 3.52 us -> 2.19 us  [shift(): return lax.ppermute(x, axis, [(s, (s + step) % size) for s in range(size)])]
    pallas_call x0 -> x1, Pallas kernels: none -> 0.9 us  [body(): pl.pallas_call(functools.partial(linear_kernel, total, planes), out_shape...]
    ppermute x3, waiting for transfers between devices: 1.4 us -> 0.51 us  [body(): pair_scores[q, h] = lax.ppermute(source, ('cache', 'pair'), perm)]
    pallas_call x1, Pallas kernels: 0.89 us -> 0.15 us  [body(): pl.pallas_call(functools.partial(score_kernel, total, planes, parts), out...]
    ppermute x10, starting transfers between devices: 17.6 us -> 17.1 us  [shift(): return lax.ppermute(x, axis, [(s, (s + step) % size) for s in range(size)])]
  transfers between devices with their start and end apart: 13 -> 13, of which waited for: 5 -> 5; matrix products, arithmetic and copies ran while one was open for 0% -> 0% of each run, Pallas kernels for 24% -> 28%
where the time goes in v14:
time: 31.6 us; the launch traced here: 31.4 us
  starting transfers between devices  19.3 us (61%)
  Pallas kernels  8.84 us (28%)
  waiting for transfers between devices  2.7 us (9%)
  other arithmetic  0.52 us (2%)
    ppermute x10, starting transfers between devices, shift(): return lax.ppermute(x, axis, [(s, (s + step) % size) for s in range(size)])  17.1 us
    pallas_call x1, Pallas kernels, body(): pl.pallas_call(functools.partial(pair_kernel, total, cap, slots, user_sta...  5.18 us
    ppermute x3, starting transfers between devices, body(): pair_scores[q, h] = lax.ppermute(source, ('cache', 'pair'), perm)  2.2 us
    pallas_call x1, Pallas kernels, body(): pl.pallas_call(turn_kernel, out_shape=(jax.ShapeDtypeStruct((width, rows)...  2.2 us
    ppermute x10, waiting for transfers between devices, shift(): return lax.ppermute(x, axis, [(s, (s + step) % size) for s in range(size)])  2.19 us
    pallas_call x1, Pallas kernels, body(): pl.pallas_call(functools.partial(linear_kernel, total, planes), out_shape...  0.9 us
  transfers between devices with their start and end apart: 13, of which 5 were waited for; matrix products, arithmetic and copies ran while one was open for 0% of the time, Pallas kernels for 28%

profile of v14, /device:TPU:0, one launch (start us, length us, event | category | flops | bytes accessed | tf_op | source)
XLA Modules:
  0.0 31.4 jit_solution(13738435114455509081)
XLA Ops:
  0.0 2.9 %collective-permute-start.9 = (bf16[128,3072]{1,0:T(8,128)(2,1)}, bf16[128,3072]{1,0:T(8,128)(2,1)S(1)}, u32[]{:S(2)}, u32[]{:S(2)}) collective-permute-start(bf16[128,3072]{1,0:T(8,128)(2,1)} %refs_4_.1), channel_id=1, source_target_pairs={{0,2},{2,0},{1,3},{3,1},{4,6},{6,4},{5,7},{7,5},{8,10},{10,8},{9,1... | collective-permute-start | bytes 2359304 | tf_op jit(solution)/shard_map/item_rows/ppermute | solution.py:193
  2.9 1.6 %collective-permute-start = (s32[8]{0:T(128)}, s32[8]{0:T(128)S(1)}, u32[]{:S(2)}, u32[]{:S(2)}) collective-permute-start(s32[8]{0:T(128)} %refs_0_.1), channel_id=1, source_target_pairs={{0,4},{4,8},{8,12},{12,0},{1,5},{5,9},{9,13},{13,1},{2,6},{6,10},{... | collective-permute-start | bytes 104 | tf_op jit(solution)/shard_map/ids/ppermute | solution.py:193
  4.5 2.6 %collective-permute-start.1 = (s32[8]{0:T(128)}, s32[8]{0:T(128)S(1)}, u32[]{:S(2)}, u32[]{:S(2)}) collective-permute-start(s32[8]{0:T(128)} %refs_0_.1), channel_id=1, source_target_pairs={{0,8},{4,12},{8,0},{12,4},{1,9},{5,13},{9,1},{13,5},{2,10},{6,14},... | collective-permute-start | bytes 104 | tf_op jit(solution)/shard_map/ids/ppermute | solution.py:193
  7.1 1.3 %collective-permute-start.2 = (s32[8]{0:T(128)}, s32[8]{0:T(128)S(1)}, u32[]{:S(2)}, u32[]{:S(2)}) collective-permute-start(s32[8]{0:T(128)} %refs_0_.1), channel_id=1, source_target_pairs={{0,12},{4,0},{8,4},{12,8},{1,13},{5,1},{9,5},{13,9},{2,14},{6,2},{... | collective-permute-start | bytes 104 | tf_op jit(solution)/shard_map/ids/ppermute | solution.py:193
  8.5 2.2 %turn.1 = (f32[3072,128]{1,0:T(8,128)S(1)}, bf16[3072,128]{1,0:T(8,128)(2,1)S(1)}, bf16[64,64,256]{2,1,0:T(8,128)(2,1)S(1)}, bf16[128,3072]{1,0:T(8,128)(2,1)S(1...) custom-call(bf16[128,3072]{1,0:T(8,128)(2,1)} %refs_4_.1, bf16[64,64,256]{2,1,0:T(8,128)(2,1)} %bitcast.12, ...), custom_call_target="tpu_custom_call" | custom-call | flops 1610612736 | bytes 8388608 | tf_op jit(solution)/shard_map/turn/pallas_call | solution.py:221
  10.7 0.0 collective-permute-done.refs_1_
  10.7 0.0 collective-permute-done.1.refs_2_
  10.7 0.1 collective-permute-done.2.refs_3_
  10.8 0.4 %states.1.refs_8_.refs_0_ = bf16[16,3200]{1,0:T(8,128)(2,1)S(1)} custom-call(s32[1,8]{1,0:T(1,128)S(1)} %get-tuple-element.26.refs_0_, s32[1,8]{1,0:T(1,128)S(1)} %bitcast.9, s32[1,8]{1,0:T(1,128)S(1)} %bitcast.10, s32[1,8]{1,0:T(1,128)S(1)} %bitcast.11, bf16[16,128]{1,0:T(8,128)(2,1)S(1)} %get-tuple-element.27.refs_4_, ...), custom_call_target="tpu_custom_call" | custom-call | flops 12582912 | bytes 1048576 | tf_op jit(solution)/shard_map/states/pallas_call | solution.py:249
  11.2 1.0 %collective-permute-start.3 = (bf16[16,3200]{1,0:T(8,128)(2,1)S(1)}, bf16[16,3200]{1,0:T(8,128)(2,1)S(1)}, u32[]{:S(2)}, u32[]{:S(2)}) collective-permute-start(bf16[16,3200]{1,0:T(8,128)(2,1)S(1)} %states.1.refs_8_.refs_0_), channel_id=1, source_target_pairs={{0,8},{4,12},{8,0},{12,4},{1,9},{5,13},{9,1},{13,5},{2,10},{6,14},... | collective-permute-start | bytes 307208 | tf_op jit(solution)/shard_map/states/ppermute | solution.py:193
  12.1 2.8 %collective-permute-start.6 = (bf16[16,3200]{1,0:T(8,128)(2,1)S(1)}, bf16[16,3200]{1,0:T(8,128)(2,1)S(1)}, u32[]{:S(2)}, u32[]{:S(2)}) collective-permute-start(bf16[16,3200]{1,0:T(8,128)(2,1)S(1)} %states.1.refs_8_.refs_0_), channel_id=1, source_target_pairs={{0,4},{4,8},{8,12},{12,0},{1,5},{5,9},{9,13},{13,1},{2,6},{6,10},{... | collective-permute-start | bytes 307208 | tf_op jit(solution)/shard_map/states/ppermute | solution.py:193
  14.9 1.0 %collective-permute-start.8 = (bf16[16,3200]{1,0:T(8,128)(2,1)S(1)}, bf16[16,3200]{1,0:T(8,128)(2,1)S(1)}, u32[]{:S(2)}, u32[]{:S(2)}) collective-permute-start(bf16[16,3200]{1,0:T(8,128)(2,1)S(1)} %states.1.refs_8_.refs_0_), channel_id=1, source_target_pairs={{0,12},{4,0},{8,4},{12,8},{1,13},{5,1},{9,5},{13,9},{2,14},{6,2},{... | collective-permute-start | bytes 307208 | tf_op jit(solution)/shard_map/states/ppermute | solution.py:193
  16.0 0.0 copy-start
  16.0 5.2 %pairs.1 = (f32[1,128]{1,0:T(1,128)S(1)}, s32[4,128]{1,0:T(4,128)S(1)}) custom-call(s32[8]{0:T(128)} %refs_0_.1, s32[8]{0:T(128)S(1)} %collective-permute-done.refs_1_, s32[8]{0:T(128)S(1)} %collective-permute-done.1.refs_2_, s32[8]{0:T(128)S(1)} %collective-permute-done.2.refs_3_, s32[2,256]{1,0:T(2,128)} %bitcast.13, ...), custom_call_target="tpu_custom_call" | custom-call | flops 4294967296 | bytes 4194304 | tf_op jit(solution)/shard_map/pairs/pallas_call | solution.py:260
  21.2 0.6 %collective-permute-start.5 = (f32[1,128]{1,0:T(1,128)S(1)}, f32[1,128]{1,0:T(1,128)S(1)}, u32[]{:S(2)}, u32[]{:S(2)}) collective-permute-start(f32[1,128]{1,0:T(1,128)S(1)} %get-tuple-element.31.refs_0_), channel_id=1, source_target_pairs={{0,2},{1,3},{2,0},{3,1},{4,6},{5,7},{6,4},{7,5},{8,10},{9,11},{10,... | collective-permute-start | bytes 1544 | tf_op jit(solution)/shard_map/pairs/ppermute | solution.py:286
  21.8 0.0 collective-permute-done.3.refs_2_
  21.8 0.0 collective-permute-start.4
  21.8 0.0 collective-permute-done.6.refs_1_
  21.8 1.6 %collective-permute-start.7 = (f32[1,128]{1,0:T(1,128)S(1)}, f32[1,128]{1,0:T(1,128)S(1)}, u32[]{:S(2)}, u32[]{:S(2)}) collective-permute-start(f32[1,128]{1,0:T(1,128)S(1)} %get-tuple-element.31.refs_0_), channel_id=1, source_target_pairs={{0,3},{1,2},{2,1},{3,0},{4,7},{5,6},{6,5},{7,4},{8,11},{9,10},{10,... | collective-permute-start | bytes 1544 | tf_op jit(solution)/shard_map/pairs/ppermute | solution.py:286
  23.4 0.0 collective-permute-done.8.refs_3_
  23.4 0.0 collective-permute-done.9.refs_5_
  23.4 0.0 copy-done
  23.4 0.9 %scores.2 = (f32[4,128]{1,0:T(4,128)S(1)}, bf16[256,512]{1,0:T(8,128)(2,1)S(1)}) custom-call(bf16[16,3200]{1,0:T(8,128)(2,1)S(1)} %states.1.refs_8_.refs_0_, bf16[16,3200]{1,0:T(8,128)(2,1)S(1)} %collective-permute-done.6.refs_1_, bf16[16,3200]{1,0:T(8,128)(2,1)S(1)} %collective-permute-done.3.refs_2_, bf16[16,3200]{1,0:T(8,128)(2,1)S(1)} %collective-permute-done.8.refs_3_, ...), custom_call_target="tpu_custom_call" | custom-call | flops 100663296 | bytes 2097152 | tf_op jit(solution)/shard_map/scores/pallas_call | solution.py:290
  24.3 0.5 %collective-permute-done.5.refs_2_ = f32[1,128]{1,0:T(1,128)S(1)} collective-permute-done((f32[1,128]{1,0:T(1,128)S(1)}, f32[1,128]{1,0:T(1,128)S(1)}, u32[]{:S(2)}, u32[]{:S(2)}) %collective-permute-start.5) | collective-permute-done | bytes 544 | tf_op jit(solution)/shard_map/pairs/ppermute | solution.py:286
  24.8 0.0 collective-permute-done.4.refs_1_
  24.8 0.0 collective-permute-done.7.refs_3_
  24.8 0.2 scores.3
  25.0 1.1 %collective-permute-start.12 = (f32[1,128]{1,0:T(1,128)S(1)}, f32[1,128]{1,0:T(1,128)S(1)}, u32[]{:S(2)}, u32[]{:S(2)}) collective-permute-start(f32[1,128]{1,0:T(1,128)S(1)} %get-tuple-element.40), channel_id=1, source_target_pairs={{0,4},{4,8},{8,12},{12,0},{1,5},{5,9},{9,13},{13,1},{2,6},{6,10},{... | collective-permute-start | bytes 1544 | tf_op jit(solution)/shard_map/back/ppermute | solution.py:193
  26.0 0.2 collective-permute-start.11
  26.2 2.6 %collective-permute-start.10 = (f32[1,128]{1,0:T(1,128)S(1)}, f32[1,128]{1,0:T(1,128)S(1)}, u32[]{:S(2)}, u32[]{:S(2)}) collective-permute-start(f32[1,128]{1,0:T(1,128)S(1)} %get-tuple-element.38), channel_id=1, source_target_pairs={{0,12},{4,0},{8,4},{12,8},{1,13},{5,1},{9,5},{13,9},{2,14},{6,2},{... | collective-permute-start | bytes 1544 | tf_op jit(solution)/shard_map/back/ppermute | solution.py:193
  28.8 1.5 %collective-permute-done.12 = f32[1,128]{1,0:T(1,128)S(1)} collective-permute-done((f32[1,128]{1,0:T(1,128)S(1)}, f32[1,128]{1,0:T(1,128)S(1)}, u32[]{:S(2)}, u32[]{:S(2)}) %collective-permute-start.12) | collective-permute-done | bytes 544 | tf_op jit(solution)/shard_map/back/ppermute | solution.py:193
  30.4 0.1 collective-permute-done.11
  30.5 0.4 %collective-permute-done.10 = f32[1,128]{1,0:T(1,128)S(1)} collective-permute-done((f32[1,128]{1,0:T(1,128)S(1)}, f32[1,128]{1,0:T(1,128)S(1)}, u32[]{:S(2)}, u32[]{:S(2)}) %collective-permute-start.10) | collective-permute-done | bytes 544 | tf_op jit(solution)/shard_map/back/ppermute | solution.py:193
  30.9 0.5 %add_bitcast_fusion = f32[128]{0:T(128)} fusion(f32[1,128]{1,0:T(1,128)S(1)} %collective-permute-done.12, f32[1,128]{1,0:T(1,128)S(1)} %collective-permute-done.11, f32[1,128]{1,0:T(1,128)S(1)} %get-tuple-element.37, f32[1,128]{1,0:T(1,128)S(1)} %collective-permute-done.10), kind=kLoop, calls=%fused_computation | loop fusion | flops 384 | bytes 2560 | tf_op jit(solution)/shard_map/reshape | solution.py:318
Async XLA Ops:
  0.0 23.4 %collective-permute-start.9 = (bf16[128,3072]{1,0:T(8,128)(2,1)}, bf16[128,3072]{1,0:T(8,128)(2,1)S(1)}, u32[]{:S(2)}, u32[]{:S(2)}) collective-permute-start(bf16[128,3072]{1,0:T(8,128)(2,1)} %refs_4_.1), channel_id=1, source_target_pairs={{0,2},{2,0},{1,3},{3,1},{4,6},{6,4},{5,7},{7,5},{8,10},{10,8},{9,1... | collective-permute-start | bytes 2359304 | tf_op jit(solution)/shard_map/item_rows/ppermute | solution.py:193
  2.9 7.7 %collective-permute-start = (s32[8]{0:T(128)}, s32[8]{0:T(128)S(1)}, u32[]{:S(2)}, u32[]{:S(2)}) collective-permute-start(s32[8]{0:T(128)} %refs_0_.1), channel_id=1, source_target_pairs={{0,4},{4,8},{8,12},{12,0},{1,5},{5,9},{9,13},{13,1},{2,6},{6,10},{... | collective-permute-start | bytes 104 | tf_op jit(solution)/shard_map/ids/ppermute | solution.py:193
  4.5 6.2 %collective-permute-start.1 = (s32[8]{0:T(128)}, s32[8]{0:T(128)S(1)}, u32[]{:S(2)}, u32[]{:S(2)}) collective-permute-start(s32[8]{0:T(128)} %refs_0_.1), channel_id=1, source_target_pairs={{0,8},{4,12},{8,0},{12,4},{1,9},{5,13},{9,1},{13,5},{2,10},{6,14},... | collective-permute-start | bytes 104 | tf_op jit(solution)/shard_map/ids/ppermute | solution.py:193
  7.1 3.7 %collective-permute-start.2 = (s32[8]{0:T(128)}, s32[8]{0:T(128)S(1)}, u32[]{:S(2)}, u32[]{:S(2)}) collective-permute-start(s32[8]{0:T(128)} %refs_0_.1), channel_id=1, source_target_pairs={{0,12},{4,0},{8,4},{12,8},{1,13},{5,1},{9,5},{13,9},{2,14},{6,2},{... | collective-permute-start | bytes 104 | tf_op jit(solution)/shard_map/ids/ppermute | solution.py:193
  11.2 10.6 %collective-permute-start.3 = (bf16[16,3200]{1,0:T(8,128)(2,1)S(1)}, bf16[16,3200]{1,0:T(8,128)(2,1)S(1)}, u32[]{:S(2)}, u32[]{:S(2)}) collective-permute-start(bf16[16,3200]{1,0:T(8,128)(2,1)S(1)} %states.1.refs_8_.refs_0_), channel_id=1, source_target_pairs={{0,8},{4,12},{8,0},{12,4},{1,9},{5,13},{9,1},{13,5},{2,10},{6,14},... | collective-permute-start | bytes 307208 | tf_op jit(solution)/shard_map/states/ppermute | solution.py:193
  12.1 9.6 %collective-permute-start.6 = (bf16[16,3200]{1,0:T(8,128)(2,1)S(1)}, bf16[16,3200]{1,0:T(8,128)(2,1)S(1)}, u32[]{:S(2)}, u32[]{:S(2)}) collective-permute-start(bf16[16,3200]{1,0:T(8,128)(2,1)S(1)} %states.1.refs_8_.refs_0_), channel_id=1, source_target_pairs={{0,4},{4,8},{8,12},{12,0},{1,5},{5,9},{9,13},{13,1},{2,6},{6,10},{... | collective-permute-start | bytes 307208 | tf_op jit(solution)/shard_map/states/ppermute | solution.py:193
  14.9 8.4 %collective-permute-start.8 = (bf16[16,3200]{1,0:T(8,128)(2,1)S(1)}, bf16[16,3200]{1,0:T(8,128)(2,1)S(1)}, u32[]{:S(2)}, u32[]{:S(2)}) collective-permute-start(bf16[16,3200]{1,0:T(8,128)(2,1)S(1)} %states.1.refs_8_.refs_0_), channel_id=1, source_target_pairs={{0,12},{4,0},{8,4},{12,8},{1,13},{5,1},{9,5},{13,9},{2,14},{6,2},{... | collective-permute-start | bytes 307208 | tf_op jit(solution)/shard_map/states/ppermute | solution.py:193
  16.0 7.4 %copy-start = (bf16[128,3072]{1,0:T(8,128)(2,1)S(1)}, bf16[128,3072]{1,0:T(8,128)(2,1)}, u32[]{:S(2)}) copy-start(bf16[128,3072]{1,0:T(8,128)(2,1)} %refs_4_.1) | copy-start | bytes 2359300
  21.2 3.6 %collective-permute-start.5 = (f32[1,128]{1,0:T(1,128)S(1)}, f32[1,128]{1,0:T(1,128)S(1)}, u32[]{:S(2)}, u32[]{:S(2)}) collective-permute-start(f32[1,128]{1,0:T(1,128)S(1)} %get-tuple-element.31.refs_0_), channel_id=1, source_target_pairs={{0,2},{1,3},{2,0},{3,1},{4,6},{5,7},{6,4},{7,5},{8,10},{9,11},{10,... | collective-permute-start | bytes 1544 | tf_op jit(solution)/shard_map/pairs/ppermute | solution.py:286
  21.8 3.0 %collective-permute-start.4 = (f32[1,128]{1,0:T(1,128)S(1)}, f32[1,128]{1,0:T(1,128)S(1)}, u32[]{:S(2)}, u32[]{:S(2)}) collective-permute-start(f32[1,128]{1,0:T(1,128)S(1)} %get-tuple-element.31.refs_0_), channel_id=1, source_target_pairs={{0,1},{1,0},{2,3},{3,2},{4,5},{5,4},{6,7},{7,6},{8,9},{9,8},{10,11... | collective-permute-start | bytes 1544 | tf_op jit(solution)/shard_map/pairs/ppermute | solution.py:286
  21.8 3.0 %collective-permute-start.7 = (f32[1,128]{1,0:T(1,128)S(1)}, f32[1,128]{1,0:T(1,128)S(1)}, u32[]{:S(2)}, u32[]{:S(2)}) collective-permute-start(f32[1,128]{1,0:T(1,128)S(1)} %get-tuple-element.31.refs_0_), channel_id=1, source_target_pairs={{0,3},{1,2},{2,1},{3,0},{4,7},{5,6},{6,5},{7,4},{8,11},{9,10},{10,... | collective-permute-start | bytes 1544 | tf_op jit(solution)/shard_map/pairs/ppermute | solution.py:286
  25.0 5.4 %collective-permute-start.12 = (f32[1,128]{1,0:T(1,128)S(1)}, f32[1,128]{1,0:T(1,128)S(1)}, u32[]{:S(2)}, u32[]{:S(2)}) collective-permute-start(f32[1,128]{1,0:T(1,128)S(1)} %get-tuple-element.40), channel_id=1, source_target_pairs={{0,4},{4,8},{8,12},{12,0},{1,5},{5,9},{9,13},{13,1},{2,6},{6,10},{... | collective-permute-start | bytes 1544 | tf_op jit(solution)/shard_map/back/ppermute | solution.py:193
  26.0 4.4 %collective-permute-start.11 = (f32[1,128]{1,0:T(1,128)S(1)}, f32[1,128]{1,0:T(1,128)S(1)}, u32[]{:S(2)}, u32[]{:S(2)}) collective-permute-start(f32[1,128]{1,0:T(1,128)S(1)} %get-tuple-element.39), channel_id=1, source_target_pairs={{0,8},{4,12},{8,0},{12,4},{1,9},{5,13},{9,1},{13,5},{2,10},{6,14},... | collective-permute-start | bytes 1544 | tf_op jit(solution)/shard_map/back/ppermute | solution.py:193
  26.2 4.7 %collective-permute-start.10 = (f32[1,128]{1,0:T(1,128)S(1)}, f32[1,128]{1,0:T(1,128)S(1)}, u32[]{:S(2)}, u32[]{:S(2)}) collective-permute-start(f32[1,128]{1,0:T(1,128)S(1)} %get-tuple-element.38), channel_id=1, source_target_pairs={{0,12},{4,0},{8,4},{12,8},{1,13},{5,1},{9,5},{13,9},{2,14},{6,2},{... | collective-permute-start | bytes 1544 | tf_op jit(solution)/shard_map/back/ppermute | solution.py:193

commit v15 on v14

--- a/solution.py
+++ b/solution.py
@@ -145,14 +145,17 @@
     return high, middle, (rest - middle.astype(jnp.float32)).astype(jnp.bfloat16)
 
 
-def linear_kernel(total, planes, *refs):
+def linear_kernel(total, planes, parts, *refs):
     states, refs = refs[:total], refs[total:]
-    items, (places, out, hits, wanted, linear) = refs[:planes], refs[planes:]
+    own_items, refs = refs[0], refs[1:]
+    crossed, refs = refs[:(planes - 1) * parts], refs[(planes - 1) * parts:]
+    places, out, hits, wanted, linear = refs
     slots = states[0].shape[0]
-    own_rows, width = items[0].shape
+    own_rows, width = own_items.shape
     half = out.shape[1]
     me = lax.axis_index("shard")
     plane = lax.axis_index("cache")
+    core = lax.axis_index("pair")
     count = total * slots
     cands = []
     for j in range(total):
@@ -162,9 +165,17 @@
         weight = jnp.where(place == 0, float(1 << CODE_BITS), jnp.where(place == 1, 1.0, 0.0))
         cands.append(jnp.sum(digits * weight, axis=0, keepdims=True).astype(jnp.int32))
 
-    for q, rows in enumerate(items):
+    def fill(q, rows):
         for t, part in enumerate(thirds(dot(rows[...], wanted[...], NT))):
             linear[q * own_rows:(q + 1) * own_rows, t * count:(t + 1) * count] = part
+
+    fill(0, own_items)
+    for h in range(parts):
+        @pl.when(core == h)
+        def _():
+            for q in range(1, planes):
+                fill(q, crossed[(q - 1) * parts + h])
+
     ids = [iota((own_rows, 1), 0) + (me * planes + ring(plane - q, planes)) * own_rows for q in range(planes)]
     item_ids = jnp.concatenate(ids, axis=0)
     for j in range(total):
@@ -212,7 +223,10 @@
         return pltpu.with_memory_space_constraint(x, pltpu.HBM)
 
     with jax.named_scope("item_rows"):
-        items = [item_table] + [shift(item_table, "cache", q) for q in range(1, planes)]
+        items = [item_table]
+        for q in range(1, planes):
+            perm = [(c * parts, (c + q) % planes * parts) for c in range(planes)]
+            items.append(lax.ppermute(item_table, ("cache", "pair"), perm))
 
     with jax.named_scope("ids"):
         users = [in_hbm(reader_users)] + [shift(reader_users, "shard", j) for j in range(1, total)]
@@ -255,6 +269,10 @@
             cost_estimate=pl.CostEstimate(flops=2 * slots * rows * width, bytes_accessed=1024 * 1024, transcendentals=0),
         )(own_ids, *[ids.reshape(1, readers) for ids in users[1:]], digits, states_near)
         states = [picked] + [shift(picked, "shard", j) for j in range(1, total)]
+        crossed, items = items[1:], items[:1]
+        for rows_in in crossed:
+            rows_in, _ = lax.optimization_barrier((rows_in, picked))
+            items += [rows_in] + [lax.ppermute(rows_in, "pair", [(0, h)]) for h in range(1, parts)]
 
     with jax.named_scope("pairs"):
         pair_parts, places = pl.pallas_call(
@@ -280,7 +298,7 @@
             perm = [
                 (c * parts + d, (c + q) % planes * parts + (d + h) % parts) for c in range(planes) for d in range(parts)
             ]
-            source, after = pair_parts, {1: 2, 2: 1}.get(len(pair_scores) - 1, 0)
+            source, after = pair_parts, {1: 1, 2: 2}.get(len(pair_scores) - 1, 0)
             if after:
                 source, states[after] = lax.optimization_barrier((pair_parts, states[after]))
             pair_scores[q, h] = lax.ppermute(source, ("cache", "pair"), perm)
@@ -288,7 +306,7 @@
 
     with jax.named_scope("scores"):
         linear, hits = pl.pallas_call(
-            functools.partial(linear_kernel, total, planes),
+            functools.partial(linear_kernel, total, planes, parts),
             out_shape=(
                 jax.ShapeDtypeStruct((total, half), jnp.float32),
                 jax.ShapeDtypeStruct((planes * rows, total * half), jnp.bfloat16),

time: 31.6 us -> 39.1 us (1.24)
  starting transfers between devices: 19.3 us -> 23.9 us
  waiting for transfers between devices: 2.7 us -> 5.29 us
    ppermute x0 -> x2, starting transfers between devices: none -> 6.16 us  [the longest x1 4.84 us: body(): items.append(lax.ppermute(item_table, ('cache', 'pair'), perm))]
    ppermute x0 -> x2, waiting for transfers between devices: none -> 1.87 us  [the longest x1 1.86 us: body(): items.append(lax.ppermute(item_table, ('cache', 'pair'), perm))]
    ppermute x10 -> x9, starting transfers between devices: 17.1 us -> 15.5 us  [shift(): return lax.ppermute(x, axis, [(s, (s + step) % size) for s in range(size)])]
    ppermute x3, waiting for transfers between devices: 0.51 us -> 1.23 us  [body(): pair_scores[q, h] = lax.ppermute(source, ('cache', 'pair'), perm)]
    ppermute x10 -> x9, waiting for transfers between devices: 2.19 us -> 2.19 us  [shift(): return lax.ppermute(x, axis, [(s, (s + step) % size) for s in range(size)])]
  transfers between devices with their start and end apart: 13 -> 14, of which waited for: 5 -> 6; matrix products, arithmetic and copies ran while one was open for 0% -> 0% of each run, Pallas kernels for 28% -> 23%
where the time goes in v15:
time: 39.1 us; the launch traced here: 38.9 us
  starting transfers between devices  23.9 us (61%)
  Pallas kernels  9.08 us (23%)
  waiting for transfers between devices  5.29 us (14%)
  other arithmetic  0.52 us (1%)
    ppermute x9, starting transfers between devices, shift(): return lax.ppermute(x, axis, [(s, (s + step) % size) for s in range(size)])  15.5 us
    pallas_call x1, Pallas kernels, body(): pl.pallas_call(functools.partial(pair_kernel, total, cap, slots, user_sta...  5.19 us
    ppermute x1, starting transfers between devices, body(): items.append(lax.ppermute(item_table, ('cache', 'pair'), perm))  4.84 us
    ppermute x3, starting transfers between devices, body(): pair_scores[q, h] = lax.ppermute(source, ('cache', 'pair'), perm)  2.2 us
    pallas_call x1, Pallas kernels, body(): pl.pallas_call(turn_kernel, out_shape=(jax.ShapeDtypeStruct((width, rows)...  2.2 us
    ppermute x9, waiting for transfers between devices, shift(): return lax.ppermute(x, axis, [(s, (s + step) % size) for s in range(size)])  2.19 us
    ppermute x1, waiting for transfers between devices, body(): items.append(lax.ppermute(item_table, ('cache', 'pair'), perm))  1.86 us
    ppermute x1, starting transfers between devices, body(): lax.ppermute(rows_in, 'pair', [(0, h)])  1.33 us
  transfers between devices with their start and end apart: 14, of which 6 were waited for; matrix products, arithmetic and copies ran while one was open for 0% of the time, Pallas kernels for 23%

profile of v15, /device:TPU:0, one launch (start us, length us, event | category | flops | bytes accessed | tf_op | source)
XLA Modules:
  0.0 38.9 jit_solution(3756677877068618955)
XLA Ops:
  0.0 4.8 %collective-permute-start.9 = (bf16[128,3072]{1,0:T(8,128)(2,1)}, bf16[128,3072]{1,0:T(8,128)(2,1)S(1)}, u32[]{:S(2)}, u32[]{:S(2)}) collective-permute-start(bf16[128,3072]{1,0:T(8,128)(2,1)} %refs_4_.1), channel_id=1, source_target_pairs={{0,2},{2,0},{4,6},{6,4},{8,10},{10,8},{12,14},{14,12},{16,18},{18,... | collective-permute-start | bytes 2359304 | tf_op jit(solution)/shard_map/item_rows/ppermute | solution.py:229
  4.8 1.6 %collective-permute-start = (s32[8]{0:T(128)}, s32[8]{0:T(128)S(1)}, u32[]{:S(2)}, u32[]{:S(2)}) collective-permute-start(s32[8]{0:T(128)} %refs_0_.1), channel_id=1, source_target_pairs={{0,4},{4,8},{8,12},{12,0},{1,5},{5,9},{9,13},{13,1},{2,6},{6,10},{... | collective-permute-start | bytes 104 | tf_op jit(solution)/shard_map/ids/ppermute | solution.py:204
  6.5 2.6 %collective-permute-start.1 = (s32[8]{0:T(128)}, s32[8]{0:T(128)S(1)}, u32[]{:S(2)}, u32[]{:S(2)}) collective-permute-start(s32[8]{0:T(128)} %refs_0_.1), channel_id=1, source_target_pairs={{0,8},{4,12},{8,0},{12,4},{1,9},{5,13},{9,1},{13,5},{2,10},{6,14},... | collective-permute-start | bytes 104 | tf_op jit(solution)/shard_map/ids/ppermute | solution.py:204
  9.1 1.3 %collective-permute-start.2 = (s32[8]{0:T(128)}, s32[8]{0:T(128)S(1)}, u32[]{:S(2)}, u32[]{:S(2)}) collective-permute-start(s32[8]{0:T(128)} %refs_0_.1), channel_id=1, source_target_pairs={{0,12},{4,0},{8,4},{12,8},{1,13},{5,1},{9,5},{13,9},{2,14},{6,2},{... | collective-permute-start | bytes 104 | tf_op jit(solution)/shard_map/ids/ppermute | solution.py:204
  10.4 2.2 %turn.1 = (f32[3072,128]{1,0:T(8,128)S(1)}, bf16[3072,128]{1,0:T(8,128)(2,1)S(1)}, bf16[64,64,256]{2,1,0:T(8,128)(2,1)S(1)}, bf16[128,3072]{1,0:T(8,128)(2,1)S(1...) custom-call(bf16[128,3072]{1,0:T(8,128)(2,1)} %refs_4_.1, bf16[64,64,256]{2,1,0:T(8,128)(2,1)} %bitcast.12, ...), custom_call_target="tpu_custom_call" | custom-call | flops 1610612736 | bytes 8388608 | tf_op jit(solution)/shard_map/turn/pallas_call | solution.py:235
  12.6 0.0 collective-permute-done.refs_1_
  12.6 0.0 collective-permute-done.1.refs_2_
  12.6 0.1 collective-permute-done.2.refs_3_
  12.7 0.4 %states.1.refs_8_.refs_0_ = bf16[16,3200]{1,0:T(8,128)(2,1)S(1)} custom-call(s32[1,8]{1,0:T(1,128)S(1)} %get-tuple-element.27.refs_0_, s32[1,8]{1,0:T(1,128)S(1)} %bitcast.9, s32[1,8]{1,0:T(1,128)S(1)} %bitcast.10, s32[1,8]{1,0:T(1,128)S(1)} %bitcast.11, bf16[16,128]{1,0:T(8,128)(2,1)S(1)} %get-tuple-element.28.refs_4_, ...), custom_call_target="tpu_custom_call" | custom-call | flops 12582912 | bytes 1048576 | tf_op jit(solution)/shard_map/states/pallas_call | solution.py:263
  13.1 1.9 %collective-permute-done.9.refs_5_ = bf16[128,3072]{1,0:T(8,128)(2,1)S(1)} collective-permute-done((bf16[128,3072]{1,0:T(8,128)(2,1)}, bf16[128,3072]{1,0:T(8,128)(2,1)S(1)}, u32[]{:S(2)}, u32[]{:S(2)}) %collective-permute-start.9) | collective-permute-done | bytes 786464 | tf_op jit(solution)/shard_map/item_rows/ppermute | solution.py:229
  15.0 1.3 %collective-permute-start.10 = (bf16[128,3072]{1,0:T(8,128)(2,1)S(1)}, bf16[128,3072]{1,0:T(8,128)(2,1)S(1)}, u32[]{:S(2)}, u32[]{:S(2)}) collective-permute-start(bf16[128,3072]{1,0:T(8,128)(2,1)S(1)} %collective-permute-done.9.refs_5_), channel_id=1, source_target_pairs={{0,1},{2,3},{4,5},{6,7},{8,9},{10,11},{12,13},{14,15},{16,17},{18,... | collective-permute-start | bytes 2359304 | tf_op jit(solution)/shard_map/states/ppermute | solution.py:275
  16.3 2.2 %collective-permute-start.3 = (bf16[16,3200]{1,0:T(8,128)(2,1)S(1)}, bf16[16,3200]{1,0:T(8,128)(2,1)S(1)}, u32[]{:S(2)}, u32[]{:S(2)}) collective-permute-start(bf16[16,3200]{1,0:T(8,128)(2,1)S(1)} %states.1.refs_8_.refs_0_), channel_id=1, source_target_pairs={{0,4},{4,8},{8,12},{12,0},{1,5},{5,9},{9,13},{13,1},{2,6},{6,10},{... | collective-permute-start | bytes 307208 | tf_op jit(solution)/shard_map/states/ppermute | solution.py:204
  18.5 2.6 %collective-permute-start.6 = (bf16[16,3200]{1,0:T(8,128)(2,1)S(1)}, bf16[16,3200]{1,0:T(8,128)(2,1)S(1)}, u32[]{:S(2)}, u32[]{:S(2)}) collective-permute-start(bf16[16,3200]{1,0:T(8,128)(2,1)S(1)} %states.1.refs_8_.refs_0_), channel_id=1, source_target_pairs={{0,8},{4,12},{8,0},{12,4},{1,9},{5,13},{9,1},{13,5},{2,10},{6,14},... | collective-permute-start | bytes 307208 | tf_op jit(solution)/shard_map/states/ppermute | solution.py:204
  21.1 1.3 %collective-permute-start.8 = (bf16[16,3200]{1,0:T(8,128)(2,1)S(1)}, bf16[16,3200]{1,0:T(8,128)(2,1)S(1)}, u32[]{:S(2)}, u32[]{:S(2)}) collective-permute-start(bf16[16,3200]{1,0:T(8,128)(2,1)S(1)} %states.1.refs_8_.refs_0_), channel_id=1, source_target_pairs={{0,12},{4,0},{8,4},{12,8},{1,13},{5,1},{9,5},{13,9},{2,14},{6,2},{... | collective-permute-start | bytes 307208 | tf_op jit(solution)/shard_map/states/ppermute | solution.py:204
  22.4 0.0 copy-start
  22.4 5.2 %pairs.1 = (f32[1,128]{1,0:T(1,128)S(1)}, s32[4,128]{1,0:T(4,128)S(1)}) custom-call(s32[8]{0:T(128)} %refs_0_.1, s32[8]{0:T(128)S(1)} %collective-permute-done.refs_1_, s32[8]{0:T(128)S(1)} %collective-permute-done.1.refs_2_, s32[8]{0:T(128)S(1)} %collective-permute-done.2.refs_3_, s32[2,256]{1,0:T(2,128)} %bitcast.13, ...), custom_call_target="tpu_custom_call" | custom-call | flops 4294967296 | bytes 4194304 | tf_op jit(solution)/shard_map/pairs/pallas_call | solution.py:278
  27.6 1.5 %collective-permute-start.5 = (f32[1,128]{1,0:T(1,128)S(1)}, f32[1,128]{1,0:T(1,128)S(1)}, u32[]{:S(2)}, u32[]{:S(2)}) collective-permute-start(f32[1,128]{1,0:T(1,128)S(1)} %get-tuple-element.32.refs_0_), channel_id=1, source_target_pairs={{0,2},{1,3},{2,0},{3,1},{4,6},{5,7},{6,4},{7,5},{8,10},{9,11},{10,... | collective-permute-start | bytes 1544 | tf_op jit(solution)/shard_map/pairs/ppermute | solution.py:304
  29.2 0.0 collective-permute-done.3.refs_1_
  29.2 0.0 collective-permute-start.4
  29.2 0.0 collective-permute-done.6.refs_2_
  29.2 0.7 %collective-permute-start.7 = (f32[1,128]{1,0:T(1,128)S(1)}, f32[1,128]{1,0:T(1,128)S(1)}, u32[]{:S(2)}, u32[]{:S(2)}) collective-permute-start(f32[1,128]{1,0:T(1,128)S(1)} %get-tuple-element.32.refs_0_), channel_id=1, source_target_pairs={{0,3},{1,2},{2,1},{3,0},{4,7},{5,6},{6,5},{7,4},{8,11},{9,10},{10,... | collective-permute-start | bytes 1544 | tf_op jit(solution)/shard_map/pairs/ppermute | solution.py:304
  29.9 0.0 collective-permute-done.8.refs_3_
  29.9 0.0 collective-permute-done.10.refs_6_
  29.9 0.0 copy-done
  29.9 1.1 %scores.2 = (f32[4,128]{1,0:T(4,128)S(1)}, bf16[256,512]{1,0:T(8,128)(2,1)S(1)}) custom-call(bf16[16,3200]{1,0:T(8,128)(2,1)S(1)} %states.1.refs_8_.refs_0_, bf16[16,3200]{1,0:T(8,128)(2,1)S(1)} %collective-permute-done.3.refs_1_, bf16[16,3200]{1,0:T(8,128)(2,1)S(1)} %collective-permute-done.6.refs_2_, bf16[16,3200]{1,0:T(8,128)(2,1)S(1)} %collective-permute-done.8.refs_3_, ...), custom_call_target="tpu_custom_call" | custom-call | flops 100663296 | bytes 2097152 | tf_op jit(solution)/shard_map/scores/pallas_call | solution.py:308
  31.0 0.2 collective-permute-done.5.refs_2_
  31.2 0.0 collective-permute-done.4.refs_1_
  31.2 1.0 %collective-permute-done.7.refs_3_ = f32[1,128]{1,0:T(1,128)S(1)} collective-permute-done((f32[1,128]{1,0:T(1,128)S(1)}, f32[1,128]{1,0:T(1,128)S(1)}, u32[]{:S(2)}, u32[]{:S(2)}) %collective-permute-start.7) | collective-permute-done | bytes 544 | tf_op jit(solution)/shard_map/pairs/ppermute | solution.py:304
  32.2 0.2 scores.3
  32.4 0.7 %collective-permute-start.13 = (f32[1,128]{1,0:T(1,128)S(1)}, f32[1,128]{1,0:T(1,128)S(1)}, u32[]{:S(2)}, u32[]{:S(2)}) collective-permute-start(f32[1,128]{1,0:T(1,128)S(1)} %get-tuple-element.42), channel_id=1, source_target_pairs={{0,4},{4,8},{8,12},{12,0},{1,5},{5,9},{9,13},{13,1},{2,6},{6,10},{... | collective-permute-start | bytes 1544 | tf_op jit(solution)/shard_map/back/ppermute | solution.py:204
  33.1 0.3 collective-permute-start.12
  33.5 2.8 %collective-permute-start.11 = (f32[1,128]{1,0:T(1,128)S(1)}, f32[1,128]{1,0:T(1,128)S(1)}, u32[]{:S(2)}, u32[]{:S(2)}) collective-permute-start(f32[1,128]{1,0:T(1,128)S(1)} %get-tuple-element.40), channel_id=1, source_target_pairs={{0,12},{4,0},{8,4},{12,8},{1,13},{5,1},{9,5},{13,9},{2,14},{6,2},{... | collective-permute-start | bytes 1544 | tf_op jit(solution)/shard_map/back/ppermute | solution.py:204
  36.3 1.5 %collective-permute-done.13 = f32[1,128]{1,0:T(1,128)S(1)} collective-permute-done((f32[1,128]{1,0:T(1,128)S(1)}, f32[1,128]{1,0:T(1,128)S(1)}, u32[]{:S(2)}, u32[]{:S(2)}) %collective-permute-start.13) | collective-permute-done | bytes 544 | tf_op jit(solution)/shard_map/back/ppermute | solution.py:204
  37.8 0.0 collective-permute-done.12
  37.8 0.6 %collective-permute-done.11 = f32[1,128]{1,0:T(1,128)S(1)} collective-permute-done((f32[1,128]{1,0:T(1,128)S(1)}, f32[1,128]{1,0:T(1,128)S(1)}, u32[]{:S(2)}, u32[]{:S(2)}) %collective-permute-start.11) | collective-permute-done | bytes 544 | tf_op jit(solution)/shard_map/back/ppermute | solution.py:204
  38.4 0.5 %add_bitcast_fusion = f32[128]{0:T(128)} fusion(f32[1,128]{1,0:T(1,128)S(1)} %collective-permute-done.13, f32[1,128]{1,0:T(1,128)S(1)} %collective-permute-done.12, f32[1,128]{1,0:T(1,128)S(1)} %get-tuple-element.39, f32[1,128]{1,0:T(1,128)S(1)} %collective-permute-done.11), kind=kLoop, calls=%fused_computation | loop fusion | flops 384 | bytes 2560 | tf_op jit(solution)/shard_map/reshape | solution.py:336
Async XLA Ops:
  0.0 15.0 %collective-permute-start.9 = (bf16[128,3072]{1,0:T(8,128)(2,1)}, bf16[128,3072]{1,0:T(8,128)(2,1)S(1)}, u32[]{:S(2)}, u32[]{:S(2)}) collective-permute-start(bf16[128,3072]{1,0:T(8,128)(2,1)} %refs_4_.1), channel_id=1, source_target_pairs={{0,2},{2,0},{4,6},{6,4},{8,10},{10,8},{12,14},{14,12},{16,18},{18,... | collective-permute-start | bytes 2359304 | tf_op jit(solution)/shard_map/item_rows/ppermute | solution.py:229
  4.8 7.8 %collective-permute-start = (s32[8]{0:T(128)}, s32[8]{0:T(128)S(1)}, u32[]{:S(2)}, u32[]{:S(2)}) collective-permute-start(s32[8]{0:T(128)} %refs_0_.1), channel_id=1, source_target_pairs={{0,4},{4,8},{8,12},{12,0},{1,5},{5,9},{9,13},{13,1},{2,6},{6,10},{... | collective-permute-start | bytes 104 | tf_op jit(solution)/shard_map/ids/ppermute | solution.py:204
  6.5 6.2 %collective-permute-start.1 = (s32[8]{0:T(128)}, s32[8]{0:T(128)S(1)}, u32[]{:S(2)}, u32[]{:S(2)}) collective-permute-start(s32[8]{0:T(128)} %refs_0_.1), channel_id=1, source_target_pairs={{0,8},{4,12},{8,0},{12,4},{1,9},{5,13},{9,1},{13,5},{2,10},{6,14},... | collective-permute-start | bytes 104 | tf_op jit(solution)/shard_map/ids/ppermute | solution.py:204
  9.1 3.7 %collective-permute-start.2 = (s32[8]{0:T(128)}, s32[8]{0:T(128)S(1)}, u32[]{:S(2)}, u32[]{:S(2)}) collective-permute-start(s32[8]{0:T(128)} %refs_0_.1), channel_id=1, source_target_pairs={{0,12},{4,0},{8,4},{12,8},{1,13},{5,1},{9,5},{13,9},{2,14},{6,2},{... | collective-permute-start | bytes 104 | tf_op jit(solution)/shard_map/ids/ppermute | solution.py:204
  15.0 14.8 %collective-permute-start.10 = (bf16[128,3072]{1,0:T(8,128)(2,1)S(1)}, bf16[128,3072]{1,0:T(8,128)(2,1)S(1)}, u32[]{:S(2)}, u32[]{:S(2)}) collective-permute-start(bf16[128,3072]{1,0:T(8,128)(2,1)S(1)} %collective-permute-done.9.refs_5_), channel_id=1, source_target_pairs={{0,1},{2,3},{4,5},{6,7},{8,9},{10,11},{12,13},{14,15},{16,17},{18,... | collective-permute-start | bytes 2359304 | tf_op jit(solution)/shard_map/states/ppermute | solution.py:275
  16.3 12.8 %collective-permute-start.3 = (bf16[16,3200]{1,0:T(8,128)(2,1)S(1)}, bf16[16,3200]{1,0:T(8,128)(2,1)S(1)}, u32[]{:S(2)}, u32[]{:S(2)}) collective-permute-start(bf16[16,3200]{1,0:T(8,128)(2,1)S(1)} %states.1.refs_8_.refs_0_), channel_id=1, source_target_pairs={{0,4},{4,8},{8,12},{12,0},{1,5},{5,9},{9,13},{13,1},{2,6},{6,10},{... | collective-permute-start | bytes 307208 | tf_op jit(solution)/shard_map/states/ppermute | solution.py:204
  18.5 10.7 %collective-permute-start.6 = (bf16[16,3200]{1,0:T(8,128)(2,1)S(1)}, bf16[16,3200]{1,0:T(8,128)(2,1)S(1)}, u32[]{:S(2)}, u32[]{:S(2)}) collective-permute-start(bf16[16,3200]{1,0:T(8,128)(2,1)S(1)} %states.1.refs_8_.refs_0_), channel_id=1, source_target_pairs={{0,8},{4,12},{8,0},{12,4},{1,9},{5,13},{9,1},{13,5},{2,10},{6,14},... | collective-permute-start | bytes 307208 | tf_op jit(solution)/shard_map/states/ppermute | solution.py:204
  21.1 8.8 %collective-permute-start.8 = (bf16[16,3200]{1,0:T(8,128)(2,1)S(1)}, bf16[16,3200]{1,0:T(8,128)(2,1)S(1)}, u32[]{:S(2)}, u32[]{:S(2)}) collective-permute-start(bf16[16,3200]{1,0:T(8,128)(2,1)S(1)} %states.1.refs_8_.refs_0_), channel_id=1, source_target_pairs={{0,12},{4,0},{8,4},{12,8},{1,13},{5,1},{9,5},{13,9},{2,14},{6,2},{... | collective-permute-start | bytes 307208 | tf_op jit(solution)/shard_map/states/ppermute | solution.py:204
  22.4 7.4 %copy-start = (bf16[128,3072]{1,0:T(8,128)(2,1)S(1)}, bf16[128,3072]{1,0:T(8,128)(2,1)}, u32[]{:S(2)}) copy-start(bf16[128,3072]{1,0:T(8,128)(2,1)} %refs_4_.1) | copy-start | bytes 2359300
  27.6 3.6 %collective-permute-start.5 = (f32[1,128]{1,0:T(1,128)S(1)}, f32[1,128]{1,0:T(1,128)S(1)}, u32[]{:S(2)}, u32[]{:S(2)}) collective-permute-start(f32[1,128]{1,0:T(1,128)S(1)} %get-tuple-element.32.refs_0_), channel_id=1, source_target_pairs={{0,2},{1,3},{2,0},{3,1},{4,6},{5,7},{6,4},{7,5},{8,10},{9,11},{10,... | collective-permute-start | bytes 1544 | tf_op jit(solution)/shard_map/pairs/ppermute | solution.py:304
  29.2 2.1 %collective-permute-start.4 = (f32[1,128]{1,0:T(1,128)S(1)}, f32[1,128]{1,0:T(1,128)S(1)}, u32[]{:S(2)}, u32[]{:S(2)}) collective-permute-start(f32[1,128]{1,0:T(1,128)S(1)} %get-tuple-element.32.refs_0_), channel_id=1, source_target_pairs={{0,1},{1,0},{2,3},{3,2},{4,5},{5,4},{6,7},{7,6},{8,9},{9,8},{10,11... | collective-permute-start | bytes 1544 | tf_op jit(solution)/shard_map/pairs/ppermute | solution.py:304
  29.2 3.0 %collective-permute-start.7 = (f32[1,128]{1,0:T(1,128)S(1)}, f32[1,128]{1,0:T(1,128)S(1)}, u32[]{:S(2)}, u32[]{:S(2)}) collective-permute-start(f32[1,128]{1,0:T(1,128)S(1)} %get-tuple-element.32.refs_0_), channel_id=1, source_target_pairs={{0,3},{1,2},{2,1},{3,0},{4,7},{5,6},{6,5},{7,4},{8,11},{9,10},{10,... | collective-permute-start | bytes 1544 | tf_op jit(solution)/shard_map/pairs/ppermute | solution.py:304
  32.4 5.4 %collective-permute-start.13 = (f32[1,128]{1,0:T(1,128)S(1)}, f32[1,128]{1,0:T(1,128)S(1)}, u32[]{:S(2)}, u32[]{:S(2)}) collective-permute-start(f32[1,128]{1,0:T(1,128)S(1)} %get-tuple-element.42), channel_id=1, source_target_pairs={{0,4},{4,8},{8,12},{12,0},{1,5},{5,9},{9,13},{13,1},{2,6},{6,10},{... | collective-permute-start | bytes 1544 | tf_op jit(solution)/shard_map/back/ppermute | solution.py:204
  33.1 4.7 %collective-permute-start.12 = (f32[1,128]{1,0:T(1,128)S(1)}, f32[1,128]{1,0:T(1,128)S(1)}, u32[]{:S(2)}, u32[]{:S(2)}) collective-permute-start(f32[1,128]{1,0:T(1,128)S(1)} %get-tuple-element.41), channel_id=1, source_target_pairs={{0,8},{4,12},{8,0},{12,4},{1,9},{5,13},{9,1},{13,5},{2,10},{6,14},... | collective-permute-start | bytes 1544 | tf_op jit(solution)/shard_map/back/ppermute | solution.py:204
  33.5 4.9 %collective-permute-start.11 = (f32[1,128]{1,0:T(1,128)S(1)}, f32[1,128]{1,0:T(1,128)S(1)}, u32[]{:S(2)}, u32[]{:S(2)}) collective-permute-start(f32[1,128]{1,0:T(1,128)S(1)} %get-tuple-element.40), channel_id=1, source_target_pairs={{0,12},{4,0},{8,4},{12,8},{1,13},{5,1},{9,5},{13,9},{2,14},{6,2},{... | collective-permute-start | bytes 1544 | tf_op jit(solution)/shard_map/back/ppermute | solution.py:204

commit v16 on v14

--- a/solution.py
+++ b/solution.py
@@ -280,7 +280,7 @@
             perm = [
                 (c * parts + d, (c + q) % planes * parts + (d + h) % parts) for c in range(planes) for d in range(parts)
             ]
-            source, after = pair_parts, {1: 2, 2: 1}.get(len(pair_scores) - 1, 0)
+            source, after = pair_parts, {1: 1, 2: 2}.get(len(pair_scores) - 1, 0)
             if after:
                 source, states[after] = lax.optimization_barrier((pair_parts, states[after]))
             pair_scores[q, h] = lax.ppermute(source, ("cache", "pair"), perm)

time: 31.6 us -> 32.2 us (1.019)
  waiting for transfers between devices: 2.7 us -> 3.37 us
    ppermute x10, waiting for transfers between devices: 2.19 us -> 2.75 us  [shift(): return lax.ppermute(x, axis, [(s, (s + step) % size) for s in range(size)])]
  transfers between devices with their start and end apart: 13 -> 13, of which waited for: 5 -> 7; matrix products, arithmetic and copies ran while one was open for 0% -> 0% of each run, Pallas kernels for 28% -> 27%
where the time goes in v16:
time: 32.2 us; the launch traced here: 32.1 us
  starting transfers between devices  19.3 us (60%)
  Pallas kernels  8.82 us (27%)
  waiting for transfers between devices  3.37 us (10%)
  other arithmetic  0.52 us (2%)
    ppermute x10, starting transfers between devices, shift(): return lax.ppermute(x, axis, [(s, (s + step) % size) for s in range(size)])  17.2 us
    pallas_call x1, Pallas kernels, body(): pl.pallas_call(functools.partial(pair_kernel, total, cap, slots, user_sta...  5.18 us
    ppermute x10, waiting for transfers between devices, shift(): return lax.ppermute(x, axis, [(s, (s + step) % size) for s in range(size)])  2.75 us
    pallas_call x1, Pallas kernels, body(): pl.pallas_call(turn_kernel, out_shape=(jax.ShapeDtypeStruct((width, rows)...  2.2 us
    ppermute x3, starting transfers between devices, body(): pair_scores[q, h] = lax.ppermute(source, ('cache', 'pair'), perm)  2.08 us
    pallas_call x1, Pallas kernels, body(): pl.pallas_call(functools.partial(linear_kernel, total, planes), out_shape...  0.88 us
  transfers between devices with their start and end apart: 13, of which 7 were waited for; matrix products, arithmetic and copies ran while one was open for 0% of the time, Pallas kernels for 27%

profile of v16, /device:TPU:0, one launch (start us, length us, event | category | flops | bytes accessed | tf_op | source)
XLA Modules:
  0.0 32.1 jit_solution(3262164023933149701)
XLA Ops:
  0.0 2.9 %collective-permute-start.9 = (bf16[128,3072]{1,0:T(8,128)(2,1)}, bf16[128,3072]{1,0:T(8,128)(2,1)S(1)}, u32[]{:S(2)}, u32[]{:S(2)}) collective-permute-start(bf16[128,3072]{1,0:T(8,128)(2,1)} %refs_4_.1), channel_id=1, source_target_pairs={{0,2},{2,0},{1,3},{3,1},{4,6},{6,4},{5,7},{7,5},{8,10},{10,8},{9,1... | collective-permute-start | bytes 2359304 | tf_op jit(solution)/shard_map/item_rows/ppermute | solution.py:193
  2.9 1.6 %collective-permute-start = (s32[8]{0:T(128)}, s32[8]{0:T(128)S(1)}, u32[]{:S(2)}, u32[]{:S(2)}) collective-permute-start(s32[8]{0:T(128)} %refs_0_.1), channel_id=1, source_target_pairs={{0,4},{4,8},{8,12},{12,0},{1,5},{5,9},{9,13},{13,1},{2,6},{6,10},{... | collective-permute-start | bytes 104 | tf_op jit(solution)/shard_map/ids/ppermute | solution.py:193
  4.5 2.6 %collective-permute-start.1 = (s32[8]{0:T(128)}, s32[8]{0:T(128)S(1)}, u32[]{:S(2)}, u32[]{:S(2)}) collective-permute-start(s32[8]{0:T(128)} %refs_0_.1), channel_id=1, source_target_pairs={{0,8},{4,12},{8,0},{12,4},{1,9},{5,13},{9,1},{13,5},{2,10},{6,14},... | collective-permute-start | bytes 104 | tf_op jit(solution)/shard_map/ids/ppermute | solution.py:193
  7.1 1.3 %collective-permute-start.2 = (s32[8]{0:T(128)}, s32[8]{0:T(128)S(1)}, u32[]{:S(2)}, u32[]{:S(2)}) collective-permute-start(s32[8]{0:T(128)} %refs_0_.1), channel_id=1, source_target_pairs={{0,12},{4,0},{8,4},{12,8},{1,13},{5,1},{9,5},{13,9},{2,14},{6,2},{... | collective-permute-start | bytes 104 | tf_op jit(solution)/shard_map/ids/ppermute | solution.py:193
  8.5 2.2 %turn.1 = (f32[3072,128]{1,0:T(8,128)S(1)}, bf16[3072,128]{1,0:T(8,128)(2,1)S(1)}, bf16[64,64,256]{2,1,0:T(8,128)(2,1)S(1)}, bf16[128,3072]{1,0:T(8,128)(2,1)S(1...) custom-call(bf16[128,3072]{1,0:T(8,128)(2,1)} %refs_4_.1, bf16[64,64,256]{2,1,0:T(8,128)(2,1)} %bitcast.12, ...), custom_call_target="tpu_custom_call" | custom-call | flops 1610612736 | bytes 8388608 | tf_op jit(solution)/shard_map/turn/pallas_call | solution.py:221
  10.7 0.0 collective-permute-done.refs_1_
  10.7 0.0 collective-permute-done.1.refs_2_
  10.7 0.1 collective-permute-done.2.refs_3_
  10.8 0.4 %states.1.refs_8_.refs_0_ = bf16[16,3200]{1,0:T(8,128)(2,1)S(1)} custom-call(s32[1,8]{1,0:T(1,128)S(1)} %get-tuple-element.26.refs_0_, s32[1,8]{1,0:T(1,128)S(1)} %bitcast.9, s32[1,8]{1,0:T(1,128)S(1)} %bitcast.10, s32[1,8]{1,0:T(1,128)S(1)} %bitcast.11, bf16[16,128]{1,0:T(8,128)(2,1)S(1)} %get-tuple-element.27.refs_4_, ...), custom_call_target="tpu_custom_call" | custom-call | flops 12582912 | bytes 1048576 | tf_op jit(solution)/shard_map/states/pallas_call | solution.py:249
  11.2 0.6 %collective-permute-start.3 = (bf16[16,3200]{1,0:T(8,128)(2,1)S(1)}, bf16[16,3200]{1,0:T(8,128)(2,1)S(1)}, u32[]{:S(2)}, u32[]{:S(2)}) collective-permute-start(bf16[16,3200]{1,0:T(8,128)(2,1)S(1)} %states.1.refs_8_.refs_0_), channel_id=1, source_target_pairs={{0,4},{4,8},{8,12},{12,0},{1,5},{5,9},{9,13},{13,1},{2,6},{6,10},{... | collective-permute-start | bytes 307208 | tf_op jit(solution)/shard_map/states/ppermute | solution.py:193
  11.8 3.1 %collective-permute-start.6 = (bf16[16,3200]{1,0:T(8,128)(2,1)S(1)}, bf16[16,3200]{1,0:T(8,128)(2,1)S(1)}, u32[]{:S(2)}, u32[]{:S(2)}) collective-permute-start(bf16[16,3200]{1,0:T(8,128)(2,1)S(1)} %states.1.refs_8_.refs_0_), channel_id=1, source_target_pairs={{0,8},{4,12},{8,0},{12,4},{1,9},{5,13},{9,1},{13,5},{2,10},{6,14},... | collective-permute-start | bytes 307208 | tf_op jit(solution)/shard_map/states/ppermute | solution.py:193
  14.9 0.1 collective-permute-start.8
  15.1 0.0 copy-start
  15.1 5.2 %pairs.1 = (f32[1,128]{1,0:T(1,128)S(1)}, s32[4,128]{1,0:T(4,128)S(1)}) custom-call(s32[8]{0:T(128)} %refs_0_.1, s32[8]{0:T(128)S(1)} %collective-permute-done.refs_1_, s32[8]{0:T(128)S(1)} %collective-permute-done.1.refs_2_, s32[8]{0:T(128)S(1)} %collective-permute-done.2.refs_3_, s32[2,256]{1,0:T(2,128)} %bitcast.13, ...), custom_call_target="tpu_custom_call" | custom-call | flops 4294967296 | bytes 4194304 | tf_op jit(solution)/shard_map/pairs/pallas_call | solution.py:260
  20.2 0.6 %collective-permute-start.5 = (f32[1,128]{1,0:T(1,128)S(1)}, f32[1,128]{1,0:T(1,128)S(1)}, u32[]{:S(2)}, u32[]{:S(2)}) collective-permute-start(f32[1,128]{1,0:T(1,128)S(1)} %get-tuple-element.31.refs_0_), channel_id=1, source_target_pairs={{0,2},{1,3},{2,0},{3,1},{4,6},{5,7},{6,4},{7,5},{8,10},{9,11},{10,... | collective-permute-start | bytes 1544 | tf_op jit(solution)/shard_map/pairs/ppermute | solution.py:286
  20.9 0.0 collective-permute-done.3.refs_1_
  20.9 0.0 collective-permute-start.4
  20.9 0.1 collective-permute-done.6.refs_2_
  21.0 1.5 %collective-permute-start.7 = (f32[1,128]{1,0:T(1,128)S(1)}, f32[1,128]{1,0:T(1,128)S(1)}, u32[]{:S(2)}, u32[]{:S(2)}) collective-permute-start(f32[1,128]{1,0:T(1,128)S(1)} %get-tuple-element.31.refs_0_), channel_id=1, source_target_pairs={{0,3},{1,2},{2,1},{3,0},{4,7},{5,6},{6,5},{7,4},{8,11},{9,10},{10,... | collective-permute-start | bytes 1544 | tf_op jit(solution)/shard_map/pairs/ppermute | solution.py:286
  22.5 0.0 collective-permute-done.8.refs_3_
  22.5 0.0 collective-permute-done.9.refs_5_
  22.5 0.0 copy-done
  22.5 0.9 %scores.2 = (f32[4,128]{1,0:T(4,128)S(1)}, bf16[256,512]{1,0:T(8,128)(2,1)S(1)}) custom-call(bf16[16,3200]{1,0:T(8,128)(2,1)S(1)} %states.1.refs_8_.refs_0_, bf16[16,3200]{1,0:T(8,128)(2,1)S(1)} %collective-permute-done.3.refs_1_, bf16[16,3200]{1,0:T(8,128)(2,1)S(1)} %collective-permute-done.6.refs_2_, bf16[16,3200]{1,0:T(8,128)(2,1)S(1)} %collective-permute-done.8.refs_3_, ...), custom_call_target="tpu_custom_call" | custom-call | flops 100663296 | bytes 2097152 | tf_op jit(solution)/shard_map/scores/pallas_call | solution.py:290
  23.4 0.5 %collective-permute-done.5.refs_2_ = f32[1,128]{1,0:T(1,128)S(1)} collective-permute-done((f32[1,128]{1,0:T(1,128)S(1)}, f32[1,128]{1,0:T(1,128)S(1)}, u32[]{:S(2)}, u32[]{:S(2)}) %collective-permute-start.5) | collective-permute-done | bytes 544 | tf_op jit(solution)/shard_map/pairs/ppermute | solution.py:286
  23.9 0.0 collective-permute-done.4.refs_1_
  23.9 0.1 collective-permute-done.7.refs_3_
  24.0 0.2 scores.3
  24.1 1.9 %collective-permute-start.12 = (f32[1,128]{1,0:T(1,128)S(1)}, f32[1,128]{1,0:T(1,128)S(1)}, u32[]{:S(2)}, u32[]{:S(2)}) collective-permute-start(f32[1,128]{1,0:T(1,128)S(1)} %get-tuple-element.40), channel_id=1, source_target_pairs={{0,4},{4,8},{8,12},{12,0},{1,5},{5,9},{9,13},{13,1},{2,6},{6,10},{... | collective-permute-start | bytes 1544 | tf_op jit(solution)/shard_map/back/ppermute | solution.py:193
  26.0 2.0 %collective-permute-start.11 = (f32[1,128]{1,0:T(1,128)S(1)}, f32[1,128]{1,0:T(1,128)S(1)}, u32[]{:S(2)}, u32[]{:S(2)}) collective-permute-start(f32[1,128]{1,0:T(1,128)S(1)} %get-tuple-element.39), channel_id=1, source_target_pairs={{0,8},{4,12},{8,0},{12,4},{1,9},{5,13},{9,1},{13,5},{2,10},{6,14},... | collective-permute-start | bytes 1544 | tf_op jit(solution)/shard_map/back/ppermute | solution.py:193
  28.0 1.0 %collective-permute-start.10 = (f32[1,128]{1,0:T(1,128)S(1)}, f32[1,128]{1,0:T(1,128)S(1)}, u32[]{:S(2)}, u32[]{:S(2)}) collective-permute-start(f32[1,128]{1,0:T(1,128)S(1)} %get-tuple-element.38), channel_id=1, source_target_pairs={{0,12},{4,0},{8,4},{12,8},{1,13},{5,1},{9,5},{13,9},{2,14},{6,2},{... | collective-permute-start | bytes 1544 | tf_op jit(solution)/shard_map/back/ppermute | solution.py:193
  29.1 0.5 %collective-permute-done.12 = f32[1,128]{1,0:T(1,128)S(1)} collective-permute-done((f32[1,128]{1,0:T(1,128)S(1)}, f32[1,128]{1,0:T(1,128)S(1)}, u32[]{:S(2)}, u32[]{:S(2)}) %collective-permute-start.12) | collective-permute-done | bytes 544 | tf_op jit(solution)/shard_map/back/ppermute | solution.py:193
  29.5 0.9 %collective-permute-done.11 = f32[1,128]{1,0:T(1,128)S(1)} collective-permute-done((f32[1,128]{1,0:T(1,128)S(1)}, f32[1,128]{1,0:T(1,128)S(1)}, u32[]{:S(2)}, u32[]{:S(2)}) %collective-permute-start.11) | collective-permute-done | bytes 544 | tf_op jit(solution)/shard_map/back/ppermute | solution.py:193
  30.5 1.1 %collective-permute-done.10 = f32[1,128]{1,0:T(1,128)S(1)} collective-permute-done((f32[1,128]{1,0:T(1,128)S(1)}, f32[1,128]{1,0:T(1,128)S(1)}, u32[]{:S(2)}, u32[]{:S(2)}) %collective-permute-start.10) | collective-permute-done | bytes 544 | tf_op jit(solution)/shard_map/back/ppermute | solution.py:193
  31.6 0.5 %add_bitcast_fusion = f32[128]{0:T(128)} fusion(f32[1,128]{1,0:T(1,128)S(1)} %collective-permute-done.12, f32[1,128]{1,0:T(1,128)S(1)} %collective-permute-done.11, f32[1,128]{1,0:T(1,128)S(1)} %get-tuple-element.37, f32[1,128]{1,0:T(1,128)S(1)} %collective-permute-done.10), kind=kLoop, calls=%fused_computation | loop fusion | flops 384 | bytes 2560 | tf_op jit(solution)/shard_map/reshape | solution.py:318
Async XLA Ops:
  0.0 22.5 %collective-permute-start.9 = (bf16[128,3072]{1,0:T(8,128)(2,1)}, bf16[128,3072]{1,0:T(8,128)(2,1)S(1)}, u32[]{:S(2)}, u32[]{:S(2)}) collective-permute-start(bf16[128,3072]{1,0:T(8,128)(2,1)} %refs_4_.1), channel_id=1, source_target_pairs={{0,2},{2,0},{1,3},{3,1},{4,6},{6,4},{5,7},{7,5},{8,10},{10,8},{9,1... | collective-permute-start | bytes 2359304 | tf_op jit(solution)/shard_map/item_rows/ppermute | solution.py:193
  2.9 7.7 %collective-permute-start = (s32[8]{0:T(128)}, s32[8]{0:T(128)S(1)}, u32[]{:S(2)}, u32[]{:S(2)}) collective-permute-start(s32[8]{0:T(128)} %refs_0_.1), channel_id=1, source_target_pairs={{0,4},{4,8},{8,12},{12,0},{1,5},{5,9},{9,13},{13,1},{2,6},{6,10},{... | collective-permute-start | bytes 104 | tf_op jit(solution)/shard_map/ids/ppermute | solution.py:193
  4.5 6.2 %collective-permute-start.1 = (s32[8]{0:T(128)}, s32[8]{0:T(128)S(1)}, u32[]{:S(2)}, u32[]{:S(2)}) collective-permute-start(s32[8]{0:T(128)} %refs_0_.1), channel_id=1, source_target_pairs={{0,8},{4,12},{8,0},{12,4},{1,9},{5,13},{9,1},{13,5},{2,10},{6,14},... | collective-permute-start | bytes 104 | tf_op jit(solution)/shard_map/ids/ppermute | solution.py:193
  7.1 3.7 %collective-permute-start.2 = (s32[8]{0:T(128)}, s32[8]{0:T(128)S(1)}, u32[]{:S(2)}, u32[]{:S(2)}) collective-permute-start(s32[8]{0:T(128)} %refs_0_.1), channel_id=1, source_target_pairs={{0,12},{4,0},{8,4},{12,8},{1,13},{5,1},{9,5},{13,9},{2,14},{6,2},{... | collective-permute-start | bytes 104 | tf_op jit(solution)/shard_map/ids/ppermute | solution.py:193
  11.2 9.7 %collective-permute-start.3 = (bf16[16,3200]{1,0:T(8,128)(2,1)S(1)}, bf16[16,3200]{1,0:T(8,128)(2,1)S(1)}, u32[]{:S(2)}, u32[]{:S(2)}) collective-permute-start(bf16[16,3200]{1,0:T(8,128)(2,1)S(1)} %states.1.refs_8_.refs_0_), channel_id=1, source_target_pairs={{0,4},{4,8},{8,12},{12,0},{1,5},{5,9},{9,13},{13,1},{2,6},{6,10},{... | collective-permute-start | bytes 307208 | tf_op jit(solution)/shard_map/states/ppermute | solution.py:193
  11.8 9.2 %collective-permute-start.6 = (bf16[16,3200]{1,0:T(8,128)(2,1)S(1)}, bf16[16,3200]{1,0:T(8,128)(2,1)S(1)}, u32[]{:S(2)}, u32[]{:S(2)}) collective-permute-start(bf16[16,3200]{1,0:T(8,128)(2,1)S(1)} %states.1.refs_8_.refs_0_), channel_id=1, source_target_pairs={{0,8},{4,12},{8,0},{12,4},{1,9},{5,13},{9,1},{13,5},{2,10},{6,14},... | collective-permute-start | bytes 307208 | tf_op jit(solution)/shard_map/states/ppermute | solution.py:193
  14.9 7.5 %collective-permute-start.8 = (bf16[16,3200]{1,0:T(8,128)(2,1)S(1)}, bf16[16,3200]{1,0:T(8,128)(2,1)S(1)}, u32[]{:S(2)}, u32[]{:S(2)}) collective-permute-start(bf16[16,3200]{1,0:T(8,128)(2,1)S(1)} %states.1.refs_8_.refs_0_), channel_id=1, source_target_pairs={{0,12},{4,0},{8,4},{12,8},{1,13},{5,1},{9,5},{13,9},{2,14},{6,2},{... | collective-permute-start | bytes 307208 | tf_op jit(solution)/shard_map/states/ppermute | solution.py:193
  15.1 7.4 %copy-start = (bf16[128,3072]{1,0:T(8,128)(2,1)S(1)}, bf16[128,3072]{1,0:T(8,128)(2,1)}, u32[]{:S(2)}) copy-start(bf16[128,3072]{1,0:T(8,128)(2,1)} %refs_4_.1) | copy-start | bytes 2359300
  20.2 3.6 %collective-permute-start.5 = (f32[1,128]{1,0:T(1,128)S(1)}, f32[1,128]{1,0:T(1,128)S(1)}, u32[]{:S(2)}, u32[]{:S(2)}) collective-permute-start(f32[1,128]{1,0:T(1,128)S(1)} %get-tuple-element.31.refs_0_), channel_id=1, source_target_pairs={{0,2},{1,3},{2,0},{3,1},{4,6},{5,7},{6,4},{7,5},{8,10},{9,11},{10,... | collective-permute-start | bytes 1544 | tf_op jit(solution)/shard_map/pairs/ppermute | solution.py:286
  20.9 3.0 %collective-permute-start.4 = (f32[1,128]{1,0:T(1,128)S(1)}, f32[1,128]{1,0:T(1,128)S(1)}, u32[]{:S(2)}, u32[]{:S(2)}) collective-permute-start(f32[1,128]{1,0:T(1,128)S(1)} %get-tuple-element.31.refs_0_), channel_id=1, source_target_pairs={{0,1},{1,0},{2,3},{3,2},{4,5},{5,4},{6,7},{7,6},{8,9},{9,8},{10,11... | collective-permute-start | bytes 1544 | tf_op jit(solution)/shard_map/pairs/ppermute | solution.py:286
  21.0 3.0 %collective-permute-start.7 = (f32[1,128]{1,0:T(1,128)S(1)}, f32[1,128]{1,0:T(1,128)S(1)}, u32[]{:S(2)}, u32[]{:S(2)}) collective-permute-start(f32[1,128]{1,0:T(1,128)S(1)} %get-tuple-element.31.refs_0_), channel_id=1, source_target_pairs={{0,3},{1,2},{2,1},{3,0},{4,7},{5,6},{6,5},{7,4},{8,11},{9,10},{10,... | collective-permute-start | bytes 1544 | tf_op jit(solution)/shard_map/pairs/ppermute | solution.py:286
  24.1 5.4 %collective-permute-start.12 = (f32[1,128]{1,0:T(1,128)S(1)}, f32[1,128]{1,0:T(1,128)S(1)}, u32[]{:S(2)}, u32[]{:S(2)}) collective-permute-start(f32[1,128]{1,0:T(1,128)S(1)} %get-tuple-element.40), channel_id=1, source_target_pairs={{0,4},{4,8},{8,12},{12,0},{1,5},{5,9},{9,13},{13,1},{2,6},{6,10},{... | collective-permute-start | bytes 1544 | tf_op jit(solution)/shard_map/back/ppermute | solution.py:193
  26.0 4.4 %collective-permute-start.11 = (f32[1,128]{1,0:T(1,128)S(1)}, f32[1,128]{1,0:T(1,128)S(1)}, u32[]{:S(2)}, u32[]{:S(2)}) collective-permute-start(f32[1,128]{1,0:T(1,128)S(1)} %get-tuple-element.39), channel_id=1, source_target_pairs={{0,8},{4,12},{8,0},{12,4},{1,9},{5,13},{9,1},{13,5},{2,10},{6,14},... | collective-permute-start | bytes 1544 | tf_op jit(solution)/shard_map/back/ppermute | solution.py:193
  28.0 3.5 %collective-permute-start.10 = (f32[1,128]{1,0:T(1,128)S(1)}, f32[1,128]{1,0:T(1,128)S(1)}, u32[]{:S(2)}, u32[]{:S(2)}) collective-permute-start(f32[1,128]{1,0:T(1,128)S(1)} %get-tuple-element.38), channel_id=1, source_target_pairs={{0,12},{4,0},{8,4},{12,8},{1,13},{5,1},{9,5},{13,9},{2,14},{6,2},{... | collective-permute-start | bytes 1544 | tf_op jit(solution)/shard_map/back/ppermute | solution.py:193

commit v17 on v16

--- a/solution.py
+++ b/solution.py
@@ -108,30 +108,30 @@
     id_fetches = [pltpu.make_async_copy(users[j], asked.at[j], sems.at[j]) for j in range(total)]
     for copy in [fields_fetch] + id_fetches:
         copy.start()
-    count = mats.shape[2]
-    eye_pairs = (iota((count, count), 0) == iota((count, count), 1)).astype(jnp.bfloat16)
-    side = (iota((count, LANES), 0) % 2 == 0) == (iota((count, LANES), 1) < K)
+    pairs = mats.shape[2]
+    steps = pairs // 2
+    eye = (iota((steps, steps), 0) == iota((steps, steps), 1)).astype(jnp.bfloat16)
     for k in range(0, K, 2):
-        twice = jnp.concatenate([mats[k], mats[k], mats[k + 1], mats[k + 1]], axis=0)
-        turned = dot(eye_pairs, twice, NT)
-        stacked[pl.ds(k, count, stride=PITCH), :] = jnp.where(side, turned[:, :LANES], 0.0)
-        stacked[pl.ds(k + 1, count, stride=PITCH), :] = jnp.where(side, turned[:, LANES:], 0.0)
+        sides = [mats[at, :, part * steps:(part + 1) * steps] for at in (k, k + 1) for part in range(2)]
+        turned = dot(eye, jnp.concatenate(sides, axis=0), NT)
+        stacked[pl.ds(k, steps, stride=PITCH), :] = turned[:, :LANES]
+        stacked[pl.ds(k + 1, steps, stride=PITCH), :] = turned[:, LANES:]
     fields_fetch.wait()
-
-    def two(step, total):
-        first = step * 2
-        lefts, rights, mults = [], [], []
-        for p in (first, first + 1):
-            a = pl.multiple_of(fields[0, p] * K, K)
-            b = pl.multiple_of(fields[1, p] * K, K)
-            lefts.append(stacked[pl.ds(pl.multiple_of(p * PITCH, 8), K), :].astype(jnp.bfloat16))
-            rights.append(rows16[pl.ds(b, K), :])
-            mults.append(rows32[pl.ds(a, K), :])
-        moved = dot(jnp.concatenate(lefts, axis=0), jnp.concatenate(rights, axis=0), NN)
-        return total + moved * jnp.concatenate(mults, axis=0)
-
-    sums = lax.fori_loop(0, count // 2, two, jnp.zeros((2 * K, rows32.shape[1]), jnp.float32), unroll=16)
-    out[...] = jnp.sum(sums, axis=0, keepdims=True)
+    items = rows32.shape[1]
+    blank = jnp.zeros((K, items), jnp.bfloat16)
+
+    def two(p, total):
+        fields_of = [(pl.multiple_of(fields[0, q] * K, K), pl.multiple_of(fields[1, q] * K, K)) for q in (p, p + steps)]
+        left = stacked[pl.ds(pl.multiple_of(p * PITCH, 8), K), :].astype(jnp.bfloat16)
+        first, second = [rows16[pl.ds(b, K), :] for _, b in fields_of]
+        right = jnp.concatenate(
+            [jnp.concatenate([first, blank], axis=1), jnp.concatenate([blank, second], axis=1)], axis=0
+        )
+        return total + dot(left, right, NN) * jnp.concatenate([rows32[pl.ds(a, K), :] for a, _ in fields_of], axis=1)
+
+    sums = lax.fori_loop(0, steps, two, jnp.zeros((K, 2 * items), jnp.float32), unroll=16)
+    line = jnp.sum(sums, axis=0, keepdims=True)
+    out[...] = line[:, :items] + line[:, items:]
     for copy in id_fetches:
         copy.wait()
     for j, row in enumerate(slot_rows(asked, cap, slots, user_rows, places.shape[1])):
@@ -268,7 +268,7 @@
             scratch_shapes=[
                 pltpu.SMEM((total, readers), jnp.int32),
                 pltpu.SMEM((2, count), jnp.int32),
-                pltpu.VMEM((count * PITCH, LANES), jnp.float32),
+                pltpu.VMEM((count // 2 * PITCH, LANES), jnp.float32),
                 pltpu.SemaphoreType.DMA((1 + total,)),
             ],
             compiler_params=params,

time: 32.2 us -> 32.2 us (level)
  waiting for transfers between devices: 3.37 us -> 5.73 us
  starting transfers between devices: 19.3 us -> 17.8 us
  Pallas kernels: 8.82 us -> 8.01 us
    ppermute x10, waiting for transfers between devices: 2.75 us -> 4.33 us  [shift(): return lax.ppermute(x, axis, [(s, (s + step) % size) for s in range(size)])]
    ppermute x3, starting transfers between devices: 2.08 us -> 1.27 us  [body(): pair_scores[q, h] = lax.ppermute(source, ('cache', 'pair'), perm)]
    pallas_call x1, Pallas kernels: 5.18 us -> 4.38 us  [body(): pl.pallas_call(functools.partial(pair_kernel, total, cap, slots, user_sta...]
    ppermute x3, waiting for transfers between devices: 0.62 us -> 1.41 us  [body(): pair_scores[q, h] = lax.ppermute(source, ('cache', 'pair'), perm)]
    ppermute x10, starting transfers between devices: 17.2 us -> 16.5 us  [shift(): return lax.ppermute(x, axis, [(s, (s + step) % size) for s in range(size)])]
  transfers between devices with their start and end apart: 13 -> 13, of which waited for: 7 -> 7; matrix products, arithmetic and copies ran while one was open for 0% -> 0% of each run, Pallas kernels for 27% -> 24%
where the time goes in v17:
time: 32.2 us; the launch traced here: 32.1 us
  starting transfers between devices  17.8 us (55%)
  Pallas kernels  8.01 us (25%)
  waiting for transfers between devices  5.73 us (18%)
  other arithmetic  0.52 us (2%)
    ppermute x10, starting transfers between devices, shift(): return lax.ppermute(x, axis, [(s, (s + step) % size) for s in range(size)])  16.5 us
    pallas_call x1, Pallas kernels, body(): pl.pallas_call(functools.partial(pair_kernel, total, cap, slots, user_sta...  4.38 us
    ppermute x10, waiting for transfers between devices, shift(): return lax.ppermute(x, axis, [(s, (s + step) % size) for s in range(size)])  4.33 us
    pallas_call x1, Pallas kernels, body(): pl.pallas_call(turn_kernel, out_shape=(jax.ShapeDtypeStruct((width, rows)...  2.2 us
    ppermute x3, waiting for transfers between devices, body(): pair_scores[q, h] = lax.ppermute(source, ('cache', 'pair'), perm)  1.41 us
    ppermute x3, starting transfers between devices, body(): pair_scores[q, h] = lax.ppermute(source, ('cache', 'pair'), perm)  1.27 us
    pallas_call x1, Pallas kernels, body(): pl.pallas_call(functools.partial(linear_kernel, total, planes), out_shape...  0.88 us
  transfers between devices with their start and end apart: 13, of which 7 were waited for; matrix products, arithmetic and copies ran while one was open for 0% of the time, Pallas kernels for 24%

profile of v17, /device:TPU:0, one launch (start us, length us, event | category | flops | bytes accessed | tf_op | source)
XLA Modules:
  0.0 32.1 jit_solution(3085424171368524215)
XLA Ops:
  0.0 2.9 %collective-permute-start.9 = (bf16[128,3072]{1,0:T(8,128)(2,1)}, bf16[128,3072]{1,0:T(8,128)(2,1)S(1)}, u32[]{:S(2)}, u32[]{:S(2)}) collective-permute-start(bf16[128,3072]{1,0:T(8,128)(2,1)} %refs_4_.1), channel_id=1, source_target_pairs={{0,2},{2,0},{1,3},{3,1},{4,6},{6,4},{5,7},{7,5},{8,10},{10,8},{9,1... | collective-permute-start | bytes 2359304 | tf_op jit(solution)/shard_map/item_rows/ppermute | solution.py:193
  2.9 1.6 %collective-permute-start = (s32[8]{0:T(128)}, s32[8]{0:T(128)S(1)}, u32[]{:S(2)}, u32[]{:S(2)}) collective-permute-start(s32[8]{0:T(128)} %refs_0_.1), channel_id=1, source_target_pairs={{0,4},{4,8},{8,12},{12,0},{1,5},{5,9},{9,13},{13,1},{2,6},{6,10},{... | collective-permute-start | bytes 104 | tf_op jit(solution)/shard_map/ids/ppermute | solution.py:193
  4.5 2.6 %collective-permute-start.1 = (s32[8]{0:T(128)}, s32[8]{0:T(128)S(1)}, u32[]{:S(2)}, u32[]{:S(2)}) collective-permute-start(s32[8]{0:T(128)} %refs_0_.1), channel_id=1, source_target_pairs={{0,8},{4,12},{8,0},{12,4},{1,9},{5,13},{9,1},{13,5},{2,10},{6,14},... | collective-permute-start | bytes 104 | tf_op jit(solution)/shard_map/ids/ppermute | solution.py:193
  7.1 1.3 %collective-permute-start.2 = (s32[8]{0:T(128)}, s32[8]{0:T(128)S(1)}, u32[]{:S(2)}, u32[]{:S(2)}) collective-permute-start(s32[8]{0:T(128)} %refs_0_.1), channel_id=1, source_target_pairs={{0,12},{4,0},{8,4},{12,8},{1,13},{5,1},{9,5},{13,9},{2,14},{6,2},{... | collective-permute-start | bytes 104 | tf_op jit(solution)/shard_map/ids/ppermute | solution.py:193
  8.5 2.2 %turn.1 = (f32[3072,128]{1,0:T(8,128)S(1)}, bf16[3072,128]{1,0:T(8,128)(2,1)S(1)}, bf16[64,64,256]{2,1,0:T(8,128)(2,1)S(1)}, bf16[128,3072]{1,0:T(8,128)(2,1)S(1...) custom-call(bf16[128,3072]{1,0:T(8,128)(2,1)} %refs_4_.1, bf16[64,64,256]{2,1,0:T(8,128)(2,1)} %bitcast.12, ...), custom_call_target="tpu_custom_call" | custom-call | flops 1610612736 | bytes 8388608 | tf_op jit(solution)/shard_map/turn/pallas_call | solution.py:221
  10.7 0.0 collective-permute-done.refs_1_
  10.7 0.0 collective-permute-done.1.refs_2_
  10.7 0.1 collective-permute-done.2.refs_3_
  10.8 0.4 %states.1.refs_8_.refs_0_ = bf16[16,3200]{1,0:T(8,128)(2,1)S(1)} custom-call(s32[1,8]{1,0:T(1,128)S(1)} %get-tuple-element.26.refs_0_, s32[1,8]{1,0:T(1,128)S(1)} %bitcast.9, s32[1,8]{1,0:T(1,128)S(1)} %bitcast.10, s32[1,8]{1,0:T(1,128)S(1)} %bitcast.11, bf16[16,128]{1,0:T(8,128)(2,1)S(1)} %get-tuple-element.27.refs_4_, ...), custom_call_target="tpu_custom_call" | custom-call | flops 12582912 | bytes 1048576 | tf_op jit(solution)/shard_map/states/pallas_call | solution.py:249
  11.2 0.6 %collective-permute-start.3 = (bf16[16,3200]{1,0:T(8,128)(2,1)S(1)}, bf16[16,3200]{1,0:T(8,128)(2,1)S(1)}, u32[]{:S(2)}, u32[]{:S(2)}) collective-permute-start(bf16[16,3200]{1,0:T(8,128)(2,1)S(1)} %states.1.refs_8_.refs_0_), channel_id=1, source_target_pairs={{0,4},{4,8},{8,12},{12,0},{1,5},{5,9},{9,13},{13,1},{2,6},{6,10},{... | collective-permute-start | bytes 307208 | tf_op jit(solution)/shard_map/states/ppermute | solution.py:193
  11.8 3.1 %collective-permute-start.6 = (bf16[16,3200]{1,0:T(8,128)(2,1)S(1)}, bf16[16,3200]{1,0:T(8,128)(2,1)S(1)}, u32[]{:S(2)}, u32[]{:S(2)}) collective-permute-start(bf16[16,3200]{1,0:T(8,128)(2,1)S(1)} %states.1.refs_8_.refs_0_), channel_id=1, source_target_pairs={{0,8},{4,12},{8,0},{12,4},{1,9},{5,13},{9,1},{13,5},{2,10},{6,14},... | collective-permute-start | bytes 307208 | tf_op jit(solution)/shard_map/states/ppermute | solution.py:193
  14.9 0.1 collective-permute-start.8
  15.1 0.0 copy-start
  15.1 4.4 %pairs.1 = (f32[1,128]{1,0:T(1,128)S(1)}, s32[4,128]{1,0:T(4,128)S(1)}) custom-call(s32[8]{0:T(128)} %refs_0_.1, s32[8]{0:T(128)S(1)} %collective-permute-done.refs_1_, s32[8]{0:T(128)S(1)} %collective-permute-done.1.refs_2_, s32[8]{0:T(128)S(1)} %collective-permute-done.2.refs_3_, s32[2,256]{1,0:T(2,128)} %bitcast.13, ...), custom_call_target="tpu_custom_call" | custom-call | flops 4294967296 | bytes 4194304 | tf_op jit(solution)/shard_map/pairs/pallas_call | solution.py:260
  19.4 0.6 %collective-permute-start.5 = (f32[1,128]{1,0:T(1,128)S(1)}, f32[1,128]{1,0:T(1,128)S(1)}, u32[]{:S(2)}, u32[]{:S(2)}) collective-permute-start(f32[1,128]{1,0:T(1,128)S(1)} %get-tuple-element.31.refs_0_), channel_id=1, source_target_pairs={{0,2},{1,3},{2,0},{3,1},{4,6},{5,7},{6,4},{7,5},{8,10},{9,11},{10,... | collective-permute-start | bytes 1544 | tf_op jit(solution)/shard_map/pairs/ppermute | solution.py:286
  20.0 0.0 collective-permute-done.3.refs_1_
  20.0 0.0 collective-permute-start.4
  20.1 0.9 %collective-permute-done.6.refs_2_ = bf16[16,3200]{1,0:T(8,128)(2,1)S(1)} collective-permute-done((bf16[16,3200]{1,0:T(8,128)(2,1)S(1)}, bf16[16,3200]{1,0:T(8,128)(2,1)S(1)}, u32[]{:S(2)}, u32[]{:S(2)}) %collective-permute-start.6) | collective-permute-done | bytes 102432 | tf_op jit(solution)/shard_map/states/ppermute | solution.py:193
  21.0 0.7 %collective-permute-start.7 = (f32[1,128]{1,0:T(1,128)S(1)}, f32[1,128]{1,0:T(1,128)S(1)}, u32[]{:S(2)}, u32[]{:S(2)}) collective-permute-start(f32[1,128]{1,0:T(1,128)S(1)} %get-tuple-element.31.refs_0_), channel_id=1, source_target_pairs={{0,3},{1,2},{2,1},{3,0},{4,7},{5,6},{6,5},{7,4},{8,11},{9,10},{10,... | collective-permute-start | bytes 1544 | tf_op jit(solution)/shard_map/pairs/ppermute | solution.py:286
  21.7 0.0 collective-permute-done.8.refs_3_
  21.7 0.0 collective-permute-done.9.refs_5_
  21.7 0.0 copy-done
  21.7 0.9 %scores.2 = (f32[4,128]{1,0:T(4,128)S(1)}, bf16[256,512]{1,0:T(8,128)(2,1)S(1)}) custom-call(bf16[16,3200]{1,0:T(8,128)(2,1)S(1)} %states.1.refs_8_.refs_0_, bf16[16,3200]{1,0:T(8,128)(2,1)S(1)} %collective-permute-done.3.refs_1_, bf16[16,3200]{1,0:T(8,128)(2,1)S(1)} %collective-permute-done.6.refs_2_, bf16[16,3200]{1,0:T(8,128)(2,1)S(1)} %collective-permute-done.8.refs_3_, ...), custom_call_target="tpu_custom_call" | custom-call | flops 100663296 | bytes 2097152 | tf_op jit(solution)/shard_map/scores/pallas_call | solution.py:290
  22.5 0.5 %collective-permute-done.5.refs_2_ = f32[1,128]{1,0:T(1,128)S(1)} collective-permute-done((f32[1,128]{1,0:T(1,128)S(1)}, f32[1,128]{1,0:T(1,128)S(1)}, u32[]{:S(2)}, u32[]{:S(2)}) %collective-permute-start.5) | collective-permute-done | bytes 544 | tf_op jit(solution)/shard_map/pairs/ppermute | solution.py:286
  23.0 0.0 collective-permute-done.4.refs_1_
  23.1 0.9 %collective-permute-done.7.refs_3_ = f32[1,128]{1,0:T(1,128)S(1)} collective-permute-done((f32[1,128]{1,0:T(1,128)S(1)}, f32[1,128]{1,0:T(1,128)S(1)}, u32[]{:S(2)}, u32[]{:S(2)}) %collective-permute-start.7) | collective-permute-done | bytes 544 | tf_op jit(solution)/shard_map/pairs/ppermute | solution.py:286
  24.0 0.2 scores.3
  24.1 1.1 %collective-permute-start.12 = (f32[1,128]{1,0:T(1,128)S(1)}, f32[1,128]{1,0:T(1,128)S(1)}, u32[]{:S(2)}, u32[]{:S(2)}) collective-permute-start(f32[1,128]{1,0:T(1,128)S(1)} %get-tuple-element.40), channel_id=1, source_target_pairs={{0,4},{4,8},{8,12},{12,0},{1,5},{5,9},{9,13},{13,1},{2,6},{6,10},{... | collective-permute-start | bytes 1544 | tf_op jit(solution)/shard_map/back/ppermute | solution.py:193
  25.2 2.8 %collective-permute-start.11 = (f32[1,128]{1,0:T(1,128)S(1)}, f32[1,128]{1,0:T(1,128)S(1)}, u32[]{:S(2)}, u32[]{:S(2)}) collective-permute-start(f32[1,128]{1,0:T(1,128)S(1)} %get-tuple-element.39), channel_id=1, source_target_pairs={{0,8},{4,12},{8,0},{12,4},{1,9},{5,13},{9,1},{13,5},{2,10},{6,14},... | collective-permute-start | bytes 1544 | tf_op jit(solution)/shard_map/back/ppermute | solution.py:193
  28.0 0.3 collective-permute-start.10
  28.3 1.2 %collective-permute-done.12 = f32[1,128]{1,0:T(1,128)S(1)} collective-permute-done((f32[1,128]{1,0:T(1,128)S(1)}, f32[1,128]{1,0:T(1,128)S(1)}, u32[]{:S(2)}, u32[]{:S(2)}) %collective-permute-start.12) | collective-permute-done | bytes 544 | tf_op jit(solution)/shard_map/back/ppermute | solution.py:193
  29.5 0.1 collective-permute-done.11
  29.7 1.9 %collective-permute-done.10 = f32[1,128]{1,0:T(1,128)S(1)} collective-permute-done((f32[1,128]{1,0:T(1,128)S(1)}, f32[1,128]{1,0:T(1,128)S(1)}, u32[]{:S(2)}, u32[]{:S(2)}) %collective-permute-start.10) | collective-permute-done | bytes 544 | tf_op jit(solution)/shard_map/back/ppermute | solution.py:193
  31.6 0.5 %add_bitcast_fusion = f32[128]{0:T(128)} fusion(f32[1,128]{1,0:T(1,128)S(1)} %collective-permute-done.12, f32[1,128]{1,0:T(1,128)S(1)} %collective-permute-done.11, f32[1,128]{1,0:T(1,128)S(1)} %get-tuple-element.37, f32[1,128]{1,0:T(1,128)S(1)} %collective-permute-done.10), kind=kLoop, calls=%fused_computation | loop fusion | flops 384 | bytes 2560 | tf_op jit(solution)/shard_map/reshape | solution.py:318
Async XLA Ops:
  0.0 21.7 %collective-permute-start.9 = (bf16[128,3072]{1,0:T(8,128)(2,1)}, bf16[128,3072]{1,0:T(8,128)(2,1)S(1)}, u32[]{:S(2)}, u32[]{:S(2)}) collective-permute-start(bf16[128,3072]{1,0:T(8,128)(2,1)} %refs_4_.1), channel_id=1, source_target_pairs={{0,2},{2,0},{1,3},{3,1},{4,6},{6,4},{5,7},{7,5},{8,10},{10,8},{9,1... | collective-permute-start | bytes 2359304 | tf_op jit(solution)/shard_map/item_rows/ppermute | solution.py:193
  2.9 7.7 %collective-permute-start = (s32[8]{0:T(128)}, s32[8]{0:T(128)S(1)}, u32[]{:S(2)}, u32[]{:S(2)}) collective-permute-start(s32[8]{0:T(128)} %refs_0_.1), channel_id=1, source_target_pairs={{0,4},{4,8},{8,12},{12,0},{1,5},{5,9},{9,13},{13,1},{2,6},{6,10},{... | collective-permute-start | bytes 104 | tf_op jit(solution)/shard_map/ids/ppermute | solution.py:193
  4.5 6.2 %collective-permute-start.1 = (s32[8]{0:T(128)}, s32[8]{0:T(128)S(1)}, u32[]{:S(2)}, u32[]{:S(2)}) collective-permute-start(s32[8]{0:T(128)} %refs_0_.1), channel_id=1, source_target_pairs={{0,8},{4,12},{8,0},{12,4},{1,9},{5,13},{9,1},{13,5},{2,10},{6,14},... | collective-permute-start | bytes 104 | tf_op jit(solution)/shard_map/ids/ppermute | solution.py:193
  7.1 3.7 %collective-permute-start.2 = (s32[8]{0:T(128)}, s32[8]{0:T(128)S(1)}, u32[]{:S(2)}, u32[]{:S(2)}) collective-permute-start(s32[8]{0:T(128)} %refs_0_.1), channel_id=1, source_target_pairs={{0,12},{4,0},{8,4},{12,8},{1,13},{5,1},{9,5},{13,9},{2,14},{6,2},{... | collective-permute-start | bytes 104 | tf_op jit(solution)/shard_map/ids/ppermute | solution.py:193
  11.2 8.9 %collective-permute-start.3 = (bf16[16,3200]{1,0:T(8,128)(2,1)S(1)}, bf16[16,3200]{1,0:T(8,128)(2,1)S(1)}, u32[]{:S(2)}, u32[]{:S(2)}) collective-permute-start(bf16[16,3200]{1,0:T(8,128)(2,1)S(1)} %states.1.refs_8_.refs_0_), channel_id=1, source_target_pairs={{0,4},{4,8},{8,12},{12,0},{1,5},{5,9},{9,13},{13,1},{2,6},{6,10},{... | collective-permute-start | bytes 307208 | tf_op jit(solution)/shard_map/states/ppermute | solution.py:193
  11.8 9.2 %collective-permute-start.6 = (bf16[16,3200]{1,0:T(8,128)(2,1)S(1)}, bf16[16,3200]{1,0:T(8,128)(2,1)S(1)}, u32[]{:S(2)}, u32[]{:S(2)}) collective-permute-start(bf16[16,3200]{1,0:T(8,128)(2,1)S(1)} %states.1.refs_8_.refs_0_), channel_id=1, source_target_pairs={{0,8},{4,12},{8,0},{12,4},{1,9},{5,13},{9,1},{13,5},{2,10},{6,14},... | collective-permute-start | bytes 307208 | tf_op jit(solution)/shard_map/states/ppermute | solution.py:193
  14.9 6.7 %collective-permute-start.8 = (bf16[16,3200]{1,0:T(8,128)(2,1)S(1)}, bf16[16,3200]{1,0:T(8,128)(2,1)S(1)}, u32[]{:S(2)}, u32[]{:S(2)}) collective-permute-start(bf16[16,3200]{1,0:T(8,128)(2,1)S(1)} %states.1.refs_8_.refs_0_), channel_id=1, source_target_pairs={{0,12},{4,0},{8,4},{12,8},{1,13},{5,1},{9,5},{13,9},{2,14},{6,2},{... | collective-permute-start | bytes 307208 | tf_op jit(solution)/shard_map/states/ppermute | solution.py:193
  15.1 6.6 %copy-start = (bf16[128,3072]{1,0:T(8,128)(2,1)S(1)}, bf16[128,3072]{1,0:T(8,128)(2,1)}, u32[]{:S(2)}) copy-start(bf16[128,3072]{1,0:T(8,128)(2,1)} %refs_4_.1) | copy-start | bytes 2359300
  19.4 3.6 %collective-permute-start.5 = (f32[1,128]{1,0:T(1,128)S(1)}, f32[1,128]{1,0:T(1,128)S(1)}, u32[]{:S(2)}, u32[]{:S(2)}) collective-permute-start(f32[1,128]{1,0:T(1,128)S(1)} %get-tuple-element.31.refs_0_), channel_id=1, source_target_pairs={{0,2},{1,3},{2,0},{3,1},{4,6},{5,7},{6,4},{7,5},{8,10},{9,11},{10,... | collective-permute-start | bytes 1544 | tf_op jit(solution)/shard_map/pairs/ppermute | solution.py:286
  20.0 3.0 %collective-permute-start.4 = (f32[1,128]{1,0:T(1,128)S(1)}, f32[1,128]{1,0:T(1,128)S(1)}, u32[]{:S(2)}, u32[]{:S(2)}) collective-permute-start(f32[1,128]{1,0:T(1,128)S(1)} %get-tuple-element.31.refs_0_), channel_id=1, source_target_pairs={{0,1},{1,0},{2,3},{3,2},{4,5},{5,4},{6,7},{7,6},{8,9},{9,8},{10,11... | collective-permute-start | bytes 1544 | tf_op jit(solution)/shard_map/pairs/ppermute | solution.py:286
  21.0 3.0 %collective-permute-start.7 = (f32[1,128]{1,0:T(1,128)S(1)}, f32[1,128]{1,0:T(1,128)S(1)}, u32[]{:S(2)}, u32[]{:S(2)}) collective-permute-start(f32[1,128]{1,0:T(1,128)S(1)} %get-tuple-element.31.refs_0_), channel_id=1, source_target_pairs={{0,3},{1,2},{2,1},{3,0},{4,7},{5,6},{6,5},{7,4},{8,11},{9,10},{10,... | collective-permute-start | bytes 1544 | tf_op jit(solution)/shard_map/pairs/ppermute | solution.py:286
  24.1 5.4 %collective-permute-start.12 = (f32[1,128]{1,0:T(1,128)S(1)}, f32[1,128]{1,0:T(1,128)S(1)}, u32[]{:S(2)}, u32[]{:S(2)}) collective-permute-start(f32[1,128]{1,0:T(1,128)S(1)} %get-tuple-element.40), channel_id=1, source_target_pairs={{0,4},{4,8},{8,12},{12,0},{1,5},{5,9},{9,13},{13,1},{2,6},{6,10},{... | collective-permute-start | bytes 1544 | tf_op jit(solution)/shard_map/back/ppermute | solution.py:193
  25.2 4.4 %collective-permute-start.11 = (f32[1,128]{1,0:T(1,128)S(1)}, f32[1,128]{1,0:T(1,128)S(1)}, u32[]{:S(2)}, u32[]{:S(2)}) collective-permute-start(f32[1,128]{1,0:T(1,128)S(1)} %get-tuple-element.39), channel_id=1, source_target_pairs={{0,8},{4,12},{8,0},{12,4},{1,9},{5,13},{9,1},{13,5},{2,10},{6,14},... | collective-permute-start | bytes 1544 | tf_op jit(solution)/shard_map/back/ppermute | solution.py:193
  28.0 3.5 %collective-permute-start.10 = (f32[1,128]{1,0:T(1,128)S(1)}, f32[1,128]{1,0:T(1,128)S(1)}, u32[]{:S(2)}, u32[]{:S(2)}) collective-permute-start(f32[1,128]{1,0:T(1,128)S(1)} %get-tuple-element.38), channel_id=1, source_target_pairs={{0,12},{4,0},{8,4},{12,8},{1,13},{5,1},{9,5},{13,9},{2,14},{6,2},{... | collective-permute-start | bytes 1544 | tf_op jit(solution)/shard_map/back/ppermute | solution.py:193

commit v18 on v17

--- a/solution.py
+++ b/solution.py
@@ -275,14 +275,16 @@
             cost_estimate=pl.CostEstimate(flops=2 * count * K * K * rows * 16, bytes_accessed=4 * 1024 * 1024, transcendentals=0),
         )(*users, in_hbm(pair_fields.T), *turned, picked)
         pair_scores = {(0, 0): pair_parts}
-        steps = [(q, h) for q in range(planes - 1, -1, -1) for h in range(parts) if q or h]
-        for q, h in sorted(steps, key=lambda step: bool(step[0] and step[1])):
+        steps = [(q, h) for q in range(planes) for h in range(parts) if q or h]
+        for q, h in steps:
             perm = [
                 (c * parts + d, (c + q) % planes * parts + (d + h) % parts) for c in range(planes) for d in range(parts)
             ]
-            source, after = pair_parts, {1: 1, 2: 2}.get(len(pair_scores) - 1, 0)
-            if after:
-                source, states[after] = lax.optimization_barrier((pair_parts, states[after]))
+            source = pair_parts
+            if len(pair_scores) == 2:
+                source, states[1] = lax.optimization_barrier((pair_parts, states[1]))
+            if len(pair_scores) == 3:
+                source, pair_scores[0, 1] = lax.optimization_barrier((pair_parts, pair_scores[0, 1]))
             pair_scores[q, h] = lax.ppermute(source, ("cache", "pair"), perm)
         pair_scores = [pair_scores[q, h] for q in range(planes) for h in range(parts)]
 

time: 32.2 us -> 31.8 us (0.988)
  waiting for transfers between devices: 5.73 us -> 3.74 us
  starting transfers between devices: 17.8 us -> 19.3 us
    ppermute x10, waiting for transfers between devices: 4.33 us -> 1.49 us  [shift(): return lax.ppermute(x, axis, [(s, (s + step) % size) for s in range(size)])]
    ppermute x10, starting transfers between devices: 16.5 us -> 17.4 us  [shift(): return lax.ppermute(x, axis, [(s, (s + step) % size) for s in range(size)])]
    ppermute x3, waiting for transfers between devices: 1.41 us -> 2.25 us  [body(): pair_scores[q, h] = lax.ppermute(source, ('cache', 'pair'), perm)]
    ppermute x3, starting transfers between devices: 1.27 us -> 1.91 us  [body(): pair_scores[q, h] = lax.ppermute(source, ('cache', 'pair'), perm)]
  transfers between devices with their start and end apart: 13 -> 13, of which waited for: 7 -> 6; matrix products, arithmetic and copies ran while one was open for 0% -> 0% of each run, Pallas kernels for 24% -> 25%
where the time goes in v18:
time: 31.8 us; the launch traced here: 31.6 us
  starting transfers between devices  19.3 us (61%)
  Pallas kernels  8.02 us (25%)
  waiting for transfers between devices  3.74 us (12%)
  other arithmetic  0.52 us (2%)
    ppermute x10, starting transfers between devices, shift(): return lax.ppermute(x, axis, [(s, (s + step) % size) for s in range(size)])  17.4 us
    pallas_call x1, Pallas kernels, body(): pl.pallas_call(functools.partial(pair_kernel, total, cap, slots, user_sta...  4.38 us
    ppermute x3, waiting for transfers between devices, body(): pair_scores[q, h] = lax.ppermute(source, ('cache', 'pair'), perm)  2.25 us
    pallas_call x1, Pallas kernels, body(): pl.pallas_call(turn_kernel, out_shape=(jax.ShapeDtypeStruct((width, rows)...  2.2 us
    ppermute x3, starting transfers between devices, body(): pair_scores[q, h] = lax.ppermute(source, ('cache', 'pair'), perm)  1.91 us
    ppermute x10, waiting for transfers between devices, shift(): return lax.ppermute(x, axis, [(s, (s + step) % size) for s in range(size)])  1.49 us
    pallas_call x1, Pallas kernels, body(): pl.pallas_call(functools.partial(linear_kernel, total, planes), out_shape...  0.89 us
  transfers between devices with their start and end apart: 13, of which 6 were waited for; matrix products, arithmetic and copies ran while one was open for 0% of the time, Pallas kernels for 25%

profile of v18, /device:TPU:0, one launch (start us, length us, event | category | flops | bytes accessed | tf_op | source)
XLA Modules:
  0.0 31.6 jit_solution(16291596608918865863)
XLA Ops:
  0.0 2.9 %collective-permute-start.9 = (bf16[128,3072]{1,0:T(8,128)(2,1)}, bf16[128,3072]{1,0:T(8,128)(2,1)S(1)}, u32[]{:S(2)}, u32[]{:S(2)}) collective-permute-start(bf16[128,3072]{1,0:T(8,128)(2,1)} %refs_4_.1), channel_id=1, source_target_pairs={{0,2},{2,0},{1,3},{3,1},{4,6},{6,4},{5,7},{7,5},{8,10},{10,8},{9,1... | collective-permute-start | bytes 2359304 | tf_op jit(solution)/shard_map/item_rows/ppermute | solution.py:193
  2.9 1.6 %collective-permute-start = (s32[8]{0:T(128)}, s32[8]{0:T(128)S(1)}, u32[]{:S(2)}, u32[]{:S(2)}) collective-permute-start(s32[8]{0:T(128)} %refs_0_.1), channel_id=1, source_target_pairs={{0,4},{4,8},{8,12},{12,0},{1,5},{5,9},{9,13},{13,1},{2,6},{6,10},{... | collective-permute-start | bytes 104 | tf_op jit(solution)/shard_map/ids/ppermute | solution.py:193
  4.5 2.6 %collective-permute-start.1 = (s32[8]{0:T(128)}, s32[8]{0:T(128)S(1)}, u32[]{:S(2)}, u32[]{:S(2)}) collective-permute-start(s32[8]{0:T(128)} %refs_0_.1), channel_id=1, source_target_pairs={{0,8},{4,12},{8,0},{12,4},{1,9},{5,13},{9,1},{13,5},{2,10},{6,14},... | collective-permute-start | bytes 104 | tf_op jit(solution)/shard_map/ids/ppermute | solution.py:193
  7.1 1.3 %collective-permute-start.2 = (s32[8]{0:T(128)}, s32[8]{0:T(128)S(1)}, u32[]{:S(2)}, u32[]{:S(2)}) collective-permute-start(s32[8]{0:T(128)} %refs_0_.1), channel_id=1, source_target_pairs={{0,12},{4,0},{8,4},{12,8},{1,13},{5,1},{9,5},{13,9},{2,14},{6,2},{... | collective-permute-start | bytes 104 | tf_op jit(solution)/shard_map/ids/ppermute | solution.py:193
  8.5 2.2 %turn.1 = (f32[3072,128]{1,0:T(8,128)S(1)}, bf16[3072,128]{1,0:T(8,128)(2,1)S(1)}, bf16[64,64,256]{2,1,0:T(8,128)(2,1)S(1)}, bf16[128,3072]{1,0:T(8,128)(2,1)S(1...) custom-call(bf16[128,3072]{1,0:T(8,128)(2,1)} %refs_4_.1, bf16[64,64,256]{2,1,0:T(8,128)(2,1)} %bitcast.12, ...), custom_call_target="tpu_custom_call" | custom-call | flops 1610612736 | bytes 8388608 | tf_op jit(solution)/shard_map/turn/pallas_call | solution.py:221
  10.7 0.0 collective-permute-done.refs_1_
  10.7 0.0 collective-permute-done.1.refs_2_
  10.7 0.1 collective-permute-done.2.refs_3_
  10.8 0.4 %states.1.refs_8_.refs_0_ = bf16[16,3200]{1,0:T(8,128)(2,1)S(1)} custom-call(s32[1,8]{1,0:T(1,128)S(1)} %get-tuple-element.26.refs_0_, s32[1,8]{1,0:T(1,128)S(1)} %bitcast.9, s32[1,8]{1,0:T(1,128)S(1)} %bitcast.10, s32[1,8]{1,0:T(1,128)S(1)} %bitcast.11, bf16[16,128]{1,0:T(8,128)(2,1)S(1)} %get-tuple-element.27.refs_4_, ...), custom_call_target="tpu_custom_call" | custom-call | flops 12582912 | bytes 1048576 | tf_op jit(solution)/shard_map/states/pallas_call | solution.py:249
  11.2 0.6 %collective-permute-start.4 = (bf16[16,3200]{1,0:T(8,128)(2,1)S(1)}, bf16[16,3200]{1,0:T(8,128)(2,1)S(1)}, u32[]{:S(2)}, u32[]{:S(2)}) collective-permute-start(bf16[16,3200]{1,0:T(8,128)(2,1)S(1)} %states.1.refs_8_.refs_0_), channel_id=1, source_target_pairs={{0,4},{4,8},{8,12},{12,0},{1,5},{5,9},{9,13},{13,1},{2,6},{6,10},{... | collective-permute-start | bytes 307208 | tf_op jit(solution)/shard_map/states/ppermute | solution.py:193
  11.8 3.1 %collective-permute-start.7 = (bf16[16,3200]{1,0:T(8,128)(2,1)S(1)}, bf16[16,3200]{1,0:T(8,128)(2,1)S(1)}, u32[]{:S(2)}, u32[]{:S(2)}) collective-permute-start(bf16[16,3200]{1,0:T(8,128)(2,1)S(1)} %states.1.refs_8_.refs_0_), channel_id=1, source_target_pairs={{0,8},{4,12},{8,0},{12,4},{1,9},{5,13},{9,1},{13,5},{2,10},{6,14},... | collective-permute-start | bytes 307208 | tf_op jit(solution)/shard_map/states/ppermute | solution.py:193
  14.9 0.1 collective-permute-start.8
  15.1 0.0 copy-start
  15.1 4.4 %pairs.1 = (f32[1,128]{1,0:T(1,128)S(1)}, s32[4,128]{1,0:T(4,128)S(1)}) custom-call(s32[8]{0:T(128)} %refs_0_.1, s32[8]{0:T(128)S(1)} %collective-permute-done.refs_1_, s32[8]{0:T(128)S(1)} %collective-permute-done.1.refs_2_, s32[8]{0:T(128)S(1)} %collective-permute-done.2.refs_3_, s32[2,256]{1,0:T(2,128)} %bitcast.13, ...), custom_call_target="tpu_custom_call" | custom-call | flops 4294967296 | bytes 4194304 | tf_op jit(solution)/shard_map/pairs/pallas_call | solution.py:260
  19.4 0.1 collective-permute-start.3
  19.5 1.1 %collective-permute-done.3.refs_1_ = f32[1,128]{1,0:T(1,128)S(1)} collective-permute-done((f32[1,128]{1,0:T(1,128)S(1)}, f32[1,128]{1,0:T(1,128)S(1)}, u32[]{:S(2)}, u32[]{:S(2)}) %collective-permute-start.3) | collective-permute-done | bytes 544 | tf_op jit(solution)/shard_map/pairs/ppermute | solution.py:288
  20.6 0.3 %collective-permute-start.6 = (f32[1,128]{1,0:T(1,128)S(1)}, f32[1,128]{1,0:T(1,128)S(1)}, u32[]{:S(2)}, u32[]{:S(2)}) collective-permute-start(f32[1,128]{1,0:T(1,128)S(1)} %get-tuple-element.32.refs_0_), channel_id=1, source_target_pairs={{0,3},{1,2},{2,1},{3,0},{4,7},{5,6},{6,5},{7,4},{8,11},{9,10},{10,... | collective-permute-start | bytes 1544 | tf_op jit(solution)/shard_map/pairs/ppermute | solution.py:288
  21.0 0.0 collective-permute-done.4.refs_1_
  21.0 1.5 %collective-permute-start.5 = (f32[1,128]{1,0:T(1,128)S(1)}, f32[1,128]{1,0:T(1,128)S(1)}, u32[]{:S(2)}, u32[]{:S(2)}) collective-permute-start(f32[1,128]{1,0:T(1,128)S(1)} %get-tuple-element.32.refs_0_), channel_id=1, source_target_pairs={{0,2},{1,3},{2,0},{3,1},{4,6},{5,7},{6,4},{7,5},{8,10},{9,11},{10,... | collective-permute-start | bytes 1544 | tf_op jit(solution)/shard_map/pairs/ppermute | solution.py:288
  22.5 0.0 collective-permute-done.7.refs_2_
  22.5 0.0 collective-permute-done.8.refs_3_
  22.5 0.0 collective-permute-done.9.refs_5_
  22.5 0.0 copy-done
  22.5 0.9 %scores.2 = (f32[4,128]{1,0:T(4,128)S(1)}, bf16[256,512]{1,0:T(8,128)(2,1)S(1)}) custom-call(bf16[16,3200]{1,0:T(8,128)(2,1)S(1)} %states.1.refs_8_.refs_0_, bf16[16,3200]{1,0:T(8,128)(2,1)S(1)} %collective-permute-done.4.refs_1_, bf16[16,3200]{1,0:T(8,128)(2,1)S(1)} %collective-permute-done.7.refs_2_, bf16[16,3200]{1,0:T(8,128)(2,1)S(1)} %collective-permute-done.8.refs_3_, ...), custom_call_target="tpu_custom_call" | custom-call | flops 100663296 | bytes 2097152 | tf_op jit(solution)/shard_map/scores/pallas_call | solution.py:292
  23.4 0.2 collective-permute-done.6.refs_3_
  23.6 0.9 %collective-permute-done.5.refs_2_ = f32[1,128]{1,0:T(1,128)S(1)} collective-permute-done((f32[1,128]{1,0:T(1,128)S(1)}, f32[1,128]{1,0:T(1,128)S(1)}, u32[]{:S(2)}, u32[]{:S(2)}) %collective-permute-start.5) | collective-permute-done | bytes 544 | tf_op jit(solution)/shard_map/pairs/ppermute | solution.py:288
  24.5 0.2 scores.3
  24.7 2.0 %collective-permute-start.12 = (f32[1,128]{1,0:T(1,128)S(1)}, f32[1,128]{1,0:T(1,128)S(1)}, u32[]{:S(2)}, u32[]{:S(2)}) collective-permute-start(f32[1,128]{1,0:T(1,128)S(1)} %get-tuple-element.40), channel_id=1, source_target_pairs={{0,4},{4,8},{8,12},{12,0},{1,5},{5,9},{9,13},{13,1},{2,6},{6,10},{... | collective-permute-start | bytes 1544 | tf_op jit(solution)/shard_map/back/ppermute | solution.py:193
  26.7 0.2 collective-permute-start.11
  26.9 2.8 %collective-permute-start.10 = (f32[1,128]{1,0:T(1,128)S(1)}, f32[1,128]{1,0:T(1,128)S(1)}, u32[]{:S(2)}, u32[]{:S(2)}) collective-permute-start(f32[1,128]{1,0:T(1,128)S(1)} %get-tuple-element.38), channel_id=1, source_target_pairs={{0,12},{4,0},{8,4},{12,8},{1,13},{5,1},{9,5},{13,9},{2,14},{6,2},{... | collective-permute-start | bytes 1544 | tf_op jit(solution)/shard_map/back/ppermute | solution.py:193
  29.7 0.4 %collective-permute-done.12 = f32[1,128]{1,0:T(1,128)S(1)} collective-permute-done((f32[1,128]{1,0:T(1,128)S(1)}, f32[1,128]{1,0:T(1,128)S(1)}, u32[]{:S(2)}, u32[]{:S(2)}) %collective-permute-start.12) | collective-permute-done | bytes 544 | tf_op jit(solution)/shard_map/back/ppermute | solution.py:193
  30.1 1.0 %collective-permute-done.11 = f32[1,128]{1,0:T(1,128)S(1)} collective-permute-done((f32[1,128]{1,0:T(1,128)S(1)}, f32[1,128]{1,0:T(1,128)S(1)}, u32[]{:S(2)}, u32[]{:S(2)}) %collective-permute-start.11) | collective-permute-done | bytes 544 | tf_op jit(solution)/shard_map/back/ppermute | solution.py:193
  31.1 0.0 collective-permute-done.10
  31.1 0.5 %add_bitcast_fusion = f32[128]{0:T(128)} fusion(f32[1,128]{1,0:T(1,128)S(1)} %collective-permute-done.12, f32[1,128]{1,0:T(1,128)S(1)} %collective-permute-done.11, f32[1,128]{1,0:T(1,128)S(1)} %get-tuple-element.37, f32[1,128]{1,0:T(1,128)S(1)} %collective-permute-done.10), kind=kLoop, calls=%fused_computation | loop fusion | flops 384 | bytes 2560 | tf_op jit(solution)/shard_map/reshape | solution.py:320
Async XLA Ops:
  0.0 22.5 %collective-permute-start.9 = (bf16[128,3072]{1,0:T(8,128)(2,1)}, bf16[128,3072]{1,0:T(8,128)(2,1)S(1)}, u32[]{:S(2)}, u32[]{:S(2)}) collective-permute-start(bf16[128,3072]{1,0:T(8,128)(2,1)} %refs_4_.1), channel_id=1, source_target_pairs={{0,2},{2,0},{1,3},{3,1},{4,6},{6,4},{5,7},{7,5},{8,10},{10,8},{9,1... | collective-permute-start | bytes 2359304 | tf_op jit(solution)/shard_map/item_rows/ppermute | solution.py:193
  2.9 7.7 %collective-permute-start = (s32[8]{0:T(128)}, s32[8]{0:T(128)S(1)}, u32[]{:S(2)}, u32[]{:S(2)}) collective-permute-start(s32[8]{0:T(128)} %refs_0_.1), channel_id=1, source_target_pairs={{0,4},{4,8},{8,12},{12,0},{1,5},{5,9},{9,13},{13,1},{2,6},{6,10},{... | collective-permute-start | bytes 104 | tf_op jit(solution)/shard_map/ids/ppermute | solution.py:193
  4.5 6.2 %collective-permute-start.1 = (s32[8]{0:T(128)}, s32[8]{0:T(128)S(1)}, u32[]{:S(2)}, u32[]{:S(2)}) collective-permute-start(s32[8]{0:T(128)} %refs_0_.1), channel_id=1, source_target_pairs={{0,8},{4,12},{8,0},{12,4},{1,9},{5,13},{9,1},{13,5},{2,10},{6,14},... | collective-permute-start | bytes 104 | tf_op jit(solution)/shard_map/ids/ppermute | solution.py:193
  7.1 3.7 %collective-permute-start.2 = (s32[8]{0:T(128)}, s32[8]{0:T(128)S(1)}, u32[]{:S(2)}, u32[]{:S(2)}) collective-permute-start(s32[8]{0:T(128)} %refs_0_.1), channel_id=1, source_target_pairs={{0,12},{4,0},{8,4},{12,8},{1,13},{5,1},{9,5},{13,9},{2,14},{6,2},{... | collective-permute-start | bytes 104 | tf_op jit(solution)/shard_map/ids/ppermute | solution.py:193
  11.2 9.8 %collective-permute-start.4 = (bf16[16,3200]{1,0:T(8,128)(2,1)S(1)}, bf16[16,3200]{1,0:T(8,128)(2,1)S(1)}, u32[]{:S(2)}, u32[]{:S(2)}) collective-permute-start(bf16[16,3200]{1,0:T(8,128)(2,1)S(1)} %states.1.refs_8_.refs_0_), channel_id=1, source_target_pairs={{0,4},{4,8},{8,12},{12,0},{1,5},{5,9},{9,13},{13,1},{2,6},{6,10},{... | collective-permute-start | bytes 307208 | tf_op jit(solution)/shard_map/states/ppermute | solution.py:193
  11.8 10.7 %collective-permute-start.7 = (bf16[16,3200]{1,0:T(8,128)(2,1)S(1)}, bf16[16,3200]{1,0:T(8,128)(2,1)S(1)}, u32[]{:S(2)}, u32[]{:S(2)}) collective-permute-start(bf16[16,3200]{1,0:T(8,128)(2,1)S(1)} %states.1.refs_8_.refs_0_), channel_id=1, source_target_pairs={{0,8},{4,12},{8,0},{12,4},{1,9},{5,13},{9,1},{13,5},{2,10},{6,14},... | collective-permute-start | bytes 307208 | tf_op jit(solution)/shard_map/states/ppermute | solution.py:193
  14.9 7.5 %collective-permute-start.8 = (bf16[16,3200]{1,0:T(8,128)(2,1)S(1)}, bf16[16,3200]{1,0:T(8,128)(2,1)S(1)}, u32[]{:S(2)}, u32[]{:S(2)}) collective-permute-start(bf16[16,3200]{1,0:T(8,128)(2,1)S(1)} %states.1.refs_8_.refs_0_), channel_id=1, source_target_pairs={{0,12},{4,0},{8,4},{12,8},{1,13},{5,1},{9,5},{13,9},{2,14},{6,2},{... | collective-permute-start | bytes 307208 | tf_op jit(solution)/shard_map/states/ppermute | solution.py:193
  15.1 7.4 %copy-start = (bf16[128,3072]{1,0:T(8,128)(2,1)S(1)}, bf16[128,3072]{1,0:T(8,128)(2,1)}, u32[]{:S(2)}) copy-start(bf16[128,3072]{1,0:T(8,128)(2,1)} %refs_4_.1) | copy-start | bytes 2359300
  19.4 1.2 %collective-permute-start.3 = (f32[1,128]{1,0:T(1,128)S(1)}, f32[1,128]{1,0:T(1,128)S(1)}, u32[]{:S(2)}, u32[]{:S(2)}) collective-permute-start(f32[1,128]{1,0:T(1,128)S(1)} %get-tuple-element.32.refs_0_), channel_id=1, source_target_pairs={{0,1},{1,0},{2,3},{3,2},{4,5},{5,4},{6,7},{7,6},{8,9},{9,8},{10,11... | collective-permute-start | bytes 1544 | tf_op jit(solution)/shard_map/pairs/ppermute | solution.py:288
  20.6 3.0 %collective-permute-start.6 = (f32[1,128]{1,0:T(1,128)S(1)}, f32[1,128]{1,0:T(1,128)S(1)}, u32[]{:S(2)}, u32[]{:S(2)}) collective-permute-start(f32[1,128]{1,0:T(1,128)S(1)} %get-tuple-element.32.refs_0_), channel_id=1, source_target_pairs={{0,3},{1,2},{2,1},{3,0},{4,7},{5,6},{6,5},{7,4},{8,11},{9,10},{10,... | collective-permute-start | bytes 1544 | tf_op jit(solution)/shard_map/pairs/ppermute | solution.py:288
  21.0 3.5 %collective-permute-start.5 = (f32[1,128]{1,0:T(1,128)S(1)}, f32[1,128]{1,0:T(1,128)S(1)}, u32[]{:S(2)}, u32[]{:S(2)}) collective-permute-start(f32[1,128]{1,0:T(1,128)S(1)} %get-tuple-element.32.refs_0_), channel_id=1, source_target_pairs={{0,2},{1,3},{2,0},{3,1},{4,6},{5,7},{6,4},{7,5},{8,10},{9,11},{10,... | collective-permute-start | bytes 1544 | tf_op jit(solution)/shard_map/pairs/ppermute | solution.py:288
  24.7 5.4 %collective-permute-start.12 = (f32[1,128]{1,0:T(1,128)S(1)}, f32[1,128]{1,0:T(1,128)S(1)}, u32[]{:S(2)}, u32[]{:S(2)}) collective-permute-start(f32[1,128]{1,0:T(1,128)S(1)} %get-tuple-element.40), channel_id=1, source_target_pairs={{0,4},{4,8},{8,12},{12,0},{1,5},{5,9},{9,13},{13,1},{2,6},{6,10},{... | collective-permute-start | bytes 1544 | tf_op jit(solution)/shard_map/back/ppermute | solution.py:193
  26.7 4.4 %collective-permute-start.11 = (f32[1,128]{1,0:T(1,128)S(1)}, f32[1,128]{1,0:T(1,128)S(1)}, u32[]{:S(2)}, u32[]{:S(2)}) collective-permute-start(f32[1,128]{1,0:T(1,128)S(1)} %get-tuple-element.39), channel_id=1, source_target_pairs={{0,8},{4,12},{8,0},{12,4},{1,9},{5,13},{9,1},{13,5},{2,10},{6,14},... | collective-permute-start | bytes 1544 | tf_op jit(solution)/shard_map/back/ppermute | solution.py:193
  26.9 4.2 %collective-permute-start.10 = (f32[1,128]{1,0:T(1,128)S(1)}, f32[1,128]{1,0:T(1,128)S(1)}, u32[]{:S(2)}, u32[]{:S(2)}) collective-permute-start(f32[1,128]{1,0:T(1,128)S(1)} %get-tuple-element.38), channel_id=1, source_target_pairs={{0,12},{4,0},{8,4},{12,8},{1,13},{5,1},{9,5},{13,9},{2,14},{6,2},{... | collective-permute-start | bytes 1544 | tf_op jit(solution)/shard_map/back/ppermute | solution.py:193

commit v19 on v17

--- a/solution.py
+++ b/solution.py
@@ -178,7 +178,7 @@
 def score_kernel(total, planes, parts, *refs):
     pairs, (linear, hits), outs = refs[:planes * parts], refs[planes * parts:planes * parts + 2], refs[planes * parts + 2:]
     half = linear.shape[1]
-    sums = [sum(pairs[q * parts + h][...] for h in range(parts)) for q in range(planes)]
+    sums = [sum(pairs[(h + 1) * planes - 1 - q][...] for h in range(parts)) for q in range(planes)]
     row = jnp.concatenate(sums, axis=1)
     pieces = jnp.zeros((16, row.shape[1]), jnp.float32)
     for t, part in enumerate(thirds(row)):
@@ -276,7 +276,7 @@
         )(*users, in_hbm(pair_fields.T), *turned, picked)
         pair_scores = {(0, 0): pair_parts}
         steps = [(q, h) for q in range(planes - 1, -1, -1) for h in range(parts) if q or h]
-        for q, h in sorted(steps, key=lambda step: bool(step[0] and step[1])):
+        for q, h in steps:
             perm = [
                 (c * parts + d, (c + q) % planes * parts + (d + h) % parts) for c in range(planes) for d in range(parts)
             ]
@@ -284,7 +284,7 @@
             if after:
                 source, states[after] = lax.optimization_barrier((pair_parts, states[after]))
             pair_scores[q, h] = lax.ppermute(source, ("cache", "pair"), perm)
-        pair_scores = [pair_scores[q, h] for q in range(planes) for h in range(parts)]
+        pair_scores = [pair_scores[q, h] for h in range(parts) for q in range(planes - 1, -1, -1)]
 
     with jax.named_scope("scores"):
         linear, hits = pl.pallas_call(

time: 32.2 us -> 30.5 us (0.947)
  waiting for transfers between devices: 5.73 us -> 3.1 us
  starting transfers between devices: 17.8 us -> 18.6 us
    ppermute x10, waiting for transfers between devices: 4.33 us -> 2.59 us  [shift(): return lax.ppermute(x, axis, [(s, (s + step) % size) for s in range(size)])]
    ppermute x3, waiting for transfers between devices: 1.41 us -> 0.5 us  [body(): pair_scores[q, h] = lax.ppermute(source, ('cache', 'pair'), perm)]
    ppermute x10, starting transfers between devices: 16.5 us -> 17.4 us  [shift(): return lax.ppermute(x, axis, [(s, (s + step) % size) for s in range(size)])]
  transfers between devices with their start and end apart: 13 -> 13, of which waited for: 7 -> 6; matrix products, arithmetic and copies ran while one was open for 0% -> 0% of each run, Pallas kernels for 24% -> 26%
where the time goes in v19:
time: 30.5 us; the launch traced here: 30.3 us
  starting transfers between devices  18.6 us (61%)
  Pallas kernels  8.01 us (26%)
  waiting for transfers between devices  3.1 us (10%)
  other arithmetic  0.52 us (2%)
    ppermute x10, starting transfers between devices, shift(): return lax.ppermute(x, axis, [(s, (s + step) % size) for s in range(size)])  17.4 us
    pallas_call x1, Pallas kernels, body(): pl.pallas_call(functools.partial(pair_kernel, total, cap, slots, user_sta...  4.38 us
    ppermute x10, waiting for transfers between devices, shift(): return lax.ppermute(x, axis, [(s, (s + step) % size) for s in range(size)])  2.59 us
    pallas_call x1, Pallas kernels, body(): pl.pallas_call(turn_kernel, out_shape=(jax.ShapeDtypeStruct((width, rows)...  2.2 us
    ppermute x3, starting transfers between devices, body(): pair_scores[q, h] = lax.ppermute(source, ('cache', 'pair'), perm)  1.27 us
    pallas_call x1, Pallas kernels, body(): pl.pallas_call(functools.partial(linear_kernel, total, planes), out_shape...  0.88 us
  transfers between devices with their start and end apart: 13, of which 6 were waited for; matrix products, arithmetic and copies ran while one was open for 0% of the time, Pallas kernels for 26%

profile of v19, /device:TPU:0, one launch (start us, length us, event | category | flops | bytes accessed | tf_op | source)
XLA Modules:
  0.0 30.3 jit_solution(3598068913218219125)
XLA Ops:
  0.0 2.9 %collective-permute-start.9 = (bf16[128,3072]{1,0:T(8,128)(2,1)}, bf16[128,3072]{1,0:T(8,128)(2,1)S(1)}, u32[]{:S(2)}, u32[]{:S(2)}) collective-permute-start(bf16[128,3072]{1,0:T(8,128)(2,1)} %refs_4_.1), channel_id=1, source_target_pairs={{0,2},{2,0},{1,3},{3,1},{4,6},{6,4},{5,7},{7,5},{8,10},{10,8},{9,1... | collective-permute-start | bytes 2359304 | tf_op jit(solution)/shard_map/item_rows/ppermute | solution.py:193
  2.9 1.6 %collective-permute-start = (s32[8]{0:T(128)}, s32[8]{0:T(128)S(1)}, u32[]{:S(2)}, u32[]{:S(2)}) collective-permute-start(s32[8]{0:T(128)} %refs_0_.1), channel_id=1, source_target_pairs={{0,4},{4,8},{8,12},{12,0},{1,5},{5,9},{9,13},{13,1},{2,6},{6,10},{... | collective-permute-start | bytes 104 | tf_op jit(solution)/shard_map/ids/ppermute | solution.py:193
  4.5 2.6 %collective-permute-start.1 = (s32[8]{0:T(128)}, s32[8]{0:T(128)S(1)}, u32[]{:S(2)}, u32[]{:S(2)}) collective-permute-start(s32[8]{0:T(128)} %refs_0_.1), channel_id=1, source_target_pairs={{0,8},{4,12},{8,0},{12,4},{1,9},{5,13},{9,1},{13,5},{2,10},{6,14},... | collective-permute-start | bytes 104 | tf_op jit(solution)/shard_map/ids/ppermute | solution.py:193
  7.1 1.3 %collective-permute-start.2 = (s32[8]{0:T(128)}, s32[8]{0:T(128)S(1)}, u32[]{:S(2)}, u32[]{:S(2)}) collective-permute-start(s32[8]{0:T(128)} %refs_0_.1), channel_id=1, source_target_pairs={{0,12},{4,0},{8,4},{12,8},{1,13},{5,1},{9,5},{13,9},{2,14},{6,2},{... | collective-permute-start | bytes 104 | tf_op jit(solution)/shard_map/ids/ppermute | solution.py:193
  8.5 2.2 %turn.1 = (f32[3072,128]{1,0:T(8,128)S(1)}, bf16[3072,128]{1,0:T(8,128)(2,1)S(1)}, bf16[64,64,256]{2,1,0:T(8,128)(2,1)S(1)}, bf16[128,3072]{1,0:T(8,128)(2,1)S(1...) custom-call(bf16[128,3072]{1,0:T(8,128)(2,1)} %refs_4_.1, bf16[64,64,256]{2,1,0:T(8,128)(2,1)} %bitcast.12, ...), custom_call_target="tpu_custom_call" | custom-call | flops 1610612736 | bytes 8388608 | tf_op jit(solution)/shard_map/turn/pallas_call | solution.py:221
  10.7 0.0 collective-permute-done.refs_1_
  10.7 0.0 collective-permute-done.1.refs_2_
  10.7 0.1 collective-permute-done.2.refs_3_
  10.8 0.4 %states.1.refs_8_.refs_0_ = bf16[16,3200]{1,0:T(8,128)(2,1)S(1)} custom-call(s32[1,8]{1,0:T(1,128)S(1)} %get-tuple-element.26.refs_0_, s32[1,8]{1,0:T(1,128)S(1)} %bitcast.9, s32[1,8]{1,0:T(1,128)S(1)} %bitcast.10, s32[1,8]{1,0:T(1,128)S(1)} %bitcast.11, bf16[16,128]{1,0:T(8,128)(2,1)S(1)} %get-tuple-element.27.refs_4_, ...), custom_call_target="tpu_custom_call" | custom-call | flops 12582912 | bytes 1048576 | tf_op jit(solution)/shard_map/states/pallas_call | solution.py:249
  11.2 0.6 %collective-permute-start.4 = (bf16[16,3200]{1,0:T(8,128)(2,1)S(1)}, bf16[16,3200]{1,0:T(8,128)(2,1)S(1)}, u32[]{:S(2)}, u32[]{:S(2)}) collective-permute-start(bf16[16,3200]{1,0:T(8,128)(2,1)S(1)} %states.1.refs_8_.refs_0_), channel_id=1, source_target_pairs={{0,4},{4,8},{8,12},{12,0},{1,5},{5,9},{9,13},{13,1},{2,6},{6,10},{... | collective-permute-start | bytes 307208 | tf_op jit(solution)/shard_map/states/ppermute | solution.py:193
  11.8 3.1 %collective-permute-start.6 = (bf16[16,3200]{1,0:T(8,128)(2,1)S(1)}, bf16[16,3200]{1,0:T(8,128)(2,1)S(1)}, u32[]{:S(2)}, u32[]{:S(2)}) collective-permute-start(bf16[16,3200]{1,0:T(8,128)(2,1)S(1)} %states.1.refs_8_.refs_0_), channel_id=1, source_target_pairs={{0,8},{4,12},{8,0},{12,4},{1,9},{5,13},{9,1},{13,5},{2,10},{6,14},... | collective-permute-start | bytes 307208 | tf_op jit(solution)/shard_map/states/ppermute | solution.py:193
  14.9 0.1 collective-permute-start.8
  15.1 0.0 copy-start
  15.1 4.4 %pairs.1 = (f32[1,128]{1,0:T(1,128)S(1)}, s32[4,128]{1,0:T(4,128)S(1)}) custom-call(s32[8]{0:T(128)} %refs_0_.1, s32[8]{0:T(128)S(1)} %collective-permute-done.refs_1_, s32[8]{0:T(128)S(1)} %collective-permute-done.1.refs_2_, s32[8]{0:T(128)S(1)} %collective-permute-done.2.refs_3_, s32[2,256]{1,0:T(2,128)} %bitcast.13, ...), custom_call_target="tpu_custom_call" | custom-call | flops 4294967296 | bytes 4194304 | tf_op jit(solution)/shard_map/pairs/pallas_call | solution.py:260
  19.4 0.6 %collective-permute-start.3 = (f32[1,128]{1,0:T(1,128)S(1)}, f32[1,128]{1,0:T(1,128)S(1)}, u32[]{:S(2)}, u32[]{:S(2)}) collective-permute-start(f32[1,128]{1,0:T(1,128)S(1)} %get-tuple-element.31.refs_1_), channel_id=1, source_target_pairs={{0,2},{1,3},{2,0},{3,1},{4,6},{5,7},{6,4},{7,5},{8,10},{9,11},{10,... | collective-permute-start | bytes 1544 | tf_op jit(solution)/shard_map/pairs/ppermute | solution.py:286
  20.0 0.0 collective-permute-done.4.refs_1_
  20.0 0.0 collective-permute-start.5
  20.1 0.9 %collective-permute-done.6.refs_2_ = bf16[16,3200]{1,0:T(8,128)(2,1)S(1)} collective-permute-done((bf16[16,3200]{1,0:T(8,128)(2,1)S(1)}, bf16[16,3200]{1,0:T(8,128)(2,1)S(1)}, u32[]{:S(2)}, u32[]{:S(2)}) %collective-permute-start.6) | collective-permute-done | bytes 102432 | tf_op jit(solution)/shard_map/states/ppermute | solution.py:193
  21.0 0.7 %collective-permute-start.7 = (f32[1,128]{1,0:T(1,128)S(1)}, f32[1,128]{1,0:T(1,128)S(1)}, u32[]{:S(2)}, u32[]{:S(2)}) collective-permute-start(f32[1,128]{1,0:T(1,128)S(1)} %get-tuple-element.31.refs_1_), channel_id=1, source_target_pairs={{0,1},{1,0},{2,3},{3,2},{4,5},{5,4},{6,7},{7,6},{8,9},{9,8},{10,11... | collective-permute-start | bytes 1544 | tf_op jit(solution)/shard_map/pairs/ppermute | solution.py:286
  21.7 0.0 collective-permute-done.8.refs_3_
  21.7 0.0 collective-permute-done.9.refs_5_
  21.7 0.0 copy-done
  21.7 0.9 %scores.2 = (f32[4,128]{1,0:T(4,128)S(1)}, bf16[256,512]{1,0:T(8,128)(2,1)S(1)}) custom-call(bf16[16,3200]{1,0:T(8,128)(2,1)S(1)} %states.1.refs_8_.refs_0_, bf16[16,3200]{1,0:T(8,128)(2,1)S(1)} %collective-permute-done.4.refs_1_, bf16[16,3200]{1,0:T(8,128)(2,1)S(1)} %collective-permute-done.6.refs_2_, bf16[16,3200]{1,0:T(8,128)(2,1)S(1)} %collective-permute-done.8.refs_3_, ...), custom_call_target="tpu_custom_call" | custom-call | flops 100663296 | bytes 2097152 | tf_op jit(solution)/shard_map/scores/pallas_call | solution.py:290
  22.5 0.5 %collective-permute-done.3.refs_0_ = f32[1,128]{1,0:T(1,128)S(1)} collective-permute-done((f32[1,128]{1,0:T(1,128)S(1)}, f32[1,128]{1,0:T(1,128)S(1)}, u32[]{:S(2)}, u32[]{:S(2)}) %collective-permute-start.3) | collective-permute-done | bytes 544 | tf_op jit(solution)/shard_map/pairs/ppermute | solution.py:286
  23.0 0.0 collective-permute-done.5.refs_2_
  23.1 0.0 collective-permute-done.7.refs_3_
  23.1 0.2 scores.3
  23.2 2.0 %collective-permute-start.12 = (f32[1,128]{1,0:T(1,128)S(1)}, f32[1,128]{1,0:T(1,128)S(1)}, u32[]{:S(2)}, u32[]{:S(2)}) collective-permute-start(f32[1,128]{1,0:T(1,128)S(1)} %get-tuple-element.40), channel_id=1, source_target_pairs={{0,4},{4,8},{8,12},{12,0},{1,5},{5,9},{9,13},{13,1},{2,6},{6,10},{... | collective-permute-start | bytes 1544 | tf_op jit(solution)/shard_map/back/ppermute | solution.py:193
  25.2 1.1 %collective-permute-start.11 = (f32[1,128]{1,0:T(1,128)S(1)}, f32[1,128]{1,0:T(1,128)S(1)}, u32[]{:S(2)}, u32[]{:S(2)}) collective-permute-start(f32[1,128]{1,0:T(1,128)S(1)} %get-tuple-element.39), channel_id=1, source_target_pairs={{0,8},{4,12},{8,0},{12,4},{1,9},{5,13},{9,1},{13,5},{2,10},{6,14},... | collective-permute-start | bytes 1544 | tf_op jit(solution)/shard_map/back/ppermute | solution.py:193
  26.3 2.0 %collective-permute-start.10 = (f32[1,128]{1,0:T(1,128)S(1)}, f32[1,128]{1,0:T(1,128)S(1)}, u32[]{:S(2)}, u32[]{:S(2)}) collective-permute-start(f32[1,128]{1,0:T(1,128)S(1)} %get-tuple-element.38), channel_id=1, source_target_pairs={{0,12},{4,0},{8,4},{12,8},{1,13},{5,1},{9,5},{13,9},{2,14},{6,2},{... | collective-permute-start | bytes 1544 | tf_op jit(solution)/shard_map/back/ppermute | solution.py:193
  28.3 0.4 %collective-permute-done.12 = f32[1,128]{1,0:T(1,128)S(1)} collective-permute-done((f32[1,128]{1,0:T(1,128)S(1)}, f32[1,128]{1,0:T(1,128)S(1)}, u32[]{:S(2)}, u32[]{:S(2)}) %collective-permute-start.12) | collective-permute-done | bytes 544 | tf_op jit(solution)/shard_map/back/ppermute | solution.py:193
  28.6 1.0 %collective-permute-done.11 = f32[1,128]{1,0:T(1,128)S(1)} collective-permute-done((f32[1,128]{1,0:T(1,128)S(1)}, f32[1,128]{1,0:T(1,128)S(1)}, u32[]{:S(2)}, u32[]{:S(2)}) %collective-permute-start.11) | collective-permute-done | bytes 544 | tf_op jit(solution)/shard_map/back/ppermute | solution.py:193
  29.6 0.2 collective-permute-done.10
  29.8 0.5 %add_bitcast_fusion = f32[128]{0:T(128)} fusion(f32[1,128]{1,0:T(1,128)S(1)} %collective-permute-done.12, f32[1,128]{1,0:T(1,128)S(1)} %collective-permute-done.11, f32[1,128]{1,0:T(1,128)S(1)} %get-tuple-element.37, f32[1,128]{1,0:T(1,128)S(1)} %collective-permute-done.10), kind=kLoop, calls=%fused_computation | loop fusion | flops 384 | bytes 2560 | tf_op jit(solution)/shard_map/reshape | solution.py:318
Async XLA Ops:
  0.0 21.7 %collective-permute-start.9 = (bf16[128,3072]{1,0:T(8,128)(2,1)}, bf16[128,3072]{1,0:T(8,128)(2,1)S(1)}, u32[]{:S(2)}, u32[]{:S(2)}) collective-permute-start(bf16[128,3072]{1,0:T(8,128)(2,1)} %refs_4_.1), channel_id=1, source_target_pairs={{0,2},{2,0},{1,3},{3,1},{4,6},{6,4},{5,7},{7,5},{8,10},{10,8},{9,1... | collective-permute-start | bytes 2359304 | tf_op jit(solution)/shard_map/item_rows/ppermute | solution.py:193
  2.9 7.7 %collective-permute-start = (s32[8]{0:T(128)}, s32[8]{0:T(128)S(1)}, u32[]{:S(2)}, u32[]{:S(2)}) collective-permute-start(s32[8]{0:T(128)} %refs_0_.1), channel_id=1, source_target_pairs={{0,4},{4,8},{8,12},{12,0},{1,5},{5,9},{9,13},{13,1},{2,6},{6,10},{... | collective-permute-start | bytes 104 | tf_op jit(solution)/shard_map/ids/ppermute | solution.py:193
  4.5 6.2 %collective-permute-start.1 = (s32[8]{0:T(128)}, s32[8]{0:T(128)S(1)}, u32[]{:S(2)}, u32[]{:S(2)}) collective-permute-start(s32[8]{0:T(128)} %refs_0_.1), channel_id=1, source_target_pairs={{0,8},{4,12},{8,0},{12,4},{1,9},{5,13},{9,1},{13,5},{2,10},{6,14},... | collective-permute-start | bytes 104 | tf_op jit(solution)/shard_map/ids/ppermute | solution.py:193
  7.1 3.7 %collective-permute-start.2 = (s32[8]{0:T(128)}, s32[8]{0:T(128)S(1)}, u32[]{:S(2)}, u32[]{:S(2)}) collective-permute-start(s32[8]{0:T(128)} %refs_0_.1), channel_id=1, source_target_pairs={{0,12},{4,0},{8,4},{12,8},{1,13},{5,1},{9,5},{13,9},{2,14},{6,2},{... | collective-permute-start | bytes 104 | tf_op jit(solution)/shard_map/ids/ppermute | solution.py:193
  11.2 8.9 %collective-permute-start.4 = (bf16[16,3200]{1,0:T(8,128)(2,1)S(1)}, bf16[16,3200]{1,0:T(8,128)(2,1)S(1)}, u32[]{:S(2)}, u32[]{:S(2)}) collective-permute-start(bf16[16,3200]{1,0:T(8,128)(2,1)S(1)} %states.1.refs_8_.refs_0_), channel_id=1, source_target_pairs={{0,4},{4,8},{8,12},{12,0},{1,5},{5,9},{9,13},{13,1},{2,6},{6,10},{... | collective-permute-start | bytes 307208 | tf_op jit(solution)/shard_map/states/ppermute | solution.py:193
  11.8 9.2 %collective-permute-start.6 = (bf16[16,3200]{1,0:T(8,128)(2,1)S(1)}, bf16[16,3200]{1,0:T(8,128)(2,1)S(1)}, u32[]{:S(2)}, u32[]{:S(2)}) collective-permute-start(bf16[16,3200]{1,0:T(8,128)(2,1)S(1)} %states.1.refs_8_.refs_0_), channel_id=1, source_target_pairs={{0,8},{4,12},{8,0},{12,4},{1,9},{5,13},{9,1},{13,5},{2,10},{6,14},... | collective-permute-start | bytes 307208 | tf_op jit(solution)/shard_map/states/ppermute | solution.py:193
  14.9 6.7 %collective-permute-start.8 = (bf16[16,3200]{1,0:T(8,128)(2,1)S(1)}, bf16[16,3200]{1,0:T(8,128)(2,1)S(1)}, u32[]{:S(2)}, u32[]{:S(2)}) collective-permute-start(bf16[16,3200]{1,0:T(8,128)(2,1)S(1)} %states.1.refs_8_.refs_0_), channel_id=1, source_target_pairs={{0,12},{4,0},{8,4},{12,8},{1,13},{5,1},{9,5},{13,9},{2,14},{6,2},{... | collective-permute-start | bytes 307208 | tf_op jit(solution)/shard_map/states/ppermute | solution.py:193
  15.1 6.6 %copy-start = (bf16[128,3072]{1,0:T(8,128)(2,1)S(1)}, bf16[128,3072]{1,0:T(8,128)(2,1)}, u32[]{:S(2)}) copy-start(bf16[128,3072]{1,0:T(8,128)(2,1)} %refs_4_.1) | copy-start | bytes 2359300
  19.4 3.6 %collective-permute-start.3 = (f32[1,128]{1,0:T(1,128)S(1)}, f32[1,128]{1,0:T(1,128)S(1)}, u32[]{:S(2)}, u32[]{:S(2)}) collective-permute-start(f32[1,128]{1,0:T(1,128)S(1)} %get-tuple-element.31.refs_1_), channel_id=1, source_target_pairs={{0,2},{1,3},{2,0},{3,1},{4,6},{5,7},{6,4},{7,5},{8,10},{9,11},{10,... | collective-permute-start | bytes 1544 | tf_op jit(solution)/shard_map/pairs/ppermute | solution.py:286
  20.0 3.0 %collective-permute-start.5 = (f32[1,128]{1,0:T(1,128)S(1)}, f32[1,128]{1,0:T(1,128)S(1)}, u32[]{:S(2)}, u32[]{:S(2)}) collective-permute-start(f32[1,128]{1,0:T(1,128)S(1)} %get-tuple-element.31.refs_1_), channel_id=1, source_target_pairs={{0,3},{1,2},{2,1},{3,0},{4,7},{5,6},{6,5},{7,4},{8,11},{9,10},{10,... | collective-permute-start | bytes 1544 | tf_op jit(solution)/shard_map/pairs/ppermute | solution.py:286
  21.0 2.1 %collective-permute-start.7 = (f32[1,128]{1,0:T(1,128)S(1)}, f32[1,128]{1,0:T(1,128)S(1)}, u32[]{:S(2)}, u32[]{:S(2)}) collective-permute-start(f32[1,128]{1,0:T(1,128)S(1)} %get-tuple-element.31.refs_1_), channel_id=1, source_target_pairs={{0,1},{1,0},{2,3},{3,2},{4,5},{5,4},{6,7},{7,6},{8,9},{9,8},{10,11... | collective-permute-start | bytes 1544 | tf_op jit(solution)/shard_map/pairs/ppermute | solution.py:286
  23.2 5.4 %collective-permute-start.12 = (f32[1,128]{1,0:T(1,128)S(1)}, f32[1,128]{1,0:T(1,128)S(1)}, u32[]{:S(2)}, u32[]{:S(2)}) collective-permute-start(f32[1,128]{1,0:T(1,128)S(1)} %get-tuple-element.40), channel_id=1, source_target_pairs={{0,4},{4,8},{8,12},{12,0},{1,5},{5,9},{9,13},{13,1},{2,6},{6,10},{... | collective-permute-start | bytes 1544 | tf_op jit(solution)/shard_map/back/ppermute | solution.py:193
  25.2 4.4 %collective-permute-start.11 = (f32[1,128]{1,0:T(1,128)S(1)}, f32[1,128]{1,0:T(1,128)S(1)}, u32[]{:S(2)}, u32[]{:S(2)}) collective-permute-start(f32[1,128]{1,0:T(1,128)S(1)} %get-tuple-element.39), channel_id=1, source_target_pairs={{0,8},{4,12},{8,0},{12,4},{1,9},{5,13},{9,1},{13,5},{2,10},{6,14},... | collective-permute-start | bytes 1544 | tf_op jit(solution)/shard_map/back/ppermute | solution.py:193
  26.3 3.5 %collective-permute-start.10 = (f32[1,128]{1,0:T(1,128)S(1)}, f32[1,128]{1,0:T(1,128)S(1)}, u32[]{:S(2)}, u32[]{:S(2)}) collective-permute-start(f32[1,128]{1,0:T(1,128)S(1)} %get-tuple-element.38), channel_id=1, source_target_pairs={{0,12},{4,0},{8,4},{12,8},{1,13},{5,1},{9,5},{13,9},{2,14},{6,2},{... | collective-permute-start | bytes 1544 | tf_op jit(solution)/shard_map/back/ppermute | solution.py:193

commit v20 on v19

--- a/solution.py
+++ b/solution.py
@@ -176,7 +176,7 @@
 
 
 def score_kernel(total, planes, parts, *refs):
-    pairs, (linear, hits), outs = refs[:planes * parts], refs[planes * parts:planes * parts + 2], refs[planes * parts + 2:]
+    pairs, (linear, hits, stays, goes, rows) = refs[:planes * parts], refs[planes * parts:]
     half = linear.shape[1]
     sums = [sum(pairs[(h + 1) * planes - 1 - q][...] for h in range(parts)) for q in range(planes)]
     row = jnp.concatenate(sums, axis=1)
@@ -185,12 +185,27 @@
         pieces = jnp.where(iota(pieces.shape, 0) == t, part.astype(jnp.float32), pieces)
     added = jnp.sum(dot(pieces.astype(jnp.bfloat16), hits[...], NN), axis=0, keepdims=True)
     for j in range(total):
-        outs[j][...] = linear[j:j + 1, :] + added[:, j * half:(j + 1) * half]
+        rows[j:j + 1, :] = linear[j:j + 1, :] + added[:, j * half:(j + 1) * half]
+    me = lax.axis_index("shard")
+    for mask in range(total):
+        target = stays if mask < total // 2 else goes
+        at = mask % (total // 2)
+        target[at:at + 1, :] = rows[pl.ds(ring(me - (me ^ mask), total), 1), :]
+
+
+def halve_kernel(held, came, stays, goes):
+    count = stays.shape[0]
+    stays[...] = held[:count, :] + came[:count, :]
+    goes[...] = held[count:, :] + came[count:, :]
 
 
 def shift(x, axis, step):
     size = lax.axis_size(axis)
     return lax.ppermute(x, axis, [(s, (s + step) % size) for s in range(size)])
+
+
+def swap(x, axis, mask):
+    return lax.ppermute(x, axis, [(s, s ^ mask) for s in range(lax.axis_size(axis))])
 
 
 def body(cand_items, reader_users, item_table, user_states, pair_mats, pair_fields):
@@ -302,20 +317,30 @@
             compiler_params=params,
             cost_estimate=pl.CostEstimate(flops=2 * 64 * 256 * width, bytes_accessed=2 * 1024 * 1024, transcendentals=0),
         )(*states, *items, places)
-        outs = pl.pallas_call(
+        cut = [jax.ShapeDtypeStruct((total // 2, half), jnp.float32)] * 2
+        stays, goes = pl.pallas_call(
             functools.partial(score_kernel, total, planes, parts),
-            out_shape=[jax.ShapeDtypeStruct((1, half), jnp.float32)] * total,
+            out_shape=cut,
             in_specs=[vmem] * (planes * parts + 2),
-            out_specs=[vmem] * total,
+            out_specs=[vmem] * 2,
+            scratch_shapes=[pltpu.VMEM((-(-total // 8) * 8, half), jnp.float32)],
             compiler_params=params,
             cost_estimate=pl.CostEstimate(flops=2 * 16 * 256 * 512, bytes_accessed=512 * 1024, transcendentals=0),
         )(*pair_scores, linear, hits)
 
     with jax.named_scope("back"):
-        result = outs[0]
-        for j in range(1, total):
-            result = result + shift(outs[j], "shard", -j)
-    return result.reshape(half)
+        mask = total // 2
+        while mask > 1:
+            came = swap(goes, "shard", mask)
+            mask //= 2
+            stays, goes = pl.pallas_call(
+                halve_kernel,
+                out_shape=[jax.ShapeDtypeStruct((mask, half), jnp.float32)] * 2,
+                in_specs=[vmem] * 2,
+                out_specs=[vmem] * 2,
+                compiler_params=params,
+            )(stays, came)
+        return (stays + swap(goes, "shard", mask)).reshape(half)
 
 
 def solution(mesh):

time: 30.5 us -> 32 us (1.049)
  waiting for transfers between devices: 3.1 us -> 5.6 us
  starting transfers between devices: 18.6 us -> 17.6 us
    ppermute x10 -> x7, starting transfers between devices: 17.4 us -> 12.3 us  [shift(): return lax.ppermute(x, axis, [(s, (s + step) % size) for s in range(size)])]
    ppermute x0 -> x2, waiting for transfers between devices: none -> 4.04 us  [swap(): lax.ppermute(x, axis, [(s, s ^ mask) for s in range(lax.axis_size(axis))])]
    ppermute x0 -> x2, starting transfers between devices: none -> 4.03 us  [swap(): lax.ppermute(x, axis, [(s, s ^ mask) for s in range(lax.axis_size(axis))])]
    ppermute x10 -> x7, waiting for transfers between devices: 2.59 us -> 1.05 us  [shift(): return lax.ppermute(x, axis, [(s, (s + step) % size) for s in range(size)])]
  transfers between devices with their start and end apart: 13 -> 12, of which waited for: 6 -> 5; matrix products, arithmetic and copies ran while one was open for 0% -> 0% of each run, Pallas kernels for 26% -> 25%
where the time goes in v20:
time: 32 us; the launch traced here: 31.8 us
  starting transfers between devices  17.6 us (55%)
  Pallas kernels  8.02 us (25%)
  waiting for transfers between devices  5.6 us (18%)
  other arithmetic  0.51 us (2%)
    ppermute x7, starting transfers between devices, shift(): return lax.ppermute(x, axis, [(s, (s + step) % size) for s in range(size)])  12.3 us
    pallas_call x1, Pallas kernels, body(): pl.pallas_call(functools.partial(pair_kernel, total, cap, slots, user_sta...  4.38 us
    ppermute x2, waiting for transfers between devices, swap(): lax.ppermute(x, axis, [(s, s ^ mask) for s in range(lax.axis_size(axis))])  4.04 us
    ppermute x2, starting transfers between devices, swap(): lax.ppermute(x, axis, [(s, s ^ mask) for s in range(lax.axis_size(axis))])  4.03 us
    pallas_call x1, Pallas kernels, body(): pl.pallas_call(turn_kernel, out_shape=(jax.ShapeDtypeStruct((width, rows)...  2.2 us
    ppermute x3, starting transfers between devices, body(): pair_scores[q, h] = lax.ppermute(source, ('cache', 'pair'), perm)  1.27 us
    ppermute x7, waiting for transfers between devices, shift(): return lax.ppermute(x, axis, [(s, (s + step) % size) for s in range(size)])  1.05 us
    pallas_call x1, Pallas kernels, body(): pl.pallas_call(functools.partial(linear_kernel, total, planes), out_shape...  0.88 us
  transfers between devices with their start and end apart: 12, of which 5 were waited for; matrix products, arithmetic and copies ran while one was open for 0% of the time, Pallas kernels for 25%

profile of v20, /device:TPU:0, one launch (start us, length us, event | category | flops | bytes accessed | tf_op | source)
XLA Modules:
  0.0 31.8 jit_solution(1586335790214680566)
XLA Ops:
  0.0 2.9 %collective-permute-start.9 = (bf16[128,3072]{1,0:T(8,128)(2,1)}, bf16[128,3072]{1,0:T(8,128)(2,1)S(1)}, u32[]{:S(2)}, u32[]{:S(2)}) collective-permute-start(bf16[128,3072]{1,0:T(8,128)(2,1)} %refs_4_.1), channel_id=1, source_target_pairs={{0,2},{2,0},{1,3},{3,1},{4,6},{6,4},{5,7},{7,5},{8,10},{10,8},{9,1... | collective-permute-start | bytes 2359304 | tf_op jit(solution)/shard_map/item_rows/ppermute | solution.py:204
  2.9 1.6 %collective-permute-start = (s32[8]{0:T(128)}, s32[8]{0:T(128)S(1)}, u32[]{:S(2)}, u32[]{:S(2)}) collective-permute-start(s32[8]{0:T(128)} %refs_0_.1), channel_id=1, source_target_pairs={{0,4},{4,8},{8,12},{12,0},{1,5},{5,9},{9,13},{13,1},{2,6},{6,10},{... | collective-permute-start | bytes 104 | tf_op jit(solution)/shard_map/ids/ppermute | solution.py:204
  4.5 2.6 %collective-permute-start.1 = (s32[8]{0:T(128)}, s32[8]{0:T(128)S(1)}, u32[]{:S(2)}, u32[]{:S(2)}) collective-permute-start(s32[8]{0:T(128)} %refs_0_.1), channel_id=1, source_target_pairs={{0,8},{4,12},{8,0},{12,4},{1,9},{5,13},{9,1},{13,5},{2,10},{6,14},... | collective-permute-start | bytes 104 | tf_op jit(solution)/shard_map/ids/ppermute | solution.py:204
  7.1 1.3 %collective-permute-start.2 = (s32[8]{0:T(128)}, s32[8]{0:T(128)S(1)}, u32[]{:S(2)}, u32[]{:S(2)}) collective-permute-start(s32[8]{0:T(128)} %refs_0_.1), channel_id=1, source_target_pairs={{0,12},{4,0},{8,4},{12,8},{1,13},{5,1},{9,5},{13,9},{2,14},{6,2},{... | collective-permute-start | bytes 104 | tf_op jit(solution)/shard_map/ids/ppermute | solution.py:204
  8.5 2.2 %turn.1 = (f32[3072,128]{1,0:T(8,128)S(1)}, bf16[3072,128]{1,0:T(8,128)(2,1)S(1)}, bf16[64,64,256]{2,1,0:T(8,128)(2,1)S(1)}, bf16[128,3072]{1,0:T(8,128)(2,1)S(1...) custom-call(bf16[128,3072]{1,0:T(8,128)(2,1)} %refs_4_.1, bf16[64,64,256]{2,1,0:T(8,128)(2,1)} %bitcast.12, ...), custom_call_target="tpu_custom_call" | custom-call | flops 1610612736 | bytes 8388608 | tf_op jit(solution)/shard_map/turn/pallas_call | solution.py:236
  10.7 0.0 collective-permute-done.refs_1_
  10.7 0.0 collective-permute-done.1.refs_2_
  10.7 0.1 collective-permute-done.2.refs_3_
  10.8 0.4 %states.1.refs_8_.refs_0_ = bf16[16,3200]{1,0:T(8,128)(2,1)S(1)} custom-call(s32[1,8]{1,0:T(1,128)S(1)} %get-tuple-element.26.refs_0_, s32[1,8]{1,0:T(1,128)S(1)} %bitcast.9, s32[1,8]{1,0:T(1,128)S(1)} %bitcast.10, s32[1,8]{1,0:T(1,128)S(1)} %bitcast.11, bf16[16,128]{1,0:T(8,128)(2,1)S(1)} %get-tuple-element.27.refs_4_, ...), custom_call_target="tpu_custom_call" | custom-call | flops 12582912 | bytes 1048576 | tf_op jit(solution)/shard_map/states/pallas_call | solution.py:264
  11.2 0.6 %collective-permute-start.4 = (bf16[16,3200]{1,0:T(8,128)(2,1)S(1)}, bf16[16,3200]{1,0:T(8,128)(2,1)S(1)}, u32[]{:S(2)}, u32[]{:S(2)}) collective-permute-start(bf16[16,3200]{1,0:T(8,128)(2,1)S(1)} %states.1.refs_8_.refs_0_), channel_id=1, source_target_pairs={{0,4},{4,8},{8,12},{12,0},{1,5},{5,9},{9,13},{13,1},{2,6},{6,10},{... | collective-permute-start | bytes 307208 | tf_op jit(solution)/shard_map/states/ppermute | solution.py:204
  11.8 3.1 %collective-permute-start.6 = (bf16[16,3200]{1,0:T(8,128)(2,1)S(1)}, bf16[16,3200]{1,0:T(8,128)(2,1)S(1)}, u32[]{:S(2)}, u32[]{:S(2)}) collective-permute-start(bf16[16,3200]{1,0:T(8,128)(2,1)S(1)} %states.1.refs_8_.refs_0_), channel_id=1, source_target_pairs={{0,8},{4,12},{8,0},{12,4},{1,9},{5,13},{9,1},{13,5},{2,10},{6,14},... | collective-permute-start | bytes 307208 | tf_op jit(solution)/shard_map/states/ppermute | solution.py:204
  14.9 0.1 collective-permute-start.8
  15.1 0.0 copy-start
  15.1 4.4 %pairs.1 = (f32[1,128]{1,0:T(1,128)S(1)}, s32[4,128]{1,0:T(4,128)S(1)}) custom-call(s32[8]{0:T(128)} %refs_0_.1, s32[8]{0:T(128)S(1)} %collective-permute-done.refs_1_, s32[8]{0:T(128)S(1)} %collective-permute-done.1.refs_2_, s32[8]{0:T(128)S(1)} %collective-permute-done.2.refs_3_, s32[2,256]{1,0:T(2,128)} %bitcast.13, ...), custom_call_target="tpu_custom_call" | custom-call | flops 4294967296 | bytes 4194304 | tf_op jit(solution)/shard_map/pairs/pallas_call | solution.py:275
  19.4 0.6 %collective-permute-start.3 = (f32[1,128]{1,0:T(1,128)S(1)}, f32[1,128]{1,0:T(1,128)S(1)}, u32[]{:S(2)}, u32[]{:S(2)}) collective-permute-start(f32[1,128]{1,0:T(1,128)S(1)} %get-tuple-element.31.refs_1_), channel_id=1, source_target_pairs={{0,2},{1,3},{2,0},{3,1},{4,6},{5,7},{6,4},{7,5},{8,10},{9,11},{10,... | collective-permute-start | bytes 1544 | tf_op jit(solution)/shard_map/pairs/ppermute | solution.py:301
  20.0 0.0 collective-permute-done.4.refs_1_
  20.0 0.0 collective-permute-start.5
  20.1 0.9 %collective-permute-done.6.refs_2_ = bf16[16,3200]{1,0:T(8,128)(2,1)S(1)} collective-permute-done((bf16[16,3200]{1,0:T(8,128)(2,1)S(1)}, bf16[16,3200]{1,0:T(8,128)(2,1)S(1)}, u32[]{:S(2)}, u32[]{:S(2)}) %collective-permute-start.6) | collective-permute-done | bytes 102432 | tf_op jit(solution)/shard_map/states/ppermute | solution.py:204
  21.0 0.7 %collective-permute-start.7 = (f32[1,128]{1,0:T(1,128)S(1)}, f32[1,128]{1,0:T(1,128)S(1)}, u32[]{:S(2)}, u32[]{:S(2)}) collective-permute-start(f32[1,128]{1,0:T(1,128)S(1)} %get-tuple-element.31.refs_1_), channel_id=1, source_target_pairs={{0,1},{1,0},{2,3},{3,2},{4,5},{5,4},{6,7},{7,6},{8,9},{9,8},{10,11... | collective-permute-start | bytes 1544 | tf_op jit(solution)/shard_map/pairs/ppermute | solution.py:301
  21.7 0.0 collective-permute-done.8.refs_3_
  21.7 0.0 collective-permute-done.9.refs_5_
  21.7 0.0 copy-done
  21.7 0.9 %scores.2 = (f32[4,128]{1,0:T(4,128)S(1)}, bf16[256,512]{1,0:T(8,128)(2,1)S(1)}) custom-call(bf16[16,3200]{1,0:T(8,128)(2,1)S(1)} %states.1.refs_8_.refs_0_, bf16[16,3200]{1,0:T(8,128)(2,1)S(1)} %collective-permute-done.4.refs_1_, bf16[16,3200]{1,0:T(8,128)(2,1)S(1)} %collective-permute-done.6.refs_2_, bf16[16,3200]{1,0:T(8,128)(2,1)S(1)} %collective-permute-done.8.refs_3_, ...), custom_call_target="tpu_custom_call" | custom-call | flops 100663296 | bytes 2097152 | tf_op jit(solution)/shard_map/scores/pallas_call | solution.py:305
  22.5 0.5 %collective-permute-done.3.refs_0_ = f32[1,128]{1,0:T(1,128)S(1)} collective-permute-done((f32[1,128]{1,0:T(1,128)S(1)}, f32[1,128]{1,0:T(1,128)S(1)}, u32[]{:S(2)}, u32[]{:S(2)}) %collective-permute-start.3) | collective-permute-done | bytes 544 | tf_op jit(solution)/shard_map/pairs/ppermute | solution.py:301
  23.0 0.0 collective-permute-done.5.refs_2_
  23.1 0.0 collective-permute-done.7.refs_3_
  23.1 0.2 scores.3
  23.2 2.1 %collective-permute-start.10 = (f32[2,128]{1,0:T(2,128)S(1)}, f32[2,128]{1,0:T(2,128)S(1)}, u32[]{:S(2)}, u32[]{:S(2)}) collective-permute-start(f32[2,128]{1,0:T(2,128)S(1)} %get-tuple-element.38), channel_id=1, source_target_pairs={{0,8},{4,12},{8,0},{12,4},{1,9},{5,13},{9,1},{13,5},{2,10},{6,14},... | collective-permute-start | bytes 3080 | tf_op jit(solution)/shard_map/back/ppermute | solution.py:208
  25.3 2.4 %collective-permute-done.10.came = f32[2,128]{1,0:T(2,128)S(1)} collective-permute-done((f32[2,128]{1,0:T(2,128)S(1)}, f32[2,128]{1,0:T(2,128)S(1)}, u32[]{:S(2)}, u32[]{:S(2)}) %collective-permute-start.10) | collective-permute-done | bytes 1056 | tf_op jit(solution)/shard_map/back/ppermute | solution.py:208
  27.8 1.9 %collective-permute-start.11 = (f32[1,128]{1,0:T(1,128)S(1)}, f32[1,128]{1,0:T(1,128)S(1)}, u32[]{:S(2)}, u32[]{:S(2)}) collective-permute-start(f32[1,128]{1,0:T(1,128)S(1)} %get-tuple-element.40), channel_id=1, source_target_pairs={{0,4},{4,0},{8,12},{12,8},{1,5},{5,1},{9,13},{13,9},{2,6},{6,2},{1... | collective-permute-start | bytes 1544 | tf_op jit(solution)/shard_map/back/ppermute | solution.py:208
  29.7 1.6 %collective-permute-done.11 = f32[1,128]{1,0:T(1,128)S(1)} collective-permute-done((f32[1,128]{1,0:T(1,128)S(1)}, f32[1,128]{1,0:T(1,128)S(1)}, u32[]{:S(2)}, u32[]{:S(2)}) %collective-permute-start.11) | collective-permute-done | bytes 544 | tf_op jit(solution)/shard_map/back/ppermute | solution.py:208
  31.3 0.5 %add_bitcast_fusion = f32[128]{0:T(128)} fusion(f32[1,128]{1,0:T(1,128)S(1)} %get-tuple-element.39, f32[1,128]{1,0:T(1,128)S(1)} %collective-permute-done.11), kind=kLoop, calls=%fused_computation | loop fusion | flops 128 | bytes 1536 | tf_op jit(solution)/shard_map/back/reshape | solution.py:343
  (1 shorter events, 0.0 us)
Async XLA Ops:
  0.0 21.7 %collective-permute-start.9 = (bf16[128,3072]{1,0:T(8,128)(2,1)}, bf16[128,3072]{1,0:T(8,128)(2,1)S(1)}, u32[]{:S(2)}, u32[]{:S(2)}) collective-permute-start(bf16[128,3072]{1,0:T(8,128)(2,1)} %refs_4_.1), channel_id=1, source_target_pairs={{0,2},{2,0},{1,3},{3,1},{4,6},{6,4},{5,7},{7,5},{8,10},{10,8},{9,1... | collective-permute-start | bytes 2359304 | tf_op jit(solution)/shard_map/item_rows/ppermute | solution.py:204
  2.9 7.7 %collective-permute-start = (s32[8]{0:T(128)}, s32[8]{0:T(128)S(1)}, u32[]{:S(2)}, u32[]{:S(2)}) collective-permute-start(s32[8]{0:T(128)} %refs_0_.1), channel_id=1, source_target_pairs={{0,4},{4,8},{8,12},{12,0},{1,5},{5,9},{9,13},{13,1},{2,6},{6,10},{... | collective-permute-start | bytes 104 | tf_op jit(solution)/shard_map/ids/ppermute | solution.py:204
  4.5 6.2 %collective-permute-start.1 = (s32[8]{0:T(128)}, s32[8]{0:T(128)S(1)}, u32[]{:S(2)}, u32[]{:S(2)}) collective-permute-start(s32[8]{0:T(128)} %refs_0_.1), channel_id=1, source_target_pairs={{0,8},{4,12},{8,0},{12,4},{1,9},{5,13},{9,1},{13,5},{2,10},{6,14},... | collective-permute-start | bytes 104 | tf_op jit(solution)/shard_map/ids/ppermute | solution.py:204
  7.1 3.7 %collective-permute-start.2 = (s32[8]{0:T(128)}, s32[8]{0:T(128)S(1)}, u32[]{:S(2)}, u32[]{:S(2)}) collective-permute-start(s32[8]{0:T(128)} %refs_0_.1), channel_id=1, source_target_pairs={{0,12},{4,0},{8,4},{12,8},{1,13},{5,1},{9,5},{13,9},{2,14},{6,2},{... | collective-permute-start | bytes 104 | tf_op jit(solution)/shard_map/ids/ppermute | solution.py:204
  11.2 8.9 %collective-permute-start.4 = (bf16[16,3200]{1,0:T(8,128)(2,1)S(1)}, bf16[16,3200]{1,0:T(8,128)(2,1)S(1)}, u32[]{:S(2)}, u32[]{:S(2)}) collective-permute-start(bf16[16,3200]{1,0:T(8,128)(2,1)S(1)} %states.1.refs_8_.refs_0_), channel_id=1, source_target_pairs={{0,4},{4,8},{8,12},{12,0},{1,5},{5,9},{9,13},{13,1},{2,6},{6,10},{... | collective-permute-start | bytes 307208 | tf_op jit(solution)/shard_map/states/ppermute | solution.py:204
  11.8 9.2 %collective-permute-start.6 = (bf16[16,3200]{1,0:T(8,128)(2,1)S(1)}, bf16[16,3200]{1,0:T(8,128)(2,1)S(1)}, u32[]{:S(2)}, u32[]{:S(2)}) collective-permute-start(bf16[16,3200]{1,0:T(8,128)(2,1)S(1)} %states.1.refs_8_.refs_0_), channel_id=1, source_target_pairs={{0,8},{4,12},{8,0},{12,4},{1,9},{5,13},{9,1},{13,5},{2,10},{6,14},... | collective-permute-start | bytes 307208 | tf_op jit(solution)/shard_map/states/ppermute | solution.py:204
  14.9 6.7 %collective-permute-start.8 = (bf16[16,3200]{1,0:T(8,128)(2,1)S(1)}, bf16[16,3200]{1,0:T(8,128)(2,1)S(1)}, u32[]{:S(2)}, u32[]{:S(2)}) collective-permute-start(bf16[16,3200]{1,0:T(8,128)(2,1)S(1)} %states.1.refs_8_.refs_0_), channel_id=1, source_target_pairs={{0,12},{4,0},{8,4},{12,8},{1,13},{5,1},{9,5},{13,9},{2,14},{6,2},{... | collective-permute-start | bytes 307208 | tf_op jit(solution)/shard_map/states/ppermute | solution.py:204
  15.1 6.6 %copy-start = (bf16[128,3072]{1,0:T(8,128)(2,1)S(1)}, bf16[128,3072]{1,0:T(8,128)(2,1)}, u32[]{:S(2)}) copy-start(bf16[128,3072]{1,0:T(8,128)(2,1)} %refs_4_.1) | copy-start | bytes 2359300
  19.4 3.6 %collective-permute-start.3 = (f32[1,128]{1,0:T(1,128)S(1)}, f32[1,128]{1,0:T(1,128)S(1)}, u32[]{:S(2)}, u32[]{:S(2)}) collective-permute-start(f32[1,128]{1,0:T(1,128)S(1)} %get-tuple-element.31.refs_1_), channel_id=1, source_target_pairs={{0,2},{1,3},{2,0},{3,1},{4,6},{5,7},{6,4},{7,5},{8,10},{9,11},{10,... | collective-permute-start | bytes 1544 | tf_op jit(solution)/shard_map/pairs/ppermute | solution.py:301
  20.0 3.0 %collective-permute-start.5 = (f32[1,128]{1,0:T(1,128)S(1)}, f32[1,128]{1,0:T(1,128)S(1)}, u32[]{:S(2)}, u32[]{:S(2)}) collective-permute-start(f32[1,128]{1,0:T(1,128)S(1)} %get-tuple-element.31.refs_1_), channel_id=1, source_target_pairs={{0,3},{1,2},{2,1},{3,0},{4,7},{5,6},{6,5},{7,4},{8,11},{9,10},{10,... | collective-permute-start | bytes 1544 | tf_op jit(solution)/shard_map/pairs/ppermute | solution.py:301
  21.0 2.1 %collective-permute-start.7 = (f32[1,128]{1,0:T(1,128)S(1)}, f32[1,128]{1,0:T(1,128)S(1)}, u32[]{:S(2)}, u32[]{:S(2)}) collective-permute-start(f32[1,128]{1,0:T(1,128)S(1)} %get-tuple-element.31.refs_1_), channel_id=1, source_target_pairs={{0,1},{1,0},{2,3},{3,2},{4,5},{5,4},{6,7},{7,6},{8,9},{9,8},{10,11... | collective-permute-start | bytes 1544 | tf_op jit(solution)/shard_map/pairs/ppermute | solution.py:301
  23.2 4.5 %collective-permute-start.10 = (f32[2,128]{1,0:T(2,128)S(1)}, f32[2,128]{1,0:T(2,128)S(1)}, u32[]{:S(2)}, u32[]{:S(2)}) collective-permute-start(f32[2,128]{1,0:T(2,128)S(1)} %get-tuple-element.38), channel_id=1, source_target_pairs={{0,8},{4,12},{8,0},{12,4},{1,9},{5,13},{9,1},{13,5},{2,10},{6,14},... | collective-permute-start | bytes 3080 | tf_op jit(solution)/shard_map/back/ppermute | solution.py:208
  27.8 3.5 %collective-permute-start.11 = (f32[1,128]{1,0:T(1,128)S(1)}, f32[1,128]{1,0:T(1,128)S(1)}, u32[]{:S(2)}, u32[]{:S(2)}) collective-permute-start(f32[1,128]{1,0:T(1,128)S(1)} %get-tuple-element.40), channel_id=1, source_target_pairs={{0,4},{4,0},{8,12},{12,8},{1,5},{5,1},{9,13},{13,9},{2,6},{6,2},{1... | collective-permute-start | bytes 1544 | tf_op jit(solution)/shard_map/back/ppermute | solution.py:208

commit v21 on v19

--- a/solution.py
+++ b/solution.py
@@ -176,7 +176,8 @@
 
 
 def score_kernel(total, planes, parts, *refs):
-    pairs, (linear, hits), outs = refs[:planes * parts], refs[planes * parts:planes * parts + 2], refs[planes * parts + 2:]
+    pairs, (linear, hits), refs = refs[:planes * parts], refs[planes * parts:planes * parts + 2], refs[planes * parts + 2:]
+    outs, rows = refs[:total], refs[total]
     half = linear.shape[1]
     sums = [sum(pairs[(h + 1) * planes - 1 - q][...] for h in range(parts)) for q in range(planes)]
     row = jnp.concatenate(sums, axis=1)
@@ -185,12 +186,19 @@
         pieces = jnp.where(iota(pieces.shape, 0) == t, part.astype(jnp.float32), pieces)
     added = jnp.sum(dot(pieces.astype(jnp.bfloat16), hits[...], NN), axis=0, keepdims=True)
     for j in range(total):
-        outs[j][...] = linear[j:j + 1, :] + added[:, j * half:(j + 1) * half]
+        rows[j:j + 1, :] = linear[j:j + 1, :] + added[:, j * half:(j + 1) * half]
+    me = lax.axis_index("shard")
+    for mask in range(total):
+        outs[mask][...] = rows[pl.ds(ring(me - (me ^ mask), total), 1), :]
 
 
 def shift(x, axis, step):
     size = lax.axis_size(axis)
     return lax.ppermute(x, axis, [(s, (s + step) % size) for s in range(size)])
+
+
+def swap(x, axis, mask):
+    return lax.ppermute(x, axis, [(s, s ^ mask) for s in range(lax.axis_size(axis))])
 
 
 def body(cand_items, reader_users, item_table, user_states, pair_mats, pair_fields):
@@ -307,6 +315,7 @@
             out_shape=[jax.ShapeDtypeStruct((1, half), jnp.float32)] * total,
             in_specs=[vmem] * (planes * parts + 2),
             out_specs=[vmem] * total,
+            scratch_shapes=[pltpu.VMEM((-(-total // 8) * 8, half), jnp.float32)],
             compiler_params=params,
             cost_estimate=pl.CostEstimate(flops=2 * 16 * 256 * 512, bytes_accessed=512 * 1024, transcendentals=0),
         )(*pair_scores, linear, hits)
@@ -314,7 +323,7 @@
     with jax.named_scope("back"):
         result = outs[0]
         for j in range(1, total):
-            result = result + shift(outs[j], "shard", -j)
+            result = result + swap(outs[j], "shard", j)
     return result.reshape(half)
 
 

time: 30.5 us -> 30.9 us (1.013)
  waiting for transfers between devices: 3.1 us -> 4.09 us
  starting transfers between devices: 18.6 us -> 18 us
    ppermute x10 -> x7, starting transfers between devices: 17.4 us -> 12.3 us  [shift(): return lax.ppermute(x, axis, [(s, (s + step) % size) for s in range(size)])]
    ppermute x0 -> x3, starting transfers between devices: none -> 4.45 us  [swap(): lax.ppermute(x, axis, [(s, s ^ mask) for s in range(lax.axis_size(axis))])]
    ppermute x0 -> x3, waiting for transfers between devices: none -> 2.53 us  [swap(): lax.ppermute(x, axis, [(s, s ^ mask) for s in range(lax.axis_size(axis))])]
    ppermute x10 -> x7, waiting for transfers between devices: 2.59 us -> 1.05 us  [shift(): return lax.ppermute(x, axis, [(s, (s + step) % size) for s in range(size)])]
where the time goes in v21:
time: 30.9 us; the launch traced here: 30.7 us
  starting transfers between devices  18 us (58%)
  Pallas kernels  8.02 us (26%)
  waiting for transfers between devices  4.09 us (13%)
  other arithmetic  0.52 us (2%)
    ppermute x7, starting transfers between devices, shift(): return lax.ppermute(x, axis, [(s, (s + step) % size) for s in range(size)])  12.3 us
    ppermute x3, starting transfers between devices, swap(): lax.ppermute(x, axis, [(s, s ^ mask) for s in range(lax.axis_size(axis))])  4.45 us
    pallas_call x1, Pallas kernels, body(): pl.pallas_call(functools.partial(pair_kernel, total, cap, slots, user_sta...  4.38 us
    ppermute x3, waiting for transfers between devices, swap(): lax.ppermute(x, axis, [(s, s ^ mask) for s in range(lax.axis_size(axis))])  2.53 us
    pallas_call x1, Pallas kernels, body(): pl.pallas_call(turn_kernel, out_shape=(jax.ShapeDtypeStruct((width, rows)...  2.2 us
    ppermute x3, starting transfers between devices, body(): pair_scores[q, h] = lax.ppermute(source, ('cache', 'pair'), perm)  1.27 us
    ppermute x7, waiting for transfers between devices, shift(): return lax.ppermute(x, axis, [(s, (s + step) % size) for s in range(size)])  1.05 us
    pallas_call x1, Pallas kernels, body(): pl.pallas_call(functools.partial(linear_kernel, total, planes), out_shape...  0.88 us
  transfers between devices with their start and end apart: 13, of which 6 were waited for; matrix products, arithmetic and copies ran while one was open for 0% of the time, Pallas kernels for 26%

profile of v21, /device:TPU:0, one launch (start us, length us, event | category | flops | bytes accessed | tf_op | source)
XLA Modules:
  0.0 30.7 jit_solution(5473637718533599842)
XLA Ops:
  0.0 2.9 %collective-permute-start.9 = (bf16[128,3072]{1,0:T(8,128)(2,1)}, bf16[128,3072]{1,0:T(8,128)(2,1)S(1)}, u32[]{:S(2)}, u32[]{:S(2)}) collective-permute-start(bf16[128,3072]{1,0:T(8,128)(2,1)} %refs_4_.1), channel_id=1, source_target_pairs={{0,2},{2,0},{1,3},{3,1},{4,6},{6,4},{5,7},{7,5},{8,10},{10,8},{9,1... | collective-permute-start | bytes 2359304 | tf_op jit(solution)/shard_map/item_rows/ppermute | solution.py:197
  2.9 1.6 %collective-permute-start = (s32[8]{0:T(128)}, s32[8]{0:T(128)S(1)}, u32[]{:S(2)}, u32[]{:S(2)}) collective-permute-start(s32[8]{0:T(128)} %refs_0_.1), channel_id=1, source_target_pairs={{0,4},{4,8},{8,12},{12,0},{1,5},{5,9},{9,13},{13,1},{2,6},{6,10},{... | collective-permute-start | bytes 104 | tf_op jit(solution)/shard_map/ids/ppermute | solution.py:197
  4.5 2.6 %collective-permute-start.1 = (s32[8]{0:T(128)}, s32[8]{0:T(128)S(1)}, u32[]{:S(2)}, u32[]{:S(2)}) collective-permute-start(s32[8]{0:T(128)} %refs_0_.1), channel_id=1, source_target_pairs={{0,8},{4,12},{8,0},{12,4},{1,9},{5,13},{9,1},{13,5},{2,10},{6,14},... | collective-permute-start | bytes 104 | tf_op jit(solution)/shard_map/ids/ppermute | solution.py:197
  7.1 1.3 %collective-permute-start.2 = (s32[8]{0:T(128)}, s32[8]{0:T(128)S(1)}, u32[]{:S(2)}, u32[]{:S(2)}) collective-permute-start(s32[8]{0:T(128)} %refs_0_.1), channel_id=1, source_target_pairs={{0,12},{4,0},{8,4},{12,8},{1,13},{5,1},{9,5},{13,9},{2,14},{6,2},{... | collective-permute-start | bytes 104 | tf_op jit(solution)/shard_map/ids/ppermute | solution.py:197
  8.5 2.2 %turn.1 = (f32[3072,128]{1,0:T(8,128)S(1)}, bf16[3072,128]{1,0:T(8,128)(2,1)S(1)}, bf16[64,64,256]{2,1,0:T(8,128)(2,1)S(1)}, bf16[128,3072]{1,0:T(8,128)(2,1)S(1...) custom-call(bf16[128,3072]{1,0:T(8,128)(2,1)} %refs_4_.1, bf16[64,64,256]{2,1,0:T(8,128)(2,1)} %bitcast.12, ...), custom_call_target="tpu_custom_call" | custom-call | flops 1610612736 | bytes 8388608 | tf_op jit(solution)/shard_map/turn/pallas_call | solution.py:229
  10.7 0.0 collective-permute-done.refs_1_
  10.7 0.0 collective-permute-done.1.refs_2_
  10.7 0.1 collective-permute-done.2.refs_3_
  10.8 0.4 %states.1.refs_8_.refs_0_ = bf16[16,3200]{1,0:T(8,128)(2,1)S(1)} custom-call(s32[1,8]{1,0:T(1,128)S(1)} %get-tuple-element.26.refs_0_, s32[1,8]{1,0:T(1,128)S(1)} %bitcast.9, s32[1,8]{1,0:T(1,128)S(1)} %bitcast.10, s32[1,8]{1,0:T(1,128)S(1)} %bitcast.11, bf16[16,128]{1,0:T(8,128)(2,1)S(1)} %get-tuple-element.27.refs_4_, ...), custom_call_target="tpu_custom_call" | custom-call | flops 12582912 | bytes 1048576 | tf_op jit(solution)/shard_map/states/pallas_call | solution.py:257
  11.2 0.6 %collective-permute-start.4 = (bf16[16,3200]{1,0:T(8,128)(2,1)S(1)}, bf16[16,3200]{1,0:T(8,128)(2,1)S(1)}, u32[]{:S(2)}, u32[]{:S(2)}) collective-permute-start(bf16[16,3200]{1,0:T(8,128)(2,1)S(1)} %states.1.refs_8_.refs_0_), channel_id=1, source_target_pairs={{0,4},{4,8},{8,12},{12,0},{1,5},{5,9},{9,13},{13,1},{2,6},{6,10},{... | collective-permute-start | bytes 307208 | tf_op jit(solution)/shard_map/states/ppermute | solution.py:197
  11.8 3.1 %collective-permute-start.6 = (bf16[16,3200]{1,0:T(8,128)(2,1)S(1)}, bf16[16,3200]{1,0:T(8,128)(2,1)S(1)}, u32[]{:S(2)}, u32[]{:S(2)}) collective-permute-start(bf16[16,3200]{1,0:T(8,128)(2,1)S(1)} %states.1.refs_8_.refs_0_), channel_id=1, source_target_pairs={{0,8},{4,12},{8,0},{12,4},{1,9},{5,13},{9,1},{13,5},{2,10},{6,14},... | collective-permute-start | bytes 307208 | tf_op jit(solution)/shard_map/states/ppermute | solution.py:197
  14.9 0.1 collective-permute-start.8
  15.1 0.0 copy-start
  15.1 4.4 %pairs.1 = (f32[1,128]{1,0:T(1,128)S(1)}, s32[4,128]{1,0:T(4,128)S(1)}) custom-call(s32[8]{0:T(128)} %refs_0_.1, s32[8]{0:T(128)S(1)} %collective-permute-done.refs_1_, s32[8]{0:T(128)S(1)} %collective-permute-done.1.refs_2_, s32[8]{0:T(128)S(1)} %collective-permute-done.2.refs_3_, s32[2,256]{1,0:T(2,128)} %bitcast.13, ...), custom_call_target="tpu_custom_call" | custom-call | flops 4294967296 | bytes 4194304 | tf_op jit(solution)/shard_map/pairs/pallas_call | solution.py:268
  19.4 0.6 %collective-permute-start.3 = (f32[1,128]{1,0:T(1,128)S(1)}, f32[1,128]{1,0:T(1,128)S(1)}, u32[]{:S(2)}, u32[]{:S(2)}) collective-permute-start(f32[1,128]{1,0:T(1,128)S(1)} %get-tuple-element.31.refs_1_), channel_id=1, source_target_pairs={{0,2},{1,3},{2,0},{3,1},{4,6},{5,7},{6,4},{7,5},{8,10},{9,11},{10,... | collective-permute-start | bytes 1544 | tf_op jit(solution)/shard_map/pairs/ppermute | solution.py:294
  20.0 0.0 collective-permute-done.4.refs_1_
  20.0 0.0 collective-permute-start.5
  20.1 0.9 %collective-permute-done.6.refs_2_ = bf16[16,3200]{1,0:T(8,128)(2,1)S(1)} collective-permute-done((bf16[16,3200]{1,0:T(8,128)(2,1)S(1)}, bf16[16,3200]{1,0:T(8,128)(2,1)S(1)}, u32[]{:S(2)}, u32[]{:S(2)}) %collective-permute-start.6) | collective-permute-done | bytes 102432 | tf_op jit(solution)/shard_map/states/ppermute | solution.py:197
  21.0 0.7 %collective-permute-start.7 = (f32[1,128]{1,0:T(1,128)S(1)}, f32[1,128]{1,0:T(1,128)S(1)}, u32[]{:S(2)}, u32[]{:S(2)}) collective-permute-start(f32[1,128]{1,0:T(1,128)S(1)} %get-tuple-element.31.refs_1_), channel_id=1, source_target_pairs={{0,1},{1,0},{2,3},{3,2},{4,5},{5,4},{6,7},{7,6},{8,9},{9,8},{10,11... | collective-permute-start | bytes 1544 | tf_op jit(solution)/shard_map/pairs/ppermute | solution.py:294
  21.7 0.0 collective-permute-done.8.refs_3_
  21.7 0.0 collective-permute-done.9.refs_5_
  21.7 0.0 copy-done
  21.7 0.9 %scores.2 = (f32[4,128]{1,0:T(4,128)S(1)}, bf16[256,512]{1,0:T(8,128)(2,1)S(1)}) custom-call(bf16[16,3200]{1,0:T(8,128)(2,1)S(1)} %states.1.refs_8_.refs_0_, bf16[16,3200]{1,0:T(8,128)(2,1)S(1)} %collective-permute-done.4.refs_1_, bf16[16,3200]{1,0:T(8,128)(2,1)S(1)} %collective-permute-done.6.refs_2_, bf16[16,3200]{1,0:T(8,128)(2,1)S(1)} %collective-permute-done.8.refs_3_, ...), custom_call_target="tpu_custom_call" | custom-call | flops 100663296 | bytes 2097152 | tf_op jit(solution)/shard_map/scores/pallas_call | solution.py:298
  22.5 0.5 %collective-permute-done.3.refs_0_ = f32[1,128]{1,0:T(1,128)S(1)} collective-permute-done((f32[1,128]{1,0:T(1,128)S(1)}, f32[1,128]{1,0:T(1,128)S(1)}, u32[]{:S(2)}, u32[]{:S(2)}) %collective-permute-start.3) | collective-permute-done | bytes 544 | tf_op jit(solution)/shard_map/pairs/ppermute | solution.py:294
  23.0 0.0 collective-permute-done.5.refs_2_
  23.1 0.0 collective-permute-done.7.refs_3_
  23.1 0.2 scores.3
  23.2 2.5 %collective-permute-start.12 = (f32[1,128]{1,0:T(1,128)S(1)}, f32[1,128]{1,0:T(1,128)S(1)}, u32[]{:S(2)}, u32[]{:S(2)}) collective-permute-start(f32[1,128]{1,0:T(1,128)S(1)} %get-tuple-element.40), channel_id=1, source_target_pairs={{0,12},{4,8},{8,4},{12,0},{1,13},{5,9},{9,5},{13,1},{2,14},{6,10},... | collective-permute-start | bytes 1544 | tf_op jit(solution)/shard_map/back/ppermute | solution.py:201
  25.7 1.0 %collective-permute-start.11 = (f32[1,128]{1,0:T(1,128)S(1)}, f32[1,128]{1,0:T(1,128)S(1)}, u32[]{:S(2)}, u32[]{:S(2)}) collective-permute-start(f32[1,128]{1,0:T(1,128)S(1)} %get-tuple-element.39), channel_id=1, source_target_pairs={{0,8},{4,12},{8,0},{12,4},{1,9},{5,13},{9,1},{13,5},{2,10},{6,14},... | collective-permute-start | bytes 1544 | tf_op jit(solution)/shard_map/back/ppermute | solution.py:201
  26.7 1.0 %collective-permute-start.10 = (f32[1,128]{1,0:T(1,128)S(1)}, f32[1,128]{1,0:T(1,128)S(1)}, u32[]{:S(2)}, u32[]{:S(2)}) collective-permute-start(f32[1,128]{1,0:T(1,128)S(1)} %get-tuple-element.38), channel_id=1, source_target_pairs={{0,4},{4,0},{8,12},{12,8},{1,5},{5,1},{9,13},{13,9},{2,6},{6,2},{1... | collective-permute-start | bytes 1544 | tf_op jit(solution)/shard_map/back/ppermute | solution.py:201
  27.7 0.9 %collective-permute-done.12 = f32[1,128]{1,0:T(1,128)S(1)} collective-permute-done((f32[1,128]{1,0:T(1,128)S(1)}, f32[1,128]{1,0:T(1,128)S(1)}, u32[]{:S(2)}, u32[]{:S(2)}) %collective-permute-start.12) | collective-permute-done | bytes 544 | tf_op jit(solution)/shard_map/back/ppermute | solution.py:201
  28.6 1.5 %collective-permute-done.11 = f32[1,128]{1,0:T(1,128)S(1)} collective-permute-done((f32[1,128]{1,0:T(1,128)S(1)}, f32[1,128]{1,0:T(1,128)S(1)}, u32[]{:S(2)}, u32[]{:S(2)}) %collective-permute-start.11) | collective-permute-done | bytes 544 | tf_op jit(solution)/shard_map/back/ppermute | solution.py:201
  30.1 0.1 collective-permute-done.10
  30.2 0.5 %add_bitcast_fusion = f32[128]{0:T(128)} fusion(f32[1,128]{1,0:T(1,128)S(1)} %collective-permute-done.12, f32[1,128]{1,0:T(1,128)S(1)} %collective-permute-done.11, f32[1,128]{1,0:T(1,128)S(1)} %get-tuple-element.37, f32[1,128]{1,0:T(1,128)S(1)} %collective-permute-done.10), kind=kLoop, calls=%fused_computation | loop fusion | flops 384 | bytes 2560 | tf_op jit(solution)/shard_map/reshape | solution.py:327
Async XLA Ops:
  0.0 21.7 %collective-permute-start.9 = (bf16[128,3072]{1,0:T(8,128)(2,1)}, bf16[128,3072]{1,0:T(8,128)(2,1)S(1)}, u32[]{:S(2)}, u32[]{:S(2)}) collective-permute-start(bf16[128,3072]{1,0:T(8,128)(2,1)} %refs_4_.1), channel_id=1, source_target_pairs={{0,2},{2,0},{1,3},{3,1},{4,6},{6,4},{5,7},{7,5},{8,10},{10,8},{9,1... | collective-permute-start | bytes 2359304 | tf_op jit(solution)/shard_map/item_rows/ppermute | solution.py:197
  2.9 7.7 %collective-permute-start = (s32[8]{0:T(128)}, s32[8]{0:T(128)S(1)}, u32[]{:S(2)}, u32[]{:S(2)}) collective-permute-start(s32[8]{0:T(128)} %refs_0_.1), channel_id=1, source_target_pairs={{0,4},{4,8},{8,12},{12,0},{1,5},{5,9},{9,13},{13,1},{2,6},{6,10},{... | collective-permute-start | bytes 104 | tf_op jit(solution)/shard_map/ids/ppermute | solution.py:197
  4.5 6.2 %collective-permute-start.1 = (s32[8]{0:T(128)}, s32[8]{0:T(128)S(1)}, u32[]{:S(2)}, u32[]{:S(2)}) collective-permute-start(s32[8]{0:T(128)} %refs_0_.1), channel_id=1, source_target_pairs={{0,8},{4,12},{8,0},{12,4},{1,9},{5,13},{9,1},{13,5},{2,10},{6,14},... | collective-permute-start | bytes 104 | tf_op jit(solution)/shard_map/ids/ppermute | solution.py:197
  7.1 3.7 %collective-permute-start.2 = (s32[8]{0:T(128)}, s32[8]{0:T(128)S(1)}, u32[]{:S(2)}, u32[]{:S(2)}) collective-permute-start(s32[8]{0:T(128)} %refs_0_.1), channel_id=1, source_target_pairs={{0,12},{4,0},{8,4},{12,8},{1,13},{5,1},{9,5},{13,9},{2,14},{6,2},{... | collective-permute-start | bytes 104 | tf_op jit(solution)/shard_map/ids/ppermute | solution.py:197
  11.2 8.9 %collective-permute-start.4 = (bf16[16,3200]{1,0:T(8,128)(2,1)S(1)}, bf16[16,3200]{1,0:T(8,128)(2,1)S(1)}, u32[]{:S(2)}, u32[]{:S(2)}) collective-permute-start(bf16[16,3200]{1,0:T(8,128)(2,1)S(1)} %states.1.refs_8_.refs_0_), channel_id=1, source_target_pairs={{0,4},{4,8},{8,12},{12,0},{1,5},{5,9},{9,13},{13,1},{2,6},{6,10},{... | collective-permute-start | bytes 307208 | tf_op jit(solution)/shard_map/states/ppermute | solution.py:197
  11.8 9.2 %collective-permute-start.6 = (bf16[16,3200]{1,0:T(8,128)(2,1)S(1)}, bf16[16,3200]{1,0:T(8,128)(2,1)S(1)}, u32[]{:S(2)}, u32[]{:S(2)}) collective-permute-start(bf16[16,3200]{1,0:T(8,128)(2,1)S(1)} %states.1.refs_8_.refs_0_), channel_id=1, source_target_pairs={{0,8},{4,12},{8,0},{12,4},{1,9},{5,13},{9,1},{13,5},{2,10},{6,14},... | collective-permute-start | bytes 307208 | tf_op jit(solution)/shard_map/states/ppermute | solution.py:197
  14.9 6.7 %collective-permute-start.8 = (bf16[16,3200]{1,0:T(8,128)(2,1)S(1)}, bf16[16,3200]{1,0:T(8,128)(2,1)S(1)}, u32[]{:S(2)}, u32[]{:S(2)}) collective-permute-start(bf16[16,3200]{1,0:T(8,128)(2,1)S(1)} %states.1.refs_8_.refs_0_), channel_id=1, source_target_pairs={{0,12},{4,0},{8,4},{12,8},{1,13},{5,1},{9,5},{13,9},{2,14},{6,2},{... | collective-permute-start | bytes 307208 | tf_op jit(solution)/shard_map/states/ppermute | solution.py:197
  15.1 6.6 %copy-start = (bf16[128,3072]{1,0:T(8,128)(2,1)S(1)}, bf16[128,3072]{1,0:T(8,128)(2,1)}, u32[]{:S(2)}) copy-start(bf16[128,3072]{1,0:T(8,128)(2,1)} %refs_4_.1) | copy-start | bytes 2359300
  19.4 3.6 %collective-permute-start.3 = (f32[1,128]{1,0:T(1,128)S(1)}, f32[1,128]{1,0:T(1,128)S(1)}, u32[]{:S(2)}, u32[]{:S(2)}) collective-permute-start(f32[1,128]{1,0:T(1,128)S(1)} %get-tuple-element.31.refs_1_), channel_id=1, source_target_pairs={{0,2},{1,3},{2,0},{3,1},{4,6},{5,7},{6,4},{7,5},{8,10},{9,11},{10,... | collective-permute-start | bytes 1544 | tf_op jit(solution)/shard_map/pairs/ppermute | solution.py:294
  20.0 3.0 %collective-permute-start.5 = (f32[1,128]{1,0:T(1,128)S(1)}, f32[1,128]{1,0:T(1,128)S(1)}, u32[]{:S(2)}, u32[]{:S(2)}) collective-permute-start(f32[1,128]{1,0:T(1,128)S(1)} %get-tuple-element.31.refs_1_), channel_id=1, source_target_pairs={{0,3},{1,2},{2,1},{3,0},{4,7},{5,6},{6,5},{7,4},{8,11},{9,10},{10,... | collective-permute-start | bytes 1544 | tf_op jit(solution)/shard_map/pairs/ppermute | solution.py:294
  21.0 2.1 %collective-permute-start.7 = (f32[1,128]{1,0:T(1,128)S(1)}, f32[1,128]{1,0:T(1,128)S(1)}, u32[]{:S(2)}, u32[]{:S(2)}) collective-permute-start(f32[1,128]{1,0:T(1,128)S(1)} %get-tuple-element.31.refs_1_), channel_id=1, source_target_pairs={{0,1},{1,0},{2,3},{3,2},{4,5},{5,4},{6,7},{7,6},{8,9},{9,8},{10,11... | collective-permute-start | bytes 1544 | tf_op jit(solution)/shard_map/pairs/ppermute | solution.py:294
  23.2 5.4 %collective-permute-start.12 = (f32[1,128]{1,0:T(1,128)S(1)}, f32[1,128]{1,0:T(1,128)S(1)}, u32[]{:S(2)}, u32[]{:S(2)}) collective-permute-start(f32[1,128]{1,0:T(1,128)S(1)} %get-tuple-element.40), channel_id=1, source_target_pairs={{0,12},{4,8},{8,4},{12,0},{1,13},{5,9},{9,5},{13,1},{2,14},{6,10},... | collective-permute-start | bytes 1544 | tf_op jit(solution)/shard_map/back/ppermute | solution.py:201
  25.7 4.4 %collective-permute-start.11 = (f32[1,128]{1,0:T(1,128)S(1)}, f32[1,128]{1,0:T(1,128)S(1)}, u32[]{:S(2)}, u32[]{:S(2)}) collective-permute-start(f32[1,128]{1,0:T(1,128)S(1)} %get-tuple-element.39), channel_id=1, source_target_pairs={{0,8},{4,12},{8,0},{12,4},{1,9},{5,13},{9,1},{13,5},{2,10},{6,14},... | collective-permute-start | bytes 1544 | tf_op jit(solution)/shard_map/back/ppermute | solution.py:201
  26.7 3.5 %collective-permute-start.10 = (f32[1,128]{1,0:T(1,128)S(1)}, f32[1,128]{1,0:T(1,128)S(1)}, u32[]{:S(2)}, u32[]{:S(2)}) collective-permute-start(f32[1,128]{1,0:T(1,128)S(1)} %get-tuple-element.38), channel_id=1, source_target_pairs={{0,4},{4,0},{8,12},{12,8},{1,5},{5,1},{9,13},{13,9},{2,6},{6,2},{1... | collective-permute-start | bytes 1544 | tf_op jit(solution)/shard_map/back/ppermute | solution.py:201

commit v22 on v19

--- a/solution.py
+++ b/solution.py
@@ -50,24 +50,6 @@
         chosen = chosen + dot(to_slot, from_row, NN)
     out[:, width:] = digits[...]
     out[:, :width] = dot(chosen.astype(jnp.bfloat16), states[...], NN).astype(jnp.bfloat16)
-
-
-def slot_rows(asked, cap, slots, user_rows, half):
-    total, readers = asked.shape
-    me = lax.axis_index("shard")
-    lane = iota((1, half), 1) // (half // readers)
-    rows = []
-    for j in range(total):
-        source = ring(me - j, total)
-        holders = [asked[j, r] // user_rows for r in range(readers)]
-        row = jnp.zeros((1, half), jnp.int32)
-        for r, holder in enumerate(holders):
-            rank = jnp.int32(0)
-            for earlier in holders[:r]:
-                rank = rank + (earlier == holder).astype(jnp.int32)
-            row = jnp.where(lane == r, ring(me - holder, total) * slots + source * cap + rank, row)
-        rows.append(row)
-    return rows
 
 
 def turn_kernel(items_hbm, mats_hbm, states_hbm, ids_hbm, cands_hbm, rows32, rows16, mats, states, ids, digits, items, cands, sems):
@@ -100,14 +82,10 @@
     states_fetch.wait()
 
 
-def pair_kernel(total, cap, slots, user_rows, *refs):
-    users, refs = refs[:total], refs[total:]
-    fields_hbm, rows32, rows16, mats, picked, out, places, asked, fields, stacked, sems = refs
+def pair_kernel(fields_hbm, rows32, rows16, mats, picked, out, fields, stacked, sem):
     del picked
-    fields_fetch = pltpu.make_async_copy(fields_hbm, fields, sems.at[total])
-    id_fetches = [pltpu.make_async_copy(users[j], asked.at[j], sems.at[j]) for j in range(total)]
-    for copy in [fields_fetch] + id_fetches:
-        copy.start()
+    fields_fetch = pltpu.make_async_copy(fields_hbm, fields, sem)
+    fields_fetch.start()
     pairs = mats.shape[2]
     steps = pairs // 2
     eye = (iota((steps, steps), 0) == iota((steps, steps), 1)).astype(jnp.bfloat16)
@@ -129,13 +107,9 @@
         )
         return total + dot(left, right, NN) * jnp.concatenate([rows32[pl.ds(a, K), :] for a, _ in fields_of], axis=1)
 
-    sums = lax.fori_loop(0, steps, two, jnp.zeros((K, 2 * items), jnp.float32), unroll=16)
+    sums = lax.fori_loop(0, steps, two, jnp.zeros((K, 2 * items), jnp.float32), unroll=32)
     line = jnp.sum(sums, axis=0, keepdims=True)
     out[...] = line[:, :items] + line[:, items:]
-    for copy in id_fetches:
-        copy.wait()
-    for j, row in enumerate(slot_rows(asked, cap, slots, user_rows, places.shape[1])):
-        places[j:j + 1, :] = row
 
 
 def thirds(x):
@@ -145,9 +119,10 @@
     return high, middle, (rest - middle.astype(jnp.float32)).astype(jnp.bfloat16)
 
 
-def linear_kernel(total, planes, *refs):
+def linear_kernel(total, planes, cap, user_rows, *refs):
     states, refs = refs[:total], refs[total:]
-    items, (places, out, hits, wanted, linear) = refs[:planes], refs[planes:]
+    items, refs = refs[:planes], refs[planes:]
+    users, (out, hits, wanted, linear) = refs[:total], refs[total:]
     slots = states[0].shape[0]
     own_rows, width = items[0].shape
     half = out.shape[1]
@@ -167,8 +142,18 @@
             linear[q * own_rows:(q + 1) * own_rows, t * count:(t + 1) * count] = part
     ids = [iota((own_rows, 1), 0) + (me * planes + ring(plane - q, planes)) * own_rows for q in range(planes)]
     item_ids = jnp.concatenate(ids, axis=0)
+    readers = users[0].shape[1]
+    across = iota((readers, readers), 1)
+    down = iota((readers, readers), 0)
+    asks = (iota((readers, half), 1) // (half // readers) == iota((readers, half), 0)).astype(jnp.float32).astype(jnp.bfloat16)
     for j in range(total):
-        spread = (iota((count, half), 0) == places[j:j + 1, :]).astype(jnp.float32).astype(jnp.bfloat16)
+        holder = users[j][...] >> (user_rows.bit_length() - 1)
+        column = jnp.sum(jnp.where(across == down, holder, 0), axis=1, keepdims=True)
+        rank = jnp.sum(jnp.where((down < across) & (column == holder), 1, 0), axis=0, keepdims=True)
+        arrival = jnp.where(holder > me, me - holder + total, me - holder)
+        slot = arrival * slots + ring(me - j, total) * cap + rank
+        at_slot = (iota((count, readers), 0) == slot).astype(jnp.float32).astype(jnp.bfloat16)
+        spread = dot(at_slot, asks, NN).astype(jnp.bfloat16)
         scores = dot(linear[...], jnp.concatenate([spread] * 3, axis=0), NN)
         hit = item_ids == cands[j]
         out[j:j + 1, :] = jnp.sum(jnp.where(hit, scores, 0.0), axis=0, keepdims=True)
@@ -215,7 +200,7 @@
         items = [item_table] + [shift(item_table, "cache", q) for q in range(1, planes)]
 
     with jax.named_scope("ids"):
-        users = [in_hbm(reader_users)] + [shift(reader_users, "shard", j) for j in range(1, total)]
+        users = [shift(reader_users, "shard", j) for j in range(1, total)]
 
     with jax.named_scope("turn"):
         *turned, states_near, own_ids, digits = pl.pallas_call(
@@ -246,6 +231,7 @@
         )
 
     with jax.named_scope("states"):
+        users_near = [own_ids] + [ids.reshape(1, readers) for ids in users]
         picked = pl.pallas_call(
             functools.partial(pick_kernel, total, cap),
             out_shape=jax.ShapeDtypeStruct((slots, width + half), jnp.bfloat16),
@@ -253,27 +239,23 @@
             out_specs=vmem,
             compiler_params=params,
             cost_estimate=pl.CostEstimate(flops=2 * slots * rows * width, bytes_accessed=1024 * 1024, transcendentals=0),
-        )(own_ids, *[ids.reshape(1, readers) for ids in users[1:]], digits, states_near)
+        )(*users_near, digits, states_near)
         states = [picked] + [shift(picked, "shard", j) for j in range(1, total)]
 
     with jax.named_scope("pairs"):
-        pair_parts, places = pl.pallas_call(
-            functools.partial(pair_kernel, total, cap, slots, user_states.shape[0]),
-            out_shape=(
-                jax.ShapeDtypeStruct((1, rows), jnp.float32),
-                jax.ShapeDtypeStruct((total, half), jnp.int32),
-            ),
-            in_specs=[anywhere] * total + [hbm, vmem, vmem, vmem, anywhere],
-            out_specs=(vmem, vmem),
+        pair_parts = pl.pallas_call(
+            pair_kernel,
+            out_shape=jax.ShapeDtypeStruct((1, rows), jnp.float32),
+            in_specs=[hbm, vmem, vmem, vmem, anywhere],
+            out_specs=vmem,
             scratch_shapes=[
-                pltpu.SMEM((total, readers), jnp.int32),
                 pltpu.SMEM((2, count), jnp.int32),
-                pltpu.VMEM((count // 2 * PITCH, LANES), jnp.float32),
-                pltpu.SemaphoreType.DMA((1 + total,)),
+                pltpu.VMEM((count // 2 * PITCH + K, LANES), jnp.float32),
+                pltpu.SemaphoreType.DMA,
             ],
             compiler_params=params,
             cost_estimate=pl.CostEstimate(flops=2 * count * K * K * rows * 16, bytes_accessed=4 * 1024 * 1024, transcendentals=0),
-        )(*users, in_hbm(pair_fields.T), *turned, picked)
+        )(in_hbm(pair_fields.T), *turned, picked)
         pair_scores = {(0, 0): pair_parts}
         steps = [(q, h) for q in range(planes - 1, -1, -1) for h in range(parts) if q or h]
         for q, h in steps:
@@ -288,12 +270,12 @@
 
     with jax.named_scope("scores"):
         linear, hits = pl.pallas_call(
-            functools.partial(linear_kernel, total, planes),
+            functools.partial(linear_kernel, total, planes, cap, user_states.shape[0]),
             out_shape=(
                 jax.ShapeDtypeStruct((total, half), jnp.float32),
                 jax.ShapeDtypeStruct((planes * rows, total * half), jnp.bfloat16),
             ),
-            in_specs=[vmem] * (total + len(items) + 1),
+            in_specs=[vmem] * (2 * total + len(items)),
             out_specs=(vmem, vmem),
             scratch_shapes=[
                 pltpu.VMEM((total * slots, width), jnp.bfloat16),
@@ -301,7 +283,7 @@
             ],
             compiler_params=params,
             cost_estimate=pl.CostEstimate(flops=2 * 64 * 256 * width, bytes_accessed=2 * 1024 * 1024, transcendentals=0),
-        )(*states, *items, places)
+        )(*states, *items, *users_near)
         outs = pl.pallas_call(
             functools.partial(score_kernel, total, planes, parts),
             out_shape=[jax.ShapeDtypeStruct((1, half), jnp.float32)] * total,

time: 30.5 us -> 30.8 us (level)
  waiting for transfers between devices: 3.1 us -> 4.08 us
  Pallas kernels: 8.01 us -> 7.4 us
    ppermute x10, waiting for transfers between devices: 2.59 us -> 4.07 us  [shift(): return lax.ppermute(x, axis, [(s, (s + step) % size) for s in range(size)])]
    ppermute x3, starting transfers between devices: 1.27 us -> 0.6 us  [body(): pair_scores[q, h] = lax.ppermute(source, ('cache', 'pair'), perm)]
    pallas_call x2, Pallas kernels: 5.25 us -> 4.65 us  [the longest x1 3.41 us: body(): pl.pallas_call(pair_kernel, out_shape=jax.ShapeDtypeStruct((1, rows), jnp...]
    ppermute x10, starting transfers between devices: 17.4 us -> 18 us  [shift(): return lax.ppermute(x, axis, [(s, (s + step) % size) for s in range(size)])]
    ppermute x3, waiting for transfers between devices: 0.5 us -> 0.01 us  [body(): pair_scores[q, h] = lax.ppermute(source, ('cache', 'pair'), perm)]
  transfers between devices with their start and end apart: 13 -> 13, of which waited for: 6 -> 4; matrix products, arithmetic and copies ran while one was open for 0% -> 0% of each run, Pallas kernels for 26% -> 24%
where the time goes in v22:
time: 30.8 us; the launch traced here: 30.7 us
  starting transfers between devices  18.6 us (60%)
  Pallas kernels  7.4 us (24%)
  waiting for transfers between devices  4.08 us (13%)
  other arithmetic  0.52 us (2%)
    ppermute x10, starting transfers between devices, shift(): return lax.ppermute(x, axis, [(s, (s + step) % size) for s in range(size)])  18 us
    ppermute x10, waiting for transfers between devices, shift(): return lax.ppermute(x, axis, [(s, (s + step) % size) for s in range(size)])  4.07 us
    pallas_call x1, Pallas kernels, body(): pl.pallas_call(pair_kernel, out_shape=jax.ShapeDtypeStruct((1, rows), jnp...  3.41 us
    pallas_call x1, Pallas kernels, body(): pl.pallas_call(turn_kernel, out_shape=(jax.ShapeDtypeStruct((width, rows)...  2.2 us
    pallas_call x1, Pallas kernels, body(): pl.pallas_call(functools.partial(linear_kernel, total, planes, cap, user_...  1.23 us
  transfers between devices with their start and end apart: 13, of which 4 were waited for; matrix products, arithmetic and copies ran while one was open for 0% of the time, Pallas kernels for 24%

profile of v22, /device:TPU:0, one launch (start us, length us, event | category | flops | bytes accessed | tf_op | source)
XLA Modules:
  0.0 30.7 jit_solution(12372747034528878083)
XLA Ops:
  0.0 2.9 %collective-permute-start.9 = (bf16[128,3072]{1,0:T(8,128)(2,1)}, bf16[128,3072]{1,0:T(8,128)(2,1)S(1)}, u32[]{:S(2)}, u32[]{:S(2)}) collective-permute-start(bf16[128,3072]{1,0:T(8,128)(2,1)} %refs_4_.1), channel_id=1, source_target_pairs={{0,2},{2,0},{1,3},{3,1},{4,6},{6,4},{5,7},{7,5},{8,10},{10,8},{9,1... | collective-permute-start | bytes 2359304 | tf_op jit(solution)/shard_map/item_rows/ppermute | solution.py:178
  2.9 1.6 %collective-permute-start = (s32[8]{0:T(128)}, s32[8]{0:T(128)S(1)}, u32[]{:S(2)}, u32[]{:S(2)}) collective-permute-start(s32[8]{0:T(128)} %param.7), channel_id=1, source_target_pairs={{0,4},{4,8},{8,12},{12,0},{1,5},{5,9},{9,13},{13,1},{2,6},{6,10},{... | collective-permute-start | bytes 104 | tf_op jit(solution)/shard_map/ids/ppermute | solution.py:178
  4.5 2.6 %collective-permute-start.1 = (s32[8]{0:T(128)}, s32[8]{0:T(128)S(1)}, u32[]{:S(2)}, u32[]{:S(2)}) collective-permute-start(s32[8]{0:T(128)} %param.7), channel_id=1, source_target_pairs={{0,8},{4,12},{8,0},{12,4},{1,9},{5,13},{9,1},{13,5},{2,10},{6,14},... | collective-permute-start | bytes 104 | tf_op jit(solution)/shard_map/ids/ppermute | solution.py:178
  7.1 1.3 %collective-permute-start.2 = (s32[8]{0:T(128)}, s32[8]{0:T(128)S(1)}, u32[]{:S(2)}, u32[]{:S(2)}) collective-permute-start(s32[8]{0:T(128)} %param.7), channel_id=1, source_target_pairs={{0,12},{4,0},{8,4},{12,8},{1,13},{5,1},{9,5},{13,9},{2,14},{6,2},{... | collective-permute-start | bytes 104 | tf_op jit(solution)/shard_map/ids/ppermute | solution.py:178
  8.5 2.2 %turn.1 = (f32[3072,128]{1,0:T(8,128)S(1)}, bf16[3072,128]{1,0:T(8,128)(2,1)S(1)}, bf16[64,64,256]{2,1,0:T(8,128)(2,1)S(1)}, bf16[128,3072]{1,0:T(8,128)(2,1)S(1...) custom-call(bf16[128,3072]{1,0:T(8,128)(2,1)} %refs_4_.1, bf16[64,64,256]{2,1,0:T(8,128)(2,1)} %bitcast.15, ...), custom_call_target="tpu_custom_call" | custom-call | flops 1610612736 | bytes 8388608 | tf_op jit(solution)/shard_map/turn/pallas_call | solution.py:206
  10.7 0.0 collective-permute-done
  10.7 0.0 collective-permute-done.1
  10.7 0.1 collective-permute-done.2
  10.8 0.4 %states.1.picked.refs_0_ = bf16[16,3200]{1,0:T(8,128)(2,1)S(1)} custom-call(s32[1,8]{1,0:T(1,128)S(1)} %get-tuple-element.24.refs_0_.refs_6_, s32[1,8]{1,0:T(1,128)S(1)} %bitcast.9, s32[1,8]{1,0:T(1,128)S(1)} %bitcast.11, s32[1,8]{1,0:T(1,128)S(1)} %bitcast.13, bf16[16,128]{1,0:T(8,128)(2,1)S(1)} %get-tuple-element.25.refs_4_, ...), custom_call_target="tpu_custom_call" | custom-call | flops 12582912 | bytes 1048576 | tf_op jit(solution)/shard_map/states/pallas_call | solution.py:235
  11.2 0.6 %collective-permute-start.4 = (bf16[16,3200]{1,0:T(8,128)(2,1)S(1)}, bf16[16,3200]{1,0:T(8,128)(2,1)S(1)}, u32[]{:S(2)}, u32[]{:S(2)}) collective-permute-start(bf16[16,3200]{1,0:T(8,128)(2,1)S(1)} %states.1.picked.refs_0_), channel_id=1, source_target_pairs={{0,4},{4,8},{8,12},{12,0},{1,5},{5,9},{9,13},{13,1},{2,6},{6,10},{... | collective-permute-start | bytes 307208 | tf_op jit(solution)/shard_map/states/ppermute | solution.py:178
  11.8 3.1 %collective-permute-start.6 = (bf16[16,3200]{1,0:T(8,128)(2,1)S(1)}, bf16[16,3200]{1,0:T(8,128)(2,1)S(1)}, u32[]{:S(2)}, u32[]{:S(2)}) collective-permute-start(bf16[16,3200]{1,0:T(8,128)(2,1)S(1)} %states.1.picked.refs_0_), channel_id=1, source_target_pairs={{0,8},{4,12},{8,0},{12,4},{1,9},{5,13},{9,1},{13,5},{2,10},{6,14},... | collective-permute-start | bytes 307208 | tf_op jit(solution)/shard_map/states/ppermute | solution.py:178
  14.9 0.1 collective-permute-start.8
  15.1 0.0 copy-start
  15.1 3.4 %pairs.1.refs_1_ = f32[1,128]{1,0:T(1,128)S(1)} custom-call(s32[2,256]{1,0:T(2,128)} %bitcast.16, f32[3072,128]{1,0:T(8,128)S(1)} %get-tuple-element.21.rows32, bf16[3072,128]{1,0:T(8,128)(2,1)S(1)} %get-tuple-element.22.rows16, bf16[64,64,256]{2,1,0:T(8,128)(2,1)S(1)} %get-tuple-element.23.mats, bf16[16,3200]{1,0:T(8,128)(2,1)S(1)} %states.1.picked.refs_0_), custom_call_target="tpu_custom_call" | custom-call | flops 4294967296 | bytes 4194304 | tf_op jit(solution)/shard_map/pairs/pallas_call | solution.py:246
  18.5 0.6 %collective-permute-start.3 = (f32[1,128]{1,0:T(1,128)S(1)}, f32[1,128]{1,0:T(1,128)S(1)}, u32[]{:S(2)}, u32[]{:S(2)}) collective-permute-start(f32[1,128]{1,0:T(1,128)S(1)} %pairs.1.refs_1_), channel_id=1, source_target_pairs={{0,2},{1,3},{2,0},{3,1},{4,6},{5,7},{6,4},{7,5},{8,10},{9,11},{10,... | collective-permute-start | bytes 1544 | tf_op jit(solution)/shard_map/pairs/ppermute | solution.py:268
  19.1 0.0 collective-permute-done.4.refs_1_
  19.1 0.0 collective-permute-start.5
  19.1 1.9 %collective-permute-done.6.refs_2_ = bf16[16,3200]{1,0:T(8,128)(2,1)S(1)} collective-permute-done((bf16[16,3200]{1,0:T(8,128)(2,1)S(1)}, bf16[16,3200]{1,0:T(8,128)(2,1)S(1)}, u32[]{:S(2)}, u32[]{:S(2)}) %collective-permute-start.6) | collective-permute-done | bytes 102432 | tf_op jit(solution)/shard_map/states/ppermute | solution.py:178
  21.0 0.0 collective-permute-start.7
  21.0 0.0 collective-permute-done.8.refs_3_
  21.0 0.0 collective-permute-done.9.refs_5_
  21.0 0.0 copy-done
  21.0 1.2 %scores.2 = (f32[4,128]{1,0:T(4,128)S(1)}, bf16[256,512]{1,0:T(8,128)(2,1)S(1)}) custom-call(bf16[16,3200]{1,0:T(8,128)(2,1)S(1)} %states.1.picked.refs_0_, bf16[16,3200]{1,0:T(8,128)(2,1)S(1)} %collective-permute-done.4.refs_1_, bf16[16,3200]{1,0:T(8,128)(2,1)S(1)} %collective-permute-done.6.refs_2_, bf16[16,3200]{1,0:T(8,128)(2,1)S(1)} %collective-permute-done.8.refs_3_, ...), custom_call_target="tpu_custom_call" | custom-call | flops 100663296 | bytes 2097152 | tf_op jit(solution)/shard_map/scores/pallas_call | solution.py:272
  22.2 0.0 collective-permute-done.3.refs_0_
  22.3 0.0 collective-permute-done.5.refs_2_
  22.3 0.0 collective-permute-done.7.refs_3_
  22.3 0.2 scores.3
  22.4 2.1 %collective-permute-start.12 = (f32[1,128]{1,0:T(1,128)S(1)}, f32[1,128]{1,0:T(1,128)S(1)}, u32[]{:S(2)}, u32[]{:S(2)}) collective-permute-start(f32[1,128]{1,0:T(1,128)S(1)} %get-tuple-element.36), channel_id=1, source_target_pairs={{0,4},{4,8},{8,12},{12,0},{1,5},{5,9},{9,13},{13,1},{2,6},{6,10},{... | collective-permute-start | bytes 1544 | tf_op jit(solution)/shard_map/back/ppermute | solution.py:178
  24.6 2.0 %collective-permute-start.11 = (f32[1,128]{1,0:T(1,128)S(1)}, f32[1,128]{1,0:T(1,128)S(1)}, u32[]{:S(2)}, u32[]{:S(2)}) collective-permute-start(f32[1,128]{1,0:T(1,128)S(1)} %get-tuple-element.35), channel_id=1, source_target_pairs={{0,8},{4,12},{8,0},{12,4},{1,9},{5,13},{9,1},{13,5},{2,10},{6,14},... | collective-permute-start | bytes 1544 | tf_op jit(solution)/shard_map/back/ppermute | solution.py:178
  26.6 1.5 %collective-permute-start.10 = (f32[1,128]{1,0:T(1,128)S(1)}, f32[1,128]{1,0:T(1,128)S(1)}, u32[]{:S(2)}, u32[]{:S(2)}) collective-permute-start(f32[1,128]{1,0:T(1,128)S(1)} %get-tuple-element.34), channel_id=1, source_target_pairs={{0,12},{4,0},{8,4},{12,8},{1,13},{5,1},{9,5},{13,9},{2,14},{6,2},{... | collective-permute-start | bytes 1544 | tf_op jit(solution)/shard_map/back/ppermute | solution.py:178
  28.1 0.0 collective-permute-done.12
  28.1 0.9 %collective-permute-done.11 = f32[1,128]{1,0:T(1,128)S(1)} collective-permute-done((f32[1,128]{1,0:T(1,128)S(1)}, f32[1,128]{1,0:T(1,128)S(1)}, u32[]{:S(2)}, u32[]{:S(2)}) %collective-permute-start.11) | collective-permute-done | bytes 544 | tf_op jit(solution)/shard_map/back/ppermute | solution.py:178
  29.0 1.1 %collective-permute-done.10 = f32[1,128]{1,0:T(1,128)S(1)} collective-permute-done((f32[1,128]{1,0:T(1,128)S(1)}, f32[1,128]{1,0:T(1,128)S(1)}, u32[]{:S(2)}, u32[]{:S(2)}) %collective-permute-start.10) | collective-permute-done | bytes 544 | tf_op jit(solution)/shard_map/back/ppermute | solution.py:178
  30.1 0.5 %add_bitcast_fusion = f32[128]{0:T(128)} fusion(f32[1,128]{1,0:T(1,128)S(1)} %collective-permute-done.12, f32[1,128]{1,0:T(1,128)S(1)} %collective-permute-done.11, f32[1,128]{1,0:T(1,128)S(1)} %get-tuple-element.33, f32[1,128]{1,0:T(1,128)S(1)} %collective-permute-done.10), kind=kLoop, calls=%fused_computation | loop fusion | flops 384 | bytes 2560 | tf_op jit(solution)/shard_map/reshape | solution.py:300
Async XLA Ops:
  0.0 21.0 %collective-permute-start.9 = (bf16[128,3072]{1,0:T(8,128)(2,1)}, bf16[128,3072]{1,0:T(8,128)(2,1)S(1)}, u32[]{:S(2)}, u32[]{:S(2)}) collective-permute-start(bf16[128,3072]{1,0:T(8,128)(2,1)} %refs_4_.1), channel_id=1, source_target_pairs={{0,2},{2,0},{1,3},{3,1},{4,6},{6,4},{5,7},{7,5},{8,10},{10,8},{9,1... | collective-permute-start | bytes 2359304 | tf_op jit(solution)/shard_map/item_rows/ppermute | solution.py:178
  2.9 7.7 %collective-permute-start = (s32[8]{0:T(128)}, s32[8]{0:T(128)S(1)}, u32[]{:S(2)}, u32[]{:S(2)}) collective-permute-start(s32[8]{0:T(128)} %param.7), channel_id=1, source_target_pairs={{0,4},{4,8},{8,12},{12,0},{1,5},{5,9},{9,13},{13,1},{2,6},{6,10},{... | collective-permute-start | bytes 104 | tf_op jit(solution)/shard_map/ids/ppermute | solution.py:178
  4.5 6.2 %collective-permute-start.1 = (s32[8]{0:T(128)}, s32[8]{0:T(128)S(1)}, u32[]{:S(2)}, u32[]{:S(2)}) collective-permute-start(s32[8]{0:T(128)} %param.7), channel_id=1, source_target_pairs={{0,8},{4,12},{8,0},{12,4},{1,9},{5,13},{9,1},{13,5},{2,10},{6,14},... | collective-permute-start | bytes 104 | tf_op jit(solution)/shard_map/ids/ppermute | solution.py:178
  7.1 3.7 %collective-permute-start.2 = (s32[8]{0:T(128)}, s32[8]{0:T(128)S(1)}, u32[]{:S(2)}, u32[]{:S(2)}) collective-permute-start(s32[8]{0:T(128)} %param.7), channel_id=1, source_target_pairs={{0,12},{4,0},{8,4},{12,8},{1,13},{5,1},{9,5},{13,9},{2,14},{6,2},{... | collective-permute-start | bytes 104 | tf_op jit(solution)/shard_map/ids/ppermute | solution.py:178
  11.2 7.9 %collective-permute-start.4 = (bf16[16,3200]{1,0:T(8,128)(2,1)S(1)}, bf16[16,3200]{1,0:T(8,128)(2,1)S(1)}, u32[]{:S(2)}, u32[]{:S(2)}) collective-permute-start(bf16[16,3200]{1,0:T(8,128)(2,1)S(1)} %states.1.picked.refs_0_), channel_id=1, source_target_pairs={{0,4},{4,8},{8,12},{12,0},{1,5},{5,9},{9,13},{13,1},{2,6},{6,10},{... | collective-permute-start | bytes 307208 | tf_op jit(solution)/shard_map/states/ppermute | solution.py:178
  11.8 9.2 %collective-permute-start.6 = (bf16[16,3200]{1,0:T(8,128)(2,1)S(1)}, bf16[16,3200]{1,0:T(8,128)(2,1)S(1)}, u32[]{:S(2)}, u32[]{:S(2)}) collective-permute-start(bf16[16,3200]{1,0:T(8,128)(2,1)S(1)} %states.1.picked.refs_0_), channel_id=1, source_target_pairs={{0,8},{4,12},{8,0},{12,4},{1,9},{5,13},{9,1},{13,5},{2,10},{6,14},... | collective-permute-start | bytes 307208 | tf_op jit(solution)/shard_map/states/ppermute | solution.py:178
  14.9 6.1 %collective-permute-start.8 = (bf16[16,3200]{1,0:T(8,128)(2,1)S(1)}, bf16[16,3200]{1,0:T(8,128)(2,1)S(1)}, u32[]{:S(2)}, u32[]{:S(2)}) collective-permute-start(bf16[16,3200]{1,0:T(8,128)(2,1)S(1)} %states.1.picked.refs_0_), channel_id=1, source_target_pairs={{0,12},{4,0},{8,4},{12,8},{1,13},{5,1},{9,5},{13,9},{2,14},{6,2},{... | collective-permute-start | bytes 307208 | tf_op jit(solution)/shard_map/states/ppermute | solution.py:178
  15.1 6.0 %copy-start = (bf16[128,3072]{1,0:T(8,128)(2,1)S(1)}, bf16[128,3072]{1,0:T(8,128)(2,1)}, u32[]{:S(2)}) copy-start(bf16[128,3072]{1,0:T(8,128)(2,1)} %refs_4_.1) | copy-start | bytes 2359300
  18.5 3.8 %collective-permute-start.3 = (f32[1,128]{1,0:T(1,128)S(1)}, f32[1,128]{1,0:T(1,128)S(1)}, u32[]{:S(2)}, u32[]{:S(2)}) collective-permute-start(f32[1,128]{1,0:T(1,128)S(1)} %pairs.1.refs_1_), channel_id=1, source_target_pairs={{0,2},{1,3},{2,0},{3,1},{4,6},{5,7},{6,4},{7,5},{8,10},{9,11},{10,... | collective-permute-start | bytes 1544 | tf_op jit(solution)/shard_map/pairs/ppermute | solution.py:268
  19.1 3.2 %collective-permute-start.5 = (f32[1,128]{1,0:T(1,128)S(1)}, f32[1,128]{1,0:T(1,128)S(1)}, u32[]{:S(2)}, u32[]{:S(2)}) collective-permute-start(f32[1,128]{1,0:T(1,128)S(1)} %pairs.1.refs_1_), channel_id=1, source_target_pairs={{0,3},{1,2},{2,1},{3,0},{4,7},{5,6},{6,5},{7,4},{8,11},{9,10},{10,... | collective-permute-start | bytes 1544 | tf_op jit(solution)/shard_map/pairs/ppermute | solution.py:268
  21.0 1.3 %collective-permute-start.7 = (f32[1,128]{1,0:T(1,128)S(1)}, f32[1,128]{1,0:T(1,128)S(1)}, u32[]{:S(2)}, u32[]{:S(2)}) collective-permute-start(f32[1,128]{1,0:T(1,128)S(1)} %pairs.1.refs_1_), channel_id=1, source_target_pairs={{0,1},{1,0},{2,3},{3,2},{4,5},{5,4},{6,7},{7,6},{8,9},{9,8},{10,11... | collective-permute-start | bytes 1544 | tf_op jit(solution)/shard_map/pairs/ppermute | solution.py:268
  22.4 5.6 %collective-permute-start.12 = (f32[1,128]{1,0:T(1,128)S(1)}, f32[1,128]{1,0:T(1,128)S(1)}, u32[]{:S(2)}, u32[]{:S(2)}) collective-permute-start(f32[1,128]{1,0:T(1,128)S(1)} %get-tuple-element.36), channel_id=1, source_target_pairs={{0,4},{4,8},{8,12},{12,0},{1,5},{5,9},{9,13},{13,1},{2,6},{6,10},{... | collective-permute-start | bytes 1544 | tf_op jit(solution)/shard_map/back/ppermute | solution.py:178
  24.6 4.4 %collective-permute-start.11 = (f32[1,128]{1,0:T(1,128)S(1)}, f32[1,128]{1,0:T(1,128)S(1)}, u32[]{:S(2)}, u32[]{:S(2)}) collective-permute-start(f32[1,128]{1,0:T(1,128)S(1)} %get-tuple-element.35), channel_id=1, source_target_pairs={{0,8},{4,12},{8,0},{12,4},{1,9},{5,13},{9,1},{13,5},{2,10},{6,14},... | collective-permute-start | bytes 1544 | tf_op jit(solution)/shard_map/back/ppermute | solution.py:178
  26.6 3.5 %collective-permute-start.10 = (f32[1,128]{1,0:T(1,128)S(1)}, f32[1,128]{1,0:T(1,128)S(1)}, u32[]{:S(2)}, u32[]{:S(2)}) collective-permute-start(f32[1,128]{1,0:T(1,128)S(1)} %get-tuple-element.34), channel_id=1, source_target_pairs={{0,12},{4,0},{8,4},{12,8},{1,13},{5,1},{9,5},{13,9},{2,14},{6,2},{... | collective-permute-start | bytes 1544 | tf_op jit(solution)/shard_map/back/ppermute | solution.py:178

commit v23 on v22

--- a/solution.py
+++ b/solution.py
@@ -82,10 +82,23 @@
     states_fetch.wait()
 
 
-def pair_kernel(fields_hbm, rows32, rows16, mats, picked, out, fields, stacked, sem):
+def pair_kernel(total, cap, slots, user_rows, *refs):
+    users, (fields_hbm, rows32, rows16, mats, picked, out, places, fields, stacked, sem) = refs[:total], refs[total:]
     del picked
     fields_fetch = pltpu.make_async_copy(fields_hbm, fields, sem)
     fields_fetch.start()
+    me = lax.axis_index("shard")
+    readers, half = users[0].shape[1], places.shape[1]
+    across = iota((readers, readers), 1)
+    down = iota((readers, readers), 0)
+    asks = (iota((readers, half), 1) // (half // readers) == iota((readers, half), 0)).astype(jnp.float32)
+    for j in range(total):
+        holder = users[j][...] >> (user_rows.bit_length() - 1)
+        column = jnp.sum(jnp.where(across == down, holder, 0), axis=1, keepdims=True)
+        rank = jnp.sum(jnp.where((down < across) & (column == holder), 1, 0), axis=0, keepdims=True)
+        arrival = jnp.where(holder > me, me - holder + total, me - holder)
+        slot = (arrival * slots + ring(me - j, total) * cap + rank).astype(jnp.float32)
+        places[j:j + 1, :] = dot(slot, asks, NN, precision=lax.Precision.HIGHEST).astype(jnp.int32)
     pairs = mats.shape[2]
     steps = pairs // 2
     eye = (iota((steps, steps), 0) == iota((steps, steps), 1)).astype(jnp.bfloat16)
@@ -119,10 +132,10 @@
     return high, middle, (rest - middle.astype(jnp.float32)).astype(jnp.bfloat16)
 
 
-def linear_kernel(total, planes, cap, user_rows, *refs):
+def linear_kernel(total, planes, *refs):
     states, refs = refs[:total], refs[total:]
     items, refs = refs[:planes], refs[planes:]
-    users, (out, hits, wanted, linear) = refs[:total], refs[total:]
+    places, out, hits, wanted, linear = refs
     slots = states[0].shape[0]
     own_rows, width = items[0].shape
     half = out.shape[1]
@@ -142,18 +155,8 @@
             linear[q * own_rows:(q + 1) * own_rows, t * count:(t + 1) * count] = part
     ids = [iota((own_rows, 1), 0) + (me * planes + ring(plane - q, planes)) * own_rows for q in range(planes)]
     item_ids = jnp.concatenate(ids, axis=0)
-    readers = users[0].shape[1]
-    across = iota((readers, readers), 1)
-    down = iota((readers, readers), 0)
-    asks = (iota((readers, half), 1) // (half // readers) == iota((readers, half), 0)).astype(jnp.float32).astype(jnp.bfloat16)
-    for j in range(total):
-        holder = users[j][...] >> (user_rows.bit_length() - 1)
-        column = jnp.sum(jnp.where(across == down, holder, 0), axis=1, keepdims=True)
-        rank = jnp.sum(jnp.where((down < across) & (column == holder), 1, 0), axis=0, keepdims=True)
-        arrival = jnp.where(holder > me, me - holder + total, me - holder)
-        slot = arrival * slots + ring(me - j, total) * cap + rank
-        at_slot = (iota((count, readers), 0) == slot).astype(jnp.float32).astype(jnp.bfloat16)
-        spread = dot(at_slot, asks, NN).astype(jnp.bfloat16)
+    for j in range(total):
+        spread = (iota((count, half), 0) == places[j:j + 1, :]).astype(jnp.float32).astype(jnp.bfloat16)
         scores = dot(linear[...], jnp.concatenate([spread] * 3, axis=0), NN)
         hit = item_ids == cands[j]
         out[j:j + 1, :] = jnp.sum(jnp.where(hit, scores, 0.0), axis=0, keepdims=True)
@@ -243,11 +246,14 @@
         states = [picked] + [shift(picked, "shard", j) for j in range(1, total)]
 
     with jax.named_scope("pairs"):
-        pair_parts = pl.pallas_call(
-            pair_kernel,
-            out_shape=jax.ShapeDtypeStruct((1, rows), jnp.float32),
-            in_specs=[hbm, vmem, vmem, vmem, anywhere],
-            out_specs=vmem,
+        pair_parts, places = pl.pallas_call(
+            functools.partial(pair_kernel, total, cap, slots, user_states.shape[0]),
+            out_shape=(
+                jax.ShapeDtypeStruct((1, rows), jnp.float32),
+                jax.ShapeDtypeStruct((total, half), jnp.int32),
+            ),
+            in_specs=[vmem] * total + [hbm, vmem, vmem, vmem, anywhere],
+            out_specs=(vmem, vmem),
             scratch_shapes=[
                 pltpu.SMEM((2, count), jnp.int32),
                 pltpu.VMEM((count // 2 * PITCH + K, LANES), jnp.float32),
@@ -255,7 +261,7 @@
             ],
             compiler_params=params,
             cost_estimate=pl.CostEstimate(flops=2 * count * K * K * rows * 16, bytes_accessed=4 * 1024 * 1024, transcendentals=0),
-        )(in_hbm(pair_fields.T), *turned, picked)
+        )(*users_near, in_hbm(pair_fields.T), *turned, picked)
         pair_scores = {(0, 0): pair_parts}
         steps = [(q, h) for q in range(planes - 1, -1, -1) for h in range(parts) if q or h]
         for q, h in steps:
@@ -270,12 +276,12 @@
 
     with jax.named_scope("scores"):
         linear, hits = pl.pallas_call(
-            functools.partial(linear_kernel, total, planes, cap, user_states.shape[0]),
+            functools.partial(linear_kernel, total, planes),
             out_shape=(
                 jax.ShapeDtypeStruct((total, half), jnp.float32),
                 jax.ShapeDtypeStruct((planes * rows, total * half), jnp.bfloat16),
             ),
-            in_specs=[vmem] * (2 * total + len(items)),
+            in_specs=[vmem] * (total + len(items) + 1),
             out_specs=(vmem, vmem),
             scratch_shapes=[
                 pltpu.VMEM((total * slots, width), jnp.bfloat16),
@@ -283,7 +289,7 @@
             ],
             compiler_params=params,
             cost_estimate=pl.CostEstimate(flops=2 * 64 * 256 * width, bytes_accessed=2 * 1024 * 1024, transcendentals=0),
-        )(*states, *items, *users_near)
+        )(*states, *items, places)
         outs = pl.pallas_call(
             functools.partial(score_kernel, total, planes, parts),
             out_shape=[jax.ShapeDtypeStruct((1, half), jnp.float32)] * total,

time: 30.8 us -> 30.5 us (level)
    ppermute x10, waiting for transfers between devices: 4.07 us -> 3.66 us  [shift(): return lax.ppermute(x, axis, [(s, (s + step) % size) for s in range(size)])]
  transfers between devices with their start and end apart: 13 -> 13, of which waited for: 4 -> 5; matrix products, arithmetic and copies ran while one was open for 0% -> 0% of each run, Pallas kernels for 24% -> 23%
where the time goes in v23:
time: 30.5 us; the launch traced here: 30.3 us
  starting transfers between devices  18.7 us (61%)
  Pallas kernels  7.14 us (23%)
  waiting for transfers between devices  3.9 us (13%)
  other arithmetic  0.52 us (2%)
    ppermute x10, starting transfers between devices, shift(): return lax.ppermute(x, axis, [(s, (s + step) % size) for s in range(size)])  18.1 us
    ppermute x10, waiting for transfers between devices, shift(): return lax.ppermute(x, axis, [(s, (s + step) % size) for s in range(size)])  3.66 us
    pallas_call x1, Pallas kernels, body(): pl.pallas_call(functools.partial(pair_kernel, total, cap, slots, user_sta...  3.48 us
    pallas_call x1, Pallas kernels, body(): pl.pallas_call(turn_kernel, out_shape=(jax.ShapeDtypeStruct((width, rows)...  2.2 us
    pallas_call x1, Pallas kernels, body(): pl.pallas_call(functools.partial(linear_kernel, total, planes), out_shape...  0.9 us
  transfers between devices with their start and end apart: 13, of which 5 were waited for; matrix products, arithmetic and copies ran while one was open for 0% of the time, Pallas kernels for 23%

profile of v23, /device:TPU:0, one launch (start us, length us, event | category | flops | bytes accessed | tf_op | source)
XLA Modules:
  0.0 30.3 jit_solution(7713260313504849744)
XLA Ops:
  0.0 2.9 %collective-permute-start.9 = (bf16[128,3072]{1,0:T(8,128)(2,1)}, bf16[128,3072]{1,0:T(8,128)(2,1)S(1)}, u32[]{:S(2)}, u32[]{:S(2)}) collective-permute-start(bf16[128,3072]{1,0:T(8,128)(2,1)} %refs_4_.1), channel_id=1, source_target_pairs={{0,2},{2,0},{1,3},{3,1},{4,6},{6,4},{5,7},{7,5},{8,10},{10,8},{9,1... | collective-permute-start | bytes 2359304 | tf_op jit(solution)/shard_map/item_rows/ppermute | solution.py:181
  2.9 1.6 %collective-permute-start = (s32[8]{0:T(128)}, s32[8]{0:T(128)S(1)}, u32[]{:S(2)}, u32[]{:S(2)}) collective-permute-start(s32[8]{0:T(128)} %param.7), channel_id=1, source_target_pairs={{0,4},{4,8},{8,12},{12,0},{1,5},{5,9},{9,13},{13,1},{2,6},{6,10},{... | collective-permute-start | bytes 104 | tf_op jit(solution)/shard_map/ids/ppermute | solution.py:181
  4.5 2.6 %collective-permute-start.1 = (s32[8]{0:T(128)}, s32[8]{0:T(128)S(1)}, u32[]{:S(2)}, u32[]{:S(2)}) collective-permute-start(s32[8]{0:T(128)} %param.7), channel_id=1, source_target_pairs={{0,8},{4,12},{8,0},{12,4},{1,9},{5,13},{9,1},{13,5},{2,10},{6,14},... | collective-permute-start | bytes 104 | tf_op jit(solution)/shard_map/ids/ppermute | solution.py:181
  7.1 1.3 %collective-permute-start.2 = (s32[8]{0:T(128)}, s32[8]{0:T(128)S(1)}, u32[]{:S(2)}, u32[]{:S(2)}) collective-permute-start(s32[8]{0:T(128)} %param.7), channel_id=1, source_target_pairs={{0,12},{4,0},{8,4},{12,8},{1,13},{5,1},{9,5},{13,9},{2,14},{6,2},{... | collective-permute-start | bytes 104 | tf_op jit(solution)/shard_map/ids/ppermute | solution.py:181
  8.5 2.2 %turn.1 = (f32[3072,128]{1,0:T(8,128)S(1)}, bf16[3072,128]{1,0:T(8,128)(2,1)S(1)}, bf16[64,64,256]{2,1,0:T(8,128)(2,1)S(1)}, bf16[128,3072]{1,0:T(8,128)(2,1)S(1...) custom-call(bf16[128,3072]{1,0:T(8,128)(2,1)} %refs_4_.1, bf16[64,64,256]{2,1,0:T(8,128)(2,1)} %bitcast.15, ...), custom_call_target="tpu_custom_call" | custom-call | flops 1610612736 | bytes 8388608 | tf_op jit(solution)/shard_map/turn/pallas_call | solution.py:209
  10.7 0.0 collective-permute-done
  10.7 0.0 collective-permute-done.1
  10.7 0.1 collective-permute-done.2
  10.8 0.4 %states.1.refs_8_.refs_0_ = bf16[16,3200]{1,0:T(8,128)(2,1)S(1)} custom-call(s32[1,8]{1,0:T(1,128)S(1)} %get-tuple-element.23.refs_0_, s32[1,8]{1,0:T(1,128)S(1)} %bitcast.9, s32[1,8]{1,0:T(1,128)S(1)} %bitcast.11, s32[1,8]{1,0:T(1,128)S(1)} %bitcast.13, bf16[16,128]{1,0:T(8,128)(2,1)S(1)} %get-tuple-element.27.refs_4_, ...), custom_call_target="tpu_custom_call" | custom-call | flops 12582912 | bytes 1048576 | tf_op jit(solution)/shard_map/states/pallas_call | solution.py:238
  11.2 0.6 %collective-permute-start.4 = (bf16[16,3200]{1,0:T(8,128)(2,1)S(1)}, bf16[16,3200]{1,0:T(8,128)(2,1)S(1)}, u32[]{:S(2)}, u32[]{:S(2)}) collective-permute-start(bf16[16,3200]{1,0:T(8,128)(2,1)S(1)} %states.1.refs_8_.refs_0_), channel_id=1, source_target_pairs={{0,4},{4,8},{8,12},{12,0},{1,5},{5,9},{9,13},{13,1},{2,6},{6,10},{... | collective-permute-start | bytes 307208 | tf_op jit(solution)/shard_map/states/ppermute | solution.py:181
  11.8 3.1 %collective-permute-start.6 = (bf16[16,3200]{1,0:T(8,128)(2,1)S(1)}, bf16[16,3200]{1,0:T(8,128)(2,1)S(1)}, u32[]{:S(2)}, u32[]{:S(2)}) collective-permute-start(bf16[16,3200]{1,0:T(8,128)(2,1)S(1)} %states.1.refs_8_.refs_0_), channel_id=1, source_target_pairs={{0,8},{4,12},{8,0},{12,4},{1,9},{5,13},{9,1},{13,5},{2,10},{6,14},... | collective-permute-start | bytes 307208 | tf_op jit(solution)/shard_map/states/ppermute | solution.py:181
  14.9 0.1 collective-permute-start.8
  15.1 0.0 copy-start
  15.1 3.5 %pairs.1 = (f32[1,128]{1,0:T(1,128)S(1)}, s32[4,128]{1,0:T(4,128)S(1)}) custom-call(s32[1,8]{1,0:T(1,128)S(1)} %get-tuple-element.23.refs_0_, s32[1,8]{1,0:T(1,128)S(1)} %bitcast.10, s32[1,8]{1,0:T(1,128)S(1)} %bitcast.12, s32[1,8]{1,0:T(1,128)S(1)} %bitcast.14, s32[2,256]{1,0:T(2,128)} %bitcast.16, f32[3072,128]{1,0:T(8,128)S(1)} %get-tuple-element.24.refs_5_, ...), custom_call_target="tpu_custom_call" | custom-call | flops 4294967296 | bytes 4194304 | tf_op jit(solution)/shard_map/pairs/pallas_call | solution.py:249
  18.5 0.6 %collective-permute-start.3 = (f32[1,128]{1,0:T(1,128)S(1)}, f32[1,128]{1,0:T(1,128)S(1)}, u32[]{:S(2)}, u32[]{:S(2)}) collective-permute-start(f32[1,128]{1,0:T(1,128)S(1)} %get-tuple-element.31.refs_1_), channel_id=1, source_target_pairs={{0,2},{1,3},{2,0},{3,1},{4,6},{5,7},{6,4},{7,5},{8,10},{9,11},{10,... | collective-permute-start | bytes 1544 | tf_op jit(solution)/shard_map/pairs/ppermute | solution.py:274
  19.1 0.0 collective-permute-done.4.refs_1_
  19.1 0.0 collective-permute-start.5
  19.2 1.8 %collective-permute-done.6.refs_2_ = bf16[16,3200]{1,0:T(8,128)(2,1)S(1)} collective-permute-done((bf16[16,3200]{1,0:T(8,128)(2,1)S(1)}, bf16[16,3200]{1,0:T(8,128)(2,1)S(1)}, u32[]{:S(2)}, u32[]{:S(2)}) %collective-permute-start.6) | collective-permute-done | bytes 102432 | tf_op jit(solution)/shard_map/states/ppermute | solution.py:181
  21.0 0.0 collective-permute-start.7
  21.0 0.0 collective-permute-done.8.refs_3_
  21.0 0.0 collective-permute-done.9.refs_5_
  21.0 0.0 copy-done
  21.0 0.9 %scores.2 = (f32[4,128]{1,0:T(4,128)S(1)}, bf16[256,512]{1,0:T(8,128)(2,1)S(1)}) custom-call(bf16[16,3200]{1,0:T(8,128)(2,1)S(1)} %states.1.refs_8_.refs_0_, bf16[16,3200]{1,0:T(8,128)(2,1)S(1)} %collective-permute-done.4.refs_1_, bf16[16,3200]{1,0:T(8,128)(2,1)S(1)} %collective-permute-done.6.refs_2_, bf16[16,3200]{1,0:T(8,128)(2,1)S(1)} %collective-permute-done.8.refs_3_, ...), custom_call_target="tpu_custom_call" | custom-call | flops 100663296 | bytes 2097152 | tf_op jit(solution)/shard_map/scores/pallas_call | solution.py:278
  21.9 0.2 collective-permute-done.3.refs_0_
  22.2 0.0 collective-permute-done.5.refs_2_
  22.2 0.0 collective-permute-done.7.refs_3_
  22.2 0.2 scores.3
  22.3 2.0 %collective-permute-start.12 = (f32[1,128]{1,0:T(1,128)S(1)}, f32[1,128]{1,0:T(1,128)S(1)}, u32[]{:S(2)}, u32[]{:S(2)}) collective-permute-start(f32[1,128]{1,0:T(1,128)S(1)} %get-tuple-element.40), channel_id=1, source_target_pairs={{0,4},{4,8},{8,12},{12,0},{1,5},{5,9},{9,13},{13,1},{2,6},{6,10},{... | collective-permute-start | bytes 1544 | tf_op jit(solution)/shard_map/back/ppermute | solution.py:181
  24.3 2.0 %collective-permute-start.11 = (f32[1,128]{1,0:T(1,128)S(1)}, f32[1,128]{1,0:T(1,128)S(1)}, u32[]{:S(2)}, u32[]{:S(2)}) collective-permute-start(f32[1,128]{1,0:T(1,128)S(1)} %get-tuple-element.39), channel_id=1, source_target_pairs={{0,8},{4,12},{8,0},{12,4},{1,9},{5,13},{9,1},{13,5},{2,10},{6,14},... | collective-permute-start | bytes 1544 | tf_op jit(solution)/shard_map/back/ppermute | solution.py:181
  26.3 1.8 %collective-permute-start.10 = (f32[1,128]{1,0:T(1,128)S(1)}, f32[1,128]{1,0:T(1,128)S(1)}, u32[]{:S(2)}, u32[]{:S(2)}) collective-permute-start(f32[1,128]{1,0:T(1,128)S(1)} %get-tuple-element.38), channel_id=1, source_target_pairs={{0,12},{4,0},{8,4},{12,8},{1,13},{5,1},{9,5},{13,9},{2,14},{6,2},{... | collective-permute-start | bytes 1544 | tf_op jit(solution)/shard_map/back/ppermute | solution.py:181
  28.1 0.0 collective-permute-done.12
  28.1 0.6 %collective-permute-done.11 = f32[1,128]{1,0:T(1,128)S(1)} collective-permute-done((f32[1,128]{1,0:T(1,128)S(1)}, f32[1,128]{1,0:T(1,128)S(1)}, u32[]{:S(2)}, u32[]{:S(2)}) %collective-permute-start.11) | collective-permute-done | bytes 544 | tf_op jit(solution)/shard_map/back/ppermute | solution.py:181
  28.7 1.1 %collective-permute-done.10 = f32[1,128]{1,0:T(1,128)S(1)} collective-permute-done((f32[1,128]{1,0:T(1,128)S(1)}, f32[1,128]{1,0:T(1,128)S(1)}, u32[]{:S(2)}, u32[]{:S(2)}) %collective-permute-start.10) | collective-permute-done | bytes 544 | tf_op jit(solution)/shard_map/back/ppermute | solution.py:181
  29.8 0.5 %add_bitcast_fusion = f32[128]{0:T(128)} fusion(f32[1,128]{1,0:T(1,128)S(1)} %collective-permute-done.12, f32[1,128]{1,0:T(1,128)S(1)} %collective-permute-done.11, f32[1,128]{1,0:T(1,128)S(1)} %get-tuple-element.37, f32[1,128]{1,0:T(1,128)S(1)} %collective-permute-done.10), kind=kLoop, calls=%fused_computation | loop fusion | flops 384 | bytes 2560 | tf_op jit(solution)/shard_map/reshape | solution.py:306
Async XLA Ops:
  0.0 21.0 %collective-permute-start.9 = (bf16[128,3072]{1,0:T(8,128)(2,1)}, bf16[128,3072]{1,0:T(8,128)(2,1)S(1)}, u32[]{:S(2)}, u32[]{:S(2)}) collective-permute-start(bf16[128,3072]{1,0:T(8,128)(2,1)} %refs_4_.1), channel_id=1, source_target_pairs={{0,2},{2,0},{1,3},{3,1},{4,6},{6,4},{5,7},{7,5},{8,10},{10,8},{9,1... | collective-permute-start | bytes 2359304 | tf_op jit(solution)/shard_map/item_rows/ppermute | solution.py:181
  2.9 7.7 %collective-permute-start = (s32[8]{0:T(128)}, s32[8]{0:T(128)S(1)}, u32[]{:S(2)}, u32[]{:S(2)}) collective-permute-start(s32[8]{0:T(128)} %param.7), channel_id=1, source_target_pairs={{0,4},{4,8},{8,12},{12,0},{1,5},{5,9},{9,13},{13,1},{2,6},{6,10},{... | collective-permute-start | bytes 104 | tf_op jit(solution)/shard_map/ids/ppermute | solution.py:181
  4.5 6.2 %collective-permute-start.1 = (s32[8]{0:T(128)}, s32[8]{0:T(128)S(1)}, u32[]{:S(2)}, u32[]{:S(2)}) collective-permute-start(s32[8]{0:T(128)} %param.7), channel_id=1, source_target_pairs={{0,8},{4,12},{8,0},{12,4},{1,9},{5,13},{9,1},{13,5},{2,10},{6,14},... | collective-permute-start | bytes 104 | tf_op jit(solution)/shard_map/ids/ppermute | solution.py:181
  7.1 3.7 %collective-permute-start.2 = (s32[8]{0:T(128)}, s32[8]{0:T(128)S(1)}, u32[]{:S(2)}, u32[]{:S(2)}) collective-permute-start(s32[8]{0:T(128)} %param.7), channel_id=1, source_target_pairs={{0,12},{4,0},{8,4},{12,8},{1,13},{5,1},{9,5},{13,9},{2,14},{6,2},{... | collective-permute-start | bytes 104 | tf_op jit(solution)/shard_map/ids/ppermute | solution.py:181
  11.2 8.0 %collective-permute-start.4 = (bf16[16,3200]{1,0:T(8,128)(2,1)S(1)}, bf16[16,3200]{1,0:T(8,128)(2,1)S(1)}, u32[]{:S(2)}, u32[]{:S(2)}) collective-permute-start(bf16[16,3200]{1,0:T(8,128)(2,1)S(1)} %states.1.refs_8_.refs_0_), channel_id=1, source_target_pairs={{0,4},{4,8},{8,12},{12,0},{1,5},{5,9},{9,13},{13,1},{2,6},{6,10},{... | collective-permute-start | bytes 307208 | tf_op jit(solution)/shard_map/states/ppermute | solution.py:181
  11.8 9.2 %collective-permute-start.6 = (bf16[16,3200]{1,0:T(8,128)(2,1)S(1)}, bf16[16,3200]{1,0:T(8,128)(2,1)S(1)}, u32[]{:S(2)}, u32[]{:S(2)}) collective-permute-start(bf16[16,3200]{1,0:T(8,128)(2,1)S(1)} %states.1.refs_8_.refs_0_), channel_id=1, source_target_pairs={{0,8},{4,12},{8,0},{12,4},{1,9},{5,13},{9,1},{13,5},{2,10},{6,14},... | collective-permute-start | bytes 307208 | tf_op jit(solution)/shard_map/states/ppermute | solution.py:181
  14.9 6.1 %collective-permute-start.8 = (bf16[16,3200]{1,0:T(8,128)(2,1)S(1)}, bf16[16,3200]{1,0:T(8,128)(2,1)S(1)}, u32[]{:S(2)}, u32[]{:S(2)}) collective-permute-start(bf16[16,3200]{1,0:T(8,128)(2,1)S(1)} %states.1.refs_8_.refs_0_), channel_id=1, source_target_pairs={{0,12},{4,0},{8,4},{12,8},{1,13},{5,1},{9,5},{13,9},{2,14},{6,2},{... | collective-permute-start | bytes 307208 | tf_op jit(solution)/shard_map/states/ppermute | solution.py:181
  15.1 6.0 %copy-start = (bf16[128,3072]{1,0:T(8,128)(2,1)S(1)}, bf16[128,3072]{1,0:T(8,128)(2,1)}, u32[]{:S(2)}) copy-start(bf16[128,3072]{1,0:T(8,128)(2,1)} %refs_4_.1) | copy-start | bytes 2359300
  18.5 3.6 %collective-permute-start.3 = (f32[1,128]{1,0:T(1,128)S(1)}, f32[1,128]{1,0:T(1,128)S(1)}, u32[]{:S(2)}, u32[]{:S(2)}) collective-permute-start(f32[1,128]{1,0:T(1,128)S(1)} %get-tuple-element.31.refs_1_), channel_id=1, source_target_pairs={{0,2},{1,3},{2,0},{3,1},{4,6},{5,7},{6,4},{7,5},{8,10},{9,11},{10,... | collective-permute-start | bytes 1544 | tf_op jit(solution)/shard_map/pairs/ppermute | solution.py:274
  19.1 3.0 %collective-permute-start.5 = (f32[1,128]{1,0:T(1,128)S(1)}, f32[1,128]{1,0:T(1,128)S(1)}, u32[]{:S(2)}, u32[]{:S(2)}) collective-permute-start(f32[1,128]{1,0:T(1,128)S(1)} %get-tuple-element.31.refs_1_), channel_id=1, source_target_pairs={{0,3},{1,2},{2,1},{3,0},{4,7},{5,6},{6,5},{7,4},{8,11},{9,10},{10,... | collective-permute-start | bytes 1544 | tf_op jit(solution)/shard_map/pairs/ppermute | solution.py:274
  21.0 1.2 %collective-permute-start.7 = (f32[1,128]{1,0:T(1,128)S(1)}, f32[1,128]{1,0:T(1,128)S(1)}, u32[]{:S(2)}, u32[]{:S(2)}) collective-permute-start(f32[1,128]{1,0:T(1,128)S(1)} %get-tuple-element.31.refs_1_), channel_id=1, source_target_pairs={{0,1},{1,0},{2,3},{3,2},{4,5},{5,4},{6,7},{7,6},{8,9},{9,8},{10,11... | collective-permute-start | bytes 1544 | tf_op jit(solution)/shard_map/pairs/ppermute | solution.py:274
  22.3 5.8 %collective-permute-start.12 = (f32[1,128]{1,0:T(1,128)S(1)}, f32[1,128]{1,0:T(1,128)S(1)}, u32[]{:S(2)}, u32[]{:S(2)}) collective-permute-start(f32[1,128]{1,0:T(1,128)S(1)} %get-tuple-element.40), channel_id=1, source_target_pairs={{0,4},{4,8},{8,12},{12,0},{1,5},{5,9},{9,13},{13,1},{2,6},{6,10},{... | collective-permute-start | bytes 1544 | tf_op jit(solution)/shard_map/back/ppermute | solution.py:181
  24.3 4.4 %collective-permute-start.11 = (f32[1,128]{1,0:T(1,128)S(1)}, f32[1,128]{1,0:T(1,128)S(1)}, u32[]{:S(2)}, u32[]{:S(2)}) collective-permute-start(f32[1,128]{1,0:T(1,128)S(1)} %get-tuple-element.39), channel_id=1, source_target_pairs={{0,8},{4,12},{8,0},{12,4},{1,9},{5,13},{9,1},{13,5},{2,10},{6,14},... | collective-permute-start | bytes 1544 | tf_op jit(solution)/shard_map/back/ppermute | solution.py:181
  26.3 3.5 %collective-permute-start.10 = (f32[1,128]{1,0:T(1,128)S(1)}, f32[1,128]{1,0:T(1,128)S(1)}, u32[]{:S(2)}, u32[]{:S(2)}) collective-permute-start(f32[1,128]{1,0:T(1,128)S(1)} %get-tuple-element.38), channel_id=1, source_target_pairs={{0,12},{4,0},{8,4},{12,8},{1,13},{5,1},{9,5},{13,9},{2,14},{6,2},{... | collective-permute-start | bytes 1544 | tf_op jit(solution)/shard_map/back/ppermute | solution.py:181

commit v24 on v23

--- a/solution.py
+++ b/solution.py
@@ -38,13 +38,13 @@
     across = iota((readers, readers), 1)
     down = iota((readers, readers), 0)
     chosen = jnp.zeros((slots, own_rows), jnp.float32)
-    for j in range(total):
-        row = users[j][...]
+    for mask in range(total):
+        row = users[mask][...]
         column = jnp.sum(jnp.where(across == down, row, 0), axis=1, keepdims=True)
         mine = (column >= first) & (column < first + own_rows)
         rank = jnp.sum(jnp.where((down < across) & mine, 1, 0), axis=0, keepdims=True)
         held = (row >= first) & (row < first + own_rows)
-        slot = jnp.where(held, ring(me - j, total) * cap + rank, -1)
+        slot = jnp.where(held, (me ^ mask) * cap + rank, -1)
         to_slot = (iota((slots, readers), 0) == slot).astype(jnp.float32).astype(jnp.bfloat16)
         from_row = (iota((readers, own_rows), 1) + first == column).astype(jnp.float32).astype(jnp.bfloat16)
         chosen = chosen + dot(to_slot, from_row, NN)
@@ -92,13 +92,14 @@
     across = iota((readers, readers), 1)
     down = iota((readers, readers), 0)
     asks = (iota((readers, half), 1) // (half // readers) == iota((readers, half), 0)).astype(jnp.float32)
-    for j in range(total):
-        holder = users[j][...] >> (user_rows.bit_length() - 1)
+    for mask in range(total):
+        holder = users[mask][...] >> (user_rows.bit_length() - 1)
         column = jnp.sum(jnp.where(across == down, holder, 0), axis=1, keepdims=True)
         rank = jnp.sum(jnp.where((down < across) & (column == holder), 1, 0), axis=0, keepdims=True)
         arrival = jnp.where(holder > me, me - holder + total, me - holder)
-        slot = (arrival * slots + ring(me - j, total) * cap + rank).astype(jnp.float32)
-        places[j:j + 1, :] = dot(slot, asks, NN, precision=lax.Precision.HIGHEST).astype(jnp.int32)
+        slot = (arrival * slots + (me ^ mask) * cap + rank).astype(jnp.float32)
+        row = dot(slot, asks, NN, precision=lax.Precision.HIGHEST).astype(jnp.int32)
+        places[pl.ds(ring(me - (me ^ mask), total), 1), :] = row
     pairs = mats.shape[2]
     steps = pairs // 2
     eye = (iota((steps, steps), 0) == iota((steps, steps), 1)).astype(jnp.bfloat16)
@@ -181,6 +182,10 @@
     return lax.ppermute(x, axis, [(s, (s + step) % size) for s in range(size)])
 
 
+def swap(x, axis, mask):
+    return lax.ppermute(x, axis, [(s, s ^ mask) for s in range(lax.axis_size(axis))])
+
+
 def body(cand_items, reader_users, item_table, user_states, pair_mats, pair_fields):
     total = lax.axis_size("shard")
     planes = lax.axis_size("cache")
@@ -203,7 +208,7 @@
         items = [item_table] + [shift(item_table, "cache", q) for q in range(1, planes)]
 
     with jax.named_scope("ids"):
-        users = [shift(reader_users, "shard", j) for j in range(1, total)]
+        users = [swap(reader_users, "shard", mask) for mask in range(total - 1, 0, -1)]
 
     with jax.named_scope("turn"):
         *turned, states_near, own_ids, digits = pl.pallas_call(
@@ -234,7 +239,7 @@
         )
 
     with jax.named_scope("states"):
-        users_near = [own_ids] + [ids.reshape(1, readers) for ids in users]
+        users_near = [own_ids] + [ids.reshape(1, readers) for ids in users[::-1]]
         picked = pl.pallas_call(
             functools.partial(pick_kernel, total, cap),
             out_shape=jax.ShapeDtypeStruct((slots, width + half), jnp.bfloat16),

time: 30.5 us -> 31.1 us (1.020)
  waiting for transfers between devices: 3.9 us -> 5.89 us
  starting transfers between devices: 18.7 us -> 17.3 us
    ppermute x10 -> x7, starting transfers between devices: 18.1 us -> 11.8 us  [shift(): return lax.ppermute(x, axis, [(s, (s + step) % size) for s in range(size)])]
    ppermute x0 -> x3, starting transfers between devices: none -> 4.39 us  [swap(): lax.ppermute(x, axis, [(s, s ^ mask) for s in range(lax.axis_size(axis))])]
    ppermute x0 -> x3, waiting for transfers between devices: none -> 3.03 us  [swap(): lax.ppermute(x, axis, [(s, s ^ mask) for s in range(lax.axis_size(axis))])]
    ppermute x10 -> x7, waiting for transfers between devices: 3.66 us -> 2.36 us  [shift(): return lax.ppermute(x, axis, [(s, (s + step) % size) for s in range(size)])]
    ppermute x3, starting transfers between devices: 0.61 us -> 1.15 us  [body(): pair_scores[q, h] = lax.ppermute(source, ('cache', 'pair'), perm)]
where the time goes in v24:
time: 31.1 us; the launch traced here: 30.9 us
  starting transfers between devices  17.3 us (56%)
  Pallas kernels  7.13 us (23%)
  waiting for transfers between devices  5.89 us (19%)
  other arithmetic  0.51 us (2%)
    ppermute x7, starting transfers between devices, shift(): return lax.ppermute(x, axis, [(s, (s + step) % size) for s in range(size)])  11.8 us
    ppermute x3, starting transfers between devices, swap(): lax.ppermute(x, axis, [(s, s ^ mask) for s in range(lax.axis_size(axis))])  4.39 us
    pallas_call x1, Pallas kernels, body(): pl.pallas_call(functools.partial(pair_kernel, total, cap, slots, user_sta...  3.48 us
    ppermute x3, waiting for transfers between devices, swap(): lax.ppermute(x, axis, [(s, s ^ mask) for s in range(lax.axis_size(axis))])  3.03 us
    ppermute x7, waiting for transfers between devices, shift(): return lax.ppermute(x, axis, [(s, (s + step) % size) for s in range(size)])  2.36 us
    pallas_call x1, Pallas kernels, body(): pl.pallas_call(turn_kernel, out_shape=(jax.ShapeDtypeStruct((width, rows)...  2.2 us
    ppermute x3, starting transfers between devices, body(): pair_scores[q, h] = lax.ppermute(source, ('cache', 'pair'), perm)  1.15 us
    pallas_call x1, Pallas kernels, body(): pl.pallas_call(functools.partial(linear_kernel, total, planes), out_shape...  0.88 us
  transfers between devices with their start and end apart: 13, of which 5 were waited for; matrix products, arithmetic and copies ran while one was open for 0% of the time, Pallas kernels for 23%

profile of v24, /device:TPU:0, one launch (start us, length us, event | category | flops | bytes accessed | tf_op | source)
XLA Modules:
  0.0 30.9 jit_solution(4563295109708291937)
XLA Ops:
  0.0 2.9 %collective-permute-start.9 = (bf16[128,3072]{1,0:T(8,128)(2,1)}, bf16[128,3072]{1,0:T(8,128)(2,1)S(1)}, u32[]{:S(2)}, u32[]{:S(2)}) collective-permute-start(bf16[128,3072]{1,0:T(8,128)(2,1)} %refs_4_.1), channel_id=1, source_target_pairs={{0,2},{2,0},{1,3},{3,1},{4,6},{6,4},{5,7},{7,5},{8,10},{10,8},{9,1... | collective-permute-start | bytes 2359304 | tf_op jit(solution)/shard_map/item_rows/ppermute | solution.py:182
  2.9 1.6 %collective-permute-start = (s32[8]{0:T(128)}, s32[8]{0:T(128)S(1)}, u32[]{:S(2)}, u32[]{:S(2)}) collective-permute-start(s32[8]{0:T(128)} %param.7), channel_id=1, source_target_pairs={{0,4},{4,0},{8,12},{12,8},{1,5},{5,1},{9,13},{13,9},{2,6},{6,2},{1... | collective-permute-start | bytes 104 | tf_op jit(solution)/shard_map/ids/ppermute | solution.py:186
  4.5 2.6 %collective-permute-start.1 = (s32[8]{0:T(128)}, s32[8]{0:T(128)S(1)}, u32[]{:S(2)}, u32[]{:S(2)}) collective-permute-start(s32[8]{0:T(128)} %param.7), channel_id=1, source_target_pairs={{0,8},{4,12},{8,0},{12,4},{1,9},{5,13},{9,1},{13,5},{2,10},{6,14},... | collective-permute-start | bytes 104 | tf_op jit(solution)/shard_map/ids/ppermute | solution.py:186
  7.1 0.2 collective-permute-start.2
  7.3 2.2 %turn.1 = (f32[3072,128]{1,0:T(8,128)S(1)}, bf16[3072,128]{1,0:T(8,128)(2,1)S(1)}, bf16[64,64,256]{2,1,0:T(8,128)(2,1)S(1)}, bf16[128,3072]{1,0:T(8,128)(2,1)S(1...) custom-call(bf16[128,3072]{1,0:T(8,128)(2,1)} %refs_4_.1, bf16[64,64,256]{2,1,0:T(8,128)(2,1)} %bitcast.15, ...), custom_call_target="tpu_custom_call" | custom-call | flops 1610612736 | bytes 8388608 | tf_op jit(solution)/shard_map/turn/pallas_call | solution.py:214
  9.5 0.0 collective-permute-done
  9.5 0.0 collective-permute-done.1
  9.6 3.0 %collective-permute-done.2 = s32[8]{0:T(128)S(1)} collective-permute-done((s32[8]{0:T(128)}, s32[8]{0:T(128)S(1)}, u32[]{:S(2)}, u32[]{:S(2)}) %collective-permute-start.2) | collective-permute-done | bytes 64 | tf_op jit(solution)/shard_map/ids/ppermute | solution.py:186
  12.6 0.4 %states.1.refs_8_.refs_0_ = bf16[16,3200]{1,0:T(8,128)(2,1)S(1)} custom-call(s32[1,8]{1,0:T(1,128)S(1)} %get-tuple-element.23.refs_0_, s32[1,8]{1,0:T(1,128)S(1)} %bitcast.9, s32[1,8]{1,0:T(1,128)S(1)} %bitcast.11, s32[1,8]{1,0:T(1,128)S(1)} %bitcast.13, bf16[16,128]{1,0:T(8,128)(2,1)S(1)} %get-tuple-element.27.refs_4_, ...), custom_call_target="tpu_custom_call" | custom-call | flops 12582912 | bytes 1048576 | tf_op jit(solution)/shard_map/states/pallas_call | solution.py:243
  13.0 0.0 collective-permute-start.4
  13.0 1.1 %collective-permute-start.6 = (bf16[16,3200]{1,0:T(8,128)(2,1)S(1)}, bf16[16,3200]{1,0:T(8,128)(2,1)S(1)}, u32[]{:S(2)}, u32[]{:S(2)}) collective-permute-start(bf16[16,3200]{1,0:T(8,128)(2,1)S(1)} %states.1.refs_8_.refs_0_), channel_id=1, source_target_pairs={{0,8},{4,12},{8,0},{12,4},{1,9},{5,13},{9,1},{13,5},{2,10},{6,14},... | collective-permute-start | bytes 307208 | tf_op jit(solution)/shard_map/states/ppermute | solution.py:182
  14.2 2.7 %collective-permute-start.8 = (bf16[16,3200]{1,0:T(8,128)(2,1)S(1)}, bf16[16,3200]{1,0:T(8,128)(2,1)S(1)}, u32[]{:S(2)}, u32[]{:S(2)}) collective-permute-start(bf16[16,3200]{1,0:T(8,128)(2,1)S(1)} %states.1.refs_8_.refs_0_), channel_id=1, source_target_pairs={{0,12},{4,0},{8,4},{12,8},{1,13},{5,1},{9,5},{13,9},{2,14},{6,2},{... | collective-permute-start | bytes 307208 | tf_op jit(solution)/shard_map/states/ppermute | solution.py:182
  16.9 0.0 copy-start
  16.9 3.5 %pairs.1 = (f32[1,128]{1,0:T(1,128)S(1)}, s32[4,128]{1,0:T(4,128)S(1)}) custom-call(s32[1,8]{1,0:T(1,128)S(1)} %get-tuple-element.23.refs_0_, s32[1,8]{1,0:T(1,128)S(1)} %bitcast.10, s32[1,8]{1,0:T(1,128)S(1)} %bitcast.12, s32[1,8]{1,0:T(1,128)S(1)} %bitcast.14, s32[2,256]{1,0:T(2,128)} %bitcast.16, f32[3072,128]{1,0:T(8,128)S(1)} %get-tuple-element.24.refs_5_, ...), custom_call_target="tpu_custom_call" | custom-call | flops 4294967296 | bytes 4194304 | tf_op jit(solution)/shard_map/pairs/pallas_call | solution.py:254
  20.3 0.6 %collective-permute-start.3 = (f32[1,128]{1,0:T(1,128)S(1)}, f32[1,128]{1,0:T(1,128)S(1)}, u32[]{:S(2)}, u32[]{:S(2)}) collective-permute-start(f32[1,128]{1,0:T(1,128)S(1)} %get-tuple-element.31.refs_1_), channel_id=1, source_target_pairs={{0,2},{1,3},{2,0},{3,1},{4,6},{5,7},{6,4},{7,5},{8,10},{9,11},{10,... | collective-permute-start | bytes 1544 | tf_op jit(solution)/shard_map/pairs/ppermute | solution.py:279
  20.9 0.0 collective-permute-done.4.refs_1_
  21.0 0.0 collective-permute-start.5
  21.0 1.1 %collective-permute-done.6.refs_2_ = bf16[16,3200]{1,0:T(8,128)(2,1)S(1)} collective-permute-done((bf16[16,3200]{1,0:T(8,128)(2,1)S(1)}, bf16[16,3200]{1,0:T(8,128)(2,1)S(1)}, u32[]{:S(2)}, u32[]{:S(2)}) %collective-permute-start.6) | collective-permute-done | bytes 102432 | tf_op jit(solution)/shard_map/states/ppermute | solution.py:182
  22.0 0.5 %collective-permute-start.7 = (f32[1,128]{1,0:T(1,128)S(1)}, f32[1,128]{1,0:T(1,128)S(1)}, u32[]{:S(2)}, u32[]{:S(2)}) collective-permute-start(f32[1,128]{1,0:T(1,128)S(1)} %get-tuple-element.31.refs_1_), channel_id=1, source_target_pairs={{0,1},{1,0},{2,3},{3,2},{4,5},{5,4},{6,7},{7,6},{8,9},{9,8},{10,11... | collective-permute-start | bytes 1544 | tf_op jit(solution)/shard_map/pairs/ppermute | solution.py:279
  22.6 0.0 collective-permute-done.8.refs_3_
  22.6 0.0 collective-permute-done.9.refs_5_
  22.6 0.0 copy-done
  22.6 0.9 %scores.2 = (f32[4,128]{1,0:T(4,128)S(1)}, bf16[256,512]{1,0:T(8,128)(2,1)S(1)}) custom-call(bf16[16,3200]{1,0:T(8,128)(2,1)S(1)} %states.1.refs_8_.refs_0_, bf16[16,3200]{1,0:T(8,128)(2,1)S(1)} %collective-permute-done.4.refs_1_, bf16[16,3200]{1,0:T(8,128)(2,1)S(1)} %collective-permute-done.6.refs_2_, bf16[16,3200]{1,0:T(8,128)(2,1)S(1)} %collective-permute-done.8.refs_3_, ...), custom_call_target="tpu_custom_call" | custom-call | flops 100663296 | bytes 2097152 | tf_op jit(solution)/shard_map/scores/pallas_call | solution.py:283
  23.5 0.5 %collective-permute-done.3.refs_0_ = f32[1,128]{1,0:T(1,128)S(1)} collective-permute-done((f32[1,128]{1,0:T(1,128)S(1)}, f32[1,128]{1,0:T(1,128)S(1)}, u32[]{:S(2)}, u32[]{:S(2)}) %collective-permute-start.3) | collective-permute-done | bytes 544 | tf_op jit(solution)/shard_map/pairs/ppermute | solution.py:279
  24.0 0.0 collective-permute-done.5.refs_2_
  24.0 0.0 collective-permute-done.7.refs_3_
  24.0 0.2 scores.3
  24.1 0.8 %collective-permute-start.12 = (f32[1,128]{1,0:T(1,128)S(1)}, f32[1,128]{1,0:T(1,128)S(1)}, u32[]{:S(2)}, u32[]{:S(2)}) collective-permute-start(f32[1,128]{1,0:T(1,128)S(1)} %get-tuple-element.40), channel_id=1, source_target_pairs={{0,4},{4,8},{8,12},{12,0},{1,5},{5,9},{9,13},{13,1},{2,6},{6,10},{... | collective-permute-start | bytes 1544 | tf_op jit(solution)/shard_map/back/ppermute | solution.py:182
  24.9 1.4 %collective-permute-start.11 = (f32[1,128]{1,0:T(1,128)S(1)}, f32[1,128]{1,0:T(1,128)S(1)}, u32[]{:S(2)}, u32[]{:S(2)}) collective-permute-start(f32[1,128]{1,0:T(1,128)S(1)} %get-tuple-element.39), channel_id=1, source_target_pairs={{0,8},{4,12},{8,0},{12,4},{1,9},{5,13},{9,1},{13,5},{2,10},{6,14},... | collective-permute-start | bytes 1544 | tf_op jit(solution)/shard_map/back/ppermute | solution.py:182
  26.3 2.8 %collective-permute-start.10 = (f32[1,128]{1,0:T(1,128)S(1)}, f32[1,128]{1,0:T(1,128)S(1)}, u32[]{:S(2)}, u32[]{:S(2)}) collective-permute-start(f32[1,128]{1,0:T(1,128)S(1)} %get-tuple-element.38), channel_id=1, source_target_pairs={{0,12},{4,0},{8,4},{12,8},{1,13},{5,1},{9,5},{13,9},{2,14},{6,2},{... | collective-permute-start | bytes 1544 | tf_op jit(solution)/shard_map/back/ppermute | solution.py:182
  29.1 0.4 %collective-permute-done.12 = f32[1,128]{1,0:T(1,128)S(1)} collective-permute-done((f32[1,128]{1,0:T(1,128)S(1)}, f32[1,128]{1,0:T(1,128)S(1)}, u32[]{:S(2)}, u32[]{:S(2)}) %collective-permute-start.12) | collective-permute-done | bytes 544 | tf_op jit(solution)/shard_map/back/ppermute | solution.py:182
  29.5 0.0 collective-permute-done.11
  29.5 0.9 %collective-permute-done.10 = f32[1,128]{1,0:T(1,128)S(1)} collective-permute-done((f32[1,128]{1,0:T(1,128)S(1)}, f32[1,128]{1,0:T(1,128)S(1)}, u32[]{:S(2)}, u32[]{:S(2)}) %collective-permute-start.10) | collective-permute-done | bytes 544 | tf_op jit(solution)/shard_map/back/ppermute | solution.py:182
  30.4 0.5 %add_bitcast_fusion = f32[128]{0:T(128)} fusion(f32[1,128]{1,0:T(1,128)S(1)} %collective-permute-done.12, f32[1,128]{1,0:T(1,128)S(1)} %collective-permute-done.11, f32[1,128]{1,0:T(1,128)S(1)} %get-tuple-element.37, f32[1,128]{1,0:T(1,128)S(1)} %collective-permute-done.10), kind=kLoop, calls=%fused_computation | loop fusion | flops 384 | bytes 2560 | tf_op jit(solution)/shard_map/reshape | solution.py:311
Async XLA Ops:
  0.0 22.6 %collective-permute-start.9 = (bf16[128,3072]{1,0:T(8,128)(2,1)}, bf16[128,3072]{1,0:T(8,128)(2,1)S(1)}, u32[]{:S(2)}, u32[]{:S(2)}) collective-permute-start(bf16[128,3072]{1,0:T(8,128)(2,1)} %refs_4_.1), channel_id=1, source_target_pairs={{0,2},{2,0},{1,3},{3,1},{4,6},{6,4},{5,7},{7,5},{8,10},{10,8},{9,1... | collective-permute-start | bytes 2359304 | tf_op jit(solution)/shard_map/item_rows/ppermute | solution.py:182
  2.9 6.6 %collective-permute-start = (s32[8]{0:T(128)}, s32[8]{0:T(128)S(1)}, u32[]{:S(2)}, u32[]{:S(2)}) collective-permute-start(s32[8]{0:T(128)} %param.7), channel_id=1, source_target_pairs={{0,4},{4,0},{8,12},{12,8},{1,5},{5,1},{9,13},{13,9},{2,6},{6,2},{1... | collective-permute-start | bytes 104 | tf_op jit(solution)/shard_map/ids/ppermute | solution.py:186
  4.5 5.0 %collective-permute-start.1 = (s32[8]{0:T(128)}, s32[8]{0:T(128)S(1)}, u32[]{:S(2)}, u32[]{:S(2)}) collective-permute-start(s32[8]{0:T(128)} %param.7), channel_id=1, source_target_pairs={{0,8},{4,12},{8,0},{12,4},{1,9},{5,13},{9,1},{13,5},{2,10},{6,14},... | collective-permute-start | bytes 104 | tf_op jit(solution)/shard_map/ids/ppermute | solution.py:186
  7.1 5.5 %collective-permute-start.2 = (s32[8]{0:T(128)}, s32[8]{0:T(128)S(1)}, u32[]{:S(2)}, u32[]{:S(2)}) collective-permute-start(s32[8]{0:T(128)} %param.7), channel_id=1, source_target_pairs={{0,12},{4,8},{8,4},{12,0},{1,13},{5,9},{9,5},{13,1},{2,14},{6,10},... | collective-permute-start | bytes 104 | tf_op jit(solution)/shard_map/ids/ppermute | solution.py:186
  13.0 8.0 %collective-permute-start.4 = (bf16[16,3200]{1,0:T(8,128)(2,1)S(1)}, bf16[16,3200]{1,0:T(8,128)(2,1)S(1)}, u32[]{:S(2)}, u32[]{:S(2)}) collective-permute-start(bf16[16,3200]{1,0:T(8,128)(2,1)S(1)} %states.1.refs_8_.refs_0_), channel_id=1, source_target_pairs={{0,4},{4,8},{8,12},{12,0},{1,5},{5,9},{9,13},{13,1},{2,6},{6,10},{... | collective-permute-start | bytes 307208 | tf_op jit(solution)/shard_map/states/ppermute | solution.py:182
  13.0 9.0 %collective-permute-start.6 = (bf16[16,3200]{1,0:T(8,128)(2,1)S(1)}, bf16[16,3200]{1,0:T(8,128)(2,1)S(1)}, u32[]{:S(2)}, u32[]{:S(2)}) collective-permute-start(bf16[16,3200]{1,0:T(8,128)(2,1)S(1)} %states.1.refs_8_.refs_0_), channel_id=1, source_target_pairs={{0,8},{4,12},{8,0},{12,4},{1,9},{5,13},{9,1},{13,5},{2,10},{6,14},... | collective-permute-start | bytes 307208 | tf_op jit(solution)/shard_map/states/ppermute | solution.py:182
  14.2 8.4 %collective-permute-start.8 = (bf16[16,3200]{1,0:T(8,128)(2,1)S(1)}, bf16[16,3200]{1,0:T(8,128)(2,1)S(1)}, u32[]{:S(2)}, u32[]{:S(2)}) collective-permute-start(bf16[16,3200]{1,0:T(8,128)(2,1)S(1)} %states.1.refs_8_.refs_0_), channel_id=1, source_target_pairs={{0,12},{4,0},{8,4},{12,8},{1,13},{5,1},{9,5},{13,9},{2,14},{6,2},{... | collective-permute-start | bytes 307208 | tf_op jit(solution)/shard_map/states/ppermute | solution.py:182
  16.9 5.7 %copy-start = (bf16[128,3072]{1,0:T(8,128)(2,1)S(1)}, bf16[128,3072]{1,0:T(8,128)(2,1)}, u32[]{:S(2)}) copy-start(bf16[128,3072]{1,0:T(8,128)(2,1)} %refs_4_.1) | copy-start | bytes 2359300
  20.3 3.6 %collective-permute-start.3 = (f32[1,128]{1,0:T(1,128)S(1)}, f32[1,128]{1,0:T(1,128)S(1)}, u32[]{:S(2)}, u32[]{:S(2)}) collective-permute-start(f32[1,128]{1,0:T(1,128)S(1)} %get-tuple-element.31.refs_1_), channel_id=1, source_target_pairs={{0,2},{1,3},{2,0},{3,1},{4,6},{5,7},{6,4},{7,5},{8,10},{9,11},{10,... | collective-permute-start | bytes 1544 | tf_op jit(solution)/shard_map/pairs/ppermute | solution.py:279
  21.0 3.0 %collective-permute-start.5 = (f32[1,128]{1,0:T(1,128)S(1)}, f32[1,128]{1,0:T(1,128)S(1)}, u32[]{:S(2)}, u32[]{:S(2)}) collective-permute-start(f32[1,128]{1,0:T(1,128)S(1)} %get-tuple-element.31.refs_1_), channel_id=1, source_target_pairs={{0,3},{1,2},{2,1},{3,0},{4,7},{5,6},{6,5},{7,4},{8,11},{9,10},{10,... | collective-permute-start | bytes 1544 | tf_op jit(solution)/shard_map/pairs/ppermute | solution.py:279
  22.0 1.9 %collective-permute-start.7 = (f32[1,128]{1,0:T(1,128)S(1)}, f32[1,128]{1,0:T(1,128)S(1)}, u32[]{:S(2)}, u32[]{:S(2)}) collective-permute-start(f32[1,128]{1,0:T(1,128)S(1)} %get-tuple-element.31.refs_1_), channel_id=1, source_target_pairs={{0,1},{1,0},{2,3},{3,2},{4,5},{5,4},{6,7},{7,6},{8,9},{9,8},{10,11... | collective-permute-start | bytes 1544 | tf_op jit(solution)/shard_map/pairs/ppermute | solution.py:279
  24.1 5.4 %collective-permute-start.12 = (f32[1,128]{1,0:T(1,128)S(1)}, f32[1,128]{1,0:T(1,128)S(1)}, u32[]{:S(2)}, u32[]{:S(2)}) collective-permute-start(f32[1,128]{1,0:T(1,128)S(1)} %get-tuple-element.40), channel_id=1, source_target_pairs={{0,4},{4,8},{8,12},{12,0},{1,5},{5,9},{9,13},{13,1},{2,6},{6,10},{... | collective-permute-start | bytes 1544 | tf_op jit(solution)/shard_map/back/ppermute | solution.py:182
  24.9 4.6 %collective-permute-start.11 = (f32[1,128]{1,0:T(1,128)S(1)}, f32[1,128]{1,0:T(1,128)S(1)}, u32[]{:S(2)}, u32[]{:S(2)}) collective-permute-start(f32[1,128]{1,0:T(1,128)S(1)} %get-tuple-element.39), channel_id=1, source_target_pairs={{0,8},{4,12},{8,0},{12,4},{1,9},{5,13},{9,1},{13,5},{2,10},{6,14},... | collective-permute-start | bytes 1544 | tf_op jit(solution)/shard_map/back/ppermute | solution.py:182
  26.3 4.1 %collective-permute-start.10 = (f32[1,128]{1,0:T(1,128)S(1)}, f32[1,128]{1,0:T(1,128)S(1)}, u32[]{:S(2)}, u32[]{:S(2)}) collective-permute-start(f32[1,128]{1,0:T(1,128)S(1)} %get-tuple-element.38), channel_id=1, source_target_pairs={{0,12},{4,0},{8,4},{12,8},{1,13},{5,1},{9,5},{13,9},{2,14},{6,2},{... | collective-permute-start | bytes 1544 | tf_op jit(solution)/shard_map/back/ppermute | solution.py:182

commit v25 on v24

--- a/solution.py
+++ b/solution.py
@@ -39,7 +39,7 @@
     down = iota((readers, readers), 0)
     chosen = jnp.zeros((slots, own_rows), jnp.float32)
     for mask in range(total):
-        row = users[mask][...]
+        row = users[-mask % total][...]
         column = jnp.sum(jnp.where(across == down, row, 0), axis=1, keepdims=True)
         mine = (column >= first) & (column < first + own_rows)
         rank = jnp.sum(jnp.where((down < across) & mine, 1, 0), axis=0, keepdims=True)
@@ -93,7 +93,7 @@
     down = iota((readers, readers), 0)
     asks = (iota((readers, half), 1) // (half // readers) == iota((readers, half), 0)).astype(jnp.float32)
     for mask in range(total):
-        holder = users[mask][...] >> (user_rows.bit_length() - 1)
+        holder = users[-mask % total][...] >> (user_rows.bit_length() - 1)
         column = jnp.sum(jnp.where(across == down, holder, 0), axis=1, keepdims=True)
         rank = jnp.sum(jnp.where((down < across) & (column == holder), 1, 0), axis=0, keepdims=True)
         arrival = jnp.where(holder > me, me - holder + total, me - holder)
@@ -239,7 +239,7 @@
         )
 
     with jax.named_scope("states"):
-        users_near = [own_ids] + [ids.reshape(1, readers) for ids in users[::-1]]
+        users_near = [own_ids] + [ids.reshape(1, readers) for ids in users]
         picked = pl.pallas_call(
             functools.partial(pick_kernel, total, cap),
             out_shape=jax.ShapeDtypeStruct((slots, width + half), jnp.bfloat16),

time: 31.1 us -> 30.5 us (0.981)
  waiting for transfers between devices: 5.89 us -> 3.62 us
  starting transfers between devices: 17.3 us -> 19 us
    ppermute x3, waiting for transfers between devices: 3.03 us -> 1.58 us  [swap(): lax.ppermute(x, axis, [(s, s ^ mask) for s in range(lax.axis_size(axis))])]
    ppermute x7, starting transfers between devices: 11.8 us -> 12.7 us  [shift(): return lax.ppermute(x, axis, [(s, (s + step) % size) for s in range(size)])]
    ppermute x3, starting transfers between devices: 1.15 us -> 2 us  [body(): pair_scores[q, h] = lax.ppermute(source, ('cache', 'pair'), perm)]
    ppermute x7, waiting for transfers between devices: 2.36 us -> 1.55 us  [shift(): return lax.ppermute(x, axis, [(s, (s + step) % size) for s in range(size)])]
where the time goes in v25:
time: 30.5 us; the launch traced here: 30.4 us
  starting transfers between devices  19 us (62%)
  Pallas kernels  7.13 us (23%)
  waiting for transfers between devices  3.62 us (12%)
  other arithmetic  0.52 us (2%)
    ppermute x7, starting transfers between devices, shift(): return lax.ppermute(x, axis, [(s, (s + step) % size) for s in range(size)])  12.7 us
    ppermute x3, starting transfers between devices, swap(): lax.ppermute(x, axis, [(s, s ^ mask) for s in range(lax.axis_size(axis))])  4.39 us
    pallas_call x1, Pallas kernels, body(): pl.pallas_call(functools.partial(pair_kernel, total, cap, slots, user_sta...  3.48 us
    pallas_call x1, Pallas kernels, body(): pl.pallas_call(turn_kernel, out_shape=(jax.ShapeDtypeStruct((width, rows)...  2.2 us
    ppermute x3, starting transfers between devices, body(): pair_scores[q, h] = lax.ppermute(source, ('cache', 'pair'), perm)  2 us
    ppermute x3, waiting for transfers between devices, swap(): lax.ppermute(x, axis, [(s, s ^ mask) for s in range(lax.axis_size(axis))])  1.58 us
    ppermute x7, waiting for transfers between devices, shift(): return lax.ppermute(x, axis, [(s, (s + step) % size) for s in range(size)])  1.55 us
    pallas_call x1, Pallas kernels, body(): pl.pallas_call(functools.partial(linear_kernel, total, planes), out_shape...  0.89 us
  transfers between devices with their start and end apart: 13, of which 5 were waited for; matrix products, arithmetic and copies ran while one was open for 0% of the time, Pallas kernels for 23%

profile of v25, /device:TPU:0, one launch (start us, length us, event | category | flops | bytes accessed | tf_op | source)
XLA Modules:
  0.0 30.4 jit_solution(7281412785364986121)
XLA Ops:
  0.0 2.9 %collective-permute-start.9 = (bf16[128,3072]{1,0:T(8,128)(2,1)}, bf16[128,3072]{1,0:T(8,128)(2,1)S(1)}, u32[]{:S(2)}, u32[]{:S(2)}) collective-permute-start(bf16[128,3072]{1,0:T(8,128)(2,1)} %refs_4_.1), channel_id=1, source_target_pairs={{0,2},{2,0},{1,3},{3,1},{4,6},{6,4},{5,7},{7,5},{8,10},{10,8},{9,1... | collective-permute-start | bytes 2359304 | tf_op jit(solution)/shard_map/item_rows/ppermute | solution.py:182
  2.9 3.6 %collective-permute-start = (s32[8]{0:T(128)}, s32[8]{0:T(128)S(1)}, u32[]{:S(2)}, u32[]{:S(2)}) collective-permute-start(s32[8]{0:T(128)} %param.7), channel_id=1, source_target_pairs={{0,12},{4,8},{8,4},{12,0},{1,13},{5,9},{9,5},{13,1},{2,14},{6,10},... | collective-permute-start | bytes 104 | tf_op jit(solution)/shard_map/ids/ppermute | solution.py:186
  6.5 0.0 collective-permute-start.1
  6.5 0.8 %collective-permute-start.2 = (s32[8]{0:T(128)}, s32[8]{0:T(128)S(1)}, u32[]{:S(2)}, u32[]{:S(2)}) collective-permute-start(s32[8]{0:T(128)} %param.7), channel_id=1, source_target_pairs={{0,4},{4,0},{8,12},{12,8},{1,5},{5,1},{9,13},{13,9},{2,6},{6,2},{1... | collective-permute-start | bytes 104 | tf_op jit(solution)/shard_map/ids/ppermute | solution.py:186
  7.3 2.2 %turn.1 = (f32[3072,128]{1,0:T(8,128)S(1)}, bf16[3072,128]{1,0:T(8,128)(2,1)S(1)}, bf16[64,64,256]{2,1,0:T(8,128)(2,1)S(1)}, bf16[128,3072]{1,0:T(8,128)(2,1)S(1...) custom-call(bf16[128,3072]{1,0:T(8,128)(2,1)} %refs_4_.1, bf16[64,64,256]{2,1,0:T(8,128)(2,1)} %bitcast.15, ...), custom_call_target="tpu_custom_call" | custom-call | flops 1610612736 | bytes 8388608 | tf_op jit(solution)/shard_map/turn/pallas_call | solution.py:214
  9.5 0.0 collective-permute-done
  9.5 1.6 %collective-permute-done.1 = s32[8]{0:T(128)S(1)} collective-permute-done((s32[8]{0:T(128)}, s32[8]{0:T(128)S(1)}, u32[]{:S(2)}, u32[]{:S(2)}) %collective-permute-start.1) | collective-permute-done | bytes 64 | tf_op jit(solution)/shard_map/ids/ppermute | solution.py:186
  11.1 0.0 collective-permute-done.2
  11.1 0.4 %states.1.refs_8_.refs_0_ = bf16[16,3200]{1,0:T(8,128)(2,1)S(1)} custom-call(s32[1,8]{1,0:T(1,128)S(1)} %get-tuple-element.23.refs_0_, s32[1,8]{1,0:T(1,128)S(1)} %bitcast.9, s32[1,8]{1,0:T(1,128)S(1)} %bitcast.11, s32[1,8]{1,0:T(1,128)S(1)} %bitcast.13, bf16[16,128]{1,0:T(8,128)(2,1)S(1)} %get-tuple-element.27.refs_4_, ...), custom_call_target="tpu_custom_call" | custom-call | flops 12582912 | bytes 1048576 | tf_op jit(solution)/shard_map/states/pallas_call | solution.py:243
  11.5 0.0 collective-permute-start.4
  11.6 2.6 %collective-permute-start.6 = (bf16[16,3200]{1,0:T(8,128)(2,1)S(1)}, bf16[16,3200]{1,0:T(8,128)(2,1)S(1)}, u32[]{:S(2)}, u32[]{:S(2)}) collective-permute-start(bf16[16,3200]{1,0:T(8,128)(2,1)S(1)} %states.1.refs_8_.refs_0_), channel_id=1, source_target_pairs={{0,8},{4,12},{8,0},{12,4},{1,9},{5,13},{9,1},{13,5},{2,10},{6,14},... | collective-permute-start | bytes 307208 | tf_op jit(solution)/shard_map/states/ppermute | solution.py:182
  14.2 2.3 %collective-permute-start.8 = (bf16[16,3200]{1,0:T(8,128)(2,1)S(1)}, bf16[16,3200]{1,0:T(8,128)(2,1)S(1)}, u32[]{:S(2)}, u32[]{:S(2)}) collective-permute-start(bf16[16,3200]{1,0:T(8,128)(2,1)S(1)} %states.1.refs_8_.refs_0_), channel_id=1, source_target_pairs={{0,12},{4,0},{8,4},{12,8},{1,13},{5,1},{9,5},{13,9},{2,14},{6,2},{... | collective-permute-start | bytes 307208 | tf_op jit(solution)/shard_map/states/ppermute | solution.py:182
  16.5 0.0 copy-start
  16.5 3.5 %pairs.1 = (f32[1,128]{1,0:T(1,128)S(1)}, s32[4,128]{1,0:T(4,128)S(1)}) custom-call(s32[1,8]{1,0:T(1,128)S(1)} %get-tuple-element.23.refs_0_, s32[1,8]{1,0:T(1,128)S(1)} %bitcast.10, s32[1,8]{1,0:T(1,128)S(1)} %bitcast.12, s32[1,8]{1,0:T(1,128)S(1)} %bitcast.14, s32[2,256]{1,0:T(2,128)} %bitcast.16, f32[3072,128]{1,0:T(8,128)S(1)} %get-tuple-element.24.refs_5_, ...), custom_call_target="tpu_custom_call" | custom-call | flops 4294967296 | bytes 4194304 | tf_op jit(solution)/shard_map/pairs/pallas_call | solution.py:254
  20.0 0.6 %collective-permute-start.3 = (f32[1,128]{1,0:T(1,128)S(1)}, f32[1,128]{1,0:T(1,128)S(1)}, u32[]{:S(2)}, u32[]{:S(2)}) collective-permute-start(f32[1,128]{1,0:T(1,128)S(1)} %get-tuple-element.31.refs_1_), channel_id=1, source_target_pairs={{0,2},{1,3},{2,0},{3,1},{4,6},{5,7},{6,4},{7,5},{8,10},{9,11},{10,... | collective-permute-start | bytes 1544 | tf_op jit(solution)/shard_map/pairs/ppermute | solution.py:279
  20.6 0.0 collective-permute-done.4.refs_1_
  20.6 0.0 collective-permute-start.5
  20.6 0.2 collective-permute-done.6.refs_2_
  20.8 1.4 %collective-permute-start.7 = (f32[1,128]{1,0:T(1,128)S(1)}, f32[1,128]{1,0:T(1,128)S(1)}, u32[]{:S(2)}, u32[]{:S(2)}) collective-permute-start(f32[1,128]{1,0:T(1,128)S(1)} %get-tuple-element.31.refs_1_), channel_id=1, source_target_pairs={{0,1},{1,0},{2,3},{3,2},{4,5},{5,4},{6,7},{7,6},{8,9},{9,8},{10,11... | collective-permute-start | bytes 1544 | tf_op jit(solution)/shard_map/pairs/ppermute | solution.py:279
  22.2 0.0 collective-permute-done.8.refs_3_
  22.2 0.0 collective-permute-done.9.refs_5_
  22.2 0.0 copy-done
  22.2 0.9 %scores.2 = (f32[4,128]{1,0:T(4,128)S(1)}, bf16[256,512]{1,0:T(8,128)(2,1)S(1)}) custom-call(bf16[16,3200]{1,0:T(8,128)(2,1)S(1)} %states.1.refs_8_.refs_0_, bf16[16,3200]{1,0:T(8,128)(2,1)S(1)} %collective-permute-done.4.refs_1_, bf16[16,3200]{1,0:T(8,128)(2,1)S(1)} %collective-permute-done.6.refs_2_, bf16[16,3200]{1,0:T(8,128)(2,1)S(1)} %collective-permute-done.8.refs_3_, ...), custom_call_target="tpu_custom_call" | custom-call | flops 100663296 | bytes 2097152 | tf_op jit(solution)/shard_map/scores/pallas_call | solution.py:283
  23.1 0.5 %collective-permute-done.3.refs_0_ = f32[1,128]{1,0:T(1,128)S(1)} collective-permute-done((f32[1,128]{1,0:T(1,128)S(1)}, f32[1,128]{1,0:T(1,128)S(1)}, u32[]{:S(2)}, u32[]{:S(2)}) %collective-permute-start.3) | collective-permute-done | bytes 544 | tf_op jit(solution)/shard_map/pairs/ppermute | solution.py:279
  23.6 0.0 collective-permute-done.5.refs_2_
  23.6 0.0 collective-permute-done.7.refs_3_
  23.6 0.2 scores.3
  23.8 0.2 collective-permute-start.12
  23.9 2.4 %collective-permute-start.11 = (f32[1,128]{1,0:T(1,128)S(1)}, f32[1,128]{1,0:T(1,128)S(1)}, u32[]{:S(2)}, u32[]{:S(2)}) collective-permute-start(f32[1,128]{1,0:T(1,128)S(1)} %get-tuple-element.39), channel_id=1, source_target_pairs={{0,8},{4,12},{8,0},{12,4},{1,9},{5,13},{9,1},{13,5},{2,10},{6,14},... | collective-permute-start | bytes 1544 | tf_op jit(solution)/shard_map/back/ppermute | solution.py:182
  26.3 2.2 %collective-permute-start.10 = (f32[1,128]{1,0:T(1,128)S(1)}, f32[1,128]{1,0:T(1,128)S(1)}, u32[]{:S(2)}, u32[]{:S(2)}) collective-permute-start(f32[1,128]{1,0:T(1,128)S(1)} %get-tuple-element.38), channel_id=1, source_target_pairs={{0,12},{4,0},{8,4},{12,8},{1,13},{5,1},{9,5},{13,9},{2,14},{6,2},{... | collective-permute-start | bytes 1544 | tf_op jit(solution)/shard_map/back/ppermute | solution.py:182
  28.5 0.7 %collective-permute-done.12 = f32[1,128]{1,0:T(1,128)S(1)} collective-permute-done((f32[1,128]{1,0:T(1,128)S(1)}, f32[1,128]{1,0:T(1,128)S(1)}, u32[]{:S(2)}, u32[]{:S(2)}) %collective-permute-start.12) | collective-permute-done | bytes 544 | tf_op jit(solution)/shard_map/back/ppermute | solution.py:182
  29.2 0.0 collective-permute-done.11
  29.2 0.7 %collective-permute-done.10 = f32[1,128]{1,0:T(1,128)S(1)} collective-permute-done((f32[1,128]{1,0:T(1,128)S(1)}, f32[1,128]{1,0:T(1,128)S(1)}, u32[]{:S(2)}, u32[]{:S(2)}) %collective-permute-start.10) | collective-permute-done | bytes 544 | tf_op jit(solution)/shard_map/back/ppermute | solution.py:182
  29.9 0.5 %add_bitcast_fusion = f32[128]{0:T(128)} fusion(f32[1,128]{1,0:T(1,128)S(1)} %collective-permute-done.12, f32[1,128]{1,0:T(1,128)S(1)} %collective-permute-done.11, f32[1,128]{1,0:T(1,128)S(1)} %get-tuple-element.37, f32[1,128]{1,0:T(1,128)S(1)} %collective-permute-done.10), kind=kLoop, calls=%fused_computation | loop fusion | flops 384 | bytes 2560 | tf_op jit(solution)/shard_map/reshape | solution.py:311
Async XLA Ops:
  0.0 22.2 %collective-permute-start.9 = (bf16[128,3072]{1,0:T(8,128)(2,1)}, bf16[128,3072]{1,0:T(8,128)(2,1)S(1)}, u32[]{:S(2)}, u32[]{:S(2)}) collective-permute-start(bf16[128,3072]{1,0:T(8,128)(2,1)} %refs_4_.1), channel_id=1, source_target_pairs={{0,2},{2,0},{1,3},{3,1},{4,6},{6,4},{5,7},{7,5},{8,10},{10,8},{9,1... | collective-permute-start | bytes 2359304 | tf_op jit(solution)/shard_map/item_rows/ppermute | solution.py:182
  2.9 6.6 %collective-permute-start = (s32[8]{0:T(128)}, s32[8]{0:T(128)S(1)}, u32[]{:S(2)}, u32[]{:S(2)}) collective-permute-start(s32[8]{0:T(128)} %param.7), channel_id=1, source_target_pairs={{0,12},{4,8},{8,4},{12,0},{1,13},{5,9},{9,5},{13,1},{2,14},{6,10},... | collective-permute-start | bytes 104 | tf_op jit(solution)/shard_map/ids/ppermute | solution.py:186
  6.5 4.6 %collective-permute-start.1 = (s32[8]{0:T(128)}, s32[8]{0:T(128)S(1)}, u32[]{:S(2)}, u32[]{:S(2)}) collective-permute-start(s32[8]{0:T(128)} %param.7), channel_id=1, source_target_pairs={{0,8},{4,12},{8,0},{12,4},{1,9},{5,13},{9,1},{13,5},{2,10},{6,14},... | collective-permute-start | bytes 104 | tf_op jit(solution)/shard_map/ids/ppermute | solution.py:186
  6.5 4.6 %collective-permute-start.2 = (s32[8]{0:T(128)}, s32[8]{0:T(128)S(1)}, u32[]{:S(2)}, u32[]{:S(2)}) collective-permute-start(s32[8]{0:T(128)} %param.7), channel_id=1, source_target_pairs={{0,4},{4,0},{8,12},{12,8},{1,5},{5,1},{9,13},{13,9},{2,6},{6,2},{1... | collective-permute-start | bytes 104 | tf_op jit(solution)/shard_map/ids/ppermute | solution.py:186
  11.5 9.1 %collective-permute-start.4 = (bf16[16,3200]{1,0:T(8,128)(2,1)S(1)}, bf16[16,3200]{1,0:T(8,128)(2,1)S(1)}, u32[]{:S(2)}, u32[]{:S(2)}) collective-permute-start(bf16[16,3200]{1,0:T(8,128)(2,1)S(1)} %states.1.refs_8_.refs_0_), channel_id=1, source_target_pairs={{0,4},{4,8},{8,12},{12,0},{1,5},{5,9},{9,13},{13,1},{2,6},{6,10},{... | collective-permute-start | bytes 307208 | tf_op jit(solution)/shard_map/states/ppermute | solution.py:182
  11.6 9.3 %collective-permute-start.6 = (bf16[16,3200]{1,0:T(8,128)(2,1)S(1)}, bf16[16,3200]{1,0:T(8,128)(2,1)S(1)}, u32[]{:S(2)}, u32[]{:S(2)}) collective-permute-start(bf16[16,3200]{1,0:T(8,128)(2,1)S(1)} %states.1.refs_8_.refs_0_), channel_id=1, source_target_pairs={{0,8},{4,12},{8,0},{12,4},{1,9},{5,13},{9,1},{13,5},{2,10},{6,14},... | collective-permute-start | bytes 307208 | tf_op jit(solution)/shard_map/states/ppermute | solution.py:182
  14.2 8.0 %collective-permute-start.8 = (bf16[16,3200]{1,0:T(8,128)(2,1)S(1)}, bf16[16,3200]{1,0:T(8,128)(2,1)S(1)}, u32[]{:S(2)}, u32[]{:S(2)}) collective-permute-start(bf16[16,3200]{1,0:T(8,128)(2,1)S(1)} %states.1.refs_8_.refs_0_), channel_id=1, source_target_pairs={{0,12},{4,0},{8,4},{12,8},{1,13},{5,1},{9,5},{13,9},{2,14},{6,2},{... | collective-permute-start | bytes 307208 | tf_op jit(solution)/shard_map/states/ppermute | solution.py:182
  16.5 5.7 %copy-start = (bf16[128,3072]{1,0:T(8,128)(2,1)S(1)}, bf16[128,3072]{1,0:T(8,128)(2,1)}, u32[]{:S(2)}) copy-start(bf16[128,3072]{1,0:T(8,128)(2,1)} %refs_4_.1) | copy-start | bytes 2359300
  20.0 3.6 %collective-permute-start.3 = (f32[1,128]{1,0:T(1,128)S(1)}, f32[1,128]{1,0:T(1,128)S(1)}, u32[]{:S(2)}, u32[]{:S(2)}) collective-permute-start(f32[1,128]{1,0:T(1,128)S(1)} %get-tuple-element.31.refs_1_), channel_id=1, source_target_pairs={{0,2},{1,3},{2,0},{3,1},{4,6},{5,7},{6,4},{7,5},{8,10},{9,11},{10,... | collective-permute-start | bytes 1544 | tf_op jit(solution)/shard_map/pairs/ppermute | solution.py:279
  20.6 3.0 %collective-permute-start.5 = (f32[1,128]{1,0:T(1,128)S(1)}, f32[1,128]{1,0:T(1,128)S(1)}, u32[]{:S(2)}, u32[]{:S(2)}) collective-permute-start(f32[1,128]{1,0:T(1,128)S(1)} %get-tuple-element.31.refs_1_), channel_id=1, source_target_pairs={{0,3},{1,2},{2,1},{3,0},{4,7},{5,6},{6,5},{7,4},{8,11},{9,10},{10,... | collective-permute-start | bytes 1544 | tf_op jit(solution)/shard_map/pairs/ppermute | solution.py:279
  20.8 2.8 %collective-permute-start.7 = (f32[1,128]{1,0:T(1,128)S(1)}, f32[1,128]{1,0:T(1,128)S(1)}, u32[]{:S(2)}, u32[]{:S(2)}) collective-permute-start(f32[1,128]{1,0:T(1,128)S(1)} %get-tuple-element.31.refs_1_), channel_id=1, source_target_pairs={{0,1},{1,0},{2,3},{3,2},{4,5},{5,4},{6,7},{7,6},{8,9},{9,8},{10,11... | collective-permute-start | bytes 1544 | tf_op jit(solution)/shard_map/pairs/ppermute | solution.py:279
  23.8 5.4 %collective-permute-start.12 = (f32[1,128]{1,0:T(1,128)S(1)}, f32[1,128]{1,0:T(1,128)S(1)}, u32[]{:S(2)}, u32[]{:S(2)}) collective-permute-start(f32[1,128]{1,0:T(1,128)S(1)} %get-tuple-element.40), channel_id=1, source_target_pairs={{0,4},{4,8},{8,12},{12,0},{1,5},{5,9},{9,13},{13,1},{2,6},{6,10},{... | collective-permute-start | bytes 1544 | tf_op jit(solution)/shard_map/back/ppermute | solution.py:182
  23.9 5.2 %collective-permute-start.11 = (f32[1,128]{1,0:T(1,128)S(1)}, f32[1,128]{1,0:T(1,128)S(1)}, u32[]{:S(2)}, u32[]{:S(2)}) collective-permute-start(f32[1,128]{1,0:T(1,128)S(1)} %get-tuple-element.39), channel_id=1, source_target_pairs={{0,8},{4,12},{8,0},{12,4},{1,9},{5,13},{9,1},{13,5},{2,10},{6,14},... | collective-permute-start | bytes 1544 | tf_op jit(solution)/shard_map/back/ppermute | solution.py:182
  26.3 3.5 %collective-permute-start.10 = (f32[1,128]{1,0:T(1,128)S(1)}, f32[1,128]{1,0:T(1,128)S(1)}, u32[]{:S(2)}, u32[]{:S(2)}) collective-permute-start(f32[1,128]{1,0:T(1,128)S(1)} %get-tuple-element.38), channel_id=1, source_target_pairs={{0,12},{4,0},{8,4},{12,8},{1,13},{5,1},{9,5},{13,9},{2,14},{6,2},{... | collective-permute-start | bytes 1544 | tf_op jit(solution)/shard_map/back/ppermute | solution.py:182

commit v26 on v23

--- a/solution.py
+++ b/solution.py
@@ -301,7 +301,7 @@
 
     with jax.named_scope("back"):
         result = outs[0]
-        for j in range(1, total):
+        for j in sorted(range(1, total), key=lambda step: step == total // 2):
             result = result + shift(outs[j], "shard", -j)
     return result.reshape(half)
 

time: 30.5 us -> 31.2 us (1.023)
  starting transfers between devices: 18.7 us -> 19.6 us
    ppermute x10, starting transfers between devices: 18.1 us -> 19 us  [shift(): return lax.ppermute(x, axis, [(s, (s + step) % size) for s in range(size)])]
  transfers between devices with their start and end apart: 13 -> 13, of which waited for: 5 -> 4; matrix products, arithmetic and copies ran while one was open for 0% -> 0% of each run, Pallas kernels for 23% -> 23%
where the time goes in v26:
time: 31.2 us; the launch traced here: 31 us
  starting transfers between devices  19.6 us (63%)
  Pallas kernels  7.14 us (23%)
  waiting for transfers between devices  3.71 us (12%)
  other arithmetic  0.52 us (2%)
    ppermute x10, starting transfers between devices, shift(): return lax.ppermute(x, axis, [(s, (s + step) % size) for s in range(size)])  19 us
    pallas_call x1, Pallas kernels, body(): pl.pallas_call(functools.partial(pair_kernel, total, cap, slots, user_sta...  3.48 us
    ppermute x10, waiting for transfers between devices, shift(): return lax.ppermute(x, axis, [(s, (s + step) % size) for s in range(size)])  3.47 us
    pallas_call x1, Pallas kernels, body(): pl.pallas_call(turn_kernel, out_shape=(jax.ShapeDtypeStruct((width, rows)...  2.2 us
    pallas_call x1, Pallas kernels, body(): pl.pallas_call(functools.partial(linear_kernel, total, planes), out_shape...  0.9 us
  transfers between devices with their start and end apart: 13, of which 4 were waited for; matrix products, arithmetic and copies ran while one was open for 0% of the time, Pallas kernels for 23%

profile of v26, /device:TPU:0, one launch (start us, length us, event | category | flops | bytes accessed | tf_op | source)
XLA Modules:
  0.0 31.0 jit_solution(13445486714230478395)
XLA Ops:
  0.0 2.9 %collective-permute-start.9 = (bf16[128,3072]{1,0:T(8,128)(2,1)}, bf16[128,3072]{1,0:T(8,128)(2,1)S(1)}, u32[]{:S(2)}, u32[]{:S(2)}) collective-permute-start(bf16[128,3072]{1,0:T(8,128)(2,1)} %refs_4_.1), channel_id=1, source_target_pairs={{0,2},{2,0},{1,3},{3,1},{4,6},{6,4},{5,7},{7,5},{8,10},{10,8},{9,1... | collective-permute-start | bytes 2359304 | tf_op jit(solution)/shard_map/item_rows/ppermute | solution.py:181
  2.9 1.6 %collective-permute-start = (s32[8]{0:T(128)}, s32[8]{0:T(128)S(1)}, u32[]{:S(2)}, u32[]{:S(2)}) collective-permute-start(s32[8]{0:T(128)} %param.7), channel_id=1, source_target_pairs={{0,4},{4,8},{8,12},{12,0},{1,5},{5,9},{9,13},{13,1},{2,6},{6,10},{... | collective-permute-start | bytes 104 | tf_op jit(solution)/shard_map/ids/ppermute | solution.py:181
  4.5 2.6 %collective-permute-start.1 = (s32[8]{0:T(128)}, s32[8]{0:T(128)S(1)}, u32[]{:S(2)}, u32[]{:S(2)}) collective-permute-start(s32[8]{0:T(128)} %param.7), channel_id=1, source_target_pairs={{0,8},{4,12},{8,0},{12,4},{1,9},{5,13},{9,1},{13,5},{2,10},{6,14},... | collective-permute-start | bytes 104 | tf_op jit(solution)/shard_map/ids/ppermute | solution.py:181
  7.1 1.3 %collective-permute-start.2 = (s32[8]{0:T(128)}, s32[8]{0:T(128)S(1)}, u32[]{:S(2)}, u32[]{:S(2)}) collective-permute-start(s32[8]{0:T(128)} %param.7), channel_id=1, source_target_pairs={{0,12},{4,0},{8,4},{12,8},{1,13},{5,1},{9,5},{13,9},{2,14},{6,2},{... | collective-permute-start | bytes 104 | tf_op jit(solution)/shard_map/ids/ppermute | solution.py:181
  8.5 2.2 %turn.1 = (f32[3072,128]{1,0:T(8,128)S(1)}, bf16[3072,128]{1,0:T(8,128)(2,1)S(1)}, bf16[64,64,256]{2,1,0:T(8,128)(2,1)S(1)}, bf16[128,3072]{1,0:T(8,128)(2,1)S(1...) custom-call(bf16[128,3072]{1,0:T(8,128)(2,1)} %refs_4_.1, bf16[64,64,256]{2,1,0:T(8,128)(2,1)} %bitcast.15, ...), custom_call_target="tpu_custom_call" | custom-call | flops 1610612736 | bytes 8388608 | tf_op jit(solution)/shard_map/turn/pallas_call | solution.py:209
  10.7 0.0 collective-permute-done
  10.7 0.0 collective-permute-done.1
  10.7 0.1 collective-permute-done.2
  10.8 0.4 %states.1.refs_8_.refs_0_ = bf16[16,3200]{1,0:T(8,128)(2,1)S(1)} custom-call(s32[1,8]{1,0:T(1,128)S(1)} %get-tuple-element.23.refs_0_, s32[1,8]{1,0:T(1,128)S(1)} %bitcast.9, s32[1,8]{1,0:T(1,128)S(1)} %bitcast.11, s32[1,8]{1,0:T(1,128)S(1)} %bitcast.13, bf16[16,128]{1,0:T(8,128)(2,1)S(1)} %get-tuple-element.27.refs_4_, ...), custom_call_target="tpu_custom_call" | custom-call | flops 12582912 | bytes 1048576 | tf_op jit(solution)/shard_map/states/pallas_call | solution.py:238
  11.2 0.6 %collective-permute-start.4 = (bf16[16,3200]{1,0:T(8,128)(2,1)S(1)}, bf16[16,3200]{1,0:T(8,128)(2,1)S(1)}, u32[]{:S(2)}, u32[]{:S(2)}) collective-permute-start(bf16[16,3200]{1,0:T(8,128)(2,1)S(1)} %states.1.refs_8_.refs_0_), channel_id=1, source_target_pairs={{0,4},{4,8},{8,12},{12,0},{1,5},{5,9},{9,13},{13,1},{2,6},{6,10},{... | collective-permute-start | bytes 307208 | tf_op jit(solution)/shard_map/states/ppermute | solution.py:181
  11.8 3.1 %collective-permute-start.6 = (bf16[16,3200]{1,0:T(8,128)(2,1)S(1)}, bf16[16,3200]{1,0:T(8,128)(2,1)S(1)}, u32[]{:S(2)}, u32[]{:S(2)}) collective-permute-start(bf16[16,3200]{1,0:T(8,128)(2,1)S(1)} %states.1.refs_8_.refs_0_), channel_id=1, source_target_pairs={{0,8},{4,12},{8,0},{12,4},{1,9},{5,13},{9,1},{13,5},{2,10},{6,14},... | collective-permute-start | bytes 307208 | tf_op jit(solution)/shard_map/states/ppermute | solution.py:181
  14.9 0.1 collective-permute-start.8
  15.1 0.0 copy-start
  15.1 3.5 %pairs.1 = (f32[1,128]{1,0:T(1,128)S(1)}, s32[4,128]{1,0:T(4,128)S(1)}) custom-call(s32[1,8]{1,0:T(1,128)S(1)} %get-tuple-element.23.refs_0_, s32[1,8]{1,0:T(1,128)S(1)} %bitcast.10, s32[1,8]{1,0:T(1,128)S(1)} %bitcast.12, s32[1,8]{1,0:T(1,128)S(1)} %bitcast.14, s32[2,256]{1,0:T(2,128)} %bitcast.16, f32[3072,128]{1,0:T(8,128)S(1)} %get-tuple-element.24.refs_5_, ...), custom_call_target="tpu_custom_call" | custom-call | flops 4294967296 | bytes 4194304 | tf_op jit(solution)/shard_map/pairs/pallas_call | solution.py:249
  18.5 0.6 %collective-permute-start.3 = (f32[1,128]{1,0:T(1,128)S(1)}, f32[1,128]{1,0:T(1,128)S(1)}, u32[]{:S(2)}, u32[]{:S(2)}) collective-permute-start(f32[1,128]{1,0:T(1,128)S(1)} %get-tuple-element.31.refs_1_), channel_id=1, source_target_pairs={{0,2},{1,3},{2,0},{3,1},{4,6},{5,7},{6,4},{7,5},{8,10},{9,11},{10,... | collective-permute-start | bytes 1544 | tf_op jit(solution)/shard_map/pairs/ppermute | solution.py:274
  19.1 0.0 collective-permute-done.4.refs_1_
  19.1 0.0 collective-permute-start.5
  19.2 1.8 %collective-permute-done.6.refs_2_ = bf16[16,3200]{1,0:T(8,128)(2,1)S(1)} collective-permute-done((bf16[16,3200]{1,0:T(8,128)(2,1)S(1)}, bf16[16,3200]{1,0:T(8,128)(2,1)S(1)}, u32[]{:S(2)}, u32[]{:S(2)}) %collective-permute-start.6) | collective-permute-done | bytes 102432 | tf_op jit(solution)/shard_map/states/ppermute | solution.py:181
  21.0 0.0 collective-permute-start.7
  21.0 0.0 collective-permute-done.8.refs_3_
  21.0 0.0 collective-permute-done.9.refs_5_
  21.0 0.0 copy-done
  21.0 0.9 %scores.2 = (f32[4,128]{1,0:T(4,128)S(1)}, bf16[256,512]{1,0:T(8,128)(2,1)S(1)}) custom-call(bf16[16,3200]{1,0:T(8,128)(2,1)S(1)} %states.1.refs_8_.refs_0_, bf16[16,3200]{1,0:T(8,128)(2,1)S(1)} %collective-permute-done.4.refs_1_, bf16[16,3200]{1,0:T(8,128)(2,1)S(1)} %collective-permute-done.6.refs_2_, bf16[16,3200]{1,0:T(8,128)(2,1)S(1)} %collective-permute-done.8.refs_3_, ...), custom_call_target="tpu_custom_call" | custom-call | flops 100663296 | bytes 2097152 | tf_op jit(solution)/shard_map/scores/pallas_call | solution.py:278
  21.9 0.2 collective-permute-done.3.refs_0_
  22.2 0.0 collective-permute-done.5.refs_2_
  22.2 0.0 collective-permute-done.7.refs_3_
  22.2 0.2 scores.3
  22.3 2.8 %collective-permute-start.12 = (f32[1,128]{1,0:T(1,128)S(1)}, f32[1,128]{1,0:T(1,128)S(1)}, u32[]{:S(2)}, u32[]{:S(2)}) collective-permute-start(f32[1,128]{1,0:T(1,128)S(1)} %get-tuple-element.40), channel_id=1, source_target_pairs={{0,8},{4,12},{8,0},{12,4},{1,9},{5,13},{9,1},{13,5},{2,10},{6,14},... | collective-permute-start | bytes 1544 | tf_op jit(solution)/shard_map/back/ppermute | solution.py:181
  25.2 1.1 %collective-permute-start.11 = (f32[1,128]{1,0:T(1,128)S(1)}, f32[1,128]{1,0:T(1,128)S(1)}, u32[]{:S(2)}, u32[]{:S(2)}) collective-permute-start(f32[1,128]{1,0:T(1,128)S(1)} %get-tuple-element.39), channel_id=1, source_target_pairs={{0,4},{4,8},{8,12},{12,0},{1,5},{5,9},{9,13},{13,1},{2,6},{6,10},{... | collective-permute-start | bytes 1544 | tf_op jit(solution)/shard_map/back/ppermute | solution.py:181
  26.3 2.7 %collective-permute-start.10 = (f32[1,128]{1,0:T(1,128)S(1)}, f32[1,128]{1,0:T(1,128)S(1)}, u32[]{:S(2)}, u32[]{:S(2)}) collective-permute-start(f32[1,128]{1,0:T(1,128)S(1)} %get-tuple-element.38), channel_id=1, source_target_pairs={{0,12},{4,0},{8,4},{12,8},{1,13},{5,1},{9,5},{13,9},{2,14},{6,2},{... | collective-permute-start | bytes 1544 | tf_op jit(solution)/shard_map/back/ppermute | solution.py:181
  29.0 0.0 collective-permute-done.12
  29.0 1.5 %collective-permute-done.11 = f32[1,128]{1,0:T(1,128)S(1)} collective-permute-done((f32[1,128]{1,0:T(1,128)S(1)}, f32[1,128]{1,0:T(1,128)S(1)}, u32[]{:S(2)}, u32[]{:S(2)}) %collective-permute-start.11) | collective-permute-done | bytes 544 | tf_op jit(solution)/shard_map/back/ppermute | solution.py:181
  30.5 0.0 collective-permute-done.10
  30.5 0.5 %add_bitcast_fusion = f32[128]{0:T(128)} fusion(f32[1,128]{1,0:T(1,128)S(1)} %collective-permute-done.12, f32[1,128]{1,0:T(1,128)S(1)} %collective-permute-done.11, f32[1,128]{1,0:T(1,128)S(1)} %get-tuple-element.37, f32[1,128]{1,0:T(1,128)S(1)} %collective-permute-done.10), kind=kLoop, calls=%fused_computation | loop fusion | flops 384 | bytes 2560 | tf_op jit(solution)/shard_map/reshape | solution.py:306
Async XLA Ops:
  0.0 21.0 %collective-permute-start.9 = (bf16[128,3072]{1,0:T(8,128)(2,1)}, bf16[128,3072]{1,0:T(8,128)(2,1)S(1)}, u32[]{:S(2)}, u32[]{:S(2)}) collective-permute-start(bf16[128,3072]{1,0:T(8,128)(2,1)} %refs_4_.1), channel_id=1, source_target_pairs={{0,2},{2,0},{1,3},{3,1},{4,6},{6,4},{5,7},{7,5},{8,10},{10,8},{9,1... | collective-permute-start | bytes 2359304 | tf_op jit(solution)/shard_map/item_rows/ppermute | solution.py:181
  2.9 7.7 %collective-permute-start = (s32[8]{0:T(128)}, s32[8]{0:T(128)S(1)}, u32[]{:S(2)}, u32[]{:S(2)}) collective-permute-start(s32[8]{0:T(128)} %param.7), channel_id=1, source_target_pairs={{0,4},{4,8},{8,12},{12,0},{1,5},{5,9},{9,13},{13,1},{2,6},{6,10},{... | collective-permute-start | bytes 104 | tf_op jit(solution)/shard_map/ids/ppermute | solution.py:181
  4.5 6.2 %collective-permute-start.1 = (s32[8]{0:T(128)}, s32[8]{0:T(128)S(1)}, u32[]{:S(2)}, u32[]{:S(2)}) collective-permute-start(s32[8]{0:T(128)} %param.7), channel_id=1, source_target_pairs={{0,8},{4,12},{8,0},{12,4},{1,9},{5,13},{9,1},{13,5},{2,10},{6,14},... | collective-permute-start | bytes 104 | tf_op jit(solution)/shard_map/ids/ppermute | solution.py:181
  7.1 3.7 %collective-permute-start.2 = (s32[8]{0:T(128)}, s32[8]{0:T(128)S(1)}, u32[]{:S(2)}, u32[]{:S(2)}) collective-permute-start(s32[8]{0:T(128)} %param.7), channel_id=1, source_target_pairs={{0,12},{4,0},{8,4},{12,8},{1,13},{5,1},{9,5},{13,9},{2,14},{6,2},{... | collective-permute-start | bytes 104 | tf_op jit(solution)/shard_map/ids/ppermute | solution.py:181
  11.2 8.0 %collective-permute-start.4 = (bf16[16,3200]{1,0:T(8,128)(2,1)S(1)}, bf16[16,3200]{1,0:T(8,128)(2,1)S(1)}, u32[]{:S(2)}, u32[]{:S(2)}) collective-permute-start(bf16[16,3200]{1,0:T(8,128)(2,1)S(1)} %states.1.refs_8_.refs_0_), channel_id=1, source_target_pairs={{0,4},{4,8},{8,12},{12,0},{1,5},{5,9},{9,13},{13,1},{2,6},{6,10},{... | collective-permute-start | bytes 307208 | tf_op jit(solution)/shard_map/states/ppermute | solution.py:181
  11.8 9.2 %collective-permute-start.6 = (bf16[16,3200]{1,0:T(8,128)(2,1)S(1)}, bf16[16,3200]{1,0:T(8,128)(2,1)S(1)}, u32[]{:S(2)}, u32[]{:S(2)}) collective-permute-start(bf16[16,3200]{1,0:T(8,128)(2,1)S(1)} %states.1.refs_8_.refs_0_), channel_id=1, source_target_pairs={{0,8},{4,12},{8,0},{12,4},{1,9},{5,13},{9,1},{13,5},{2,10},{6,14},... | collective-permute-start | bytes 307208 | tf_op jit(solution)/shard_map/states/ppermute | solution.py:181
  14.9 6.1 %collective-permute-start.8 = (bf16[16,3200]{1,0:T(8,128)(2,1)S(1)}, bf16[16,3200]{1,0:T(8,128)(2,1)S(1)}, u32[]{:S(2)}, u32[]{:S(2)}) collective-permute-start(bf16[16,3200]{1,0:T(8,128)(2,1)S(1)} %states.1.refs_8_.refs_0_), channel_id=1, source_target_pairs={{0,12},{4,0},{8,4},{12,8},{1,13},{5,1},{9,5},{13,9},{2,14},{6,2},{... | collective-permute-start | bytes 307208 | tf_op jit(solution)/shard_map/states/ppermute | solution.py:181
  15.1 6.0 %copy-start = (bf16[128,3072]{1,0:T(8,128)(2,1)S(1)}, bf16[128,3072]{1,0:T(8,128)(2,1)}, u32[]{:S(2)}) copy-start(bf16[128,3072]{1,0:T(8,128)(2,1)} %refs_4_.1) | copy-start | bytes 2359300
  18.5 3.6 %collective-permute-start.3 = (f32[1,128]{1,0:T(1,128)S(1)}, f32[1,128]{1,0:T(1,128)S(1)}, u32[]{:S(2)}, u32[]{:S(2)}) collective-permute-start(f32[1,128]{1,0:T(1,128)S(1)} %get-tuple-element.31.refs_1_), channel_id=1, source_target_pairs={{0,2},{1,3},{2,0},{3,1},{4,6},{5,7},{6,4},{7,5},{8,10},{9,11},{10,... | collective-permute-start | bytes 1544 | tf_op jit(solution)/shard_map/pairs/ppermute | solution.py:274
  19.1 3.0 %collective-permute-start.5 = (f32[1,128]{1,0:T(1,128)S(1)}, f32[1,128]{1,0:T(1,128)S(1)}, u32[]{:S(2)}, u32[]{:S(2)}) collective-permute-start(f32[1,128]{1,0:T(1,128)S(1)} %get-tuple-element.31.refs_1_), channel_id=1, source_target_pairs={{0,3},{1,2},{2,1},{3,0},{4,7},{5,6},{6,5},{7,4},{8,11},{9,10},{10,... | collective-permute-start | bytes 1544 | tf_op jit(solution)/shard_map/pairs/ppermute | solution.py:274
  21.0 1.2 %collective-permute-start.7 = (f32[1,128]{1,0:T(1,128)S(1)}, f32[1,128]{1,0:T(1,128)S(1)}, u32[]{:S(2)}, u32[]{:S(2)}) collective-permute-start(f32[1,128]{1,0:T(1,128)S(1)} %get-tuple-element.31.refs_1_), channel_id=1, source_target_pairs={{0,1},{1,0},{2,3},{3,2},{4,5},{5,4},{6,7},{7,6},{8,9},{9,8},{10,11... | collective-permute-start | bytes 1544 | tf_op jit(solution)/shard_map/pairs/ppermute | solution.py:274
  22.3 6.7 %collective-permute-start.12 = (f32[1,128]{1,0:T(1,128)S(1)}, f32[1,128]{1,0:T(1,128)S(1)}, u32[]{:S(2)}, u32[]{:S(2)}) collective-permute-start(f32[1,128]{1,0:T(1,128)S(1)} %get-tuple-element.40), channel_id=1, source_target_pairs={{0,8},{4,12},{8,0},{12,4},{1,9},{5,13},{9,1},{13,5},{2,10},{6,14},... | collective-permute-start | bytes 1544 | tf_op jit(solution)/shard_map/back/ppermute | solution.py:181
  25.2 5.3 %collective-permute-start.11 = (f32[1,128]{1,0:T(1,128)S(1)}, f32[1,128]{1,0:T(1,128)S(1)}, u32[]{:S(2)}, u32[]{:S(2)}) collective-permute-start(f32[1,128]{1,0:T(1,128)S(1)} %get-tuple-element.39), channel_id=1, source_target_pairs={{0,4},{4,8},{8,12},{12,0},{1,5},{5,9},{9,13},{13,1},{2,6},{6,10},{... | collective-permute-start | bytes 1544 | tf_op jit(solution)/shard_map/back/ppermute | solution.py:181
  26.3 4.2 %collective-permute-start.10 = (f32[1,128]{1,0:T(1,128)S(1)}, f32[1,128]{1,0:T(1,128)S(1)}, u32[]{:S(2)}, u32[]{:S(2)}) collective-permute-start(f32[1,128]{1,0:T(1,128)S(1)} %get-tuple-element.38), channel_id=1, source_target_pairs={{0,12},{4,0},{8,4},{12,8},{1,13},{5,1},{9,5},{13,9},{2,14},{6,2},{... | collective-permute-start | bytes 1544 | tf_op jit(solution)/shard_map/back/ppermute | solution.py:181

commit v27 on v23

--- a/solution.py
+++ b/solution.py
@@ -268,7 +268,7 @@
             perm = [
                 (c * parts + d, (c + q) % planes * parts + (d + h) % parts) for c in range(planes) for d in range(parts)
             ]
-            source, after = pair_parts, {1: 1, 2: 2}.get(len(pair_scores) - 1, 0)
+            source, after = pair_parts, {1: 2, 2: 1}.get(len(pair_scores) - 1, 0)
             if after:
                 source, states[after] = lax.optimization_barrier((pair_parts, states[after]))
             pair_scores[q, h] = lax.ppermute(source, ("cache", "pair"), perm)

time: 30.5 us -> 30.5 us (level)
  starting transfers between devices: 18.7 us -> 19.7 us
  waiting for transfers between devices: 3.9 us -> 2.96 us
    ppermute x3, starting transfers between devices: 0.61 us -> 2.12 us  [body(): pair_scores[q, h] = lax.ppermute(source, ('cache', 'pair'), perm)]
    ppermute x10, waiting for transfers between devices: 3.66 us -> 2.41 us  [shift(): return lax.ppermute(x, axis, [(s, (s + step) % size) for s in range(size)])]
    ppermute x10, starting transfers between devices: 18.1 us -> 17.5 us  [shift(): return lax.ppermute(x, axis, [(s, (s + step) % size) for s in range(size)])]
    ppermute x3, waiting for transfers between devices: 0.24 us -> 0.55 us  [body(): pair_scores[q, h] = lax.ppermute(source, ('cache', 'pair'), perm)]
  transfers between devices with their start and end apart: 13 -> 13, of which waited for: 5 -> 7; matrix products, arithmetic and copies ran while one was open for 0% -> 0% of each run, Pallas kernels for 23% -> 23%
where the time goes in v27:
time: 30.5 us; the launch traced here: 30.3 us
  starting transfers between devices  19.7 us (65%)
  Pallas kernels  7.12 us (23%)
  waiting for transfers between devices  2.96 us (10%)
  other arithmetic  0.52 us (2%)
    ppermute x10, starting transfers between devices, shift(): return lax.ppermute(x, axis, [(s, (s + step) % size) for s in range(size)])  17.5 us
    pallas_call x1, Pallas kernels, body(): pl.pallas_call(functools.partial(pair_kernel, total, cap, slots, user_sta...  3.48 us
    ppermute x10, waiting for transfers between devices, shift(): return lax.ppermute(x, axis, [(s, (s + step) % size) for s in range(size)])  2.41 us
    pallas_call x1, Pallas kernels, body(): pl.pallas_call(turn_kernel, out_shape=(jax.ShapeDtypeStruct((width, rows)...  2.2 us
    ppermute x3, starting transfers between devices, body(): pair_scores[q, h] = lax.ppermute(source, ('cache', 'pair'), perm)  2.12 us
    pallas_call x1, Pallas kernels, body(): pl.pallas_call(functools.partial(linear_kernel, total, planes), out_shape...  0.88 us
  transfers between devices with their start and end apart: 13, of which 7 were waited for; matrix products, arithmetic and copies ran while one was open for 0% of the time, Pallas kernels for 23%

profile of v27, /device:TPU:0, one launch (start us, length us, event | category | flops | bytes accessed | tf_op | source)
XLA Modules:
  0.0 30.3 jit_solution(5734963000910711446)
XLA Ops:
  0.0 2.9 %collective-permute-start.9 = (bf16[128,3072]{1,0:T(8,128)(2,1)}, bf16[128,3072]{1,0:T(8,128)(2,1)S(1)}, u32[]{:S(2)}, u32[]{:S(2)}) collective-permute-start(bf16[128,3072]{1,0:T(8,128)(2,1)} %refs_4_.1), channel_id=1, source_target_pairs={{0,2},{2,0},{1,3},{3,1},{4,6},{6,4},{5,7},{7,5},{8,10},{10,8},{9,1... | collective-permute-start | bytes 2359304 | tf_op jit(solution)/shard_map/item_rows/ppermute | solution.py:181
  2.9 1.6 %collective-permute-start = (s32[8]{0:T(128)}, s32[8]{0:T(128)S(1)}, u32[]{:S(2)}, u32[]{:S(2)}) collective-permute-start(s32[8]{0:T(128)} %param.7), channel_id=1, source_target_pairs={{0,4},{4,8},{8,12},{12,0},{1,5},{5,9},{9,13},{13,1},{2,6},{6,10},{... | collective-permute-start | bytes 104 | tf_op jit(solution)/shard_map/ids/ppermute | solution.py:181
  4.5 2.6 %collective-permute-start.1 = (s32[8]{0:T(128)}, s32[8]{0:T(128)S(1)}, u32[]{:S(2)}, u32[]{:S(2)}) collective-permute-start(s32[8]{0:T(128)} %param.7), channel_id=1, source_target_pairs={{0,8},{4,12},{8,0},{12,4},{1,9},{5,13},{9,1},{13,5},{2,10},{6,14},... | collective-permute-start | bytes 104 | tf_op jit(solution)/shard_map/ids/ppermute | solution.py:181
  7.1 1.3 %collective-permute-start.2 = (s32[8]{0:T(128)}, s32[8]{0:T(128)S(1)}, u32[]{:S(2)}, u32[]{:S(2)}) collective-permute-start(s32[8]{0:T(128)} %param.7), channel_id=1, source_target_pairs={{0,12},{4,0},{8,4},{12,8},{1,13},{5,1},{9,5},{13,9},{2,14},{6,2},{... | collective-permute-start | bytes 104 | tf_op jit(solution)/shard_map/ids/ppermute | solution.py:181
  8.5 2.2 %turn.1 = (f32[3072,128]{1,0:T(8,128)S(1)}, bf16[3072,128]{1,0:T(8,128)(2,1)S(1)}, bf16[64,64,256]{2,1,0:T(8,128)(2,1)S(1)}, bf16[128,3072]{1,0:T(8,128)(2,1)S(1...) custom-call(bf16[128,3072]{1,0:T(8,128)(2,1)} %refs_4_.1, bf16[64,64,256]{2,1,0:T(8,128)(2,1)} %bitcast.15, ...), custom_call_target="tpu_custom_call" | custom-call | flops 1610612736 | bytes 8388608 | tf_op jit(solution)/shard_map/turn/pallas_call | solution.py:209
  10.7 0.0 collective-permute-done
  10.7 0.0 collective-permute-done.1
  10.7 0.1 collective-permute-done.2
  10.8 0.4 %states.1.refs_8_.refs_0_ = bf16[16,3200]{1,0:T(8,128)(2,1)S(1)} custom-call(s32[1,8]{1,0:T(1,128)S(1)} %get-tuple-element.23.refs_0_, s32[1,8]{1,0:T(1,128)S(1)} %bitcast.9, s32[1,8]{1,0:T(1,128)S(1)} %bitcast.11, s32[1,8]{1,0:T(1,128)S(1)} %bitcast.13, bf16[16,128]{1,0:T(8,128)(2,1)S(1)} %get-tuple-element.27.refs_4_, ...), custom_call_target="tpu_custom_call" | custom-call | flops 12582912 | bytes 1048576 | tf_op jit(solution)/shard_map/states/pallas_call | solution.py:238
  11.2 1.0 %collective-permute-start.4 = (bf16[16,3200]{1,0:T(8,128)(2,1)S(1)}, bf16[16,3200]{1,0:T(8,128)(2,1)S(1)}, u32[]{:S(2)}, u32[]{:S(2)}) collective-permute-start(bf16[16,3200]{1,0:T(8,128)(2,1)S(1)} %states.1.refs_8_.refs_0_), channel_id=1, source_target_pairs={{0,8},{4,12},{8,0},{12,4},{1,9},{5,13},{9,1},{13,5},{2,10},{6,14},... | collective-permute-start | bytes 307208 | tf_op jit(solution)/shard_map/states/ppermute | solution.py:181
  12.1 2.8 %collective-permute-start.6 = (bf16[16,3200]{1,0:T(8,128)(2,1)S(1)}, bf16[16,3200]{1,0:T(8,128)(2,1)S(1)}, u32[]{:S(2)}, u32[]{:S(2)}) collective-permute-start(bf16[16,3200]{1,0:T(8,128)(2,1)S(1)} %states.1.refs_8_.refs_0_), channel_id=1, source_target_pairs={{0,4},{4,8},{8,12},{12,0},{1,5},{5,9},{9,13},{13,1},{2,6},{6,10},{... | collective-permute-start | bytes 307208 | tf_op jit(solution)/shard_map/states/ppermute | solution.py:181
  14.9 1.0 %collective-permute-start.8 = (bf16[16,3200]{1,0:T(8,128)(2,1)S(1)}, bf16[16,3200]{1,0:T(8,128)(2,1)S(1)}, u32[]{:S(2)}, u32[]{:S(2)}) collective-permute-start(bf16[16,3200]{1,0:T(8,128)(2,1)S(1)} %states.1.refs_8_.refs_0_), channel_id=1, source_target_pairs={{0,12},{4,0},{8,4},{12,8},{1,13},{5,1},{9,5},{13,9},{2,14},{6,2},{... | collective-permute-start | bytes 307208 | tf_op jit(solution)/shard_map/states/ppermute | solution.py:181
  16.0 0.0 copy-start
  16.0 3.5 %pairs.1 = (f32[1,128]{1,0:T(1,128)S(1)}, s32[4,128]{1,0:T(4,128)S(1)}) custom-call(s32[1,8]{1,0:T(1,128)S(1)} %get-tuple-element.23.refs_0_, s32[1,8]{1,0:T(1,128)S(1)} %bitcast.10, s32[1,8]{1,0:T(1,128)S(1)} %bitcast.12, s32[1,8]{1,0:T(1,128)S(1)} %bitcast.14, s32[2,256]{1,0:T(2,128)} %bitcast.16, f32[3072,128]{1,0:T(8,128)S(1)} %get-tuple-element.24.refs_5_, ...), custom_call_target="tpu_custom_call" | custom-call | flops 4294967296 | bytes 4194304 | tf_op jit(solution)/shard_map/pairs/pallas_call | solution.py:249
  19.5 0.6 %collective-permute-start.3 = (f32[1,128]{1,0:T(1,128)S(1)}, f32[1,128]{1,0:T(1,128)S(1)}, u32[]{:S(2)}, u32[]{:S(2)}) collective-permute-start(f32[1,128]{1,0:T(1,128)S(1)} %get-tuple-element.31.refs_1_), channel_id=1, source_target_pairs={{0,2},{1,3},{2,0},{3,1},{4,6},{5,7},{6,4},{7,5},{8,10},{9,11},{10,... | collective-permute-start | bytes 1544 | tf_op jit(solution)/shard_map/pairs/ppermute | solution.py:274
  20.1 0.1 collective-permute-done.4.refs_2_
  20.1 0.0 collective-permute-start.5
  20.2 0.0 collective-permute-done.6.refs_1_
  20.2 1.5 %collective-permute-start.7 = (f32[1,128]{1,0:T(1,128)S(1)}, f32[1,128]{1,0:T(1,128)S(1)}, u32[]{:S(2)}, u32[]{:S(2)}) collective-permute-start(f32[1,128]{1,0:T(1,128)S(1)} %get-tuple-element.31.refs_1_), channel_id=1, source_target_pairs={{0,1},{1,0},{2,3},{3,2},{4,5},{5,4},{6,7},{7,6},{8,9},{9,8},{10,11... | collective-permute-start | bytes 1544 | tf_op jit(solution)/shard_map/pairs/ppermute | solution.py:274
  21.7 0.0 collective-permute-done.8.refs_3_
  21.7 0.0 collective-permute-done.9.refs_5_
  21.7 0.0 copy-done
  21.7 0.9 %scores.2 = (f32[4,128]{1,0:T(4,128)S(1)}, bf16[256,512]{1,0:T(8,128)(2,1)S(1)}) custom-call(bf16[16,3200]{1,0:T(8,128)(2,1)S(1)} %states.1.refs_8_.refs_0_, bf16[16,3200]{1,0:T(8,128)(2,1)S(1)} %collective-permute-done.6.refs_1_, bf16[16,3200]{1,0:T(8,128)(2,1)S(1)} %collective-permute-done.4.refs_2_, bf16[16,3200]{1,0:T(8,128)(2,1)S(1)} %collective-permute-done.8.refs_3_, ...), custom_call_target="tpu_custom_call" | custom-call | flops 100663296 | bytes 2097152 | tf_op jit(solution)/shard_map/scores/pallas_call | solution.py:278
  22.6 0.5 %collective-permute-done.3.refs_0_ = f32[1,128]{1,0:T(1,128)S(1)} collective-permute-done((f32[1,128]{1,0:T(1,128)S(1)}, f32[1,128]{1,0:T(1,128)S(1)}, u32[]{:S(2)}, u32[]{:S(2)}) %collective-permute-start.3) | collective-permute-done | bytes 544 | tf_op jit(solution)/shard_map/pairs/ppermute | solution.py:274
  23.1 0.1 collective-permute-done.5.refs_2_
  23.1 0.0 collective-permute-done.7.refs_3_
  23.1 0.2 scores.3
  23.3 1.0 %collective-permute-start.12 = (f32[1,128]{1,0:T(1,128)S(1)}, f32[1,128]{1,0:T(1,128)S(1)}, u32[]{:S(2)}, u32[]{:S(2)}) collective-permute-start(f32[1,128]{1,0:T(1,128)S(1)} %get-tuple-element.40), channel_id=1, source_target_pairs={{0,4},{4,8},{8,12},{12,0},{1,5},{5,9},{9,13},{13,1},{2,6},{6,10},{... | collective-permute-start | bytes 1544 | tf_op jit(solution)/shard_map/back/ppermute | solution.py:181
  24.3 2.0 %collective-permute-start.11 = (f32[1,128]{1,0:T(1,128)S(1)}, f32[1,128]{1,0:T(1,128)S(1)}, u32[]{:S(2)}, u32[]{:S(2)}) collective-permute-start(f32[1,128]{1,0:T(1,128)S(1)} %get-tuple-element.39), channel_id=1, source_target_pairs={{0,8},{4,12},{8,0},{12,4},{1,9},{5,13},{9,1},{13,5},{2,10},{6,14},... | collective-permute-start | bytes 1544 | tf_op jit(solution)/shard_map/back/ppermute | solution.py:181
  26.3 1.3 %collective-permute-start.10 = (f32[1,128]{1,0:T(1,128)S(1)}, f32[1,128]{1,0:T(1,128)S(1)}, u32[]{:S(2)}, u32[]{:S(2)}) collective-permute-start(f32[1,128]{1,0:T(1,128)S(1)} %get-tuple-element.38), channel_id=1, source_target_pairs={{0,12},{4,0},{8,4},{12,8},{1,13},{5,1},{9,5},{13,9},{2,14},{6,2},{... | collective-permute-start | bytes 1544 | tf_op jit(solution)/shard_map/back/ppermute | solution.py:181
  27.6 1.1 %collective-permute-done.12 = f32[1,128]{1,0:T(1,128)S(1)} collective-permute-done((f32[1,128]{1,0:T(1,128)S(1)}, f32[1,128]{1,0:T(1,128)S(1)}, u32[]{:S(2)}, u32[]{:S(2)}) %collective-permute-start.12) | collective-permute-done | bytes 544 | tf_op jit(solution)/shard_map/back/ppermute | solution.py:181
  28.7 0.1 collective-permute-done.11
  28.7 1.1 %collective-permute-done.10 = f32[1,128]{1,0:T(1,128)S(1)} collective-permute-done((f32[1,128]{1,0:T(1,128)S(1)}, f32[1,128]{1,0:T(1,128)S(1)}, u32[]{:S(2)}, u32[]{:S(2)}) %collective-permute-start.10) | collective-permute-done | bytes 544 | tf_op jit(solution)/shard_map/back/ppermute | solution.py:181
  29.8 0.5 %add_bitcast_fusion = f32[128]{0:T(128)} fusion(f32[1,128]{1,0:T(1,128)S(1)} %collective-permute-done.12, f32[1,128]{1,0:T(1,128)S(1)} %collective-permute-done.11, f32[1,128]{1,0:T(1,128)S(1)} %get-tuple-element.37, f32[1,128]{1,0:T(1,128)S(1)} %collective-permute-done.10), kind=kLoop, calls=%fused_computation | loop fusion | flops 384 | bytes 2560 | tf_op jit(solution)/shard_map/reshape | solution.py:306
Async XLA Ops:
  0.0 21.7 %collective-permute-start.9 = (bf16[128,3072]{1,0:T(8,128)(2,1)}, bf16[128,3072]{1,0:T(8,128)(2,1)S(1)}, u32[]{:S(2)}, u32[]{:S(2)}) collective-permute-start(bf16[128,3072]{1,0:T(8,128)(2,1)} %refs_4_.1), channel_id=1, source_target_pairs={{0,2},{2,0},{1,3},{3,1},{4,6},{6,4},{5,7},{7,5},{8,10},{10,8},{9,1... | collective-permute-start | bytes 2359304 | tf_op jit(solution)/shard_map/item_rows/ppermute | solution.py:181
  2.9 7.7 %collective-permute-start = (s32[8]{0:T(128)}, s32[8]{0:T(128)S(1)}, u32[]{:S(2)}, u32[]{:S(2)}) collective-permute-start(s32[8]{0:T(128)} %param.7), channel_id=1, source_target_pairs={{0,4},{4,8},{8,12},{12,0},{1,5},{5,9},{9,13},{13,1},{2,6},{6,10},{... | collective-permute-start | bytes 104 | tf_op jit(solution)/shard_map/ids/ppermute | solution.py:181
  4.5 6.2 %collective-permute-start.1 = (s32[8]{0:T(128)}, s32[8]{0:T(128)S(1)}, u32[]{:S(2)}, u32[]{:S(2)}) collective-permute-start(s32[8]{0:T(128)} %param.7), channel_id=1, source_target_pairs={{0,8},{4,12},{8,0},{12,4},{1,9},{5,13},{9,1},{13,5},{2,10},{6,14},... | collective-permute-start | bytes 104 | tf_op jit(solution)/shard_map/ids/ppermute | solution.py:181
  7.1 3.7 %collective-permute-start.2 = (s32[8]{0:T(128)}, s32[8]{0:T(128)S(1)}, u32[]{:S(2)}, u32[]{:S(2)}) collective-permute-start(s32[8]{0:T(128)} %param.7), channel_id=1, source_target_pairs={{0,12},{4,0},{8,4},{12,8},{1,13},{5,1},{9,5},{13,9},{2,14},{6,2},{... | collective-permute-start | bytes 104 | tf_op jit(solution)/shard_map/ids/ppermute | solution.py:181
  11.2 9.0 %collective-permute-start.4 = (bf16[16,3200]{1,0:T(8,128)(2,1)S(1)}, bf16[16,3200]{1,0:T(8,128)(2,1)S(1)}, u32[]{:S(2)}, u32[]{:S(2)}) collective-permute-start(bf16[16,3200]{1,0:T(8,128)(2,1)S(1)} %states.1.refs_8_.refs_0_), channel_id=1, source_target_pairs={{0,8},{4,12},{8,0},{12,4},{1,9},{5,13},{9,1},{13,5},{2,10},{6,14},... | collective-permute-start | bytes 307208 | tf_op jit(solution)/shard_map/states/ppermute | solution.py:181
  12.1 8.0 %collective-permute-start.6 = (bf16[16,3200]{1,0:T(8,128)(2,1)S(1)}, bf16[16,3200]{1,0:T(8,128)(2,1)S(1)}, u32[]{:S(2)}, u32[]{:S(2)}) collective-permute-start(bf16[16,3200]{1,0:T(8,128)(2,1)S(1)} %states.1.refs_8_.refs_0_), channel_id=1, source_target_pairs={{0,4},{4,8},{8,12},{12,0},{1,5},{5,9},{9,13},{13,1},{2,6},{6,10},{... | collective-permute-start | bytes 307208 | tf_op jit(solution)/shard_map/states/ppermute | solution.py:181
  14.9 6.7 %collective-permute-start.8 = (bf16[16,3200]{1,0:T(8,128)(2,1)S(1)}, bf16[16,3200]{1,0:T(8,128)(2,1)S(1)}, u32[]{:S(2)}, u32[]{:S(2)}) collective-permute-start(bf16[16,3200]{1,0:T(8,128)(2,1)S(1)} %states.1.refs_8_.refs_0_), channel_id=1, source_target_pairs={{0,12},{4,0},{8,4},{12,8},{1,13},{5,1},{9,5},{13,9},{2,14},{6,2},{... | collective-permute-start | bytes 307208 | tf_op jit(solution)/shard_map/states/ppermute | solution.py:181
  16.0 5.7 %copy-start = (bf16[128,3072]{1,0:T(8,128)(2,1)S(1)}, bf16[128,3072]{1,0:T(8,128)(2,1)}, u32[]{:S(2)}) copy-start(bf16[128,3072]{1,0:T(8,128)(2,1)} %refs_4_.1) | copy-start | bytes 2359300
  19.5 3.6 %collective-permute-start.3 = (f32[1,128]{1,0:T(1,128)S(1)}, f32[1,128]{1,0:T(1,128)S(1)}, u32[]{:S(2)}, u32[]{:S(2)}) collective-permute-start(f32[1,128]{1,0:T(1,128)S(1)} %get-tuple-element.31.refs_1_), channel_id=1, source_target_pairs={{0,2},{1,3},{2,0},{3,1},{4,6},{5,7},{6,4},{7,5},{8,10},{9,11},{10,... | collective-permute-start | bytes 1544 | tf_op jit(solution)/shard_map/pairs/ppermute | solution.py:274
  20.1 3.0 %collective-permute-start.5 = (f32[1,128]{1,0:T(1,128)S(1)}, f32[1,128]{1,0:T(1,128)S(1)}, u32[]{:S(2)}, u32[]{:S(2)}) collective-permute-start(f32[1,128]{1,0:T(1,128)S(1)} %get-tuple-element.31.refs_1_), channel_id=1, source_target_pairs={{0,3},{1,2},{2,1},{3,0},{4,7},{5,6},{6,5},{7,4},{8,11},{9,10},{10,... | collective-permute-start | bytes 1544 | tf_op jit(solution)/shard_map/pairs/ppermute | solution.py:274
  20.2 3.0 %collective-permute-start.7 = (f32[1,128]{1,0:T(1,128)S(1)}, f32[1,128]{1,0:T(1,128)S(1)}, u32[]{:S(2)}, u32[]{:S(2)}) collective-permute-start(f32[1,128]{1,0:T(1,128)S(1)} %get-tuple-element.31.refs_1_), channel_id=1, source_target_pairs={{0,1},{1,0},{2,3},{3,2},{4,5},{5,4},{6,7},{7,6},{8,9},{9,8},{10,11... | collective-permute-start | bytes 1544 | tf_op jit(solution)/shard_map/pairs/ppermute | solution.py:274
  23.3 5.4 %collective-permute-start.12 = (f32[1,128]{1,0:T(1,128)S(1)}, f32[1,128]{1,0:T(1,128)S(1)}, u32[]{:S(2)}, u32[]{:S(2)}) collective-permute-start(f32[1,128]{1,0:T(1,128)S(1)} %get-tuple-element.40), channel_id=1, source_target_pairs={{0,4},{4,8},{8,12},{12,0},{1,5},{5,9},{9,13},{13,1},{2,6},{6,10},{... | collective-permute-start | bytes 1544 | tf_op jit(solution)/shard_map/back/ppermute | solution.py:181
  24.3 4.4 %collective-permute-start.11 = (f32[1,128]{1,0:T(1,128)S(1)}, f32[1,128]{1,0:T(1,128)S(1)}, u32[]{:S(2)}, u32[]{:S(2)}) collective-permute-start(f32[1,128]{1,0:T(1,128)S(1)} %get-tuple-element.39), channel_id=1, source_target_pairs={{0,8},{4,12},{8,0},{12,4},{1,9},{5,13},{9,1},{13,5},{2,10},{6,14},... | collective-permute-start | bytes 1544 | tf_op jit(solution)/shard_map/back/ppermute | solution.py:181
  26.3 3.5 %collective-permute-start.10 = (f32[1,128]{1,0:T(1,128)S(1)}, f32[1,128]{1,0:T(1,128)S(1)}, u32[]{:S(2)}, u32[]{:S(2)}) collective-permute-start(f32[1,128]{1,0:T(1,128)S(1)} %get-tuple-element.38), channel_id=1, source_target_pairs={{0,12},{4,0},{8,4},{12,8},{1,13},{5,1},{9,5},{13,9},{2,14},{6,2},{... | collective-permute-start | bytes 1544 | tf_op jit(solution)/shard_map/back/ppermute | solution.py:181

commit v28 on v23

--- a/solution.py
+++ b/solution.py
@@ -164,7 +164,8 @@
 
 
 def score_kernel(total, planes, parts, *refs):
-    pairs, (linear, hits), outs = refs[:planes * parts], refs[planes * parts:planes * parts + 2], refs[planes * parts + 2:]
+    pairs, (linear, hits), refs = refs[:planes * parts], refs[planes * parts:planes * parts + 2], refs[planes * parts + 2:]
+    outs, rows = refs[:total], refs[total]
     half = linear.shape[1]
     sums = [sum(pairs[(h + 1) * planes - 1 - q][...] for h in range(parts)) for q in range(planes)]
     row = jnp.concatenate(sums, axis=1)
@@ -173,12 +174,19 @@
         pieces = jnp.where(iota(pieces.shape, 0) == t, part.astype(jnp.float32), pieces)
     added = jnp.sum(dot(pieces.astype(jnp.bfloat16), hits[...], NN), axis=0, keepdims=True)
     for j in range(total):
-        outs[j][...] = linear[j:j + 1, :] + added[:, j * half:(j + 1) * half]
+        rows[j:j + 1, :] = linear[j:j + 1, :] + added[:, j * half:(j + 1) * half]
+    me = lax.axis_index("shard")
+    for mask in range(total):
+        outs[mask][...] = rows[pl.ds(ring(me - (me ^ mask), total), 1), :]
 
 
 def shift(x, axis, step):
     size = lax.axis_size(axis)
     return lax.ppermute(x, axis, [(s, (s + step) % size) for s in range(size)])
+
+
+def swap(x, axis, mask):
+    return lax.ppermute(x, axis, [(s, s ^ mask) for s in range(lax.axis_size(axis))])
 
 
 def body(cand_items, reader_users, item_table, user_states, pair_mats, pair_fields):
@@ -295,6 +303,7 @@
             out_shape=[jax.ShapeDtypeStruct((1, half), jnp.float32)] * total,
             in_specs=[vmem] * (planes * parts + 2),
             out_specs=[vmem] * total,
+            scratch_shapes=[pltpu.VMEM((-(-total // 8) * 8, half), jnp.float32)],
             compiler_params=params,
             cost_estimate=pl.CostEstimate(flops=2 * 16 * 256 * 512, bytes_accessed=512 * 1024, transcendentals=0),
         )(*pair_scores, linear, hits)
@@ -302,7 +311,7 @@
     with jax.named_scope("back"):
         result = outs[0]
         for j in range(1, total):
-            result = result + shift(outs[j], "shard", -j)
+            result = result + swap(outs[j], "shard", j)
     return result.reshape(half)
 
 

time: 30.5 us -> 30.8 us (level)
  waiting for transfers between devices: 3.9 us -> 5.56 us
  starting transfers between devices: 18.7 us -> 17.4 us
    ppermute x10 -> x7, starting transfers between devices: 18.1 us -> 12.3 us  [shift(): return lax.ppermute(x, axis, [(s, (s + step) % size) for s in range(size)])]
    ppermute x0 -> x3, starting transfers between devices: none -> 4.45 us  [swap(): lax.ppermute(x, axis, [(s, s ^ mask) for s in range(lax.axis_size(axis))])]
    ppermute x0 -> x3, waiting for transfers between devices: none -> 3.37 us  [swap(): lax.ppermute(x, axis, [(s, s ^ mask) for s in range(lax.axis_size(axis))])]
    ppermute x10 -> x7, waiting for transfers between devices: 3.66 us -> 1.95 us  [shift(): return lax.ppermute(x, axis, [(s, (s + step) % size) for s in range(size)])]
where the time goes in v28:
time: 30.8 us; the launch traced here: 30.7 us
  starting transfers between devices  17.4 us (56%)
  Pallas kernels  7.15 us (23%)
  waiting for transfers between devices  5.56 us (18%)
  other arithmetic  0.52 us (2%)
    ppermute x7, starting transfers between devices, shift(): return lax.ppermute(x, axis, [(s, (s + step) % size) for s in range(size)])  12.3 us
    ppermute x3, starting transfers between devices, swap(): lax.ppermute(x, axis, [(s, s ^ mask) for s in range(lax.axis_size(axis))])  4.45 us
    pallas_call x1, Pallas kernels, body(): pl.pallas_call(functools.partial(pair_kernel, total, cap, slots, user_sta...  3.48 us
    ppermute x3, waiting for transfers between devices, swap(): lax.ppermute(x, axis, [(s, s ^ mask) for s in range(lax.axis_size(axis))])  3.37 us
    pallas_call x1, Pallas kernels, body(): pl.pallas_call(turn_kernel, out_shape=(jax.ShapeDtypeStruct((width, rows)...  2.2 us
    ppermute x7, waiting for transfers between devices, shift(): return lax.ppermute(x, axis, [(s, (s + step) % size) for s in range(size)])  1.95 us
    pallas_call x1, Pallas kernels, body(): pl.pallas_call(functools.partial(linear_kernel, total, planes), out_shape...  0.9 us
  transfers between devices with their start and end apart: 13, of which 5 were waited for; matrix products, arithmetic and copies ran while one was open for 0% of the time, Pallas kernels for 23%

profile of v28, /device:TPU:0, one launch (start us, length us, event | category | flops | bytes accessed | tf_op | source)
XLA Modules:
  0.0 30.7 jit_solution(5912508911561868045)
XLA Ops:
  0.0 2.9 %collective-permute-start.9 = (bf16[128,3072]{1,0:T(8,128)(2,1)}, bf16[128,3072]{1,0:T(8,128)(2,1)S(1)}, u32[]{:S(2)}, u32[]{:S(2)}) collective-permute-start(bf16[128,3072]{1,0:T(8,128)(2,1)} %refs_4_.1), channel_id=1, source_target_pairs={{0,2},{2,0},{1,3},{3,1},{4,6},{6,4},{5,7},{7,5},{8,10},{10,8},{9,1... | collective-permute-start | bytes 2359304 | tf_op jit(solution)/shard_map/item_rows/ppermute | solution.py:185
  2.9 1.6 %collective-permute-start = (s32[8]{0:T(128)}, s32[8]{0:T(128)S(1)}, u32[]{:S(2)}, u32[]{:S(2)}) collective-permute-start(s32[8]{0:T(128)} %param.7), channel_id=1, source_target_pairs={{0,4},{4,8},{8,12},{12,0},{1,5},{5,9},{9,13},{13,1},{2,6},{6,10},{... | collective-permute-start | bytes 104 | tf_op jit(solution)/shard_map/ids/ppermute | solution.py:185
  4.5 2.6 %collective-permute-start.1 = (s32[8]{0:T(128)}, s32[8]{0:T(128)S(1)}, u32[]{:S(2)}, u32[]{:S(2)}) collective-permute-start(s32[8]{0:T(128)} %param.7), channel_id=1, source_target_pairs={{0,8},{4,12},{8,0},{12,4},{1,9},{5,13},{9,1},{13,5},{2,10},{6,14},... | collective-permute-start | bytes 104 | tf_op jit(solution)/shard_map/ids/ppermute | solution.py:185
  7.1 1.3 %collective-permute-start.2 = (s32[8]{0:T(128)}, s32[8]{0:T(128)S(1)}, u32[]{:S(2)}, u32[]{:S(2)}) collective-permute-start(s32[8]{0:T(128)} %param.7), channel_id=1, source_target_pairs={{0,12},{4,0},{8,4},{12,8},{1,13},{5,1},{9,5},{13,9},{2,14},{6,2},{... | collective-permute-start | bytes 104 | tf_op jit(solution)/shard_map/ids/ppermute | solution.py:185
  8.5 2.2 %turn.1 = (f32[3072,128]{1,0:T(8,128)S(1)}, bf16[3072,128]{1,0:T(8,128)(2,1)S(1)}, bf16[64,64,256]{2,1,0:T(8,128)(2,1)S(1)}, bf16[128,3072]{1,0:T(8,128)(2,1)S(1...) custom-call(bf16[128,3072]{1,0:T(8,128)(2,1)} %refs_4_.1, bf16[64,64,256]{2,1,0:T(8,128)(2,1)} %bitcast.15, ...), custom_call_target="tpu_custom_call" | custom-call | flops 1610612736 | bytes 8388608 | tf_op jit(solution)/shard_map/turn/pallas_call | solution.py:217
  10.7 0.0 collective-permute-done
  10.7 0.0 collective-permute-done.1
  10.7 0.1 collective-permute-done.2
  10.8 0.4 %states.1.refs_8_.refs_0_ = bf16[16,3200]{1,0:T(8,128)(2,1)S(1)} custom-call(s32[1,8]{1,0:T(1,128)S(1)} %get-tuple-element.23.refs_0_, s32[1,8]{1,0:T(1,128)S(1)} %bitcast.9, s32[1,8]{1,0:T(1,128)S(1)} %bitcast.11, s32[1,8]{1,0:T(1,128)S(1)} %bitcast.13, bf16[16,128]{1,0:T(8,128)(2,1)S(1)} %get-tuple-element.27.refs_4_, ...), custom_call_target="tpu_custom_call" | custom-call | flops 12582912 | bytes 1048576 | tf_op jit(solution)/shard_map/states/pallas_call | solution.py:246
  11.2 0.6 %collective-permute-start.4 = (bf16[16,3200]{1,0:T(8,128)(2,1)S(1)}, bf16[16,3200]{1,0:T(8,128)(2,1)S(1)}, u32[]{:S(2)}, u32[]{:S(2)}) collective-permute-start(bf16[16,3200]{1,0:T(8,128)(2,1)S(1)} %states.1.refs_8_.refs_0_), channel_id=1, source_target_pairs={{0,4},{4,8},{8,12},{12,0},{1,5},{5,9},{9,13},{13,1},{2,6},{6,10},{... | collective-permute-start | bytes 307208 | tf_op jit(solution)/shard_map/states/ppermute | solution.py:185
  11.8 3.1 %collective-permute-start.6 = (bf16[16,3200]{1,0:T(8,128)(2,1)S(1)}, bf16[16,3200]{1,0:T(8,128)(2,1)S(1)}, u32[]{:S(2)}, u32[]{:S(2)}) collective-permute-start(bf16[16,3200]{1,0:T(8,128)(2,1)S(1)} %states.1.refs_8_.refs_0_), channel_id=1, source_target_pairs={{0,8},{4,12},{8,0},{12,4},{1,9},{5,13},{9,1},{13,5},{2,10},{6,14},... | collective-permute-start | bytes 307208 | tf_op jit(solution)/shard_map/states/ppermute | solution.py:185
  14.9 0.1 collective-permute-start.8
  15.1 0.0 copy-start
  15.1 3.5 %pairs.1 = (f32[1,128]{1,0:T(1,128)S(1)}, s32[4,128]{1,0:T(4,128)S(1)}) custom-call(s32[1,8]{1,0:T(1,128)S(1)} %get-tuple-element.23.refs_0_, s32[1,8]{1,0:T(1,128)S(1)} %bitcast.10, s32[1,8]{1,0:T(1,128)S(1)} %bitcast.12, s32[1,8]{1,0:T(1,128)S(1)} %bitcast.14, s32[2,256]{1,0:T(2,128)} %bitcast.16, f32[3072,128]{1,0:T(8,128)S(1)} %get-tuple-element.24.refs_5_, ...), custom_call_target="tpu_custom_call" | custom-call | flops 4294967296 | bytes 4194304 | tf_op jit(solution)/shard_map/pairs/pallas_call | solution.py:257
  18.5 0.6 %collective-permute-start.3 = (f32[1,128]{1,0:T(1,128)S(1)}, f32[1,128]{1,0:T(1,128)S(1)}, u32[]{:S(2)}, u32[]{:S(2)}) collective-permute-start(f32[1,128]{1,0:T(1,128)S(1)} %get-tuple-element.31.refs_1_), channel_id=1, source_target_pairs={{0,2},{1,3},{2,0},{3,1},{4,6},{5,7},{6,4},{7,5},{8,10},{9,11},{10,... | collective-permute-start | bytes 1544 | tf_op jit(solution)/shard_map/pairs/ppermute | solution.py:282
  19.1 0.0 collective-permute-done.4.refs_1_
  19.1 0.0 collective-permute-start.5
  19.2 1.8 %collective-permute-done.6.refs_2_ = bf16[16,3200]{1,0:T(8,128)(2,1)S(1)} collective-permute-done((bf16[16,3200]{1,0:T(8,128)(2,1)S(1)}, bf16[16,3200]{1,0:T(8,128)(2,1)S(1)}, u32[]{:S(2)}, u32[]{:S(2)}) %collective-permute-start.6) | collective-permute-done | bytes 102432 | tf_op jit(solution)/shard_map/states/ppermute | solution.py:185
  21.0 0.0 collective-permute-start.7
  21.0 0.0 collective-permute-done.8.refs_3_
  21.0 0.0 collective-permute-done.9.refs_5_
  21.0 0.0 copy-done
  21.0 0.9 %scores.2 = (f32[4,128]{1,0:T(4,128)S(1)}, bf16[256,512]{1,0:T(8,128)(2,1)S(1)}) custom-call(bf16[16,3200]{1,0:T(8,128)(2,1)S(1)} %states.1.refs_8_.refs_0_, bf16[16,3200]{1,0:T(8,128)(2,1)S(1)} %collective-permute-done.4.refs_1_, bf16[16,3200]{1,0:T(8,128)(2,1)S(1)} %collective-permute-done.6.refs_2_, bf16[16,3200]{1,0:T(8,128)(2,1)S(1)} %collective-permute-done.8.refs_3_, ...), custom_call_target="tpu_custom_call" | custom-call | flops 100663296 | bytes 2097152 | tf_op jit(solution)/shard_map/scores/pallas_call | solution.py:286
  21.9 0.2 collective-permute-done.3.refs_0_
  22.2 0.0 collective-permute-done.5.refs_2_
  22.2 0.0 collective-permute-done.7.refs_3_
  22.2 0.2 scores.3
  22.3 3.4 %collective-permute-start.12 = (f32[1,128]{1,0:T(1,128)S(1)}, f32[1,128]{1,0:T(1,128)S(1)}, u32[]{:S(2)}, u32[]{:S(2)}) collective-permute-start(f32[1,128]{1,0:T(1,128)S(1)} %get-tuple-element.40), channel_id=1, source_target_pairs={{0,12},{4,8},{8,4},{12,0},{1,13},{5,9},{9,5},{13,1},{2,14},{6,10},... | collective-permute-start | bytes 1544 | tf_op jit(solution)/shard_map/back/ppermute | solution.py:189
  25.7 0.1 collective-permute-start.11
  25.8 1.0 %collective-permute-start.10 = (f32[1,128]{1,0:T(1,128)S(1)}, f32[1,128]{1,0:T(1,128)S(1)}, u32[]{:S(2)}, u32[]{:S(2)}) collective-permute-start(f32[1,128]{1,0:T(1,128)S(1)} %get-tuple-element.38), channel_id=1, source_target_pairs={{0,4},{4,0},{8,12},{12,8},{1,5},{5,1},{9,13},{13,9},{2,6},{6,2},{1... | collective-permute-start | bytes 1544 | tf_op jit(solution)/shard_map/back/ppermute | solution.py:189
  26.8 0.9 %collective-permute-done.12 = f32[1,128]{1,0:T(1,128)S(1)} collective-permute-done((f32[1,128]{1,0:T(1,128)S(1)}, f32[1,128]{1,0:T(1,128)S(1)}, u32[]{:S(2)}, u32[]{:S(2)}) %collective-permute-start.12) | collective-permute-done | bytes 544 | tf_op jit(solution)/shard_map/back/ppermute | solution.py:189
  27.7 2.4 %collective-permute-done.11 = f32[1,128]{1,0:T(1,128)S(1)} collective-permute-done((f32[1,128]{1,0:T(1,128)S(1)}, f32[1,128]{1,0:T(1,128)S(1)}, u32[]{:S(2)}, u32[]{:S(2)}) %collective-permute-start.11) | collective-permute-done | bytes 544 | tf_op jit(solution)/shard_map/back/ppermute | solution.py:189
  30.1 0.0 collective-permute-done.10
  30.1 0.5 %add_bitcast_fusion = f32[128]{0:T(128)} fusion(f32[1,128]{1,0:T(1,128)S(1)} %collective-permute-done.12, f32[1,128]{1,0:T(1,128)S(1)} %collective-permute-done.11, f32[1,128]{1,0:T(1,128)S(1)} %get-tuple-element.37, f32[1,128]{1,0:T(1,128)S(1)} %collective-permute-done.10), kind=kLoop, calls=%fused_computation | loop fusion | flops 384 | bytes 2560 | tf_op jit(solution)/shard_map/reshape | solution.py:315
Async XLA Ops:
  0.0 21.0 %collective-permute-start.9 = (bf16[128,3072]{1,0:T(8,128)(2,1)}, bf16[128,3072]{1,0:T(8,128)(2,1)S(1)}, u32[]{:S(2)}, u32[]{:S(2)}) collective-permute-start(bf16[128,3072]{1,0:T(8,128)(2,1)} %refs_4_.1), channel_id=1, source_target_pairs={{0,2},{2,0},{1,3},{3,1},{4,6},{6,4},{5,7},{7,5},{8,10},{10,8},{9,1... | collective-permute-start | bytes 2359304 | tf_op jit(solution)/shard_map/item_rows/ppermute | solution.py:185
  2.9 7.7 %collective-permute-start = (s32[8]{0:T(128)}, s32[8]{0:T(128)S(1)}, u32[]{:S(2)}, u32[]{:S(2)}) collective-permute-start(s32[8]{0:T(128)} %param.7), channel_id=1, source_target_pairs={{0,4},{4,8},{8,12},{12,0},{1,5},{5,9},{9,13},{13,1},{2,6},{6,10},{... | collective-permute-start | bytes 104 | tf_op jit(solution)/shard_map/ids/ppermute | solution.py:185
  4.5 6.2 %collective-permute-start.1 = (s32[8]{0:T(128)}, s32[8]{0:T(128)S(1)}, u32[]{:S(2)}, u32[]{:S(2)}) collective-permute-start(s32[8]{0:T(128)} %param.7), channel_id=1, source_target_pairs={{0,8},{4,12},{8,0},{12,4},{1,9},{5,13},{9,1},{13,5},{2,10},{6,14},... | collective-permute-start | bytes 104 | tf_op jit(solution)/shard_map/ids/ppermute | solution.py:185
  7.1 3.7 %collective-permute-start.2 = (s32[8]{0:T(128)}, s32[8]{0:T(128)S(1)}, u32[]{:S(2)}, u32[]{:S(2)}) collective-permute-start(s32[8]{0:T(128)} %param.7), channel_id=1, source_target_pairs={{0,12},{4,0},{8,4},{12,8},{1,13},{5,1},{9,5},{13,9},{2,14},{6,2},{... | collective-permute-start | bytes 104 | tf_op jit(solution)/shard_map/ids/ppermute | solution.py:185
  11.2 8.0 %collective-permute-start.4 = (bf16[16,3200]{1,0:T(8,128)(2,1)S(1)}, bf16[16,3200]{1,0:T(8,128)(2,1)S(1)}, u32[]{:S(2)}, u32[]{:S(2)}) collective-permute-start(bf16[16,3200]{1,0:T(8,128)(2,1)S(1)} %states.1.refs_8_.refs_0_), channel_id=1, source_target_pairs={{0,4},{4,8},{8,12},{12,0},{1,5},{5,9},{9,13},{13,1},{2,6},{6,10},{... | collective-permute-start | bytes 307208 | tf_op jit(solution)/shard_map/states/ppermute | solution.py:185
  11.8 9.2 %collective-permute-start.6 = (bf16[16,3200]{1,0:T(8,128)(2,1)S(1)}, bf16[16,3200]{1,0:T(8,128)(2,1)S(1)}, u32[]{:S(2)}, u32[]{:S(2)}) collective-permute-start(bf16[16,3200]{1,0:T(8,128)(2,1)S(1)} %states.1.refs_8_.refs_0_), channel_id=1, source_target_pairs={{0,8},{4,12},{8,0},{12,4},{1,9},{5,13},{9,1},{13,5},{2,10},{6,14},... | collective-permute-start | bytes 307208 | tf_op jit(solution)/shard_map/states/ppermute | solution.py:185
  14.9 6.1 %collective-permute-start.8 = (bf16[16,3200]{1,0:T(8,128)(2,1)S(1)}, bf16[16,3200]{1,0:T(8,128)(2,1)S(1)}, u32[]{:S(2)}, u32[]{:S(2)}) collective-permute-start(bf16[16,3200]{1,0:T(8,128)(2,1)S(1)} %states.1.refs_8_.refs_0_), channel_id=1, source_target_pairs={{0,12},{4,0},{8,4},{12,8},{1,13},{5,1},{9,5},{13,9},{2,14},{6,2},{... | collective-permute-start | bytes 307208 | tf_op jit(solution)/shard_map/states/ppermute | solution.py:185
  15.1 6.0 %copy-start = (bf16[128,3072]{1,0:T(8,128)(2,1)S(1)}, bf16[128,3072]{1,0:T(8,128)(2,1)}, u32[]{:S(2)}) copy-start(bf16[128,3072]{1,0:T(8,128)(2,1)} %refs_4_.1) | copy-start | bytes 2359300
  18.5 3.6 %collective-permute-start.3 = (f32[1,128]{1,0:T(1,128)S(1)}, f32[1,128]{1,0:T(1,128)S(1)}, u32[]{:S(2)}, u32[]{:S(2)}) collective-permute-start(f32[1,128]{1,0:T(1,128)S(1)} %get-tuple-element.31.refs_1_), channel_id=1, source_target_pairs={{0,2},{1,3},{2,0},{3,1},{4,6},{5,7},{6,4},{7,5},{8,10},{9,11},{10,... | collective-permute-start | bytes 1544 | tf_op jit(solution)/shard_map/pairs/ppermute | solution.py:282
  19.1 3.0 %collective-permute-start.5 = (f32[1,128]{1,0:T(1,128)S(1)}, f32[1,128]{1,0:T(1,128)S(1)}, u32[]{:S(2)}, u32[]{:S(2)}) collective-permute-start(f32[1,128]{1,0:T(1,128)S(1)} %get-tuple-element.31.refs_1_), channel_id=1, source_target_pairs={{0,3},{1,2},{2,1},{3,0},{4,7},{5,6},{6,5},{7,4},{8,11},{9,10},{10,... | collective-permute-start | bytes 1544 | tf_op jit(solution)/shard_map/pairs/ppermute | solution.py:282
  21.0 1.2 %collective-permute-start.7 = (f32[1,128]{1,0:T(1,128)S(1)}, f32[1,128]{1,0:T(1,128)S(1)}, u32[]{:S(2)}, u32[]{:S(2)}) collective-permute-start(f32[1,128]{1,0:T(1,128)S(1)} %get-tuple-element.31.refs_1_), channel_id=1, source_target_pairs={{0,1},{1,0},{2,3},{3,2},{4,5},{5,4},{6,7},{7,6},{8,9},{9,8},{10,11... | collective-permute-start | bytes 1544 | tf_op jit(solution)/shard_map/pairs/ppermute | solution.py:282
  22.3 5.4 %collective-permute-start.12 = (f32[1,128]{1,0:T(1,128)S(1)}, f32[1,128]{1,0:T(1,128)S(1)}, u32[]{:S(2)}, u32[]{:S(2)}) collective-permute-start(f32[1,128]{1,0:T(1,128)S(1)} %get-tuple-element.40), channel_id=1, source_target_pairs={{0,12},{4,8},{8,4},{12,0},{1,13},{5,9},{9,5},{13,1},{2,14},{6,10},... | collective-permute-start | bytes 1544 | tf_op jit(solution)/shard_map/back/ppermute | solution.py:189
  25.7 4.4 %collective-permute-start.11 = (f32[1,128]{1,0:T(1,128)S(1)}, f32[1,128]{1,0:T(1,128)S(1)}, u32[]{:S(2)}, u32[]{:S(2)}) collective-permute-start(f32[1,128]{1,0:T(1,128)S(1)} %get-tuple-element.39), channel_id=1, source_target_pairs={{0,8},{4,12},{8,0},{12,4},{1,9},{5,13},{9,1},{13,5},{2,10},{6,14},... | collective-permute-start | bytes 1544 | tf_op jit(solution)/shard_map/back/ppermute | solution.py:189
  25.8 4.4 %collective-permute-start.10 = (f32[1,128]{1,0:T(1,128)S(1)}, f32[1,128]{1,0:T(1,128)S(1)}, u32[]{:S(2)}, u32[]{:S(2)}) collective-permute-start(f32[1,128]{1,0:T(1,128)S(1)} %get-tuple-element.38), channel_id=1, source_target_pairs={{0,4},{4,0},{8,12},{12,8},{1,5},{5,1},{9,13},{13,9},{2,6},{6,2},{1... | collective-permute-start | bytes 1544 | tf_op jit(solution)/shard_map/back/ppermute | solution.py:189

commit v29 on v23

--- a/solution.py
+++ b/solution.py
@@ -44,7 +44,7 @@
         mine = (column >= first) & (column < first + own_rows)
         rank = jnp.sum(jnp.where((down < across) & mine, 1, 0), axis=0, keepdims=True)
         held = (row >= first) & (row < first + own_rows)
-        slot = jnp.where(held, ring(me - j, total) * cap + rank, -1)
+        slot = jnp.where(held, ring(me + j, total) * cap + rank, -1)
         to_slot = (iota((slots, readers), 0) == slot).astype(jnp.float32).astype(jnp.bfloat16)
         from_row = (iota((readers, own_rows), 1) + first == column).astype(jnp.float32).astype(jnp.bfloat16)
         chosen = chosen + dot(to_slot, from_row, NN)
@@ -96,8 +96,8 @@
         holder = users[j][...] >> (user_rows.bit_length() - 1)
         column = jnp.sum(jnp.where(across == down, holder, 0), axis=1, keepdims=True)
         rank = jnp.sum(jnp.where((down < across) & (column == holder), 1, 0), axis=0, keepdims=True)
-        arrival = jnp.where(holder > me, me - holder + total, me - holder)
-        slot = (arrival * slots + ring(me - j, total) * cap + rank).astype(jnp.float32)
+        arrival = jnp.where(holder < me, holder - me + total, holder - me)
+        slot = (arrival * slots + ring(me + j, total) * cap + rank).astype(jnp.float32)
         places[j:j + 1, :] = dot(slot, asks, NN, precision=lax.Precision.HIGHEST).astype(jnp.int32)
     pairs = mats.shape[2]
     steps = pairs // 2
@@ -203,7 +203,7 @@
         items = [item_table] + [shift(item_table, "cache", q) for q in range(1, planes)]
 
     with jax.named_scope("ids"):
-        users = [shift(reader_users, "shard", j) for j in range(1, total)]
+        users = [shift(reader_users, "shard", -j) for j in range(1, total)]
 
     with jax.named_scope("turn"):
         *turned, states_near, own_ids, digits = pl.pallas_call(
@@ -243,7 +243,7 @@
             compiler_params=params,
             cost_estimate=pl.CostEstimate(flops=2 * slots * rows * width, bytes_accessed=1024 * 1024, transcendentals=0),
         )(*users_near, digits, states_near)
-        states = [picked] + [shift(picked, "shard", j) for j in range(1, total)]
+        states = [picked] + [shift(picked, "shard", -j) for j in range(1, total)]
 
     with jax.named_scope("pairs"):
         pair_parts, places = pl.pallas_call(
@@ -302,7 +302,7 @@
     with jax.named_scope("back"):
         result = outs[0]
         for j in range(1, total):
-            result = result + shift(outs[j], "shard", -j)
+            result = result + shift(outs[j], "shard", j)
     return result.reshape(half)
 
 

time: 30.5 us -> 33.1 us (1.085)
  waiting for transfers between devices: 3.9 us -> 10.6 us
  starting transfers between devices: 18.7 us -> 14.6 us
    ppermute x10, waiting for transfers between devices: 3.66 us -> 10.4 us  [shift(): return lax.ppermute(x, axis, [(s, (s + step) % size) for s in range(size)])]
    ppermute x10, starting transfers between devices: 18.1 us -> 14 us  [shift(): return lax.ppermute(x, axis, [(s, (s + step) % size) for s in range(size)])]
  transfers between devices with their start and end apart: 13 -> 13, of which waited for: 5 -> 7; matrix products, arithmetic and copies ran while one was open for 0% -> 0% of each run, Pallas kernels for 23% -> 21%
where the time goes in v29:
time: 33.1 us; the launch traced here: 32.9 us
  starting transfers between devices  14.6 us (44%)
  waiting for transfers between devices  10.6 us (32%)
  Pallas kernels  7.12 us (22%)
  other arithmetic  0.52 us (2%)
    ppermute x10, starting transfers between devices, shift(): return lax.ppermute(x, axis, [(s, (s + step) % size) for s in range(size)])  14 us
    ppermute x10, waiting for transfers between devices, shift(): return lax.ppermute(x, axis, [(s, (s + step) % size) for s in range(size)])  10.4 us
    pallas_call x1, Pallas kernels, body(): pl.pallas_call(functools.partial(pair_kernel, total, cap, slots, user_sta...  3.49 us
    pallas_call x1, Pallas kernels, body(): pl.pallas_call(turn_kernel, out_shape=(jax.ShapeDtypeStruct((width, rows)...  2.2 us
    pallas_call x1, Pallas kernels, body(): pl.pallas_call(functools.partial(linear_kernel, total, planes), out_shape...  0.88 us
  transfers between devices with their start and end apart: 13, of which 7 were waited for; matrix products, arithmetic and copies ran while one was open for 0% of the time, Pallas kernels for 21%

profile of v29, /device:TPU:0, one launch (start us, length us, event | category | flops | bytes accessed | tf_op | source)
XLA Modules:
  0.0 32.9 jit_solution(7095649091133169976)
XLA Ops:
  0.0 2.9 %collective-permute-start.9 = (bf16[128,3072]{1,0:T(8,128)(2,1)}, bf16[128,3072]{1,0:T(8,128)(2,1)S(1)}, u32[]{:S(2)}, u32[]{:S(2)}) collective-permute-start(bf16[128,3072]{1,0:T(8,128)(2,1)} %refs_4_.1), channel_id=1, source_target_pairs={{0,2},{2,0},{1,3},{3,1},{4,6},{6,4},{5,7},{7,5},{8,10},{10,8},{9,1... | collective-permute-start | bytes 2359304 | tf_op jit(solution)/shard_map/item_rows/ppermute | solution.py:181
  2.9 3.6 %collective-permute-start = (s32[8]{0:T(128)}, s32[8]{0:T(128)S(1)}, u32[]{:S(2)}, u32[]{:S(2)}) collective-permute-start(s32[8]{0:T(128)} %param.7), channel_id=1, source_target_pairs={{0,12},{4,0},{8,4},{12,8},{1,13},{5,1},{9,5},{13,9},{2,14},{6,2},{... | collective-permute-start | bytes 104 | tf_op jit(solution)/shard_map/ids/ppermute | solution.py:181
  6.5 0.0 collective-permute-start.1
  6.5 1.0 %collective-permute-start.2 = (s32[8]{0:T(128)}, s32[8]{0:T(128)S(1)}, u32[]{:S(2)}, u32[]{:S(2)}) collective-permute-start(s32[8]{0:T(128)} %param.7), channel_id=1, source_target_pairs={{0,4},{4,8},{8,12},{12,0},{1,5},{5,9},{9,13},{13,1},{2,6},{6,10},{... | collective-permute-start | bytes 104 | tf_op jit(solution)/shard_map/ids/ppermute | solution.py:181
  7.6 2.2 %turn.1 = (f32[3072,128]{1,0:T(8,128)S(1)}, bf16[3072,128]{1,0:T(8,128)(2,1)S(1)}, bf16[64,64,256]{2,1,0:T(8,128)(2,1)S(1)}, bf16[128,3072]{1,0:T(8,128)(2,1)S(1...) custom-call(bf16[128,3072]{1,0:T(8,128)(2,1)} %refs_4_.1, bf16[64,64,256]{2,1,0:T(8,128)(2,1)} %bitcast.15, ...), custom_call_target="tpu_custom_call" | custom-call | flops 1610612736 | bytes 8388608 | tf_op jit(solution)/shard_map/turn/pallas_call | solution.py:209
  9.8 0.0 collective-permute-done
  9.8 1.3 %collective-permute-done.1 = s32[8]{0:T(128)S(1)} collective-permute-done((s32[8]{0:T(128)}, s32[8]{0:T(128)S(1)}, u32[]{:S(2)}, u32[]{:S(2)}) %collective-permute-start.1) | collective-permute-done | bytes 64 | tf_op jit(solution)/shard_map/ids/ppermute | solution.py:181
  11.1 0.9 %collective-permute-done.2 = s32[8]{0:T(128)S(1)} collective-permute-done((s32[8]{0:T(128)}, s32[8]{0:T(128)S(1)}, u32[]{:S(2)}, u32[]{:S(2)}) %collective-permute-start.2) | collective-permute-done | bytes 64 | tf_op jit(solution)/shard_map/ids/ppermute | solution.py:181
  12.0 0.4 %states.1.refs_8_.refs_0_ = bf16[16,3200]{1,0:T(8,128)(2,1)S(1)} custom-call(s32[1,8]{1,0:T(1,128)S(1)} %get-tuple-element.23.refs_0_, s32[1,8]{1,0:T(1,128)S(1)} %bitcast.9, s32[1,8]{1,0:T(1,128)S(1)} %bitcast.11, s32[1,8]{1,0:T(1,128)S(1)} %bitcast.13, bf16[16,128]{1,0:T(8,128)(2,1)S(1)} %get-tuple-element.27.refs_4_, ...), custom_call_target="tpu_custom_call" | custom-call | flops 12582912 | bytes 1048576 | tf_op jit(solution)/shard_map/states/pallas_call | solution.py:238
  12.4 0.6 %collective-permute-start.4 = (bf16[16,3200]{1,0:T(8,128)(2,1)S(1)}, bf16[16,3200]{1,0:T(8,128)(2,1)S(1)}, u32[]{:S(2)}, u32[]{:S(2)}) collective-permute-start(bf16[16,3200]{1,0:T(8,128)(2,1)S(1)} %states.1.refs_8_.refs_0_), channel_id=1, source_target_pairs={{0,12},{4,0},{8,4},{12,8},{1,13},{5,1},{9,5},{13,9},{2,14},{6,2},{... | collective-permute-start | bytes 307208 | tf_op jit(solution)/shard_map/states/ppermute | solution.py:181
  13.1 1.1 %collective-permute-start.6 = (bf16[16,3200]{1,0:T(8,128)(2,1)S(1)}, bf16[16,3200]{1,0:T(8,128)(2,1)S(1)}, u32[]{:S(2)}, u32[]{:S(2)}) collective-permute-start(bf16[16,3200]{1,0:T(8,128)(2,1)S(1)} %states.1.refs_8_.refs_0_), channel_id=1, source_target_pairs={{0,8},{4,12},{8,0},{12,4},{1,9},{5,13},{9,1},{13,5},{2,10},{6,14},... | collective-permute-start | bytes 307208 | tf_op jit(solution)/shard_map/states/ppermute | solution.py:181
  14.2 1.4 %collective-permute-start.8 = (bf16[16,3200]{1,0:T(8,128)(2,1)S(1)}, bf16[16,3200]{1,0:T(8,128)(2,1)S(1)}, u32[]{:S(2)}, u32[]{:S(2)}) collective-permute-start(bf16[16,3200]{1,0:T(8,128)(2,1)S(1)} %states.1.refs_8_.refs_0_), channel_id=1, source_target_pairs={{0,4},{4,8},{8,12},{12,0},{1,5},{5,9},{9,13},{13,1},{2,6},{6,10},{... | collective-permute-start | bytes 307208 | tf_op jit(solution)/shard_map/states/ppermute | solution.py:181
  15.6 0.0 copy-start
  15.6 3.5 %pairs.1 = (f32[1,128]{1,0:T(1,128)S(1)}, s32[4,128]{1,0:T(4,128)S(1)}) custom-call(s32[1,8]{1,0:T(1,128)S(1)} %get-tuple-element.23.refs_0_, s32[1,8]{1,0:T(1,128)S(1)} %bitcast.10, s32[1,8]{1,0:T(1,128)S(1)} %bitcast.12, s32[1,8]{1,0:T(1,128)S(1)} %bitcast.14, s32[2,256]{1,0:T(2,128)} %bitcast.16, f32[3072,128]{1,0:T(8,128)S(1)} %get-tuple-element.24.refs_5_, ...), custom_call_target="tpu_custom_call" | custom-call | flops 4294967296 | bytes 4194304 | tf_op jit(solution)/shard_map/pairs/pallas_call | solution.py:249
  19.1 0.6 %collective-permute-start.3 = (f32[1,128]{1,0:T(1,128)S(1)}, f32[1,128]{1,0:T(1,128)S(1)}, u32[]{:S(2)}, u32[]{:S(2)}) collective-permute-start(f32[1,128]{1,0:T(1,128)S(1)} %get-tuple-element.31.refs_1_), channel_id=1, source_target_pairs={{0,2},{1,3},{2,0},{3,1},{4,6},{5,7},{6,4},{7,5},{8,10},{9,11},{10,... | collective-permute-start | bytes 1544 | tf_op jit(solution)/shard_map/pairs/ppermute | solution.py:274
  19.7 0.0 collective-permute-done.4.refs_1_
  19.7 0.0 collective-permute-start.5
  19.7 3.2 %collective-permute-done.6.refs_2_ = bf16[16,3200]{1,0:T(8,128)(2,1)S(1)} collective-permute-done((bf16[16,3200]{1,0:T(8,128)(2,1)S(1)}, bf16[16,3200]{1,0:T(8,128)(2,1)S(1)}, u32[]{:S(2)}, u32[]{:S(2)}) %collective-permute-start.6) | collective-permute-done | bytes 102432 | tf_op jit(solution)/shard_map/states/ppermute | solution.py:181
  22.9 0.0 collective-permute-start.7
  22.9 0.0 collective-permute-done.8.refs_3_
  22.9 0.0 collective-permute-done.9.refs_5_
  23.0 0.0 copy-done
  23.0 0.9 %scores.2 = (f32[4,128]{1,0:T(4,128)S(1)}, bf16[256,512]{1,0:T(8,128)(2,1)S(1)}) custom-call(bf16[16,3200]{1,0:T(8,128)(2,1)S(1)} %states.1.refs_8_.refs_0_, bf16[16,3200]{1,0:T(8,128)(2,1)S(1)} %collective-permute-done.4.refs_1_, bf16[16,3200]{1,0:T(8,128)(2,1)S(1)} %collective-permute-done.6.refs_2_, bf16[16,3200]{1,0:T(8,128)(2,1)S(1)} %collective-permute-done.8.refs_3_, ...), custom_call_target="tpu_custom_call" | custom-call | flops 100663296 | bytes 2097152 | tf_op jit(solution)/shard_map/scores/pallas_call | solution.py:278
  23.8 0.0 collective-permute-done.3.refs_0_
  23.9 0.0 collective-permute-done.5.refs_2_
  23.9 0.2 collective-permute-done.7.refs_3_
  24.1 0.2 scores.3
  24.2 1.5 %collective-permute-start.12 = (f32[1,128]{1,0:T(1,128)S(1)}, f32[1,128]{1,0:T(1,128)S(1)}, u32[]{:S(2)}, u32[]{:S(2)}) collective-permute-start(f32[1,128]{1,0:T(1,128)S(1)} %get-tuple-element.40), channel_id=1, source_target_pairs={{0,12},{4,0},{8,4},{12,8},{1,13},{5,1},{9,5},{13,9},{2,14},{6,2},{... | collective-permute-start | bytes 1544 | tf_op jit(solution)/shard_map/back/ppermute | solution.py:181
  25.7 1.4 %collective-permute-start.11 = (f32[1,128]{1,0:T(1,128)S(1)}, f32[1,128]{1,0:T(1,128)S(1)}, u32[]{:S(2)}, u32[]{:S(2)}) collective-permute-start(f32[1,128]{1,0:T(1,128)S(1)} %get-tuple-element.39), channel_id=1, source_target_pairs={{0,8},{4,12},{8,0},{12,4},{1,9},{5,13},{9,1},{13,5},{2,10},{6,14},... | collective-permute-start | bytes 1544 | tf_op jit(solution)/shard_map/back/ppermute | solution.py:181
  27.1 0.4 %collective-permute-start.10 = (f32[1,128]{1,0:T(1,128)S(1)}, f32[1,128]{1,0:T(1,128)S(1)}, u32[]{:S(2)}, u32[]{:S(2)}) collective-permute-start(f32[1,128]{1,0:T(1,128)S(1)} %get-tuple-element.38), channel_id=1, source_target_pairs={{0,4},{4,8},{8,12},{12,0},{1,5},{5,9},{9,13},{13,1},{2,6},{6,10},{... | collective-permute-start | bytes 1544 | tf_op jit(solution)/shard_map/back/ppermute | solution.py:181
  27.5 0.4 %collective-permute-done.12 = f32[1,128]{1,0:T(1,128)S(1)} collective-permute-done((f32[1,128]{1,0:T(1,128)S(1)}, f32[1,128]{1,0:T(1,128)S(1)}, u32[]{:S(2)}, u32[]{:S(2)}) %collective-permute-start.12) | collective-permute-done | bytes 544 | tf_op jit(solution)/shard_map/back/ppermute | solution.py:181
  27.8 2.3 %collective-permute-done.11 = f32[1,128]{1,0:T(1,128)S(1)} collective-permute-done((f32[1,128]{1,0:T(1,128)S(1)}, f32[1,128]{1,0:T(1,128)S(1)}, u32[]{:S(2)}, u32[]{:S(2)}) %collective-permute-start.11) | collective-permute-done | bytes 544 | tf_op jit(solution)/shard_map/back/ppermute | solution.py:181
  30.1 2.3 %collective-permute-done.10 = f32[1,128]{1,0:T(1,128)S(1)} collective-permute-done((f32[1,128]{1,0:T(1,128)S(1)}, f32[1,128]{1,0:T(1,128)S(1)}, u32[]{:S(2)}, u32[]{:S(2)}) %collective-permute-start.10) | collective-permute-done | bytes 544 | tf_op jit(solution)/shard_map/back/ppermute | solution.py:181
  32.4 0.5 %add_bitcast_fusion = f32[128]{0:T(128)} fusion(f32[1,128]{1,0:T(1,128)S(1)} %collective-permute-done.12, f32[1,128]{1,0:T(1,128)S(1)} %collective-permute-done.11, f32[1,128]{1,0:T(1,128)S(1)} %get-tuple-element.37, f32[1,128]{1,0:T(1,128)S(1)} %collective-permute-done.10), kind=kLoop, calls=%fused_computation | loop fusion | flops 384 | bytes 2560 | tf_op jit(solution)/shard_map/reshape | solution.py:306
Async XLA Ops:
  0.0 22.9 %collective-permute-start.9 = (bf16[128,3072]{1,0:T(8,128)(2,1)}, bf16[128,3072]{1,0:T(8,128)(2,1)S(1)}, u32[]{:S(2)}, u32[]{:S(2)}) collective-permute-start(bf16[128,3072]{1,0:T(8,128)(2,1)} %refs_4_.1), channel_id=1, source_target_pairs={{0,2},{2,0},{1,3},{3,1},{4,6},{6,4},{5,7},{7,5},{8,10},{10,8},{9,1... | collective-permute-start | bytes 2359304 | tf_op jit(solution)/shard_map/item_rows/ppermute | solution.py:181
  2.9 6.8 %collective-permute-start = (s32[8]{0:T(128)}, s32[8]{0:T(128)S(1)}, u32[]{:S(2)}, u32[]{:S(2)}) collective-permute-start(s32[8]{0:T(128)} %param.7), channel_id=1, source_target_pairs={{0,12},{4,0},{8,4},{12,8},{1,13},{5,1},{9,5},{13,9},{2,14},{6,2},{... | collective-permute-start | bytes 104 | tf_op jit(solution)/shard_map/ids/ppermute | solution.py:181
  6.5 4.6 %collective-permute-start.1 = (s32[8]{0:T(128)}, s32[8]{0:T(128)S(1)}, u32[]{:S(2)}, u32[]{:S(2)}) collective-permute-start(s32[8]{0:T(128)} %param.7), channel_id=1, source_target_pairs={{0,8},{4,12},{8,0},{12,4},{1,9},{5,13},{9,1},{13,5},{2,10},{6,14},... | collective-permute-start | bytes 104 | tf_op jit(solution)/shard_map/ids/ppermute | solution.py:181
  6.5 5.5 %collective-permute-start.2 = (s32[8]{0:T(128)}, s32[8]{0:T(128)S(1)}, u32[]{:S(2)}, u32[]{:S(2)}) collective-permute-start(s32[8]{0:T(128)} %param.7), channel_id=1, source_target_pairs={{0,4},{4,8},{8,12},{12,0},{1,5},{5,9},{9,13},{13,1},{2,6},{6,10},{... | collective-permute-start | bytes 104 | tf_op jit(solution)/shard_map/ids/ppermute | solution.py:181
  12.4 7.3 %collective-permute-start.4 = (bf16[16,3200]{1,0:T(8,128)(2,1)S(1)}, bf16[16,3200]{1,0:T(8,128)(2,1)S(1)}, u32[]{:S(2)}, u32[]{:S(2)}) collective-permute-start(bf16[16,3200]{1,0:T(8,128)(2,1)S(1)} %states.1.refs_8_.refs_0_), channel_id=1, source_target_pairs={{0,12},{4,0},{8,4},{12,8},{1,13},{5,1},{9,5},{13,9},{2,14},{6,2},{... | collective-permute-start | bytes 307208 | tf_op jit(solution)/shard_map/states/ppermute | solution.py:181
  13.1 9.9 %collective-permute-start.6 = (bf16[16,3200]{1,0:T(8,128)(2,1)S(1)}, bf16[16,3200]{1,0:T(8,128)(2,1)S(1)}, u32[]{:S(2)}, u32[]{:S(2)}) collective-permute-start(bf16[16,3200]{1,0:T(8,128)(2,1)S(1)} %states.1.refs_8_.refs_0_), channel_id=1, source_target_pairs={{0,8},{4,12},{8,0},{12,4},{1,9},{5,13},{9,1},{13,5},{2,10},{6,14},... | collective-permute-start | bytes 307208 | tf_op jit(solution)/shard_map/states/ppermute | solution.py:181
  14.2 8.8 %collective-permute-start.8 = (bf16[16,3200]{1,0:T(8,128)(2,1)S(1)}, bf16[16,3200]{1,0:T(8,128)(2,1)S(1)}, u32[]{:S(2)}, u32[]{:S(2)}) collective-permute-start(bf16[16,3200]{1,0:T(8,128)(2,1)S(1)} %states.1.refs_8_.refs_0_), channel_id=1, source_target_pairs={{0,4},{4,8},{8,12},{12,0},{1,5},{5,9},{9,13},{13,1},{2,6},{6,10},{... | collective-permute-start | bytes 307208 | tf_op jit(solution)/shard_map/states/ppermute | solution.py:181
  15.6 7.3 %copy-start = (bf16[128,3072]{1,0:T(8,128)(2,1)S(1)}, bf16[128,3072]{1,0:T(8,128)(2,1)}, u32[]{:S(2)}) copy-start(bf16[128,3072]{1,0:T(8,128)(2,1)} %refs_4_.1) | copy-start | bytes 2359300
  19.1 4.7 %collective-permute-start.3 = (f32[1,128]{1,0:T(1,128)S(1)}, f32[1,128]{1,0:T(1,128)S(1)}, u32[]{:S(2)}, u32[]{:S(2)}) collective-permute-start(f32[1,128]{1,0:T(1,128)S(1)} %get-tuple-element.31.refs_1_), channel_id=1, source_target_pairs={{0,2},{1,3},{2,0},{3,1},{4,6},{5,7},{6,4},{7,5},{8,10},{9,11},{10,... | collective-permute-start | bytes 1544 | tf_op jit(solution)/shard_map/pairs/ppermute | solution.py:274
  19.7 4.1 %collective-permute-start.5 = (f32[1,128]{1,0:T(1,128)S(1)}, f32[1,128]{1,0:T(1,128)S(1)}, u32[]{:S(2)}, u32[]{:S(2)}) collective-permute-start(f32[1,128]{1,0:T(1,128)S(1)} %get-tuple-element.31.refs_1_), channel_id=1, source_target_pairs={{0,3},{1,2},{2,1},{3,0},{4,7},{5,6},{6,5},{7,4},{8,11},{9,10},{10,... | collective-permute-start | bytes 1544 | tf_op jit(solution)/shard_map/pairs/ppermute | solution.py:274
  22.9 1.1 %collective-permute-start.7 = (f32[1,128]{1,0:T(1,128)S(1)}, f32[1,128]{1,0:T(1,128)S(1)}, u32[]{:S(2)}, u32[]{:S(2)}) collective-permute-start(f32[1,128]{1,0:T(1,128)S(1)} %get-tuple-element.31.refs_1_), channel_id=1, source_target_pairs={{0,1},{1,0},{2,3},{3,2},{4,5},{5,4},{6,7},{7,6},{8,9},{9,8},{10,11... | collective-permute-start | bytes 1544 | tf_op jit(solution)/shard_map/pairs/ppermute | solution.py:274
  24.2 3.6 %collective-permute-start.12 = (f32[1,128]{1,0:T(1,128)S(1)}, f32[1,128]{1,0:T(1,128)S(1)}, u32[]{:S(2)}, u32[]{:S(2)}) collective-permute-start(f32[1,128]{1,0:T(1,128)S(1)} %get-tuple-element.40), channel_id=1, source_target_pairs={{0,12},{4,0},{8,4},{12,8},{1,13},{5,1},{9,5},{13,9},{2,14},{6,2},{... | collective-permute-start | bytes 1544 | tf_op jit(solution)/shard_map/back/ppermute | solution.py:181
  25.7 4.4 %collective-permute-start.11 = (f32[1,128]{1,0:T(1,128)S(1)}, f32[1,128]{1,0:T(1,128)S(1)}, u32[]{:S(2)}, u32[]{:S(2)}) collective-permute-start(f32[1,128]{1,0:T(1,128)S(1)} %get-tuple-element.39), channel_id=1, source_target_pairs={{0,8},{4,12},{8,0},{12,4},{1,9},{5,13},{9,1},{13,5},{2,10},{6,14},... | collective-permute-start | bytes 1544 | tf_op jit(solution)/shard_map/back/ppermute | solution.py:181
  27.1 5.3 %collective-permute-start.10 = (f32[1,128]{1,0:T(1,128)S(1)}, f32[1,128]{1,0:T(1,128)S(1)}, u32[]{:S(2)}, u32[]{:S(2)}) collective-permute-start(f32[1,128]{1,0:T(1,128)S(1)} %get-tuple-element.38), channel_id=1, source_target_pairs={{0,4},{4,8},{8,12},{12,0},{1,5},{5,9},{9,13},{13,1},{2,6},{6,10},{... | collective-permute-start | bytes 1544 | tf_op jit(solution)/shard_map/back/ppermute | solution.py:181

commit v30 on v26

--- a/solution.py
+++ b/solution.py
@@ -301,7 +301,7 @@
 
     with jax.named_scope("back"):
         result = outs[0]
-        for j in sorted(range(1, total), key=lambda step: step == total // 2):
+        for j in sorted(range(1, total), key=lambda step: (step > total // 2, -step)):
             result = result + shift(outs[j], "shard", -j)
     return result.reshape(half)
 

time: 31.2 us -> 31.3 us (level)
  waiting for transfers between devices: 3.71 us -> 5.64 us
  starting transfers between devices: 19.6 us -> 17.8 us
    ppermute x10, waiting for transfers between devices: 3.47 us -> 5.4 us  [shift(): return lax.ppermute(x, axis, [(s, (s + step) % size) for s in range(size)])]
    ppermute x10, starting transfers between devices: 19 us -> 17.2 us  [shift(): return lax.ppermute(x, axis, [(s, (s + step) % size) for s in range(size)])]
  transfers between devices with their start and end apart: 13 -> 13, of which waited for: 4 -> 6; matrix products, arithmetic and copies ran while one was open for 0% -> 0% of each run, Pallas kernels for 23% -> 22%
where the time goes in v30:
time: 31.3 us; the launch traced here: 31.2 us
  starting transfers between devices  17.8 us (57%)
  Pallas kernels  7.14 us (23%)
  waiting for transfers between devices  5.64 us (18%)
  other arithmetic  0.52 us (2%)
    ppermute x10, starting transfers between devices, shift(): return lax.ppermute(x, axis, [(s, (s + step) % size) for s in range(size)])  17.2 us
    ppermute x10, waiting for transfers between devices, shift(): return lax.ppermute(x, axis, [(s, (s + step) % size) for s in range(size)])  5.4 us
    pallas_call x1, Pallas kernels, body(): pl.pallas_call(functools.partial(pair_kernel, total, cap, slots, user_sta...  3.48 us
    pallas_call x1, Pallas kernels, body(): pl.pallas_call(turn_kernel, out_shape=(jax.ShapeDtypeStruct((width, rows)...  2.2 us
    pallas_call x1, Pallas kernels, body(): pl.pallas_call(functools.partial(linear_kernel, total, planes), out_shape...  0.9 us
  transfers between devices with their start and end apart: 13, of which 6 were waited for; matrix products, arithmetic and copies ran while one was open for 0% of the time, Pallas kernels for 22%

profile of v30, /device:TPU:0, one launch (start us, length us, event | category | flops | bytes accessed | tf_op | source)
XLA Modules:
  0.0 31.2 jit_solution(12725108226371291482)
XLA Ops:
  0.0 2.9 %collective-permute-start.9 = (bf16[128,3072]{1,0:T(8,128)(2,1)}, bf16[128,3072]{1,0:T(8,128)(2,1)S(1)}, u32[]{:S(2)}, u32[]{:S(2)}) collective-permute-start(bf16[128,3072]{1,0:T(8,128)(2,1)} %refs_4_.1), channel_id=1, source_target_pairs={{0,2},{2,0},{1,3},{3,1},{4,6},{6,4},{5,7},{7,5},{8,10},{10,8},{9,1... | collective-permute-start | bytes 2359304 | tf_op jit(solution)/shard_map/item_rows/ppermute | solution.py:181
  2.9 1.6 %collective-permute-start = (s32[8]{0:T(128)}, s32[8]{0:T(128)S(1)}, u32[]{:S(2)}, u32[]{:S(2)}) collective-permute-start(s32[8]{0:T(128)} %param.7), channel_id=1, source_target_pairs={{0,4},{4,8},{8,12},{12,0},{1,5},{5,9},{9,13},{13,1},{2,6},{6,10},{... | collective-permute-start | bytes 104 | tf_op jit(solution)/shard_map/ids/ppermute | solution.py:181
  4.5 2.6 %collective-permute-start.1 = (s32[8]{0:T(128)}, s32[8]{0:T(128)S(1)}, u32[]{:S(2)}, u32[]{:S(2)}) collective-permute-start(s32[8]{0:T(128)} %param.7), channel_id=1, source_target_pairs={{0,8},{4,12},{8,0},{12,4},{1,9},{5,13},{9,1},{13,5},{2,10},{6,14},... | collective-permute-start | bytes 104 | tf_op jit(solution)/shard_map/ids/ppermute | solution.py:181
  7.1 1.3 %collective-permute-start.2 = (s32[8]{0:T(128)}, s32[8]{0:T(128)S(1)}, u32[]{:S(2)}, u32[]{:S(2)}) collective-permute-start(s32[8]{0:T(128)} %param.7), channel_id=1, source_target_pairs={{0,12},{4,0},{8,4},{12,8},{1,13},{5,1},{9,5},{13,9},{2,14},{6,2},{... | collective-permute-start | bytes 104 | tf_op jit(solution)/shard_map/ids/ppermute | solution.py:181
  8.5 2.2 %turn.1 = (f32[3072,128]{1,0:T(8,128)S(1)}, bf16[3072,128]{1,0:T(8,128)(2,1)S(1)}, bf16[64,64,256]{2,1,0:T(8,128)(2,1)S(1)}, bf16[128,3072]{1,0:T(8,128)(2,1)S(1...) custom-call(bf16[128,3072]{1,0:T(8,128)(2,1)} %refs_4_.1, bf16[64,64,256]{2,1,0:T(8,128)(2,1)} %bitcast.15, ...), custom_call_target="tpu_custom_call" | custom-call | flops 1610612736 | bytes 8388608 | tf_op jit(solution)/shard_map/turn/pallas_call | solution.py:209
  10.7 0.0 collective-permute-done
  10.7 0.0 collective-permute-done.1
  10.7 0.1 collective-permute-done.2
  10.8 0.4 %states.1.refs_8_.refs_0_ = bf16[16,3200]{1,0:T(8,128)(2,1)S(1)} custom-call(s32[1,8]{1,0:T(1,128)S(1)} %get-tuple-element.23.refs_0_, s32[1,8]{1,0:T(1,128)S(1)} %bitcast.9, s32[1,8]{1,0:T(1,128)S(1)} %bitcast.11, s32[1,8]{1,0:T(1,128)S(1)} %bitcast.13, bf16[16,128]{1,0:T(8,128)(2,1)S(1)} %get-tuple-element.27.refs_4_, ...), custom_call_target="tpu_custom_call" | custom-call | flops 12582912 | bytes 1048576 | tf_op jit(solution)/shard_map/states/pallas_call | solution.py:238
  11.2 0.6 %collective-permute-start.4 = (bf16[16,3200]{1,0:T(8,128)(2,1)S(1)}, bf16[16,3200]{1,0:T(8,128)(2,1)S(1)}, u32[]{:S(2)}, u32[]{:S(2)}) collective-permute-start(bf16[16,3200]{1,0:T(8,128)(2,1)S(1)} %states.1.refs_8_.refs_0_), channel_id=1, source_target_pairs={{0,4},{4,8},{8,12},{12,0},{1,5},{5,9},{9,13},{13,1},{2,6},{6,10},{... | collective-permute-start | bytes 307208 | tf_op jit(solution)/shard_map/states/ppermute | solution.py:181
  11.8 3.1 %collective-permute-start.6 = (bf16[16,3200]{1,0:T(8,128)(2,1)S(1)}, bf16[16,3200]{1,0:T(8,128)(2,1)S(1)}, u32[]{:S(2)}, u32[]{:S(2)}) collective-permute-start(bf16[16,3200]{1,0:T(8,128)(2,1)S(1)} %states.1.refs_8_.refs_0_), channel_id=1, source_target_pairs={{0,8},{4,12},{8,0},{12,4},{1,9},{5,13},{9,1},{13,5},{2,10},{6,14},... | collective-permute-start | bytes 307208 | tf_op jit(solution)/shard_map/states/ppermute | solution.py:181
  14.9 0.1 collective-permute-start.8
  15.1 0.0 copy-start
  15.1 3.5 %pairs.1 = (f32[1,128]{1,0:T(1,128)S(1)}, s32[4,128]{1,0:T(4,128)S(1)}) custom-call(s32[1,8]{1,0:T(1,128)S(1)} %get-tuple-element.23.refs_0_, s32[1,8]{1,0:T(1,128)S(1)} %bitcast.10, s32[1,8]{1,0:T(1,128)S(1)} %bitcast.12, s32[1,8]{1,0:T(1,128)S(1)} %bitcast.14, s32[2,256]{1,0:T(2,128)} %bitcast.16, f32[3072,128]{1,0:T(8,128)S(1)} %get-tuple-element.24.refs_5_, ...), custom_call_target="tpu_custom_call" | custom-call | flops 4294967296 | bytes 4194304 | tf_op jit(solution)/shard_map/pairs/pallas_call | solution.py:249
  18.5 0.6 %collective-permute-start.3 = (f32[1,128]{1,0:T(1,128)S(1)}, f32[1,128]{1,0:T(1,128)S(1)}, u32[]{:S(2)}, u32[]{:S(2)}) collective-permute-start(f32[1,128]{1,0:T(1,128)S(1)} %get-tuple-element.31.refs_1_), channel_id=1, source_target_pairs={{0,2},{1,3},{2,0},{3,1},{4,6},{5,7},{6,4},{7,5},{8,10},{9,11},{10,... | collective-permute-start | bytes 1544 | tf_op jit(solution)/shard_map/pairs/ppermute | solution.py:274
  19.1 0.0 collective-permute-done.4.refs_1_
  19.1 0.0 collective-permute-start.5
  19.2 1.8 %collective-permute-done.6.refs_2_ = bf16[16,3200]{1,0:T(8,128)(2,1)S(1)} collective-permute-done((bf16[16,3200]{1,0:T(8,128)(2,1)S(1)}, bf16[16,3200]{1,0:T(8,128)(2,1)S(1)}, u32[]{:S(2)}, u32[]{:S(2)}) %collective-permute-start.6) | collective-permute-done | bytes 102432 | tf_op jit(solution)/shard_map/states/ppermute | solution.py:181
  21.0 0.0 collective-permute-start.7
  21.0 0.0 collective-permute-done.8.refs_3_
  21.0 0.0 collective-permute-done.9.refs_5_
  21.0 0.0 copy-done
  21.0 0.9 %scores.2 = (f32[4,128]{1,0:T(4,128)S(1)}, bf16[256,512]{1,0:T(8,128)(2,1)S(1)}) custom-call(bf16[16,3200]{1,0:T(8,128)(2,1)S(1)} %states.1.refs_8_.refs_0_, bf16[16,3200]{1,0:T(8,128)(2,1)S(1)} %collective-permute-done.4.refs_1_, bf16[16,3200]{1,0:T(8,128)(2,1)S(1)} %collective-permute-done.6.refs_2_, bf16[16,3200]{1,0:T(8,128)(2,1)S(1)} %collective-permute-done.8.refs_3_, ...), custom_call_target="tpu_custom_call" | custom-call | flops 100663296 | bytes 2097152 | tf_op jit(solution)/shard_map/scores/pallas_call | solution.py:278
  21.9 0.2 collective-permute-done.3.refs_0_
  22.2 0.0 collective-permute-done.5.refs_2_
  22.2 0.0 collective-permute-done.7.refs_3_
  22.2 0.2 scores.3
  22.3 2.0 %collective-permute-start.12 = (f32[1,128]{1,0:T(1,128)S(1)}, f32[1,128]{1,0:T(1,128)S(1)}, u32[]{:S(2)}, u32[]{:S(2)}) collective-permute-start(f32[1,128]{1,0:T(1,128)S(1)} %get-tuple-element.40), channel_id=1, source_target_pairs={{0,4},{4,8},{8,12},{12,0},{1,5},{5,9},{9,13},{13,1},{2,6},{6,10},{... | collective-permute-start | bytes 1544 | tf_op jit(solution)/shard_map/back/ppermute | solution.py:181
  24.3 1.9 %collective-permute-start.11 = (f32[1,128]{1,0:T(1,128)S(1)}, f32[1,128]{1,0:T(1,128)S(1)}, u32[]{:S(2)}, u32[]{:S(2)}) collective-permute-start(f32[1,128]{1,0:T(1,128)S(1)} %get-tuple-element.39), channel_id=1, source_target_pairs={{0,12},{4,0},{8,4},{12,8},{1,13},{5,1},{9,5},{13,9},{2,14},{6,2},{... | collective-permute-start | bytes 1544 | tf_op jit(solution)/shard_map/back/ppermute | solution.py:181
  26.2 1.0 %collective-permute-start.10 = (f32[1,128]{1,0:T(1,128)S(1)}, f32[1,128]{1,0:T(1,128)S(1)}, u32[]{:S(2)}, u32[]{:S(2)}) collective-permute-start(f32[1,128]{1,0:T(1,128)S(1)} %get-tuple-element.38), channel_id=1, source_target_pairs={{0,8},{4,12},{8,0},{12,4},{1,9},{5,13},{9,1},{13,5},{2,10},{6,14},... | collective-permute-start | bytes 1544 | tf_op jit(solution)/shard_map/back/ppermute | solution.py:181
  27.2 0.5 %collective-permute-done.12 = f32[1,128]{1,0:T(1,128)S(1)} collective-permute-done((f32[1,128]{1,0:T(1,128)S(1)}, f32[1,128]{1,0:T(1,128)S(1)}, u32[]{:S(2)}, u32[]{:S(2)}) %collective-permute-start.12) | collective-permute-done | bytes 544 | tf_op jit(solution)/shard_map/back/ppermute | solution.py:181
  27.7 0.1 collective-permute-done.11
  27.8 2.8 %collective-permute-done.10 = f32[1,128]{1,0:T(1,128)S(1)} collective-permute-done((f32[1,128]{1,0:T(1,128)S(1)}, f32[1,128]{1,0:T(1,128)S(1)}, u32[]{:S(2)}, u32[]{:S(2)}) %collective-permute-start.10) | collective-permute-done | bytes 544 | tf_op jit(solution)/shard_map/back/ppermute | solution.py:181
  30.6 0.5 %add_bitcast_fusion = f32[128]{0:T(128)} fusion(f32[1,128]{1,0:T(1,128)S(1)} %collective-permute-done.12, f32[1,128]{1,0:T(1,128)S(1)} %collective-permute-done.11, f32[1,128]{1,0:T(1,128)S(1)} %get-tuple-element.37, f32[1,128]{1,0:T(1,128)S(1)} %collective-permute-done.10), kind=kLoop, calls=%fused_computation | loop fusion | flops 384 | bytes 2560 | tf_op jit(solution)/shard_map/reshape | solution.py:306
Async XLA Ops:
  0.0 21.0 %collective-permute-start.9 = (bf16[128,3072]{1,0:T(8,128)(2,1)}, bf16[128,3072]{1,0:T(8,128)(2,1)S(1)}, u32[]{:S(2)}, u32[]{:S(2)}) collective-permute-start(bf16[128,3072]{1,0:T(8,128)(2,1)} %refs_4_.1), channel_id=1, source_target_pairs={{0,2},{2,0},{1,3},{3,1},{4,6},{6,4},{5,7},{7,5},{8,10},{10,8},{9,1... | collective-permute-start | bytes 2359304 | tf_op jit(solution)/shard_map/item_rows/ppermute | solution.py:181
  2.9 7.7 %collective-permute-start = (s32[8]{0:T(128)}, s32[8]{0:T(128)S(1)}, u32[]{:S(2)}, u32[]{:S(2)}) collective-permute-start(s32[8]{0:T(128)} %param.7), channel_id=1, source_target_pairs={{0,4},{4,8},{8,12},{12,0},{1,5},{5,9},{9,13},{13,1},{2,6},{6,10},{... | collective-permute-start | bytes 104 | tf_op jit(solution)/shard_map/ids/ppermute | solution.py:181
  4.5 6.2 %collective-permute-start.1 = (s32[8]{0:T(128)}, s32[8]{0:T(128)S(1)}, u32[]{:S(2)}, u32[]{:S(2)}) collective-permute-start(s32[8]{0:T(128)} %param.7), channel_id=1, source_target_pairs={{0,8},{4,12},{8,0},{12,4},{1,9},{5,13},{9,1},{13,5},{2,10},{6,14},... | collective-permute-start | bytes 104 | tf_op jit(solution)/shard_map/ids/ppermute | solution.py:181
  7.1 3.7 %collective-permute-start.2 = (s32[8]{0:T(128)}, s32[8]{0:T(128)S(1)}, u32[]{:S(2)}, u32[]{:S(2)}) collective-permute-start(s32[8]{0:T(128)} %param.7), channel_id=1, source_target_pairs={{0,12},{4,0},{8,4},{12,8},{1,13},{5,1},{9,5},{13,9},{2,14},{6,2},{... | collective-permute-start | bytes 104 | tf_op jit(solution)/shard_map/ids/ppermute | solution.py:181
  11.2 8.0 %collective-permute-start.4 = (bf16[16,3200]{1,0:T(8,128)(2,1)S(1)}, bf16[16,3200]{1,0:T(8,128)(2,1)S(1)}, u32[]{:S(2)}, u32[]{:S(2)}) collective-permute-start(bf16[16,3200]{1,0:T(8,128)(2,1)S(1)} %states.1.refs_8_.refs_0_), channel_id=1, source_target_pairs={{0,4},{4,8},{8,12},{12,0},{1,5},{5,9},{9,13},{13,1},{2,6},{6,10},{... | collective-permute-start | bytes 307208 | tf_op jit(solution)/shard_map/states/ppermute | solution.py:181
  11.8 9.2 %collective-permute-start.6 = (bf16[16,3200]{1,0:T(8,128)(2,1)S(1)}, bf16[16,3200]{1,0:T(8,128)(2,1)S(1)}, u32[]{:S(2)}, u32[]{:S(2)}) collective-permute-start(bf16[16,3200]{1,0:T(8,128)(2,1)S(1)} %states.1.refs_8_.refs_0_), channel_id=1, source_target_pairs={{0,8},{4,12},{8,0},{12,4},{1,9},{5,13},{9,1},{13,5},{2,10},{6,14},... | collective-permute-start | bytes 307208 | tf_op jit(solution)/shard_map/states/ppermute | solution.py:181
  14.9 6.1 %collective-permute-start.8 = (bf16[16,3200]{1,0:T(8,128)(2,1)S(1)}, bf16[16,3200]{1,0:T(8,128)(2,1)S(1)}, u32[]{:S(2)}, u32[]{:S(2)}) collective-permute-start(bf16[16,3200]{1,0:T(8,128)(2,1)S(1)} %states.1.refs_8_.refs_0_), channel_id=1, source_target_pairs={{0,12},{4,0},{8,4},{12,8},{1,13},{5,1},{9,5},{13,9},{2,14},{6,2},{... | collective-permute-start | bytes 307208 | tf_op jit(solution)/shard_map/states/ppermute | solution.py:181
  15.1 6.0 %copy-start = (bf16[128,3072]{1,0:T(8,128)(2,1)S(1)}, bf16[128,3072]{1,0:T(8,128)(2,1)}, u32[]{:S(2)}) copy-start(bf16[128,3072]{1,0:T(8,128)(2,1)} %refs_4_.1) | copy-start | bytes 2359300
  18.5 3.6 %collective-permute-start.3 = (f32[1,128]{1,0:T(1,128)S(1)}, f32[1,128]{1,0:T(1,128)S(1)}, u32[]{:S(2)}, u32[]{:S(2)}) collective-permute-start(f32[1,128]{1,0:T(1,128)S(1)} %get-tuple-element.31.refs_1_), channel_id=1, source_target_pairs={{0,2},{1,3},{2,0},{3,1},{4,6},{5,7},{6,4},{7,5},{8,10},{9,11},{10,... | collective-permute-start | bytes 1544 | tf_op jit(solution)/shard_map/pairs/ppermute | solution.py:274
  19.1 3.0 %collective-permute-start.5 = (f32[1,128]{1,0:T(1,128)S(1)}, f32[1,128]{1,0:T(1,128)S(1)}, u32[]{:S(2)}, u32[]{:S(2)}) collective-permute-start(f32[1,128]{1,0:T(1,128)S(1)} %get-tuple-element.31.refs_1_), channel_id=1, source_target_pairs={{0,3},{1,2},{2,1},{3,0},{4,7},{5,6},{6,5},{7,4},{8,11},{9,10},{10,... | collective-permute-start | bytes 1544 | tf_op jit(solution)/shard_map/pairs/ppermute | solution.py:274
  21.0 1.2 %collective-permute-start.7 = (f32[1,128]{1,0:T(1,128)S(1)}, f32[1,128]{1,0:T(1,128)S(1)}, u32[]{:S(2)}, u32[]{:S(2)}) collective-permute-start(f32[1,128]{1,0:T(1,128)S(1)} %get-tuple-element.31.refs_1_), channel_id=1, source_target_pairs={{0,1},{1,0},{2,3},{3,2},{4,5},{5,4},{6,7},{7,6},{8,9},{9,8},{10,11... | collective-permute-start | bytes 1544 | tf_op jit(solution)/shard_map/pairs/ppermute | solution.py:274
  22.3 5.4 %collective-permute-start.12 = (f32[1,128]{1,0:T(1,128)S(1)}, f32[1,128]{1,0:T(1,128)S(1)}, u32[]{:S(2)}, u32[]{:S(2)}) collective-permute-start(f32[1,128]{1,0:T(1,128)S(1)} %get-tuple-element.40), channel_id=1, source_target_pairs={{0,4},{4,8},{8,12},{12,0},{1,5},{5,9},{9,13},{13,1},{2,6},{6,10},{... | collective-permute-start | bytes 1544 | tf_op jit(solution)/shard_map/back/ppermute | solution.py:181
  24.3 3.5 %collective-permute-start.11 = (f32[1,128]{1,0:T(1,128)S(1)}, f32[1,128]{1,0:T(1,128)S(1)}, u32[]{:S(2)}, u32[]{:S(2)}) collective-permute-start(f32[1,128]{1,0:T(1,128)S(1)} %get-tuple-element.39), channel_id=1, source_target_pairs={{0,12},{4,0},{8,4},{12,8},{1,13},{5,1},{9,5},{13,9},{2,14},{6,2},{... | collective-permute-start | bytes 1544 | tf_op jit(solution)/shard_map/back/ppermute | solution.py:181
  26.2 4.4 %collective-permute-start.10 = (f32[1,128]{1,0:T(1,128)S(1)}, f32[1,128]{1,0:T(1,128)S(1)}, u32[]{:S(2)}, u32[]{:S(2)}) collective-permute-start(f32[1,128]{1,0:T(1,128)S(1)} %get-tuple-element.38), channel_id=1, source_target_pairs={{0,8},{4,12},{8,0},{12,4},{1,9},{5,13},{9,1},{13,5},{2,10},{6,14},... | collective-permute-start | bytes 1544 | tf_op jit(solution)/shard_map/back/ppermute | solution.py:181

commit v31 on v23

--- a/solution.py
+++ b/solution.py
@@ -120,7 +120,7 @@
         )
         return total + dot(left, right, NN) * jnp.concatenate([rows32[pl.ds(a, K), :] for a, _ in fields_of], axis=1)
 
-    sums = lax.fori_loop(0, steps, two, jnp.zeros((K, 2 * items), jnp.float32), unroll=32)
+    sums = lax.fori_loop(0, steps, two, jnp.zeros((K, 2 * items), jnp.float32), unroll=64)
     line = jnp.sum(sums, axis=0, keepdims=True)
     out[...] = line[:, :items] + line[:, items:]
 

time: 30.5 us -> 30.5 us (level)
  transfers between devices with their start and end apart: 13 -> 13, of which waited for: 5 -> 5; matrix products, arithmetic and copies ran while one was open for 0% -> 0% of each run, Pallas kernels for 23% -> 22%
where the time goes in v31:
time: 30.5 us; the launch traced here: 30.3 us
  starting transfers between devices  18.7 us (61%)
  Pallas kernels  6.89 us (23%)
  waiting for transfers between devices  4.09 us (13%)
  other arithmetic  0.52 us (2%)
    ppermute x10, starting transfers between devices, shift(): return lax.ppermute(x, axis, [(s, (s + step) % size) for s in range(size)])  18.1 us
    ppermute x10, waiting for transfers between devices, shift(): return lax.ppermute(x, axis, [(s, (s + step) % size) for s in range(size)])  3.9 us
    pallas_call x1, Pallas kernels, body(): pl.pallas_call(functools.partial(pair_kernel, total, cap, slots, user_sta...  3.23 us
    pallas_call x1, Pallas kernels, body(): pl.pallas_call(turn_kernel, out_shape=(jax.ShapeDtypeStruct((width, rows)...  2.2 us
    pallas_call x1, Pallas kernels, body(): pl.pallas_call(functools.partial(linear_kernel, total, planes), out_shape...  0.9 us
  transfers between devices with their start and end apart: 13, of which 5 were waited for; matrix products, arithmetic and copies ran while one was open for 0% of the time, Pallas kernels for 22%

profile of v31, /device:TPU:0, one launch (start us, length us, event | category | flops | bytes accessed | tf_op | source)
XLA Modules:
  0.0 30.3 jit_solution(11370661374078250429)
XLA Ops:
  0.0 2.9 %collective-permute-start.9 = (bf16[128,3072]{1,0:T(8,128)(2,1)}, bf16[128,3072]{1,0:T(8,128)(2,1)S(1)}, u32[]{:S(2)}, u32[]{:S(2)}) collective-permute-start(bf16[128,3072]{1,0:T(8,128)(2,1)} %refs_4_.1), channel_id=1, source_target_pairs={{0,2},{2,0},{1,3},{3,1},{4,6},{6,4},{5,7},{7,5},{8,10},{10,8},{9,1... | collective-permute-start | bytes 2359304 | tf_op jit(solution)/shard_map/item_rows/ppermute | solution.py:181
  2.9 1.6 %collective-permute-start = (s32[8]{0:T(128)}, s32[8]{0:T(128)S(1)}, u32[]{:S(2)}, u32[]{:S(2)}) collective-permute-start(s32[8]{0:T(128)} %param.7), channel_id=1, source_target_pairs={{0,4},{4,8},{8,12},{12,0},{1,5},{5,9},{9,13},{13,1},{2,6},{6,10},{... | collective-permute-start | bytes 104 | tf_op jit(solution)/shard_map/ids/ppermute | solution.py:181
  4.5 2.6 %collective-permute-start.1 = (s32[8]{0:T(128)}, s32[8]{0:T(128)S(1)}, u32[]{:S(2)}, u32[]{:S(2)}) collective-permute-start(s32[8]{0:T(128)} %param.7), channel_id=1, source_target_pairs={{0,8},{4,12},{8,0},{12,4},{1,9},{5,13},{9,1},{13,5},{2,10},{6,14},... | collective-permute-start | bytes 104 | tf_op jit(solution)/shard_map/ids/ppermute | solution.py:181
  7.1 1.3 %collective-permute-start.2 = (s32[8]{0:T(128)}, s32[8]{0:T(128)S(1)}, u32[]{:S(2)}, u32[]{:S(2)}) collective-permute-start(s32[8]{0:T(128)} %param.7), channel_id=1, source_target_pairs={{0,12},{4,0},{8,4},{12,8},{1,13},{5,1},{9,5},{13,9},{2,14},{6,2},{... | collective-permute-start | bytes 104 | tf_op jit(solution)/shard_map/ids/ppermute | solution.py:181
  8.5 2.2 %turn.1 = (f32[3072,128]{1,0:T(8,128)S(1)}, bf16[3072,128]{1,0:T(8,128)(2,1)S(1)}, bf16[64,64,256]{2,1,0:T(8,128)(2,1)S(1)}, bf16[128,3072]{1,0:T(8,128)(2,1)S(1...) custom-call(bf16[128,3072]{1,0:T(8,128)(2,1)} %refs_4_.1, bf16[64,64,256]{2,1,0:T(8,128)(2,1)} %bitcast.15, ...), custom_call_target="tpu_custom_call" | custom-call | flops 1610612736 | bytes 8388608 | tf_op jit(solution)/shard_map/turn/pallas_call | solution.py:209
  10.7 0.0 collective-permute-done
  10.7 0.0 collective-permute-done.1
  10.7 0.1 collective-permute-done.2
  10.8 0.4 %states.1.refs_8_.refs_0_ = bf16[16,3200]{1,0:T(8,128)(2,1)S(1)} custom-call(s32[1,8]{1,0:T(1,128)S(1)} %get-tuple-element.23.refs_0_, s32[1,8]{1,0:T(1,128)S(1)} %bitcast.9, s32[1,8]{1,0:T(1,128)S(1)} %bitcast.11, s32[1,8]{1,0:T(1,128)S(1)} %bitcast.13, bf16[16,128]{1,0:T(8,128)(2,1)S(1)} %get-tuple-element.27.refs_4_, ...), custom_call_target="tpu_custom_call" | custom-call | flops 12582912 | bytes 1048576 | tf_op jit(solution)/shard_map/states/pallas_call | solution.py:238
  11.2 0.6 %collective-permute-start.4 = (bf16[16,3200]{1,0:T(8,128)(2,1)S(1)}, bf16[16,3200]{1,0:T(8,128)(2,1)S(1)}, u32[]{:S(2)}, u32[]{:S(2)}) collective-permute-start(bf16[16,3200]{1,0:T(8,128)(2,1)S(1)} %states.1.refs_8_.refs_0_), channel_id=1, source_target_pairs={{0,4},{4,8},{8,12},{12,0},{1,5},{5,9},{9,13},{13,1},{2,6},{6,10},{... | collective-permute-start | bytes 307208 | tf_op jit(solution)/shard_map/states/ppermute | solution.py:181
  11.8 3.1 %collective-permute-start.6 = (bf16[16,3200]{1,0:T(8,128)(2,1)S(1)}, bf16[16,3200]{1,0:T(8,128)(2,1)S(1)}, u32[]{:S(2)}, u32[]{:S(2)}) collective-permute-start(bf16[16,3200]{1,0:T(8,128)(2,1)S(1)} %states.1.refs_8_.refs_0_), channel_id=1, source_target_pairs={{0,8},{4,12},{8,0},{12,4},{1,9},{5,13},{9,1},{13,5},{2,10},{6,14},... | collective-permute-start | bytes 307208 | tf_op jit(solution)/shard_map/states/ppermute | solution.py:181
  14.9 0.1 collective-permute-start.8
  15.1 0.0 copy-start
  15.1 3.2 %pairs.1 = (f32[1,128]{1,0:T(1,128)S(1)}, s32[4,128]{1,0:T(4,128)S(1)}) custom-call(s32[1,8]{1,0:T(1,128)S(1)} %get-tuple-element.23.refs_0_, s32[1,8]{1,0:T(1,128)S(1)} %bitcast.10, s32[1,8]{1,0:T(1,128)S(1)} %bitcast.12, s32[1,8]{1,0:T(1,128)S(1)} %bitcast.14, s32[2,256]{1,0:T(2,128)} %bitcast.16, f32[3072,128]{1,0:T(8,128)S(1)} %get-tuple-element.24.refs_5_, ...), custom_call_target="tpu_custom_call" | custom-call | flops 4294967296 | bytes 4194304 | tf_op jit(solution)/shard_map/pairs/pallas_call | solution.py:249
  18.3 0.6 %collective-permute-start.3 = (f32[1,128]{1,0:T(1,128)S(1)}, f32[1,128]{1,0:T(1,128)S(1)}, u32[]{:S(2)}, u32[]{:S(2)}) collective-permute-start(f32[1,128]{1,0:T(1,128)S(1)} %get-tuple-element.31.refs_1_), channel_id=1, source_target_pairs={{0,2},{1,3},{2,0},{3,1},{4,6},{5,7},{6,4},{7,5},{8,10},{9,11},{10,... | collective-permute-start | bytes 1544 | tf_op jit(solution)/shard_map/pairs/ppermute | solution.py:274
  18.9 0.0 collective-permute-done.4.refs_1_
  18.9 0.0 collective-permute-start.5
  18.9 2.1 %collective-permute-done.6.refs_2_ = bf16[16,3200]{1,0:T(8,128)(2,1)S(1)} collective-permute-done((bf16[16,3200]{1,0:T(8,128)(2,1)S(1)}, bf16[16,3200]{1,0:T(8,128)(2,1)S(1)}, u32[]{:S(2)}, u32[]{:S(2)}) %collective-permute-start.6) | collective-permute-done | bytes 102432 | tf_op jit(solution)/shard_map/states/ppermute | solution.py:181
  21.0 0.0 collective-permute-start.7
  21.0 0.0 collective-permute-done.8.refs_3_
  21.0 0.0 collective-permute-done.9.refs_5_
  21.0 0.0 copy-done
  21.0 0.9 %scores.2 = (f32[4,128]{1,0:T(4,128)S(1)}, bf16[256,512]{1,0:T(8,128)(2,1)S(1)}) custom-call(bf16[16,3200]{1,0:T(8,128)(2,1)S(1)} %states.1.refs_8_.refs_0_, bf16[16,3200]{1,0:T(8,128)(2,1)S(1)} %collective-permute-done.4.refs_1_, bf16[16,3200]{1,0:T(8,128)(2,1)S(1)} %collective-permute-done.6.refs_2_, bf16[16,3200]{1,0:T(8,128)(2,1)S(1)} %collective-permute-done.8.refs_3_, ...), custom_call_target="tpu_custom_call" | custom-call | flops 100663296 | bytes 2097152 | tf_op jit(solution)/shard_map/scores/pallas_call | solution.py:278
  21.9 0.0 collective-permute-done.3.refs_0_
  21.9 0.0 collective-permute-done.5.refs_2_
  21.9 0.2 collective-permute-done.7.refs_3_
  22.1 0.2 scores.3
  22.3 1.9 %collective-permute-start.12 = (f32[1,128]{1,0:T(1,128)S(1)}, f32[1,128]{1,0:T(1,128)S(1)}, u32[]{:S(2)}, u32[]{:S(2)}) collective-permute-start(f32[1,128]{1,0:T(1,128)S(1)} %get-tuple-element.40), channel_id=1, source_target_pairs={{0,4},{4,8},{8,12},{12,0},{1,5},{5,9},{9,13},{13,1},{2,6},{6,10},{... | collective-permute-start | bytes 1544 | tf_op jit(solution)/shard_map/back/ppermute | solution.py:181
  24.2 2.0 %collective-permute-start.11 = (f32[1,128]{1,0:T(1,128)S(1)}, f32[1,128]{1,0:T(1,128)S(1)}, u32[]{:S(2)}, u32[]{:S(2)}) collective-permute-start(f32[1,128]{1,0:T(1,128)S(1)} %get-tuple-element.39), channel_id=1, source_target_pairs={{0,8},{4,12},{8,0},{12,4},{1,9},{5,13},{9,1},{13,5},{2,10},{6,14},... | collective-permute-start | bytes 1544 | tf_op jit(solution)/shard_map/back/ppermute | solution.py:181
  26.3 1.8 %collective-permute-start.10 = (f32[1,128]{1,0:T(1,128)S(1)}, f32[1,128]{1,0:T(1,128)S(1)}, u32[]{:S(2)}, u32[]{:S(2)}) collective-permute-start(f32[1,128]{1,0:T(1,128)S(1)} %get-tuple-element.38), channel_id=1, source_target_pairs={{0,12},{4,0},{8,4},{12,8},{1,13},{5,1},{9,5},{13,9},{2,14},{6,2},{... | collective-permute-start | bytes 1544 | tf_op jit(solution)/shard_map/back/ppermute | solution.py:181
  28.1 0.0 collective-permute-done.12
  28.1 0.6 %collective-permute-done.11 = f32[1,128]{1,0:T(1,128)S(1)} collective-permute-done((f32[1,128]{1,0:T(1,128)S(1)}, f32[1,128]{1,0:T(1,128)S(1)}, u32[]{:S(2)}, u32[]{:S(2)}) %collective-permute-start.11) | collective-permute-done | bytes 544 | tf_op jit(solution)/shard_map/back/ppermute | solution.py:181
  28.7 1.1 %collective-permute-done.10 = f32[1,128]{1,0:T(1,128)S(1)} collective-permute-done((f32[1,128]{1,0:T(1,128)S(1)}, f32[1,128]{1,0:T(1,128)S(1)}, u32[]{:S(2)}, u32[]{:S(2)}) %collective-permute-start.10) | collective-permute-done | bytes 544 | tf_op jit(solution)/shard_map/back/ppermute | solution.py:181
  29.8 0.5 %add_bitcast_fusion = f32[128]{0:T(128)} fusion(f32[1,128]{1,0:T(1,128)S(1)} %collective-permute-done.12, f32[1,128]{1,0:T(1,128)S(1)} %collective-permute-done.11, f32[1,128]{1,0:T(1,128)S(1)} %get-tuple-element.37, f32[1,128]{1,0:T(1,128)S(1)} %collective-permute-done.10), kind=kLoop, calls=%fused_computation | loop fusion | flops 384 | bytes 2560 | tf_op jit(solution)/shard_map/reshape | solution.py:306
Async XLA Ops:
  0.0 21.0 %collective-permute-start.9 = (bf16[128,3072]{1,0:T(8,128)(2,1)}, bf16[128,3072]{1,0:T(8,128)(2,1)S(1)}, u32[]{:S(2)}, u32[]{:S(2)}) collective-permute-start(bf16[128,3072]{1,0:T(8,128)(2,1)} %refs_4_.1), channel_id=1, source_target_pairs={{0,2},{2,0},{1,3},{3,1},{4,6},{6,4},{5,7},{7,5},{8,10},{10,8},{9,1... | collective-permute-start | bytes 2359304 | tf_op jit(solution)/shard_map/item_rows/ppermute | solution.py:181
  2.9 7.7 %collective-permute-start = (s32[8]{0:T(128)}, s32[8]{0:T(128)S(1)}, u32[]{:S(2)}, u32[]{:S(2)}) collective-permute-start(s32[8]{0:T(128)} %param.7), channel_id=1, source_target_pairs={{0,4},{4,8},{8,12},{12,0},{1,5},{5,9},{9,13},{13,1},{2,6},{6,10},{... | collective-permute-start | bytes 104 | tf_op jit(solution)/shard_map/ids/ppermute | solution.py:181
  4.5 6.2 %collective-permute-start.1 = (s32[8]{0:T(128)}, s32[8]{0:T(128)S(1)}, u32[]{:S(2)}, u32[]{:S(2)}) collective-permute-start(s32[8]{0:T(128)} %param.7), channel_id=1, source_target_pairs={{0,8},{4,12},{8,0},{12,4},{1,9},{5,13},{9,1},{13,5},{2,10},{6,14},... | collective-permute-start | bytes 104 | tf_op jit(solution)/shard_map/ids/ppermute | solution.py:181
  7.1 3.7 %collective-permute-start.2 = (s32[8]{0:T(128)}, s32[8]{0:T(128)S(1)}, u32[]{:S(2)}, u32[]{:S(2)}) collective-permute-start(s32[8]{0:T(128)} %param.7), channel_id=1, source_target_pairs={{0,12},{4,0},{8,4},{12,8},{1,13},{5,1},{9,5},{13,9},{2,14},{6,2},{... | collective-permute-start | bytes 104 | tf_op jit(solution)/shard_map/ids/ppermute | solution.py:181
  11.2 7.7 %collective-permute-start.4 = (bf16[16,3200]{1,0:T(8,128)(2,1)S(1)}, bf16[16,3200]{1,0:T(8,128)(2,1)S(1)}, u32[]{:S(2)}, u32[]{:S(2)}) collective-permute-start(bf16[16,3200]{1,0:T(8,128)(2,1)S(1)} %states.1.refs_8_.refs_0_), channel_id=1, source_target_pairs={{0,4},{4,8},{8,12},{12,0},{1,5},{5,9},{9,13},{13,1},{2,6},{6,10},{... | collective-permute-start | bytes 307208 | tf_op jit(solution)/shard_map/states/ppermute | solution.py:181
  11.8 9.2 %collective-permute-start.6 = (bf16[16,3200]{1,0:T(8,128)(2,1)S(1)}, bf16[16,3200]{1,0:T(8,128)(2,1)S(1)}, u32[]{:S(2)}, u32[]{:S(2)}) collective-permute-start(bf16[16,3200]{1,0:T(8,128)(2,1)S(1)} %states.1.refs_8_.refs_0_), channel_id=1, source_target_pairs={{0,8},{4,12},{8,0},{12,4},{1,9},{5,13},{9,1},{13,5},{2,10},{6,14},... | collective-permute-start | bytes 307208 | tf_op jit(solution)/shard_map/states/ppermute | solution.py:181
  14.9 6.1 %collective-permute-start.8 = (bf16[16,3200]{1,0:T(8,128)(2,1)S(1)}, bf16[16,3200]{1,0:T(8,128)(2,1)S(1)}, u32[]{:S(2)}, u32[]{:S(2)}) collective-permute-start(bf16[16,3200]{1,0:T(8,128)(2,1)S(1)} %states.1.refs_8_.refs_0_), channel_id=1, source_target_pairs={{0,12},{4,0},{8,4},{12,8},{1,13},{5,1},{9,5},{13,9},{2,14},{6,2},{... | collective-permute-start | bytes 307208 | tf_op jit(solution)/shard_map/states/ppermute | solution.py:181
  15.1 6.0 %copy-start = (bf16[128,3072]{1,0:T(8,128)(2,1)S(1)}, bf16[128,3072]{1,0:T(8,128)(2,1)}, u32[]{:S(2)}) copy-start(bf16[128,3072]{1,0:T(8,128)(2,1)} %refs_4_.1) | copy-start | bytes 2359300
  18.3 3.6 %collective-permute-start.3 = (f32[1,128]{1,0:T(1,128)S(1)}, f32[1,128]{1,0:T(1,128)S(1)}, u32[]{:S(2)}, u32[]{:S(2)}) collective-permute-start(f32[1,128]{1,0:T(1,128)S(1)} %get-tuple-element.31.refs_1_), channel_id=1, source_target_pairs={{0,2},{1,3},{2,0},{3,1},{4,6},{5,7},{6,4},{7,5},{8,10},{9,11},{10,... | collective-permute-start | bytes 1544 | tf_op jit(solution)/shard_map/pairs/ppermute | solution.py:274
  18.9 3.0 %collective-permute-start.5 = (f32[1,128]{1,0:T(1,128)S(1)}, f32[1,128]{1,0:T(1,128)S(1)}, u32[]{:S(2)}, u32[]{:S(2)}) collective-permute-start(f32[1,128]{1,0:T(1,128)S(1)} %get-tuple-element.31.refs_1_), channel_id=1, source_target_pairs={{0,3},{1,2},{2,1},{3,0},{4,7},{5,6},{6,5},{7,4},{8,11},{9,10},{10,... | collective-permute-start | bytes 1544 | tf_op jit(solution)/shard_map/pairs/ppermute | solution.py:274
  21.0 1.1 %collective-permute-start.7 = (f32[1,128]{1,0:T(1,128)S(1)}, f32[1,128]{1,0:T(1,128)S(1)}, u32[]{:S(2)}, u32[]{:S(2)}) collective-permute-start(f32[1,128]{1,0:T(1,128)S(1)} %get-tuple-element.31.refs_1_), channel_id=1, source_target_pairs={{0,1},{1,0},{2,3},{3,2},{4,5},{5,4},{6,7},{7,6},{8,9},{9,8},{10,11... | collective-permute-start | bytes 1544 | tf_op jit(solution)/shard_map/pairs/ppermute | solution.py:274
  22.3 5.8 %collective-permute-start.12 = (f32[1,128]{1,0:T(1,128)S(1)}, f32[1,128]{1,0:T(1,128)S(1)}, u32[]{:S(2)}, u32[]{:S(2)}) collective-permute-start(f32[1,128]{1,0:T(1,128)S(1)} %get-tuple-element.40), channel_id=1, source_target_pairs={{0,4},{4,8},{8,12},{12,0},{1,5},{5,9},{9,13},{13,1},{2,6},{6,10},{... | collective-permute-start | bytes 1544 | tf_op jit(solution)/shard_map/back/ppermute | solution.py:181
  24.2 4.4 %collective-permute-start.11 = (f32[1,128]{1,0:T(1,128)S(1)}, f32[1,128]{1,0:T(1,128)S(1)}, u32[]{:S(2)}, u32[]{:S(2)}) collective-permute-start(f32[1,128]{1,0:T(1,128)S(1)} %get-tuple-element.39), channel_id=1, source_target_pairs={{0,8},{4,12},{8,0},{12,4},{1,9},{5,13},{9,1},{13,5},{2,10},{6,14},... | collective-permute-start | bytes 1544 | tf_op jit(solution)/shard_map/back/ppermute | solution.py:181
  26.3 3.5 %collective-permute-start.10 = (f32[1,128]{1,0:T(1,128)S(1)}, f32[1,128]{1,0:T(1,128)S(1)}, u32[]{:S(2)}, u32[]{:S(2)}) collective-permute-start(f32[1,128]{1,0:T(1,128)S(1)} %get-tuple-element.38), channel_id=1, source_target_pairs={{0,12},{4,0},{8,4},{12,8},{1,13},{5,1},{9,5},{13,9},{2,14},{6,2},{... | collective-permute-start | bytes 1544 | tf_op jit(solution)/shard_map/back/ppermute | solution.py:181

commit v32 on v31

--- a/solution.py
+++ b/solution.py
@@ -301,7 +301,7 @@
 
     with jax.named_scope("back"):
         result = outs[0]
-        for j in range(1, total):
+        for j in sorted(range(1, total), key=lambda step: (step == 1, step)):
             result = result + shift(outs[j], "shard", -j)
     return result.reshape(half)
 

time: 30.5 us -> 31.7 us (1.039)
  waiting for transfers between devices: 4.09 us -> 6.22 us
  starting transfers between devices: 18.7 us -> 17.8 us
    ppermute x10, waiting for transfers between devices: 3.9 us -> 6.04 us  [shift(): return lax.ppermute(x, axis, [(s, (s + step) % size) for s in range(size)])]
    ppermute x10, starting transfers between devices: 18.1 us -> 17.2 us  [shift(): return lax.ppermute(x, axis, [(s, (s + step) % size) for s in range(size)])]
  transfers between devices with their start and end apart: 13 -> 13, of which waited for: 5 -> 4; matrix products, arithmetic and copies ran while one was open for 0% -> 0% of each run, Pallas kernels for 22% -> 21%
where the time goes in v32:
time: 31.7 us; the launch traced here: 31.6 us
  starting transfers between devices  17.8 us (56%)
  Pallas kernels  6.89 us (22%)
  waiting for transfers between devices  6.22 us (20%)
  other arithmetic  0.52 us (2%)
    ppermute x10, starting transfers between devices, shift(): return lax.ppermute(x, axis, [(s, (s + step) % size) for s in range(size)])  17.2 us
    ppermute x10, waiting for transfers between devices, shift(): return lax.ppermute(x, axis, [(s, (s + step) % size) for s in range(size)])  6.04 us
    pallas_call x1, Pallas kernels, body(): pl.pallas_call(functools.partial(pair_kernel, total, cap, slots, user_sta...  3.23 us
    pallas_call x1, Pallas kernels, body(): pl.pallas_call(turn_kernel, out_shape=(jax.ShapeDtypeStruct((width, rows)...  2.2 us
    pallas_call x1, Pallas kernels, body(): pl.pallas_call(functools.partial(linear_kernel, total, planes), out_shape...  0.9 us
  transfers between devices with their start and end apart: 13, of which 4 were waited for; matrix products, arithmetic and copies ran while one was open for 0% of the time, Pallas kernels for 21%

profile of v32, /device:TPU:0, one launch (start us, length us, event | category | flops | bytes accessed | tf_op | source)
XLA Modules:
  0.0 31.6 jit_solution(7601649804859338072)
XLA Ops:
  0.0 2.9 %collective-permute-start.9 = (bf16[128,3072]{1,0:T(8,128)(2,1)}, bf16[128,3072]{1,0:T(8,128)(2,1)S(1)}, u32[]{:S(2)}, u32[]{:S(2)}) collective-permute-start(bf16[128,3072]{1,0:T(8,128)(2,1)} %refs_4_.1), channel_id=1, source_target_pairs={{0,2},{2,0},{1,3},{3,1},{4,6},{6,4},{5,7},{7,5},{8,10},{10,8},{9,1... | collective-permute-start | bytes 2359304 | tf_op jit(solution)/shard_map/item_rows/ppermute | solution.py:181
  2.9 1.6 %collective-permute-start = (s32[8]{0:T(128)}, s32[8]{0:T(128)S(1)}, u32[]{:S(2)}, u32[]{:S(2)}) collective-permute-start(s32[8]{0:T(128)} %param.7), channel_id=1, source_target_pairs={{0,4},{4,8},{8,12},{12,0},{1,5},{5,9},{9,13},{13,1},{2,6},{6,10},{... | collective-permute-start | bytes 104 | tf_op jit(solution)/shard_map/ids/ppermute | solution.py:181
  4.5 2.6 %collective-permute-start.1 = (s32[8]{0:T(128)}, s32[8]{0:T(128)S(1)}, u32[]{:S(2)}, u32[]{:S(2)}) collective-permute-start(s32[8]{0:T(128)} %param.7), channel_id=1, source_target_pairs={{0,8},{4,12},{8,0},{12,4},{1,9},{5,13},{9,1},{13,5},{2,10},{6,14},... | collective-permute-start | bytes 104 | tf_op jit(solution)/shard_map/ids/ppermute | solution.py:181
  7.1 1.3 %collective-permute-start.2 = (s32[8]{0:T(128)}, s32[8]{0:T(128)S(1)}, u32[]{:S(2)}, u32[]{:S(2)}) collective-permute-start(s32[8]{0:T(128)} %param.7), channel_id=1, source_target_pairs={{0,12},{4,0},{8,4},{12,8},{1,13},{5,1},{9,5},{13,9},{2,14},{6,2},{... | collective-permute-start | bytes 104 | tf_op jit(solution)/shard_map/ids/ppermute | solution.py:181
  8.5 2.2 %turn.1 = (f32[3072,128]{1,0:T(8,128)S(1)}, bf16[3072,128]{1,0:T(8,128)(2,1)S(1)}, bf16[64,64,256]{2,1,0:T(8,128)(2,1)S(1)}, bf16[128,3072]{1,0:T(8,128)(2,1)S(1...) custom-call(bf16[128,3072]{1,0:T(8,128)(2,1)} %refs_4_.1, bf16[64,64,256]{2,1,0:T(8,128)(2,1)} %bitcast.15, ...), custom_call_target="tpu_custom_call" | custom-call | flops 1610612736 | bytes 8388608 | tf_op jit(solution)/shard_map/turn/pallas_call | solution.py:209
  10.7 0.0 collective-permute-done
  10.7 0.0 collective-permute-done.1
  10.7 0.1 collective-permute-done.2
  10.8 0.4 %states.1.refs_8_.refs_0_ = bf16[16,3200]{1,0:T(8,128)(2,1)S(1)} custom-call(s32[1,8]{1,0:T(1,128)S(1)} %get-tuple-element.23.refs_0_, s32[1,8]{1,0:T(1,128)S(1)} %bitcast.9, s32[1,8]{1,0:T(1,128)S(1)} %bitcast.11, s32[1,8]{1,0:T(1,128)S(1)} %bitcast.13, bf16[16,128]{1,0:T(8,128)(2,1)S(1)} %get-tuple-element.27.refs_4_, ...), custom_call_target="tpu_custom_call" | custom-call | flops 12582912 | bytes 1048576 | tf_op jit(solution)/shard_map/states/pallas_call | solution.py:238
  11.2 0.6 %collective-permute-start.4 = (bf16[16,3200]{1,0:T(8,128)(2,1)S(1)}, bf16[16,3200]{1,0:T(8,128)(2,1)S(1)}, u32[]{:S(2)}, u32[]{:S(2)}) collective-permute-start(bf16[16,3200]{1,0:T(8,128)(2,1)S(1)} %states.1.refs_8_.refs_0_), channel_id=1, source_target_pairs={{0,4},{4,8},{8,12},{12,0},{1,5},{5,9},{9,13},{13,1},{2,6},{6,10},{... | collective-permute-start | bytes 307208 | tf_op jit(solution)/shard_map/states/ppermute | solution.py:181
  11.8 3.1 %collective-permute-start.6 = (bf16[16,3200]{1,0:T(8,128)(2,1)S(1)}, bf16[16,3200]{1,0:T(8,128)(2,1)S(1)}, u32[]{:S(2)}, u32[]{:S(2)}) collective-permute-start(bf16[16,3200]{1,0:T(8,128)(2,1)S(1)} %states.1.refs_8_.refs_0_), channel_id=1, source_target_pairs={{0,8},{4,12},{8,0},{12,4},{1,9},{5,13},{9,1},{13,5},{2,10},{6,14},... | collective-permute-start | bytes 307208 | tf_op jit(solution)/shard_map/states/ppermute | solution.py:181
  14.9 0.1 collective-permute-start.8
  15.1 0.0 copy-start
  15.1 3.2 %pairs.1 = (f32[1,128]{1,0:T(1,128)S(1)}, s32[4,128]{1,0:T(4,128)S(1)}) custom-call(s32[1,8]{1,0:T(1,128)S(1)} %get-tuple-element.23.refs_0_, s32[1,8]{1,0:T(1,128)S(1)} %bitcast.10, s32[1,8]{1,0:T(1,128)S(1)} %bitcast.12, s32[1,8]{1,0:T(1,128)S(1)} %bitcast.14, s32[2,256]{1,0:T(2,128)} %bitcast.16, f32[3072,128]{1,0:T(8,128)S(1)} %get-tuple-element.24.refs_5_, ...), custom_call_target="tpu_custom_call" | custom-call | flops 4294967296 | bytes 4194304 | tf_op jit(solution)/shard_map/pairs/pallas_call | solution.py:249
  18.3 0.6 %collective-permute-start.3 = (f32[1,128]{1,0:T(1,128)S(1)}, f32[1,128]{1,0:T(1,128)S(1)}, u32[]{:S(2)}, u32[]{:S(2)}) collective-permute-start(f32[1,128]{1,0:T(1,128)S(1)} %get-tuple-element.31.refs_1_), channel_id=1, source_target_pairs={{0,2},{1,3},{2,0},{3,1},{4,6},{5,7},{6,4},{7,5},{8,10},{9,11},{10,... | collective-permute-start | bytes 1544 | tf_op jit(solution)/shard_map/pairs/ppermute | solution.py:274
  18.9 0.0 collective-permute-done.4.refs_1_
  18.9 0.0 collective-permute-start.5
  18.9 2.1 %collective-permute-done.6.refs_2_ = bf16[16,3200]{1,0:T(8,128)(2,1)S(1)} collective-permute-done((bf16[16,3200]{1,0:T(8,128)(2,1)S(1)}, bf16[16,3200]{1,0:T(8,128)(2,1)S(1)}, u32[]{:S(2)}, u32[]{:S(2)}) %collective-permute-start.6) | collective-permute-done | bytes 102432 | tf_op jit(solution)/shard_map/states/ppermute | solution.py:181
  21.0 0.0 collective-permute-start.7
  21.0 0.0 collective-permute-done.8.refs_3_
  21.0 0.0 collective-permute-done.9.refs_5_
  21.0 0.0 copy-done
  21.0 0.9 %scores.2 = (f32[4,128]{1,0:T(4,128)S(1)}, bf16[256,512]{1,0:T(8,128)(2,1)S(1)}) custom-call(bf16[16,3200]{1,0:T(8,128)(2,1)S(1)} %states.1.refs_8_.refs_0_, bf16[16,3200]{1,0:T(8,128)(2,1)S(1)} %collective-permute-done.4.refs_1_, bf16[16,3200]{1,0:T(8,128)(2,1)S(1)} %collective-permute-done.6.refs_2_, bf16[16,3200]{1,0:T(8,128)(2,1)S(1)} %collective-permute-done.8.refs_3_, ...), custom_call_target="tpu_custom_call" | custom-call | flops 100663296 | bytes 2097152 | tf_op jit(solution)/shard_map/scores/pallas_call | solution.py:278
  21.9 0.0 collective-permute-done.3.refs_0_
  21.9 0.0 collective-permute-done.5.refs_2_
  21.9 0.2 collective-permute-done.7.refs_3_
  22.1 0.2 scores.3
  22.3 3.4 %collective-permute-start.12 = (f32[1,128]{1,0:T(1,128)S(1)}, f32[1,128]{1,0:T(1,128)S(1)}, u32[]{:S(2)}, u32[]{:S(2)}) collective-permute-start(f32[1,128]{1,0:T(1,128)S(1)} %get-tuple-element.40), channel_id=1, source_target_pairs={{0,12},{4,0},{8,4},{12,8},{1,13},{5,1},{9,5},{13,9},{2,14},{6,2},{... | collective-permute-start | bytes 1544 | tf_op jit(solution)/shard_map/back/ppermute | solution.py:181
  25.7 0.0 collective-permute-start.11
  25.7 1.5 %collective-permute-start.10 = (f32[1,128]{1,0:T(1,128)S(1)}, f32[1,128]{1,0:T(1,128)S(1)}, u32[]{:S(2)}, u32[]{:S(2)}) collective-permute-start(f32[1,128]{1,0:T(1,128)S(1)} %get-tuple-element.38), channel_id=1, source_target_pairs={{0,8},{4,12},{8,0},{12,4},{1,9},{5,13},{9,1},{13,5},{2,10},{6,14},... | collective-permute-start | bytes 1544 | tf_op jit(solution)/shard_map/back/ppermute | solution.py:181
  27.2 0.0 collective-permute-done.12
  27.2 3.8 %collective-permute-done.11 = f32[1,128]{1,0:T(1,128)S(1)} collective-permute-done((f32[1,128]{1,0:T(1,128)S(1)}, f32[1,128]{1,0:T(1,128)S(1)}, u32[]{:S(2)}, u32[]{:S(2)}) %collective-permute-start.11) | collective-permute-done | bytes 544 | tf_op jit(solution)/shard_map/back/ppermute | solution.py:181
  31.0 0.0 collective-permute-done.10
  31.0 0.5 %add_bitcast_fusion = f32[128]{0:T(128)} fusion(f32[1,128]{1,0:T(1,128)S(1)} %collective-permute-done.12, f32[1,128]{1,0:T(1,128)S(1)} %collective-permute-done.11, f32[1,128]{1,0:T(1,128)S(1)} %get-tuple-element.37, f32[1,128]{1,0:T(1,128)S(1)} %collective-permute-done.10), kind=kLoop, calls=%fused_computation | loop fusion | flops 384 | bytes 2560 | tf_op jit(solution)/shard_map/reshape | solution.py:306
Async XLA Ops:
  0.0 21.0 %collective-permute-start.9 = (bf16[128,3072]{1,0:T(8,128)(2,1)}, bf16[128,3072]{1,0:T(8,128)(2,1)S(1)}, u32[]{:S(2)}, u32[]{:S(2)}) collective-permute-start(bf16[128,3072]{1,0:T(8,128)(2,1)} %refs_4_.1), channel_id=1, source_target_pairs={{0,2},{2,0},{1,3},{3,1},{4,6},{6,4},{5,7},{7,5},{8,10},{10,8},{9,1... | collective-permute-start | bytes 2359304 | tf_op jit(solution)/shard_map/item_rows/ppermute | solution.py:181
  2.9 7.7 %collective-permute-start = (s32[8]{0:T(128)}, s32[8]{0:T(128)S(1)}, u32[]{:S(2)}, u32[]{:S(2)}) collective-permute-start(s32[8]{0:T(128)} %param.7), channel_id=1, source_target_pairs={{0,4},{4,8},{8,12},{12,0},{1,5},{5,9},{9,13},{13,1},{2,6},{6,10},{... | collective-permute-start | bytes 104 | tf_op jit(solution)/shard_map/ids/ppermute | solution.py:181
  4.5 6.2 %collective-permute-start.1 = (s32[8]{0:T(128)}, s32[8]{0:T(128)S(1)}, u32[]{:S(2)}, u32[]{:S(2)}) collective-permute-start(s32[8]{0:T(128)} %param.7), channel_id=1, source_target_pairs={{0,8},{4,12},{8,0},{12,4},{1,9},{5,13},{9,1},{13,5},{2,10},{6,14},... | collective-permute-start | bytes 104 | tf_op jit(solution)/shard_map/ids/ppermute | solution.py:181
  7.1 3.7 %collective-permute-start.2 = (s32[8]{0:T(128)}, s32[8]{0:T(128)S(1)}, u32[]{:S(2)}, u32[]{:S(2)}) collective-permute-start(s32[8]{0:T(128)} %param.7), channel_id=1, source_target_pairs={{0,12},{4,0},{8,4},{12,8},{1,13},{5,1},{9,5},{13,9},{2,14},{6,2},{... | collective-permute-start | bytes 104 | tf_op jit(solution)/shard_map/ids/ppermute | solution.py:181
  11.2 7.7 %collective-permute-start.4 = (bf16[16,3200]{1,0:T(8,128)(2,1)S(1)}, bf16[16,3200]{1,0:T(8,128)(2,1)S(1)}, u32[]{:S(2)}, u32[]{:S(2)}) collective-permute-start(bf16[16,3200]{1,0:T(8,128)(2,1)S(1)} %states.1.refs_8_.refs_0_), channel_id=1, source_target_pairs={{0,4},{4,8},{8,12},{12,0},{1,5},{5,9},{9,13},{13,1},{2,6},{6,10},{... | collective-permute-start | bytes 307208 | tf_op jit(solution)/shard_map/states/ppermute | solution.py:181
  11.8 9.2 %collective-permute-start.6 = (bf16[16,3200]{1,0:T(8,128)(2,1)S(1)}, bf16[16,3200]{1,0:T(8,128)(2,1)S(1)}, u32[]{:S(2)}, u32[]{:S(2)}) collective-permute-start(bf16[16,3200]{1,0:T(8,128)(2,1)S(1)} %states.1.refs_8_.refs_0_), channel_id=1, source_target_pairs={{0,8},{4,12},{8,0},{12,4},{1,9},{5,13},{9,1},{13,5},{2,10},{6,14},... | collective-permute-start | bytes 307208 | tf_op jit(solution)/shard_map/states/ppermute | solution.py:181
  14.9 6.1 %collective-permute-start.8 = (bf16[16,3200]{1,0:T(8,128)(2,1)S(1)}, bf16[16,3200]{1,0:T(8,128)(2,1)S(1)}, u32[]{:S(2)}, u32[]{:S(2)}) collective-permute-start(bf16[16,3200]{1,0:T(8,128)(2,1)S(1)} %states.1.refs_8_.refs_0_), channel_id=1, source_target_pairs={{0,12},{4,0},{8,4},{12,8},{1,13},{5,1},{9,5},{13,9},{2,14},{6,2},{... | collective-permute-start | bytes 307208 | tf_op jit(solution)/shard_map/states/ppermute | solution.py:181
  15.1 6.0 %copy-start = (bf16[128,3072]{1,0:T(8,128)(2,1)S(1)}, bf16[128,3072]{1,0:T(8,128)(2,1)}, u32[]{:S(2)}) copy-start(bf16[128,3072]{1,0:T(8,128)(2,1)} %refs_4_.1) | copy-start | bytes 2359300
  18.3 3.6 %collective-permute-start.3 = (f32[1,128]{1,0:T(1,128)S(1)}, f32[1,128]{1,0:T(1,128)S(1)}, u32[]{:S(2)}, u32[]{:S(2)}) collective-permute-start(f32[1,128]{1,0:T(1,128)S(1)} %get-tuple-element.31.refs_1_), channel_id=1, source_target_pairs={{0,2},{1,3},{2,0},{3,1},{4,6},{5,7},{6,4},{7,5},{8,10},{9,11},{10,... | collective-permute-start | bytes 1544 | tf_op jit(solution)/shard_map/pairs/ppermute | solution.py:274
  18.9 3.0 %collective-permute-start.5 = (f32[1,128]{1,0:T(1,128)S(1)}, f32[1,128]{1,0:T(1,128)S(1)}, u32[]{:S(2)}, u32[]{:S(2)}) collective-permute-start(f32[1,128]{1,0:T(1,128)S(1)} %get-tuple-element.31.refs_1_), channel_id=1, source_target_pairs={{0,3},{1,2},{2,1},{3,0},{4,7},{5,6},{6,5},{7,4},{8,11},{9,10},{10,... | collective-permute-start | bytes 1544 | tf_op jit(solution)/shard_map/pairs/ppermute | solution.py:274
  21.0 1.1 %collective-permute-start.7 = (f32[1,128]{1,0:T(1,128)S(1)}, f32[1,128]{1,0:T(1,128)S(1)}, u32[]{:S(2)}, u32[]{:S(2)}) collective-permute-start(f32[1,128]{1,0:T(1,128)S(1)} %get-tuple-element.31.refs_1_), channel_id=1, source_target_pairs={{0,1},{1,0},{2,3},{3,2},{4,5},{5,4},{6,7},{7,6},{8,9},{9,8},{10,11... | collective-permute-start | bytes 1544 | tf_op jit(solution)/shard_map/pairs/ppermute | solution.py:274
  22.3 4.9 %collective-permute-start.12 = (f32[1,128]{1,0:T(1,128)S(1)}, f32[1,128]{1,0:T(1,128)S(1)}, u32[]{:S(2)}, u32[]{:S(2)}) collective-permute-start(f32[1,128]{1,0:T(1,128)S(1)} %get-tuple-element.40), channel_id=1, source_target_pairs={{0,12},{4,0},{8,4},{12,8},{1,13},{5,1},{9,5},{13,9},{2,14},{6,2},{... | collective-permute-start | bytes 1544 | tf_op jit(solution)/shard_map/back/ppermute | solution.py:181
  25.7 5.3 %collective-permute-start.11 = (f32[1,128]{1,0:T(1,128)S(1)}, f32[1,128]{1,0:T(1,128)S(1)}, u32[]{:S(2)}, u32[]{:S(2)}) collective-permute-start(f32[1,128]{1,0:T(1,128)S(1)} %get-tuple-element.39), channel_id=1, source_target_pairs={{0,4},{4,8},{8,12},{12,0},{1,5},{5,9},{9,13},{13,1},{2,6},{6,10},{... | collective-permute-start | bytes 1544 | tf_op jit(solution)/shard_map/back/ppermute | solution.py:181
  25.7 5.3 %collective-permute-start.10 = (f32[1,128]{1,0:T(1,128)S(1)}, f32[1,128]{1,0:T(1,128)S(1)}, u32[]{:S(2)}, u32[]{:S(2)}) collective-permute-start(f32[1,128]{1,0:T(1,128)S(1)} %get-tuple-element.38), channel_id=1, source_target_pairs={{0,8},{4,12},{8,0},{12,4},{1,9},{5,13},{9,1},{13,5},{2,10},{6,14},... | collective-permute-start | bytes 1544 | tf_op jit(solution)/shard_map/back/ppermute | solution.py:181

commit v33 on v31

--- a/solution.py
+++ b/solution.py
@@ -268,7 +268,7 @@
             perm = [
                 (c * parts + d, (c + q) % planes * parts + (d + h) % parts) for c in range(planes) for d in range(parts)
             ]
-            source, after = pair_parts, {1: 1, 2: 2}.get(len(pair_scores) - 1, 0)
+            source, after = pair_parts, {1: 2, 2: 1}.get(len(pair_scores) - 1, 0)
             if after:
                 source, states[after] = lax.optimization_barrier((pair_parts, states[after]))
             pair_scores[q, h] = lax.ppermute(source, ("cache", "pair"), perm)

time: 30.5 us -> 30.5 us (level)
  starting transfers between devices: 18.7 us -> 19.4 us
  waiting for transfers between devices: 4.09 us -> 3.44 us
    ppermute x3, starting transfers between devices: 0.61 us -> 1.87 us  [body(): pair_scores[q, h] = lax.ppermute(source, ('cache', 'pair'), perm)]
    ppermute x10, waiting for transfers between devices: 3.9 us -> 2.64 us  [shift(): return lax.ppermute(x, axis, [(s, (s + step) % size) for s in range(size)])]
    ppermute x3, waiting for transfers between devices: 0.18 us -> 0.79 us  [body(): pair_scores[q, h] = lax.ppermute(source, ('cache', 'pair'), perm)]
    ppermute x10, starting transfers between devices: 18.1 us -> 17.5 us  [shift(): return lax.ppermute(x, axis, [(s, (s + step) % size) for s in range(size)])]
  transfers between devices with their start and end apart: 13 -> 13, of which waited for: 5 -> 6; matrix products, arithmetic and copies ran while one was open for 0% -> 0% of each run, Pallas kernels for 22% -> 22%
where the time goes in v33:
time: 30.5 us; the launch traced here: 30.3 us
  starting transfers between devices  19.4 us (64%)
  Pallas kernels  6.88 us (23%)
  waiting for transfers between devices  3.44 us (11%)
  other arithmetic  0.52 us (2%)
    ppermute x10, starting transfers between devices, shift(): return lax.ppermute(x, axis, [(s, (s + step) % size) for s in range(size)])  17.5 us
    pallas_call x1, Pallas kernels, body(): pl.pallas_call(functools.partial(pair_kernel, total, cap, slots, user_sta...  3.23 us
    ppermute x10, waiting for transfers between devices, shift(): return lax.ppermute(x, axis, [(s, (s + step) % size) for s in range(size)])  2.64 us
    pallas_call x1, Pallas kernels, body(): pl.pallas_call(turn_kernel, out_shape=(jax.ShapeDtypeStruct((width, rows)...  2.2 us
    ppermute x3, starting transfers between devices, body(): pair_scores[q, h] = lax.ppermute(source, ('cache', 'pair'), perm)  1.87 us
    pallas_call x1, Pallas kernels, body(): pl.pallas_call(functools.partial(linear_kernel, total, planes), out_shape...  0.89 us
    ppermute x3, waiting for transfers between devices, body(): pair_scores[q, h] = lax.ppermute(source, ('cache', 'pair'), perm)  0.79 us
  transfers between devices with their start and end apart: 13, of which 6 were waited for; matrix products, arithmetic and copies ran while one was open for 0% of the time, Pallas kernels for 22%

profile of v33, /device:TPU:0, one launch (start us, length us, event | category | flops | bytes accessed | tf_op | source)
XLA Modules:
  0.0 30.3 jit_solution(17879186432800700290)
XLA Ops:
  0.0 2.9 %collective-permute-start.9 = (bf16[128,3072]{1,0:T(8,128)(2,1)}, bf16[128,3072]{1,0:T(8,128)(2,1)S(1)}, u32[]{:S(2)}, u32[]{:S(2)}) collective-permute-start(bf16[128,3072]{1,0:T(8,128)(2,1)} %refs_4_.1), channel_id=1, source_target_pairs={{0,2},{2,0},{1,3},{3,1},{4,6},{6,4},{5,7},{7,5},{8,10},{10,8},{9,1... | collective-permute-start | bytes 2359304 | tf_op jit(solution)/shard_map/item_rows/ppermute | solution.py:181
  2.9 1.6 %collective-permute-start = (s32[8]{0:T(128)}, s32[8]{0:T(128)S(1)}, u32[]{:S(2)}, u32[]{:S(2)}) collective-permute-start(s32[8]{0:T(128)} %param.7), channel_id=1, source_target_pairs={{0,4},{4,8},{8,12},{12,0},{1,5},{5,9},{9,13},{13,1},{2,6},{6,10},{... | collective-permute-start | bytes 104 | tf_op jit(solution)/shard_map/ids/ppermute | solution.py:181
  4.5 2.6 %collective-permute-start.1 = (s32[8]{0:T(128)}, s32[8]{0:T(128)S(1)}, u32[]{:S(2)}, u32[]{:S(2)}) collective-permute-start(s32[8]{0:T(128)} %param.7), channel_id=1, source_target_pairs={{0,8},{4,12},{8,0},{12,4},{1,9},{5,13},{9,1},{13,5},{2,10},{6,14},... | collective-permute-start | bytes 104 | tf_op jit(solution)/shard_map/ids/ppermute | solution.py:181
  7.1 1.3 %collective-permute-start.2 = (s32[8]{0:T(128)}, s32[8]{0:T(128)S(1)}, u32[]{:S(2)}, u32[]{:S(2)}) collective-permute-start(s32[8]{0:T(128)} %param.7), channel_id=1, source_target_pairs={{0,12},{4,0},{8,4},{12,8},{1,13},{5,1},{9,5},{13,9},{2,14},{6,2},{... | collective-permute-start | bytes 104 | tf_op jit(solution)/shard_map/ids/ppermute | solution.py:181
  8.5 2.2 %turn.1 = (f32[3072,128]{1,0:T(8,128)S(1)}, bf16[3072,128]{1,0:T(8,128)(2,1)S(1)}, bf16[64,64,256]{2,1,0:T(8,128)(2,1)S(1)}, bf16[128,3072]{1,0:T(8,128)(2,1)S(1...) custom-call(bf16[128,3072]{1,0:T(8,128)(2,1)} %refs_4_.1, bf16[64,64,256]{2,1,0:T(8,128)(2,1)} %bitcast.15, ...), custom_call_target="tpu_custom_call" | custom-call | flops 1610612736 | bytes 8388608 | tf_op jit(solution)/shard_map/turn/pallas_call | solution.py:209
  10.7 0.0 collective-permute-done
  10.7 0.0 collective-permute-done.1
  10.7 0.1 collective-permute-done.2
  10.8 0.4 %states.1.refs_8_.refs_0_ = bf16[16,3200]{1,0:T(8,128)(2,1)S(1)} custom-call(s32[1,8]{1,0:T(1,128)S(1)} %get-tuple-element.23.refs_0_, s32[1,8]{1,0:T(1,128)S(1)} %bitcast.9, s32[1,8]{1,0:T(1,128)S(1)} %bitcast.11, s32[1,8]{1,0:T(1,128)S(1)} %bitcast.13, bf16[16,128]{1,0:T(8,128)(2,1)S(1)} %get-tuple-element.27.refs_4_, ...), custom_call_target="tpu_custom_call" | custom-call | flops 12582912 | bytes 1048576 | tf_op jit(solution)/shard_map/states/pallas_call | solution.py:238
  11.2 1.0 %collective-permute-start.4 = (bf16[16,3200]{1,0:T(8,128)(2,1)S(1)}, bf16[16,3200]{1,0:T(8,128)(2,1)S(1)}, u32[]{:S(2)}, u32[]{:S(2)}) collective-permute-start(bf16[16,3200]{1,0:T(8,128)(2,1)S(1)} %states.1.refs_8_.refs_0_), channel_id=1, source_target_pairs={{0,8},{4,12},{8,0},{12,4},{1,9},{5,13},{9,1},{13,5},{2,10},{6,14},... | collective-permute-start | bytes 307208 | tf_op jit(solution)/shard_map/states/ppermute | solution.py:181
  12.1 2.8 %collective-permute-start.6 = (bf16[16,3200]{1,0:T(8,128)(2,1)S(1)}, bf16[16,3200]{1,0:T(8,128)(2,1)S(1)}, u32[]{:S(2)}, u32[]{:S(2)}) collective-permute-start(bf16[16,3200]{1,0:T(8,128)(2,1)S(1)} %states.1.refs_8_.refs_0_), channel_id=1, source_target_pairs={{0,4},{4,8},{8,12},{12,0},{1,5},{5,9},{9,13},{13,1},{2,6},{6,10},{... | collective-permute-start | bytes 307208 | tf_op jit(solution)/shard_map/states/ppermute | solution.py:181
  14.9 1.0 %collective-permute-start.8 = (bf16[16,3200]{1,0:T(8,128)(2,1)S(1)}, bf16[16,3200]{1,0:T(8,128)(2,1)S(1)}, u32[]{:S(2)}, u32[]{:S(2)}) collective-permute-start(bf16[16,3200]{1,0:T(8,128)(2,1)S(1)} %states.1.refs_8_.refs_0_), channel_id=1, source_target_pairs={{0,12},{4,0},{8,4},{12,8},{1,13},{5,1},{9,5},{13,9},{2,14},{6,2},{... | collective-permute-start | bytes 307208 | tf_op jit(solution)/shard_map/states/ppermute | solution.py:181
  16.0 0.0 copy-start
  16.0 3.2 %pairs.1 = (f32[1,128]{1,0:T(1,128)S(1)}, s32[4,128]{1,0:T(4,128)S(1)}) custom-call(s32[1,8]{1,0:T(1,128)S(1)} %get-tuple-element.23.refs_0_, s32[1,8]{1,0:T(1,128)S(1)} %bitcast.10, s32[1,8]{1,0:T(1,128)S(1)} %bitcast.12, s32[1,8]{1,0:T(1,128)S(1)} %bitcast.14, s32[2,256]{1,0:T(2,128)} %bitcast.16, f32[3072,128]{1,0:T(8,128)S(1)} %get-tuple-element.24.refs_5_, ...), custom_call_target="tpu_custom_call" | custom-call | flops 4294967296 | bytes 4194304 | tf_op jit(solution)/shard_map/pairs/pallas_call | solution.py:249
  19.2 0.6 %collective-permute-start.3 = (f32[1,128]{1,0:T(1,128)S(1)}, f32[1,128]{1,0:T(1,128)S(1)}, u32[]{:S(2)}, u32[]{:S(2)}) collective-permute-start(f32[1,128]{1,0:T(1,128)S(1)} %get-tuple-element.31.refs_1_), channel_id=1, source_target_pairs={{0,2},{1,3},{2,0},{3,1},{4,6},{5,7},{6,4},{7,5},{8,10},{9,11},{10,... | collective-permute-start | bytes 1544 | tf_op jit(solution)/shard_map/pairs/ppermute | solution.py:274
  19.8 0.3 %collective-permute-done.4.refs_2_ = bf16[16,3200]{1,0:T(8,128)(2,1)S(1)} collective-permute-done((bf16[16,3200]{1,0:T(8,128)(2,1)S(1)}, bf16[16,3200]{1,0:T(8,128)(2,1)S(1)}, u32[]{:S(2)}, u32[]{:S(2)}) %collective-permute-start.4) | collective-permute-done | bytes 102432 | tf_op jit(solution)/shard_map/states/ppermute | solution.py:181
  20.1 0.0 collective-permute-start.5
  20.2 0.0 collective-permute-done.6.refs_1_
  20.2 1.3 %collective-permute-start.7 = (f32[1,128]{1,0:T(1,128)S(1)}, f32[1,128]{1,0:T(1,128)S(1)}, u32[]{:S(2)}, u32[]{:S(2)}) collective-permute-start(f32[1,128]{1,0:T(1,128)S(1)} %get-tuple-element.31.refs_1_), channel_id=1, source_target_pairs={{0,1},{1,0},{2,3},{3,2},{4,5},{5,4},{6,7},{7,6},{8,9},{9,8},{10,11... | collective-permute-start | bytes 1544 | tf_op jit(solution)/shard_map/pairs/ppermute | solution.py:274
  21.4 0.0 collective-permute-done.8.refs_3_
  21.4 0.0 collective-permute-done.9.refs_5_
  21.4 0.0 copy-done
  21.4 0.9 %scores.2 = (f32[4,128]{1,0:T(4,128)S(1)}, bf16[256,512]{1,0:T(8,128)(2,1)S(1)}) custom-call(bf16[16,3200]{1,0:T(8,128)(2,1)S(1)} %states.1.refs_8_.refs_0_, bf16[16,3200]{1,0:T(8,128)(2,1)S(1)} %collective-permute-done.6.refs_1_, bf16[16,3200]{1,0:T(8,128)(2,1)S(1)} %collective-permute-done.4.refs_2_, bf16[16,3200]{1,0:T(8,128)(2,1)S(1)} %collective-permute-done.8.refs_3_, ...), custom_call_target="tpu_custom_call" | custom-call | flops 100663296 | bytes 2097152 | tf_op jit(solution)/shard_map/scores/pallas_call | solution.py:278
  22.3 0.5 %collective-permute-done.3.refs_0_ = f32[1,128]{1,0:T(1,128)S(1)} collective-permute-done((f32[1,128]{1,0:T(1,128)S(1)}, f32[1,128]{1,0:T(1,128)S(1)}, u32[]{:S(2)}, u32[]{:S(2)}) %collective-permute-start.3) | collective-permute-done | bytes 544 | tf_op jit(solution)/shard_map/pairs/ppermute | solution.py:274
  22.8 0.3 collective-permute-done.5.refs_2_
  23.1 0.0 collective-permute-done.7.refs_3_
  23.1 0.2 scores.3
  23.3 0.8 %collective-permute-start.12 = (f32[1,128]{1,0:T(1,128)S(1)}, f32[1,128]{1,0:T(1,128)S(1)}, u32[]{:S(2)}, u32[]{:S(2)}) collective-permute-start(f32[1,128]{1,0:T(1,128)S(1)} %get-tuple-element.40), channel_id=1, source_target_pairs={{0,4},{4,8},{8,12},{12,0},{1,5},{5,9},{9,13},{13,1},{2,6},{6,10},{... | collective-permute-start | bytes 1544 | tf_op jit(solution)/shard_map/back/ppermute | solution.py:181
  24.1 2.2 %collective-permute-start.11 = (f32[1,128]{1,0:T(1,128)S(1)}, f32[1,128]{1,0:T(1,128)S(1)}, u32[]{:S(2)}, u32[]{:S(2)}) collective-permute-start(f32[1,128]{1,0:T(1,128)S(1)} %get-tuple-element.39), channel_id=1, source_target_pairs={{0,8},{4,12},{8,0},{12,4},{1,9},{5,13},{9,1},{13,5},{2,10},{6,14},... | collective-permute-start | bytes 1544 | tf_op jit(solution)/shard_map/back/ppermute | solution.py:181
  26.3 1.3 %collective-permute-start.10 = (f32[1,128]{1,0:T(1,128)S(1)}, f32[1,128]{1,0:T(1,128)S(1)}, u32[]{:S(2)}, u32[]{:S(2)}) collective-permute-start(f32[1,128]{1,0:T(1,128)S(1)} %get-tuple-element.38), channel_id=1, source_target_pairs={{0,12},{4,0},{8,4},{12,8},{1,13},{5,1},{9,5},{13,9},{2,14},{6,2},{... | collective-permute-start | bytes 1544 | tf_op jit(solution)/shard_map/back/ppermute | solution.py:181
  27.6 1.1 %collective-permute-done.12 = f32[1,128]{1,0:T(1,128)S(1)} collective-permute-done((f32[1,128]{1,0:T(1,128)S(1)}, f32[1,128]{1,0:T(1,128)S(1)}, u32[]{:S(2)}, u32[]{:S(2)}) %collective-permute-start.12) | collective-permute-done | bytes 544 | tf_op jit(solution)/shard_map/back/ppermute | solution.py:181
  28.7 0.0 collective-permute-done.11
  28.7 1.1 %collective-permute-done.10 = f32[1,128]{1,0:T(1,128)S(1)} collective-permute-done((f32[1,128]{1,0:T(1,128)S(1)}, f32[1,128]{1,0:T(1,128)S(1)}, u32[]{:S(2)}, u32[]{:S(2)}) %collective-permute-start.10) | collective-permute-done | bytes 544 | tf_op jit(solution)/shard_map/back/ppermute | solution.py:181
  29.8 0.5 %add_bitcast_fusion = f32[128]{0:T(128)} fusion(f32[1,128]{1,0:T(1,128)S(1)} %collective-permute-done.12, f32[1,128]{1,0:T(1,128)S(1)} %collective-permute-done.11, f32[1,128]{1,0:T(1,128)S(1)} %get-tuple-element.37, f32[1,128]{1,0:T(1,128)S(1)} %collective-permute-done.10), kind=kLoop, calls=%fused_computation | loop fusion | flops 384 | bytes 2560 | tf_op jit(solution)/shard_map/reshape | solution.py:306
Async XLA Ops:
  0.0 21.4 %collective-permute-start.9 = (bf16[128,3072]{1,0:T(8,128)(2,1)}, bf16[128,3072]{1,0:T(8,128)(2,1)S(1)}, u32[]{:S(2)}, u32[]{:S(2)}) collective-permute-start(bf16[128,3072]{1,0:T(8,128)(2,1)} %refs_4_.1), channel_id=1, source_target_pairs={{0,2},{2,0},{1,3},{3,1},{4,6},{6,4},{5,7},{7,5},{8,10},{10,8},{9,1... | collective-permute-start | bytes 2359304 | tf_op jit(solution)/shard_map/item_rows/ppermute | solution.py:181
  2.9 7.7 %collective-permute-start = (s32[8]{0:T(128)}, s32[8]{0:T(128)S(1)}, u32[]{:S(2)}, u32[]{:S(2)}) collective-permute-start(s32[8]{0:T(128)} %param.7), channel_id=1, source_target_pairs={{0,4},{4,8},{8,12},{12,0},{1,5},{5,9},{9,13},{13,1},{2,6},{6,10},{... | collective-permute-start | bytes 104 | tf_op jit(solution)/shard_map/ids/ppermute | solution.py:181
  4.5 6.2 %collective-permute-start.1 = (s32[8]{0:T(128)}, s32[8]{0:T(128)S(1)}, u32[]{:S(2)}, u32[]{:S(2)}) collective-permute-start(s32[8]{0:T(128)} %param.7), channel_id=1, source_target_pairs={{0,8},{4,12},{8,0},{12,4},{1,9},{5,13},{9,1},{13,5},{2,10},{6,14},... | collective-permute-start | bytes 104 | tf_op jit(solution)/shard_map/ids/ppermute | solution.py:181
  7.1 3.7 %collective-permute-start.2 = (s32[8]{0:T(128)}, s32[8]{0:T(128)S(1)}, u32[]{:S(2)}, u32[]{:S(2)}) collective-permute-start(s32[8]{0:T(128)} %param.7), channel_id=1, source_target_pairs={{0,12},{4,0},{8,4},{12,8},{1,13},{5,1},{9,5},{13,9},{2,14},{6,2},{... | collective-permute-start | bytes 104 | tf_op jit(solution)/shard_map/ids/ppermute | solution.py:181
  11.2 9.0 %collective-permute-start.4 = (bf16[16,3200]{1,0:T(8,128)(2,1)S(1)}, bf16[16,3200]{1,0:T(8,128)(2,1)S(1)}, u32[]{:S(2)}, u32[]{:S(2)}) collective-permute-start(bf16[16,3200]{1,0:T(8,128)(2,1)S(1)} %states.1.refs_8_.refs_0_), channel_id=1, source_target_pairs={{0,8},{4,12},{8,0},{12,4},{1,9},{5,13},{9,1},{13,5},{2,10},{6,14},... | collective-permute-start | bytes 307208 | tf_op jit(solution)/shard_map/states/ppermute | solution.py:181
  12.1 8.0 %collective-permute-start.6 = (bf16[16,3200]{1,0:T(8,128)(2,1)S(1)}, bf16[16,3200]{1,0:T(8,128)(2,1)S(1)}, u32[]{:S(2)}, u32[]{:S(2)}) collective-permute-start(bf16[16,3200]{1,0:T(8,128)(2,1)S(1)} %states.1.refs_8_.refs_0_), channel_id=1, source_target_pairs={{0,4},{4,8},{8,12},{12,0},{1,5},{5,9},{9,13},{13,1},{2,6},{6,10},{... | collective-permute-start | bytes 307208 | tf_op jit(solution)/shard_map/states/ppermute | solution.py:181
  14.9 6.5 %collective-permute-start.8 = (bf16[16,3200]{1,0:T(8,128)(2,1)S(1)}, bf16[16,3200]{1,0:T(8,128)(2,1)S(1)}, u32[]{:S(2)}, u32[]{:S(2)}) collective-permute-start(bf16[16,3200]{1,0:T(8,128)(2,1)S(1)} %states.1.refs_8_.refs_0_), channel_id=1, source_target_pairs={{0,12},{4,0},{8,4},{12,8},{1,13},{5,1},{9,5},{13,9},{2,14},{6,2},{... | collective-permute-start | bytes 307208 | tf_op jit(solution)/shard_map/states/ppermute | solution.py:181
  16.0 5.5 %copy-start = (bf16[128,3072]{1,0:T(8,128)(2,1)S(1)}, bf16[128,3072]{1,0:T(8,128)(2,1)}, u32[]{:S(2)}) copy-start(bf16[128,3072]{1,0:T(8,128)(2,1)} %refs_4_.1) | copy-start | bytes 2359300
  19.2 3.6 %collective-permute-start.3 = (f32[1,128]{1,0:T(1,128)S(1)}, f32[1,128]{1,0:T(1,128)S(1)}, u32[]{:S(2)}, u32[]{:S(2)}) collective-permute-start(f32[1,128]{1,0:T(1,128)S(1)} %get-tuple-element.31.refs_1_), channel_id=1, source_target_pairs={{0,2},{1,3},{2,0},{3,1},{4,6},{5,7},{6,4},{7,5},{8,10},{9,11},{10,... | collective-permute-start | bytes 1544 | tf_op jit(solution)/shard_map/pairs/ppermute | solution.py:274
  20.1 3.0 %collective-permute-start.5 = (f32[1,128]{1,0:T(1,128)S(1)}, f32[1,128]{1,0:T(1,128)S(1)}, u32[]{:S(2)}, u32[]{:S(2)}) collective-permute-start(f32[1,128]{1,0:T(1,128)S(1)} %get-tuple-element.31.refs_1_), channel_id=1, source_target_pairs={{0,3},{1,2},{2,1},{3,0},{4,7},{5,6},{6,5},{7,4},{8,11},{9,10},{10,... | collective-permute-start | bytes 1544 | tf_op jit(solution)/shard_map/pairs/ppermute | solution.py:274
  20.2 3.0 %collective-permute-start.7 = (f32[1,128]{1,0:T(1,128)S(1)}, f32[1,128]{1,0:T(1,128)S(1)}, u32[]{:S(2)}, u32[]{:S(2)}) collective-permute-start(f32[1,128]{1,0:T(1,128)S(1)} %get-tuple-element.31.refs_1_), channel_id=1, source_target_pairs={{0,1},{1,0},{2,3},{3,2},{4,5},{5,4},{6,7},{7,6},{8,9},{9,8},{10,11... | collective-permute-start | bytes 1544 | tf_op jit(solution)/shard_map/pairs/ppermute | solution.py:274
  23.3 5.4 %collective-permute-start.12 = (f32[1,128]{1,0:T(1,128)S(1)}, f32[1,128]{1,0:T(1,128)S(1)}, u32[]{:S(2)}, u32[]{:S(2)}) collective-permute-start(f32[1,128]{1,0:T(1,128)S(1)} %get-tuple-element.40), channel_id=1, source_target_pairs={{0,4},{4,8},{8,12},{12,0},{1,5},{5,9},{9,13},{13,1},{2,6},{6,10},{... | collective-permute-start | bytes 1544 | tf_op jit(solution)/shard_map/back/ppermute | solution.py:181
  24.1 4.6 %collective-permute-start.11 = (f32[1,128]{1,0:T(1,128)S(1)}, f32[1,128]{1,0:T(1,128)S(1)}, u32[]{:S(2)}, u32[]{:S(2)}) collective-permute-start(f32[1,128]{1,0:T(1,128)S(1)} %get-tuple-element.39), channel_id=1, source_target_pairs={{0,8},{4,12},{8,0},{12,4},{1,9},{5,13},{9,1},{13,5},{2,10},{6,14},... | collective-permute-start | bytes 1544 | tf_op jit(solution)/shard_map/back/ppermute | solution.py:181
  26.3 3.5 %collective-permute-start.10 = (f32[1,128]{1,0:T(1,128)S(1)}, f32[1,128]{1,0:T(1,128)S(1)}, u32[]{:S(2)}, u32[]{:S(2)}) collective-permute-start(f32[1,128]{1,0:T(1,128)S(1)} %get-tuple-element.38), channel_id=1, source_target_pairs={{0,12},{4,0},{8,4},{12,8},{1,13},{5,1},{9,5},{13,9},{2,14},{6,2},{... | collective-permute-start | bytes 1544 | tf_op jit(solution)/shard_map/back/ppermute | solution.py:181

commit v34 on v22

--- a/solution.py
+++ b/solution.py
@@ -107,7 +107,7 @@
         )
         return total + dot(left, right, NN) * jnp.concatenate([rows32[pl.ds(a, K), :] for a, _ in fields_of], axis=1)
 
-    sums = lax.fori_loop(0, steps, two, jnp.zeros((K, 2 * items), jnp.float32), unroll=32)
+    sums = lax.fori_loop(0, steps, two, jnp.zeros((K, 2 * items), jnp.float32), unroll=64)
     line = jnp.sum(sums, axis=0, keepdims=True)
     out[...] = line[:, :items] + line[:, items:]
 
@@ -262,7 +262,7 @@
             perm = [
                 (c * parts + d, (c + q) % planes * parts + (d + h) % parts) for c in range(planes) for d in range(parts)
             ]
-            source, after = pair_parts, {1: 1, 2: 2}.get(len(pair_scores) - 1, 0)
+            source, after = pair_parts, {1: 2, 2: 1}.get(len(pair_scores) - 1, 0)
             if after:
                 source, states[after] = lax.optimization_barrier((pair_parts, states[after]))
             pair_scores[q, h] = lax.ppermute(source, ("cache", "pair"), perm)

time: 30.8 us -> 30.8 us (level)
  starting transfers between devices: 18.6 us -> 19.7 us
  waiting for transfers between devices: 4.08 us -> 3.23 us
    ppermute x10, waiting for transfers between devices: 4.07 us -> 2.71 us  [shift(): return lax.ppermute(x, axis, [(s, (s + step) % size) for s in range(size)])]
    ppermute x3, starting transfers between devices: 0.6 us -> 1.8 us  [body(): pair_scores[q, h] = lax.ppermute(source, ('cache', 'pair'), perm)]
    ppermute x3, waiting for transfers between devices: 0.01 us -> 0.52 us  [body(): pair_scores[q, h] = lax.ppermute(source, ('cache', 'pair'), perm)]
  transfers between devices with their start and end apart: 13 -> 13, of which waited for: 4 -> 6; matrix products, arithmetic and copies ran while one was open for 0% -> 0% of each run, Pallas kernels for 24% -> 23%
where the time goes in v34:
time: 30.8 us; the launch traced here: 30.7 us
  starting transfers between devices  19.7 us (64%)
  Pallas kernels  7.15 us (23%)
  waiting for transfers between devices  3.23 us (10%)
  other arithmetic  0.52 us (2%)
    ppermute x10, starting transfers between devices, shift(): return lax.ppermute(x, axis, [(s, (s + step) % size) for s in range(size)])  17.9 us
    pallas_call x1, Pallas kernels, body(): pl.pallas_call(pair_kernel, out_shape=jax.ShapeDtypeStruct((1, rows), jnp...  3.17 us
    ppermute x10, waiting for transfers between devices, shift(): return lax.ppermute(x, axis, [(s, (s + step) % size) for s in range(size)])  2.71 us
    pallas_call x1, Pallas kernels, body(): pl.pallas_call(turn_kernel, out_shape=(jax.ShapeDtypeStruct((width, rows)...  2.2 us
    ppermute x3, starting transfers between devices, body(): pair_scores[q, h] = lax.ppermute(source, ('cache', 'pair'), perm)  1.8 us
    pallas_call x1, Pallas kernels, body(): pl.pallas_call(functools.partial(linear_kernel, total, planes, cap, user_...  1.23 us
  transfers between devices with their start and end apart: 13, of which 6 were waited for; matrix products, arithmetic and copies ran while one was open for 0% of the time, Pallas kernels for 23%

profile of v34, /device:TPU:0, one launch (start us, length us, event | category | flops | bytes accessed | tf_op | source)
XLA Modules:
  0.0 30.7 jit_solution(6782896736988971503)
XLA Ops:
  0.0 2.9 %collective-permute-start.9 = (bf16[128,3072]{1,0:T(8,128)(2,1)}, bf16[128,3072]{1,0:T(8,128)(2,1)S(1)}, u32[]{:S(2)}, u32[]{:S(2)}) collective-permute-start(bf16[128,3072]{1,0:T(8,128)(2,1)} %refs_4_.1), channel_id=1, source_target_pairs={{0,2},{2,0},{1,3},{3,1},{4,6},{6,4},{5,7},{7,5},{8,10},{10,8},{9,1... | collective-permute-start | bytes 2359304 | tf_op jit(solution)/shard_map/item_rows/ppermute | solution.py:178
  2.9 1.6 %collective-permute-start = (s32[8]{0:T(128)}, s32[8]{0:T(128)S(1)}, u32[]{:S(2)}, u32[]{:S(2)}) collective-permute-start(s32[8]{0:T(128)} %param.7), channel_id=1, source_target_pairs={{0,4},{4,8},{8,12},{12,0},{1,5},{5,9},{9,13},{13,1},{2,6},{6,10},{... | collective-permute-start | bytes 104 | tf_op jit(solution)/shard_map/ids/ppermute | solution.py:178
  4.5 2.6 %collective-permute-start.1 = (s32[8]{0:T(128)}, s32[8]{0:T(128)S(1)}, u32[]{:S(2)}, u32[]{:S(2)}) collective-permute-start(s32[8]{0:T(128)} %param.7), channel_id=1, source_target_pairs={{0,8},{4,12},{8,0},{12,4},{1,9},{5,13},{9,1},{13,5},{2,10},{6,14},... | collective-permute-start | bytes 104 | tf_op jit(solution)/shard_map/ids/ppermute | solution.py:178
  7.1 1.3 %collective-permute-start.2 = (s32[8]{0:T(128)}, s32[8]{0:T(128)S(1)}, u32[]{:S(2)}, u32[]{:S(2)}) collective-permute-start(s32[8]{0:T(128)} %param.7), channel_id=1, source_target_pairs={{0,12},{4,0},{8,4},{12,8},{1,13},{5,1},{9,5},{13,9},{2,14},{6,2},{... | collective-permute-start | bytes 104 | tf_op jit(solution)/shard_map/ids/ppermute | solution.py:178
  8.5 2.2 %turn.1 = (f32[3072,128]{1,0:T(8,128)S(1)}, bf16[3072,128]{1,0:T(8,128)(2,1)S(1)}, bf16[64,64,256]{2,1,0:T(8,128)(2,1)S(1)}, bf16[128,3072]{1,0:T(8,128)(2,1)S(1...) custom-call(bf16[128,3072]{1,0:T(8,128)(2,1)} %refs_4_.1, bf16[64,64,256]{2,1,0:T(8,128)(2,1)} %bitcast.15, ...), custom_call_target="tpu_custom_call" | custom-call | flops 1610612736 | bytes 8388608 | tf_op jit(solution)/shard_map/turn/pallas_call | solution.py:206
  10.7 0.0 collective-permute-done
  10.7 0.0 collective-permute-done.1
  10.7 0.1 collective-permute-done.2
  10.8 0.4 %states.1.picked.refs_0_ = bf16[16,3200]{1,0:T(8,128)(2,1)S(1)} custom-call(s32[1,8]{1,0:T(1,128)S(1)} %get-tuple-element.24.refs_0_.refs_6_, s32[1,8]{1,0:T(1,128)S(1)} %bitcast.9, s32[1,8]{1,0:T(1,128)S(1)} %bitcast.11, s32[1,8]{1,0:T(1,128)S(1)} %bitcast.13, bf16[16,128]{1,0:T(8,128)(2,1)S(1)} %get-tuple-element.25.refs_4_, ...), custom_call_target="tpu_custom_call" | custom-call | flops 12582912 | bytes 1048576 | tf_op jit(solution)/shard_map/states/pallas_call | solution.py:235
  11.2 1.0 %collective-permute-start.4 = (bf16[16,3200]{1,0:T(8,128)(2,1)S(1)}, bf16[16,3200]{1,0:T(8,128)(2,1)S(1)}, u32[]{:S(2)}, u32[]{:S(2)}) collective-permute-start(bf16[16,3200]{1,0:T(8,128)(2,1)S(1)} %states.1.picked.refs_0_), channel_id=1, source_target_pairs={{0,8},{4,12},{8,0},{12,4},{1,9},{5,13},{9,1},{13,5},{2,10},{6,14},... | collective-permute-start | bytes 307208 | tf_op jit(solution)/shard_map/states/ppermute | solution.py:178
  12.1 2.8 %collective-permute-start.6 = (bf16[16,3200]{1,0:T(8,128)(2,1)S(1)}, bf16[16,3200]{1,0:T(8,128)(2,1)S(1)}, u32[]{:S(2)}, u32[]{:S(2)}) collective-permute-start(bf16[16,3200]{1,0:T(8,128)(2,1)S(1)} %states.1.picked.refs_0_), channel_id=1, source_target_pairs={{0,4},{4,8},{8,12},{12,0},{1,5},{5,9},{9,13},{13,1},{2,6},{6,10},{... | collective-permute-start | bytes 307208 | tf_op jit(solution)/shard_map/states/ppermute | solution.py:178
  14.9 1.0 %collective-permute-start.8 = (bf16[16,3200]{1,0:T(8,128)(2,1)S(1)}, bf16[16,3200]{1,0:T(8,128)(2,1)S(1)}, u32[]{:S(2)}, u32[]{:S(2)}) collective-permute-start(bf16[16,3200]{1,0:T(8,128)(2,1)S(1)} %states.1.picked.refs_0_), channel_id=1, source_target_pairs={{0,12},{4,0},{8,4},{12,8},{1,13},{5,1},{9,5},{13,9},{2,14},{6,2},{... | collective-permute-start | bytes 307208 | tf_op jit(solution)/shard_map/states/ppermute | solution.py:178
  16.0 0.0 copy-start
  16.0 3.2 %pairs.1.refs_1_ = f32[1,128]{1,0:T(1,128)S(1)} custom-call(s32[2,256]{1,0:T(2,128)} %bitcast.16, f32[3072,128]{1,0:T(8,128)S(1)} %get-tuple-element.21.rows32, bf16[3072,128]{1,0:T(8,128)(2,1)S(1)} %get-tuple-element.22.rows16, bf16[64,64,256]{2,1,0:T(8,128)(2,1)S(1)} %get-tuple-element.23.mats, bf16[16,3200]{1,0:T(8,128)(2,1)S(1)} %states.1.picked.refs_0_), custom_call_target="tpu_custom_call" | custom-call | flops 4294967296 | bytes 4194304 | tf_op jit(solution)/shard_map/pairs/pallas_call | solution.py:246
  19.1 0.6 %collective-permute-start.3 = (f32[1,128]{1,0:T(1,128)S(1)}, f32[1,128]{1,0:T(1,128)S(1)}, u32[]{:S(2)}, u32[]{:S(2)}) collective-permute-start(f32[1,128]{1,0:T(1,128)S(1)} %pairs.1.refs_1_), channel_id=1, source_target_pairs={{0,2},{1,3},{2,0},{3,1},{4,6},{5,7},{6,4},{7,5},{8,10},{9,11},{10,... | collective-permute-start | bytes 1544 | tf_op jit(solution)/shard_map/pairs/ppermute | solution.py:268
  19.7 0.4 %collective-permute-done.4.refs_2_ = bf16[16,3200]{1,0:T(8,128)(2,1)S(1)} collective-permute-done((bf16[16,3200]{1,0:T(8,128)(2,1)S(1)}, bf16[16,3200]{1,0:T(8,128)(2,1)S(1)}, u32[]{:S(2)}, u32[]{:S(2)}) %collective-permute-start.4) | collective-permute-done | bytes 102432 | tf_op jit(solution)/shard_map/states/ppermute | solution.py:178
  20.1 0.0 collective-permute-start.5
  20.2 0.0 collective-permute-done.6.refs_1_
  20.2 1.2 %collective-permute-start.7 = (f32[1,128]{1,0:T(1,128)S(1)}, f32[1,128]{1,0:T(1,128)S(1)}, u32[]{:S(2)}, u32[]{:S(2)}) collective-permute-start(f32[1,128]{1,0:T(1,128)S(1)} %pairs.1.refs_1_), channel_id=1, source_target_pairs={{0,1},{1,0},{2,3},{3,2},{4,5},{5,4},{6,7},{7,6},{8,9},{9,8},{10,11... | collective-permute-start | bytes 1544 | tf_op jit(solution)/shard_map/pairs/ppermute | solution.py:268
  21.4 0.0 collective-permute-done.8.refs_3_
  21.4 0.0 collective-permute-done.9.refs_5_
  21.4 0.0 copy-done
  21.4 1.2 %scores.2 = (f32[4,128]{1,0:T(4,128)S(1)}, bf16[256,512]{1,0:T(8,128)(2,1)S(1)}) custom-call(bf16[16,3200]{1,0:T(8,128)(2,1)S(1)} %states.1.picked.refs_0_, bf16[16,3200]{1,0:T(8,128)(2,1)S(1)} %collective-permute-done.6.refs_1_, bf16[16,3200]{1,0:T(8,128)(2,1)S(1)} %collective-permute-done.4.refs_2_, bf16[16,3200]{1,0:T(8,128)(2,1)S(1)} %collective-permute-done.8.refs_3_, ...), custom_call_target="tpu_custom_call" | custom-call | flops 100663296 | bytes 2097152 | tf_op jit(solution)/shard_map/scores/pallas_call | solution.py:272
  22.6 0.1 collective-permute-done.3.refs_0_
  22.7 0.4 %collective-permute-done.5.refs_2_ = f32[1,128]{1,0:T(1,128)S(1)} collective-permute-done((f32[1,128]{1,0:T(1,128)S(1)}, f32[1,128]{1,0:T(1,128)S(1)}, u32[]{:S(2)}, u32[]{:S(2)}) %collective-permute-start.5) | collective-permute-done | bytes 544 | tf_op jit(solution)/shard_map/pairs/ppermute | solution.py:268
  23.1 0.0 collective-permute-done.7.refs_3_
  23.1 0.2 scores.3
  23.3 0.9 %collective-permute-start.12 = (f32[1,128]{1,0:T(1,128)S(1)}, f32[1,128]{1,0:T(1,128)S(1)}, u32[]{:S(2)}, u32[]{:S(2)}) collective-permute-start(f32[1,128]{1,0:T(1,128)S(1)} %get-tuple-element.36), channel_id=1, source_target_pairs={{0,4},{4,8},{8,12},{12,0},{1,5},{5,9},{9,13},{13,1},{2,6},{6,10},{... | collective-permute-start | bytes 1544 | tf_op jit(solution)/shard_map/back/ppermute | solution.py:178
  24.2 2.4 %collective-permute-start.11 = (f32[1,128]{1,0:T(1,128)S(1)}, f32[1,128]{1,0:T(1,128)S(1)}, u32[]{:S(2)}, u32[]{:S(2)}) collective-permute-start(f32[1,128]{1,0:T(1,128)S(1)} %get-tuple-element.35), channel_id=1, source_target_pairs={{0,8},{4,12},{8,0},{12,4},{1,9},{5,13},{9,1},{13,5},{2,10},{6,14},... | collective-permute-start | bytes 1544 | tf_op jit(solution)/shard_map/back/ppermute | solution.py:178
  26.6 1.4 %collective-permute-start.10 = (f32[1,128]{1,0:T(1,128)S(1)}, f32[1,128]{1,0:T(1,128)S(1)}, u32[]{:S(2)}, u32[]{:S(2)}) collective-permute-start(f32[1,128]{1,0:T(1,128)S(1)} %get-tuple-element.34), channel_id=1, source_target_pairs={{0,12},{4,0},{8,4},{12,8},{1,13},{5,1},{9,5},{13,9},{2,14},{6,2},{... | collective-permute-start | bytes 1544 | tf_op jit(solution)/shard_map/back/ppermute | solution.py:178
  28.0 0.7 %collective-permute-done.12 = f32[1,128]{1,0:T(1,128)S(1)} collective-permute-done((f32[1,128]{1,0:T(1,128)S(1)}, f32[1,128]{1,0:T(1,128)S(1)}, u32[]{:S(2)}, u32[]{:S(2)}) %collective-permute-start.12) | collective-permute-done | bytes 544 | tf_op jit(solution)/shard_map/back/ppermute | solution.py:178
  28.7 0.0 collective-permute-done.11
  28.7 1.5 %collective-permute-done.10 = f32[1,128]{1,0:T(1,128)S(1)} collective-permute-done((f32[1,128]{1,0:T(1,128)S(1)}, f32[1,128]{1,0:T(1,128)S(1)}, u32[]{:S(2)}, u32[]{:S(2)}) %collective-permute-start.10) | collective-permute-done | bytes 544 | tf_op jit(solution)/shard_map/back/ppermute | solution.py:178
  30.1 0.5 %add_bitcast_fusion = f32[128]{0:T(128)} fusion(f32[1,128]{1,0:T(1,128)S(1)} %collective-permute-done.12, f32[1,128]{1,0:T(1,128)S(1)} %collective-permute-done.11, f32[1,128]{1,0:T(1,128)S(1)} %get-tuple-element.33, f32[1,128]{1,0:T(1,128)S(1)} %collective-permute-done.10), kind=kLoop, calls=%fused_computation | loop fusion | flops 384 | bytes 2560 | tf_op jit(solution)/shard_map/reshape | solution.py:300
Async XLA Ops:
  0.0 21.4 %collective-permute-start.9 = (bf16[128,3072]{1,0:T(8,128)(2,1)}, bf16[128,3072]{1,0:T(8,128)(2,1)S(1)}, u32[]{:S(2)}, u32[]{:S(2)}) collective-permute-start(bf16[128,3072]{1,0:T(8,128)(2,1)} %refs_4_.1), channel_id=1, source_target_pairs={{0,2},{2,0},{1,3},{3,1},{4,6},{6,4},{5,7},{7,5},{8,10},{10,8},{9,1... | collective-permute-start | bytes 2359304 | tf_op jit(solution)/shard_map/item_rows/ppermute | solution.py:178
  2.9 7.7 %collective-permute-start = (s32[8]{0:T(128)}, s32[8]{0:T(128)S(1)}, u32[]{:S(2)}, u32[]{:S(2)}) collective-permute-start(s32[8]{0:T(128)} %param.7), channel_id=1, source_target_pairs={{0,4},{4,8},{8,12},{12,0},{1,5},{5,9},{9,13},{13,1},{2,6},{6,10},{... | collective-permute-start | bytes 104 | tf_op jit(solution)/shard_map/ids/ppermute | solution.py:178
  4.5 6.2 %collective-permute-start.1 = (s32[8]{0:T(128)}, s32[8]{0:T(128)S(1)}, u32[]{:S(2)}, u32[]{:S(2)}) collective-permute-start(s32[8]{0:T(128)} %param.7), channel_id=1, source_target_pairs={{0,8},{4,12},{8,0},{12,4},{1,9},{5,13},{9,1},{13,5},{2,10},{6,14},... | collective-permute-start | bytes 104 | tf_op jit(solution)/shard_map/ids/ppermute | solution.py:178
  7.1 3.7 %collective-permute-start.2 = (s32[8]{0:T(128)}, s32[8]{0:T(128)S(1)}, u32[]{:S(2)}, u32[]{:S(2)}) collective-permute-start(s32[8]{0:T(128)} %param.7), channel_id=1, source_target_pairs={{0,12},{4,0},{8,4},{12,8},{1,13},{5,1},{9,5},{13,9},{2,14},{6,2},{... | collective-permute-start | bytes 104 | tf_op jit(solution)/shard_map/ids/ppermute | solution.py:178
  11.2 9.0 %collective-permute-start.4 = (bf16[16,3200]{1,0:T(8,128)(2,1)S(1)}, bf16[16,3200]{1,0:T(8,128)(2,1)S(1)}, u32[]{:S(2)}, u32[]{:S(2)}) collective-permute-start(bf16[16,3200]{1,0:T(8,128)(2,1)S(1)} %states.1.picked.refs_0_), channel_id=1, source_target_pairs={{0,8},{4,12},{8,0},{12,4},{1,9},{5,13},{9,1},{13,5},{2,10},{6,14},... | collective-permute-start | bytes 307208 | tf_op jit(solution)/shard_map/states/ppermute | solution.py:178
  12.1 8.0 %collective-permute-start.6 = (bf16[16,3200]{1,0:T(8,128)(2,1)S(1)}, bf16[16,3200]{1,0:T(8,128)(2,1)S(1)}, u32[]{:S(2)}, u32[]{:S(2)}) collective-permute-start(bf16[16,3200]{1,0:T(8,128)(2,1)S(1)} %states.1.picked.refs_0_), channel_id=1, source_target_pairs={{0,4},{4,8},{8,12},{12,0},{1,5},{5,9},{9,13},{13,1},{2,6},{6,10},{... | collective-permute-start | bytes 307208 | tf_op jit(solution)/shard_map/states/ppermute | solution.py:178
  14.9 6.4 %collective-permute-start.8 = (bf16[16,3200]{1,0:T(8,128)(2,1)S(1)}, bf16[16,3200]{1,0:T(8,128)(2,1)S(1)}, u32[]{:S(2)}, u32[]{:S(2)}) collective-permute-start(bf16[16,3200]{1,0:T(8,128)(2,1)S(1)} %states.1.picked.refs_0_), channel_id=1, source_target_pairs={{0,12},{4,0},{8,4},{12,8},{1,13},{5,1},{9,5},{13,9},{2,14},{6,2},{... | collective-permute-start | bytes 307208 | tf_op jit(solution)/shard_map/states/ppermute | solution.py:178
  16.0 5.4 %copy-start = (bf16[128,3072]{1,0:T(8,128)(2,1)S(1)}, bf16[128,3072]{1,0:T(8,128)(2,1)}, u32[]{:S(2)}) copy-start(bf16[128,3072]{1,0:T(8,128)(2,1)} %refs_4_.1) | copy-start | bytes 2359300
  19.1 3.6 %collective-permute-start.3 = (f32[1,128]{1,0:T(1,128)S(1)}, f32[1,128]{1,0:T(1,128)S(1)}, u32[]{:S(2)}, u32[]{:S(2)}) collective-permute-start(f32[1,128]{1,0:T(1,128)S(1)} %pairs.1.refs_1_), channel_id=1, source_target_pairs={{0,2},{1,3},{2,0},{3,1},{4,6},{5,7},{6,4},{7,5},{8,10},{9,11},{10,... | collective-permute-start | bytes 1544 | tf_op jit(solution)/shard_map/pairs/ppermute | solution.py:268
  20.1 3.0 %collective-permute-start.5 = (f32[1,128]{1,0:T(1,128)S(1)}, f32[1,128]{1,0:T(1,128)S(1)}, u32[]{:S(2)}, u32[]{:S(2)}) collective-permute-start(f32[1,128]{1,0:T(1,128)S(1)} %pairs.1.refs_1_), channel_id=1, source_target_pairs={{0,3},{1,2},{2,1},{3,0},{4,7},{5,6},{6,5},{7,4},{8,11},{9,10},{10,... | collective-permute-start | bytes 1544 | tf_op jit(solution)/shard_map/pairs/ppermute | solution.py:268
  20.2 3.0 %collective-permute-start.7 = (f32[1,128]{1,0:T(1,128)S(1)}, f32[1,128]{1,0:T(1,128)S(1)}, u32[]{:S(2)}, u32[]{:S(2)}) collective-permute-start(f32[1,128]{1,0:T(1,128)S(1)} %pairs.1.refs_1_), channel_id=1, source_target_pairs={{0,1},{1,0},{2,3},{3,2},{4,5},{5,4},{6,7},{7,6},{8,9},{9,8},{10,11... | collective-permute-start | bytes 1544 | tf_op jit(solution)/shard_map/pairs/ppermute | solution.py:268
  23.3 5.4 %collective-permute-start.12 = (f32[1,128]{1,0:T(1,128)S(1)}, f32[1,128]{1,0:T(1,128)S(1)}, u32[]{:S(2)}, u32[]{:S(2)}) collective-permute-start(f32[1,128]{1,0:T(1,128)S(1)} %get-tuple-element.36), channel_id=1, source_target_pairs={{0,4},{4,8},{8,12},{12,0},{1,5},{5,9},{9,13},{13,1},{2,6},{6,10},{... | collective-permute-start | bytes 1544 | tf_op jit(solution)/shard_map/back/ppermute | solution.py:178
  24.2 4.5 %collective-permute-start.11 = (f32[1,128]{1,0:T(1,128)S(1)}, f32[1,128]{1,0:T(1,128)S(1)}, u32[]{:S(2)}, u32[]{:S(2)}) collective-permute-start(f32[1,128]{1,0:T(1,128)S(1)} %get-tuple-element.35), channel_id=1, source_target_pairs={{0,8},{4,12},{8,0},{12,4},{1,9},{5,13},{9,1},{13,5},{2,10},{6,14},... | collective-permute-start | bytes 1544 | tf_op jit(solution)/shard_map/back/ppermute | solution.py:178
  26.6 3.5 %collective-permute-start.10 = (f32[1,128]{1,0:T(1,128)S(1)}, f32[1,128]{1,0:T(1,128)S(1)}, u32[]{:S(2)}, u32[]{:S(2)}) collective-permute-start(f32[1,128]{1,0:T(1,128)S(1)} %get-tuple-element.34), channel_id=1, source_target_pairs={{0,12},{4,0},{8,4},{12,8},{1,13},{5,1},{9,5},{13,9},{2,14},{6,2},{... | collective-permute-start | bytes 1544 | tf_op jit(solution)/shard_map/back/ppermute | solution.py:178

commit v35 on v32

--- a/solution.py
+++ b/solution.py
@@ -301,7 +301,7 @@
 
     with jax.named_scope("back"):
         result = outs[0]
-        for j in sorted(range(1, total), key=lambda step: (step == 1, step)):
+        for j in sorted(range(1, total), key=lambda step: (step + 1) % total):
             result = result + shift(outs[j], "shard", -j)
     return result.reshape(half)
 

time: 31.7 us -> 32.6 us (1.028)
  waiting for transfers between devices: 6.22 us -> 7.11 us
    ppermute x10, waiting for transfers between devices: 6.04 us -> 6.93 us  [shift(): return lax.ppermute(x, axis, [(s, (s + step) % size) for s in range(size)])]
  transfers between devices with their start and end apart: 13 -> 13, of which waited for: 4 -> 5; matrix products, arithmetic and copies ran while one was open for 0% -> 0% of each run, Pallas kernels for 21% -> 21%
where the time goes in v35:
time: 32.6 us; the launch traced here: 32.5 us
  starting transfers between devices  17.8 us (55%)
  waiting for transfers between devices  7.11 us (22%)
  Pallas kernels  6.89 us (21%)
  other arithmetic  0.52 us (2%)
    ppermute x10, starting transfers between devices, shift(): return lax.ppermute(x, axis, [(s, (s + step) % size) for s in range(size)])  17.2 us
    ppermute x10, waiting for transfers between devices, shift(): return lax.ppermute(x, axis, [(s, (s + step) % size) for s in range(size)])  6.93 us
    pallas_call x1, Pallas kernels, body(): pl.pallas_call(functools.partial(pair_kernel, total, cap, slots, user_sta...  3.23 us
    pallas_call x1, Pallas kernels, body(): pl.pallas_call(turn_kernel, out_shape=(jax.ShapeDtypeStruct((width, rows)...  2.2 us
    pallas_call x1, Pallas kernels, body(): pl.pallas_call(functools.partial(linear_kernel, total, planes), out_shape...  0.9 us
  transfers between devices with their start and end apart: 13, of which 5 were waited for; matrix products, arithmetic and copies ran while one was open for 0% of the time, Pallas kernels for 21%

profile of v35, /device:TPU:0, one launch (start us, length us, event | category | flops | bytes accessed | tf_op | source)
XLA Modules:
  0.0 32.5 jit_solution(10188425883288990750)
XLA Ops:
  0.0 2.9 %collective-permute-start.9 = (bf16[128,3072]{1,0:T(8,128)(2,1)}, bf16[128,3072]{1,0:T(8,128)(2,1)S(1)}, u32[]{:S(2)}, u32[]{:S(2)}) collective-permute-start(bf16[128,3072]{1,0:T(8,128)(2,1)} %refs_4_.1), channel_id=1, source_target_pairs={{0,2},{2,0},{1,3},{3,1},{4,6},{6,4},{5,7},{7,5},{8,10},{10,8},{9,1... | collective-permute-start | bytes 2359304 | tf_op jit(solution)/shard_map/item_rows/ppermute | solution.py:181
  2.9 1.6 %collective-permute-start = (s32[8]{0:T(128)}, s32[8]{0:T(128)S(1)}, u32[]{:S(2)}, u32[]{:S(2)}) collective-permute-start(s32[8]{0:T(128)} %param.7), channel_id=1, source_target_pairs={{0,4},{4,8},{8,12},{12,0},{1,5},{5,9},{9,13},{13,1},{2,6},{6,10},{... | collective-permute-start | bytes 104 | tf_op jit(solution)/shard_map/ids/ppermute | solution.py:181
  4.5 2.6 %collective-permute-start.1 = (s32[8]{0:T(128)}, s32[8]{0:T(128)S(1)}, u32[]{:S(2)}, u32[]{:S(2)}) collective-permute-start(s32[8]{0:T(128)} %param.7), channel_id=1, source_target_pairs={{0,8},{4,12},{8,0},{12,4},{1,9},{5,13},{9,1},{13,5},{2,10},{6,14},... | collective-permute-start | bytes 104 | tf_op jit(solution)/shard_map/ids/ppermute | solution.py:181
  7.1 1.3 %collective-permute-start.2 = (s32[8]{0:T(128)}, s32[8]{0:T(128)S(1)}, u32[]{:S(2)}, u32[]{:S(2)}) collective-permute-start(s32[8]{0:T(128)} %param.7), channel_id=1, source_target_pairs={{0,12},{4,0},{8,4},{12,8},{1,13},{5,1},{9,5},{13,9},{2,14},{6,2},{... | collective-permute-start | bytes 104 | tf_op jit(solution)/shard_map/ids/ppermute | solution.py:181
  8.5 2.2 %turn.1 = (f32[3072,128]{1,0:T(8,128)S(1)}, bf16[3072,128]{1,0:T(8,128)(2,1)S(1)}, bf16[64,64,256]{2,1,0:T(8,128)(2,1)S(1)}, bf16[128,3072]{1,0:T(8,128)(2,1)S(1...) custom-call(bf16[128,3072]{1,0:T(8,128)(2,1)} %refs_4_.1, bf16[64,64,256]{2,1,0:T(8,128)(2,1)} %bitcast.15, ...), custom_call_target="tpu_custom_call" | custom-call | flops 1610612736 | bytes 8388608 | tf_op jit(solution)/shard_map/turn/pallas_call | solution.py:209
  10.7 0.0 collective-permute-done
  10.7 0.0 collective-permute-done.1
  10.7 0.1 collective-permute-done.2
  10.8 0.4 %states.1.refs_8_.refs_0_ = bf16[16,3200]{1,0:T(8,128)(2,1)S(1)} custom-call(s32[1,8]{1,0:T(1,128)S(1)} %get-tuple-element.23.refs_0_, s32[1,8]{1,0:T(1,128)S(1)} %bitcast.9, s32[1,8]{1,0:T(1,128)S(1)} %bitcast.11, s32[1,8]{1,0:T(1,128)S(1)} %bitcast.13, bf16[16,128]{1,0:T(8,128)(2,1)S(1)} %get-tuple-element.27.refs_4_, ...), custom_call_target="tpu_custom_call" | custom-call | flops 12582912 | bytes 1048576 | tf_op jit(solution)/shard_map/states/pallas_call | solution.py:238
  11.2 0.6 %collective-permute-start.4 = (bf16[16,3200]{1,0:T(8,128)(2,1)S(1)}, bf16[16,3200]{1,0:T(8,128)(2,1)S(1)}, u32[]{:S(2)}, u32[]{:S(2)}) collective-permute-start(bf16[16,3200]{1,0:T(8,128)(2,1)S(1)} %states.1.refs_8_.refs_0_), channel_id=1, source_target_pairs={{0,4},{4,8},{8,12},{12,0},{1,5},{5,9},{9,13},{13,1},{2,6},{6,10},{... | collective-permute-start | bytes 307208 | tf_op jit(solution)/shard_map/states/ppermute | solution.py:181
  11.8 3.1 %collective-permute-start.6 = (bf16[16,3200]{1,0:T(8,128)(2,1)S(1)}, bf16[16,3200]{1,0:T(8,128)(2,1)S(1)}, u32[]{:S(2)}, u32[]{:S(2)}) collective-permute-start(bf16[16,3200]{1,0:T(8,128)(2,1)S(1)} %states.1.refs_8_.refs_0_), channel_id=1, source_target_pairs={{0,8},{4,12},{8,0},{12,4},{1,9},{5,13},{9,1},{13,5},{2,10},{6,14},... | collective-permute-start | bytes 307208 | tf_op jit(solution)/shard_map/states/ppermute | solution.py:181
  14.9 0.1 collective-permute-start.8
  15.1 0.0 copy-start
  15.1 3.2 %pairs.1 = (f32[1,128]{1,0:T(1,128)S(1)}, s32[4,128]{1,0:T(4,128)S(1)}) custom-call(s32[1,8]{1,0:T(1,128)S(1)} %get-tuple-element.23.refs_0_, s32[1,8]{1,0:T(1,128)S(1)} %bitcast.10, s32[1,8]{1,0:T(1,128)S(1)} %bitcast.12, s32[1,8]{1,0:T(1,128)S(1)} %bitcast.14, s32[2,256]{1,0:T(2,128)} %bitcast.16, f32[3072,128]{1,0:T(8,128)S(1)} %get-tuple-element.24.refs_5_, ...), custom_call_target="tpu_custom_call" | custom-call | flops 4294967296 | bytes 4194304 | tf_op jit(solution)/shard_map/pairs/pallas_call | solution.py:249
  18.3 0.6 %collective-permute-start.3 = (f32[1,128]{1,0:T(1,128)S(1)}, f32[1,128]{1,0:T(1,128)S(1)}, u32[]{:S(2)}, u32[]{:S(2)}) collective-permute-start(f32[1,128]{1,0:T(1,128)S(1)} %get-tuple-element.31.refs_1_), channel_id=1, source_target_pairs={{0,2},{1,3},{2,0},{3,1},{4,6},{5,7},{6,4},{7,5},{8,10},{9,11},{10,... | collective-permute-start | bytes 1544 | tf_op jit(solution)/shard_map/pairs/ppermute | solution.py:274
  18.9 0.0 collective-permute-done.4.refs_1_
  18.9 0.0 collective-permute-start.5
  18.9 2.1 %collective-permute-done.6.refs_2_ = bf16[16,3200]{1,0:T(8,128)(2,1)S(1)} collective-permute-done((bf16[16,3200]{1,0:T(8,128)(2,1)S(1)}, bf16[16,3200]{1,0:T(8,128)(2,1)S(1)}, u32[]{:S(2)}, u32[]{:S(2)}) %collective-permute-start.6) | collective-permute-done | bytes 102432 | tf_op jit(solution)/shard_map/states/ppermute | solution.py:181
  21.0 0.0 collective-permute-start.7
  21.0 0.0 collective-permute-done.8.refs_3_
  21.0 0.0 collective-permute-done.9.refs_5_
  21.0 0.0 copy-done
  21.0 0.9 %scores.2 = (f32[4,128]{1,0:T(4,128)S(1)}, bf16[256,512]{1,0:T(8,128)(2,1)S(1)}) custom-call(bf16[16,3200]{1,0:T(8,128)(2,1)S(1)} %states.1.refs_8_.refs_0_, bf16[16,3200]{1,0:T(8,128)(2,1)S(1)} %collective-permute-done.4.refs_1_, bf16[16,3200]{1,0:T(8,128)(2,1)S(1)} %collective-permute-done.6.refs_2_, bf16[16,3200]{1,0:T(8,128)(2,1)S(1)} %collective-permute-done.8.refs_3_, ...), custom_call_target="tpu_custom_call" | custom-call | flops 100663296 | bytes 2097152 | tf_op jit(solution)/shard_map/scores/pallas_call | solution.py:278
  21.9 0.0 collective-permute-done.3.refs_0_
  21.9 0.0 collective-permute-done.5.refs_2_
  21.9 0.2 collective-permute-done.7.refs_3_
  22.1 0.2 scores.3
  22.3 2.9 %collective-permute-start.12 = (f32[1,128]{1,0:T(1,128)S(1)}, f32[1,128]{1,0:T(1,128)S(1)}, u32[]{:S(2)}, u32[]{:S(2)}) collective-permute-start(f32[1,128]{1,0:T(1,128)S(1)} %get-tuple-element.40), channel_id=1, source_target_pairs={{0,8},{4,12},{8,0},{12,4},{1,9},{5,13},{9,1},{13,5},{2,10},{6,14},... | collective-permute-start | bytes 1544 | tf_op jit(solution)/shard_map/back/ppermute | solution.py:181
  25.2 1.4 %collective-permute-start.11 = (f32[1,128]{1,0:T(1,128)S(1)}, f32[1,128]{1,0:T(1,128)S(1)}, u32[]{:S(2)}, u32[]{:S(2)}) collective-permute-start(f32[1,128]{1,0:T(1,128)S(1)} %get-tuple-element.39), channel_id=1, source_target_pairs={{0,12},{4,0},{8,4},{12,8},{1,13},{5,1},{9,5},{13,9},{2,14},{6,2},{... | collective-permute-start | bytes 1544 | tf_op jit(solution)/shard_map/back/ppermute | solution.py:181
  26.6 0.6 %collective-permute-start.10 = (f32[1,128]{1,0:T(1,128)S(1)}, f32[1,128]{1,0:T(1,128)S(1)}, u32[]{:S(2)}, u32[]{:S(2)}) collective-permute-start(f32[1,128]{1,0:T(1,128)S(1)} %get-tuple-element.38), channel_id=1, source_target_pairs={{0,4},{4,8},{8,12},{12,0},{1,5},{5,9},{9,13},{13,1},{2,6},{6,10},{... | collective-permute-start | bytes 1544 | tf_op jit(solution)/shard_map/back/ppermute | solution.py:181
  27.2 0.0 collective-permute-done.12
  27.2 1.5 %collective-permute-done.11 = f32[1,128]{1,0:T(1,128)S(1)} collective-permute-done((f32[1,128]{1,0:T(1,128)S(1)}, f32[1,128]{1,0:T(1,128)S(1)}, u32[]{:S(2)}, u32[]{:S(2)}) %collective-permute-start.11) | collective-permute-done | bytes 544 | tf_op jit(solution)/shard_map/back/ppermute | solution.py:181
  28.7 3.2 %collective-permute-done.10 = f32[1,128]{1,0:T(1,128)S(1)} collective-permute-done((f32[1,128]{1,0:T(1,128)S(1)}, f32[1,128]{1,0:T(1,128)S(1)}, u32[]{:S(2)}, u32[]{:S(2)}) %collective-permute-start.10) | collective-permute-done | bytes 544 | tf_op jit(solution)/shard_map/back/ppermute | solution.py:181
  31.9 0.5 %add_bitcast_fusion = f32[128]{0:T(128)} fusion(f32[1,128]{1,0:T(1,128)S(1)} %collective-permute-done.12, f32[1,128]{1,0:T(1,128)S(1)} %collective-permute-done.11, f32[1,128]{1,0:T(1,128)S(1)} %get-tuple-element.37, f32[1,128]{1,0:T(1,128)S(1)} %collective-permute-done.10), kind=kLoop, calls=%fused_computation | loop fusion | flops 384 | bytes 2560 | tf_op jit(solution)/shard_map/reshape | solution.py:306
Async XLA Ops:
  0.0 21.0 %collective-permute-start.9 = (bf16[128,3072]{1,0:T(8,128)(2,1)}, bf16[128,3072]{1,0:T(8,128)(2,1)S(1)}, u32[]{:S(2)}, u32[]{:S(2)}) collective-permute-start(bf16[128,3072]{1,0:T(8,128)(2,1)} %refs_4_.1), channel_id=1, source_target_pairs={{0,2},{2,0},{1,3},{3,1},{4,6},{6,4},{5,7},{7,5},{8,10},{10,8},{9,1... | collective-permute-start | bytes 2359304 | tf_op jit(solution)/shard_map/item_rows/ppermute | solution.py:181
  2.9 7.7 %collective-permute-start = (s32[8]{0:T(128)}, s32[8]{0:T(128)S(1)}, u32[]{:S(2)}, u32[]{:S(2)}) collective-permute-start(s32[8]{0:T(128)} %param.7), channel_id=1, source_target_pairs={{0,4},{4,8},{8,12},{12,0},{1,5},{5,9},{9,13},{13,1},{2,6},{6,10},{... | collective-permute-start | bytes 104 | tf_op jit(solution)/shard_map/ids/ppermute | solution.py:181
  4.5 6.2 %collective-permute-start.1 = (s32[8]{0:T(128)}, s32[8]{0:T(128)S(1)}, u32[]{:S(2)}, u32[]{:S(2)}) collective-permute-start(s32[8]{0:T(128)} %param.7), channel_id=1, source_target_pairs={{0,8},{4,12},{8,0},{12,4},{1,9},{5,13},{9,1},{13,5},{2,10},{6,14},... | collective-permute-start | bytes 104 | tf_op jit(solution)/shard_map/ids/ppermute | solution.py:181
  7.1 3.7 %collective-permute-start.2 = (s32[8]{0:T(128)}, s32[8]{0:T(128)S(1)}, u32[]{:S(2)}, u32[]{:S(2)}) collective-permute-start(s32[8]{0:T(128)} %param.7), channel_id=1, source_target_pairs={{0,12},{4,0},{8,4},{12,8},{1,13},{5,1},{9,5},{13,9},{2,14},{6,2},{... | collective-permute-start | bytes 104 | tf_op jit(solution)/shard_map/ids/ppermute | solution.py:181
  11.2 7.7 %collective-permute-start.4 = (bf16[16,3200]{1,0:T(8,128)(2,1)S(1)}, bf16[16,3200]{1,0:T(8,128)(2,1)S(1)}, u32[]{:S(2)}, u32[]{:S(2)}) collective-permute-start(bf16[16,3200]{1,0:T(8,128)(2,1)S(1)} %states.1.refs_8_.refs_0_), channel_id=1, source_target_pairs={{0,4},{4,8},{8,12},{12,0},{1,5},{5,9},{9,13},{13,1},{2,6},{6,10},{... | collective-permute-start | bytes 307208 | tf_op jit(solution)/shard_map/states/ppermute | solution.py:181
  11.8 9.2 %collective-permute-start.6 = (bf16[16,3200]{1,0:T(8,128)(2,1)S(1)}, bf16[16,3200]{1,0:T(8,128)(2,1)S(1)}, u32[]{:S(2)}, u32[]{:S(2)}) collective-permute-start(bf16[16,3200]{1,0:T(8,128)(2,1)S(1)} %states.1.refs_8_.refs_0_), channel_id=1, source_target_pairs={{0,8},{4,12},{8,0},{12,4},{1,9},{5,13},{9,1},{13,5},{2,10},{6,14},... | collective-permute-start | bytes 307208 | tf_op jit(solution)/shard_map/states/ppermute | solution.py:181
  14.9 6.1 %collective-permute-start.8 = (bf16[16,3200]{1,0:T(8,128)(2,1)S(1)}, bf16[16,3200]{1,0:T(8,128)(2,1)S(1)}, u32[]{:S(2)}, u32[]{:S(2)}) collective-permute-start(bf16[16,3200]{1,0:T(8,128)(2,1)S(1)} %states.1.refs_8_.refs_0_), channel_id=1, source_target_pairs={{0,12},{4,0},{8,4},{12,8},{1,13},{5,1},{9,5},{13,9},{2,14},{6,2},{... | collective-permute-start | bytes 307208 | tf_op jit(solution)/shard_map/states/ppermute | solution.py:181
  15.1 6.0 %copy-start = (bf16[128,3072]{1,0:T(8,128)(2,1)S(1)}, bf16[128,3072]{1,0:T(8,128)(2,1)}, u32[]{:S(2)}) copy-start(bf16[128,3072]{1,0:T(8,128)(2,1)} %refs_4_.1) | copy-start | bytes 2359300
  18.3 3.6 %collective-permute-start.3 = (f32[1,128]{1,0:T(1,128)S(1)}, f32[1,128]{1,0:T(1,128)S(1)}, u32[]{:S(2)}, u32[]{:S(2)}) collective-permute-start(f32[1,128]{1,0:T(1,128)S(1)} %get-tuple-element.31.refs_1_), channel_id=1, source_target_pairs={{0,2},{1,3},{2,0},{3,1},{4,6},{5,7},{6,4},{7,5},{8,10},{9,11},{10,... | collective-permute-start | bytes 1544 | tf_op jit(solution)/shard_map/pairs/ppermute | solution.py:274
  18.9 3.0 %collective-permute-start.5 = (f32[1,128]{1,0:T(1,128)S(1)}, f32[1,128]{1,0:T(1,128)S(1)}, u32[]{:S(2)}, u32[]{:S(2)}) collective-permute-start(f32[1,128]{1,0:T(1,128)S(1)} %get-tuple-element.31.refs_1_), channel_id=1, source_target_pairs={{0,3},{1,2},{2,1},{3,0},{4,7},{5,6},{6,5},{7,4},{8,11},{9,10},{10,... | collective-permute-start | bytes 1544 | tf_op jit(solution)/shard_map/pairs/ppermute | solution.py:274
  21.0 1.1 %collective-permute-start.7 = (f32[1,128]{1,0:T(1,128)S(1)}, f32[1,128]{1,0:T(1,128)S(1)}, u32[]{:S(2)}, u32[]{:S(2)}) collective-permute-start(f32[1,128]{1,0:T(1,128)S(1)} %get-tuple-element.31.refs_1_), channel_id=1, source_target_pairs={{0,1},{1,0},{2,3},{3,2},{4,5},{5,4},{6,7},{7,6},{8,9},{9,8},{10,11... | collective-permute-start | bytes 1544 | tf_op jit(solution)/shard_map/pairs/ppermute | solution.py:274
  22.3 4.9 %collective-permute-start.12 = (f32[1,128]{1,0:T(1,128)S(1)}, f32[1,128]{1,0:T(1,128)S(1)}, u32[]{:S(2)}, u32[]{:S(2)}) collective-permute-start(f32[1,128]{1,0:T(1,128)S(1)} %get-tuple-element.40), channel_id=1, source_target_pairs={{0,8},{4,12},{8,0},{12,4},{1,9},{5,13},{9,1},{13,5},{2,10},{6,14},... | collective-permute-start | bytes 1544 | tf_op jit(solution)/shard_map/back/ppermute | solution.py:181
  25.2 3.5 %collective-permute-start.11 = (f32[1,128]{1,0:T(1,128)S(1)}, f32[1,128]{1,0:T(1,128)S(1)}, u32[]{:S(2)}, u32[]{:S(2)}) collective-permute-start(f32[1,128]{1,0:T(1,128)S(1)} %get-tuple-element.39), channel_id=1, source_target_pairs={{0,12},{4,0},{8,4},{12,8},{1,13},{5,1},{9,5},{13,9},{2,14},{6,2},{... | collective-permute-start | bytes 1544 | tf_op jit(solution)/shard_map/back/ppermute | solution.py:181
  26.6 5.3 %collective-permute-start.10 = (f32[1,128]{1,0:T(1,128)S(1)}, f32[1,128]{1,0:T(1,128)S(1)}, u32[]{:S(2)}, u32[]{:S(2)}) collective-permute-start(f32[1,128]{1,0:T(1,128)S(1)} %get-tuple-element.38), channel_id=1, source_target_pairs={{0,4},{4,8},{8,12},{12,0},{1,5},{5,9},{9,13},{13,1},{2,6},{6,10},{... | collective-permute-start | bytes 1544 | tf_op jit(solution)/shard_map/back/ppermute | solution.py:181

commit v36 on v33

--- a/solution.py
+++ b/solution.py
@@ -120,7 +120,7 @@
         )
         return total + dot(left, right, NN) * jnp.concatenate([rows32[pl.ds(a, K), :] for a, _ in fields_of], axis=1)
 
-    sums = lax.fori_loop(0, steps, two, jnp.zeros((K, 2 * items), jnp.float32), unroll=64)
+    sums = lax.fori_loop(0, steps, two, jnp.zeros((K, 2 * items), jnp.float32), unroll=128)
     line = jnp.sum(sums, axis=0, keepdims=True)
     out[...] = line[:, :items] + line[:, items:]
 

time: 30.5 us -> 30.5 us (level)
  waiting for transfers between devices: 3.44 us -> 4.17 us
  Pallas kernels: 6.88 us -> 6.51 us
    ppermute x3, waiting for transfers between devices: 0.79 us -> 1.16 us  [body(): pair_scores[q, h] = lax.ppermute(source, ('cache', 'pair'), perm)]
    ppermute x10, waiting for transfers between devices: 2.64 us -> 3.01 us  [shift(): return lax.ppermute(x, axis, [(s, (s + step) % size) for s in range(size)])]
    pallas_call x1, Pallas kernels: 3.23 us -> 2.87 us  [body(): pl.pallas_call(functools.partial(pair_kernel, total, cap, slots, user_sta...]
    ppermute x3, starting transfers between devices: 1.87 us -> 1.51 us  [body(): pair_scores[q, h] = lax.ppermute(source, ('cache', 'pair'), perm)]
  transfers between devices with their start and end apart: 13 -> 13, of which waited for: 6 -> 6; matrix products, arithmetic and copies ran while one was open for 0% -> 0% of each run, Pallas kernels for 22% -> 21%
where the time goes in v36:
time: 30.5 us; the launch traced here: 30.3 us
  starting transfers between devices  19.1 us (63%)
  Pallas kernels  6.51 us (21%)
  waiting for transfers between devices  4.17 us (14%)
  other arithmetic  0.52 us (2%)
    ppermute x10, starting transfers between devices, shift(): return lax.ppermute(x, axis, [(s, (s + step) % size) for s in range(size)])  17.5 us
    ppermute x10, waiting for transfers between devices, shift(): return lax.ppermute(x, axis, [(s, (s + step) % size) for s in range(size)])  3.01 us
    pallas_call x1, Pallas kernels, body(): pl.pallas_call(functools.partial(pair_kernel, total, cap, slots, user_sta...  2.87 us
    pallas_call x1, Pallas kernels, body(): pl.pallas_call(turn_kernel, out_shape=(jax.ShapeDtypeStruct((width, rows)...  2.2 us
    ppermute x3, starting transfers between devices, body(): pair_scores[q, h] = lax.ppermute(source, ('cache', 'pair'), perm)  1.51 us
    ppermute x3, waiting for transfers between devices, body(): pair_scores[q, h] = lax.ppermute(source, ('cache', 'pair'), perm)  1.16 us
    pallas_call x1, Pallas kernels, body(): pl.pallas_call(functools.partial(linear_kernel, total, planes), out_shape...  0.88 us
  transfers between devices with their start and end apart: 13, of which 6 were waited for; matrix products, arithmetic and copies ran while one was open for 0% of the time, Pallas kernels for 21%

profile of v36, /device:TPU:0, one launch (start us, length us, event | category | flops | bytes accessed | tf_op | source)
XLA Modules:
  0.0 30.3 jit_solution(3054651973543080656)
XLA Ops:
  0.0 2.9 %collective-permute-start.9 = (bf16[128,3072]{1,0:T(8,128)(2,1)}, bf16[128,3072]{1,0:T(8,128)(2,1)S(1)}, u32[]{:S(2)}, u32[]{:S(2)}) collective-permute-start(bf16[128,3072]{1,0:T(8,128)(2,1)} %refs_4_.1), channel_id=1, source_target_pairs={{0,2},{2,0},{1,3},{3,1},{4,6},{6,4},{5,7},{7,5},{8,10},{10,8},{9,1... | collective-permute-start | bytes 2359304 | tf_op jit(solution)/shard_map/item_rows/ppermute | solution.py:181
  2.9 1.6 %collective-permute-start = (s32[8]{0:T(128)}, s32[8]{0:T(128)S(1)}, u32[]{:S(2)}, u32[]{:S(2)}) collective-permute-start(s32[8]{0:T(128)} %param.7), channel_id=1, source_target_pairs={{0,4},{4,8},{8,12},{12,0},{1,5},{5,9},{9,13},{13,1},{2,6},{6,10},{... | collective-permute-start | bytes 104 | tf_op jit(solution)/shard_map/ids/ppermute | solution.py:181
  4.5 2.6 %collective-permute-start.1 = (s32[8]{0:T(128)}, s32[8]{0:T(128)S(1)}, u32[]{:S(2)}, u32[]{:S(2)}) collective-permute-start(s32[8]{0:T(128)} %param.7), channel_id=1, source_target_pairs={{0,8},{4,12},{8,0},{12,4},{1,9},{5,13},{9,1},{13,5},{2,10},{6,14},... | collective-permute-start | bytes 104 | tf_op jit(solution)/shard_map/ids/ppermute | solution.py:181
  7.1 1.3 %collective-permute-start.2 = (s32[8]{0:T(128)}, s32[8]{0:T(128)S(1)}, u32[]{:S(2)}, u32[]{:S(2)}) collective-permute-start(s32[8]{0:T(128)} %param.7), channel_id=1, source_target_pairs={{0,12},{4,0},{8,4},{12,8},{1,13},{5,1},{9,5},{13,9},{2,14},{6,2},{... | collective-permute-start | bytes 104 | tf_op jit(solution)/shard_map/ids/ppermute | solution.py:181
  8.5 2.2 %turn.1 = (f32[3072,128]{1,0:T(8,128)S(1)}, bf16[3072,128]{1,0:T(8,128)(2,1)S(1)}, bf16[64,64,256]{2,1,0:T(8,128)(2,1)S(1)}, bf16[128,3072]{1,0:T(8,128)(2,1)S(1...) custom-call(bf16[128,3072]{1,0:T(8,128)(2,1)} %refs_4_.1, bf16[64,64,256]{2,1,0:T(8,128)(2,1)} %bitcast.15, ...), custom_call_target="tpu_custom_call" | custom-call | flops 1610612736 | bytes 8388608 | tf_op jit(solution)/shard_map/turn/pallas_call | solution.py:209
  10.7 0.0 collective-permute-done
  10.7 0.0 collective-permute-done.1
  10.7 0.1 collective-permute-done.2
  10.8 0.4 %states.1.refs_8_.refs_0_ = bf16[16,3200]{1,0:T(8,128)(2,1)S(1)} custom-call(s32[1,8]{1,0:T(1,128)S(1)} %get-tuple-element.23.refs_0_, s32[1,8]{1,0:T(1,128)S(1)} %bitcast.9, s32[1,8]{1,0:T(1,128)S(1)} %bitcast.11, s32[1,8]{1,0:T(1,128)S(1)} %bitcast.13, bf16[16,128]{1,0:T(8,128)(2,1)S(1)} %get-tuple-element.27.refs_4_, ...), custom_call_target="tpu_custom_call" | custom-call | flops 12582912 | bytes 1048576 | tf_op jit(solution)/shard_map/states/pallas_call | solution.py:238
  11.2 1.0 %collective-permute-start.4 = (bf16[16,3200]{1,0:T(8,128)(2,1)S(1)}, bf16[16,3200]{1,0:T(8,128)(2,1)S(1)}, u32[]{:S(2)}, u32[]{:S(2)}) collective-permute-start(bf16[16,3200]{1,0:T(8,128)(2,1)S(1)} %states.1.refs_8_.refs_0_), channel_id=1, source_target_pairs={{0,8},{4,12},{8,0},{12,4},{1,9},{5,13},{9,1},{13,5},{2,10},{6,14},... | collective-permute-start | bytes 307208 | tf_op jit(solution)/shard_map/states/ppermute | solution.py:181
  12.1 2.8 %collective-permute-start.6 = (bf16[16,3200]{1,0:T(8,128)(2,1)S(1)}, bf16[16,3200]{1,0:T(8,128)(2,1)S(1)}, u32[]{:S(2)}, u32[]{:S(2)}) collective-permute-start(bf16[16,3200]{1,0:T(8,128)(2,1)S(1)} %states.1.refs_8_.refs_0_), channel_id=1, source_target_pairs={{0,4},{4,8},{8,12},{12,0},{1,5},{5,9},{9,13},{13,1},{2,6},{6,10},{... | collective-permute-start | bytes 307208 | tf_op jit(solution)/shard_map/states/ppermute | solution.py:181
  14.9 1.0 %collective-permute-start.8 = (bf16[16,3200]{1,0:T(8,128)(2,1)S(1)}, bf16[16,3200]{1,0:T(8,128)(2,1)S(1)}, u32[]{:S(2)}, u32[]{:S(2)}) collective-permute-start(bf16[16,3200]{1,0:T(8,128)(2,1)S(1)} %states.1.refs_8_.refs_0_), channel_id=1, source_target_pairs={{0,12},{4,0},{8,4},{12,8},{1,13},{5,1},{9,5},{13,9},{2,14},{6,2},{... | collective-permute-start | bytes 307208 | tf_op jit(solution)/shard_map/states/ppermute | solution.py:181
  16.0 0.0 copy-start
  16.0 2.9 %pairs.1 = (f32[1,128]{1,0:T(1,128)S(1)}, s32[4,128]{1,0:T(4,128)S(1)}) custom-call(s32[1,8]{1,0:T(1,128)S(1)} %get-tuple-element.23.refs_0_, s32[1,8]{1,0:T(1,128)S(1)} %bitcast.10, s32[1,8]{1,0:T(1,128)S(1)} %bitcast.12, s32[1,8]{1,0:T(1,128)S(1)} %bitcast.14, s32[2,256]{1,0:T(2,128)} %bitcast.16, f32[3072,128]{1,0:T(8,128)S(1)} %get-tuple-element.24.refs_5_, ...), custom_call_target="tpu_custom_call" | custom-call | flops 4294967296 | bytes 4194304 | tf_op jit(solution)/shard_map/pairs/pallas_call | solution.py:249
  18.8 0.6 %collective-permute-start.3 = (f32[1,128]{1,0:T(1,128)S(1)}, f32[1,128]{1,0:T(1,128)S(1)}, u32[]{:S(2)}, u32[]{:S(2)}) collective-permute-start(f32[1,128]{1,0:T(1,128)S(1)} %get-tuple-element.31.refs_1_), channel_id=1, source_target_pairs={{0,2},{1,3},{2,0},{3,1},{4,6},{5,7},{6,4},{7,5},{8,10},{9,11},{10,... | collective-permute-start | bytes 1544 | tf_op jit(solution)/shard_map/pairs/ppermute | solution.py:274
  19.4 0.7 %collective-permute-done.4.refs_2_ = bf16[16,3200]{1,0:T(8,128)(2,1)S(1)} collective-permute-done((bf16[16,3200]{1,0:T(8,128)(2,1)S(1)}, bf16[16,3200]{1,0:T(8,128)(2,1)S(1)}, u32[]{:S(2)}, u32[]{:S(2)}) %collective-permute-start.4) | collective-permute-done | bytes 102432 | tf_op jit(solution)/shard_map/states/ppermute | solution.py:181
  20.1 0.0 collective-permute-start.5
  20.2 0.0 collective-permute-done.6.refs_1_
  20.2 0.9 %collective-permute-start.7 = (f32[1,128]{1,0:T(1,128)S(1)}, f32[1,128]{1,0:T(1,128)S(1)}, u32[]{:S(2)}, u32[]{:S(2)}) collective-permute-start(f32[1,128]{1,0:T(1,128)S(1)} %get-tuple-element.31.refs_1_), channel_id=1, source_target_pairs={{0,1},{1,0},{2,3},{3,2},{4,5},{5,4},{6,7},{7,6},{8,9},{9,8},{10,11... | collective-permute-start | bytes 1544 | tf_op jit(solution)/shard_map/pairs/ppermute | solution.py:274
  21.1 0.0 collective-permute-done.8.refs_3_
  21.1 0.0 collective-permute-done.9.refs_5_
  21.1 0.0 copy-done
  21.1 0.9 %scores.2 = (f32[4,128]{1,0:T(4,128)S(1)}, bf16[256,512]{1,0:T(8,128)(2,1)S(1)}) custom-call(bf16[16,3200]{1,0:T(8,128)(2,1)S(1)} %states.1.refs_8_.refs_0_, bf16[16,3200]{1,0:T(8,128)(2,1)S(1)} %collective-permute-done.6.refs_1_, bf16[16,3200]{1,0:T(8,128)(2,1)S(1)} %collective-permute-done.4.refs_2_, bf16[16,3200]{1,0:T(8,128)(2,1)S(1)} %collective-permute-done.8.refs_3_, ...), custom_call_target="tpu_custom_call" | custom-call | flops 100663296 | bytes 2097152 | tf_op jit(solution)/shard_map/scores/pallas_call | solution.py:278
  22.0 0.5 %collective-permute-done.3.refs_0_ = f32[1,128]{1,0:T(1,128)S(1)} collective-permute-done((f32[1,128]{1,0:T(1,128)S(1)}, f32[1,128]{1,0:T(1,128)S(1)}, u32[]{:S(2)}, u32[]{:S(2)}) %collective-permute-start.3) | collective-permute-done | bytes 544 | tf_op jit(solution)/shard_map/pairs/ppermute | solution.py:274
  22.5 0.7 %collective-permute-done.5.refs_2_ = f32[1,128]{1,0:T(1,128)S(1)} collective-permute-done((f32[1,128]{1,0:T(1,128)S(1)}, f32[1,128]{1,0:T(1,128)S(1)}, u32[]{:S(2)}, u32[]{:S(2)}) %collective-permute-start.5) | collective-permute-done | bytes 544 | tf_op jit(solution)/shard_map/pairs/ppermute | solution.py:274
  23.1 0.0 collective-permute-done.7.refs_3_
  23.1 0.2 scores.3
  23.3 0.6 %collective-permute-start.12 = (f32[1,128]{1,0:T(1,128)S(1)}, f32[1,128]{1,0:T(1,128)S(1)}, u32[]{:S(2)}, u32[]{:S(2)}) collective-permute-start(f32[1,128]{1,0:T(1,128)S(1)} %get-tuple-element.40), channel_id=1, source_target_pairs={{0,4},{4,8},{8,12},{12,0},{1,5},{5,9},{9,13},{13,1},{2,6},{6,10},{... | collective-permute-start | bytes 1544 | tf_op jit(solution)/shard_map/back/ppermute | solution.py:181
  23.8 2.4 %collective-permute-start.11 = (f32[1,128]{1,0:T(1,128)S(1)}, f32[1,128]{1,0:T(1,128)S(1)}, u32[]{:S(2)}, u32[]{:S(2)}) collective-permute-start(f32[1,128]{1,0:T(1,128)S(1)} %get-tuple-element.39), channel_id=1, source_target_pairs={{0,8},{4,12},{8,0},{12,4},{1,9},{5,13},{9,1},{13,5},{2,10},{6,14},... | collective-permute-start | bytes 1544 | tf_op jit(solution)/shard_map/back/ppermute | solution.py:181
  26.3 1.3 %collective-permute-start.10 = (f32[1,128]{1,0:T(1,128)S(1)}, f32[1,128]{1,0:T(1,128)S(1)}, u32[]{:S(2)}, u32[]{:S(2)}) collective-permute-start(f32[1,128]{1,0:T(1,128)S(1)} %get-tuple-element.38), channel_id=1, source_target_pairs={{0,12},{4,0},{8,4},{12,8},{1,13},{5,1},{9,5},{13,9},{2,14},{6,2},{... | collective-permute-start | bytes 1544 | tf_op jit(solution)/shard_map/back/ppermute | solution.py:181
  27.6 1.1 %collective-permute-done.12 = f32[1,128]{1,0:T(1,128)S(1)} collective-permute-done((f32[1,128]{1,0:T(1,128)S(1)}, f32[1,128]{1,0:T(1,128)S(1)}, u32[]{:S(2)}, u32[]{:S(2)}) %collective-permute-start.12) | collective-permute-done | bytes 544 | tf_op jit(solution)/shard_map/back/ppermute | solution.py:181
  28.7 0.0 collective-permute-done.11
  28.7 1.1 %collective-permute-done.10 = f32[1,128]{1,0:T(1,128)S(1)} collective-permute-done((f32[1,128]{1,0:T(1,128)S(1)}, f32[1,128]{1,0:T(1,128)S(1)}, u32[]{:S(2)}, u32[]{:S(2)}) %collective-permute-start.10) | collective-permute-done | bytes 544 | tf_op jit(solution)/shard_map/back/ppermute | solution.py:181
  29.8 0.5 %add_bitcast_fusion = f32[128]{0:T(128)} fusion(f32[1,128]{1,0:T(1,128)S(1)} %collective-permute-done.12, f32[1,128]{1,0:T(1,128)S(1)} %collective-permute-done.11, f32[1,128]{1,0:T(1,128)S(1)} %get-tuple-element.37, f32[1,128]{1,0:T(1,128)S(1)} %collective-permute-done.10), kind=kLoop, calls=%fused_computation | loop fusion | flops 384 | bytes 2560 | tf_op jit(solution)/shard_map/reshape | solution.py:306
Async XLA Ops:
  0.0 21.1 %collective-permute-start.9 = (bf16[128,3072]{1,0:T(8,128)(2,1)}, bf16[128,3072]{1,0:T(8,128)(2,1)S(1)}, u32[]{:S(2)}, u32[]{:S(2)}) collective-permute-start(bf16[128,3072]{1,0:T(8,128)(2,1)} %refs_4_.1), channel_id=1, source_target_pairs={{0,2},{2,0},{1,3},{3,1},{4,6},{6,4},{5,7},{7,5},{8,10},{10,8},{9,1... | collective-permute-start | bytes 2359304 | tf_op jit(solution)/shard_map/item_rows/ppermute | solution.py:181
  2.9 7.7 %collective-permute-start = (s32[8]{0:T(128)}, s32[8]{0:T(128)S(1)}, u32[]{:S(2)}, u32[]{:S(2)}) collective-permute-start(s32[8]{0:T(128)} %param.7), channel_id=1, source_target_pairs={{0,4},{4,8},{8,12},{12,0},{1,5},{5,9},{9,13},{13,1},{2,6},{6,10},{... | collective-permute-start | bytes 104 | tf_op jit(solution)/shard_map/ids/ppermute | solution.py:181
  4.5 6.2 %collective-permute-start.1 = (s32[8]{0:T(128)}, s32[8]{0:T(128)S(1)}, u32[]{:S(2)}, u32[]{:S(2)}) collective-permute-start(s32[8]{0:T(128)} %param.7), channel_id=1, source_target_pairs={{0,8},{4,12},{8,0},{12,4},{1,9},{5,13},{9,1},{13,5},{2,10},{6,14},... | collective-permute-start | bytes 104 | tf_op jit(solution)/shard_map/ids/ppermute | solution.py:181
  7.1 3.7 %collective-permute-start.2 = (s32[8]{0:T(128)}, s32[8]{0:T(128)S(1)}, u32[]{:S(2)}, u32[]{:S(2)}) collective-permute-start(s32[8]{0:T(128)} %param.7), channel_id=1, source_target_pairs={{0,12},{4,0},{8,4},{12,8},{1,13},{5,1},{9,5},{13,9},{2,14},{6,2},{... | collective-permute-start | bytes 104 | tf_op jit(solution)/shard_map/ids/ppermute | solution.py:181
  11.2 9.0 %collective-permute-start.4 = (bf16[16,3200]{1,0:T(8,128)(2,1)S(1)}, bf16[16,3200]{1,0:T(8,128)(2,1)S(1)}, u32[]{:S(2)}, u32[]{:S(2)}) collective-permute-start(bf16[16,3200]{1,0:T(8,128)(2,1)S(1)} %states.1.refs_8_.refs_0_), channel_id=1, source_target_pairs={{0,8},{4,12},{8,0},{12,4},{1,9},{5,13},{9,1},{13,5},{2,10},{6,14},... | collective-permute-start | bytes 307208 | tf_op jit(solution)/shard_map/states/ppermute | solution.py:181
  12.1 8.0 %collective-permute-start.6 = (bf16[16,3200]{1,0:T(8,128)(2,1)S(1)}, bf16[16,3200]{1,0:T(8,128)(2,1)S(1)}, u32[]{:S(2)}, u32[]{:S(2)}) collective-permute-start(bf16[16,3200]{1,0:T(8,128)(2,1)S(1)} %states.1.refs_8_.refs_0_), channel_id=1, source_target_pairs={{0,4},{4,8},{8,12},{12,0},{1,5},{5,9},{9,13},{13,1},{2,6},{6,10},{... | collective-permute-start | bytes 307208 | tf_op jit(solution)/shard_map/states/ppermute | solution.py:181
  14.9 6.1 %collective-permute-start.8 = (bf16[16,3200]{1,0:T(8,128)(2,1)S(1)}, bf16[16,3200]{1,0:T(8,128)(2,1)S(1)}, u32[]{:S(2)}, u32[]{:S(2)}) collective-permute-start(bf16[16,3200]{1,0:T(8,128)(2,1)S(1)} %states.1.refs_8_.refs_0_), channel_id=1, source_target_pairs={{0,12},{4,0},{8,4},{12,8},{1,13},{5,1},{9,5},{13,9},{2,14},{6,2},{... | collective-permute-start | bytes 307208 | tf_op jit(solution)/shard_map/states/ppermute | solution.py:181
  16.0 5.1 %copy-start = (bf16[128,3072]{1,0:T(8,128)(2,1)S(1)}, bf16[128,3072]{1,0:T(8,128)(2,1)}, u32[]{:S(2)}) copy-start(bf16[128,3072]{1,0:T(8,128)(2,1)} %refs_4_.1) | copy-start | bytes 2359300
  18.8 3.6 %collective-permute-start.3 = (f32[1,128]{1,0:T(1,128)S(1)}, f32[1,128]{1,0:T(1,128)S(1)}, u32[]{:S(2)}, u32[]{:S(2)}) collective-permute-start(f32[1,128]{1,0:T(1,128)S(1)} %get-tuple-element.31.refs_1_), channel_id=1, source_target_pairs={{0,2},{1,3},{2,0},{3,1},{4,6},{5,7},{6,4},{7,5},{8,10},{9,11},{10,... | collective-permute-start | bytes 1544 | tf_op jit(solution)/shard_map/pairs/ppermute | solution.py:274
  20.1 3.0 %collective-permute-start.5 = (f32[1,128]{1,0:T(1,128)S(1)}, f32[1,128]{1,0:T(1,128)S(1)}, u32[]{:S(2)}, u32[]{:S(2)}) collective-permute-start(f32[1,128]{1,0:T(1,128)S(1)} %get-tuple-element.31.refs_1_), channel_id=1, source_target_pairs={{0,3},{1,2},{2,1},{3,0},{4,7},{5,6},{6,5},{7,4},{8,11},{9,10},{10,... | collective-permute-start | bytes 1544 | tf_op jit(solution)/shard_map/pairs/ppermute | solution.py:274
  20.2 3.0 %collective-permute-start.7 = (f32[1,128]{1,0:T(1,128)S(1)}, f32[1,128]{1,0:T(1,128)S(1)}, u32[]{:S(2)}, u32[]{:S(2)}) collective-permute-start(f32[1,128]{1,0:T(1,128)S(1)} %get-tuple-element.31.refs_1_), channel_id=1, source_target_pairs={{0,1},{1,0},{2,3},{3,2},{4,5},{5,4},{6,7},{7,6},{8,9},{9,8},{10,11... | collective-permute-start | bytes 1544 | tf_op jit(solution)/shard_map/pairs/ppermute | solution.py:274
  23.3 5.4 %collective-permute-start.12 = (f32[1,128]{1,0:T(1,128)S(1)}, f32[1,128]{1,0:T(1,128)S(1)}, u32[]{:S(2)}, u32[]{:S(2)}) collective-permute-start(f32[1,128]{1,0:T(1,128)S(1)} %get-tuple-element.40), channel_id=1, source_target_pairs={{0,4},{4,8},{8,12},{12,0},{1,5},{5,9},{9,13},{13,1},{2,6},{6,10},{... | collective-permute-start | bytes 1544 | tf_op jit(solution)/shard_map/back/ppermute | solution.py:181
  23.8 4.8 %collective-permute-start.11 = (f32[1,128]{1,0:T(1,128)S(1)}, f32[1,128]{1,0:T(1,128)S(1)}, u32[]{:S(2)}, u32[]{:S(2)}) collective-permute-start(f32[1,128]{1,0:T(1,128)S(1)} %get-tuple-element.39), channel_id=1, source_target_pairs={{0,8},{4,12},{8,0},{12,4},{1,9},{5,13},{9,1},{13,5},{2,10},{6,14},... | collective-permute-start | bytes 1544 | tf_op jit(solution)/shard_map/back/ppermute | solution.py:181
  26.3 3.5 %collective-permute-start.10 = (f32[1,128]{1,0:T(1,128)S(1)}, f32[1,128]{1,0:T(1,128)S(1)}, u32[]{:S(2)}, u32[]{:S(2)}) collective-permute-start(f32[1,128]{1,0:T(1,128)S(1)} %get-tuple-element.38), channel_id=1, source_target_pairs={{0,12},{4,0},{8,4},{12,8},{1,13},{5,1},{9,5},{13,9},{2,14},{6,2},{... | collective-permute-start | bytes 1544 | tf_op jit(solution)/shard_map/back/ppermute | solution.py:181
